TPU v7x, 32 devices: a whole 2x2x4 slice. The times are simulated.
32 devices in a mesh: cells: 32 (over z, y, x, core).
Axes of the slice: x: 2, y: 2, z: 4, core: 2. Of those that a mesh axis runs over, the one named last changes fastest.
Arguments:
- block: bfloat16 [6912, 128], P('cells'), may hold values from -6 to 6
- cell_matrix: bfloat16 [32, 343, 343], P('cells'), may hold values from -1 to 3
- connectivity: int32 [32, 343], P('cells'), may hold values from 0 to 342, as said below
- potential: float32 [10976], P('cells'), may hold values from -1.5 to 1.5
- locked: bfloat16 [6912, 704], P('cells'), may hold values from -0.078125 to 0.078125
Outputs:
- filtered: bfloat16 [6912, 128], P('cells')
- intersection: float32 [704, 128], replicated
Inputs may be any that keep to these rules, and one draw needn't show every extreme that they name: `connectivity`: A partition's 1 row list each of its 1 x 1 x 1 cells once, in some order; a row gives the local slots of that sixth-order hexahedron's 343 nodes, in some order, where a node with local coordinates (i, j, k), each from 0 to 6, has slot (i * 7 + j) * 7 + k; neighbouring cells share nodes.
All inputs are finite; a program needn't handle non-finite values.
Results may differ from a plain program's by a relative error of at most 0.0067.
Values may be sent and summed in bfloat16 or wider, within the bound.
No kernel may reach another device: no remote copies, remote signals or barrier semaphores. Data moves between devices by JAX's collectives and lax.ppermute only.
A program may use at most 64 MiB of HBM per device.

v0:
```python
import jax
import jax.numpy as jnp
from jax import lax
from jax.sharding import PartitionSpec as P

GRID_Y = 4
GRID_Z = 4
SIDE = 7


chebyshev_coeffs = ((-1.0 / 7.0, 0.0), (-7.0 / 41.0, 8.0 / 41.0), (-41.0 / 259.0, 28.0 / 259.0))
centre = 6.0


def passed_along(value, axis, by):
    count = lax.axis_size(axis)
    pairs = [(i, i + by) for i in range(count) if 0 <= i + by < count]
    return lax.ppermute(value, axis, pairs)


def advance(applied, previous, older, coeffs):
    return (
        coeffs[0] * (applied - centre * previous.astype(jnp.float32))
        - coeffs[1] * older.astype(jnp.float32)
    ).astype(jnp.bfloat16)


def set_first(field, plane, axis_dim):
    rest = lax.slice_in_dim(field, 1, field.shape[axis_dim], axis=axis_dim)
    return jnp.concatenate([jnp.expand_dims(plane, axis_dim), rest], axis=axis_dim)


def add_last(field, plane, axis_dim):
    length = field.shape[axis_dim]
    front = lax.slice_in_dim(field, 0, length - 1, axis=axis_dim)
    last_plane = lax.index_in_dim(field, length - 1, axis_dim, keepdims=False) + plane
    return jnp.concatenate([front, jnp.expand_dims(last_plane, axis_dim)], axis=axis_dim)


def per_device(block, cell_matrix, connectivity, potential, locked):
    owned_rows = block.shape[0]
    slot_count = potential.shape[0]
    columns = block.shape[1]
    edge = SIDE - 1
    position = lax.axis_index("cells")
    grid_x = lax.axis_size("cells") // (GRID_Y * GRID_Z)
    coords = (position // (GRID_Y * GRID_Z), position // GRID_Z % GRID_Y, position % GRID_Z)
    counts = (grid_x, GRID_Y, GRID_Z)
    stride = (GRID_Y * GRID_Z, GRID_Z, 1)
    older = block
    current = block
    for coeffs in chebyshev_coeffs:
        field = (
            jnp.zeros((SIDE, SIDE, SIDE, columns), jnp.bfloat16)
            .at[1:, 1:, 1:]
            .set(current.reshape(edge, edge, edge, columns))
        )
        for axis_dim in range(3):
            plane = lax.index_in_dim(field, SIDE - 1, axis_dim, keepdims=False)
            arrived = passed_along(plane, "cells", stride[axis_dim])
            arrived = jnp.where(coords[axis_dim] > 0, arrived, jnp.zeros_like(arrived))
            field = set_first(field, arrived, axis_dim)
        local_rows = field.reshape(slot_count, columns)
        gathered = jnp.take(local_rows, connectivity, axis=0)
        products = jnp.einsum(
            "cij,cjs->cis", cell_matrix, gathered, preferred_element_type=jnp.float32
        )
        summed = (
            jnp.zeros((slot_count, columns), jnp.float32)
            .at[connectivity.reshape(-1)]
            .add(products.reshape(-1, columns))
        )
        partial_value = (summed + potential[:, None] * local_rows.astype(jnp.float32)).reshape(
            SIDE, SIDE, SIDE, columns
        )
        for axis_dim in (2, 1, 0):
            plane = lax.index_in_dim(partial_value, 0, axis_dim, keepdims=False)
            arrived = passed_along(plane, "cells", -stride[axis_dim])
            arrived = jnp.where(coords[axis_dim] < counts[axis_dim] - 1, arrived, 0.0)
            partial_value = add_last(partial_value, arrived, axis_dim)
        following = advance(
            partial_value[1:, 1:, 1:].reshape(owned_rows, columns), current, older, coeffs
        )
        older = current
        current = following
    partial_intersection = jnp.einsum(
        "nl,ns->ls", locked, current, preferred_element_type=jnp.float32
    )
    intersection = lax.psum(partial_intersection, "cells")
    return (current, intersection)


def solution(mesh):
    in_specs = (
        P("cells", None),
        P("cells", None, None),
        P("cells", None),
        P("cells"),
        P("cells", None),
    )
    out_specs = (P("cells", None), P())
    return jax.shard_map(
        per_device, mesh=mesh, in_specs=in_specs, out_specs=out_specs, check_vma=False
    )
```

profile of v0, /device:TPU:0, one launch (start us, length us, event | category | flops | bytes accessed | tf_op | source)
XLA Modules:
  0.0 261.0 jit_solution(1577498445836857648)
XLA Ops:
  8.1 5.9 %collective-permute-start = (bf16[7,7,128]{2,0,1:T(8,128)(2,1)S(1)}, bf16[7,7,128]{2,0,1:T(8,128)(2,1)S(1)}, u32[]{:S(2)}, u32[]{:S(2)}) collective-permute-start(bf16[7,7,128]{2,0,1:T(8,128)(2,1)S(1)} %bitcast.195), channel_id=1, source_target_pairs={{0,16},{1,17},{2,18},{3,19},{4,20},{5,21},{6,22},{7,23},{8,24},{9,... | collective-permute-start | bytes 37640 | tf_op jit(solution)/shard_map/ppermute | solution.py:18
  14.2 1.3 collective-permute-done
  15.5 3.4 %collective-permute-start.1 = (bf16[7,7,128]{2,1,0:T(8,128)(2,1)S(1)}, bf16[7,7,128]{2,1,0:T(8,128)(2,1)S(1)}, u32[]{:S(2)}, u32[]{:S(2)}) collective-permute-start(bf16[7,7,128]{2,1,0:T(8,128)(2,1)S(1)} %maximum_bitcast_fusion), channel_id=1, source_target_pairs={{0,4},{1,5},{2,6},{3,7},{4,8},{5,9},{6,10},{7,11},{8,12},{9,13},{1... | collective-permute-start | bytes 37640 | tf_op jit(solution)/shard_map/ppermute | solution.py:18
  19.0 1.4 collective-permute-done.1
  22.7 1.4 gather_fusion
  25.5 2.4 scatter_fusion
  28.0 1.3 collective-permute-start.3
  29.3 3.5 %collective-permute-done.3 = f32[7,7,128]{2,1,0:T(8,128)S(1)} collective-permute-done((f32[7,7,128]{2,1,0:T(8,128)S(1)}, f32[7,7,128]{2,1,0:T(8,128)S(1)}, u32[]{:S(2)}, u32[]{:S(2)}) %collective-permute-start.3) | collective-permute-done | bytes 25120 | tf_op jit(solution)/shard_map/ppermute | solution.py:18
  34.2 7.5 %collective-permute-done.4 = f32[7,7,128]{2,1,0:T(8,128)S(1)} collective-permute-done((f32[7,7,128]{2,1,0:T(8,128)S(1)}, f32[7,7,128]{2,1,0:T(8,128)S(1)}, u32[]{:S(2)}, u32[]{:S(2)}) %collective-permute-start.4) | collective-permute-done | bytes 25120 | tf_op jit(solution)/shard_map/ppermute | solution.py:18
  41.7 1.3 collective-permute-start.5
  43.1 7.0 %collective-permute-done.5 = f32[7,7,128]{2,1,0:T(8,128)S(1)} collective-permute-done((f32[7,7,128]{2,1,0:T(8,128)S(1)}, f32[7,7,128]{2,1,0:T(8,128)S(1)}, u32[]{:S(2)}, u32[]{:S(2)}) %collective-permute-start.5) | collective-permute-done | bytes 25120 | tf_op jit(solution)/shard_map/ppermute | solution.py:18
  51.0 1.6 collective-permute-start.6
  52.7 1.4 collective-permute-done.6
  54.1 3.3 %collective-permute-start.7 = (bf16[7,7,128]{2,1,0:T(8,128)(2,1)S(1)}, bf16[7,7,128]{2,1,0:T(8,128)(2,1)S(1)}, u32[]{:S(2)}, u32[]{:S(2)}) collective-permute-start(bf16[7,7,128]{2,1,0:T(8,128)(2,1)S(1)} %bitcast.197), channel_id=1, source_target_pairs={{0,4},{1,5},{2,6},{3,7},{4,8},{5,9},{6,10},{7,11},{8,12},{9,13},{1... | collective-permute-start | bytes 37640 | tf_op jit(solution)/shard_map/ppermute | solution.py:18
  57.4 1.4 collective-permute-done.7
  61.1 1.4 gather_fusion.1
  63.0 2.4 scatter_fusion.1
  65.6 1.3 collective-permute-start.9
  66.9 2.2 collective-permute-done.9
  70.5 8.5 %collective-permute-done.10 = f32[7,7,128]{2,1,0:T(8,128)S(1)} collective-permute-done((f32[7,7,128]{2,1,0:T(8,128)S(1)}, f32[7,7,128]{2,1,0:T(8,128)S(1)}, u32[]{:S(2)}, u32[]{:S(2)}) %collective-permute-start.10) | collective-permute-done | bytes 25120 | tf_op jit(solution)/shard_map/ppermute | solution.py:18
  80.3 7.4 %collective-permute-done.11 = f32[7,7,128]{2,1,0:T(8,128)S(1)} collective-permute-done((f32[7,7,128]{2,1,0:T(8,128)S(1)}, f32[7,7,128]{2,1,0:T(8,128)S(1)}, u32[]{:S(2)}, u32[]{:S(2)}) %collective-permute-start.11) | collective-permute-done | bytes 25120 | tf_op jit(solution)/shard_map/ppermute | solution.py:18
  87.9 1.6 collective-permute-start.12
  89.6 1.4 collective-permute-done.12
  91.0 3.6 %collective-permute-start.13 = (bf16[7,7,128]{2,1,0:T(8,128)(2,1)S(1)}, bf16[7,7,128]{2,1,0:T(8,128)(2,1)S(1)}, u32[]{:S(2)}, u32[]{:S(2)}) collective-permute-start(bf16[7,7,128]{2,1,0:T(8,128)(2,1)S(1)} %bitcast.198), channel_id=1, source_target_pairs={{0,4},{1,5},{2,6},{3,7},{4,8},{5,9},{6,10},{7,11},{8,12},{9,13},{1... | collective-permute-start | bytes 37640 | tf_op jit(solution)/shard_map/ppermute | solution.py:18
  94.7 1.4 collective-permute-done.13
  98.4 1.4 gather_fusion.2
  100.3 2.4 scatter_fusion.2
  104.1 1.8 collective-permute-done.15
  107.3 8.9 %collective-permute-done.16 = f32[7,7,128]{2,1,0:T(8,128)S(1)} collective-permute-done((f32[7,7,128]{2,1,0:T(8,128)S(1)}, f32[7,7,128]{2,1,0:T(8,128)S(1)}, u32[]{:S(2)}, u32[]{:S(2)}) %collective-permute-start.16) | collective-permute-done | bytes 25120 | tf_op jit(solution)/shard_map/ppermute | solution.py:18
  117.6 7.1 %collective-permute-done.17 = f32[7,7,128]{2,1,0:T(8,128)S(1)} collective-permute-done((f32[7,7,128]{2,1,0:T(8,128)S(1)}, f32[7,7,128]{2,1,0:T(8,128)S(1)}, u32[]{:S(2)}, u32[]{:S(2)}) %collective-permute-start.17) | collective-permute-done | bytes 25120 | tf_op jit(solution)/shard_map/ppermute | solution.py:18
  125.9 126.5 %all-reduce.5.cloned.1.call-done = f32[704,128]{1,0:T(8,128)} async-done(((f32[704,128]{1,0:T(8,128)}), f32[704,128]{1,0:T(8,128)}) %all-reduce.5.cloned.1.call-update) | async-done | bytes 360464 | tf_op jit(solution)/shard_map/psum | solution.py:89
  252.4 1.7 copy.336
  (126 shorter events, 20.8 us)
Async XLA Ops:
  7.2 117.7 %copy-start = (bf16[216,704]{1,0:T(8,128)(2,1)S(1)}, bf16[216,704]{1,0:T(8,128)(2,1)}, u32[]{:S(2)}) copy-start(bf16[216,704]{1,0:T(8,128)(2,1)} %param.17) | copy-start | bytes 912388
  7.2 245.2 %all-reduce.5.cloned.1.call-start = ((), (), s32[]{:S(2)}) async-start(), calls=%async_computation | async-start | bytes 720896 | tf_op jit(solution)/shard_map/psum | solution.py:89
  8.1 6.0 %copy-start.5 = (s32[1,343]{1,0:T(1,128)S(1)}, s32[1,343]{1,0:T(1,128)}, u32[]{:S(2)}) copy-start(s32[1,343]{1,0:T(1,128)} %param.15) | copy-start | bytes 4120
  8.1 7.4 %collective-permute-start = (bf16[7,7,128]{2,0,1:T(8,128)(2,1)S(1)}, bf16[7,7,128]{2,0,1:T(8,128)(2,1)S(1)}, u32[]{:S(2)}, u32[]{:S(2)}) collective-permute-start(bf16[7,7,128]{2,0,1:T(8,128)(2,1)S(1)} %bitcast.195), channel_id=1, source_target_pairs={{0,16},{1,17},{2,18},{3,19},{4,20},{5,21},{6,22},{7,23},{8,24},{9,... | collective-permute-start | bytes 37640 | tf_op jit(solution)/shard_map/ppermute | solution.py:18
  15.5 4.8 %collective-permute-start.1 = (bf16[7,7,128]{2,1,0:T(8,128)(2,1)S(1)}, bf16[7,7,128]{2,1,0:T(8,128)(2,1)S(1)}, u32[]{:S(2)}, u32[]{:S(2)}) collective-permute-start(bf16[7,7,128]{2,1,0:T(8,128)(2,1)S(1)} %maximum_bitcast_fusion), channel_id=1, source_target_pairs={{0,4},{1,5},{2,6},{3,7},{4,8},{5,9},{6,10},{7,11},{8,12},{9,13},{1... | collective-permute-start | bytes 37640 | tf_op jit(solution)/shard_map/ppermute | solution.py:18
  20.5 2.1 collective-permute-start.2
  22.7 1.4 copy-start.4
  24.2 1.0 copy-start.1
  28.0 4.8 %collective-permute-start.3 = (f32[7,7,128]{2,1,0:T(8,128)S(1)}, f32[7,7,128]{2,1,0:T(8,128)S(1)}, u32[]{:S(2)}, u32[]{:S(2)}) collective-permute-start(f32[7,7,128]{2,1,0:T(8,128)S(1)} %bitcast.192), channel_id=1, source_target_pairs={{1,0},{2,1},{3,2},{4,3},{5,4},{6,5},{7,6},{8,7},{9,8},{10,9},{11,1... | collective-permute-start | bytes 75272 | tf_op jit(solution)/shard_map/ppermute | solution.py:18
  32.9 8.8 %collective-permute-start.4 = (f32[7,7,128]{2,1,0:T(8,128)S(1)}, f32[7,7,128]{2,1,0:T(8,128)S(1)}, u32[]{:S(2)}, u32[]{:S(2)}) collective-permute-start(f32[7,7,128]{2,1,0:T(8,128)S(1)} %fusion.69), channel_id=1, source_target_pairs={{4,0},{5,1},{6,2},{7,3},{8,4},{9,5},{10,6},{11,7},{12,8},{13,9},{1... | collective-permute-start | bytes 75272 | tf_op jit(solution)/shard_map/ppermute | solution.py:18
  41.7 8.3 %collective-permute-start.5 = (f32[7,7,128]{2,1,0:T(8,128)S(1)}, f32[7,7,128]{2,1,0:T(8,128)S(1)}, u32[]{:S(2)}, u32[]{:S(2)}) collective-permute-start(f32[7,7,128]{2,1,0:T(8,128)S(1)} %fusion.68), channel_id=1, source_target_pairs={{16,0},{17,1},{18,2},{19,3},{20,4},{21,5},{22,6},{23,7},{24,8},{25... | collective-permute-start | bytes 75272 | tf_op jit(solution)/shard_map/ppermute | solution.py:18
  50.1 0.8 copy-start.2
  51.0 3.0 %collective-permute-start.6 = (bf16[7,7,128]{2,0,1:T(8,128)(2,1)S(1)}, bf16[7,7,128]{2,0,1:T(8,128)(2,1)S(1)}, u32[]{:S(2)}, u32[]{:S(2)}) collective-permute-start(bf16[7,7,128]{2,0,1:T(8,128)(2,1)S(1)} %fusion.75), channel_id=1, source_target_pairs={{0,16},{1,17},{2,18},{3,19},{4,20},{5,21},{6,22},{7,23},{8,24},{9,... | collective-permute-start | bytes 37640 | tf_op jit(solution)/shard_map/ppermute | solution.py:18
  54.1 4.7 %collective-permute-start.7 = (bf16[7,7,128]{2,1,0:T(8,128)(2,1)S(1)}, bf16[7,7,128]{2,1,0:T(8,128)(2,1)S(1)}, u32[]{:S(2)}, u32[]{:S(2)}) collective-permute-start(bf16[7,7,128]{2,1,0:T(8,128)(2,1)S(1)} %bitcast.197), channel_id=1, source_target_pairs={{0,4},{1,5},{2,6},{3,7},{4,8},{5,9},{6,10},{7,11},{8,12},{9,13},{1... | collective-permute-start | bytes 37640 | tf_op jit(solution)/shard_map/ppermute | solution.py:18
  58.9 2.1 collective-permute-start.8
  65.6 3.5 %collective-permute-start.9 = (f32[7,7,128]{2,0,1:T(8,128)S(1)}, f32[7,7,128]{2,0,1:T(8,128)S(1)}, u32[]{:S(2)}, u32[]{:S(2)}) collective-permute-start(f32[7,7,128]{2,0,1:T(8,128)S(1)} %bitcast.193), channel_id=1, source_target_pairs={{1,0},{2,1},{3,2},{4,3},{5,4},{6,5},{7,6},{8,7},{9,8},{10,9},{11,1... | collective-permute-start | bytes 75272 | tf_op jit(solution)/shard_map/ppermute | solution.py:18
  69.2 9.8 %collective-permute-start.10 = (f32[7,7,128]{2,1,0:T(8,128)S(1)}, f32[7,7,128]{2,1,0:T(8,128)S(1)}, u32[]{:S(2)}, u32[]{:S(2)}) collective-permute-start(f32[7,7,128]{2,1,0:T(8,128)S(1)} %fusion.67), channel_id=1, source_target_pairs={{4,0},{5,1},{6,2},{7,3},{8,4},{9,5},{10,6},{11,7},{12,8},{13,9},{1... | collective-permute-start | bytes 75272 | tf_op jit(solution)/shard_map/ppermute | solution.py:18
  79.0 8.8 %collective-permute-start.11 = (f32[7,7,128]{2,1,0:T(8,128)S(1)}, f32[7,7,128]{2,1,0:T(8,128)S(1)}, u32[]{:S(2)}, u32[]{:S(2)}) collective-permute-start(f32[7,7,128]{2,1,0:T(8,128)S(1)} %fusion.66), channel_id=1, source_target_pairs={{16,0},{17,1},{18,2},{19,3},{20,4},{21,5},{22,6},{23,7},{24,8},{25... | collective-permute-start | bytes 75272 | tf_op jit(solution)/shard_map/ppermute | solution.py:18
  87.9 3.0 %collective-permute-start.12 = (bf16[7,7,128]{2,0,1:T(8,128)(2,1)S(1)}, bf16[7,7,128]{2,0,1:T(8,128)(2,1)S(1)}, u32[]{:S(2)}, u32[]{:S(2)}) collective-permute-start(bf16[7,7,128]{2,0,1:T(8,128)(2,1)S(1)} %fusion.76), channel_id=1, source_target_pairs={{0,16},{1,17},{2,18},{3,19},{4,20},{5,21},{6,22},{7,23},{8,24},{9,... | collective-permute-start | bytes 37640 | tf_op jit(solution)/shard_map/ppermute | solution.py:18
  91.0 5.0 %collective-permute-start.13 = (bf16[7,7,128]{2,1,0:T(8,128)(2,1)S(1)}, bf16[7,7,128]{2,1,0:T(8,128)(2,1)S(1)}, u32[]{:S(2)}, u32[]{:S(2)}) collective-permute-start(bf16[7,7,128]{2,1,0:T(8,128)(2,1)S(1)} %bitcast.198), channel_id=1, source_target_pairs={{0,4},{1,5},{2,6},{3,7},{4,8},{5,9},{6,10},{7,11},{8,12},{9,13},{1... | collective-permute-start | bytes 37640 | tf_op jit(solution)/shard_map/ppermute | solution.py:18
  96.2 2.1 collective-permute-start.14
  102.8 3.1 %collective-permute-start.15 = (f32[7,7,128]{2,0,1:T(8,128)S(1)}, f32[7,7,128]{2,0,1:T(8,128)S(1)}, u32[]{:S(2)}, u32[]{:S(2)}) collective-permute-start(f32[7,7,128]{2,0,1:T(8,128)S(1)} %bitcast.194), channel_id=1, source_target_pairs={{1,0},{2,1},{3,2},{4,3},{5,4},{6,5},{7,6},{8,7},{9,8},{10,9},{11,1... | collective-permute-start | bytes 75272 | tf_op jit(solution)/shard_map/ppermute | solution.py:18
  106.0 10.2 %collective-permute-start.16 = (f32[7,7,128]{2,1,0:T(8,128)S(1)}, f32[7,7,128]{2,1,0:T(8,128)S(1)}, u32[]{:S(2)}, u32[]{:S(2)}) collective-permute-start(f32[7,7,128]{2,1,0:T(8,128)S(1)} %fusion.65), channel_id=1, source_target_pairs={{4,0},{5,1},{6,2},{7,3},{8,4},{9,5},{10,6},{11,7},{12,8},{13,9},{1... | collective-permute-start | bytes 75272 | tf_op jit(solution)/shard_map/ppermute | solution.py:18
  116.3 8.4 %collective-permute-start.17 = (f32[7,7,128]{2,1,0:T(8,128)S(1)}, f32[7,7,128]{2,1,0:T(8,128)S(1)}, u32[]{:S(2)}, u32[]{:S(2)}) collective-permute-start(f32[7,7,128]{2,1,0:T(8,128)S(1)} %fusion.64), channel_id=1, source_target_pairs={{16,0},{17,1},{18,2},{19,3},{20,4},{21,5},{22,6},{23,7},{24,8},{25... | collective-permute-start | bytes 75272 | tf_op jit(solution)/shard_map/ppermute | solution.py:18
  124.8 1.1 copy-start.3
Sparse Core Ops, SparseCore 0:
  126.0 126.3 all-reduce.4
where the time goes:
time: 262 us; the launch traced here: 261 us
  waiting for transfers between devices  191 us (73%)
  starting transfers between devices  35 us (13%)
  between operations  14.9 us (6%)
  local copies, waits for them, and re-layouts  9.41 us (4%)
  other arithmetic  8.6 us (3%)
    psum x1, waiting for transfers between devices, per_device(): intersection = lax.psum(partial_intersection, 'cells')  126 us
    ppermute x18, waiting for transfers between devices, passed_along(): return lax.ppermute(value, axis, pairs)  64.4 us
    ppermute x18, starting transfers between devices, passed_along(): return lax.ppermute(value, axis, pairs)  35 us
    scatter-add x3, other arithmetic, per_device(): summed = jnp.zeros((slot_count, columns), jnp.float32).at[connectivity.re...  7.32 us
  transfers between devices with their start and end apart: 19, of which 19 were waited for; matrix products, arithmetic and copies ran while one was open for 0% of the time, Pallas kernels for 0%

commit v1 on v0

v1 whole, which is shorter than its diff:
```python
import jax
import jax.numpy as jnp
from jax import lax
from jax.sharding import PartitionSpec as P

GRID_Y = 4
GRID_Z = 4
SIDE = 7
AXIS = "cells"

chebyshev_coeffs = ((-1.0 / 7.0, 0.0), (-7.0 / 41.0, 8.0 / 41.0), (-41.0 / 259.0, 28.0 / 259.0))
centre = 6.0


class Grid:
    def __init__(self):
        self.devices = lax.axis_size(AXIS)
        self.counts = (self.devices // (GRID_Y * GRID_Z), GRID_Y, GRID_Z)
        self.stride = (GRID_Y * GRID_Z, GRID_Z, 1)
        position = lax.axis_index(AXIS)
        self.coords = tuple(
            position // self.stride[d] % self.counts[d] for d in range(3)
        )

    def coord_of(self, device, dim):
        return device // self.stride[dim] % self.counts[dim]

    def up(self, value, dim):
        by = self.stride[dim]
        pairs = [
            (i, i + by)
            for i in range(self.devices)
            if self.coord_of(i, dim) + 1 < self.counts[dim]
        ]
        return lax.ppermute(value, AXIS, pairs)

    def down(self, value, dim):
        by = self.stride[dim]
        pairs = [
            (i, i - by) for i in range(self.devices) if self.coord_of(i, dim) > 0
        ]
        return lax.ppermute(value, AXIS, pairs)

    def swapped(self, low, high, dim, odd):
        by = self.stride[dim]
        pairs = []
        for i in range(self.devices):
            c = self.coord_of(i, dim)
            if c % 2 == odd and c + 1 < self.counts[dim]:
                pairs += [(i, i + by), (i + by, i)]
        lower = self.coords[dim] % 2 == odd
        arrived = lax.ppermute(jnp.where(lower, high, low), AXIS, pairs)
        zero = jnp.zeros_like(arrived)
        return jnp.where(lower, zero, arrived), jnp.where(lower, arrived, zero)


def plane(field, dim, at):
    return lax.slice_in_dim(field, at, at + 1, axis=dim)


def with_ends(field, dim, low, high):
    last = field.shape[dim] - 1
    parts = [
        plane(field, dim, 0) if low is None else low,
        lax.slice_in_dim(field, 1, last, axis=dim),
        plane(field, dim, last) if high is None else high,
    ]
    return jnp.concatenate(parts, axis=dim)


def slots_matrix(cell_matrix, connectivity, slot_count):
    total = None
    for c in range(cell_matrix.shape[0]):
        chosen = (
            connectivity[c][:, None] == jnp.arange(slot_count, dtype=jnp.int32)[None, :]
        ).astype(jnp.bfloat16)
        rows = lax.dot_general(
            chosen, cell_matrix[c], (((0,), (0,)), ((), ())), preferred_element_type=jnp.float32
        ).astype(jnp.bfloat16)
        both = jnp.dot(rows, chosen, preferred_element_type=jnp.float32)
        total = both if total is None else total + both
    return total.astype(jnp.bfloat16)


def summed_everywhere(value):
    n = lax.axis_size(AXIS)
    rows, columns = value.shape
    per = -(-rows // n)
    padded = jnp.pad(value.astype(jnp.bfloat16), ((0, n * per - rows), (0, 0)))
    dealt = lax.all_to_all(padded.reshape(n, per, columns), AXIS, 0, 0)
    mine = jnp.sum(dealt.astype(jnp.float32), axis=0).astype(jnp.bfloat16)
    back = lax.all_to_all(jnp.broadcast_to(mine[None], (n, per, columns)), AXIS, 0, 0)
    return back.reshape(n * per, columns)[:rows].astype(jnp.float32)


def per_device(block, cell_matrix, connectivity, potential, locked):
    owned_rows, columns = block.shape
    slot_count = potential.shape[0]
    edge = SIDE - 1
    grid = Grid()
    shape = (SIDE, SIDE, SIDE, columns)
    matrix = slots_matrix(cell_matrix, connectivity, slot_count)
    lumped = potential[:, None]

    field = (
        jnp.zeros(shape, jnp.bfloat16)
        .at[1:, 1:, 1:]
        .set(block.reshape(edge, edge, edge, columns))
    )
    for dim in range(3):
        field = with_ends(field, dim, grid.up(plane(field, dim, SIDE - 1), dim), None)

    inside = jnp.ones((SIDE, SIDE, SIDE, 1), jnp.bool_)
    for dim in range(3):
        at = lax.broadcasted_iota(jnp.int32, (SIDE, SIDE, SIDE, 1), dim)
        inside = inside & ((at > 0) | (grid.coords[dim] > 0))

    older = field
    current = field
    steps = len(chebyshev_coeffs)
    for step, coeffs in enumerate(chebyshev_coeffs):
        rows = current.reshape(slot_count, columns)
        partial = jnp.dot(matrix, rows, preferred_element_type=jnp.float32)
        partial = (partial + lumped * rows.astype(jnp.float32)).reshape(shape)
        for dim in (2, 1, 0):
            low, high = plane(partial, dim, 0), plane(partial, dim, SIDE - 1)
            if step < steps - 1:
                low16, high16 = low.astype(jnp.bfloat16), high.astype(jnp.bfloat16)
                for odd in (0, 1):
                    if grid.counts[dim] > odd + 1:
                        to_low, to_high = grid.swapped(low16, high16, dim, odd)
                        low = low + to_low.astype(jnp.float32)
                        high = high + to_high.astype(jnp.float32)
                partial = with_ends(partial, dim, low, high)
            else:
                arrived = grid.down(low.astype(jnp.bfloat16), dim)
                partial = with_ends(partial, dim, None, high + arrived.astype(jnp.float32))
        following = coeffs[0] * (partial - centre * current.astype(jnp.float32)) - coeffs[
            1
        ] * older.astype(jnp.float32)
        following = jnp.where(inside, following, 0.0).astype(jnp.bfloat16)
        older = current
        current = following
    filtered = current[1:, 1:, 1:].reshape(owned_rows, columns)
    partial_intersection = jnp.einsum(
        "nl,ns->ls", locked, filtered, preferred_element_type=jnp.float32
    )
    return filtered, summed_everywhere(partial_intersection)


def solution(mesh):
    in_specs = (
        P(AXIS, None),
        P(AXIS, None, None),
        P(AXIS, None),
        P(AXIS),
        P(AXIS, None),
    )
    out_specs = (P(AXIS, None), P())
    return jax.shard_map(
        per_device, mesh=mesh, in_specs=in_specs, out_specs=out_specs, check_vma=False
    )
```

time: 262 us -> 99.2 us (0.38)
  waiting for transfers between devices: 191 us -> 24.8 us
  blocking collectives: 0 us -> 27.2 us
  between operations: 14.9 us -> 1.22 us
  other arithmetic: 8.6 us -> 1.22 us
  local copies, waits for them, and re-layouts: 9.41 us -> 3.3 us
  starting transfers between devices: 35 us -> 38.9 us
    psum x1 -> x0, waiting for transfers between devices: 126 us -> none  [per_device(): intersection = lax.psum(partial_intersection, 'cells')]
    ppermute x18 -> x16, waiting for transfers between devices: 64.4 us -> 24.8 us  [the longest x3 15.2 us: down(): return lax.ppermute(value, AXIS, pairs)]
    all_to_all x0 -> x2, blocking collectives: none -> 27.2 us  [the longest x1 15.8 us: summed_everywhere(): dealt = lax.all_to_all(padded.reshape(n, per, columns), AXIS, 0, 0)]
    scatter-add x3 -> x0, other arithmetic: 7.32 us -> none  [per_device(): summed = jnp.zeros((slot_count, columns), jnp.float32).at[connectivity.re...]
    gather x3 -> x0, local copies, waits for them, and re-layouts: 4.26 us -> none  [per_device(): gathered = jnp.take(local_rows, connectivity, axis=0)]
    ppermute x18 -> x16, starting transfers between devices: 35 us -> 38.9 us  [the longest x10 24.4 us: swapped(): arrived = lax.ppermute(jnp.where(lower, high, low), AXIS, pairs)]
  transfers between devices with their start and end apart: 19 -> 16, of which waited for: 19 -> 12; matrix products, arithmetic and copies ran while one was open for 0% -> 1% of each run, Pallas kernels for 0% -> 0%
where the time goes in v1:
time: 99.2 us; the launch traced here: 98.7 us
  starting transfers between devices  38.9 us (39%)
  blocking collectives  27.2 us (27%)
  waiting for transfers between devices  24.8 us (25%)
  local copies, waits for them, and re-layouts  3.3 us (3%)
  matrix products  1.98 us (2%)
  other arithmetic  1.22 us (1%)
  between operations  1.22 us (1%)
    ppermute x10, starting transfers between devices, swapped(): arrived = lax.ppermute(jnp.where(lower, high, low), AXIS, pairs)  24.4 us
    all_to_all x1, blocking collectives, summed_everywhere(): dealt = lax.all_to_all(padded.reshape(n, per, columns), AXIS, 0, 0)  15.8 us
    ppermute x3, waiting for transfers between devices, down(): return lax.ppermute(value, AXIS, pairs)  15.2 us
    all_to_all x1, blocking collectives, summed_everywhere(): lax.all_to_all(jnp.broadcast_to(mine[None], (n, per, columns)), AXIS, 0, 0)  11.4 us
    ppermute x3, starting transfers between devices, up(): return lax.ppermute(value, AXIS, pairs)  10.6 us
    ppermute x10, waiting for transfers between devices, swapped(): arrived = lax.ppermute(jnp.where(lower, high, low), AXIS, pairs)  6.96 us
    ppermute x3, starting transfers between devices, down(): return lax.ppermute(value, AXIS, pairs)  3.88 us
    ppermute x3, waiting for transfers between devices, up(): return lax.ppermute(value, AXIS, pairs)  2.7 us
  transfers between devices with their start and end apart: 16, of which 12 were waited for; matrix products, arithmetic and copies ran while one was open for 1% of the time, Pallas kernels for 0%

profile of v1, /device:TPU:0, one launch (start us, length us, event | category | flops | bytes accessed | tf_op | source)
XLA Modules:
  0.0 98.7 jit_solution(11086867415722206861)
XLA Ops:
  0.7 0.9 reshape.98
  1.6 5.9 %collective-permute-start = (bf16[1,7,7,128]{3,2,1,0:T(8,128)(2,1)S(1)}, bf16[1,7,7,128]{3,2,1,0:T(8,128)(2,1)S(1)}, u32[]{:S(2)}, u32[]{:S(2)}) collective-permute-start(bf16[1,7,7,128]{3,2,1,0:T(8,128)(2,1)S(1)} %pad_slice_fusion.9), channel_id=1, source_target_pairs={{0,16},{1,17},{2,18},{3,19},{4,20},{5,21},{6,22},{7,23},{8,24},{9,... | collective-permute-start | bytes 37640 | tf_op jit(solution)/shard_map/ppermute | solution.py:35
  7.6 1.3 %collective-permute-done = bf16[1,7,7,128]{3,2,1,0:T(8,128)(2,1)S(1)} collective-permute-done((bf16[1,7,7,128]{3,2,1,0:T(8,128)(2,1)S(1)}, bf16[1,7,7,128]{3,2,1,0:T(8,128)(2,1)S(1)}, u32[]{:S(2)}, u32[]{:S(2)}) %collective-permute-start) | collective-permute-done | bytes 12576 | tf_op jit(solution)/shard_map/ppermute | solution.py:35
  8.9 3.4 %collective-permute-start.1 = (bf16[7,1,7,128]{3,2,1,0:T(8,128)(2,1)S(1)}, bf16[7,1,7,128]{3,2,1,0:T(8,128)(2,1)S(1)}, u32[]{:S(2)}, u32[]{:S(2)}) collective-permute-start(bf16[7,1,7,128]{3,2,1,0:T(8,128)(2,1)S(1)} %pad_maximum_fusion.10), channel_id=1, source_target_pairs={{0,4},{1,5},{2,6},{3,7},{4,8},{5,9},{6,10},{7,11},{8,12},{9,13},{1... | collective-permute-start | bytes 37640 | tf_op jit(solution)/shard_map/ppermute | solution.py:35
  12.4 0.7 convolution_convert_fusion
  13.1 0.6 collective-permute-done.1
  13.8 1.3 %collective-permute-start.2 = (bf16[7,7,1,128]{3,2,1,0:T(2,128)(2,1)S(1)}, bf16[7,7,1,128]{3,2,1,0:T(2,128)(2,1)S(1)}, u32[]{:S(2)}, u32[]{:S(2)}) collective-permute-start(bf16[7,7,1,128]{3,2,1,0:T(2,128)(2,1)S(1)} %slice.183), channel_id=1, source_target_pairs={{0,1},{1,2},{2,3},{4,5},{5,6},{6,7},{8,9},{9,10},{10,11},{12,13},{... | collective-permute-start | bytes 37640 | tf_op jit(solution)/shard_map/ppermute | solution.py:35
  15.2 0.7 collective-permute-done.2
  16.1 0.6 copy-done.2
  17.1 2.4 %collective-permute-start.3 = (bf16[7,7,1,128]{3,2,1,0:T(2,128)(2,1)S(1)}, bf16[7,7,1,128]{3,2,1,0:T(2,128)(2,1)S(1)}, u32[]{:S(2)}, u32[]{:S(2)}) collective-permute-start(bf16[7,7,1,128]{3,2,1,0:T(2,128)(2,1)S(1)} %get-tuple-element.34), channel_id=1, source_target_pairs={{0,1},{1,0},{2,3},{3,2},{4,5},{5,4},{6,7},{7,6},{8,9},{9,8},{10,11... | collective-permute-start | bytes 37640 | tf_op jit(solution)/shard_map/ppermute | solution.py:52
  19.4 0.7 collective-permute-start.4
  20.4 0.7 collective-permute-start.6
  21.1 6.0 %collective-permute-start.5 = (bf16[7,1,7,128]{3,2,1,0:T(8,128)(2,1)S(1)}, bf16[7,1,7,128]{3,2,1,0:T(8,128)(2,1)S(1)}, u32[]{:S(2)}, u32[]{:S(2)}) collective-permute-start(bf16[7,1,7,128]{3,2,1,0:T(8,128)(2,1)S(1)} %get-tuple-element.17), channel_id=1, source_target_pairs={{0,4},{4,0},{1,5},{5,1},{2,6},{6,2},{3,7},{7,3},{8,12},{12,8},{9,1... | collective-permute-start | bytes 37640 | tf_op jit(solution)/shard_map/ppermute | solution.py:52
  27.1 1.7 %collective-permute-done.5 = bf16[7,1,7,128]{3,2,1,0:T(8,128)(2,1)S(1)} collective-permute-done((bf16[7,1,7,128]{3,2,1,0:T(8,128)(2,1)S(1)}, bf16[7,1,7,128]{3,2,1,0:T(8,128)(2,1)S(1)}, u32[]{:S(2)}, u32[]{:S(2)}) %collective-permute-start.5) | collective-permute-done | bytes 12576 | tf_op jit(solution)/shard_map/ppermute | solution.py:52
  28.9 3.3 %collective-permute-start.7 = (bf16[1,7,7,128]{3,2,1,0:T(8,128)(2,1)S(1)}, bf16[1,7,7,128]{3,2,1,0:T(8,128)(2,1)S(1)}, u32[]{:S(2)}, u32[]{:S(2)}) collective-permute-start(bf16[1,7,7,128]{3,2,1,0:T(8,128)(2,1)S(1)} %fusion.69), channel_id=1, source_target_pairs={{0,16},{16,0},{1,17},{17,1},{2,18},{18,2},{3,19},{19,3},{4,20},{20... | collective-permute-start | bytes 37640 | tf_op jit(solution)/shard_map/ppermute | solution.py:52
  32.5 1.5 %collective-permute-done.7 = bf16[1,7,7,128]{3,2,1,0:T(8,128)(2,1)S(1)} collective-permute-done((bf16[1,7,7,128]{3,2,1,0:T(8,128)(2,1)S(1)}, bf16[1,7,7,128]{3,2,1,0:T(8,128)(2,1)S(1)}, u32[]{:S(2)}, u32[]{:S(2)}) %collective-permute-start.7) | collective-permute-done | bytes 12576 | tf_op jit(solution)/shard_map/ppermute | solution.py:52
  34.4 2.9 %collective-permute-start.8 = (bf16[7,7,1,128]{3,2,1,0:T(2,128)(2,1)S(1)}, bf16[7,7,1,128]{3,2,1,0:T(2,128)(2,1)S(1)}, u32[]{:S(2)}, u32[]{:S(2)}) collective-permute-start(bf16[7,7,1,128]{3,2,1,0:T(2,128)(2,1)S(1)} %get-tuple-element.32), channel_id=1, source_target_pairs={{0,1},{1,0},{2,3},{3,2},{4,5},{5,4},{6,7},{7,6},{8,9},{9,8},{10,11... | collective-permute-start | bytes 37640 | tf_op jit(solution)/shard_map/ppermute | solution.py:52
  37.3 0.7 collective-permute-start.9
  38.3 0.7 collective-permute-start.11
  39.0 4.3 %collective-permute-start.10 = (bf16[7,1,7,128]{3,2,1,0:T(8,128)(2,1)S(1)}, bf16[7,1,7,128]{3,2,1,0:T(8,128)(2,1)S(1)}, u32[]{:S(2)}, u32[]{:S(2)}) collective-permute-start(bf16[7,1,7,128]{3,2,1,0:T(8,128)(2,1)S(1)} %get-tuple-element.14), channel_id=1, source_target_pairs={{0,4},{4,0},{1,5},{5,1},{2,6},{6,2},{3,7},{7,3},{8,12},{12,8},{9,1... | collective-permute-start | bytes 37640 | tf_op jit(solution)/shard_map/ppermute | solution.py:52
  43.3 1.7 %collective-permute-done.10 = bf16[7,1,7,128]{3,2,1,0:T(8,128)(2,1)S(1)} collective-permute-done((bf16[7,1,7,128]{3,2,1,0:T(8,128)(2,1)S(1)}, bf16[7,1,7,128]{3,2,1,0:T(8,128)(2,1)S(1)}, u32[]{:S(2)}, u32[]{:S(2)}) %collective-permute-start.10) | collective-permute-done | bytes 12576 | tf_op jit(solution)/shard_map/ppermute | solution.py:52
  45.1 2.8 %collective-permute-start.12 = (bf16[1,7,7,128]{3,2,1,0:T(8,128)(2,1)S(1)}, bf16[1,7,7,128]{3,2,1,0:T(8,128)(2,1)S(1)}, u32[]{:S(2)}, u32[]{:S(2)}) collective-permute-start(bf16[1,7,7,128]{3,2,1,0:T(8,128)(2,1)S(1)} %fusion.70), channel_id=1, source_target_pairs={{0,16},{16,0},{1,17},{17,1},{2,18},{18,2},{3,19},{19,3},{4,20},{20... | collective-permute-start | bytes 37640 | tf_op jit(solution)/shard_map/ppermute | solution.py:52
  47.9 1.8 %collective-permute-done.12 = bf16[1,7,7,128]{3,2,1,0:T(8,128)(2,1)S(1)} collective-permute-done((bf16[1,7,7,128]{3,2,1,0:T(8,128)(2,1)S(1)}, bf16[1,7,7,128]{3,2,1,0:T(8,128)(2,1)S(1)}, u32[]{:S(2)}, u32[]{:S(2)}) %collective-permute-start.12) | collective-permute-done | bytes 12576 | tf_op jit(solution)/shard_map/ppermute | solution.py:52
  50.4 1.3 %collective-permute-start.13 = (bf16[7,7,1,128]{3,2,1,0:T(2,128)(2,1)S(1)}, bf16[7,7,1,128]{3,2,1,0:T(2,128)(2,1)S(1)}, u32[]{:S(2)}, u32[]{:S(2)}) collective-permute-start(bf16[7,7,1,128]{3,2,1,0:T(2,128)(2,1)S(1)} %slice.281), channel_id=1, source_target_pairs={{1,0},{2,1},{3,2},{5,4},{6,5},{7,6},{9,8},{10,9},{11,10},{13,12},{... | collective-permute-start | bytes 37640 | tf_op jit(solution)/shard_map/ppermute | solution.py:42
  51.8 5.7 %collective-permute-done.13 = bf16[7,7,1,128]{3,2,1,0:T(2,128)(2,1)S(1)} collective-permute-done((bf16[7,7,1,128]{3,2,1,0:T(2,128)(2,1)S(1)}, bf16[7,7,1,128]{3,2,1,0:T(2,128)(2,1)S(1)}, u32[]{:S(2)}, u32[]{:S(2)}) %collective-permute-start.13) | collective-permute-done | bytes 12576 | tf_op jit(solution)/shard_map/ppermute | solution.py:42
  57.6 1.3 %collective-permute-start.14 = (bf16[7,1,7,128]{3,2,1,0:T(8,128)(2,1)S(1)}, bf16[7,1,7,128]{3,2,1,0:T(8,128)(2,1)S(1)}, u32[]{:S(2)}, u32[]{:S(2)}) collective-permute-start(bf16[7,1,7,128]{3,2,1,0:T(8,128)(2,1)S(1)} %fusion.52), channel_id=1, source_target_pairs={{4,0},{5,1},{6,2},{7,3},{8,4},{9,5},{10,6},{11,7},{12,8},{13,9},{1... | collective-permute-start | bytes 37640 | tf_op jit(solution)/shard_map/ppermute | solution.py:42
  58.9 4.3 %collective-permute-done.14 = bf16[7,1,7,128]{3,2,1,0:T(8,128)(2,1)S(1)} collective-permute-done((bf16[7,1,7,128]{3,2,1,0:T(8,128)(2,1)S(1)}, bf16[7,1,7,128]{3,2,1,0:T(8,128)(2,1)S(1)}, u32[]{:S(2)}, u32[]{:S(2)}) %collective-permute-start.14) | collective-permute-done | bytes 12576 | tf_op jit(solution)/shard_map/ppermute | solution.py:42
  63.2 1.3 %collective-permute-start.15 = (bf16[1,7,7,128]{3,2,1,0:T(8,128)(2,1)S(1)}, bf16[1,7,7,128]{3,2,1,0:T(8,128)(2,1)S(1)}, u32[]{:S(2)}, u32[]{:S(2)}) collective-permute-start(bf16[1,7,7,128]{3,2,1,0:T(8,128)(2,1)S(1)} %fusion.51), channel_id=1, source_target_pairs={{16,0},{17,1},{18,2},{19,3},{20,4},{21,5},{22,6},{23,7},{24,8},{25... | collective-permute-start | bytes 37640 | tf_op jit(solution)/shard_map/ppermute | solution.py:42
  64.5 5.2 %collective-permute-done.15 = bf16[1,7,7,128]{3,2,1,0:T(8,128)(2,1)S(1)} collective-permute-done((bf16[1,7,7,128]{3,2,1,0:T(8,128)(2,1)S(1)}, bf16[1,7,7,128]{3,2,1,0:T(8,128)(2,1)S(1)}, u32[]{:S(2)}, u32[]{:S(2)}) %collective-permute-start.15) | collective-permute-done | bytes 12576 | tf_op jit(solution)/shard_map/ppermute | solution.py:42
  70.6 15.8 %all_to_all.10 = bf16[32,22,128]{2,1,0:T(8,128)(2,1)S(1)} all-to-all(bf16[32,22,128]{2,1,0:T(8,128)(2,1)S(1)} %reshape.104), channel_id=1, replica_groups=mesh['cells'=32] {'cells'}, dimensions={0} | all-to-all | bytes 360448 | tf_op jit(solution)/shard_map/all_to_all | solution.py:90
  86.5 11.4 %all_to_all.11 = bf16[32,22,128]{2,1,0:T(8,128)(2,1)S(1)} all-to-all(bf16[32,22,128]{2,1,0:T(8,128)(2,1)S(1)} %broadcast_in_dim.31), channel_id=1, replica_groups=mesh['cells'=32] {'cells'}, dimensions={0} | all-to-all | bytes 360448 | tf_op jit(solution)/shard_map/all_to_all | solution.py:92
  97.9 0.8 reshape.105
  (74 shorter events, 3.8 us)
Async XLA Ops:
  0.6 69.2 %copy-start = (bf16[216,704]{1,0:T(8,128)(2,1)S(1)}, bf16[216,704]{1,0:T(8,128)(2,1)}, u32[]{:S(2)}) copy-start(bf16[216,704]{1,0:T(8,128)(2,1)} %param.11) | copy-start | bytes 912388
  0.6 11.7 %copy-start.4 = (bf16[1,343,343]{2,1,0:T(8,128)(2,1)S(1)}, bf16[1,343,343]{2,1,0:T(8,128)(2,1)}, u32[]{:S(2)}) copy-start(bf16[1,343,343]{2,1,0:T(8,128)(2,1)} %param.8) | copy-start | bytes 705898
  1.6 6.0 %copy-start.3 = (s32[1,343]{1,0:T(1,128)S(1)}, s32[1,343]{1,0:T(1,128)}, u32[]{:S(2)}) copy-start(s32[1,343]{1,0:T(1,128)} %param.9) | copy-start | bytes 4120
  1.6 7.4 %collective-permute-start = (bf16[1,7,7,128]{3,2,1,0:T(8,128)(2,1)S(1)}, bf16[1,7,7,128]{3,2,1,0:T(8,128)(2,1)S(1)}, u32[]{:S(2)}, u32[]{:S(2)}) collective-permute-start(bf16[1,7,7,128]{3,2,1,0:T(8,128)(2,1)S(1)} %pad_slice_fusion.9), channel_id=1, source_target_pairs={{0,16},{1,17},{2,18},{3,19},{4,20},{5,21},{6,22},{7,23},{8,24},{9,... | collective-permute-start | bytes 37640 | tf_op jit(solution)/shard_map/ppermute | solution.py:35
  8.9 4.8 %collective-permute-start.1 = (bf16[7,1,7,128]{3,2,1,0:T(8,128)(2,1)S(1)}, bf16[7,1,7,128]{3,2,1,0:T(8,128)(2,1)S(1)}, u32[]{:S(2)}, u32[]{:S(2)}) collective-permute-start(bf16[7,1,7,128]{3,2,1,0:T(8,128)(2,1)S(1)} %pad_maximum_fusion.10), channel_id=1, source_target_pairs={{0,4},{1,5},{2,6},{3,7},{4,8},{5,9},{6,10},{7,11},{8,12},{9,13},{1... | collective-permute-start | bytes 37640 | tf_op jit(solution)/shard_map/ppermute | solution.py:35
  13.8 2.1 %collective-permute-start.2 = (bf16[7,7,1,128]{3,2,1,0:T(2,128)(2,1)S(1)}, bf16[7,7,1,128]{3,2,1,0:T(2,128)(2,1)S(1)}, u32[]{:S(2)}, u32[]{:S(2)}) collective-permute-start(bf16[7,7,1,128]{3,2,1,0:T(2,128)(2,1)S(1)} %slice.183), channel_id=1, source_target_pairs={{0,1},{1,2},{2,3},{4,5},{5,6},{6,7},{8,9},{9,10},{10,11},{12,13},{... | collective-permute-start | bytes 37640 | tf_op jit(solution)/shard_map/ppermute | solution.py:35
  16.0 0.7 copy-start.2
  17.1 3.2 %collective-permute-start.3 = (bf16[7,7,1,128]{3,2,1,0:T(2,128)(2,1)S(1)}, bf16[7,7,1,128]{3,2,1,0:T(2,128)(2,1)S(1)}, u32[]{:S(2)}, u32[]{:S(2)}) collective-permute-start(bf16[7,7,1,128]{3,2,1,0:T(2,128)(2,1)S(1)} %get-tuple-element.34), channel_id=1, source_target_pairs={{0,1},{1,0},{2,3},{3,2},{4,5},{5,4},{6,7},{7,6},{8,9},{9,8},{10,11... | collective-permute-start | bytes 37640 | tf_op jit(solution)/shard_map/ppermute | solution.py:52
  19.4 0.9 collective-permute-start.4
  20.4 6.7 %collective-permute-start.6 = (bf16[7,1,7,128]{3,2,1,0:T(8,128)(2,1)S(1)}, bf16[7,1,7,128]{3,2,1,0:T(8,128)(2,1)S(1)}, u32[]{:S(2)}, u32[]{:S(2)}) collective-permute-start(bf16[7,1,7,128]{3,2,1,0:T(8,128)(2,1)S(1)} %broadcast_select_fusion.13), channel_id=1, source_target_pairs={{4,8},{8,4},{5,9},{9,5},{6,10},{10,6},{7,11},{11,7},{20,24},{24,20... | collective-permute-start | bytes 37640 | tf_op jit(solution)/shard_map/ppermute | solution.py:52
  21.1 7.7 %collective-permute-start.5 = (bf16[7,1,7,128]{3,2,1,0:T(8,128)(2,1)S(1)}, bf16[7,1,7,128]{3,2,1,0:T(8,128)(2,1)S(1)}, u32[]{:S(2)}, u32[]{:S(2)}) collective-permute-start(bf16[7,1,7,128]{3,2,1,0:T(8,128)(2,1)S(1)} %get-tuple-element.17), channel_id=1, source_target_pairs={{0,4},{4,0},{1,5},{5,1},{2,6},{6,2},{3,7},{7,3},{8,12},{12,8},{9,1... | collective-permute-start | bytes 37640 | tf_op jit(solution)/shard_map/ppermute | solution.py:52
  28.9 5.0 %collective-permute-start.7 = (bf16[1,7,7,128]{3,2,1,0:T(8,128)(2,1)S(1)}, bf16[1,7,7,128]{3,2,1,0:T(8,128)(2,1)S(1)}, u32[]{:S(2)}, u32[]{:S(2)}) collective-permute-start(bf16[1,7,7,128]{3,2,1,0:T(8,128)(2,1)S(1)} %fusion.69), channel_id=1, source_target_pairs={{0,16},{16,0},{1,17},{17,1},{2,18},{18,2},{3,19},{19,3},{4,20},{20... | collective-permute-start | bytes 37640 | tf_op jit(solution)/shard_map/ppermute | solution.py:52
  34.4 3.8 %collective-permute-start.8 = (bf16[7,7,1,128]{3,2,1,0:T(2,128)(2,1)S(1)}, bf16[7,7,1,128]{3,2,1,0:T(2,128)(2,1)S(1)}, u32[]{:S(2)}, u32[]{:S(2)}) collective-permute-start(bf16[7,7,1,128]{3,2,1,0:T(2,128)(2,1)S(1)} %get-tuple-element.32), channel_id=1, source_target_pairs={{0,1},{1,0},{2,3},{3,2},{4,5},{5,4},{6,7},{7,6},{8,9},{9,8},{10,11... | collective-permute-start | bytes 37640 | tf_op jit(solution)/shard_map/ppermute | solution.py:52
  37.3 0.9 collective-permute-start.9
  38.3 4.9 %collective-permute-start.11 = (bf16[7,1,7,128]{3,2,1,0:T(8,128)(2,1)S(1)}, bf16[7,1,7,128]{3,2,1,0:T(8,128)(2,1)S(1)}, u32[]{:S(2)}, u32[]{:S(2)}) collective-permute-start(bf16[7,1,7,128]{3,2,1,0:T(8,128)(2,1)S(1)} %broadcast_select_fusion.12), channel_id=1, source_target_pairs={{4,8},{8,4},{5,9},{9,5},{6,10},{10,6},{7,11},{11,7},{20,24},{24,20... | collective-permute-start | bytes 37640 | tf_op jit(solution)/shard_map/ppermute | solution.py:52
  39.0 6.0 %collective-permute-start.10 = (bf16[7,1,7,128]{3,2,1,0:T(8,128)(2,1)S(1)}, bf16[7,1,7,128]{3,2,1,0:T(8,128)(2,1)S(1)}, u32[]{:S(2)}, u32[]{:S(2)}) collective-permute-start(bf16[7,1,7,128]{3,2,1,0:T(8,128)(2,1)S(1)} %get-tuple-element.14), channel_id=1, source_target_pairs={{0,4},{4,0},{1,5},{5,1},{2,6},{6,2},{3,7},{7,3},{8,12},{12,8},{9,1... | collective-permute-start | bytes 37640 | tf_op jit(solution)/shard_map/ppermute | solution.py:52
  45.1 4.7 %collective-permute-start.12 = (bf16[1,7,7,128]{3,2,1,0:T(8,128)(2,1)S(1)}, bf16[1,7,7,128]{3,2,1,0:T(8,128)(2,1)S(1)}, u32[]{:S(2)}, u32[]{:S(2)}) collective-permute-start(bf16[1,7,7,128]{3,2,1,0:T(8,128)(2,1)S(1)} %fusion.70), channel_id=1, source_target_pairs={{0,16},{16,0},{1,17},{17,1},{2,18},{18,2},{3,19},{19,3},{4,20},{20... | collective-permute-start | bytes 37640 | tf_op jit(solution)/shard_map/ppermute | solution.py:52
  50.4 7.1 %collective-permute-start.13 = (bf16[7,7,1,128]{3,2,1,0:T(2,128)(2,1)S(1)}, bf16[7,7,1,128]{3,2,1,0:T(2,128)(2,1)S(1)}, u32[]{:S(2)}, u32[]{:S(2)}) collective-permute-start(bf16[7,7,1,128]{3,2,1,0:T(2,128)(2,1)S(1)} %slice.281), channel_id=1, source_target_pairs={{1,0},{2,1},{3,2},{5,4},{6,5},{7,6},{9,8},{10,9},{11,10},{13,12},{... | collective-permute-start | bytes 37640 | tf_op jit(solution)/shard_map/ppermute | solution.py:42
  57.6 5.6 %collective-permute-start.14 = (bf16[7,1,7,128]{3,2,1,0:T(8,128)(2,1)S(1)}, bf16[7,1,7,128]{3,2,1,0:T(8,128)(2,1)S(1)}, u32[]{:S(2)}, u32[]{:S(2)}) collective-permute-start(bf16[7,1,7,128]{3,2,1,0:T(8,128)(2,1)S(1)} %fusion.52), channel_id=1, source_target_pairs={{4,0},{5,1},{6,2},{7,3},{8,4},{9,5},{10,6},{11,7},{12,8},{13,9},{1... | collective-permute-start | bytes 37640 | tf_op jit(solution)/shard_map/ppermute | solution.py:42
  63.2 6.5 %collective-permute-start.15 = (bf16[1,7,7,128]{3,2,1,0:T(8,128)(2,1)S(1)}, bf16[1,7,7,128]{3,2,1,0:T(8,128)(2,1)S(1)}, u32[]{:S(2)}, u32[]{:S(2)}) collective-permute-start(bf16[1,7,7,128]{3,2,1,0:T(8,128)(2,1)S(1)} %fusion.51), channel_id=1, source_target_pairs={{16,0},{17,1},{18,2},{19,3},{20,4},{21,5},{22,6},{23,7},{24,8},{25... | collective-permute-start | bytes 37640 | tf_op jit(solution)/shard_map/ppermute | solution.py:42
  69.9 0.6 copy-start.1

commit v2 on v1

--- a/solution.py
+++ b/solution.py
@@ -25,22 +25,6 @@
     def coord_of(self, device, dim):
         return device // self.stride[dim] % self.counts[dim]
 
-    def up(self, value, dim):
-        by = self.stride[dim]
-        pairs = [
-            (i, i + by)
-            for i in range(self.devices)
-            if self.coord_of(i, dim) + 1 < self.counts[dim]
-        ]
-        return lax.ppermute(value, AXIS, pairs)
-
-    def down(self, value, dim):
-        by = self.stride[dim]
-        pairs = [
-            (i, i - by) for i in range(self.devices) if self.coord_of(i, dim) > 0
-        ]
-        return lax.ppermute(value, AXIS, pairs)
-
     def swapped(self, low, high, dim, odd):
         by = self.stride[dim]
         pairs = []
@@ -52,6 +36,13 @@
         arrived = lax.ppermute(jnp.where(lower, high, low), AXIS, pairs)
         zero = jnp.zeros_like(arrived)
         return jnp.where(lower, zero, arrived), jnp.where(lower, arrived, zero)
+
+    def exchanged(self, low, high, dim):
+        to_low, to_high = self.swapped(low, high, dim, 0)
+        if self.counts[dim] > 2:
+            more_low, more_high = self.swapped(low, high, dim, 1)
+            to_low, to_high = to_low + more_low, to_high + more_high
+        return to_low, to_high
 
 
 def plane(field, dim, at):
@@ -84,13 +75,24 @@
 
 def summed_everywhere(value):
     n = lax.axis_size(AXIS)
+    groups = [list(range(first, n, 2)) for first in range(2)]
+    second = lax.axis_index(AXIS) % 2 == 1
+    partner = [(i, i ^ 1) for i in range(n)]
     rows, columns = value.shape
     per = -(-rows // n)
-    padded = jnp.pad(value.astype(jnp.bfloat16), ((0, n * per - rows), (0, 0)))
-    dealt = lax.all_to_all(padded.reshape(n, per, columns), AXIS, 0, 0)
+    halves = jnp.pad(value, ((0, n * per - rows), (0, 0))).reshape(2, n * per // 2, columns)
+    away = jnp.where(second, halves[0], halves[1]).astype(jnp.bfloat16)
+    arrived = lax.ppermute(away, AXIS, partner)
+    kept = jnp.where(second, halves[1], halves[0]) + arrived.astype(jnp.float32)
+    parts = kept.astype(jnp.bfloat16).reshape(n // 2, per, columns)
+    dealt = lax.all_to_all(parts, AXIS, 0, 0, axis_index_groups=groups)
     mine = jnp.sum(dealt.astype(jnp.float32), axis=0).astype(jnp.bfloat16)
-    back = lax.all_to_all(jnp.broadcast_to(mine[None], (n, per, columns)), AXIS, 0, 0)
-    return back.reshape(n * per, columns)[:rows].astype(jnp.float32)
+    back = lax.all_to_all(
+        jnp.broadcast_to(mine[None], parts.shape), AXIS, 0, 0, axis_index_groups=groups
+    ).reshape(n * per // 2, columns)
+    other = lax.ppermute(back, AXIS, partner)
+    both = jnp.concatenate([jnp.where(second, other, back), jnp.where(second, back, other)])
+    return both[:rows].astype(jnp.float32)
 
 
 def per_device(block, cell_matrix, connectivity, potential, locked):
@@ -108,7 +110,8 @@
         .set(block.reshape(edge, edge, edge, columns))
     )
     for dim in range(3):
-        field = with_ends(field, dim, grid.up(plane(field, dim, SIDE - 1), dim), None)
+        high = plane(field, dim, SIDE - 1)
+        field = with_ends(field, dim, grid.exchanged(high, high, dim)[0], None)
 
     inside = jnp.ones((SIDE, SIDE, SIDE, 1), jnp.bool_)
     for dim in range(3):
@@ -124,17 +127,15 @@
         partial = (partial + lumped * rows.astype(jnp.float32)).reshape(shape)
         for dim in (2, 1, 0):
             low, high = plane(partial, dim, 0), plane(partial, dim, SIDE - 1)
-            if step < steps - 1:
-                low16, high16 = low.astype(jnp.bfloat16), high.astype(jnp.bfloat16)
-                for odd in (0, 1):
-                    if grid.counts[dim] > odd + 1:
-                        to_low, to_high = grid.swapped(low16, high16, dim, odd)
-                        low = low + to_low.astype(jnp.float32)
-                        high = high + to_high.astype(jnp.float32)
-                partial = with_ends(partial, dim, low, high)
-            else:
-                arrived = grid.down(low.astype(jnp.bfloat16), dim)
-                partial = with_ends(partial, dim, None, high + arrived.astype(jnp.float32))
+            to_low, to_high = grid.exchanged(
+                low.astype(jnp.bfloat16), high.astype(jnp.bfloat16), dim
+            )
+            partial = with_ends(
+                partial,
+                dim,
+                None if step == steps - 1 else low + to_low.astype(jnp.float32),
+                high + to_high.astype(jnp.float32),
+            )
         following = coeffs[0] * (partial - centre * current.astype(jnp.float32)) - coeffs[
             1
         ] * older.astype(jnp.float32)

time: 99.2 us -> 104 us (1.048)
  starting transfers between devices: 38.9 us -> 53.1 us
  waiting for transfers between devices: 24.8 us -> 15.1 us
    ppermute x10 -> x20, starting transfers between devices: 24.4 us -> 48.4 us  [swapped(): arrived = lax.ppermute(jnp.where(lower, high, low), AXIS, pairs)]
    ppermute x6 -> x2, waiting for transfers between devices: 17.9 us -> 2.21 us  [the longest x1 1.28 us: summed_everywhere(): other = lax.ppermute(back, AXIS, partner)]
    ppermute x6 -> x2, starting transfers between devices: 14.5 us -> 4.72 us  [the longest x1 4.65 us: summed_everywhere(): arrived = lax.ppermute(away, AXIS, partner)]
    ppermute x10 -> x20, waiting for transfers between devices: 6.96 us -> 12.9 us  [swapped(): arrived = lax.ppermute(jnp.where(lower, high, low), AXIS, pairs)]
  transfers between devices with their start and end apart: 16 -> 22, of which waited for: 12 -> 14; matrix products, arithmetic and copies ran while one was open for 1% -> 1% of each run, Pallas kernels for 0% -> 0%
where the time goes in v2:
time: 104 us; the launch traced here: 103 us
  starting transfers between devices  53.1 us (51%)
  blocking collectives  26.6 us (26%)
  waiting for transfers between devices  15.1 us (15%)
  local copies, waits for them, and re-layouts  3.15 us (3%)
  other arithmetic  2.2 us (2%)
  matrix products  1.98 us (2%)
  between operations  1.29 us (1%)
    ppermute x20, starting transfers between devices, swapped(): arrived = lax.ppermute(jnp.where(lower, high, low), AXIS, pairs)  48.4 us
    all_to_all x1, blocking collectives, summed_everywhere(): dealt = lax.all_to_all(parts, AXIS, 0, 0, axis_index_groups=groups)  16.4 us
    ppermute x20, waiting for transfers between devices, swapped(): arrived = lax.ppermute(jnp.where(lower, high, low), AXIS, pairs)  12.9 us
    all_to_all x1, blocking collectives, summed_everywhere(): lax.all_to_all(jnp.broadcast_to(mine[None], parts.shape), AXIS, 0, 0, axi...  10.3 us
    ppermute x1, starting transfers between devices, summed_everywhere(): arrived = lax.ppermute(away, AXIS, partner)  4.65 us
  transfers between devices with their start and end apart: 22, of which 14 were waited for; matrix products, arithmetic and copies ran while one was open for 1% of the time, Pallas kernels for 0%

profile of v2, /device:TPU:0, one launch (start us, length us, event | category | flops | bytes accessed | tf_op | source)
XLA Modules:
  0.0 103.4 jit_solution(6294895565429517996)
XLA Ops:
  0.6 0.9 reshape.103
  1.6 4.1 %collective-permute-start = (bf16[1,7,7,128]{3,2,1,0:T(8,128)(2,1)S(1)}, bf16[1,7,7,128]{3,2,1,0:T(8,128)(2,1)S(1)}, u32[]{:S(2)}, u32[]{:S(2)}) collective-permute-start(bf16[1,7,7,128]{3,2,1,0:T(8,128)(2,1)S(1)} %pad_slice_fusion.9), channel_id=1, source_target_pairs={{0,16},{16,0},{1,17},{17,1},{2,18},{18,2},{3,19},{19,3},{4,20},{20... | collective-permute-start | bytes 37640 | tf_op jit(solution)/shard_map/ppermute | solution.py:36
  5.8 0.7 copy-done.3
  6.4 0.9 collective-permute-done
  7.4 1.9 %collective-permute-start.1 = (bf16[7,1,7,128]{3,2,1,0:T(8,128)(2,1)S(1)}, bf16[7,1,7,128]{3,2,1,0:T(8,128)(2,1)S(1)}, u32[]{:S(2)}, u32[]{:S(2)}) collective-permute-start(bf16[7,1,7,128]{3,2,1,0:T(8,128)(2,1)S(1)} %pad_maximum_fusion.10), channel_id=1, source_target_pairs={{0,4},{4,0},{1,5},{5,1},{2,6},{6,2},{3,7},{7,3},{8,12},{12,8},{9,1... | collective-permute-start | bytes 37640 | tf_op jit(solution)/shard_map/ppermute | solution.py:36
  10.0 0.7 convolution_convert_fusion
  11.3 0.7 collective-permute-start.4
  13.7 4.5 %collective-permute-start.5 = (bf16[7,7,1,128]{3,2,1,0:T(2,128)(2,1)S(1)}, bf16[7,7,1,128]{3,2,1,0:T(2,128)(2,1)S(1)}, u32[]{:S(2)}, u32[]{:S(2)}) collective-permute-start(bf16[7,7,1,128]{3,2,1,0:T(2,128)(2,1)S(1)} %get-tuple-element.38), channel_id=1, source_target_pairs={{0,1},{1,0},{2,3},{3,2},{4,5},{5,4},{6,7},{7,6},{8,9},{9,8},{10,11... | collective-permute-start | bytes 37640 | tf_op jit(solution)/shard_map/ppermute | solution.py:36
  18.2 0.7 collective-permute-start.6
  19.2 0.7 collective-permute-start.8
  19.8 9.0 %collective-permute-start.7 = (bf16[7,1,7,128]{3,2,1,0:T(8,128)(2,1)S(1)}, bf16[7,1,7,128]{3,2,1,0:T(8,128)(2,1)S(1)}, u32[]{:S(2)}, u32[]{:S(2)}) collective-permute-start(bf16[7,1,7,128]{3,2,1,0:T(8,128)(2,1)S(1)} %get-tuple-element.19), channel_id=1, source_target_pairs={{0,4},{4,0},{1,5},{5,1},{2,6},{6,2},{3,7},{7,3},{8,12},{12,8},{9,1... | collective-permute-start | bytes 37640 | tf_op jit(solution)/shard_map/ppermute | solution.py:36
  28.8 1.7 %collective-permute-done.7 = bf16[7,1,7,128]{3,2,1,0:T(8,128)(2,1)S(1)} collective-permute-done((bf16[7,1,7,128]{3,2,1,0:T(8,128)(2,1)S(1)}, bf16[7,1,7,128]{3,2,1,0:T(8,128)(2,1)S(1)}, u32[]{:S(2)}, u32[]{:S(2)}) %collective-permute-start.7) | collective-permute-done | bytes 12576 | tf_op jit(solution)/shard_map/ppermute | solution.py:36
  30.6 2.7 %collective-permute-start.9 = (bf16[1,7,7,128]{3,2,1,0:T(8,128)(2,1)S(1)}, bf16[1,7,7,128]{3,2,1,0:T(8,128)(2,1)S(1)}, u32[]{:S(2)}, u32[]{:S(2)}) collective-permute-start(bf16[1,7,7,128]{3,2,1,0:T(8,128)(2,1)S(1)} %fusion.66), channel_id=1, source_target_pairs={{0,16},{16,0},{1,17},{17,1},{2,18},{18,2},{3,19},{19,3},{4,20},{20... | collective-permute-start | bytes 37640 | tf_op jit(solution)/shard_map/ppermute | solution.py:36
  33.5 1.8 %collective-permute-done.9 = bf16[1,7,7,128]{3,2,1,0:T(8,128)(2,1)S(1)} collective-permute-done((bf16[1,7,7,128]{3,2,1,0:T(8,128)(2,1)S(1)}, bf16[1,7,7,128]{3,2,1,0:T(8,128)(2,1)S(1)}, u32[]{:S(2)}, u32[]{:S(2)}) %collective-permute-start.9) | collective-permute-done | bytes 12576 | tf_op jit(solution)/shard_map/ppermute | solution.py:36
  35.8 2.1 %collective-permute-start.10 = (bf16[7,7,1,128]{3,2,1,0:T(2,128)(2,1)S(1)}, bf16[7,7,1,128]{3,2,1,0:T(2,128)(2,1)S(1)}, u32[]{:S(2)}, u32[]{:S(2)}) collective-permute-start(bf16[7,7,1,128]{3,2,1,0:T(2,128)(2,1)S(1)} %get-tuple-element.36), channel_id=1, source_target_pairs={{0,1},{1,0},{2,3},{3,2},{4,5},{5,4},{6,7},{7,6},{8,9},{9,8},{10,11... | collective-permute-start | bytes 37640 | tf_op jit(solution)/shard_map/ppermute | solution.py:36
  38.9 0.7 collective-permute-start.13
  39.5 4.1 %collective-permute-start.12 = (bf16[7,1,7,128]{3,2,1,0:T(8,128)(2,1)S(1)}, bf16[7,1,7,128]{3,2,1,0:T(8,128)(2,1)S(1)}, u32[]{:S(2)}, u32[]{:S(2)}) collective-permute-start(bf16[7,1,7,128]{3,2,1,0:T(8,128)(2,1)S(1)} %get-tuple-element.16), channel_id=1, source_target_pairs={{0,4},{4,0},{1,5},{5,1},{2,6},{6,2},{3,7},{7,3},{8,12},{12,8},{9,1... | collective-permute-start | bytes 37640 | tf_op jit(solution)/shard_map/ppermute | solution.py:36
  43.7 1.7 %collective-permute-done.12 = bf16[7,1,7,128]{3,2,1,0:T(8,128)(2,1)S(1)} collective-permute-done((bf16[7,1,7,128]{3,2,1,0:T(8,128)(2,1)S(1)}, bf16[7,1,7,128]{3,2,1,0:T(8,128)(2,1)S(1)}, u32[]{:S(2)}, u32[]{:S(2)}) %collective-permute-start.12) | collective-permute-done | bytes 12576 | tf_op jit(solution)/shard_map/ppermute | solution.py:36
  45.5 2.7 %collective-permute-start.14 = (bf16[1,7,7,128]{3,2,1,0:T(8,128)(2,1)S(1)}, bf16[1,7,7,128]{3,2,1,0:T(8,128)(2,1)S(1)}, u32[]{:S(2)}, u32[]{:S(2)}) collective-permute-start(bf16[1,7,7,128]{3,2,1,0:T(8,128)(2,1)S(1)} %fusion.67), channel_id=1, source_target_pairs={{0,16},{16,0},{1,17},{17,1},{2,18},{18,2},{3,19},{19,3},{4,20},{20... | collective-permute-start | bytes 37640 | tf_op jit(solution)/shard_map/ppermute | solution.py:36
  48.2 2.0 %collective-permute-done.14 = bf16[1,7,7,128]{3,2,1,0:T(8,128)(2,1)S(1)} collective-permute-done((bf16[1,7,7,128]{3,2,1,0:T(8,128)(2,1)S(1)}, bf16[1,7,7,128]{3,2,1,0:T(8,128)(2,1)S(1)}, u32[]{:S(2)}, u32[]{:S(2)}) %collective-permute-start.14) | collective-permute-done | bytes 12576 | tf_op jit(solution)/shard_map/ppermute | solution.py:36
  50.8 3.8 %collective-permute-start.15 = (bf16[7,7,1,128]{3,2,1,0:T(2,128)(2,1)S(1)}, bf16[7,7,1,128]{3,2,1,0:T(2,128)(2,1)S(1)}, u32[]{:S(2)}, u32[]{:S(2)}) collective-permute-start(bf16[7,7,1,128]{3,2,1,0:T(2,128)(2,1)S(1)} %get-tuple-element.34), channel_id=1, source_target_pairs={{0,1},{1,0},{2,3},{3,2},{4,5},{5,4},{6,7},{7,6},{8,9},{9,8},{10,11... | collective-permute-start | bytes 37640 | tf_op jit(solution)/shard_map/ppermute | solution.py:36
  55.6 0.7 collective-permute-start.18
  56.3 5.4 %collective-permute-start.17 = (bf16[7,1,7,128]{3,2,1,0:T(8,128)(2,1)S(1)}, bf16[7,1,7,128]{3,2,1,0:T(8,128)(2,1)S(1)}, u32[]{:S(2)}, u32[]{:S(2)}) collective-permute-start(bf16[7,1,7,128]{3,2,1,0:T(8,128)(2,1)S(1)} %get-tuple-element.14), channel_id=1, source_target_pairs={{0,4},{4,0},{1,5},{5,1},{2,6},{6,2},{3,7},{7,3},{8,12},{12,8},{9,1... | collective-permute-start | bytes 37640 | tf_op jit(solution)/shard_map/ppermute | solution.py:36
  61.7 1.6 %collective-permute-done.17 = bf16[7,1,7,128]{3,2,1,0:T(8,128)(2,1)S(1)} collective-permute-done((bf16[7,1,7,128]{3,2,1,0:T(8,128)(2,1)S(1)}, bf16[7,1,7,128]{3,2,1,0:T(8,128)(2,1)S(1)}, u32[]{:S(2)}, u32[]{:S(2)}) %collective-permute-start.17) | collective-permute-done | bytes 12576 | tf_op jit(solution)/shard_map/ppermute | solution.py:36
  63.4 2.7 %collective-permute-start.19 = (bf16[1,7,7,128]{3,2,1,0:T(8,128)(2,1)S(1)}, bf16[1,7,7,128]{3,2,1,0:T(8,128)(2,1)S(1)}, u32[]{:S(2)}, u32[]{:S(2)}) collective-permute-start(bf16[1,7,7,128]{3,2,1,0:T(8,128)(2,1)S(1)} %fusion.68), channel_id=1, source_target_pairs={{0,16},{16,0},{1,17},{17,1},{2,18},{18,2},{3,19},{19,3},{4,20},{20... | collective-permute-start | bytes 37640 | tf_op jit(solution)/shard_map/ppermute | solution.py:36
  66.1 2.0 %collective-permute-done.19 = bf16[1,7,7,128]{3,2,1,0:T(8,128)(2,1)S(1)} collective-permute-done((bf16[1,7,7,128]{3,2,1,0:T(8,128)(2,1)S(1)}, bf16[1,7,7,128]{3,2,1,0:T(8,128)(2,1)S(1)}, u32[]{:S(2)}, u32[]{:S(2)}) %collective-permute-start.19) | collective-permute-done | bytes 12576 | tf_op jit(solution)/shard_map/ppermute | solution.py:36
  68.9 4.6 %collective-permute-start.20 = (bf16[352,128]{1,0:T(8,128)(2,1)S(1)}, bf16[352,128]{1,0:T(8,128)(2,1)S(1)}, u32[]{:S(2)}, u32[]{:S(2)}) collective-permute-start(bf16[352,128]{1,0:T(8,128)(2,1)S(1)} %select_convert_fusion), channel_id=1, source_target_pairs={{0,1},{1,0},{2,3},{3,2},{4,5},{5,4},{6,7},{7,6},{8,9},{9,8},{10,11... | collective-permute-start | bytes 270344 | tf_op jit(solution)/shard_map/ppermute | solution.py:85
  73.6 0.9 collective-permute-done.20
  74.6 16.4 %all_to_all.10 = bf16[16,22,128]{2,1,0:T(8,128)(2,1)S(1)} all-to-all(bf16[16,22,128]{2,1,0:T(8,128)(2,1)S(1)} %reshape.109), channel_id=1, replica_groups={{0,2,4,6,8,10,12,14,16,18,20,22,24,26,28,30},{1,3,5,7,9,11,13,15,17,19,..., dimensions={0} | all-to-all | bytes 180224 | tf_op jit(solution)/shard_map/all_to_all | solution.py:88
  91.0 10.3 %all_to_all.11 = bf16[16,22,128]{2,1,0:T(8,128)(2,1)S(1)} all-to-all(bf16[16,22,128]{2,1,0:T(8,128)(2,1)S(1)} %broadcast_in_dim.31), channel_id=1, replica_groups={{0,2,4,6,8,10,12,14,16,18,20,22,24,26,28,30},{1,3,5,7,9,11,13,15,17,19,..., dimensions={0} | all-to-all | bytes 180224 | tf_op jit(solution)/shard_map/all_to_all | solution.py:90
  101.4 1.3 %collective-permute-done.21 = bf16[352,128]{1,0:T(8,128)(2,1)S(1)} collective-permute-done((bf16[352,128]{1,0:T(8,128)(2,1)S(1)}, bf16[352,128]{1,0:T(8,128)(2,1)S(1)}, u32[]{:S(2)}, u32[]{:S(2)}) %collective-permute-start.21) | collective-permute-done | bytes 90144 | tf_op jit(solution)/shard_map/ppermute | solution.py:93
  102.6 0.8 maximum_convert_fusion
  (94 shorter events, 7.6 us)
Async XLA Ops:
  0.6 67.6 %copy-start = (bf16[216,704]{1,0:T(8,128)(2,1)S(1)}, bf16[216,704]{1,0:T(8,128)(2,1)}, u32[]{:S(2)}) copy-start(bf16[216,704]{1,0:T(8,128)(2,1)} %param.11) | copy-start | bytes 912388
  1.5 8.5 %copy-start.4 = (bf16[1,343,343]{2,1,0:T(8,128)(2,1)S(1)}, bf16[1,343,343]{2,1,0:T(8,128)(2,1)}, u32[]{:S(2)}) copy-start(bf16[1,343,343]{2,1,0:T(8,128)(2,1)} %param.8) | copy-start | bytes 705898
  1.6 5.8 %collective-permute-start = (bf16[1,7,7,128]{3,2,1,0:T(8,128)(2,1)S(1)}, bf16[1,7,7,128]{3,2,1,0:T(8,128)(2,1)S(1)}, u32[]{:S(2)}, u32[]{:S(2)}) collective-permute-start(bf16[1,7,7,128]{3,2,1,0:T(8,128)(2,1)S(1)} %pad_slice_fusion.9), channel_id=1, source_target_pairs={{0,16},{16,0},{1,17},{17,1},{2,18},{18,2},{3,19},{19,3},{4,20},{20... | collective-permute-start | bytes 37640 | tf_op jit(solution)/shard_map/ppermute | solution.py:36
  5.7 0.7 copy-start.3
  7.4 3.8 %collective-permute-start.1 = (bf16[7,1,7,128]{3,2,1,0:T(8,128)(2,1)S(1)}, bf16[7,1,7,128]{3,2,1,0:T(8,128)(2,1)S(1)}, u32[]{:S(2)}, u32[]{:S(2)}) collective-permute-start(bf16[7,1,7,128]{3,2,1,0:T(8,128)(2,1)S(1)} %pad_maximum_fusion.10), channel_id=1, source_target_pairs={{0,4},{4,0},{1,5},{5,1},{2,6},{6,2},{3,7},{7,3},{8,12},{12,8},{9,1... | collective-permute-start | bytes 37640 | tf_op jit(solution)/shard_map/ppermute | solution.py:36
  9.3 1.8 %collective-permute-start.2 = (bf16[7,1,7,128]{3,2,1,0:T(8,128)(2,1)S(1)}, bf16[7,1,7,128]{3,2,1,0:T(8,128)(2,1)S(1)}, u32[]{:S(2)}, u32[]{:S(2)}) collective-permute-start(bf16[7,1,7,128]{3,2,1,0:T(8,128)(2,1)S(1)} %pad_maximum_fusion.10), channel_id=1, source_target_pairs={{4,8},{8,4},{5,9},{9,5},{6,10},{10,6},{7,11},{11,7},{20,24},{24,20... | collective-permute-start | bytes 37640 | tf_op jit(solution)/shard_map/ppermute | solution.py:36
  11.2 1.3 %collective-permute-start.3 = (bf16[7,7,1,128]{3,2,1,0:T(2,128)(2,1)S(1)}, bf16[7,7,1,128]{3,2,1,0:T(2,128)(2,1)S(1)}, u32[]{:S(2)}, u32[]{:S(2)}) collective-permute-start(bf16[7,7,1,128]{3,2,1,0:T(2,128)(2,1)S(1)} %slice.195), channel_id=1, source_target_pairs={{0,1},{1,0},{2,3},{3,2},{4,5},{5,4},{6,7},{7,6},{8,9},{9,8},{10,11... | collective-permute-start | bytes 37640 | tf_op jit(solution)/shard_map/ppermute | solution.py:36
  11.3 1.2 %collective-permute-start.4 = (bf16[7,7,1,128]{3,2,1,0:T(2,128)(2,1)S(1)}, bf16[7,7,1,128]{3,2,1,0:T(2,128)(2,1)S(1)}, u32[]{:S(2)}, u32[]{:S(2)}) collective-permute-start(bf16[7,7,1,128]{3,2,1,0:T(2,128)(2,1)S(1)} %slice.195), channel_id=1, source_target_pairs={{1,2},{2,1},{5,6},{6,5},{9,10},{10,9},{13,14},{14,13},{17,18},{18,... | collective-permute-start | bytes 37640 | tf_op jit(solution)/shard_map/ppermute | solution.py:36
  12.6 0.7 copy-start.2
  13.7 5.4 %collective-permute-start.5 = (bf16[7,7,1,128]{3,2,1,0:T(2,128)(2,1)S(1)}, bf16[7,7,1,128]{3,2,1,0:T(2,128)(2,1)S(1)}, u32[]{:S(2)}, u32[]{:S(2)}) collective-permute-start(bf16[7,7,1,128]{3,2,1,0:T(2,128)(2,1)S(1)} %get-tuple-element.38), channel_id=1, source_target_pairs={{0,1},{1,0},{2,3},{3,2},{4,5},{5,4},{6,7},{7,6},{8,9},{9,8},{10,11... | collective-permute-start | bytes 37640 | tf_op jit(solution)/shard_map/ppermute | solution.py:36
  18.2 0.9 collective-permute-start.6
  19.2 9.7 %collective-permute-start.8 = (bf16[7,1,7,128]{3,2,1,0:T(8,128)(2,1)S(1)}, bf16[7,1,7,128]{3,2,1,0:T(8,128)(2,1)S(1)}, u32[]{:S(2)}, u32[]{:S(2)}) collective-permute-start(bf16[7,1,7,128]{3,2,1,0:T(8,128)(2,1)S(1)} %broadcast_select_fusion.22), channel_id=1, source_target_pairs={{4,8},{8,4},{5,9},{9,5},{6,10},{10,6},{7,11},{11,7},{20,24},{24,20... | collective-permute-start | bytes 37640 | tf_op jit(solution)/shard_map/ppermute | solution.py:36
  19.8 10.7 %collective-permute-start.7 = (bf16[7,1,7,128]{3,2,1,0:T(8,128)(2,1)S(1)}, bf16[7,1,7,128]{3,2,1,0:T(8,128)(2,1)S(1)}, u32[]{:S(2)}, u32[]{:S(2)}) collective-permute-start(bf16[7,1,7,128]{3,2,1,0:T(8,128)(2,1)S(1)} %get-tuple-element.19), channel_id=1, source_target_pairs={{0,4},{4,0},{1,5},{5,1},{2,6},{6,2},{3,7},{7,3},{8,12},{12,8},{9,1... | collective-permute-start | bytes 37640 | tf_op jit(solution)/shard_map/ppermute | solution.py:36
  30.6 4.7 %collective-permute-start.9 = (bf16[1,7,7,128]{3,2,1,0:T(8,128)(2,1)S(1)}, bf16[1,7,7,128]{3,2,1,0:T(8,128)(2,1)S(1)}, u32[]{:S(2)}, u32[]{:S(2)}) collective-permute-start(bf16[1,7,7,128]{3,2,1,0:T(8,128)(2,1)S(1)} %fusion.66), channel_id=1, source_target_pairs={{0,16},{16,0},{1,17},{17,1},{2,18},{18,2},{3,19},{19,3},{4,20},{20... | collective-permute-start | bytes 37640 | tf_op jit(solution)/shard_map/ppermute | solution.py:36
  35.8 2.9 %collective-permute-start.10 = (bf16[7,7,1,128]{3,2,1,0:T(2,128)(2,1)S(1)}, bf16[7,7,1,128]{3,2,1,0:T(2,128)(2,1)S(1)}, u32[]{:S(2)}, u32[]{:S(2)}) collective-permute-start(bf16[7,7,1,128]{3,2,1,0:T(2,128)(2,1)S(1)} %get-tuple-element.36), channel_id=1, source_target_pairs={{0,1},{1,0},{2,3},{3,2},{4,5},{5,4},{6,7},{7,6},{8,9},{9,8},{10,11... | collective-permute-start | bytes 37640 | tf_op jit(solution)/shard_map/ppermute | solution.py:36
  37.9 0.9 collective-permute-start.11
  38.9 4.8 %collective-permute-start.13 = (bf16[7,1,7,128]{3,2,1,0:T(8,128)(2,1)S(1)}, bf16[7,1,7,128]{3,2,1,0:T(8,128)(2,1)S(1)}, u32[]{:S(2)}, u32[]{:S(2)}) collective-permute-start(bf16[7,1,7,128]{3,2,1,0:T(8,128)(2,1)S(1)} %broadcast_select_fusion.21), channel_id=1, source_target_pairs={{4,8},{8,4},{5,9},{9,5},{6,10},{10,6},{7,11},{11,7},{20,24},{24,20... | collective-permute-start | bytes 37640 | tf_op jit(solution)/shard_map/ppermute | solution.py:36
  39.5 5.8 %collective-permute-start.12 = (bf16[7,1,7,128]{3,2,1,0:T(8,128)(2,1)S(1)}, bf16[7,1,7,128]{3,2,1,0:T(8,128)(2,1)S(1)}, u32[]{:S(2)}, u32[]{:S(2)}) collective-permute-start(bf16[7,1,7,128]{3,2,1,0:T(8,128)(2,1)S(1)} %get-tuple-element.16), channel_id=1, source_target_pairs={{0,4},{4,0},{1,5},{5,1},{2,6},{6,2},{3,7},{7,3},{8,12},{12,8},{9,1... | collective-permute-start | bytes 37640 | tf_op jit(solution)/shard_map/ppermute | solution.py:36
  45.5 4.7 %collective-permute-start.14 = (bf16[1,7,7,128]{3,2,1,0:T(8,128)(2,1)S(1)}, bf16[1,7,7,128]{3,2,1,0:T(8,128)(2,1)S(1)}, u32[]{:S(2)}, u32[]{:S(2)}) collective-permute-start(bf16[1,7,7,128]{3,2,1,0:T(8,128)(2,1)S(1)} %fusion.67), channel_id=1, source_target_pairs={{0,16},{16,0},{1,17},{17,1},{2,18},{18,2},{3,19},{19,3},{4,20},{20... | collective-permute-start | bytes 37640 | tf_op jit(solution)/shard_map/ppermute | solution.py:36
  50.8 4.7 %collective-permute-start.15 = (bf16[7,7,1,128]{3,2,1,0:T(2,128)(2,1)S(1)}, bf16[7,7,1,128]{3,2,1,0:T(2,128)(2,1)S(1)}, u32[]{:S(2)}, u32[]{:S(2)}) collective-permute-start(bf16[7,7,1,128]{3,2,1,0:T(2,128)(2,1)S(1)} %get-tuple-element.34), channel_id=1, source_target_pairs={{0,1},{1,0},{2,3},{3,2},{4,5},{5,4},{6,7},{7,6},{8,9},{9,8},{10,11... | collective-permute-start | bytes 37640 | tf_op jit(solution)/shard_map/ppermute | solution.py:36
  54.6 0.9 collective-permute-start.16
  55.6 6.1 %collective-permute-start.18 = (bf16[7,1,7,128]{3,2,1,0:T(8,128)(2,1)S(1)}, bf16[7,1,7,128]{3,2,1,0:T(8,128)(2,1)S(1)}, u32[]{:S(2)}, u32[]{:S(2)}) collective-permute-start(bf16[7,1,7,128]{3,2,1,0:T(8,128)(2,1)S(1)} %broadcast_select_fusion.20), channel_id=1, source_target_pairs={{4,8},{8,4},{5,9},{9,5},{6,10},{10,6},{7,11},{11,7},{20,24},{24,20... | collective-permute-start | bytes 37640 | tf_op jit(solution)/shard_map/ppermute | solution.py:36
  56.3 7.1 %collective-permute-start.17 = (bf16[7,1,7,128]{3,2,1,0:T(8,128)(2,1)S(1)}, bf16[7,1,7,128]{3,2,1,0:T(8,128)(2,1)S(1)}, u32[]{:S(2)}, u32[]{:S(2)}) collective-permute-start(bf16[7,1,7,128]{3,2,1,0:T(8,128)(2,1)S(1)} %get-tuple-element.14), channel_id=1, source_target_pairs={{0,4},{4,0},{1,5},{5,1},{2,6},{6,2},{3,7},{7,3},{8,12},{12,8},{9,1... | collective-permute-start | bytes 37640 | tf_op jit(solution)/shard_map/ppermute | solution.py:36
  63.4 4.7 %collective-permute-start.19 = (bf16[1,7,7,128]{3,2,1,0:T(8,128)(2,1)S(1)}, bf16[1,7,7,128]{3,2,1,0:T(8,128)(2,1)S(1)}, u32[]{:S(2)}, u32[]{:S(2)}) collective-permute-start(bf16[1,7,7,128]{3,2,1,0:T(8,128)(2,1)S(1)} %fusion.68), channel_id=1, source_target_pairs={{0,16},{16,0},{1,17},{17,1},{2,18},{18,2},{3,19},{19,3},{4,20},{20... | collective-permute-start | bytes 37640 | tf_op jit(solution)/shard_map/ppermute | solution.py:36
  68.3 0.6 copy-start.1
  68.9 5.6 %collective-permute-start.20 = (bf16[352,128]{1,0:T(8,128)(2,1)S(1)}, bf16[352,128]{1,0:T(8,128)(2,1)S(1)}, u32[]{:S(2)}, u32[]{:S(2)}) collective-permute-start(bf16[352,128]{1,0:T(8,128)(2,1)S(1)} %select_convert_fusion), channel_id=1, source_target_pairs={{0,1},{1,0},{2,3},{3,2},{4,5},{5,4},{6,7},{7,6},{8,9},{9,8},{10,11... | collective-permute-start | bytes 270344 | tf_op jit(solution)/shard_map/ppermute | solution.py:85
  101.3 1.4 %collective-permute-start.21 = (bf16[352,128]{1,0:T(8,128)(2,1)S(1)}, bf16[352,128]{1,0:T(8,128)(2,1)S(1)}, u32[]{:S(2)}, u32[]{:S(2)}) collective-permute-start(bf16[352,128]{1,0:T(8,128)(2,1)S(1)} %reshape.110), channel_id=1, source_target_pairs={{0,1},{1,0},{2,3},{3,2},{4,5},{5,4},{6,7},{7,6},{8,9},{9,8},{10,11... | collective-permute-start | bytes 270344 | tf_op jit(solution)/shard_map/ppermute | solution.py:93

commit v3 on v2

v3 whole, which is shorter than its diff:
```python
import jax
import jax.numpy as jnp
from jax import lax
from jax.sharding import PartitionSpec as P

GRID_Y = 4
GRID_Z = 4
SIDE = 7
AXIS = "cells"

chebyshev_coeffs = ((-1.0 / 7.0, 0.0), (-7.0 / 41.0, 8.0 / 41.0), (-41.0 / 259.0, 28.0 / 259.0))
centre = 6.0


class Grid:
    def __init__(self):
        self.devices = lax.axis_size(AXIS)
        self.counts = (self.devices // (GRID_Y * GRID_Z), GRID_Y, GRID_Z)
        self.stride = (GRID_Y * GRID_Z, GRID_Z, 1)
        self.position = lax.axis_index(AXIS)
        self.coords = tuple(
            self.position // self.stride[d] % self.counts[d] for d in range(3)
        )

    def coord_of(self, device, dim):
        return device // self.stride[dim] % self.counts[dim]

    def swapped(self, low, high, dim, odd):
        by = self.stride[dim]
        pairs = []
        for i in range(self.devices):
            c = self.coord_of(i, dim)
            if c % 2 == odd and c + 1 < self.counts[dim]:
                pairs += [(i, i + by), (i + by, i)]
        lower = self.coords[dim] % 2 == odd
        arrived = lax.ppermute(jnp.where(lower, high, low), AXIS, pairs)
        zero = jnp.zeros_like(arrived)
        return jnp.where(lower, zero, arrived), jnp.where(lower, arrived, zero)

    def exchanged(self, low, high, dim):
        to_low, to_high = self.swapped(low, high, dim, 0)
        if self.counts[dim] > 2:
            more_low, more_high = self.swapped(low, high, dim, 1)
            to_low, to_high = to_low + more_low, to_high + more_high
        return to_low, to_high

    def partner(self, value, bit):
        return lax.ppermute(value, AXIS, [(i, i ^ bit) for i in range(self.devices)])

    def has(self, bit):
        return (self.position & bit) != 0


def line_bits():
    bit = GRID_Z // 2
    while bit:
        yield bit
        bit //= 2


def lines_gathered(grid, value):
    held = value[None]
    order = [0]
    for bit in line_bits():
        other = grid.partner(held, bit)
        mine = grid.has(bit)
        held = jnp.concatenate(
            [jnp.where(mine, other, held), jnp.where(mine, held, other)], axis=0
        )
        order = order + [i | bit for i in order]
    return [held[order.index(i)] for i in range(GRID_Z)]


def lines_transposed(grid, value):
    rows, columns = value.shape
    width = columns // GRID_Z
    blocks = [value[:, i * width : (i + 1) * width] for i in range(GRID_Z)]
    half = rows // 2
    for bit in line_bits():
        mine = grid.has(bit)
        lows = [i for i in range(GRID_Z) if not i & bit]
        away = [jnp.where(mine, blocks[i], blocks[i | bit]) for i in lows]
        packed = jnp.concatenate([b[h : h + half] for h in (0, half) for b in away], axis=1)
        arrived = grid.partner(packed, bit)
        for at, i in enumerate(lows):
            first = arrived[:, at * width : (at + 1) * width]
            second = arrived[:, (at + len(lows)) * width : (at + len(lows) + 1) * width]
            came = jnp.concatenate([first, second], axis=0)
            blocks[i], blocks[i | bit] = (
                jnp.where(mine, came, blocks[i]),
                jnp.where(mine, blocks[i | bit], came),
            )
    return jnp.concatenate(blocks, axis=1)


def plane(field, dim, at):
    return lax.slice_in_dim(field, at, at + 1, axis=dim)


def with_ends(field, dim, low, high):
    last = field.shape[dim] - 1
    parts = [
        plane(field, dim, 0) if low is None else low,
        lax.slice_in_dim(field, 1, last, axis=dim),
        plane(field, dim, last) if high is None else high,
    ]
    return jnp.concatenate(parts, axis=dim)


def to_next_partition(value, width):
    kept = value[..., :-width]
    return jnp.concatenate([jnp.zeros_like(value[..., :width]), kept], axis=-1)


def to_previous_partition(value, width):
    kept = value[..., width:]
    return jnp.concatenate([kept, jnp.zeros_like(value[..., :width])], axis=-1)


def slots_matrix(cell_matrix, connectivity, slot_count):
    total = None
    for c in range(cell_matrix.shape[0]):
        chosen = (
            connectivity[c][:, None] == jnp.arange(slot_count, dtype=jnp.int32)[None, :]
        ).astype(jnp.bfloat16)
        rows = lax.dot_general(
            chosen, cell_matrix[c], (((0,), (0,)), ((), ())), preferred_element_type=jnp.float32
        ).astype(jnp.bfloat16)
        both = jnp.dot(rows, chosen, preferred_element_type=jnp.float32)
        total = both if total is None else total + both
    return total.astype(jnp.bfloat16)


def rounded(value):
    return lax.reduce_precision(value, 8, 7).astype(jnp.bfloat16)


def summed_over_lines(grid, value):
    left = grid.devices // GRID_Z
    stride = GRID_Z
    factor = 2
    while left > 1:
        while left % factor:
            factor += 1
        at = grid.position // stride % factor
        terms = [value]
        for turn in range(1, factor):
            pairs = []
            for i in range(grid.devices):
                c = i // stride % factor
                pairs.append((i, i + ((c + turn) % factor - c) * stride))
            terms.append(lax.ppermute(value, AXIS, pairs))
        if factor == 2:
            total = terms[0].astype(jnp.float32) + terms[1].astype(jnp.float32)
        else:
            total = 0.0
            for k in range(factor):
                term = terms[0]
                for turn in range(1, factor):
                    term = jnp.where((at - turn) % factor == k, terms[turn], term)
                total = total + term.astype(jnp.float32)
        value = total.astype(jnp.bfloat16)
        left //= factor
        stride *= factor
    return value


def per_device(block, cell_matrix, connectivity, potential, locked):
    owned_rows, columns = block.shape
    slot_count = potential.shape[0]
    width = columns // GRID_Z
    edge = SIDE - 1
    grid = Grid()
    shape = (SIDE, SIDE, SIDE, columns)

    matrix = slots_matrix(cell_matrix, connectivity, slot_count)
    coarse = rounded(potential)
    fine = rounded(potential - coarse.astype(jnp.float32))
    matrix = jnp.concatenate([matrix, coarse[:, None], fine[:, None]], axis=1)
    matrices = lines_gathered(grid, matrix)
    lane_owner = lax.broadcasted_iota(jnp.int32, (1, columns), 1) // width
    lumped = jnp.zeros((slot_count, columns), jnp.float32)
    for p in range(GRID_Z):
        both = jnp.sum(matrices[p][:, slot_count:].astype(jnp.float32), axis=1, keepdims=True)
        lumped = jnp.where(lane_owner == p, both, lumped)

    mine = lines_transposed(grid, block)
    field = (
        jnp.zeros(shape, jnp.bfloat16)
        .at[1:, 1:, 1:]
        .set(mine.reshape(edge, edge, edge, columns))
    )
    field = with_ends(field, 2, to_next_partition(plane(field, 2, SIDE - 1), width), None)
    for dim in (1, 0):
        high = plane(field, dim, SIDE - 1)
        field = with_ends(field, dim, grid.exchanged(high, high, dim)[0], None)

    inside = jnp.ones(shape, jnp.bool_)
    first = (grid.coords[0] == 0, grid.coords[1] == 0, lane_owner.reshape(1, 1, 1, columns) == 0)
    for dim in range(3):
        at = lax.broadcasted_iota(jnp.int32, shape, dim)
        inside = inside & ~((at == 0) & first[dim])

    older = field
    current = field
    steps = len(chebyshev_coeffs)
    for step, coeffs in enumerate(chebyshev_coeffs):
        rows = current.reshape(slot_count, columns)
        partial = lumped * rows.astype(jnp.float32)
        for p in range(GRID_Z):
            own = jnp.where(lane_owner == p, rows, jnp.zeros_like(rows))
            partial = partial + jnp.dot(
                matrices[p][:, :slot_count], own, preferred_element_type=jnp.float32
            )
        partial = partial.reshape(shape)
        low, high = plane(partial, 2, 0), plane(partial, 2, SIDE - 1)
        partial = with_ends(
            partial,
            2,
            low + to_next_partition(high, width),
            high + to_previous_partition(low, width),
        )
        for dim in (1, 0):
            low, high = plane(partial, dim, 0), plane(partial, dim, SIDE - 1)
            to_low, to_high = grid.exchanged(
                low.astype(jnp.bfloat16), high.astype(jnp.bfloat16), dim
            )
            partial = with_ends(
                partial,
                dim,
                None if step == steps - 1 else low + to_low.astype(jnp.float32),
                high + to_high.astype(jnp.float32),
            )
        following = coeffs[0] * (partial - centre * current.astype(jnp.float32)) - coeffs[
            1
        ] * older.astype(jnp.float32)
        following = rounded(jnp.where(inside, following, 0.0))
        older = current
        current = following
        if step == 0:
            locked, current = lax.optimization_barrier((locked, current))
            all_locked = lines_gathered(grid, locked)
    filtered = current[1:, 1:, 1:].reshape(owned_rows, columns)

    share = jnp.zeros((width, locked.shape[1]), jnp.float32)
    for p in range(GRID_Z):
        share = share + lax.dot_general(
            filtered[:, p * width : (p + 1) * width],
            all_locked[p],
            (((0,), (0,)), ((), ())),
            preferred_element_type=jnp.float32,
        )
    share = summed_over_lines(grid, share.astype(jnp.bfloat16))
    intersection = jnp.concatenate(lines_gathered(grid, share)).T.astype(jnp.float32)
    return lines_transposed(grid, filtered), intersection


def solution(mesh):
    in_specs = (
        P(AXIS, None),
        P(AXIS, None, None),
        P(AXIS, None),
        P(AXIS),
        P(AXIS, None),
    )
    out_specs = (P(AXIS, None), P())
    return jax.shard_map(
        per_device, mesh=mesh, in_specs=in_specs, out_specs=out_specs, check_vma=False
    )
```

time: 104 us -> 91.7 us (0.88)
  blocking collectives: 26.6 us -> 0 us
  waiting for transfers between devices: 15.1 us -> 28.6 us
  starting transfers between devices: 53.1 us -> 46.6 us
  other arithmetic: 2.2 us -> 6.31 us
  matrix products: 1.98 us -> 4.84 us
    all_to_all x2 -> x0, blocking collectives: 26.6 us -> none  [the longest x1 16.4 us: summed_everywhere(): dealt = lax.all_to_all(parts, AXIS, 0, 0, axis_index_groups=groups)]
    ppermute x20 -> x12, starting transfers between devices: 48.4 us -> 29.8 us  [swapped(): arrived = lax.ppermute(jnp.where(lower, high, low), AXIS, pairs)]
    ppermute x2 -> x13, waiting for transfers between devices: 2.21 us -> 15.5 us  [the longest x10 9.31 us: partner(): lax.ppermute(value, AXIS, [(i, i ^ bit) for i in range(self.devices)])]
    ppermute x2 -> x13, starting transfers between devices: 4.72 us -> 16.8 us  [the longest x3 8.83 us: summed_over_lines(): terms.append(lax.ppermute(value, AXIS, pairs))]
    dot_general x4 -> x16, matrix products: 1.26 us -> 4.12 us  [the longest x12 3.04 us: per_device(): jnp.dot(matrices[p][:, :slot_count], own, preferred_element_type=jnp.floa...]
    select_n x1 -> x14, other arithmetic: 0.02 us -> 2.46 us  [the longest x4 1.43 us: lines_transposed(): away = [jnp.where(mine, blocks[i], blocks[i | bit]) for i in lows]]
    concatenate x0 -> x9, other arithmetic: none -> 1.46 us  [the longest x2 0.86 us: lines_transposed(): return jnp.concatenate(blocks, axis=1)]
    ppermute x20 -> x12, waiting for transfers between devices: 12.9 us -> 13.1 us  [swapped(): arrived = lax.ppermute(jnp.where(lower, high, low), AXIS, pairs)]
  transfers between devices with their start and end apart: 22 -> 25, of which waited for: 14 -> 16; matrix products, arithmetic and copies ran while one was open for 1% -> 4% of each run, Pallas kernels for 0% -> 0%
where the time goes in v3:
time: 91.7 us; the launch traced here: 91.5 us
  starting transfers between devices  46.6 us (51%)
  waiting for transfers between devices  28.6 us (31%)
  other arithmetic  6.31 us (7%)
  matrix products  4.84 us (5%)
  local copies, waits for them, and re-layouts  3.63 us (4%)
  between operations  1.44 us (2%)
    ppermute x12, starting transfers between devices, swapped(): arrived = lax.ppermute(jnp.where(lower, high, low), AXIS, pairs)  29.8 us
    ppermute x12, waiting for transfers between devices, swapped(): arrived = lax.ppermute(jnp.where(lower, high, low), AXIS, pairs)  13.1 us
    ppermute x10, waiting for transfers between devices, partner(): lax.ppermute(value, AXIS, [(i, i ^ bit) for i in range(self.devices)])  9.31 us
    ppermute x3, starting transfers between devices, summed_over_lines(): terms.append(lax.ppermute(value, AXIS, pairs))  8.83 us
    ppermute x10, starting transfers between devices, partner(): lax.ppermute(value, AXIS, [(i, i ^ bit) for i in range(self.devices)])  7.96 us
    ppermute x3, waiting for transfers between devices, summed_over_lines(): terms.append(lax.ppermute(value, AXIS, pairs))  6.21 us
    dot_general x12, matrix products, per_device(): jnp.dot(matrices[p][:, :slot_count], own, preferred_element_type=jnp.floa...  3.04 us
  transfers between devices with their start and end apart: 25, of which 16 were waited for; matrix products, arithmetic and copies ran while one was open for 4% of the time, Pallas kernels for 0%

profile of v3, /device:TPU:0, one launch (start us, length us, event | category | flops | bytes accessed | tf_op | source)
XLA Modules:
  0.0 91.5 jit_solution(12700269364930075743)
XLA Ops:
  0.7 1.1 %broadcast_select_fusion.21 = (bf16[216,32]{1,0:T(8,128)(2,1)S(1)}, bf16[216,32]{1,0:T(8,128)(2,1)S(1)}) fusion(pred[]{:T(512)S(6)} %ne.185, bf16[216,128]{1,0:T(8,128)(2,1)} %param.7), kind=kLoop, calls=%fused_computation.166 | loop fusion | flops 13824 | bytes 82945 | tf_op jit(solution)/shard_map/jit(_where)/select_n | solution.py:82
  1.9 3.0 %collective-permute-start.2 = (bf16[108,128]{1,0:T(8,128)(2,1)S(1)}, bf16[108,128]{1,0:T(8,128)(2,1)S(1)}, u32[]{:S(2)}, u32[]{:S(2)}) collective-permute-start(bf16[108,128]{1,0:T(8,128)(2,1)S(1)} %pad_maximum_fusion.19), channel_id=1, source_target_pairs={{0,2},{1,3},{2,0},{3,1},{4,6},{5,7},{6,4},{7,5},{8,10},{9,11},{10,... | collective-permute-start | bytes 82952 | tf_op jit(solution)/shard_map/ppermute | solution.py:48
  7.9 1.2 %collective-permute-done.3 = bf16[108,128]{1,0:T(8,128)(2,1)S(1)} collective-permute-done((bf16[108,128]{1,0:T(8,128)(2,1)S(1)}, bf16[108,128]{1,0:T(8,128)(2,1)S(1)}, u32[]{:S(2)}, u32[]{:S(2)}) %collective-permute-start.3) | collective-permute-done | bytes 27680 | tf_op jit(solution)/shard_map/ppermute | solution.py:48
  10.4 4.9 %collective-permute-start.4 = (bf16[7,1,7,128]{3,2,1,0:T(8,128)(2,1)S(1)}, bf16[7,1,7,128]{3,2,1,0:T(8,128)(2,1)S(1)}, u32[]{:S(2)}, u32[]{:S(2)}) collective-permute-start(bf16[7,1,7,128]{3,2,1,0:T(8,128)(2,1)S(1)} %slice.488), channel_id=1, source_target_pairs={{0,4},{4,0},{1,5},{5,1},{2,6},{6,2},{3,7},{7,3},{8,12},{12,8},{9,1... | collective-permute-start | bytes 37640 | tf_op jit(solution)/shard_map/ppermute | solution.py:36
  15.3 1.7 %collective-permute-done.4 = bf16[7,1,7,128]{3,2,1,0:T(8,128)(2,1)S(1)} collective-permute-done((bf16[7,1,7,128]{3,2,1,0:T(8,128)(2,1)S(1)}, bf16[7,1,7,128]{3,2,1,0:T(8,128)(2,1)S(1)}, u32[]{:S(2)}, u32[]{:S(2)}) %collective-permute-start.4) | collective-permute-done | bytes 12576 | tf_op jit(solution)/shard_map/ppermute | solution.py:36
  17.8 2.7 %collective-permute-start.6 = (bf16[1,7,7,128]{3,2,1,0:T(8,128)(2,1)S(1)}, bf16[1,7,7,128]{3,2,1,0:T(8,128)(2,1)S(1)}, u32[]{:S(2)}, u32[]{:S(2)}) collective-permute-start(bf16[1,7,7,128]{3,2,1,0:T(8,128)(2,1)S(1)} %pad_maximum_fusion.23), channel_id=1, source_target_pairs={{0,16},{16,0},{1,17},{17,1},{2,18},{18,2},{3,19},{19,3},{4,20},{20... | collective-permute-start | bytes 37640 | tf_op jit(solution)/shard_map/ppermute | solution.py:36
  20.5 2.0 %collective-permute-done.6 = bf16[1,7,7,128]{3,2,1,0:T(8,128)(2,1)S(1)} collective-permute-done((bf16[1,7,7,128]{3,2,1,0:T(8,128)(2,1)S(1)}, bf16[1,7,7,128]{3,2,1,0:T(8,128)(2,1)S(1)}, u32[]{:S(2)}, u32[]{:S(2)}) %collective-permute-start.6) | collective-permute-done | bytes 12576 | tf_op jit(solution)/shard_map/ppermute | solution.py:36
  25.8 4.7 %collective-permute-start.7 = (bf16[7,1,7,128]{3,2,1,0:T(8,128)(2,1)S(1)}, bf16[7,1,7,128]{3,2,1,0:T(8,128)(2,1)S(1)}, u32[]{:S(2)}, u32[]{:S(2)}) collective-permute-start(bf16[7,1,7,128]{3,2,1,0:T(8,128)(2,1)S(1)} %get-tuple-element.33), channel_id=1, source_target_pairs={{0,4},{4,0},{1,5},{5,1},{2,6},{6,2},{3,7},{7,3},{8,12},{12,8},{9,1... | collective-permute-start | bytes 37640 | tf_op jit(solution)/shard_map/ppermute | solution.py:36
  30.6 1.7 %collective-permute-done.7 = bf16[7,1,7,128]{3,2,1,0:T(8,128)(2,1)S(1)} collective-permute-done((bf16[7,1,7,128]{3,2,1,0:T(8,128)(2,1)S(1)}, bf16[7,1,7,128]{3,2,1,0:T(8,128)(2,1)S(1)}, u32[]{:S(2)}, u32[]{:S(2)}) %collective-permute-start.7) | collective-permute-done | bytes 12576 | tf_op jit(solution)/shard_map/ppermute | solution.py:36
  32.3 2.7 %collective-permute-start.9 = (bf16[1,7,7,128]{3,2,1,0:T(8,128)(2,1)S(1)}, bf16[1,7,7,128]{3,2,1,0:T(8,128)(2,1)S(1)}, u32[]{:S(2)}, u32[]{:S(2)}) collective-permute-start(bf16[1,7,7,128]{3,2,1,0:T(8,128)(2,1)S(1)} %fusion.95), channel_id=1, source_target_pairs={{0,16},{16,0},{1,17},{17,1},{2,18},{18,2},{3,19},{19,3},{4,20},{20... | collective-permute-start | bytes 37640 | tf_op jit(solution)/shard_map/ppermute | solution.py:36
  35.0 2.0 %collective-permute-done.9 = bf16[1,7,7,128]{3,2,1,0:T(8,128)(2,1)S(1)} collective-permute-done((bf16[1,7,7,128]{3,2,1,0:T(8,128)(2,1)S(1)}, bf16[1,7,7,128]{3,2,1,0:T(8,128)(2,1)S(1)}, u32[]{:S(2)}, u32[]{:S(2)}) %collective-permute-start.9) | collective-permute-done | bytes 12576 | tf_op jit(solution)/shard_map/ppermute | solution.py:36
  39.3 4.9 %collective-permute-start.10 = (bf16[7,1,7,128]{3,2,1,0:T(8,128)(2,1)S(1)}, bf16[7,1,7,128]{3,2,1,0:T(8,128)(2,1)S(1)}, u32[]{:S(2)}, u32[]{:S(2)}) collective-permute-start(bf16[7,1,7,128]{3,2,1,0:T(8,128)(2,1)S(1)} %get-tuple-element.30), channel_id=1, source_target_pairs={{0,4},{4,0},{1,5},{5,1},{2,6},{6,2},{3,7},{7,3},{8,12},{12,8},{9,1... | collective-permute-start | bytes 37640 | tf_op jit(solution)/shard_map/ppermute | solution.py:36
  44.1 1.7 %collective-permute-done.10 = bf16[7,1,7,128]{3,2,1,0:T(8,128)(2,1)S(1)} collective-permute-done((bf16[7,1,7,128]{3,2,1,0:T(8,128)(2,1)S(1)}, bf16[7,1,7,128]{3,2,1,0:T(8,128)(2,1)S(1)}, u32[]{:S(2)}, u32[]{:S(2)}) %collective-permute-start.10) | collective-permute-done | bytes 12576 | tf_op jit(solution)/shard_map/ppermute | solution.py:36
  45.9 2.7 %collective-permute-start.12 = (bf16[1,7,7,128]{3,2,1,0:T(8,128)(2,1)S(1)}, bf16[1,7,7,128]{3,2,1,0:T(8,128)(2,1)S(1)}, u32[]{:S(2)}, u32[]{:S(2)}) collective-permute-start(bf16[1,7,7,128]{3,2,1,0:T(8,128)(2,1)S(1)} %fusion.96), channel_id=1, source_target_pairs={{0,16},{16,0},{1,17},{17,1},{2,18},{18,2},{3,19},{19,3},{4,20},{20... | collective-permute-start | bytes 37640 | tf_op jit(solution)/shard_map/ppermute | solution.py:36
  48.6 2.0 %collective-permute-done.12 = bf16[1,7,7,128]{3,2,1,0:T(8,128)(2,1)S(1)} collective-permute-done((bf16[1,7,7,128]{3,2,1,0:T(8,128)(2,1)S(1)}, bf16[1,7,7,128]{3,2,1,0:T(8,128)(2,1)S(1)}, u32[]{:S(2)}, u32[]{:S(2)}) %collective-permute-start.12) | collective-permute-done | bytes 12576 | tf_op jit(solution)/shard_map/ppermute | solution.py:36
  52.2 2.1 %collective-permute-start.13 = (bf16[7,1,7,128]{3,2,1,0:T(8,128)(2,1)S(1)}, bf16[7,1,7,128]{3,2,1,0:T(8,128)(2,1)S(1)}, u32[]{:S(2)}, u32[]{:S(2)}) collective-permute-start(bf16[7,1,7,128]{3,2,1,0:T(8,128)(2,1)S(1)} %get-tuple-element.52), channel_id=1, source_target_pairs={{0,4},{4,0},{1,5},{5,1},{2,6},{6,2},{3,7},{7,3},{8,12},{12,8},{9,1... | collective-permute-start | bytes 37640 | tf_op jit(solution)/shard_map/ppermute | solution.py:36
  55.1 1.6 %collective-permute-start.18 = (bf16[1,216,704]{2,1,0:T(8,128)(2,1)S(1)}, bf16[1,216,704]{2,1,0:T(8,128)(2,1)S(1)}, u32[]{:S(2)}, u32[]{:S(2)}) collective-permute-start(bf16[1,216,704]{2,1,0:T(8,128)(2,1)S(1)} %bitcast.43), channel_id=1, source_target_pairs={{0,2},{1,3},{2,0},{3,1},{4,6},{5,7},{6,4},{7,5},{8,10},{9,11},{10,... | collective-permute-start | bytes 912392 | tf_op jit(solution)/shard_map/ppermute | solution.py:48
  56.8 2.7 %collective-permute-start.15 = (bf16[1,7,7,128]{3,2,1,0:T(8,128)(2,1)S(1)}, bf16[1,7,7,128]{3,2,1,0:T(8,128)(2,1)S(1)}, u32[]{:S(2)}, u32[]{:S(2)}) collective-permute-start(bf16[1,7,7,128]{3,2,1,0:T(8,128)(2,1)S(1)} %fusion.97), channel_id=1, source_target_pairs={{0,16},{16,0},{1,17},{17,1},{2,18},{18,2},{3,19},{19,3},{4,20},{20... | collective-permute-start | bytes 37640 | tf_op jit(solution)/shard_map/ppermute | solution.py:36
  59.4 2.0 %collective-permute-done.15 = bf16[1,7,7,128]{3,2,1,0:T(8,128)(2,1)S(1)} collective-permute-done((bf16[1,7,7,128]{3,2,1,0:T(8,128)(2,1)S(1)}, bf16[1,7,7,128]{3,2,1,0:T(8,128)(2,1)S(1)}, u32[]{:S(2)}, u32[]{:S(2)}) %collective-permute-start.15) | collective-permute-done | bytes 12576 | tf_op jit(solution)/shard_map/ppermute | solution.py:36
  61.9 0.9 collective-permute-start.16
  62.7 3.1 %collective-permute-done.16 = bf16[108,128]{1,0:T(8,128)(2,1)S(1)} collective-permute-done((bf16[108,128]{1,0:T(8,128)(2,1)S(1)}, bf16[108,128]{1,0:T(8,128)(2,1)S(1)}, u32[]{:S(2)}, u32[]{:S(2)}) %collective-permute-start.16) | collective-permute-done | bytes 27680 | tf_op jit(solution)/shard_map/ppermute | solution.py:48
  66.3 1.9 %collective-permute-done.19 = bf16[2,216,704]{2,1,0:T(8,128)(2,1)S(1)} collective-permute-done((bf16[2,216,704]{2,1,0:T(8,128)(2,1)S(1)}, bf16[2,216,704]{2,1,0:T(8,128)(2,1)S(1)}, u32[]{:S(2)}, u32[]{:S(2)}) %collective-permute-start.19) | collective-permute-done | bytes 608288 | tf_op jit(solution)/shard_map/ppermute | solution.py:48
  69.4 4.2 %collective-permute-start.20 = (bf16[32,704]{1,0:T(8,128)(2,1)S(1)}, bf16[32,704]{1,0:T(8,128)(2,1)S(1)}, u32[]{:S(2)}, u32[]{:S(2)}) collective-permute-start(bf16[32,704]{1,0:T(8,128)(2,1)S(1)} %fusion.2), channel_id=1, source_target_pairs={{0,4},{1,5},{2,6},{3,7},{4,0},{5,1},{6,2},{7,3},{8,12},{9,13},{10,... | collective-permute-start | bytes 135176 | tf_op jit(solution)/shard_map/ppermute | solution.py:152
  73.7 1.9 %collective-permute-done.20 = bf16[32,704]{1,0:T(8,128)(2,1)S(1)} collective-permute-done((bf16[32,704]{1,0:T(8,128)(2,1)S(1)}, bf16[32,704]{1,0:T(8,128)(2,1)S(1)}, u32[]{:S(2)}, u32[]{:S(2)}) %collective-permute-start.20) | collective-permute-done | bytes 45088 | tf_op jit(solution)/shard_map/ppermute | solution.py:152
  75.7 2.0 %collective-permute-start.21 = (bf16[32,704]{1,0:T(8,128)(2,1)S(1)}, bf16[32,704]{1,0:T(8,128)(2,1)S(1)}, u32[]{:S(2)}, u32[]{:S(2)}) collective-permute-start(bf16[32,704]{1,0:T(8,128)(2,1)S(1)} %add_convert_fusion.2), channel_id=1, source_target_pairs={{0,8},{1,9},{2,10},{3,11},{4,12},{5,13},{6,14},{7,15},{8,0},{9,1},... | collective-permute-start | bytes 135176 | tf_op jit(solution)/shard_map/ppermute | solution.py:152
  77.8 2.0 %collective-permute-done.21 = bf16[32,704]{1,0:T(8,128)(2,1)S(1)} collective-permute-done((bf16[32,704]{1,0:T(8,128)(2,1)S(1)}, bf16[32,704]{1,0:T(8,128)(2,1)S(1)}, u32[]{:S(2)}, u32[]{:S(2)}) %collective-permute-start.21) | collective-permute-done | bytes 45088 | tf_op jit(solution)/shard_map/ppermute | solution.py:152
  79.8 2.6 %collective-permute-start.22 = (bf16[32,704]{1,0:T(8,128)(2,1)S(1)}, bf16[32,704]{1,0:T(8,128)(2,1)S(1)}, u32[]{:S(2)}, u32[]{:S(2)}) collective-permute-start(bf16[32,704]{1,0:T(8,128)(2,1)S(1)} %add_convert_fusion.1), channel_id=1, source_target_pairs={{0,16},{1,17},{2,18},{3,19},{4,20},{5,21},{6,22},{7,23},{8,24},{9,... | collective-permute-start | bytes 135176 | tf_op jit(solution)/shard_map/ppermute | solution.py:152
  82.6 2.3 %collective-permute-done.22 = bf16[32,704]{1,0:T(8,128)(2,1)S(1)} collective-permute-done((bf16[32,704]{1,0:T(8,128)(2,1)S(1)}, bf16[32,704]{1,0:T(8,128)(2,1)S(1)}, u32[]{:S(2)}, u32[]{:S(2)}) %collective-permute-start.22) | collective-permute-done | bytes 45088 | tf_op jit(solution)/shard_map/ppermute | solution.py:152
  84.9 1.6 %collective-permute-start.23 = (bf16[1,32,704]{2,1,0:T(8,128)(2,1)S(1)}, bf16[1,32,704]{2,1,0:T(8,128)(2,1)S(1)}, u32[]{:S(2)}, u32[]{:S(2)}) collective-permute-start(bf16[1,32,704]{2,1,0:T(8,128)(2,1)S(1)} %fusion.76), channel_id=1, source_target_pairs={{0,2},{1,3},{2,0},{3,1},{4,6},{5,7},{6,4},{7,5},{8,10},{9,11},{10,... | collective-permute-start | bytes 135176 | tf_op jit(solution)/shard_map/ppermute | solution.py:48
  86.5 2.5 %collective-permute-done.23 = bf16[1,32,704]{2,1,0:T(8,128)(2,1)S(1)} collective-permute-done((bf16[1,32,704]{2,1,0:T(8,128)(2,1)S(1)}, bf16[1,32,704]{2,1,0:T(8,128)(2,1)S(1)}, u32[]{:S(2)}, u32[]{:S(2)}) %collective-permute-start.23) | collective-permute-done | bytes 45088 | tf_op jit(solution)/shard_map/ppermute | solution.py:48
  89.2 0.7 pad_maximum_fusion.13
  90.6 0.9 copy.67
  (155 shorter events, 16.3 us)
Async XLA Ops:
  0.6 4.5 %copy-start = (bf16[1,343,343]{2,1,0:T(8,128)(2,1)S(1)}, bf16[1,343,343]{2,1,0:T(8,128)(2,1)}, u32[]{:S(2)}) copy-start(bf16[1,343,343]{2,1,0:T(8,128)(2,1)} %param.8) | copy-start | bytes 705898
  1.8 3.1 %copy-start.4 = (s32[1,343]{1,0:T(1,128)S(1)}, s32[1,343]{1,0:T(1,128)}, u32[]{:S(2)}) copy-start(s32[1,343]{1,0:T(1,128)} %param.9) | copy-start | bytes 4120
  1.9 3.0 %copy-start.3 = (f32[343]{0:T(512)S(1)}, f32[343]{0:T(512)}, u32[]{:S(2)}) copy-start(f32[343]{0:T(512)} %param.10) | copy-start | bytes 4120
  1.9 4.9 %collective-permute-start.2 = (bf16[108,128]{1,0:T(8,128)(2,1)S(1)}, bf16[108,128]{1,0:T(8,128)(2,1)S(1)}, u32[]{:S(2)}, u32[]{:S(2)}) collective-permute-start(bf16[108,128]{1,0:T(8,128)(2,1)S(1)} %pad_maximum_fusion.19), channel_id=1, source_target_pairs={{0,2},{1,3},{2,0},{3,1},{4,6},{5,7},{6,4},{7,5},{8,10},{9,11},{10,... | collective-permute-start | bytes 82952 | tf_op jit(solution)/shard_map/ppermute | solution.py:48
  6.0 11.0 %collective-permute-start = (bf16[1,343,345]{2,1,0:T(8,128)(2,1)S(1)}, bf16[1,343,345]{2,1,0:T(8,128)(2,1)S(1)}, u32[]{:S(2)}, u32[]{:S(2)}) collective-permute-start(bf16[1,343,345]{2,1,0:T(8,128)(2,1)S(1)} %maximum_bitcast_fusion), channel_id=1, source_target_pairs={{0,2},{1,3},{2,0},{3,1},{4,6},{5,7},{6,4},{7,5},{8,10},{9,11},{10,... | collective-permute-start | bytes 710018 | tf_op jit(solution)/shard_map/ppermute | solution.py:48
  6.7 0.8 copy-start.1
  7.8 1.3 %collective-permute-start.3 = (bf16[108,128]{1,0:T(8,128)(2,1)S(1)}, bf16[108,128]{1,0:T(8,128)(2,1)S(1)}, u32[]{:S(2)}, u32[]{:S(2)}) collective-permute-start(bf16[108,128]{1,0:T(8,128)(2,1)S(1)} %pad_maximum_fusion.20), channel_id=1, source_target_pairs={{0,1},{1,0},{2,3},{3,2},{4,5},{5,4},{6,7},{7,6},{8,9},{9,8},{10,11... | collective-permute-start | bytes 82952 | tf_op jit(solution)/shard_map/ppermute | solution.py:48
  9.8 5.6 %collective-permute-start.5 = (bf16[7,1,7,128]{3,2,1,0:T(8,128)(2,1)S(1)}, bf16[7,1,7,128]{3,2,1,0:T(8,128)(2,1)S(1)}, u32[]{:S(2)}, u32[]{:S(2)}) collective-permute-start(bf16[7,1,7,128]{3,2,1,0:T(8,128)(2,1)S(1)} %slice.488), channel_id=1, source_target_pairs={{4,8},{8,4},{5,9},{9,5},{6,10},{10,6},{7,11},{11,7},{20,24},{24,20... | collective-permute-start | bytes 37640 | tf_op jit(solution)/shard_map/ppermute | solution.py:36
  10.4 6.6 %collective-permute-start.4 = (bf16[7,1,7,128]{3,2,1,0:T(8,128)(2,1)S(1)}, bf16[7,1,7,128]{3,2,1,0:T(8,128)(2,1)S(1)}, u32[]{:S(2)}, u32[]{:S(2)}) collective-permute-start(bf16[7,1,7,128]{3,2,1,0:T(8,128)(2,1)S(1)} %slice.488), channel_id=1, source_target_pairs={{0,4},{4,0},{1,5},{5,1},{2,6},{6,2},{3,7},{7,3},{8,12},{12,8},{9,1... | collective-permute-start | bytes 37640 | tf_op jit(solution)/shard_map/ppermute | solution.py:36
  17.7 4.9 %collective-permute-start.1 = (bf16[2,343,345]{2,0,1:T(2,128)(2,1)S(1)}, bf16[2,343,345]{2,0,1:T(2,128)(2,1)S(1)}, u32[]{:S(2)}, u32[]{:S(2)}) collective-permute-start(bf16[2,343,345]{2,0,1:T(2,128)(2,1)S(1)} %copy.64), channel_id=1, source_target_pairs={{0,1},{1,0},{2,3},{3,2},{4,5},{5,4},{6,7},{7,6},{8,9},{9,8},{10,11... | collective-permute-start | bytes 1420028 | tf_op jit(solution)/shard_map/ppermute | solution.py:48
  17.8 4.7 %collective-permute-start.6 = (bf16[1,7,7,128]{3,2,1,0:T(8,128)(2,1)S(1)}, bf16[1,7,7,128]{3,2,1,0:T(8,128)(2,1)S(1)}, u32[]{:S(2)}, u32[]{:S(2)}) collective-permute-start(bf16[1,7,7,128]{3,2,1,0:T(8,128)(2,1)S(1)} %pad_maximum_fusion.23), channel_id=1, source_target_pairs={{0,16},{16,0},{1,17},{17,1},{2,18},{18,2},{3,19},{19,3},{4,20},{20... | collective-permute-start | bytes 37640 | tf_op jit(solution)/shard_map/ppermute | solution.py:36
  25.1 5.4 %collective-permute-start.8 = (bf16[7,1,7,128]{3,2,1,0:T(8,128)(2,1)S(1)}, bf16[7,1,7,128]{3,2,1,0:T(8,128)(2,1)S(1)}, u32[]{:S(2)}, u32[]{:S(2)}) collective-permute-start(bf16[7,1,7,128]{3,2,1,0:T(8,128)(2,1)S(1)} %broadcast_select_fusion.38), channel_id=1, source_target_pairs={{4,8},{8,4},{5,9},{9,5},{6,10},{10,6},{7,11},{11,7},{20,24},{24,20... | collective-permute-start | bytes 37640 | tf_op jit(solution)/shard_map/ppermute | solution.py:36
  25.8 6.4 %collective-permute-start.7 = (bf16[7,1,7,128]{3,2,1,0:T(8,128)(2,1)S(1)}, bf16[7,1,7,128]{3,2,1,0:T(8,128)(2,1)S(1)}, u32[]{:S(2)}, u32[]{:S(2)}) collective-permute-start(bf16[7,1,7,128]{3,2,1,0:T(8,128)(2,1)S(1)} %get-tuple-element.33), channel_id=1, source_target_pairs={{0,4},{4,0},{1,5},{5,1},{2,6},{6,2},{3,7},{7,3},{8,12},{12,8},{9,1... | collective-permute-start | bytes 37640 | tf_op jit(solution)/shard_map/ppermute | solution.py:36
  32.3 4.7 %collective-permute-start.9 = (bf16[1,7,7,128]{3,2,1,0:T(8,128)(2,1)S(1)}, bf16[1,7,7,128]{3,2,1,0:T(8,128)(2,1)S(1)}, u32[]{:S(2)}, u32[]{:S(2)}) collective-permute-start(bf16[1,7,7,128]{3,2,1,0:T(8,128)(2,1)S(1)} %fusion.95), channel_id=1, source_target_pairs={{0,16},{16,0},{1,17},{17,1},{2,18},{18,2},{3,19},{19,3},{4,20},{20... | collective-permute-start | bytes 37640 | tf_op jit(solution)/shard_map/ppermute | solution.py:36
  38.6 5.5 %collective-permute-start.11 = (bf16[7,1,7,128]{3,2,1,0:T(8,128)(2,1)S(1)}, bf16[7,1,7,128]{3,2,1,0:T(8,128)(2,1)S(1)}, u32[]{:S(2)}, u32[]{:S(2)}) collective-permute-start(bf16[7,1,7,128]{3,2,1,0:T(8,128)(2,1)S(1)} %broadcast_select_fusion.37), channel_id=1, source_target_pairs={{4,8},{8,4},{5,9},{9,5},{6,10},{10,6},{7,11},{11,7},{20,24},{24,20... | collective-permute-start | bytes 37640 | tf_op jit(solution)/shard_map/ppermute | solution.py:36
  39.3 6.5 %collective-permute-start.10 = (bf16[7,1,7,128]{3,2,1,0:T(8,128)(2,1)S(1)}, bf16[7,1,7,128]{3,2,1,0:T(8,128)(2,1)S(1)}, u32[]{:S(2)}, u32[]{:S(2)}) collective-permute-start(bf16[7,1,7,128]{3,2,1,0:T(8,128)(2,1)S(1)} %get-tuple-element.30), channel_id=1, source_target_pairs={{0,4},{4,0},{1,5},{5,1},{2,6},{6,2},{3,7},{7,3},{8,12},{12,8},{9,1... | collective-permute-start | bytes 37640 | tf_op jit(solution)/shard_map/ppermute | solution.py:36
  45.9 4.7 %collective-permute-start.12 = (bf16[1,7,7,128]{3,2,1,0:T(8,128)(2,1)S(1)}, bf16[1,7,7,128]{3,2,1,0:T(8,128)(2,1)S(1)}, u32[]{:S(2)}, u32[]{:S(2)}) collective-permute-start(bf16[1,7,7,128]{3,2,1,0:T(8,128)(2,1)S(1)} %fusion.96), channel_id=1, source_target_pairs={{0,16},{16,0},{1,17},{17,1},{2,18},{18,2},{3,19},{19,3},{4,20},{20... | collective-permute-start | bytes 37640 | tf_op jit(solution)/shard_map/ppermute | solution.py:36
  52.1 3.0 %copy-start.2 = (bf16[216,704]{1,0:T(8,128)(2,1)S(1)}, bf16[216,704]{1,0:T(8,128)(2,1)}, u32[]{:S(2)}) copy-start(bf16[216,704]{1,0:T(8,128)(2,1)} %param.11) | copy-start | bytes 912388
  52.2 4.5 %collective-permute-start.13 = (bf16[7,1,7,128]{3,2,1,0:T(8,128)(2,1)S(1)}, bf16[7,1,7,128]{3,2,1,0:T(8,128)(2,1)S(1)}, u32[]{:S(2)}, u32[]{:S(2)}) collective-permute-start(bf16[7,1,7,128]{3,2,1,0:T(8,128)(2,1)S(1)} %get-tuple-element.52), channel_id=1, source_target_pairs={{0,4},{4,0},{1,5},{5,1},{2,6},{6,2},{3,7},{7,3},{8,12},{12,8},{9,1... | collective-permute-start | bytes 37640 | tf_op jit(solution)/shard_map/ppermute | solution.py:36
  54.3 2.4 %collective-permute-start.14 = (bf16[7,1,7,128]{3,2,1,0:T(8,128)(2,1)S(1)}, bf16[7,1,7,128]{3,2,1,0:T(8,128)(2,1)S(1)}, u32[]{:S(2)}, u32[]{:S(2)}) collective-permute-start(bf16[7,1,7,128]{3,2,1,0:T(8,128)(2,1)S(1)} %get-tuple-element.53), channel_id=1, source_target_pairs={{4,8},{8,4},{5,9},{9,5},{6,10},{10,6},{7,11},{11,7},{20,24},{24,20... | collective-permute-start | bytes 37640 | tf_op jit(solution)/shard_map/ppermute | solution.py:36
  55.1 10.7 %collective-permute-start.18 = (bf16[1,216,704]{2,1,0:T(8,128)(2,1)S(1)}, bf16[1,216,704]{2,1,0:T(8,128)(2,1)S(1)}, u32[]{:S(2)}, u32[]{:S(2)}) collective-permute-start(bf16[1,216,704]{2,1,0:T(8,128)(2,1)S(1)} %bitcast.43), channel_id=1, source_target_pairs={{0,2},{1,3},{2,0},{3,1},{4,6},{5,7},{6,4},{7,5},{8,10},{9,11},{10,... | collective-permute-start | bytes 912392 | tf_op jit(solution)/shard_map/ppermute | solution.py:48
  56.8 4.7 %collective-permute-start.15 = (bf16[1,7,7,128]{3,2,1,0:T(8,128)(2,1)S(1)}, bf16[1,7,7,128]{3,2,1,0:T(8,128)(2,1)S(1)}, u32[]{:S(2)}, u32[]{:S(2)}) collective-permute-start(bf16[1,7,7,128]{3,2,1,0:T(8,128)(2,1)S(1)} %fusion.97), channel_id=1, source_target_pairs={{0,16},{16,0},{1,17},{17,1},{2,18},{18,2},{3,19},{19,3},{4,20},{20... | collective-permute-start | bytes 37640 | tf_op jit(solution)/shard_map/ppermute | solution.py:36
  61.9 3.9 %collective-permute-start.16 = (bf16[108,128]{1,0:T(8,128)(2,1)S(1)}, bf16[108,128]{1,0:T(8,128)(2,1)S(1)}, u32[]{:S(2)}, u32[]{:S(2)}) collective-permute-start(bf16[108,128]{1,0:T(8,128)(2,1)S(1)} %pad_maximum_fusion.21), channel_id=1, source_target_pairs={{0,2},{1,3},{2,0},{3,1},{4,6},{5,7},{6,4},{7,5},{8,10},{9,11},{10,... | collective-permute-start | bytes 82952 | tf_op jit(solution)/shard_map/ppermute | solution.py:48
  66.0 2.2 %collective-permute-start.19 = (bf16[2,216,704]{2,1,0:T(8,128)(2,1)S(1)}, bf16[2,216,704]{2,1,0:T(8,128)(2,1)S(1)}, u32[]{:S(2)}, u32[]{:S(2)}) collective-permute-start(bf16[2,216,704]{2,1,0:T(8,128)(2,1)S(1)} %pad_maximum_fusion), channel_id=1, source_target_pairs={{0,1},{1,0},{2,3},{3,2},{4,5},{5,4},{6,7},{7,6},{8,9},{9,8},{10,11... | collective-permute-start | bytes 1824776 | tf_op jit(solution)/shard_map/ppermute | solution.py:48
  69.4 6.2 %collective-permute-start.20 = (bf16[32,704]{1,0:T(8,128)(2,1)S(1)}, bf16[32,704]{1,0:T(8,128)(2,1)S(1)}, u32[]{:S(2)}, u32[]{:S(2)}) collective-permute-start(bf16[32,704]{1,0:T(8,128)(2,1)S(1)} %fusion.2), channel_id=1, source_target_pairs={{0,4},{1,5},{2,6},{3,7},{4,0},{5,1},{6,2},{7,3},{8,12},{9,13},{10,... | collective-permute-start | bytes 135176 | tf_op jit(solution)/shard_map/ppermute | solution.py:152
  73.7 4.0 %collective-permute-start.17 = (bf16[108,128]{1,0:T(8,128)(2,1)S(1)}, bf16[108,128]{1,0:T(8,128)(2,1)S(1)}, u32[]{:S(2)}, u32[]{:S(2)}) collective-permute-start(bf16[108,128]{1,0:T(8,128)(2,1)S(1)} %pad_maximum_fusion.22), channel_id=1, source_target_pairs={{0,1},{1,0},{2,3},{3,2},{4,5},{5,4},{6,7},{7,6},{8,9},{9,8},{10,11... | collective-permute-start | bytes 82952 | tf_op jit(solution)/shard_map/ppermute | solution.py:48
  75.7 4.2 %collective-permute-start.21 = (bf16[32,704]{1,0:T(8,128)(2,1)S(1)}, bf16[32,704]{1,0:T(8,128)(2,1)S(1)}, u32[]{:S(2)}, u32[]{:S(2)}) collective-permute-start(bf16[32,704]{1,0:T(8,128)(2,1)S(1)} %add_convert_fusion.2), channel_id=1, source_target_pairs={{0,8},{1,9},{2,10},{3,11},{4,12},{5,13},{6,14},{7,15},{8,0},{9,1},... | collective-permute-start | bytes 135176 | tf_op jit(solution)/shard_map/ppermute | solution.py:152
  79.8 5.1 %collective-permute-start.22 = (bf16[32,704]{1,0:T(8,128)(2,1)S(1)}, bf16[32,704]{1,0:T(8,128)(2,1)S(1)}, u32[]{:S(2)}, u32[]{:S(2)}) collective-permute-start(bf16[32,704]{1,0:T(8,128)(2,1)S(1)} %add_convert_fusion.1), channel_id=1, source_target_pairs={{0,16},{1,17},{2,18},{3,19},{4,20},{5,21},{6,22},{7,23},{8,24},{9,... | collective-permute-start | bytes 135176 | tf_op jit(solution)/shard_map/ppermute | solution.py:152
  84.9 4.2 %collective-permute-start.23 = (bf16[1,32,704]{2,1,0:T(8,128)(2,1)S(1)}, bf16[1,32,704]{2,1,0:T(8,128)(2,1)S(1)}, u32[]{:S(2)}, u32[]{:S(2)}) collective-permute-start(bf16[1,32,704]{2,1,0:T(8,128)(2,1)S(1)} %fusion.76), channel_id=1, source_target_pairs={{0,2},{1,3},{2,0},{3,1},{4,6},{5,7},{6,4},{7,5},{8,10},{9,11},{10,... | collective-permute-start | bytes 135176 | tf_op jit(solution)/shard_map/ppermute | solution.py:48
  89.1 1.4 %collective-permute-start.24 = (bf16[2,32,704]{2,1,0:T(8,128)(2,1)S(1)}, bf16[2,32,704]{2,1,0:T(8,128)(2,1)S(1)}, u32[]{:S(2)}, u32[]{:S(2)}) collective-permute-start(bf16[2,32,704]{2,1,0:T(8,128)(2,1)S(1)} %pad_maximum_fusion.3), channel_id=1, source_target_pairs={{0,1},{1,0},{2,3},{3,2},{4,5},{5,4},{6,7},{7,6},{8,9},{9,8},{10,11... | collective-permute-start | bytes 270344 | tf_op jit(solution)/shard_map/ppermute | solution.py:48

commit v4 on v3

--- a/solution.py
+++ b/solution.py
@@ -71,26 +71,39 @@
     return [held[order.index(i)] for i in range(GRID_Z)]
 
 
-def lines_transposed(grid, value):
-    rows, columns = value.shape
-    width = columns // GRID_Z
-    blocks = [value[:, i * width : (i + 1) * width] for i in range(GRID_Z)]
-    half = rows // 2
-    for bit in line_bits():
-        mine = grid.has(bit)
+class Shares:
+    def __init__(self, grid, value):
+        self.grid = grid
+        self.width = value.shape[1] // GRID_Z
+        self.half = value.shape[0] // 2
+        self.blocks = [
+            value[:, i * self.width : (i + 1) * self.width] for i in range(GRID_Z)
+        ]
+
+    def packed(self, bit):
+        mine = self.grid.has(bit)
+        away = [
+            jnp.where(mine, self.blocks[i], self.blocks[i | bit])
+            for i in range(GRID_Z)
+            if not i & bit
+        ]
+        return jnp.concatenate(
+            [b[h : h + self.half] for h in (0, self.half) for b in away], axis=1
+        )
+
+    def take(self, bit, arrived):
+        mine = self.grid.has(bit)
         lows = [i for i in range(GRID_Z) if not i & bit]
-        away = [jnp.where(mine, blocks[i], blocks[i | bit]) for i in lows]
-        packed = jnp.concatenate([b[h : h + half] for h in (0, half) for b in away], axis=1)
-        arrived = grid.partner(packed, bit)
         for at, i in enumerate(lows):
-            first = arrived[:, at * width : (at + 1) * width]
-            second = arrived[:, (at + len(lows)) * width : (at + len(lows) + 1) * width]
-            came = jnp.concatenate([first, second], axis=0)
-            blocks[i], blocks[i | bit] = (
-                jnp.where(mine, came, blocks[i]),
-                jnp.where(mine, blocks[i | bit], came),
+            ends = (at * self.width, (at + len(lows)) * self.width)
+            came = jnp.concatenate([arrived[:, e : e + self.width] for e in ends], axis=0)
+            self.blocks[i], self.blocks[i | bit] = (
+                jnp.where(mine, came, self.blocks[i]),
+                jnp.where(mine, self.blocks[i | bit], came),
             )
-    return jnp.concatenate(blocks, axis=1)
+
+    def value(self):
+        return jnp.concatenate(self.blocks, axis=1)
 
 
 def plane(field, dim, at):
@@ -135,12 +148,14 @@
     return lax.reduce_precision(value, 8, 7).astype(jnp.bfloat16)
 
 
-def summed_over_lines(grid, value):
-    left = grid.devices // GRID_Z
-    stride = GRID_Z
+def plus(first, second):
+    return (first.astype(jnp.float32) + second.astype(jnp.float32)).astype(jnp.bfloat16)
+
+
+def summed_along(grid, value, stride, count):
     factor = 2
-    while left > 1:
-        while left % factor:
+    while count > 1:
+        while count % factor:
             factor += 1
         at = grid.position // stride % factor
         terms = [value]
@@ -151,7 +166,7 @@
                 pairs.append((i, i + ((c + turn) % factor - c) * stride))
             terms.append(lax.ppermute(value, AXIS, pairs))
         if factor == 2:
-            total = terms[0].astype(jnp.float32) + terms[1].astype(jnp.float32)
+            value = plus(*terms)
         else:
             total = 0.0
             for k in range(factor):
@@ -159,8 +174,8 @@
                 for turn in range(1, factor):
                     term = jnp.where((at - turn) % factor == k, terms[turn], term)
                 total = total + term.astype(jnp.float32)
-        value = total.astype(jnp.bfloat16)
-        left //= factor
+            value = total.astype(jnp.bfloat16)
+        count //= factor
         stride *= factor
     return value
 
@@ -184,11 +199,13 @@
         both = jnp.sum(matrices[p][:, slot_count:].astype(jnp.float32), axis=1, keepdims=True)
         lumped = jnp.where(lane_owner == p, both, lumped)
 
-    mine = lines_transposed(grid, block)
+    shares = Shares(grid, block)
+    for bit in line_bits():
+        shares.take(bit, grid.partner(shares.packed(bit), bit))
     field = (
         jnp.zeros(shape, jnp.bfloat16)
         .at[1:, 1:, 1:]
-        .set(mine.reshape(edge, edge, edge, columns))
+        .set(shares.value().reshape(edge, edge, edge, columns))
     )
     field = with_ends(field, 2, to_next_partition(plane(field, 2, SIDE - 1), width), None)
     for dim in (1, 0):
@@ -200,6 +217,11 @@
     for dim in range(3):
         at = lax.broadcasted_iota(jnp.int32, shape, dim)
         inside = inside & ~((at == 0) & first[dim])
+
+    locked, field = lax.optimization_barrier((locked, field))
+    above = locked[-edge * edge :]
+    below = grid.exchanged(above, above, 0)[0]
+    locked = jnp.concatenate([below, locked], axis=0)
 
     older = field
     current = field
@@ -220,6 +242,11 @@
             low + to_next_partition(high, width),
             high + to_previous_partition(low, width),
         )
+        if step == 0:
+            locked, partial = lax.optimization_barrier((locked, partial))
+            all_locked = lines_gathered(grid, locked)
+        if step == steps - 1:
+            break
         for dim in (1, 0):
             low, high = plane(partial, dim, 0), plane(partial, dim, SIDE - 1)
             to_low, to_high = grid.exchanged(
@@ -228,7 +255,7 @@
             partial = with_ends(
                 partial,
                 dim,
-                None if step == steps - 1 else low + to_low.astype(jnp.float32),
+                low + to_low.astype(jnp.float32),
                 high + to_high.astype(jnp.float32),
             )
         following = coeffs[0] * (partial - centre * current.astype(jnp.float32)) - coeffs[
@@ -237,22 +264,71 @@
         following = rounded(jnp.where(inside, following, 0.0))
         older = current
         current = following
-        if step == 0:
-            locked, current = lax.optimization_barrier((locked, current))
-            all_locked = lines_gathered(grid, locked)
-    filtered = current[1:, 1:, 1:].reshape(owned_rows, columns)
-
-    share = jnp.zeros((width, locked.shape[1]), jnp.float32)
+        if step == 1:
+            current, all_locked = lax.optimization_barrier((current, all_locked))
+
+    low = plane(partial, 1, 0).astype(jnp.bfloat16)
+    to_high = grid.exchanged(low, low, 1)[1].astype(jnp.float32)
+    partial = with_ends(partial, 1, None, plane(partial, 1, SIDE - 1) + to_high)
+    partial = coeffs[0] * partial[:, 1:, 1:].reshape(SIDE, edge * edge, columns)
+
+    def owned(field):
+        return field[1:, 1:, 1:].reshape(edge, edge * edge, columns).astype(jnp.float32)
+
+    rest = -coeffs[0] * centre * owned(current) - coeffs[1] * owned(older)
+    sums = jnp.concatenate([partial[:1], partial[1:] + rest], axis=0)
+    weights = sums.astype(jnp.bfloat16).reshape(SIDE * edge * edge, columns)
+    share = 0.0
     for p in range(GRID_Z):
         share = share + lax.dot_general(
-            filtered[:, p * width : (p + 1) * width],
             all_locked[p],
+            weights[:, p * width : (p + 1) * width],
             (((0,), (0,)), ((), ())),
             preferred_element_type=jnp.float32,
         )
-    share = summed_over_lines(grid, share.astype(jnp.bfloat16))
-    intersection = jnp.concatenate(lines_gathered(grid, share)).T.astype(jnp.float32)
-    return lines_transposed(grid, filtered), intersection
+    deep = share.shape[0] // GRID_Z
+    share = jnp.concatenate(
+        [share[i * deep : (i + 1) * deep] for i in range(GRID_Z)], axis=1
+    ).astype(jnp.bfloat16)
+
+    low = sums[0].astype(jnp.bfloat16)
+    stride, count = grid.stride[0], grid.counts[0]
+    even = grid.coords[0] % 2 == 0
+    arrived = grid.partner(jnp.concatenate([share, low], axis=0), stride)
+    share = plus(share, arrived[:deep])
+    to_high = jnp.where(even, arrived[deep:], jnp.zeros_like(low))
+    if count > 2:
+        to_high = to_high + grid.swapped(low, low, 0, 1)[1]
+    sums = jnp.concatenate(
+        [sums[1:edge], sums[edge:] + to_high[None].astype(jnp.float32)], axis=0
+    )
+    filtered = rounded(sums.reshape(owned_rows, columns))
+
+    share = summed_along(grid, share, grid.stride[1], grid.counts[1])
+    share = summed_along(grid, share, stride * 2, count // 2)
+
+    shares = Shares(grid, filtered)
+    held = share[None]
+    order = [0]
+    for bit in line_bits():
+        mine = grid.has(bit)
+        sent = held.reshape(-1, columns)
+        arrived = grid.partner(jnp.concatenate([sent, shares.packed(bit)], axis=0), bit)
+        shares.take(bit, arrived[sent.shape[0] :])
+        other = arrived[: sent.shape[0]].reshape(held.shape)
+        held = jnp.concatenate(
+            [jnp.where(mine, other, held), jnp.where(mine, held, other)], axis=0
+        )
+        order = order + [i | bit for i in order]
+    held = [held[order.index(i)] for i in range(GRID_Z)]
+    intersection = jnp.concatenate(
+        [
+            jnp.concatenate([h[:, q * width : (q + 1) * width] for h in held], axis=1)
+            for q in range(GRID_Z)
+        ],
+        axis=0,
+    ).astype(jnp.float32)
+    return shares.value(), intersection
 
 
 def solution(mesh):

time: 91.7 us -> 96.3 us (1.050)
  waiting for transfers between devices: 28.6 us -> 33.2 us
  local copies, waits for them, and re-layouts: 3.63 us -> 7.76 us
  starting transfers between devices: 46.6 us -> 44 us
  other arithmetic: 6.31 us -> 4.56 us
    ppermute x12, waiting for transfers between devices: 13.1 us -> 21.4 us  [swapped(): arrived = lax.ppermute(jnp.where(lower, high, low), AXIS, pairs)]
    ppermute x12, starting transfers between devices: 29.8 us -> 26.7 us  [swapped(): arrived = lax.ppermute(jnp.where(lower, high, low), AXIS, pairs)]
    ppermute x3 -> x2, waiting for transfers between devices: 6.21 us -> 3.87 us  [summed_along(): terms.append(lax.ppermute(value, AXIS, pairs))]
    slice x11 -> x28, local copies, waits for them, and re-layouts: 0.45 us -> 2.51 us  [the longest x2 1.18 us: __init__(): value[:, i * self.width:(i + 1) * self.width]]
    ppermute x10 -> x9, starting transfers between devices: 7.96 us -> 9.93 us  [partner(): lax.ppermute(value, AXIS, [(i, i ^ bit) for i in range(self.devices)])]
    ppermute x3 -> x2, starting transfers between devices: 8.83 us -> 7.32 us  [summed_along(): terms.append(lax.ppermute(value, AXIS, pairs))]
    ppermute x10 -> x9, waiting for transfers between devices: 9.31 us -> 7.93 us  [partner(): lax.ppermute(value, AXIS, [(i, i ^ bit) for i in range(self.devices)])]
    select_n x8 -> x11, other arithmetic: 1.85 us -> 0.63 us  [the longest x4 0.36 us: take(): jnp.where(mine, came, self.blocks[i])]
  transfers between devices with their start and end apart: 25 -> 23, of which waited for: 16 -> 15; matrix products, arithmetic and copies ran while one was open for 4% -> 5% of each run, Pallas kernels for 0% -> 0%
where the time goes in v4:
time: 96.3 us; the launch traced here: 96 us
  starting transfers between devices  44 us (46%)
  waiting for transfers between devices  33.2 us (34%)
  local copies, waits for them, and re-layouts  7.76 us (8%)
  matrix products  4.92 us (5%)
  other arithmetic  4.56 us (5%)
  between operations  1.58 us (2%)
    ppermute x12, starting transfers between devices, swapped(): arrived = lax.ppermute(jnp.where(lower, high, low), AXIS, pairs)  26.7 us
    ppermute x12, waiting for transfers between devices, swapped(): arrived = lax.ppermute(jnp.where(lower, high, low), AXIS, pairs)  21.4 us
    ppermute x9, starting transfers between devices, partner(): lax.ppermute(value, AXIS, [(i, i ^ bit) for i in range(self.devices)])  9.93 us
    ppermute x9, waiting for transfers between devices, partner(): lax.ppermute(value, AXIS, [(i, i ^ bit) for i in range(self.devices)])  7.93 us
    ppermute x2, starting transfers between devices, summed_along(): terms.append(lax.ppermute(value, AXIS, pairs))  7.32 us
    ppermute x2, waiting for transfers between devices, summed_along(): terms.append(lax.ppermute(value, AXIS, pairs))  3.87 us
    dot_general x12, matrix products, per_device(): jnp.dot(matrices[p][:, :slot_count], own, preferred_element_type=jnp.floa...  3.04 us
    unnamed x18, local copies, waits for them, and re-layouts  2.73 us
  transfers between devices with their start and end apart: 23, of which 15 were waited for; matrix products, arithmetic and copies ran while one was open for 5% of the time, Pallas kernels for 0%

profile of v4, /device:TPU:0, one launch (start us, length us, event | category | flops | bytes accessed | tf_op | source)
XLA Modules:
  0.0 96.0 jit_solution(4759942055850126906)
XLA Ops:
  0.6 1.1 %fusion.108 = (bf16[216,32]{1,0:T(8,128)(2,1)S(1)}, bf16[216,32]{1,0:T(8,128)(2,1)S(1)}, bf16[216,32]{1,0:T(8,128)(2,1)S(1)}, bf16[216,32]{1,0:T(8,128)(2,1)S(1)}) fusion(bf16[216,128]{1,0:T(8,128)(2,1)} %param.7), kind=kLoop, calls=%fused_computation.272 | loop fusion | bytes 110592 | tf_op jit(solution)/shard_map/slice | solution.py:80
  2.3 3.0 %collective-permute-start.2 = (bf16[108,128]{0,1:T(8,128)(2,1)S(1)}, bf16[108,128]{0,1:T(8,128)(2,1)S(1)}, u32[]{:S(2)}, u32[]{:S(2)}) collective-permute-start(bf16[108,128]{0,1:T(8,128)(2,1)S(1)} %pad_maximum_fusion.11), channel_id=1, source_target_pairs={{0,2},{1,3},{2,0},{3,1},{4,6},{5,7},{6,4},{7,5},{8,10},{9,11},{10,... | collective-permute-start | bytes 82952 | tf_op jit(solution)/shard_map/ppermute | solution.py:48
  5.6 0.7 convolution_convert_fusion
  7.5 1.2 %collective-permute-done.3 = bf16[108,128]{0,1:T(8,128)(2,1)S(1)} collective-permute-done((bf16[108,128]{0,1:T(8,128)(2,1)S(1)}, bf16[108,128]{0,1:T(8,128)(2,1)S(1)}, u32[]{:S(2)}, u32[]{:S(2)}) %collective-permute-start.3) | collective-permute-done | bytes 27680 | tf_op jit(solution)/shard_map/ppermute | solution.py:48
  9.3 0.7 collective-permute-start.5
  9.9 4.9 %collective-permute-start.4 = (bf16[7,1,7,128]{3,2,1,0:T(8,128)(2,1)S(1)}, bf16[7,1,7,128]{3,2,1,0:T(8,128)(2,1)S(1)}, u32[]{:S(2)}, u32[]{:S(2)}) collective-permute-start(bf16[7,1,7,128]{3,2,1,0:T(8,128)(2,1)S(1)} %slice.634), channel_id=1, source_target_pairs={{0,4},{4,0},{1,5},{5,1},{2,6},{6,2},{3,7},{7,3},{8,12},{12,8},{9,1... | collective-permute-start | bytes 37640 | tf_op jit(solution)/shard_map/ppermute | solution.py:36
  14.8 1.7 %collective-permute-done.4 = bf16[7,1,7,128]{3,2,1,0:T(8,128)(2,1)S(1)} collective-permute-done((bf16[7,1,7,128]{3,2,1,0:T(8,128)(2,1)S(1)}, bf16[7,1,7,128]{3,2,1,0:T(8,128)(2,1)S(1)}, u32[]{:S(2)}, u32[]{:S(2)}) %collective-permute-start.4) | collective-permute-done | bytes 12576 | tf_op jit(solution)/shard_map/ppermute | solution.py:36
  16.5 2.7 %collective-permute-start.6 = (bf16[1,7,7,128]{3,2,1,0:T(8,128)(2,1)S(1)}, bf16[1,7,7,128]{3,2,1,0:T(8,128)(2,1)S(1)}, u32[]{:S(2)}, u32[]{:S(2)}) collective-permute-start(bf16[1,7,7,128]{3,2,1,0:T(8,128)(2,1)S(1)} %pad_maximum_fusion.25), channel_id=1, source_target_pairs={{0,16},{16,0},{1,17},{17,1},{2,18},{18,2},{3,19},{19,3},{4,20},{20... | collective-permute-start | bytes 37640 | tf_op jit(solution)/shard_map/ppermute | solution.py:36
  19.2 2.0 %collective-permute-done.6 = bf16[1,7,7,128]{3,2,1,0:T(8,128)(2,1)S(1)} collective-permute-done((bf16[1,7,7,128]{3,2,1,0:T(8,128)(2,1)S(1)}, bf16[1,7,7,128]{3,2,1,0:T(8,128)(2,1)S(1)}, u32[]{:S(2)}, u32[]{:S(2)}) %collective-permute-start.6) | collective-permute-done | bytes 12576 | tf_op jit(solution)/shard_map/ppermute | solution.py:36
  22.8 2.7 %collective-permute-start.7 = (bf16[36,704]{0,1:T(8,128)(2,1)S(1)}, bf16[36,704]{0,1:T(8,128)(2,1)S(1)}, u32[]{:S(2)}, u32[]{:S(2)}) collective-permute-start(bf16[36,704]{0,1:T(8,128)(2,1)S(1)} %slice.636), channel_id=1, source_target_pairs={{0,16},{16,0},{1,17},{17,1},{2,18},{18,2},{3,19},{19,3},{4,20},{20... | collective-permute-start | bytes 152072 | tf_op jit(solution)/shard_map/ppermute | solution.py:36
  25.5 8.6 %collective-permute-done.7 = bf16[36,704]{0,1:T(8,128)(2,1)S(1)} collective-permute-done((bf16[36,704]{0,1:T(8,128)(2,1)S(1)}, bf16[36,704]{0,1:T(8,128)(2,1)S(1)}, u32[]{:S(2)}, u32[]{:S(2)}) %collective-permute-start.7) | collective-permute-done | bytes 50720 | tf_op jit(solution)/shard_map/ppermute | solution.py:36
  36.9 1.5 %collective-permute-start.8 = (bf16[7,1,7,128]{3,2,1,0:T(8,128)(2,1)S(1)}, bf16[7,1,7,128]{3,2,1,0:T(8,128)(2,1)S(1)}, u32[]{:S(2)}, u32[]{:S(2)}) collective-permute-start(bf16[7,1,7,128]{3,2,1,0:T(8,128)(2,1)S(1)} %get-tuple-element.76), channel_id=1, source_target_pairs={{0,4},{4,0},{1,5},{5,1},{2,6},{6,2},{3,7},{7,3},{8,12},{12,8},{9,1... | collective-permute-start | bytes 37640 | tf_op jit(solution)/shard_map/ppermute | solution.py:36
  39.1 1.6 %collective-permute-done.8 = bf16[7,1,7,128]{3,2,1,0:T(8,128)(2,1)S(1)} collective-permute-done((bf16[7,1,7,128]{3,2,1,0:T(8,128)(2,1)S(1)}, bf16[7,1,7,128]{3,2,1,0:T(8,128)(2,1)S(1)}, u32[]{:S(2)}, u32[]{:S(2)}) %collective-permute-start.8) | collective-permute-done | bytes 12576 | tf_op jit(solution)/shard_map/ppermute | solution.py:36
  40.9 1.6 %collective-permute-start.14 = (bf16[1,252,704]{1,2,0:T(8,128)(2,1)S(1)}, bf16[1,252,704]{1,2,0:T(8,128)(2,1)S(1)}, u32[]{:S(2)}, u32[]{:S(2)}) collective-permute-start(bf16[1,252,704]{1,2,0:T(8,128)(2,1)S(1)} %bitcast.50), channel_id=1, source_target_pairs={{0,2},{1,3},{2,0},{3,1},{4,6},{5,7},{6,4},{7,5},{8,10},{9,11},{10,... | collective-permute-start | bytes 1064456 | tf_op jit(solution)/shard_map/ppermute | solution.py:48
  42.4 3.0 %collective-permute-done.10 = bf16[1,7,7,128]{3,2,1,0:T(8,128)(2,1)S(1)} collective-permute-done((bf16[1,7,7,128]{3,2,1,0:T(8,128)(2,1)S(1)}, bf16[1,7,7,128]{3,2,1,0:T(8,128)(2,1)S(1)}, u32[]{:S(2)}, u32[]{:S(2)}) %collective-permute-start.10) | collective-permute-done | bytes 12576 | tf_op jit(solution)/shard_map/ppermute | solution.py:36
  47.7 7.2 %collective-permute-start.11 = (bf16[7,1,7,128]{3,2,1,0:T(8,128)(2,1)S(1)}, bf16[7,1,7,128]{3,2,1,0:T(8,128)(2,1)S(1)}, u32[]{:S(2)}, u32[]{:S(2)}) collective-permute-start(bf16[7,1,7,128]{3,2,1,0:T(8,128)(2,1)S(1)} %get-tuple-element.40), channel_id=1, source_target_pairs={{0,4},{4,0},{1,5},{5,1},{2,6},{6,2},{3,7},{7,3},{8,12},{12,8},{9,1... | collective-permute-start | bytes 37640 | tf_op jit(solution)/shard_map/ppermute | solution.py:36
  54.9 1.7 %collective-permute-done.11 = bf16[7,1,7,128]{3,2,1,0:T(8,128)(2,1)S(1)} collective-permute-done((bf16[7,1,7,128]{3,2,1,0:T(8,128)(2,1)S(1)}, bf16[7,1,7,128]{3,2,1,0:T(8,128)(2,1)S(1)}, u32[]{:S(2)}, u32[]{:S(2)}) %collective-permute-start.11) | collective-permute-done | bytes 12576 | tf_op jit(solution)/shard_map/ppermute | solution.py:36
  57.0 3.0 %collective-permute-start.13 = (bf16[1,7,7,128]{3,2,1,0:T(8,128)(2,1)S(1)}, bf16[1,7,7,128]{3,2,1,0:T(8,128)(2,1)S(1)}, u32[]{:S(2)}, u32[]{:S(2)}) collective-permute-start(bf16[1,7,7,128]{3,2,1,0:T(8,128)(2,1)S(1)} %fusion.84), channel_id=1, source_target_pairs={{0,16},{16,0},{1,17},{17,1},{2,18},{18,2},{3,19},{19,3},{4,20},{20... | collective-permute-start | bytes 37640 | tf_op jit(solution)/shard_map/ppermute | solution.py:36
  60.0 1.7 %collective-permute-done.13 = bf16[1,7,7,128]{3,2,1,0:T(8,128)(2,1)S(1)} collective-permute-done((bf16[1,7,7,128]{3,2,1,0:T(8,128)(2,1)S(1)}, bf16[1,7,7,128]{3,2,1,0:T(8,128)(2,1)S(1)}, u32[]{:S(2)}, u32[]{:S(2)}) %collective-permute-start.13) | collective-permute-done | bytes 12576 | tf_op jit(solution)/shard_map/ppermute | solution.py:36
  63.6 2.2 %collective-permute-start.16 = (bf16[7,1,7,128]{3,2,1,0:T(8,128)(2,1)S(1)}, bf16[7,1,7,128]{3,2,1,0:T(8,128)(2,1)S(1)}, u32[]{:S(2)}, u32[]{:S(2)}) collective-permute-start(bf16[7,1,7,128]{3,2,1,0:T(8,128)(2,1)S(1)} %slice.813), channel_id=1, source_target_pairs={{0,4},{4,0},{1,5},{5,1},{2,6},{6,2},{3,7},{7,3},{8,12},{12,8},{9,1... | collective-permute-start | bytes 37640 | tf_op jit(solution)/shard_map/ppermute | solution.py:36
  66.5 1.0 %collective-permute-done.16 = bf16[7,1,7,128]{3,2,1,0:T(8,128)(2,1)S(1)} collective-permute-done((bf16[7,1,7,128]{3,2,1,0:T(8,128)(2,1)S(1)}, bf16[7,1,7,128]{3,2,1,0:T(8,128)(2,1)S(1)}, u32[]{:S(2)}, u32[]{:S(2)}) %collective-permute-start.16) | collective-permute-done | bytes 12576 | tf_op jit(solution)/shard_map/ppermute | solution.py:36
  69.3 2.9 %collective-permute-start.18 = (bf16[212,128]{0,1:T(8,128)(2,1)S(1)}, bf16[212,128]{0,1:T(8,128)(2,1)S(1)}, u32[]{:S(2)}, u32[]{:S(2)}) collective-permute-start(bf16[212,128]{0,1:T(8,128)(2,1)S(1)} %pad_maximum_fusion.9), channel_id=1, source_target_pairs={{0,16},{1,17},{2,18},{3,19},{4,20},{5,21},{6,22},{7,23},{8,24},{9,... | collective-permute-start | bytes 162824 | tf_op jit(solution)/shard_map/ppermute | solution.py:48
  72.3 2.2 %collective-permute-done.18 = bf16[212,128]{0,1:T(8,128)(2,1)S(1)} collective-permute-done((bf16[212,128]{0,1:T(8,128)(2,1)S(1)}, bf16[212,128]{0,1:T(8,128)(2,1)S(1)}, u32[]{:S(2)}, u32[]{:S(2)}) %collective-permute-start.18) | collective-permute-done | bytes 54304 | tf_op jit(solution)/shard_map/ppermute | solution.py:48
  74.7 4.9 %collective-permute-start.19 = (bf16[176,128]{0,1:T(8,128)(2,1)S(1)}, bf16[176,128]{0,1:T(8,128)(2,1)S(1)}, u32[]{:S(2)}, u32[]{:S(2)}) collective-permute-start(bf16[176,128]{0,1:T(8,128)(2,1)S(1)} %add_convert_fusion.2), channel_id=1, source_target_pairs={{0,4},{1,5},{2,6},{3,7},{4,0},{5,1},{6,2},{7,3},{8,12},{9,13},{10,... | collective-permute-start | bytes 135176 | tf_op jit(solution)/shard_map/ppermute | solution.py:167
  80.2 1.7 %collective-permute-done.19 = bf16[176,128]{0,1:T(8,128)(2,1)S(1)} collective-permute-done((bf16[176,128]{0,1:T(8,128)(2,1)S(1)}, bf16[176,128]{0,1:T(8,128)(2,1)S(1)}, u32[]{:S(2)}, u32[]{:S(2)}) %collective-permute-start.19) | collective-permute-done | bytes 45088 | tf_op jit(solution)/shard_map/ppermute | solution.py:167
  81.9 2.4 %collective-permute-start.20 = (bf16[176,128]{0,1:T(8,128)(2,1)S(1)}, bf16[176,128]{0,1:T(8,128)(2,1)S(1)}, u32[]{:S(2)}, u32[]{:S(2)}) collective-permute-start(bf16[176,128]{0,1:T(8,128)(2,1)S(1)} %add_convert_fusion.1), channel_id=1, source_target_pairs={{0,8},{1,9},{2,10},{3,11},{4,12},{5,13},{6,14},{7,15},{8,0},{9,1},... | collective-permute-start | bytes 135176 | tf_op jit(solution)/shard_map/ppermute | solution.py:167
  84.4 2.2 %collective-permute-done.20 = bf16[176,128]{0,1:T(8,128)(2,1)S(1)} collective-permute-done((bf16[176,128]{0,1:T(8,128)(2,1)S(1)}, bf16[176,128]{0,1:T(8,128)(2,1)S(1)}, u32[]{:S(2)}, u32[]{:S(2)}) %collective-permute-start.20) | collective-permute-done | bytes 45088 | tf_op jit(solution)/shard_map/ppermute | solution.py:167
  86.7 1.6 %collective-permute-start.21 = (bf16[284,128]{0,1:T(8,128)(2,1)S(1)}, bf16[284,128]{0,1:T(8,128)(2,1)S(1)}, u32[]{:S(2)}, u32[]{:S(2)}) collective-permute-start(bf16[284,128]{0,1:T(8,128)(2,1)S(1)} %maximum_maximum_fusion.1), channel_id=1, source_target_pairs={{0,2},{1,3},{2,0},{3,1},{4,6},{5,7},{6,4},{7,5},{8,10},{9,11},{10,... | collective-permute-start | bytes 218120 | tf_op jit(solution)/shard_map/ppermute | solution.py:48
  88.2 3.1 %collective-permute-done.21 = bf16[284,128]{0,1:T(8,128)(2,1)S(1)} collective-permute-done((bf16[284,128]{0,1:T(8,128)(2,1)S(1)}, bf16[284,128]{0,1:T(8,128)(2,1)S(1)}, u32[]{:S(2)}, u32[]{:S(2)}) %collective-permute-start.21) | collective-permute-done | bytes 72736 | tf_op jit(solution)/shard_map/ppermute | solution.py:48
  92.2 1.3 %collective-permute-done.22 = bf16[460,128]{0,1:T(8,128)(2,1)S(1)} collective-permute-done((bf16[460,128]{0,1:T(8,128)(2,1)S(1)}, bf16[460,128]{0,1:T(8,128)(2,1)S(1)}, u32[]{:S(2)}, u32[]{:S(2)}) %collective-permute-start.22) | collective-permute-done | bytes 117792 | tf_op jit(solution)/shard_map/ppermute | solution.py:48
  94.0 0.7 copy.63
  95.1 0.9 copy.64
  (192 shorter events, 16.9 us)
Async XLA Ops:
  0.6 4.9 %copy-start = (bf16[1,343,343]{2,1,0:T(8,128)(2,1)S(1)}, bf16[1,343,343]{2,1,0:T(8,128)(2,1)}, u32[]{:S(2)}) copy-start(bf16[1,343,343]{2,1,0:T(8,128)(2,1)} %param.8) | copy-start | bytes 705898
  2.2 3.0 %copy-start.3 = (s32[1,343]{1,0:T(1,128)S(1)}, s32[1,343]{1,0:T(1,128)}, u32[]{:S(2)}) copy-start(s32[1,343]{1,0:T(1,128)} %param.9) | copy-start | bytes 4120
  2.3 3.0 %copy-start.2 = (f32[343]{0:T(512)S(1)}, f32[343]{0:T(512)}, u32[]{:S(2)}) copy-start(f32[343]{0:T(512)} %param.10) | copy-start | bytes 4120
  2.3 4.9 %collective-permute-start.2 = (bf16[108,128]{0,1:T(8,128)(2,1)S(1)}, bf16[108,128]{0,1:T(8,128)(2,1)S(1)}, u32[]{:S(2)}, u32[]{:S(2)}) collective-permute-start(bf16[108,128]{0,1:T(8,128)(2,1)S(1)} %pad_maximum_fusion.11), channel_id=1, source_target_pairs={{0,2},{1,3},{2,0},{3,1},{4,6},{5,7},{6,4},{7,5},{8,10},{9,11},{10,... | collective-permute-start | bytes 82952 | tf_op jit(solution)/shard_map/ppermute | solution.py:48
  6.4 14.8 %collective-permute-start = (bf16[1,343,345]{2,1,0:T(8,128)(2,1)S(1)}, bf16[1,343,345]{2,1,0:T(8,128)(2,1)S(1)}, u32[]{:S(2)}, u32[]{:S(2)}) collective-permute-start(bf16[1,343,345]{2,1,0:T(8,128)(2,1)S(1)} %maximum_bitcast_fusion), channel_id=1, source_target_pairs={{0,2},{1,3},{2,0},{3,1},{4,6},{5,7},{6,4},{7,5},{8,10},{9,11},{10,... | collective-permute-start | bytes 710018 | tf_op jit(solution)/shard_map/ppermute | solution.py:48
  7.4 1.3 %collective-permute-start.3 = (bf16[108,128]{0,1:T(8,128)(2,1)S(1)}, bf16[108,128]{0,1:T(8,128)(2,1)S(1)}, u32[]{:S(2)}, u32[]{:S(2)}) collective-permute-start(bf16[108,128]{0,1:T(8,128)(2,1)S(1)} %pad_maximum_fusion.12), channel_id=1, source_target_pairs={{0,1},{1,0},{2,3},{3,2},{4,5},{5,4},{6,7},{7,6},{8,9},{9,8},{10,11... | collective-permute-start | bytes 82952 | tf_op jit(solution)/shard_map/ppermute | solution.py:48
  9.3 5.6 %collective-permute-start.5 = (bf16[7,1,7,128]{3,2,1,0:T(8,128)(2,1)S(1)}, bf16[7,1,7,128]{3,2,1,0:T(8,128)(2,1)S(1)}, u32[]{:S(2)}, u32[]{:S(2)}) collective-permute-start(bf16[7,1,7,128]{3,2,1,0:T(8,128)(2,1)S(1)} %slice.634), channel_id=1, source_target_pairs={{4,8},{8,4},{5,9},{9,5},{6,10},{10,6},{7,11},{11,7},{20,24},{24,20... | collective-permute-start | bytes 37640 | tf_op jit(solution)/shard_map/ppermute | solution.py:36
  9.9 6.6 %collective-permute-start.4 = (bf16[7,1,7,128]{3,2,1,0:T(8,128)(2,1)S(1)}, bf16[7,1,7,128]{3,2,1,0:T(8,128)(2,1)S(1)}, u32[]{:S(2)}, u32[]{:S(2)}) collective-permute-start(bf16[7,1,7,128]{3,2,1,0:T(8,128)(2,1)S(1)} %slice.634), channel_id=1, source_target_pairs={{0,4},{4,0},{1,5},{5,1},{2,6},{6,2},{3,7},{7,3},{8,12},{12,8},{9,1... | collective-permute-start | bytes 37640 | tf_op jit(solution)/shard_map/ppermute | solution.py:36
  16.5 4.7 %collective-permute-start.6 = (bf16[1,7,7,128]{3,2,1,0:T(8,128)(2,1)S(1)}, bf16[1,7,7,128]{3,2,1,0:T(8,128)(2,1)S(1)}, u32[]{:S(2)}, u32[]{:S(2)}) collective-permute-start(bf16[1,7,7,128]{3,2,1,0:T(8,128)(2,1)S(1)} %pad_maximum_fusion.25), channel_id=1, source_target_pairs={{0,16},{16,0},{1,17},{17,1},{2,18},{18,2},{3,19},{19,3},{4,20},{20... | collective-permute-start | bytes 37640 | tf_op jit(solution)/shard_map/ppermute | solution.py:36
  21.5 1.0 %copy-start.1 = (bf16[216,704]{1,0:T(8,128)(2,1)S(1)}, bf16[216,704]{1,0:T(8,128)(2,1)}, u32[]{:S(2)}) copy-start(bf16[216,704]{1,0:T(8,128)(2,1)} %param.11) | copy-start | bytes 912388
  22.0 12.4 %collective-permute-start.1 = (bf16[2,343,345]{2,0,1:T(2,128)(2,1)S(1)}, bf16[2,343,345]{2,0,1:T(2,128)(2,1)S(1)}, u32[]{:S(2)}, u32[]{:S(2)}) collective-permute-start(bf16[2,343,345]{2,0,1:T(2,128)(2,1)S(1)} %copy.41), channel_id=1, source_target_pairs={{0,1},{1,0},{2,3},{3,2},{4,5},{5,4},{6,7},{7,6},{8,9},{9,8},{10,11... | collective-permute-start | bytes 1420028 | tf_op jit(solution)/shard_map/ppermute | solution.py:48
  22.8 11.3 %collective-permute-start.7 = (bf16[36,704]{0,1:T(8,128)(2,1)S(1)}, bf16[36,704]{0,1:T(8,128)(2,1)S(1)}, u32[]{:S(2)}, u32[]{:S(2)}) collective-permute-start(bf16[36,704]{0,1:T(8,128)(2,1)S(1)} %slice.636), channel_id=1, source_target_pairs={{0,16},{16,0},{1,17},{17,1},{2,18},{18,2},{3,19},{19,3},{4,20},{20... | collective-permute-start | bytes 152072 | tf_op jit(solution)/shard_map/ppermute | solution.py:36
  36.9 3.8 %collective-permute-start.8 = (bf16[7,1,7,128]{3,2,1,0:T(8,128)(2,1)S(1)}, bf16[7,1,7,128]{3,2,1,0:T(8,128)(2,1)S(1)}, u32[]{:S(2)}, u32[]{:S(2)}) collective-permute-start(bf16[7,1,7,128]{3,2,1,0:T(8,128)(2,1)S(1)} %get-tuple-element.76), channel_id=1, source_target_pairs={{0,4},{4,0},{1,5},{5,1},{2,6},{6,2},{3,7},{7,3},{8,12},{12,8},{9,1... | collective-permute-start | bytes 37640 | tf_op jit(solution)/shard_map/ppermute | solution.py:36
  38.4 2.3 %collective-permute-start.9 = (bf16[7,1,7,128]{3,2,1,0:T(8,128)(2,1)S(1)}, bf16[7,1,7,128]{3,2,1,0:T(8,128)(2,1)S(1)}, u32[]{:S(2)}, u32[]{:S(2)}) collective-permute-start(bf16[7,1,7,128]{3,2,1,0:T(8,128)(2,1)S(1)} %get-tuple-element.77), channel_id=1, source_target_pairs={{4,8},{8,4},{5,9},{9,5},{6,10},{10,6},{7,11},{11,7},{20,24},{24,20... | collective-permute-start | bytes 37640 | tf_op jit(solution)/shard_map/ppermute | solution.py:36
  40.8 4.7 %collective-permute-start.10 = (bf16[1,7,7,128]{3,2,1,0:T(8,128)(2,1)S(1)}, bf16[1,7,7,128]{3,2,1,0:T(8,128)(2,1)S(1)}, u32[]{:S(2)}, u32[]{:S(2)}) collective-permute-start(bf16[1,7,7,128]{3,2,1,0:T(8,128)(2,1)S(1)} %get-tuple-element.43), channel_id=1, source_target_pairs={{0,16},{16,0},{1,17},{17,1},{2,18},{18,2},{3,19},{19,3},{4,20},{20... | collective-permute-start | bytes 37640 | tf_op jit(solution)/shard_map/ppermute | solution.py:36
  40.9 15.7 %collective-permute-start.14 = (bf16[1,252,704]{1,2,0:T(8,128)(2,1)S(1)}, bf16[1,252,704]{1,2,0:T(8,128)(2,1)S(1)}, u32[]{:S(2)}, u32[]{:S(2)}) collective-permute-start(bf16[1,252,704]{1,2,0:T(8,128)(2,1)S(1)} %bitcast.50), channel_id=1, source_target_pairs={{0,2},{1,3},{2,0},{3,1},{4,6},{5,7},{6,4},{7,5},{8,10},{9,11},{10,... | collective-permute-start | bytes 1064456 | tf_op jit(solution)/shard_map/ppermute | solution.py:48
  47.0 7.9 %collective-permute-start.12 = (bf16[7,1,7,128]{3,2,1,0:T(8,128)(2,1)S(1)}, bf16[7,1,7,128]{3,2,1,0:T(8,128)(2,1)S(1)}, u32[]{:S(2)}, u32[]{:S(2)}) collective-permute-start(bf16[7,1,7,128]{3,2,1,0:T(8,128)(2,1)S(1)} %broadcast_select_fusion.35), channel_id=1, source_target_pairs={{4,8},{8,4},{5,9},{9,5},{6,10},{10,6},{7,11},{11,7},{20,24},{24,20... | collective-permute-start | bytes 37640 | tf_op jit(solution)/shard_map/ppermute | solution.py:36
  47.7 8.9 %collective-permute-start.11 = (bf16[7,1,7,128]{3,2,1,0:T(8,128)(2,1)S(1)}, bf16[7,1,7,128]{3,2,1,0:T(8,128)(2,1)S(1)}, u32[]{:S(2)}, u32[]{:S(2)}) collective-permute-start(bf16[7,1,7,128]{3,2,1,0:T(8,128)(2,1)S(1)} %get-tuple-element.40), channel_id=1, source_target_pairs={{0,4},{4,0},{1,5},{5,1},{2,6},{6,2},{3,7},{7,3},{8,12},{12,8},{9,1... | collective-permute-start | bytes 37640 | tf_op jit(solution)/shard_map/ppermute | solution.py:36
  56.8 5.0 %collective-permute-start.15 = (bf16[2,252,704]{1,2,0:T(8,128)(2,1)S(1)}, bf16[2,252,704]{1,2,0:T(8,128)(2,1)S(1)}, u32[]{:S(2)}, u32[]{:S(2)}) collective-permute-start(bf16[2,252,704]{1,2,0:T(8,128)(2,1)S(1)} %pad_maximum_fusion), channel_id=1, source_target_pairs={{0,1},{1,0},{2,3},{3,2},{4,5},{5,4},{6,7},{7,6},{8,9},{9,8},{10,11... | collective-permute-start | bytes 2128904 | tf_op jit(solution)/shard_map/ppermute | solution.py:48
  57.0 4.7 %collective-permute-start.13 = (bf16[1,7,7,128]{3,2,1,0:T(8,128)(2,1)S(1)}, bf16[1,7,7,128]{3,2,1,0:T(8,128)(2,1)S(1)}, u32[]{:S(2)}, u32[]{:S(2)}) collective-permute-start(bf16[1,7,7,128]{3,2,1,0:T(8,128)(2,1)S(1)} %fusion.84), channel_id=1, source_target_pairs={{0,16},{16,0},{1,17},{17,1},{2,18},{18,2},{3,19},{19,3},{4,20},{20... | collective-permute-start | bytes 37640 | tf_op jit(solution)/shard_map/ppermute | solution.py:36
  63.6 3.9 %collective-permute-start.16 = (bf16[7,1,7,128]{3,2,1,0:T(8,128)(2,1)S(1)}, bf16[7,1,7,128]{3,2,1,0:T(8,128)(2,1)S(1)}, u32[]{:S(2)}, u32[]{:S(2)}) collective-permute-start(bf16[7,1,7,128]{3,2,1,0:T(8,128)(2,1)S(1)} %slice.813), channel_id=1, source_target_pairs={{0,4},{4,0},{1,5},{5,1},{2,6},{6,2},{3,7},{7,3},{8,12},{12,8},{9,1... | collective-permute-start | bytes 37640 | tf_op jit(solution)/shard_map/ppermute | solution.py:36
  65.8 1.7 %collective-permute-start.17 = (bf16[7,1,7,128]{3,2,1,0:T(8,128)(2,1)S(1)}, bf16[7,1,7,128]{3,2,1,0:T(8,128)(2,1)S(1)}, u32[]{:S(2)}, u32[]{:S(2)}) collective-permute-start(bf16[7,1,7,128]{3,2,1,0:T(8,128)(2,1)S(1)} %slice.813), channel_id=1, source_target_pairs={{4,8},{8,4},{5,9},{9,5},{6,10},{10,6},{7,11},{11,7},{20,24},{24,20... | collective-permute-start | bytes 37640 | tf_op jit(solution)/shard_map/ppermute | solution.py:36
  69.3 5.2 %collective-permute-start.18 = (bf16[212,128]{0,1:T(8,128)(2,1)S(1)}, bf16[212,128]{0,1:T(8,128)(2,1)S(1)}, u32[]{:S(2)}, u32[]{:S(2)}) collective-permute-start(bf16[212,128]{0,1:T(8,128)(2,1)S(1)} %pad_maximum_fusion.9), channel_id=1, source_target_pairs={{0,16},{1,17},{2,18},{3,19},{4,20},{5,21},{6,22},{7,23},{8,24},{9,... | collective-permute-start | bytes 162824 | tf_op jit(solution)/shard_map/ppermute | solution.py:48
  74.7 7.1 %collective-permute-start.19 = (bf16[176,128]{0,1:T(8,128)(2,1)S(1)}, bf16[176,128]{0,1:T(8,128)(2,1)S(1)}, u32[]{:S(2)}, u32[]{:S(2)}) collective-permute-start(bf16[176,128]{0,1:T(8,128)(2,1)S(1)} %add_convert_fusion.2), channel_id=1, source_target_pairs={{0,4},{1,5},{2,6},{3,7},{4,0},{5,1},{6,2},{7,3},{8,12},{9,13},{10,... | collective-permute-start | bytes 135176 | tf_op jit(solution)/shard_map/ppermute | solution.py:167
  81.9 4.7 %collective-permute-start.20 = (bf16[176,128]{0,1:T(8,128)(2,1)S(1)}, bf16[176,128]{0,1:T(8,128)(2,1)S(1)}, u32[]{:S(2)}, u32[]{:S(2)}) collective-permute-start(bf16[176,128]{0,1:T(8,128)(2,1)S(1)} %add_convert_fusion.1), channel_id=1, source_target_pairs={{0,8},{1,9},{2,10},{3,11},{4,12},{5,13},{6,14},{7,15},{8,0},{9,1},... | collective-permute-start | bytes 135176 | tf_op jit(solution)/shard_map/ppermute | solution.py:167
  86.7 4.7 %collective-permute-start.21 = (bf16[284,128]{0,1:T(8,128)(2,1)S(1)}, bf16[284,128]{0,1:T(8,128)(2,1)S(1)}, u32[]{:S(2)}, u32[]{:S(2)}) collective-permute-start(bf16[284,128]{0,1:T(8,128)(2,1)S(1)} %maximum_maximum_fusion.1), channel_id=1, source_target_pairs={{0,2},{1,3},{2,0},{3,1},{4,6},{5,7},{6,4},{7,5},{8,10},{9,11},{10,... | collective-permute-start | bytes 218120 | tf_op jit(solution)/shard_map/ppermute | solution.py:48
  92.1 1.4 %collective-permute-start.22 = (bf16[460,128]{0,1:T(8,128)(2,1)S(1)}, bf16[460,128]{0,1:T(8,128)(2,1)S(1)}, u32[]{:S(2)}, u32[]{:S(2)}) collective-permute-start(bf16[460,128]{0,1:T(8,128)(2,1)S(1)} %maximum_maximum_fusion), channel_id=1, source_target_pairs={{0,1},{1,0},{2,3},{3,2},{4,5},{5,4},{6,7},{7,6},{8,9},{9,8},{10,11... | collective-permute-start | bytes 353288 | tf_op jit(solution)/shard_map/ppermute | solution.py:48

commit v5 on v4

--- a/solution.py
+++ b/solution.py
@@ -1,6 +1,7 @@
 import jax
 import jax.numpy as jnp
 from jax import lax
+from jax.experimental.layout import Layout, with_layout_constraint
 from jax.sharding import PartitionSpec as P
 
 GRID_Y = 4
@@ -10,6 +11,8 @@
 
 chebyshev_coeffs = ((-1.0 / 7.0, 0.0), (-7.0 / 41.0, 8.0 / 41.0), (-41.0 / 259.0, 28.0 / 259.0))
 centre = 6.0
+
+PAIRS = GRID_Z // 2
 
 
 class Grid:
@@ -17,6 +20,7 @@
         self.devices = lax.axis_size(AXIS)
         self.counts = (self.devices // (GRID_Y * GRID_Z), GRID_Y, GRID_Z)
         self.stride = (GRID_Y * GRID_Z, GRID_Z, 1)
+        self.leaders = range(1, self.devices, 2)
         self.position = lax.axis_index(AXIS)
         self.coords = tuple(
             self.position // self.stride[d] % self.counts[d] for d in range(3)
@@ -25,10 +29,10 @@
     def coord_of(self, device, dim):
         return device // self.stride[dim] % self.counts[dim]
 
-    def swapped(self, low, high, dim, odd):
+    def swapped(self, low, high, dim, odd, everyone=False):
         by = self.stride[dim]
         pairs = []
-        for i in range(self.devices):
+        for i in range(self.devices) if everyone else self.leaders:
             c = self.coord_of(i, dim)
             if c % 2 == odd and c + 1 < self.counts[dim]:
                 pairs += [(i, i + by), (i + by, i)]
@@ -37,73 +41,73 @@
         zero = jnp.zeros_like(arrived)
         return jnp.where(lower, zero, arrived), jnp.where(lower, arrived, zero)
 
-    def exchanged(self, low, high, dim):
-        to_low, to_high = self.swapped(low, high, dim, 0)
+    def exchanged(self, low, high, dim, everyone=False):
+        to_low, to_high = self.swapped(low, high, dim, 0, everyone)
         if self.counts[dim] > 2:
-            more_low, more_high = self.swapped(low, high, dim, 1)
+            more_low, more_high = self.swapped(low, high, dim, 1, everyone)
             to_low, to_high = to_low + more_low, to_high + more_high
         return to_low, to_high
 
     def partner(self, value, bit):
-        return lax.ppermute(value, AXIS, [(i, i ^ bit) for i in range(self.devices)])
+        among = range(self.devices) if bit == 1 else self.leaders
+        return lax.ppermute(value, AXIS, [(i, i ^ bit) for i in among])
 
     def has(self, bit):
         return (self.position & bit) != 0
 
 
 def line_bits():
-    bit = GRID_Z // 2
-    while bit:
+    bit = 2
+    while bit < GRID_Z:
         yield bit
-        bit //= 2
+        bit *= 2
+
+
+def joined(grid, value, bit):
+    other = grid.partner(value, bit)
+    mine = grid.has(bit)
+    return jnp.stack([jnp.where(mine, other, value), jnp.where(mine, value, other)])
 
 
 def lines_gathered(grid, value):
-    held = value[None]
-    order = [0]
+    held = joined(grid, value, 1)
     for bit in line_bits():
-        other = grid.partner(held, bit)
-        mine = grid.has(bit)
-        held = jnp.concatenate(
-            [jnp.where(mine, other, held), jnp.where(mine, held, other)], axis=0
-        )
-        order = order + [i | bit for i in order]
-    return [held[order.index(i)] for i in range(GRID_Z)]
+        held = joined(grid, held, bit).reshape((-1,) + value.shape)
+    return [held[i] for i in range(GRID_Z)]
 
 
 class Shares:
-    def __init__(self, grid, value):
+    def __init__(self, grid, blocks):
         self.grid = grid
-        self.width = value.shape[1] // GRID_Z
-        self.half = value.shape[0] // 2
-        self.blocks = [
-            value[:, i * self.width : (i + 1) * self.width] for i in range(GRID_Z)
-        ]
-
-    def packed(self, bit):
+        self.blocks = blocks
+
+    def away(self, bit):
         mine = self.grid.has(bit)
-        away = [
-            jnp.where(mine, self.blocks[i], self.blocks[i | bit])
-            for i in range(GRID_Z)
-            if not i & bit
-        ]
+        b = bit // 2
         return jnp.concatenate(
-            [b[h : h + self.half] for h in (0, self.half) for b in away], axis=1
+            [
+                jnp.where(mine, self.blocks[i], self.blocks[i | b])
+                for i in range(PAIRS)
+                if not i & b
+            ],
+            axis=0,
         )
 
     def take(self, bit, arrived):
         mine = self.grid.has(bit)
-        lows = [i for i in range(GRID_Z) if not i & bit]
+        b = bit // 2
+        rows = self.blocks[0].shape[0]
+        lows = [i for i in range(PAIRS) if not i & b]
         for at, i in enumerate(lows):
-            ends = (at * self.width, (at + len(lows)) * self.width)
-            came = jnp.concatenate([arrived[:, e : e + self.width] for e in ends], axis=0)
-            self.blocks[i], self.blocks[i | bit] = (
+            came = arrived[at * rows : (at + 1) * rows]
+            self.blocks[i], self.blocks[i | b] = (
                 jnp.where(mine, came, self.blocks[i]),
-                jnp.where(mine, self.blocks[i | bit], came),
+                jnp.where(mine, self.blocks[i | b], came),
             )
 
-    def value(self):
-        return jnp.concatenate(self.blocks, axis=1)
+
+def by_rows(value):
+    return with_layout_constraint(value, Layout(major_to_minor=tuple(range(value.ndim))))
 
 
 def plane(field, dim, at):
@@ -161,7 +165,7 @@
         terms = [value]
         for turn in range(1, factor):
             pairs = []
-            for i in range(grid.devices):
+            for i in grid.leaders:
                 c = i // stride % factor
                 pairs.append((i, i + ((c + turn) % factor - c) * stride))
             terms.append(lax.ppermute(value, AXIS, pairs))
@@ -183,29 +187,38 @@
 def per_device(block, cell_matrix, connectivity, potential, locked):
     owned_rows, columns = block.shape
     slot_count = potential.shape[0]
-    width = columns // GRID_Z
+    width = columns // PAIRS
+    lanes = width * GRID_Z
     edge = SIDE - 1
     grid = Grid()
-    shape = (SIDE, SIDE, SIDE, columns)
+    shape = (SIDE, SIDE, SIDE, lanes)
 
     matrix = slots_matrix(cell_matrix, connectivity, slot_count)
     coarse = rounded(potential)
     fine = rounded(potential - coarse.astype(jnp.float32))
     matrix = jnp.concatenate([matrix, coarse[:, None], fine[:, None]], axis=1)
     matrices = lines_gathered(grid, matrix)
-    lane_owner = lax.broadcasted_iota(jnp.int32, (1, columns), 1) // width
-    lumped = jnp.zeros((slot_count, columns), jnp.float32)
+    lane_owner = lax.broadcasted_iota(jnp.int32, (1, lanes), 1) // width
+    lumped = jnp.zeros((slot_count, lanes), jnp.float32)
     for p in range(GRID_Z):
         both = jnp.sum(matrices[p][:, slot_count:].astype(jnp.float32), axis=1, keepdims=True)
         lumped = jnp.where(lane_owner == p, both, lumped)
 
-    shares = Shares(grid, block)
+    blocks = joined(grid, block, 1)
+    shares = Shares(
+        grid,
+        [
+            jnp.concatenate([b[:, i * width : (i + 1) * width] for b in blocks], axis=1)
+            for i in range(PAIRS)
+        ],
+    )
     for bit in line_bits():
-        shares.take(bit, grid.partner(shares.packed(bit), bit))
+        shares.take(bit, grid.partner(shares.away(bit), bit))
+    mine = jnp.concatenate(shares.blocks, axis=1)
     field = (
         jnp.zeros(shape, jnp.bfloat16)
         .at[1:, 1:, 1:]
-        .set(shares.value().reshape(edge, edge, edge, columns))
+        .set(mine.reshape(edge, edge, edge, lanes))
     )
     field = with_ends(field, 2, to_next_partition(plane(field, 2, SIDE - 1), width), None)
     for dim in (1, 0):
@@ -213,21 +226,21 @@
         field = with_ends(field, dim, grid.exchanged(high, high, dim)[0], None)
 
     inside = jnp.ones(shape, jnp.bool_)
-    first = (grid.coords[0] == 0, grid.coords[1] == 0, lane_owner.reshape(1, 1, 1, columns) == 0)
+    first = (grid.coords[0] == 0, grid.coords[1] == 0, lane_owner.reshape(1, 1, 1, lanes) == 0)
     for dim in range(3):
         at = lax.broadcasted_iota(jnp.int32, shape, dim)
         inside = inside & ~((at == 0) & first[dim])
 
     locked, field = lax.optimization_barrier((locked, field))
-    above = locked[-edge * edge :]
-    below = grid.exchanged(above, above, 0)[0]
+    above = by_rows(locked[-edge * edge :])
+    below = by_rows(grid.exchanged(above, above, 0, True)[0])
     locked = jnp.concatenate([below, locked], axis=0)
 
     older = field
     current = field
     steps = len(chebyshev_coeffs)
     for step, coeffs in enumerate(chebyshev_coeffs):
-        rows = current.reshape(slot_count, columns)
+        rows = current.reshape(slot_count, lanes)
         partial = lumped * rows.astype(jnp.float32)
         for p in range(GRID_Z):
             own = jnp.where(lane_owner == p, rows, jnp.zeros_like(rows))
@@ -270,14 +283,14 @@
     low = plane(partial, 1, 0).astype(jnp.bfloat16)
     to_high = grid.exchanged(low, low, 1)[1].astype(jnp.float32)
     partial = with_ends(partial, 1, None, plane(partial, 1, SIDE - 1) + to_high)
-    partial = coeffs[0] * partial[:, 1:, 1:].reshape(SIDE, edge * edge, columns)
+    partial = coeffs[0] * partial[:, 1:, 1:].reshape(SIDE, edge * edge, lanes)
 
     def owned(field):
-        return field[1:, 1:, 1:].reshape(edge, edge * edge, columns).astype(jnp.float32)
+        return field[1:, 1:, 1:].reshape(edge, edge * edge, lanes).astype(jnp.float32)
 
     rest = -coeffs[0] * centre * owned(current) - coeffs[1] * owned(older)
     sums = jnp.concatenate([partial[:1], partial[1:] + rest], axis=0)
-    weights = sums.astype(jnp.bfloat16).reshape(SIDE * edge * edge, columns)
+    weights = sums.astype(jnp.bfloat16).reshape(SIDE * edge * edge, lanes)
     share = 0.0
     for p in range(GRID_Z):
         share = share + lax.dot_general(
@@ -286,12 +299,17 @@
             (((0,), (0,)), ((), ())),
             preferred_element_type=jnp.float32,
         )
-    deep = share.shape[0] // GRID_Z
+    deep = share.shape[0] // PAIRS
     share = jnp.concatenate(
-        [share[i * deep : (i + 1) * deep] for i in range(GRID_Z)], axis=1
+        [share[i * deep : (i + 1) * deep] for i in range(PAIRS)], axis=1
     ).astype(jnp.bfloat16)
 
-    low = sums[0].astype(jnp.bfloat16)
+    def folded(value):
+        return jnp.concatenate(
+            [value[:, i : i + columns] for i in range(0, lanes, columns)], axis=0
+        )
+
+    low = folded(sums[0].astype(jnp.bfloat16))
     stride, count = grid.stride[0], grid.counts[0]
     even = grid.coords[0] % 2 == 0
     arrived = grid.partner(jnp.concatenate([share, low], axis=0), stride)
@@ -299,36 +317,46 @@
     to_high = jnp.where(even, arrived[deep:], jnp.zeros_like(low))
     if count > 2:
         to_high = to_high + grid.swapped(low, low, 0, 1)[1]
+    to_high = to_high.reshape(lanes // columns, edge * edge, columns)
+    to_high = jnp.concatenate(list(to_high), axis=1)
     sums = jnp.concatenate(
         [sums[1:edge], sums[edge:] + to_high[None].astype(jnp.float32)], axis=0
     )
-    filtered = rounded(sums.reshape(owned_rows, columns))
+    filtered = rounded(sums.reshape(owned_rows, lanes))
 
     share = summed_along(grid, share, grid.stride[1], grid.counts[1])
     share = summed_along(grid, share, stride * 2, count // 2)
 
-    shares = Shares(grid, filtered)
+    shares = Shares(
+        grid, [filtered[:, i : i + 2 * width] for i in range(0, lanes, 2 * width)]
+    )
     held = share[None]
-    order = [0]
     for bit in line_bits():
         mine = grid.has(bit)
         sent = held.reshape(-1, columns)
-        arrived = grid.partner(jnp.concatenate([sent, shares.packed(bit)], axis=0), bit)
+        arrived = grid.partner(jnp.concatenate([sent, shares.away(bit)], axis=0), bit)
         shares.take(bit, arrived[sent.shape[0] :])
         other = arrived[: sent.shape[0]].reshape(held.shape)
         held = jnp.concatenate(
             [jnp.where(mine, other, held), jnp.where(mine, held, other)], axis=0
         )
-        order = order + [i | bit for i in order]
-    held = [held[order.index(i)] for i in range(GRID_Z)]
+    first, second = (
+        jnp.concatenate([b[:, i : i + width] for b in shares.blocks], axis=1)
+        for i in (0, width)
+    )
+    sent = jnp.concatenate([held.reshape(-1, columns), first], axis=0)
+    arrived = grid.partner(sent, 1)
+    leader = grid.has(1)
+    held = jnp.where(leader, held, arrived[:-owned_rows].reshape(held.shape))
+    filtered = jnp.where(leader, second, arrived[-owned_rows:])
     intersection = jnp.concatenate(
         [
             jnp.concatenate([h[:, q * width : (q + 1) * width] for h in held], axis=1)
-            for q in range(GRID_Z)
+            for q in range(PAIRS)
         ],
         axis=0,
     ).astype(jnp.float32)
-    return shares.value(), intersection
+    return filtered, intersection
 
 
 def solution(mesh):

time: 96.3 us -> 115 us (1.19)
  starting transfers between devices: 44 us -> 87.7 us
  waiting for transfers between devices: 33.2 us -> 4.08 us
  other arithmetic: 4.56 us -> 8.36 us
    ppermute x9, starting transfers between devices: 9.93 us -> 76.2 us  [partner(): return lax.ppermute(value, AXIS, [(i, i ^ bit) for i in among])]
    ppermute x12, waiting for transfers between devices: 21.4 us -> 1.74 us  [swapped(): arrived = lax.ppermute(jnp.where(lower, high, low), AXIS, pairs)]
    ppermute x12, starting transfers between devices: 26.7 us -> 10.1 us  [swapped(): arrived = lax.ppermute(jnp.where(lower, high, low), AXIS, pairs)]
    ppermute x2, starting transfers between devices: 7.32 us -> 1.33 us  [summed_along(): terms.append(lax.ppermute(value, AXIS, pairs))]
    ppermute x9, waiting for transfers between devices: 7.93 us -> 2.33 us  [partner(): return lax.ppermute(value, AXIS, [(i, i ^ bit) for i in among])]
    ppermute x2, waiting for transfers between devices: 3.87 us -> 0.01 us  [summed_along(): terms.append(lax.ppermute(value, AXIS, pairs))]
    slice x17 -> x8, local copies, waits for them, and re-layouts: 2.21 us -> 0.24 us  [the longest x2 0.18 us: per_device(): held = jnp.where(leader, held, arrived[:-owned_rows].reshape(held.shape))]
    another operation x1 -> x9, other arithmetic: 0.06 us -> 1.54 us  [the longest x8 1.43 us: joined(): jnp.stack([jnp.where(mine, other, value), jnp.where(mine, value, other)])]
  transfers between devices with their start and end apart: 23 -> 23, of which waited for: 15 -> 3; matrix products, arithmetic and copies ran while one was open for 5% -> 5% of each run, Pallas kernels for 0% -> 0%
where the time goes in v5:
time: 115 us
  starting transfers between devices  87.7 us (76%)
  other arithmetic  8.36 us (7%)
  local copies, waits for them, and re-layouts  7.46 us (6%)
  matrix products  5.1 us (4%)
  waiting for transfers between devices  4.08 us (4%)
  between operations  1.96 us (2%)
    ppermute x9, starting transfers between devices, partner(): return lax.ppermute(value, AXIS, [(i, i ^ bit) for i in among])  76.2 us
    ppermute x12, starting transfers between devices, swapped(): arrived = lax.ppermute(jnp.where(lower, high, low), AXIS, pairs)  10.1 us
    unnamed x41, local copies, waits for them, and re-layouts  3.61 us
    dot_general x12, matrix products, per_device(): jnp.dot(matrices[p][:, :slot_count], own, preferred_element_type=jnp.floa...  3.24 us
    ppermute x9, waiting for transfers between devices, partner(): return lax.ppermute(value, AXIS, [(i, i ^ bit) for i in among])  2.33 us
  transfers between devices with their start and end apart: 23, of which 3 were waited for; matrix products, arithmetic and copies ran while one was open for 5% of the time, Pallas kernels for 0%

profile of v5, /device:TPU:0, one launch (start us, length us, event | category | flops | bytes accessed | tf_op | source)
XLA Modules:
  0.0 114.7 jit_solution(14632314488897979367)
XLA Ops:
  0.6 1.0 copy.65
  2.1 0.7 reduce.2
  2.8 0.7 convolution_convert_fusion
  3.6 0.7 reduce-precision_convert_fusion.1
  4.6 0.7 collective-permute-start.3
  5.4 4.0 %collective-permute-start = (bf16[343,345]{1,0:T(8,128)(2,1)S(1)}, bf16[343,345]{1,0:T(8,128)(2,1)S(1)}, u32[]{:S(2)}, u32[]{:S(2)}) collective-permute-start(bf16[343,345]{1,0:T(8,128)(2,1)S(1)} %pad_maximum_fusion.8), channel_id=1, source_target_pairs={{0,1},{1,0},{2,3},{3,2},{4,5},{5,4},{6,7},{7,6},{8,9},{9,8},{10,11... | collective-permute-start | bytes 710018 | tf_op jit(solution)/shard_map/ppermute | solution.py:53
  9.9 0.7 collective-permute-start.5
  10.6 0.7 collective-permute-start.4
  11.9 0.7 collective-permute-start.6
  12.6 0.6 broadcast_compare_fusion
  13.9 0.7 collective-permute-start.1
  14.7 2.7 %collective-permute-start.7 = (bf16[36,704]{1,0:T(8,128)(2,1)S(1)}, bf16[36,704]{1,0:T(8,128)(2,1)S(1)}, u32[]{:S(2)}, u32[]{:S(2)}) collective-permute-start(bf16[36,704]{1,0:T(8,128)(2,1)S(1)} %slice.351), channel_id=1, source_target_pairs={{0,16},{16,0},{1,17},{17,1},{2,18},{18,2},{3,19},{19,3},{4,20},{20... | collective-permute-start | bytes 152072 | tf_op jit(solution)/shard_map/ppermute | solution.py:40
  18.2 1.7 %collective-permute-done.7 = bf16[36,704]{1,0:T(8,128)(2,1)S(1)} collective-permute-done((bf16[36,704]{1,0:T(8,128)(2,1)S(1)}, bf16[36,704]{1,0:T(8,128)(2,1)S(1)}, u32[]{:S(2)}, u32[]{:S(2)}) %collective-permute-start.7) | collective-permute-done | bytes 50720 | tf_op jit(solution)/shard_map/ppermute | solution.py:40
  23.2 0.7 collective-permute-start.8
  23.9 0.7 collective-permute-start.9
  24.7 0.7 collective-permute-start.10
  27.4 0.7 collective-permute-start.12
  28.0 0.7 collective-permute-start.11
  28.7 31.4 %collective-permute-start.14 = (bf16[252,704]{0,1:T(8,128)(2,1)S(1)}, bf16[252,704]{0,1:T(8,128)(2,1)S(1)}, u32[]{:S(2)}, u32[]{:S(2)}) collective-permute-start(bf16[252,704]{0,1:T(8,128)(2,1)S(1)} %pad_maximum_fusion.6), channel_id=1, source_target_pairs={{0,1},{1,0},{2,3},{3,2},{4,5},{5,4},{6,7},{7,6},{8,9},{9,8},{10,11... | collective-permute-start | bytes 1064456 | tf_op jit(solution)/shard_map/ppermute | solution.py:53
  60.3 1.2 %collective-permute-done.14 = bf16[252,704]{0,1:T(8,128)(2,1)S(1)} collective-permute-done((bf16[252,704]{0,1:T(8,128)(2,1)S(1)}, bf16[252,704]{0,1:T(8,128)(2,1)S(1)}, u32[]{:S(2)}, u32[]{:S(2)}) %collective-permute-start.14) | collective-permute-done | bytes 354848 | tf_op jit(solution)/shard_map/ppermute | solution.py:53
  61.7 0.7 collective-permute-start.15
  62.4 0.7 collective-permute-start.13
  66.3 0.7 collective-permute-start.16
  67.0 0.8 collective-permute-start.17
  69.9 0.7 collective-permute-start.18
  71.2 0.7 collective-permute-start.19
  72.1 0.7 collective-permute-start.20
  73.0 0.7 collective-permute-start.21
  74.3 36.8 %collective-permute-start.22 = (bf16[920,128]{0,1:T(8,128)(2,1)S(1)}, bf16[920,128]{0,1:T(8,128)(2,1)S(1)}, u32[]{:S(2)}, u32[]{:S(2)}) collective-permute-start(bf16[920,128]{0,1:T(8,128)(2,1)S(1)} %maximum_maximum_fusion), channel_id=1, source_target_pairs={{0,1},{1,0},{2,3},{3,2},{4,5},{5,4},{6,7},{7,6},{8,9},{9,8},{10,11... | collective-permute-start | bytes 706568 | tf_op jit(solution)/shard_map/ppermute | solution.py:53
  111.2 1.2 %collective-permute-done.22 = bf16[920,128]{0,1:T(8,128)(2,1)S(1)} collective-permute-done((bf16[920,128]{0,1:T(8,128)(2,1)S(1)}, bf16[920,128]{0,1:T(8,128)(2,1)S(1)}, u32[]{:S(2)}, u32[]{:S(2)}) %collective-permute-start.22) | collective-permute-done | bytes 235552 | tf_op jit(solution)/shard_map/ppermute | solution.py:53
  112.6 0.7 copy.81
  113.7 0.9 copy.82
  (195 shorter events, 16.2 us)
Async XLA Ops:
  0.6 2.2 %copy-start = (bf16[1,343,343]{2,1,0:T(8,128)(2,1)S(1)}, bf16[1,343,343]{2,1,0:T(8,128)(2,1)}, u32[]{:S(2)}) copy-start(bf16[1,343,343]{2,1,0:T(8,128)(2,1)} %param.8) | copy-start | bytes 705898
  1.6 2.9 %collective-permute-start.2 = (bf16[216,128]{0,1:T(8,128)(2,1)S(1)}, bf16[216,128]{0,1:T(8,128)(2,1)S(1)}, u32[]{:S(2)}, u32[]{:S(2)}) collective-permute-start(bf16[216,128]{0,1:T(8,128)(2,1)S(1)} %copy.65), channel_id=1, source_target_pairs={{0,1},{1,0},{2,3},{3,2},{4,5},{5,4},{6,7},{7,6},{8,9},{9,8},{10,11... | collective-permute-start | bytes 165896 | tf_op jit(solution)/shard_map/ppermute | solution.py:53
  4.6 4.8 %collective-permute-start.3 = (bf16[216,128]{0,1:T(8,128)(2,1)S(1)}, bf16[216,128]{0,1:T(8,128)(2,1)S(1)}, u32[]{:S(2)}, u32[]{:S(2)}) collective-permute-start(bf16[216,128]{0,1:T(8,128)(2,1)S(1)} %broadcast_select_fusion.6), channel_id=1, source_target_pairs={{1,3},{3,1},{5,7},{7,5},{9,11},{11,9},{13,15},{15,13},{17,19},{19,... | collective-permute-start | bytes 165896 | tf_op jit(solution)/shard_map/ppermute | solution.py:53
  5.4 7.8 %collective-permute-start = (bf16[343,345]{1,0:T(8,128)(2,1)S(1)}, bf16[343,345]{1,0:T(8,128)(2,1)S(1)}, u32[]{:S(2)}, u32[]{:S(2)}) collective-permute-start(bf16[343,345]{1,0:T(8,128)(2,1)S(1)} %pad_maximum_fusion.8), channel_id=1, source_target_pairs={{0,1},{1,0},{2,3},{3,2},{4,5},{5,4},{6,7},{7,6},{8,9},{9,8},{10,11... | collective-permute-start | bytes 710018 | tf_op jit(solution)/shard_map/ppermute | solution.py:53
  9.9 1.9 %collective-permute-start.5 = (bf16[7,1,7,256]{3,2,1,0:T(8,128)(2,1)S(1)}, bf16[7,1,7,256]{3,2,1,0:T(8,128)(2,1)S(1)}, u32[]{:S(2)}, u32[]{:S(2)}) collective-permute-start(bf16[7,1,7,256]{3,2,1,0:T(8,128)(2,1)S(1)} %slice.436), channel_id=1, source_target_pairs={{5,9},{9,5},{7,11},{11,7},{21,25},{25,21},{23,27},{27,23}} | collective-permute-start | bytes 75272 | tf_op jit(solution)/shard_map/ppermute | solution.py:40
  10.6 1.3 %collective-permute-start.4 = (bf16[7,1,7,256]{3,2,1,0:T(8,128)(2,1)S(1)}, bf16[7,1,7,256]{3,2,1,0:T(8,128)(2,1)S(1)}, u32[]{:S(2)}, u32[]{:S(2)}) collective-permute-start(bf16[7,1,7,256]{3,2,1,0:T(8,128)(2,1)S(1)} %slice.436), channel_id=1, source_target_pairs={{1,5},{5,1},{3,7},{7,3},{9,13},{13,9},{11,15},{15,11},{17,21},{21,... | collective-permute-start | bytes 75272 | tf_op jit(solution)/shard_map/ppermute | solution.py:40
  11.9 1.3 %collective-permute-start.6 = (bf16[1,7,7,256]{3,2,1,0:T(8,128)(2,1)S(1)}, bf16[1,7,7,256]{3,2,1,0:T(8,128)(2,1)S(1)}, u32[]{:S(2)}, u32[]{:S(2)}) collective-permute-start(bf16[1,7,7,256]{3,2,1,0:T(8,128)(2,1)S(1)} %pad_maximum_fusion.20), channel_id=1, source_target_pairs={{1,17},{17,1},{3,19},{19,3},{5,21},{21,5},{7,23},{23,7},{9,25},{25... | collective-permute-start | bytes 75272 | tf_op jit(solution)/shard_map/ppermute | solution.py:40
  13.4 1.3 %copy-start.1 = (bf16[216,704]{1,0:T(8,128)(2,1)S(1)}, bf16[216,704]{1,0:T(8,128)(2,1)}, u32[]{:S(2)}) copy-start(bf16[216,704]{1,0:T(8,128)(2,1)} %param.11) | copy-start | bytes 912388
  13.9 6.4 %collective-permute-start.1 = (bf16[2,343,345]{2,0,1:T(2,128)(2,1)S(1)}, bf16[2,343,345]{2,0,1:T(2,128)(2,1)S(1)}, u32[]{:S(2)}, u32[]{:S(2)}) collective-permute-start(bf16[2,343,345]{2,0,1:T(2,128)(2,1)S(1)} %copy.62), channel_id=1, source_target_pairs={{1,3},{3,1},{5,7},{7,5},{9,11},{11,9},{13,15},{15,13},{17,19},{19,... | collective-permute-start | bytes 1420028 | tf_op jit(solution)/shard_map/ppermute | solution.py:53
  14.7 5.2 %collective-permute-start.7 = (bf16[36,704]{1,0:T(8,128)(2,1)S(1)}, bf16[36,704]{1,0:T(8,128)(2,1)S(1)}, u32[]{:S(2)}, u32[]{:S(2)}) collective-permute-start(bf16[36,704]{1,0:T(8,128)(2,1)S(1)} %slice.351), channel_id=1, source_target_pairs={{0,16},{16,0},{1,17},{17,1},{2,18},{18,2},{3,19},{19,3},{4,20},{20... | collective-permute-start | bytes 152072 | tf_op jit(solution)/shard_map/ppermute | solution.py:40
  20.7 0.7 copy-start.2
  20.7 0.7 copy-start.4
  21.1 4.5 %copy-start.9 = (f32[343]{0:T(512)}, f32[343]{0:T(512)S(1)}, u32[]{:S(2)}) copy-start(f32[343]{0:T(512)S(1)} %get-tuple-element.122) | copy-start | bytes 4120
  21.1 4.5 %copy-start.11 = (f32[343]{0:T(512)}, f32[343]{0:T(512)S(1)}, u32[]{:S(2)}) copy-start(f32[343]{0:T(512)S(1)} %get-tuple-element.123) | copy-start | bytes 4120
  21.4 4.3 %copy-start.13 = (f32[343]{0:T(512)}, f32[343]{0:T(512)S(1)}, u32[]{:S(2)}) copy-start(f32[343]{0:T(512)S(1)} %get-tuple-element.120) | copy-start | bytes 4120
  21.4 4.3 %copy-start.15 = (f32[343]{0:T(512)}, f32[343]{0:T(512)S(1)}, u32[]{:S(2)}) copy-start(f32[343]{0:T(512)S(1)} %get-tuple-element.121) | copy-start | bytes 4120
  22.9 2.6 %copy-start.8 = (pred[7]{0:T(512)(128)(4,1)S(1)}, pred[7]{0:T(512)(128)(4,1)}, u32[]{:S(2)}) copy-start(pred[7]{0:T(512)(128)(4,1)} %iota_compare_fusion.8) | copy-start | bytes 25
  23.2 1.4 %collective-permute-start.8 = (bf16[7,1,7,256]{3,2,1,0:T(8,128)(2,1)S(1)}, bf16[7,1,7,256]{3,2,1,0:T(8,128)(2,1)S(1)}, u32[]{:S(2)}, u32[]{:S(2)}) collective-permute-start(bf16[7,1,7,256]{3,2,1,0:T(8,128)(2,1)S(1)} %get-tuple-element.76), channel_id=1, source_target_pairs={{1,5},{5,1},{3,7},{7,3},{9,13},{13,9},{11,15},{15,11},{17,21},{21,... | collective-permute-start | bytes 75272 | tf_op jit(solution)/shard_map/ppermute | solution.py:40
  23.9 0.7 collective-permute-start.9
  24.7 0.7 collective-permute-start.10
  27.4 32.8 %collective-permute-start.12 = (bf16[7,1,7,256]{3,2,1,0:T(8,128)(2,1)S(1)}, bf16[7,1,7,256]{3,2,1,0:T(8,128)(2,1)S(1)}, u32[]{:S(2)}, u32[]{:S(2)}) collective-permute-start(bf16[7,1,7,256]{3,2,1,0:T(8,128)(2,1)S(1)} %broadcast_select_fusion.10), channel_id=1, source_target_pairs={{5,9},{9,5},{7,11},{11,7},{21,25},{25,21},{23,27},{27,23}} | collective-permute-start | bytes 75272 | tf_op jit(solution)/shard_map/ppermute | solution.py:40
  28.0 32.1 %collective-permute-start.11 = (bf16[7,1,7,256]{3,2,1,0:T(8,128)(2,1)S(1)}, bf16[7,1,7,256]{3,2,1,0:T(8,128)(2,1)S(1)}, u32[]{:S(2)}, u32[]{:S(2)}) collective-permute-start(bf16[7,1,7,256]{3,2,1,0:T(8,128)(2,1)S(1)} %get-tuple-element.42), channel_id=1, source_target_pairs={{1,5},{5,1},{3,7},{7,3},{9,13},{13,9},{11,15},{15,11},{17,21},{21,... | collective-permute-start | bytes 75272 | tf_op jit(solution)/shard_map/ppermute | solution.py:40
  28.7 32.7 %collective-permute-start.14 = (bf16[252,704]{0,1:T(8,128)(2,1)S(1)}, bf16[252,704]{0,1:T(8,128)(2,1)S(1)}, u32[]{:S(2)}, u32[]{:S(2)}) collective-permute-start(bf16[252,704]{0,1:T(8,128)(2,1)S(1)} %pad_maximum_fusion.6), channel_id=1, source_target_pairs={{0,1},{1,0},{2,3},{3,2},{4,5},{5,4},{6,7},{7,6},{8,9},{9,8},{10,11... | collective-permute-start | bytes 1064456 | tf_op jit(solution)/shard_map/ppermute | solution.py:53
  61.7 1.6 %collective-permute-start.15 = (bf16[2,252,704]{1,2,0:T(8,128)(2,1)S(1)}, bf16[2,252,704]{1,2,0:T(8,128)(2,1)S(1)}, u32[]{:S(2)}, u32[]{:S(2)}) collective-permute-start(bf16[2,252,704]{1,2,0:T(8,128)(2,1)S(1)} %pad_maximum_fusion.2), channel_id=1, source_target_pairs={{1,3},{3,1},{5,7},{7,5},{9,11},{11,9},{13,15},{15,13},{17,19},{19,... | collective-permute-start | bytes 2128904 | tf_op jit(solution)/shard_map/ppermute | solution.py:53
  62.4 0.7 collective-permute-start.13
  66.3 1.6 %collective-permute-start.16 = (bf16[7,1,7,256]{3,2,1,0:T(8,128)(2,1)S(1)}, bf16[7,1,7,256]{3,2,1,0:T(8,128)(2,1)S(1)}, u32[]{:S(2)}, u32[]{:S(2)}) collective-permute-start(bf16[7,1,7,256]{3,2,1,0:T(8,128)(2,1)S(1)} %slice.581), channel_id=1, source_target_pairs={{1,5},{5,1},{3,7},{7,3},{9,13},{13,9},{11,15},{15,11},{17,21},{21,... | collective-permute-start | bytes 75272 | tf_op jit(solution)/shard_map/ppermute | solution.py:40
  67.0 0.9 collective-permute-start.17
  69.9 0.9 collective-permute-start.18
  71.2 0.9 collective-permute-start.19
  72.1 0.7 collective-permute-start.20
  73.0 0.7 collective-permute-start.21
  74.3 38.0 %collective-permute-start.22 = (bf16[920,128]{0,1:T(8,128)(2,1)S(1)}, bf16[920,128]{0,1:T(8,128)(2,1)S(1)}, u32[]{:S(2)}, u32[]{:S(2)}) collective-permute-start(bf16[920,128]{0,1:T(8,128)(2,1)S(1)} %maximum_maximum_fusion), channel_id=1, source_target_pairs={{0,1},{1,0},{2,3},{3,2},{4,5},{5,4},{6,7},{7,6},{8,9},{9,8},{10,11... | collective-permute-start | bytes 706568 | tf_op jit(solution)/shard_map/ppermute | solution.py:53
  (8 other events, 5.4 us)

commit v6 on v4

--- a/solution.py
+++ b/solution.py
@@ -1,6 +1,7 @@
 import jax
 import jax.numpy as jnp
 from jax import lax
+from jax.experimental.layout import Layout, with_layout_constraint
 from jax.sharding import PartitionSpec as P
 
 GRID_Y = 4
@@ -22,88 +23,95 @@
             self.position // self.stride[d] % self.counts[d] for d in range(3)
         )
 
+        flips = self.coords[0] + self.coords[1] + self.coords[2] // 2 + self.coords[2]
+        self.share_low = flips % 2 == 1
+
     def coord_of(self, device, dim):
         return device // self.stride[dim] % self.counts[dim]
 
-    def swapped(self, low, high, dim, odd):
-        by = self.stride[dim]
+    def swapped(self, low, high, dim, odd, raw=False, cross=1):
+        count = self.counts[dim]
         pairs = []
         for i in range(self.devices):
             c = self.coord_of(i, dim)
-            if c % 2 == odd and c + 1 < self.counts[dim]:
-                pairs += [(i, i + by), (i + by, i)]
+            up = c % 2 == odd
+            to = (c + (1 if up else -1)) % count
+            pairs.append((i, (i + (to - c) * self.stride[dim]) ^ cross))
         lower = self.coords[dim] % 2 == odd
         arrived = lax.ppermute(jnp.where(lower, high, low), AXIS, pairs)
+        if raw:
+            return arrived
         zero = jnp.zeros_like(arrived)
-        return jnp.where(lower, zero, arrived), jnp.where(lower, arrived, zero)
-
-    def exchanged(self, low, high, dim):
-        to_low, to_high = self.swapped(low, high, dim, 0)
+        to_low, to_high = jnp.where(lower, zero, arrived), jnp.where(lower, arrived, zero)
+        if odd or count % 2:
+            to_low = jnp.where(self.coords[dim] > 0, to_low, zero)
+            to_high = jnp.where(self.coords[dim] < count - 1, to_high, zero)
+        return to_low, to_high
+
+    def exchanged(self, low, high, dim, cross=1):
+        to_low, to_high = self.swapped(low, high, dim, 0, cross=cross)
         if self.counts[dim] > 2:
-            more_low, more_high = self.swapped(low, high, dim, 1)
+            more_low, more_high = self.swapped(low, high, dim, 1, cross=cross)
             to_low, to_high = to_low + more_low, to_high + more_high
         return to_low, to_high
 
-    def partner(self, value, bit):
-        return lax.ppermute(value, AXIS, [(i, i ^ bit) for i in range(self.devices)])
+    def partner(self, value, bits):
+        return lax.ppermute(value, AXIS, [(i, i ^ bits) for i in range(self.devices)])
 
     def has(self, bit):
         return (self.position & bit) != 0
 
 
-def line_bits():
-    bit = GRID_Z // 2
-    while bit:
-        yield bit
-        bit //= 2
+FIRST, SECOND = 3, 1
+
+
+def placed(near, high, low):
+    near = [
+        jnp.where(low, near[i ^ 1], near[i]) for i in range(GRID_Z)
+    ]
+    return [jnp.where(high, near[i ^ 2], near[i]) for i in range(GRID_Z)]
 
 
 def lines_gathered(grid, value):
-    held = value[None]
-    order = [0]
-    for bit in line_bits():
-        other = grid.partner(held, bit)
-        mine = grid.has(bit)
-        held = jnp.concatenate(
-            [jnp.where(mine, other, held), jnp.where(mine, held, other)], axis=0
-        )
-        order = order + [i | bit for i in order]
-    return [held[order.index(i)] for i in range(GRID_Z)]
-
-
-class Shares:
-    def __init__(self, grid, value):
-        self.grid = grid
-        self.width = value.shape[1] // GRID_Z
-        self.half = value.shape[0] // 2
-        self.blocks = [
-            value[:, i * self.width : (i + 1) * self.width] for i in range(GRID_Z)
-        ]
-
-    def packed(self, bit):
-        mine = self.grid.has(bit)
-        away = [
-            jnp.where(mine, self.blocks[i], self.blocks[i | bit])
-            for i in range(GRID_Z)
-            if not i & bit
-        ]
-        return jnp.concatenate(
-            [b[h : h + self.half] for h in (0, self.half) for b in away], axis=1
-        )
-
-    def take(self, bit, arrived):
-        mine = self.grid.has(bit)
-        lows = [i for i in range(GRID_Z) if not i & bit]
-        for at, i in enumerate(lows):
-            ends = (at * self.width, (at + len(lows)) * self.width)
-            came = jnp.concatenate([arrived[:, e : e + self.width] for e in ends], axis=0)
-            self.blocks[i], self.blocks[i | bit] = (
-                jnp.where(mine, came, self.blocks[i]),
-                jnp.where(mine, self.blocks[i | bit], came),
-            )
-
-    def value(self):
-        return jnp.concatenate(self.blocks, axis=1)
+    other = grid.partner(value, FIRST)
+    both = grid.partner(jnp.stack([value, other]), SECOND)
+    return [value, both[0], both[1], other]
+
+
+def packed(blocks):
+    half = blocks[0].shape[0] // 2
+    return jnp.concatenate([b[h : h + half] for h in (0, half) for b in blocks], axis=1)
+
+
+def unpacked(value, width):
+    return [
+        jnp.concatenate([value[:, e : e + width] for e in (i * width, (i + 2) * width)], axis=0)
+        for i in range(2)
+    ]
+
+
+def split(value, parts):
+    width = value.shape[1] // parts
+    return [value[:, i * width : (i + 1) * width] for i in range(parts)]
+
+
+def to_shares(grid, block):
+    shares = split(block, GRID_Z)
+    width = shares[0].shape[1]
+    high = grid.has(2)
+    kept = [jnp.where(high, shares[2 + i], shares[i]) for i in range(2)]
+    away = [jnp.where(high, shares[i], shares[2 + i]) for i in range(2)]
+    came = unpacked(grid.partner(packed(away), FIRST), width)
+    low = grid.share_low
+    own = [jnp.where(low, kept[1], kept[0]), jnp.where(low, came[1], came[0])]
+    away = [jnp.where(low, kept[0], kept[1]), jnp.where(low, came[0], came[1])]
+    came = unpacked(grid.partner(packed(away), SECOND), width)
+    near = [own[0], came[0], came[1], own[1]]
+    return jnp.concatenate(placed(near, high, grid.has(1)), axis=1)
+
+
+def by_rows(value):
+    return with_layout_constraint(value, Layout(major_to_minor=tuple(range(value.ndim))))
 
 
 def plane(field, dim, at):
@@ -194,18 +202,17 @@
     matrix = jnp.concatenate([matrix, coarse[:, None], fine[:, None]], axis=1)
     matrices = lines_gathered(grid, matrix)
     lane_owner = lax.broadcasted_iota(jnp.int32, (1, columns), 1) // width
+    owner_near = lane_owner ^ grid.coords[2]
     lumped = jnp.zeros((slot_count, columns), jnp.float32)
-    for p in range(GRID_Z):
-        both = jnp.sum(matrices[p][:, slot_count:].astype(jnp.float32), axis=1, keepdims=True)
-        lumped = jnp.where(lane_owner == p, both, lumped)
-
-    shares = Shares(grid, block)
-    for bit in line_bits():
-        shares.take(bit, grid.partner(shares.packed(bit), bit))
+    for r in range(GRID_Z):
+        both = jnp.sum(matrices[r][:, slot_count:].astype(jnp.float32), axis=1, keepdims=True)
+        lumped = jnp.where(owner_near == r, both, lumped)
+
+    mine = to_shares(grid, block)
     field = (
         jnp.zeros(shape, jnp.bfloat16)
         .at[1:, 1:, 1:]
-        .set(shares.value().reshape(edge, edge, edge, columns))
+        .set(mine.reshape(edge, edge, edge, columns))
     )
     field = with_ends(field, 2, to_next_partition(plane(field, 2, SIDE - 1), width), None)
     for dim in (1, 0):
@@ -219,8 +226,8 @@
         inside = inside & ~((at == 0) & first[dim])
 
     locked, field = lax.optimization_barrier((locked, field))
-    above = locked[-edge * edge :]
-    below = grid.exchanged(above, above, 0)[0]
+    above = by_rows(locked[-edge * edge :])
+    below = by_rows(grid.exchanged(above, above, 0, cross=0)[0])
     locked = jnp.concatenate([below, locked], axis=0)
 
     older = field
@@ -229,10 +236,10 @@
     for step, coeffs in enumerate(chebyshev_coeffs):
         rows = current.reshape(slot_count, columns)
         partial = lumped * rows.astype(jnp.float32)
-        for p in range(GRID_Z):
-            own = jnp.where(lane_owner == p, rows, jnp.zeros_like(rows))
+        for r in range(GRID_Z):
+            own = jnp.where(owner_near == r, rows, jnp.zeros_like(rows))
             partial = partial + jnp.dot(
-                matrices[p][:, :slot_count], own, preferred_element_type=jnp.float32
+                matrices[r][:, :slot_count], own, preferred_element_type=jnp.float32
             )
         partial = partial.reshape(shape)
         low, high = plane(partial, 2, 0), plane(partial, 2, SIDE - 1)
@@ -279,13 +286,14 @@
     sums = jnp.concatenate([partial[:1], partial[1:] + rest], axis=0)
     weights = sums.astype(jnp.bfloat16).reshape(SIDE * edge * edge, columns)
     share = 0.0
-    for p in range(GRID_Z):
+    for r in range(GRID_Z):
         share = share + lax.dot_general(
-            all_locked[p],
-            weights[:, p * width : (p + 1) * width],
+            all_locked[r],
+            jnp.where(owner_near == r, weights, jnp.zeros_like(weights)),
             (((0,), (0,)), ((), ())),
             preferred_element_type=jnp.float32,
         )
+    share = sum(split(share, GRID_Z))
     deep = share.shape[0] // GRID_Z
     share = jnp.concatenate(
         [share[i * deep : (i + 1) * deep] for i in range(GRID_Z)], axis=1
@@ -294,7 +302,7 @@
     low = sums[0].astype(jnp.bfloat16)
     stride, count = grid.stride[0], grid.counts[0]
     even = grid.coords[0] % 2 == 0
-    arrived = grid.partner(jnp.concatenate([share, low], axis=0), stride)
+    arrived = grid.partner(jnp.concatenate([share, low], axis=0), stride | 1)
     share = plus(share, arrived[:deep])
     to_high = jnp.where(even, arrived[deep:], jnp.zeros_like(low))
     if count > 2:
@@ -304,23 +312,24 @@
     )
     filtered = rounded(sums.reshape(owned_rows, columns))
 
-    share = summed_along(grid, share, grid.stride[1], grid.counts[1])
+    share = plus(share, grid.swapped(share, share, 1, 0, True))
+    share = plus(share, grid.swapped(share, share, 1, 1, True))
     share = summed_along(grid, share, stride * 2, count // 2)
 
-    shares = Shares(grid, filtered)
-    held = share[None]
-    order = [0]
-    for bit in line_bits():
-        mine = grid.has(bit)
-        sent = held.reshape(-1, columns)
-        arrived = grid.partner(jnp.concatenate([sent, shares.packed(bit)], axis=0), bit)
-        shares.take(bit, arrived[sent.shape[0] :])
-        other = arrived[: sent.shape[0]].reshape(held.shape)
-        held = jnp.concatenate(
-            [jnp.where(mine, other, held), jnp.where(mine, held, other)], axis=0
-        )
-        order = order + [i | bit for i in order]
-    held = [held[order.index(i)] for i in range(GRID_Z)]
+    high, low = grid.has(2), grid.share_low
+    near = placed(split(filtered, GRID_Z), high, grid.has(1))
+    sent = jnp.concatenate([share, packed([near[3], near[2]])], axis=0)
+    arrived = grid.partner(sent, FIRST)
+    held = jnp.stack([share, arrived[:deep]])
+    came = unpacked(arrived[deep:], width)
+    own = [near[0], came[0]]
+    away = [near[1], came[1]]
+    sent = jnp.concatenate([held.reshape(-1, columns), packed(away)], axis=0)
+    arrived = grid.partner(sent, SECOND)
+    others = arrived[: 2 * deep].reshape(held.shape)
+    came = unpacked(arrived[2 * deep :], width)
+    filtered = jnp.concatenate(placed([own[0], came[0], own[1], came[1]], high, low), axis=1)
+    held = placed([held[0], others[0], held[1], others[1]], high, low)
     intersection = jnp.concatenate(
         [
             jnp.concatenate([h[:, q * width : (q + 1) * width] for h in held], axis=1)
@@ -328,7 +337,7 @@
         ],
         axis=0,
     ).astype(jnp.float32)
-    return shares.value(), intersection
+    return filtered, intersection
 
 
 def solution(mesh):

time: 96.3 us -> 80.9 us (0.84)
  starting transfers between devices: 44 us -> 29.8 us
  local copies, waits for them, and re-layouts: 7.76 us -> 4.91 us
  other arithmetic: 4.56 us -> 6.12 us
    ppermute x11 -> x9, starting transfers between devices: 17.2 us -> 8.19 us  [partner(): lax.ppermute(value, AXIS, [(i, i ^ bits) for i in range(self.devices)])]
    ppermute x12 -> x14, starting transfers between devices: 26.7 us -> 21.6 us  [swapped(): arrived = lax.ppermute(jnp.where(lower, high, low), AXIS, pairs)]
    ppermute x12 -> x14, waiting for transfers between devices: 21.4 us -> 23.7 us  [swapped(): arrived = lax.ppermute(jnp.where(lower, high, low), AXIS, pairs)]
    ppermute x11 -> x9, waiting for transfers between devices: 11.8 us -> 9.79 us  [partner(): lax.ppermute(value, AXIS, [(i, i ^ bits) for i in range(self.devices)])]
    unnamed x18 -> x19, local copies, waits for them, and re-layouts: 2.73 us -> 0.91 us
    slice x18 -> x12, local copies, waits for them, and re-layouts: 2.22 us -> 1.19 us  [the longest x1 0.73 us: lines_gathered(): return [value, both[0], both[1], other]]
  transfers between devices with their start and end apart: 23 -> 23, of which waited for: 15 -> 17; matrix products, arithmetic and copies ran while one was open for 5% -> 7% of each run, Pallas kernels for 0% -> 0%
where the time goes in v6:
time: 80.9 us; the launch traced here: 80.7 us
  waiting for transfers between devices  33.4 us (41%)
  starting transfers between devices  29.8 us (37%)
  other arithmetic  6.12 us (8%)
  local copies, waits for them, and re-layouts  4.91 us (6%)
  matrix products  4.77 us (6%)
  between operations  1.68 us (2%)
    ppermute x14, waiting for transfers between devices, swapped(): arrived = lax.ppermute(jnp.where(lower, high, low), AXIS, pairs)  23.7 us
    ppermute x14, starting transfers between devices, swapped(): arrived = lax.ppermute(jnp.where(lower, high, low), AXIS, pairs)  21.6 us
    ppermute x9, waiting for transfers between devices, partner(): lax.ppermute(value, AXIS, [(i, i ^ bits) for i in range(self.devices)])  9.79 us
    ppermute x9, starting transfers between devices, partner(): lax.ppermute(value, AXIS, [(i, i ^ bits) for i in range(self.devices)])  8.19 us
    dot_general x12, matrix products, per_device(): jnp.dot(matrices[r][:, :slot_count], own, preferred_element_type=jnp.floa...  3.05 us
  transfers between devices with their start and end apart: 23, of which 17 were waited for; matrix products, arithmetic and copies ran while one was open for 7% of the time, Pallas kernels for 0%

profile of v6, /device:TPU:0, one launch (start us, length us, event | category | flops | bytes accessed | tf_op | source)
XLA Modules:
  0.0 80.7 jit_solution(11598404443596749783)
XLA Ops:
  0.8 0.8 copy-done.1
  1.8 2.4 %collective-permute-start.2 = (bf16[108,128]{1,0:T(8,128)(2,1)S(1)}, bf16[108,128]{1,0:T(8,128)(2,1)S(1)}, u32[]{:S(2)}, u32[]{:S(2)}) collective-permute-start(bf16[108,128]{1,0:T(8,128)(2,1)S(1)} %pad_maximum_fusion.21), channel_id=1, source_target_pairs={{0,3},{1,2},{2,1},{3,0},{4,7},{5,6},{6,5},{7,4},{8,11},{9,10},{10,... | collective-permute-start | bytes 82952 | tf_op jit(solution)/shard_map/ppermute | solution.py:59
  8.7 2.7 %collective-permute-start.5 = (bf16[7,1,7,128]{3,0,2,1:T(8,128)(2,1)S(1)}, bf16[7,1,7,128]{3,0,2,1:T(8,128)(2,1)S(1)}, u32[]{:S(2)}, u32[]{:S(2)}) collective-permute-start(bf16[7,1,7,128]{3,0,2,1:T(8,128)(2,1)S(1)} %slice.592), channel_id=1, source_target_pairs={{0,13},{1,12},{2,15},{3,14},{4,9},{5,8},{6,11},{7,10},{8,5},{9,4},... | collective-permute-start | bytes 37640 | tf_op jit(solution)/shard_map/ppermute | solution.py:41
  11.9 0.9 %collective-permute-done.5 = bf16[7,1,7,128]{3,0,2,1:T(8,128)(2,1)S(1)} collective-permute-done((bf16[7,1,7,128]{3,0,2,1:T(8,128)(2,1)S(1)}, bf16[7,1,7,128]{3,0,2,1:T(8,128)(2,1)S(1)}, u32[]{:S(2)}, u32[]{:S(2)}) %collective-permute-start.5) | collective-permute-done | bytes 12576 | tf_op jit(solution)/shard_map/ppermute | solution.py:41
  12.8 1.7 %collective-permute-done.4 = bf16[7,1,7,128]{3,0,2,1:T(8,128)(2,1)S(1)} collective-permute-done((bf16[7,1,7,128]{3,0,2,1:T(8,128)(2,1)S(1)}, bf16[7,1,7,128]{3,0,2,1:T(8,128)(2,1)S(1)}, u32[]{:S(2)}, u32[]{:S(2)}) %collective-permute-start.4) | collective-permute-done | bytes 12576 | tf_op jit(solution)/shard_map/ppermute | solution.py:41
  14.6 2.6 %collective-permute-start.6 = (bf16[1,7,7,128]{3,0,2,1:T(2,128)(2,1)S(1)}, bf16[1,7,7,128]{3,0,2,1:T(2,128)(2,1)S(1)}, u32[]{:S(2)}, u32[]{:S(2)}) collective-permute-start(bf16[1,7,7,128]{3,0,2,1:T(2,128)(2,1)S(1)} %pad_maximum_fusion.25), channel_id=1, source_target_pairs={{0,17},{1,16},{2,19},{3,18},{4,21},{5,20},{6,23},{7,22},{8,25},{9,... | collective-permute-start | bytes 37640 | tf_op jit(solution)/shard_map/ppermute | solution.py:41
  17.2 2.1 %collective-permute-done.6 = bf16[1,7,7,128]{3,0,2,1:T(2,128)(2,1)S(1)} collective-permute-done((bf16[1,7,7,128]{3,0,2,1:T(2,128)(2,1)S(1)}, bf16[1,7,7,128]{3,0,2,1:T(2,128)(2,1)S(1)}, u32[]{:S(2)}, u32[]{:S(2)}) %collective-permute-start.6) | collective-permute-done | bytes 12576 | tf_op jit(solution)/shard_map/ppermute | solution.py:41
  19.4 2.2 %collective-permute-start.7 = (bf16[36,704]{1,0:T(8,128)(2,1)S(1)}, bf16[36,704]{1,0:T(8,128)(2,1)S(1)}, u32[]{:S(2)}, u32[]{:S(2)}) collective-permute-start(bf16[36,704]{1,0:T(8,128)(2,1)S(1)} %slice.478), channel_id=1, source_target_pairs={{0,16},{1,17},{2,18},{3,19},{4,20},{5,21},{6,22},{7,23},{8,24},{9,... | collective-permute-start | bytes 152072 | tf_op jit(solution)/shard_map/ppermute | solution.py:41
  22.6 2.8 %collective-permute-done.7 = bf16[36,704]{1,0:T(8,128)(2,1)S(1)} collective-permute-done((bf16[36,704]{1,0:T(8,128)(2,1)S(1)}, bf16[36,704]{1,0:T(8,128)(2,1)S(1)}, u32[]{:S(2)}, u32[]{:S(2)}) %collective-permute-start.7) | collective-permute-done | bytes 50720 | tf_op jit(solution)/shard_map/ppermute | solution.py:41
  29.8 2.1 %collective-permute-done.8 = bf16[7,1,7,128]{3,0,2,1:T(8,128)(2,1)S(1)} collective-permute-done((bf16[7,1,7,128]{3,0,2,1:T(8,128)(2,1)S(1)}, bf16[7,1,7,128]{3,0,2,1:T(8,128)(2,1)S(1)}, u32[]{:S(2)}, u32[]{:S(2)}) %collective-permute-start.8) | collective-permute-done | bytes 12576 | tf_op jit(solution)/shard_map/ppermute | solution.py:41
  31.9 1.6 %collective-permute-done.9 = bf16[7,1,7,128]{3,0,2,1:T(8,128)(2,1)S(1)} collective-permute-done((bf16[7,1,7,128]{3,0,2,1:T(8,128)(2,1)S(1)}, bf16[7,1,7,128]{3,0,2,1:T(8,128)(2,1)S(1)}, u32[]{:S(2)}, u32[]{:S(2)}) %collective-permute-start.9) | collective-permute-done | bytes 12576 | tf_op jit(solution)/shard_map/ppermute | solution.py:41
  33.6 1.2 %collective-permute-start.10 = (bf16[1,7,7,128]{3,0,2,1:T(2,128)(2,1)S(1)}, bf16[1,7,7,128]{3,0,2,1:T(2,128)(2,1)S(1)}, u32[]{:S(2)}, u32[]{:S(2)}) collective-permute-start(bf16[1,7,7,128]{3,0,2,1:T(2,128)(2,1)S(1)} %get-tuple-element.44), channel_id=1, source_target_pairs={{0,17},{1,16},{2,19},{3,18},{4,21},{5,20},{6,23},{7,22},{8,25},{9,... | collective-permute-start | bytes 37640 | tf_op jit(solution)/shard_map/ppermute | solution.py:41
  34.7 1.2 %collective-permute-start.14 = (bf16[252,704]{0,1:T(8,128)(2,1)S(1)}, bf16[252,704]{0,1:T(8,128)(2,1)S(1)}, u32[]{:S(2)}, u32[]{:S(2)}) collective-permute-start(bf16[252,704]{0,1:T(8,128)(2,1)S(1)} %pad_maximum_fusion.2), channel_id=1, source_target_pairs={{0,3},{1,2},{2,1},{3,0},{4,7},{5,6},{6,5},{7,4},{8,11},{9,10},{10,... | collective-permute-start | bytes 1064456 | tf_op jit(solution)/shard_map/ppermute | solution.py:59
  35.9 1.9 %collective-permute-done.10 = bf16[1,7,7,128]{3,0,2,1:T(2,128)(2,1)S(1)} collective-permute-done((bf16[1,7,7,128]{3,0,2,1:T(2,128)(2,1)S(1)}, bf16[1,7,7,128]{3,0,2,1:T(2,128)(2,1)S(1)}, u32[]{:S(2)}, u32[]{:S(2)}) %collective-permute-start.10) | collective-permute-done | bytes 12576 | tf_op jit(solution)/shard_map/ppermute | solution.py:41
  39.5 0.9 %collective-permute-start.12 = (bf16[7,1,7,128]{3,0,2,1:T(8,128)(2,1)S(1)}, bf16[7,1,7,128]{3,0,2,1:T(8,128)(2,1)S(1)}, u32[]{:S(2)}, u32[]{:S(2)}) collective-permute-start(bf16[7,1,7,128]{3,0,2,1:T(8,128)(2,1)S(1)} %broadcast_select_fusion.48), channel_id=1, source_target_pairs={{0,13},{1,12},{2,15},{3,14},{4,9},{5,8},{6,11},{7,10},{8,5},{9,4},... | collective-permute-start | bytes 37640 | tf_op jit(solution)/shard_map/ppermute | solution.py:41
  40.4 1.4 %collective-permute-start.11 = (bf16[7,1,7,128]{3,0,2,1:T(8,128)(2,1)S(1)}, bf16[7,1,7,128]{3,0,2,1:T(8,128)(2,1)S(1)}, u32[]{:S(2)}, u32[]{:S(2)}) collective-permute-start(bf16[7,1,7,128]{3,0,2,1:T(8,128)(2,1)S(1)} %get-tuple-element.41), channel_id=1, source_target_pairs={{0,5},{1,4},{2,7},{3,6},{4,1},{5,0},{6,3},{7,2},{8,13},{9,12},{10,... | collective-permute-start | bytes 37640 | tf_op jit(solution)/shard_map/ppermute | solution.py:41
  41.9 1.9 %collective-permute-done.12 = bf16[7,1,7,128]{3,0,2,1:T(8,128)(2,1)S(1)} collective-permute-done((bf16[7,1,7,128]{3,0,2,1:T(8,128)(2,1)S(1)}, bf16[7,1,7,128]{3,0,2,1:T(8,128)(2,1)S(1)}, u32[]{:S(2)}, u32[]{:S(2)}) %collective-permute-start.12) | collective-permute-done | bytes 12576 | tf_op jit(solution)/shard_map/ppermute | solution.py:41
  43.8 1.5 %collective-permute-done.14 = bf16[252,704]{0,1:T(8,128)(2,1)S(1)} collective-permute-done((bf16[252,704]{0,1:T(8,128)(2,1)S(1)}, bf16[252,704]{0,1:T(8,128)(2,1)S(1)}, u32[]{:S(2)}, u32[]{:S(2)}) %collective-permute-start.14) | collective-permute-done | bytes 354848 | tf_op jit(solution)/shard_map/ppermute | solution.py:59
  45.6 2.2 %collective-permute-start.13 = (bf16[1,7,7,128]{3,0,2,1:T(2,128)(2,1)S(1)}, bf16[1,7,7,128]{3,0,2,1:T(2,128)(2,1)S(1)}, u32[]{:S(2)}, u32[]{:S(2)}) collective-permute-start(bf16[1,7,7,128]{3,0,2,1:T(2,128)(2,1)S(1)} %broadcast_select_fusion.35), channel_id=1, source_target_pairs={{0,17},{1,16},{2,19},{3,18},{4,21},{5,20},{6,23},{7,22},{8,25},{9,... | collective-permute-start | bytes 37640 | tf_op jit(solution)/shard_map/ppermute | solution.py:41
  47.8 2.0 %collective-permute-done.13 = bf16[1,7,7,128]{3,0,2,1:T(2,128)(2,1)S(1)} collective-permute-done((bf16[1,7,7,128]{3,0,2,1:T(2,128)(2,1)S(1)}, bf16[1,7,7,128]{3,0,2,1:T(2,128)(2,1)S(1)}, u32[]{:S(2)}, u32[]{:S(2)}) %collective-permute-start.13) | collective-permute-done | bytes 12576 | tf_op jit(solution)/shard_map/ppermute | solution.py:41
  51.7 1.4 %collective-permute-start.16 = (bf16[7,1,7,128]{3,0,2,1:T(8,128)(2,1)S(1)}, bf16[7,1,7,128]{3,0,2,1:T(8,128)(2,1)S(1)}, u32[]{:S(2)}, u32[]{:S(2)}) collective-permute-start(bf16[7,1,7,128]{3,0,2,1:T(8,128)(2,1)S(1)} %slice.800), channel_id=1, source_target_pairs={{0,5},{1,4},{2,7},{3,6},{4,1},{5,0},{6,3},{7,2},{8,13},{9,12},{10,... | collective-permute-start | bytes 37640 | tf_op jit(solution)/shard_map/ppermute | solution.py:41
  53.1 2.5 %collective-permute-start.17 = (bf16[7,1,7,128]{3,0,2,1:T(8,128)(2,1)S(1)}, bf16[7,1,7,128]{3,0,2,1:T(8,128)(2,1)S(1)}, u32[]{:S(2)}, u32[]{:S(2)}) collective-permute-start(bf16[7,1,7,128]{3,0,2,1:T(8,128)(2,1)S(1)} %slice.800), channel_id=1, source_target_pairs={{0,13},{1,12},{2,15},{3,14},{4,9},{5,8},{6,11},{7,10},{8,5},{9,4},... | collective-permute-start | bytes 37640 | tf_op jit(solution)/shard_map/ppermute | solution.py:41
  55.6 1.5 %collective-permute-done.17 = bf16[7,1,7,128]{3,0,2,1:T(8,128)(2,1)S(1)} collective-permute-done((bf16[7,1,7,128]{3,0,2,1:T(8,128)(2,1)S(1)}, bf16[7,1,7,128]{3,0,2,1:T(8,128)(2,1)S(1)}, u32[]{:S(2)}, u32[]{:S(2)}) %collective-permute-start.17) | collective-permute-done | bytes 12576 | tf_op jit(solution)/shard_map/ppermute | solution.py:41
  58.9 1.4 %collective-permute-start.18 = (bf16[212,128]{1,0:T(8,128)(2,1)S(1)}, bf16[212,128]{1,0:T(8,128)(2,1)S(1)}, u32[]{:S(2)}, u32[]{:S(2)}) collective-permute-start(bf16[212,128]{1,0:T(8,128)(2,1)S(1)} %pad_maximum_fusion.14), channel_id=1, source_target_pairs={{0,17},{1,16},{2,19},{3,18},{4,21},{5,20},{6,23},{7,22},{8,25},{9,... | collective-permute-start | bytes 162824 | tf_op jit(solution)/shard_map/ppermute | solution.py:59
  60.4 3.4 %collective-permute-done.18 = bf16[212,128]{1,0:T(8,128)(2,1)S(1)} collective-permute-done((bf16[212,128]{1,0:T(8,128)(2,1)S(1)}, bf16[212,128]{1,0:T(8,128)(2,1)S(1)}, u32[]{:S(2)}, u32[]{:S(2)}) %collective-permute-start.18) | collective-permute-done | bytes 54304 | tf_op jit(solution)/shard_map/ppermute | solution.py:59
  64.5 3.1 %collective-permute-done.19 = bf16[176,128]{1,0:T(8,128)(2,1)S(1)} collective-permute-done((bf16[176,128]{1,0:T(8,128)(2,1)S(1)}, bf16[176,128]{1,0:T(8,128)(2,1)S(1)}, u32[]{:S(2)}, u32[]{:S(2)}) %collective-permute-start.19) | collective-permute-done | bytes 45088 | tf_op jit(solution)/shard_map/ppermute | solution.py:41
  67.6 2.5 %collective-permute-start.20 = (bf16[176,128]{1,0:T(8,128)(2,1)S(1)}, bf16[176,128]{1,0:T(8,128)(2,1)S(1)}, u32[]{:S(2)}, u32[]{:S(2)}) collective-permute-start(bf16[176,128]{1,0:T(8,128)(2,1)S(1)} %add_convert_fusion.1), channel_id=1, source_target_pairs={{0,13},{1,12},{2,15},{3,14},{4,9},{5,8},{6,11},{7,10},{8,5},{9,4},... | collective-permute-start | bytes 135176 | tf_op jit(solution)/shard_map/ppermute | solution.py:41
  70.1 2.1 %collective-permute-done.20 = bf16[176,128]{1,0:T(8,128)(2,1)S(1)} collective-permute-done((bf16[176,128]{1,0:T(8,128)(2,1)S(1)}, bf16[176,128]{1,0:T(8,128)(2,1)S(1)}, u32[]{:S(2)}, u32[]{:S(2)}) %collective-permute-start.20) | collective-permute-done | bytes 45088 | tf_op jit(solution)/shard_map/ppermute | solution.py:41
  72.3 1.3 %collective-permute-start.21 = (bf16[284,128]{1,0:T(8,128)(2,1)S(1)}, bf16[284,128]{1,0:T(8,128)(2,1)S(1)}, u32[]{:S(2)}, u32[]{:S(2)}) collective-permute-start(bf16[284,128]{1,0:T(8,128)(2,1)S(1)} %maximum_maximum_fusion.1), channel_id=1, source_target_pairs={{0,3},{1,2},{2,1},{3,0},{4,7},{5,6},{6,5},{7,4},{8,11},{9,10},{10,... | collective-permute-start | bytes 218120 | tf_op jit(solution)/shard_map/ppermute | solution.py:59
  73.7 3.0 %collective-permute-done.21 = bf16[284,128]{1,0:T(8,128)(2,1)S(1)} collective-permute-done((bf16[284,128]{1,0:T(8,128)(2,1)S(1)}, bf16[284,128]{1,0:T(8,128)(2,1)S(1)}, u32[]{:S(2)}, u32[]{:S(2)}) %collective-permute-start.21) | collective-permute-done | bytes 72736 | tf_op jit(solution)/shard_map/ppermute | solution.py:59
  77.1 1.2 %collective-permute-done.22 = bf16[460,128]{1,0:T(8,128)(2,1)S(1)} collective-permute-done((bf16[460,128]{1,0:T(8,128)(2,1)S(1)}, bf16[460,128]{1,0:T(8,128)(2,1)S(1)}, u32[]{:S(2)}, u32[]{:S(2)}) %collective-permute-start.22) | collective-permute-done | bytes 117792 | tf_op jit(solution)/shard_map/ppermute | solution.py:59
  79.8 1.0 %maximum_convert_fusion = f32[704,128]{1,0:T(8,128)} fusion(bf16[176,32]{1,0:T(8,128)(2,1)S(1)} %get-tuple-element.132, bf16[176,32]{1,0:T(8,128)(2,1)S(1)} %get-tuple-element.128, bf16[176,32]{1,0:T(8,128)(2,1)S(1)} %get-tuple-element.124, bf16[176,32]{1,0:T(8,128)(2,1)S(1)} %get-tuple-element.120, bf16[176,32]{1,0:T(8,128)(2,1)S(1)} %get-tuple-element.133, ...), kind=kLoop, calls=%fused_computation.77 | loop fusion | flops 2883584 | bytes 540672 | tf_op jit(solution)/shard_map/convert_element_type | solution.py:339
  (183 shorter events, 18.6 us)
Async XLA Ops:
  0.6 4.1 %copy-start = (bf16[1,343,343]{2,1,0:T(8,128)(2,1)S(1)}, bf16[1,343,343]{2,1,0:T(8,128)(2,1)}, u32[]{:S(2)}) copy-start(bf16[1,343,343]{2,1,0:T(8,128)(2,1)} %param.8) | copy-start | bytes 705898
  0.7 0.9 %copy-start.1 = (bf16[216,128]{1,0:T(8,128)(2,1)S(1)}, bf16[216,128]{1,0:T(8,128)(2,1)}, u32[]{:S(2)}) copy-start(bf16[216,128]{1,0:T(8,128)(2,1)} %param.7) | copy-start | bytes 165892
  1.7 2.6 %copy-start.4 = (s32[1,343]{1,0:T(1,128)S(1)}, s32[1,343]{1,0:T(1,128)}, u32[]{:S(2)}) copy-start(s32[1,343]{1,0:T(1,128)} %param.9) | copy-start | bytes 4120
  1.8 2.5 %copy-start.3 = (f32[343]{0:T(512)S(1)}, f32[343]{0:T(512)}, u32[]{:S(2)}) copy-start(f32[343]{0:T(512)} %param.10) | copy-start | bytes 4120
  1.8 4.3 %collective-permute-start.2 = (bf16[108,128]{1,0:T(8,128)(2,1)S(1)}, bf16[108,128]{1,0:T(8,128)(2,1)S(1)}, u32[]{:S(2)}, u32[]{:S(2)}) collective-permute-start(bf16[108,128]{1,0:T(8,128)(2,1)S(1)} %pad_maximum_fusion.21), channel_id=1, source_target_pairs={{0,3},{1,2},{2,1},{3,0},{4,7},{5,6},{6,5},{7,4},{8,11},{9,10},{10,... | collective-permute-start | bytes 82952 | tf_op jit(solution)/shard_map/ppermute | solution.py:59
  5.5 16.1 %collective-permute-start = (bf16[343,345]{1,0:T(8,128)(2,1)S(1)}, bf16[343,345]{1,0:T(8,128)(2,1)S(1)}, u32[]{:S(2)}, u32[]{:S(2)}) collective-permute-start(bf16[343,345]{1,0:T(8,128)(2,1)S(1)} %pad_maximum_fusion.3), channel_id=1, source_target_pairs={{0,3},{1,2},{2,1},{3,0},{4,7},{5,6},{6,5},{7,4},{8,11},{9,10},{10,... | collective-permute-start | bytes 710018 | tf_op jit(solution)/shard_map/ppermute | solution.py:59
  6.4 1.6 %collective-permute-start.3 = (bf16[108,128]{1,0:T(8,128)(2,1)S(1)}, bf16[108,128]{1,0:T(8,128)(2,1)S(1)}, u32[]{:S(2)}, u32[]{:S(2)}) collective-permute-start(bf16[108,128]{1,0:T(8,128)(2,1)S(1)} %pad_maximum_fusion.22), channel_id=1, source_target_pairs={{0,1},{1,0},{2,3},{3,2},{4,5},{5,4},{6,7},{7,6},{8,9},{9,8},{10,11... | collective-permute-start | bytes 82952 | tf_op jit(solution)/shard_map/ppermute | solution.py:59
  8.7 4.1 %collective-permute-start.5 = (bf16[7,1,7,128]{3,0,2,1:T(8,128)(2,1)S(1)}, bf16[7,1,7,128]{3,0,2,1:T(8,128)(2,1)S(1)}, u32[]{:S(2)}, u32[]{:S(2)}) collective-permute-start(bf16[7,1,7,128]{3,0,2,1:T(8,128)(2,1)S(1)} %slice.592), channel_id=1, source_target_pairs={{0,13},{1,12},{2,15},{3,14},{4,9},{5,8},{6,11},{7,10},{8,5},{9,4},... | collective-permute-start | bytes 37640 | tf_op jit(solution)/shard_map/ppermute | solution.py:41
  11.4 3.1 %collective-permute-start.4 = (bf16[7,1,7,128]{3,0,2,1:T(8,128)(2,1)S(1)}, bf16[7,1,7,128]{3,0,2,1:T(8,128)(2,1)S(1)}, u32[]{:S(2)}, u32[]{:S(2)}) collective-permute-start(bf16[7,1,7,128]{3,0,2,1:T(8,128)(2,1)S(1)} %slice.592), channel_id=1, source_target_pairs={{0,5},{1,4},{2,7},{3,6},{4,1},{5,0},{6,3},{7,2},{8,13},{9,12},{10,... | collective-permute-start | bytes 37640 | tf_op jit(solution)/shard_map/ppermute | solution.py:41
  11.9 7.5 %copy-start.2 = (bf16[216,704]{1,0:T(8,128)(2,1)S(1)}, bf16[216,704]{1,0:T(8,128)(2,1)}, u32[]{:S(2)}) copy-start(bf16[216,704]{1,0:T(8,128)(2,1)} %param.11) | copy-start | bytes 912388
  14.6 4.7 %collective-permute-start.6 = (bf16[1,7,7,128]{3,0,2,1:T(2,128)(2,1)S(1)}, bf16[1,7,7,128]{3,0,2,1:T(2,128)(2,1)S(1)}, u32[]{:S(2)}, u32[]{:S(2)}) collective-permute-start(bf16[1,7,7,128]{3,0,2,1:T(2,128)(2,1)S(1)} %pad_maximum_fusion.25), channel_id=1, source_target_pairs={{0,17},{1,16},{2,19},{3,18},{4,21},{5,20},{6,23},{7,22},{8,25},{9,... | collective-permute-start | bytes 37640 | tf_op jit(solution)/shard_map/ppermute | solution.py:41
  19.4 6.0 %collective-permute-start.7 = (bf16[36,704]{1,0:T(8,128)(2,1)S(1)}, bf16[36,704]{1,0:T(8,128)(2,1)S(1)}, u32[]{:S(2)}, u32[]{:S(2)}) collective-permute-start(bf16[36,704]{1,0:T(8,128)(2,1)S(1)} %slice.478), channel_id=1, source_target_pairs={{0,16},{1,17},{2,18},{3,19},{4,20},{5,21},{6,22},{7,23},{8,24},{9,... | collective-permute-start | bytes 152072 | tf_op jit(solution)/shard_map/ppermute | solution.py:41
  22.1 3.8 %collective-permute-start.1 = (bf16[2,343,345]{2,0,1:T(2,128)(2,1)S(1)}, bf16[2,343,345]{2,0,1:T(2,128)(2,1)S(1)}, u32[]{:S(2)}, u32[]{:S(2)}) collective-permute-start(bf16[2,343,345]{2,0,1:T(2,128)(2,1)S(1)} %copy.169), channel_id=1, source_target_pairs={{0,1},{1,0},{2,3},{3,2},{4,5},{5,4},{6,7},{7,6},{8,9},{9,8},{10,11... | collective-permute-start | bytes 1420028 | tf_op jit(solution)/shard_map/ppermute | solution.py:59
  28.7 3.2 %collective-permute-start.8 = (bf16[7,1,7,128]{3,0,2,1:T(8,128)(2,1)S(1)}, bf16[7,1,7,128]{3,0,2,1:T(8,128)(2,1)S(1)}, u32[]{:S(2)}, u32[]{:S(2)}) collective-permute-start(bf16[7,1,7,128]{3,0,2,1:T(8,128)(2,1)S(1)} %get-tuple-element.77), channel_id=1, source_target_pairs={{0,5},{1,4},{2,7},{3,6},{4,1},{5,0},{6,3},{7,2},{8,13},{9,12},{10,... | collective-permute-start | bytes 37640 | tf_op jit(solution)/shard_map/ppermute | solution.py:41
  29.4 4.0 %collective-permute-start.9 = (bf16[7,1,7,128]{3,0,2,1:T(8,128)(2,1)S(1)}, bf16[7,1,7,128]{3,0,2,1:T(8,128)(2,1)S(1)}, u32[]{:S(2)}, u32[]{:S(2)}) collective-permute-start(bf16[7,1,7,128]{3,0,2,1:T(8,128)(2,1)S(1)} %get-tuple-element.78), channel_id=1, source_target_pairs={{0,13},{1,12},{2,15},{3,14},{4,9},{5,8},{6,11},{7,10},{8,5},{9,4},... | collective-permute-start | bytes 37640 | tf_op jit(solution)/shard_map/ppermute | solution.py:41
  33.6 4.2 %collective-permute-start.10 = (bf16[1,7,7,128]{3,0,2,1:T(2,128)(2,1)S(1)}, bf16[1,7,7,128]{3,0,2,1:T(2,128)(2,1)S(1)}, u32[]{:S(2)}, u32[]{:S(2)}) collective-permute-start(bf16[1,7,7,128]{3,0,2,1:T(2,128)(2,1)S(1)} %get-tuple-element.44), channel_id=1, source_target_pairs={{0,17},{1,16},{2,19},{3,18},{4,21},{5,20},{6,23},{7,22},{8,25},{9,... | collective-permute-start | bytes 37640 | tf_op jit(solution)/shard_map/ppermute | solution.py:41
  34.7 10.5 %collective-permute-start.14 = (bf16[252,704]{0,1:T(8,128)(2,1)S(1)}, bf16[252,704]{0,1:T(8,128)(2,1)S(1)}, u32[]{:S(2)}, u32[]{:S(2)}) collective-permute-start(bf16[252,704]{0,1:T(8,128)(2,1)S(1)} %pad_maximum_fusion.2), channel_id=1, source_target_pairs={{0,3},{1,2},{2,1},{3,0},{4,7},{5,6},{6,5},{7,4},{8,11},{9,10},{10,... | collective-permute-start | bytes 1064456 | tf_op jit(solution)/shard_map/ppermute | solution.py:59
  39.5 4.2 %collective-permute-start.12 = (bf16[7,1,7,128]{3,0,2,1:T(8,128)(2,1)S(1)}, bf16[7,1,7,128]{3,0,2,1:T(8,128)(2,1)S(1)}, u32[]{:S(2)}, u32[]{:S(2)}) collective-permute-start(bf16[7,1,7,128]{3,0,2,1:T(8,128)(2,1)S(1)} %broadcast_select_fusion.48), channel_id=1, source_target_pairs={{0,13},{1,12},{2,15},{3,14},{4,9},{5,8},{6,11},{7,10},{8,5},{9,4},... | collective-permute-start | bytes 37640 | tf_op jit(solution)/shard_map/ppermute | solution.py:41
  40.4 3.3 %collective-permute-start.11 = (bf16[7,1,7,128]{3,0,2,1:T(8,128)(2,1)S(1)}, bf16[7,1,7,128]{3,0,2,1:T(8,128)(2,1)S(1)}, u32[]{:S(2)}, u32[]{:S(2)}) collective-permute-start(bf16[7,1,7,128]{3,0,2,1:T(8,128)(2,1)S(1)} %get-tuple-element.41), channel_id=1, source_target_pairs={{0,5},{1,4},{2,7},{3,6},{4,1},{5,0},{6,3},{7,2},{8,13},{9,12},{10,... | collective-permute-start | bytes 37640 | tf_op jit(solution)/shard_map/ppermute | solution.py:41
  45.4 4.7 %collective-permute-start.15 = (bf16[2,252,704]{1,2,0:T(8,128)(2,1)S(1)}, bf16[2,252,704]{1,2,0:T(8,128)(2,1)S(1)}, u32[]{:S(2)}, u32[]{:S(2)}) collective-permute-start(bf16[2,252,704]{1,2,0:T(8,128)(2,1)S(1)} %pad_maximum_fusion), channel_id=1, source_target_pairs={{0,1},{1,0},{2,3},{3,2},{4,5},{5,4},{6,7},{7,6},{8,9},{9,8},{10,11... | collective-permute-start | bytes 2128904 | tf_op jit(solution)/shard_map/ppermute | solution.py:59
  45.6 4.3 %collective-permute-start.13 = (bf16[1,7,7,128]{3,0,2,1:T(2,128)(2,1)S(1)}, bf16[1,7,7,128]{3,0,2,1:T(2,128)(2,1)S(1)}, u32[]{:S(2)}, u32[]{:S(2)}) collective-permute-start(bf16[1,7,7,128]{3,0,2,1:T(2,128)(2,1)S(1)} %broadcast_select_fusion.35), channel_id=1, source_target_pairs={{0,17},{1,16},{2,19},{3,18},{4,21},{5,20},{6,23},{7,22},{8,25},{9,... | collective-permute-start | bytes 37640 | tf_op jit(solution)/shard_map/ppermute | solution.py:41
  51.7 3.9 %collective-permute-start.16 = (bf16[7,1,7,128]{3,0,2,1:T(8,128)(2,1)S(1)}, bf16[7,1,7,128]{3,0,2,1:T(8,128)(2,1)S(1)}, u32[]{:S(2)}, u32[]{:S(2)}) collective-permute-start(bf16[7,1,7,128]{3,0,2,1:T(8,128)(2,1)S(1)} %slice.800), channel_id=1, source_target_pairs={{0,5},{1,4},{2,7},{3,6},{4,1},{5,0},{6,3},{7,2},{8,13},{9,12},{10,... | collective-permute-start | bytes 37640 | tf_op jit(solution)/shard_map/ppermute | solution.py:41
  53.1 4.0 %collective-permute-start.17 = (bf16[7,1,7,128]{3,0,2,1:T(8,128)(2,1)S(1)}, bf16[7,1,7,128]{3,0,2,1:T(8,128)(2,1)S(1)}, u32[]{:S(2)}, u32[]{:S(2)}) collective-permute-start(bf16[7,1,7,128]{3,0,2,1:T(8,128)(2,1)S(1)} %slice.800), channel_id=1, source_target_pairs={{0,13},{1,12},{2,15},{3,14},{4,9},{5,8},{6,11},{7,10},{8,5},{9,4},... | collective-permute-start | bytes 37640 | tf_op jit(solution)/shard_map/ppermute | solution.py:41
  58.9 4.8 %collective-permute-start.18 = (bf16[212,128]{1,0:T(8,128)(2,1)S(1)}, bf16[212,128]{1,0:T(8,128)(2,1)S(1)}, u32[]{:S(2)}, u32[]{:S(2)}) collective-permute-start(bf16[212,128]{1,0:T(8,128)(2,1)S(1)} %pad_maximum_fusion.14), channel_id=1, source_target_pairs={{0,17},{1,16},{2,19},{3,18},{4,21},{5,20},{6,23},{7,22},{8,25},{9,... | collective-permute-start | bytes 162824 | tf_op jit(solution)/shard_map/ppermute | solution.py:59
  63.9 3.7 %collective-permute-start.19 = (bf16[176,128]{1,0:T(8,128)(2,1)S(1)}, bf16[176,128]{1,0:T(8,128)(2,1)S(1)}, u32[]{:S(2)}, u32[]{:S(2)}) collective-permute-start(bf16[176,128]{1,0:T(8,128)(2,1)S(1)} %add_convert_fusion.2), channel_id=1, source_target_pairs={{0,5},{1,4},{2,7},{3,6},{4,1},{5,0},{6,3},{7,2},{8,13},{9,12},{10,... | collective-permute-start | bytes 135176 | tf_op jit(solution)/shard_map/ppermute | solution.py:41
  67.6 4.6 %collective-permute-start.20 = (bf16[176,128]{1,0:T(8,128)(2,1)S(1)}, bf16[176,128]{1,0:T(8,128)(2,1)S(1)}, u32[]{:S(2)}, u32[]{:S(2)}) collective-permute-start(bf16[176,128]{1,0:T(8,128)(2,1)S(1)} %add_convert_fusion.1), channel_id=1, source_target_pairs={{0,13},{1,12},{2,15},{3,14},{4,9},{5,8},{6,11},{7,10},{8,5},{9,4},... | collective-permute-start | bytes 135176 | tf_op jit(solution)/shard_map/ppermute | solution.py:41
  72.3 4.3 %collective-permute-start.21 = (bf16[284,128]{1,0:T(8,128)(2,1)S(1)}, bf16[284,128]{1,0:T(8,128)(2,1)S(1)}, u32[]{:S(2)}, u32[]{:S(2)}) collective-permute-start(bf16[284,128]{1,0:T(8,128)(2,1)S(1)} %maximum_maximum_fusion.1), channel_id=1, source_target_pairs={{0,3},{1,2},{2,1},{3,0},{4,7},{5,6},{6,5},{7,4},{8,11},{9,10},{10,... | collective-permute-start | bytes 218120 | tf_op jit(solution)/shard_map/ppermute | solution.py:59
  76.9 1.4 %collective-permute-start.22 = (bf16[460,128]{1,0:T(8,128)(2,1)S(1)}, bf16[460,128]{1,0:T(8,128)(2,1)S(1)}, u32[]{:S(2)}, u32[]{:S(2)}) collective-permute-start(bf16[460,128]{1,0:T(8,128)(2,1)S(1)} %maximum_maximum_fusion), channel_id=1, source_target_pairs={{0,1},{1,0},{2,3},{3,2},{4,5},{5,4},{6,7},{7,6},{8,9},{9,8},{10,11... | collective-permute-start | bytes 353288 | tf_op jit(solution)/shard_map/ppermute | solution.py:59

commit v7 on v6

--- a/solution.py
+++ b/solution.py
@@ -72,12 +72,6 @@
     return [jnp.where(high, near[i ^ 2], near[i]) for i in range(GRID_Z)]
 
 
-def lines_gathered(grid, value):
-    other = grid.partner(value, FIRST)
-    both = grid.partner(jnp.stack([value, other]), SECOND)
-    return [value, both[0], both[1], other]
-
-
 def packed(blocks):
     half = blocks[0].shape[0] // 2
     return jnp.concatenate([b[h : h + half] for h in (0, half) for b in blocks], axis=1)
@@ -138,17 +132,15 @@
     return jnp.concatenate([kept, jnp.zeros_like(value[..., :width])], axis=-1)
 
 
-def slots_matrix(cell_matrix, connectivity, slot_count):
-    total = None
+def slots_matrix(cell_matrix, connectivity, potential):
+    slots = jnp.arange(potential.shape[0], dtype=jnp.int32)
+    total = jnp.where(slots[:, None] == slots[None, :], potential[:, None], 0.0)
     for c in range(cell_matrix.shape[0]):
-        chosen = (
-            connectivity[c][:, None] == jnp.arange(slot_count, dtype=jnp.int32)[None, :]
-        ).astype(jnp.bfloat16)
+        chosen = (connectivity[c][:, None] == slots[None, :]).astype(jnp.bfloat16)
         rows = lax.dot_general(
             chosen, cell_matrix[c], (((0,), (0,)), ((), ())), preferred_element_type=jnp.float32
         ).astype(jnp.bfloat16)
-        both = jnp.dot(rows, chosen, preferred_element_type=jnp.float32)
-        total = both if total is None else total + both
+        total = total + jnp.dot(rows, chosen, preferred_element_type=jnp.float32)
     return total.astype(jnp.bfloat16)
 
 
@@ -196,17 +188,15 @@
     grid = Grid()
     shape = (SIDE, SIDE, SIDE, columns)
 
-    matrix = slots_matrix(cell_matrix, connectivity, slot_count)
-    coarse = rounded(potential)
-    fine = rounded(potential - coarse.astype(jnp.float32))
-    matrix = jnp.concatenate([matrix, coarse[:, None], fine[:, None]], axis=1)
-    matrices = lines_gathered(grid, matrix)
+    matrix = slots_matrix(cell_matrix, connectivity, potential)
+    padded = jnp.pad(matrix, ((0, -slot_count % 16), (0, 0)))
+    other = grid.partner(padded, FIRST)
+    both = grid.partner(jnp.concatenate([padded, other], axis=0), SECOND)
+    above = padded.shape[0]
+    matrices = [padded, both[:above], both[above:], other]
+    matrices = [m[:slot_count] for m in matrices]
     lane_owner = lax.broadcasted_iota(jnp.int32, (1, columns), 1) // width
     owner_near = lane_owner ^ grid.coords[2]
-    lumped = jnp.zeros((slot_count, columns), jnp.float32)
-    for r in range(GRID_Z):
-        both = jnp.sum(matrices[r][:, slot_count:].astype(jnp.float32), axis=1, keepdims=True)
-        lumped = jnp.where(owner_near == r, both, lumped)
 
     mine = to_shares(grid, block)
     field = (
@@ -225,21 +215,16 @@
         at = lax.broadcasted_iota(jnp.int32, shape, dim)
         inside = inside & ~((at == 0) & first[dim])
 
-    locked, field = lax.optimization_barrier((locked, field))
-    above = by_rows(locked[-edge * edge :])
-    below = by_rows(grid.exchanged(above, above, 0, cross=0)[0])
-    locked = jnp.concatenate([below, locked], axis=0)
-
     older = field
     current = field
     steps = len(chebyshev_coeffs)
     for step, coeffs in enumerate(chebyshev_coeffs):
         rows = current.reshape(slot_count, columns)
-        partial = lumped * rows.astype(jnp.float32)
+        partial = 0.0
         for r in range(GRID_Z):
             own = jnp.where(owner_near == r, rows, jnp.zeros_like(rows))
             partial = partial + jnp.dot(
-                matrices[r][:, :slot_count], own, preferred_element_type=jnp.float32
+                matrices[r], own, preferred_element_type=jnp.float32
             )
         partial = partial.reshape(shape)
         low, high = plane(partial, 2, 0), plane(partial, 2, SIDE - 1)
@@ -249,16 +234,20 @@
             low + to_next_partition(high, width),
             high + to_previous_partition(low, width),
         )
-        if step == 0:
-            locked, partial = lax.optimization_barrier((locked, partial))
-            all_locked = lines_gathered(grid, locked)
         if step == steps - 1:
             break
         for dim in (1, 0):
             low, high = plane(partial, dim, 0), plane(partial, dim, SIDE - 1)
-            to_low, to_high = grid.exchanged(
-                low.astype(jnp.bfloat16), high.astype(jnp.bfloat16), dim
-            )
+            low16, high16 = low.astype(jnp.bfloat16), high.astype(jnp.bfloat16)
+            if (step, dim) == (0, 0):
+                locked, low16, high16 = lax.optimization_barrier((locked, low16, high16))
+                top = by_rows(locked[-edge * edge :])
+                bottom = by_rows(grid.exchanged(top, top, 0, cross=0)[0])
+                locked = jnp.concatenate([bottom, locked], axis=0)
+            if (step, dim) == (1, 1):
+                locked, low16, high16 = lax.optimization_barrier((locked, low16, high16))
+                other_locked = grid.partner(locked, FIRST)
+            to_low, to_high = grid.exchanged(low16, high16, dim)
             partial = with_ends(
                 partial,
                 dim,
@@ -271,10 +260,11 @@
         following = rounded(jnp.where(inside, following, 0.0))
         older = current
         current = following
-        if step == 1:
-            current, all_locked = lax.optimization_barrier((current, all_locked))
 
     low = plane(partial, 1, 0).astype(jnp.bfloat16)
+    locked, other_locked, low = lax.optimization_barrier((locked, other_locked, low))
+    both_locked = grid.partner(jnp.stack([locked, other_locked]), SECOND)
+    all_locked = [locked, both_locked[0], both_locked[1], other_locked]
     to_high = grid.exchanged(low, low, 1)[1].astype(jnp.float32)
     partial = with_ends(partial, 1, None, plane(partial, 1, SIDE - 1) + to_high)
     partial = coeffs[0] * partial[:, 1:, 1:].reshape(SIDE, edge * edge, columns)
@@ -329,14 +319,15 @@
     others = arrived[: 2 * deep].reshape(held.shape)
     came = unpacked(arrived[2 * deep :], width)
     filtered = jnp.concatenate(placed([own[0], came[0], own[1], came[1]], high, low), axis=1)
-    held = placed([held[0], others[0], held[1], others[1]], high, low)
-    intersection = jnp.concatenate(
-        [
-            jnp.concatenate([h[:, q * width : (q + 1) * width] for h in held], axis=1)
-            for q in range(GRID_Z)
-        ],
-        axis=0,
-    ).astype(jnp.float32)
+    held = jnp.concatenate([held[0], others[0], held[1], others[1]], axis=1)
+    size = (GRID_Z * columns, GRID_Z * columns)
+    to, at = lax.broadcasted_iota(jnp.int32, size, 1), lax.broadcasted_iota(jnp.int32, size, 0)
+    base = jnp.where(high, 2, 0) + jnp.where(low, 1, 0)
+    goal = (
+        (at // width % GRID_Z) * columns + ((at // columns) ^ base) * width + at % width
+    )
+    spread = jnp.dot(held, (goal == to).astype(jnp.bfloat16), preferred_element_type=jnp.float32)
+    intersection = jnp.concatenate(split(spread, GRID_Z), axis=0)
     return filtered, intersection
 
 

time: 80.9 us -> 91.9 us (1.14)
  waiting for transfers between devices: 33.4 us -> 49.1 us
  starting transfers between devices: 29.8 us -> 22.1 us
  matrix products: 4.77 us -> 7.26 us
  other arithmetic: 6.12 us -> 8.27 us
  local copies, waits for them, and re-layouts: 4.91 us -> 3.29 us
    ppermute x9, waiting for transfers between devices: 9.79 us -> 24.1 us  [partner(): lax.ppermute(value, AXIS, [(i, i ^ bits) for i in range(self.devices)])]
    ppermute x14, starting transfers between devices: 21.6 us -> 14.4 us  [swapped(): arrived = lax.ppermute(jnp.where(lower, high, low), AXIS, pairs)]
    dot_general x13 -> x14, matrix products: 3.77 us -> 6.28 us  [the longest x12 3.93 us: per_device(): jnp.dot(matrices[r], own, preferred_element_type=jnp.float32)]
    ppermute x14, waiting for transfers between devices: 23.7 us -> 25 us  [swapped(): arrived = lax.ppermute(jnp.where(lower, high, low), AXIS, pairs)]
    div x0 -> x2, other arithmetic: none -> 1.19 us  [the longest x1 0.6 us: per_device(): at // width % GRID_Z]
    slice x6, local copies, waits for them, and re-layouts: 1.16 us -> 0.08 us  [the longest x1 0.03 us: split(): return [value[:, i * width:(i + 1) * width] for i in range(parts)]]
  transfers between devices with their start and end apart: 23 -> 23, of which waited for: 17 -> 18; matrix products, arithmetic and copies ran while one was open for 7% -> 10% of each run, Pallas kernels for 0% -> 0%
where the time goes in v7:
time: 91.9 us; the launch traced here: 91.7 us
  waiting for transfers between devices  49.1 us (53%)
  starting transfers between devices  22.1 us (24%)
  other arithmetic  8.27 us (9%)
  matrix products  7.26 us (8%)
  local copies, waits for them, and re-layouts  3.29 us (4%)
  between operations  1.68 us (2%)
    ppermute x14, waiting for transfers between devices, swapped(): arrived = lax.ppermute(jnp.where(lower, high, low), AXIS, pairs)  25 us
    ppermute x9, waiting for transfers between devices, partner(): lax.ppermute(value, AXIS, [(i, i ^ bits) for i in range(self.devices)])  24.1 us
    ppermute x14, starting transfers between devices, swapped(): arrived = lax.ppermute(jnp.where(lower, high, low), AXIS, pairs)  14.4 us
    ppermute x9, starting transfers between devices, partner(): lax.ppermute(value, AXIS, [(i, i ^ bits) for i in range(self.devices)])  7.73 us
    dot_general x12, matrix products, per_device(): jnp.dot(matrices[r], own, preferred_element_type=jnp.float32)  3.93 us
  transfers between devices with their start and end apart: 23, of which 18 were waited for; matrix products, arithmetic and copies ran while one was open for 10% of the time, Pallas kernels for 0%

profile of v7, /device:TPU:0, one launch (start us, length us, event | category | flops | bytes accessed | tf_op | source)
XLA Modules:
  0.0 91.7 jit_solution(2869644201460995700)
XLA Ops:
  0.6 0.7 reduce.2
  1.6 1.5 %fusion = bf16[343,343]{0,1:T(8,128)(2,1)S(1)} fusion(bf16[1,343,343]{2,1,0:T(8,128)(2,1)S(1)} %copy-done, s32[343]{0:T(512)S(1)} %reduce.2, f32[343]{0:T(512)} %param.10), kind=kOutput, calls=%fused_computation.7 | convolution fusion | flops 162237968 | bytes 473340 | tf_op jit(solution)/shard_map/dot_general | solution.py:143
  3.1 2.4 %collective-permute-start.5 = (bf16[352,343]{0,1:T(8,128)(2,1)S(1)}, bf16[352,343]{0,1:T(8,128)(2,1)S(1)}, u32[]{:S(2)}, u32[]{:S(2)}) collective-permute-start(bf16[352,343]{0,1:T(8,128)(2,1)S(1)} %pad.16), channel_id=1, source_target_pairs={{0,3},{1,2},{2,1},{3,0},{4,7},{5,6},{6,5},{7,4},{8,11},{9,10},{10,... | collective-permute-start | bytes 724424 | tf_op jit(solution)/shard_map/ppermute | solution.py:59
  6.1 6.8 %collective-permute-done = bf16[108,128]{1,0:T(8,128)(2,1)S(1)} collective-permute-done((bf16[108,128]{1,0:T(8,128)(2,1)S(1)}, bf16[108,128]{1,0:T(8,128)(2,1)S(1)}, u32[]{:S(2)}, u32[]{:S(2)}) %collective-permute-start) | collective-permute-done | bytes 27680 | tf_op jit(solution)/shard_map/ppermute | solution.py:59
  13.3 1.1 %collective-permute-done.1 = bf16[108,128]{1,0:T(8,128)(2,1)S(1)} collective-permute-done((bf16[108,128]{1,0:T(8,128)(2,1)S(1)}, bf16[108,128]{1,0:T(8,128)(2,1)S(1)}, u32[]{:S(2)}, u32[]{:S(2)}) %collective-permute-start.1) | collective-permute-done | bytes 27680 | tf_op jit(solution)/shard_map/ppermute | solution.py:59
  15.1 3.3 %collective-permute-start.3 = (bf16[7,1,7,128]{3,0,2,1:T(8,128)(2,1)S(1)}, bf16[7,1,7,128]{3,0,2,1:T(8,128)(2,1)S(1)}, u32[]{:S(2)}, u32[]{:S(2)}) collective-permute-start(bf16[7,1,7,128]{3,0,2,1:T(8,128)(2,1)S(1)} %slice.516), channel_id=1, source_target_pairs={{0,13},{1,12},{2,15},{3,14},{4,9},{5,8},{6,11},{7,10},{8,5},{9,4},... | collective-permute-start | bytes 37640 | tf_op jit(solution)/shard_map/ppermute | solution.py:41
  18.8 0.9 %collective-permute-done.3 = bf16[7,1,7,128]{3,0,2,1:T(8,128)(2,1)S(1)} collective-permute-done((bf16[7,1,7,128]{3,0,2,1:T(8,128)(2,1)S(1)}, bf16[7,1,7,128]{3,0,2,1:T(8,128)(2,1)S(1)}, u32[]{:S(2)}, u32[]{:S(2)}) %collective-permute-start.3) | collective-permute-done | bytes 12576 | tf_op jit(solution)/shard_map/ppermute | solution.py:41
  19.8 1.7 %collective-permute-done.2 = bf16[7,1,7,128]{3,0,2,1:T(8,128)(2,1)S(1)} collective-permute-done((bf16[7,1,7,128]{3,0,2,1:T(8,128)(2,1)S(1)}, bf16[7,1,7,128]{3,0,2,1:T(8,128)(2,1)S(1)}, u32[]{:S(2)}, u32[]{:S(2)}) %collective-permute-start.2) | collective-permute-done | bytes 12576 | tf_op jit(solution)/shard_map/ppermute | solution.py:41
  21.6 2.6 %collective-permute-start.4 = (bf16[1,7,7,128]{3,0,2,1:T(2,128)(2,1)S(1)}, bf16[1,7,7,128]{3,0,2,1:T(2,128)(2,1)S(1)}, u32[]{:S(2)}, u32[]{:S(2)}) collective-permute-start(bf16[1,7,7,128]{3,0,2,1:T(2,128)(2,1)S(1)} %pad_maximum_fusion.25), channel_id=1, source_target_pairs={{0,17},{1,16},{2,19},{3,18},{4,21},{5,20},{6,23},{7,22},{8,25},{9,... | collective-permute-start | bytes 37640 | tf_op jit(solution)/shard_map/ppermute | solution.py:41
  24.2 2.1 %collective-permute-done.4 = bf16[1,7,7,128]{3,0,2,1:T(2,128)(2,1)S(1)} collective-permute-done((bf16[1,7,7,128]{3,0,2,1:T(2,128)(2,1)S(1)}, bf16[1,7,7,128]{3,0,2,1:T(2,128)(2,1)S(1)}, u32[]{:S(2)}, u32[]{:S(2)}) %collective-permute-start.4) | collective-permute-done | bytes 12576 | tf_op jit(solution)/shard_map/ppermute | solution.py:41
  27.4 1.1 %collective-permute-done.6 = bf16[704,343]{0,1:T(8,128)(2,1)S(1)} collective-permute-done((bf16[704,343]{0,1:T(8,128)(2,1)S(1)}, bf16[704,343]{0,1:T(8,128)(2,1)S(1)}, u32[]{:S(2)}, u32[]{:S(2)}) %collective-permute-start.6) | collective-permute-done | bytes 482976 | tf_op jit(solution)/shard_map/ppermute | solution.py:59
  30.2 0.7 collective-permute-start.7
  31.0 2.7 %collective-permute-done.8 = bf16[7,1,7,128]{3,0,2,1:T(8,128)(2,1)S(1)} collective-permute-done((bf16[7,1,7,128]{3,0,2,1:T(8,128)(2,1)S(1)}, bf16[7,1,7,128]{3,0,2,1:T(8,128)(2,1)S(1)}, u32[]{:S(2)}, u32[]{:S(2)}) %collective-permute-start.8) | collective-permute-done | bytes 12576 | tf_op jit(solution)/shard_map/ppermute | solution.py:41
  33.9 2.6 %collective-permute-start.10 = (bf16[1,7,7,128]{3,0,2,1:T(2,128)(2,1)S(1)}, bf16[1,7,7,128]{3,0,2,1:T(2,128)(2,1)S(1)}, u32[]{:S(2)}, u32[]{:S(2)}) collective-permute-start(bf16[1,7,7,128]{3,0,2,1:T(2,128)(2,1)S(1)} %broadcast_select_fusion.40), channel_id=1, source_target_pairs={{0,17},{1,16},{2,19},{3,18},{4,21},{5,20},{6,23},{7,22},{8,25},{9,... | collective-permute-start | bytes 37640 | tf_op jit(solution)/shard_map/ppermute | solution.py:41
  38.1 0.9 convert_multiply_fusion.3
  41.0 2.5 %collective-permute-done.9 = bf16[36,704]{1,0:T(8,128)(2,1)S(1)} collective-permute-done((bf16[36,704]{1,0:T(8,128)(2,1)S(1)}, bf16[36,704]{1,0:T(8,128)(2,1)S(1)}, u32[]{:S(2)}, u32[]{:S(2)}) %collective-permute-start.9) | collective-permute-done | bytes 50720 | tf_op jit(solution)/shard_map/ppermute | solution.py:41
  45.1 2.9 %collective-permute-done.13 = bf16[7,1,7,128]{3,0,2,1:T(8,128)(2,1)S(1)} collective-permute-done((bf16[7,1,7,128]{3,0,2,1:T(8,128)(2,1)S(1)}, bf16[7,1,7,128]{3,0,2,1:T(8,128)(2,1)S(1)}, u32[]{:S(2)}, u32[]{:S(2)}) %collective-permute-start.13) | collective-permute-done | bytes 12576 | tf_op jit(solution)/shard_map/ppermute | solution.py:41
  48.1 2.4 %collective-permute-start.14 = (bf16[1,7,7,128]{3,0,2,1:T(2,128)(2,1)S(1)}, bf16[1,7,7,128]{3,0,2,1:T(2,128)(2,1)S(1)}, u32[]{:S(2)}, u32[]{:S(2)}) collective-permute-start(bf16[1,7,7,128]{3,0,2,1:T(2,128)(2,1)S(1)} %broadcast_select_fusion.37), channel_id=1, source_target_pairs={{0,17},{1,16},{2,19},{3,18},{4,21},{5,20},{6,23},{7,22},{8,25},{9,... | collective-permute-start | bytes 37640 | tf_op jit(solution)/shard_map/ppermute | solution.py:41
  51.1 1.2 %collective-permute-start.11 = (bf16[252,704]{0,1:T(8,128)(2,1)S(1)}, bf16[252,704]{0,1:T(8,128)(2,1)S(1)}, u32[]{:S(2)}, u32[]{:S(2)}) collective-permute-start(bf16[252,704]{0,1:T(8,128)(2,1)S(1)} %pad_maximum_fusion.2), channel_id=1, source_target_pairs={{0,3},{1,2},{2,1},{3,0},{4,7},{5,6},{6,5},{7,4},{8,11},{9,10},{10,... | collective-permute-start | bytes 1064456 | tf_op jit(solution)/shard_map/ppermute | solution.py:59
  55.0 6.5 %collective-permute-done.11 = bf16[252,704]{0,1:T(8,128)(2,1)S(1)} collective-permute-done((bf16[252,704]{0,1:T(8,128)(2,1)S(1)}, bf16[252,704]{0,1:T(8,128)(2,1)S(1)}, u32[]{:S(2)}, u32[]{:S(2)}) %collective-permute-start.11) | collective-permute-done | bytes 354848 | tf_op jit(solution)/shard_map/ppermute | solution.py:59
  61.5 0.7 collective-permute-start.16
  62.6 2.9 %collective-permute-done.16 = bf16[7,1,7,128]{3,0,2,1:T(8,128)(2,1)S(1)} collective-permute-done((bf16[7,1,7,128]{3,0,2,1:T(8,128)(2,1)S(1)}, bf16[7,1,7,128]{3,0,2,1:T(8,128)(2,1)S(1)}, u32[]{:S(2)}, u32[]{:S(2)}) %collective-permute-start.16) | collective-permute-done | bytes 12576 | tf_op jit(solution)/shard_map/ppermute | solution.py:41
  68.0 1.4 %collective-permute-start.18 = (bf16[212,128]{1,0:T(8,128)(2,1)S(1)}, bf16[212,128]{1,0:T(8,128)(2,1)S(1)}, u32[]{:S(2)}, u32[]{:S(2)}) collective-permute-start(bf16[212,128]{1,0:T(8,128)(2,1)S(1)} %pad_maximum_fusion.14), channel_id=1, source_target_pairs={{0,17},{1,16},{2,19},{3,18},{4,21},{5,20},{6,23},{7,22},{8,25},{9,... | collective-permute-start | bytes 162824 | tf_op jit(solution)/shard_map/ppermute | solution.py:59
  69.5 4.8 %collective-permute-done.18 = bf16[212,128]{1,0:T(8,128)(2,1)S(1)} collective-permute-done((bf16[212,128]{1,0:T(8,128)(2,1)S(1)}, bf16[212,128]{1,0:T(8,128)(2,1)S(1)}, u32[]{:S(2)}, u32[]{:S(2)}) %collective-permute-start.18) | collective-permute-done | bytes 54304 | tf_op jit(solution)/shard_map/ppermute | solution.py:59
  74.6 3.6 %collective-permute-done.19 = bf16[176,128]{1,0:T(8,128)(2,1)S(1)} collective-permute-done((bf16[176,128]{1,0:T(8,128)(2,1)S(1)}, bf16[176,128]{1,0:T(8,128)(2,1)S(1)}, u32[]{:S(2)}, u32[]{:S(2)}) %collective-permute-start.19) | collective-permute-done | bytes 45088 | tf_op jit(solution)/shard_map/ppermute | solution.py:41
  78.4 4.5 %collective-permute-done.20 = bf16[176,128]{1,0:T(8,128)(2,1)S(1)} collective-permute-done((bf16[176,128]{1,0:T(8,128)(2,1)S(1)}, bf16[176,128]{1,0:T(8,128)(2,1)S(1)}, u32[]{:S(2)}, u32[]{:S(2)}) %collective-permute-start.20) | collective-permute-done | bytes 45088 | tf_op jit(solution)/shard_map/ppermute | solution.py:41
  83.1 1.7 %collective-permute-start.21 = (bf16[284,128]{1,0:T(8,128)(2,1)S(1)}, bf16[284,128]{1,0:T(8,128)(2,1)S(1)}, u32[]{:S(2)}, u32[]{:S(2)}) collective-permute-start(bf16[284,128]{1,0:T(8,128)(2,1)S(1)} %maximum_maximum_fusion.1), channel_id=1, source_target_pairs={{0,3},{1,2},{2,1},{3,0},{4,7},{5,6},{6,5},{7,4},{8,11},{9,10},{10,... | collective-permute-start | bytes 218120 | tf_op jit(solution)/shard_map/ppermute | solution.py:59
  84.7 2.6 %collective-permute-done.21 = bf16[284,128]{1,0:T(8,128)(2,1)S(1)} collective-permute-done((bf16[284,128]{1,0:T(8,128)(2,1)S(1)}, bf16[284,128]{1,0:T(8,128)(2,1)S(1)}, u32[]{:S(2)}, u32[]{:S(2)}) %collective-permute-start.21) | collective-permute-done | bytes 72736 | tf_op jit(solution)/shard_map/ppermute | solution.py:59
  87.8 1.2 %collective-permute-done.22 = bf16[460,128]{1,0:T(8,128)(2,1)S(1)} collective-permute-done((bf16[460,128]{1,0:T(8,128)(2,1)S(1)}, bf16[460,128]{1,0:T(8,128)(2,1)S(1)}, u32[]{:S(2)}, u32[]{:S(2)}) %collective-permute-start.22) | collective-permute-done | bytes 117792 | tf_op jit(solution)/shard_map/ppermute | solution.py:59
  89.0 0.9 fusion.11
  90.2 0.7 pad_maximum_fusion.18
  90.9 0.8 pad_maximum_fusion.3
  (204 shorter events, 17.6 us)
Async XLA Ops:
  1.6 4.0 %copy-start.1 = (bf16[216,128]{1,0:T(8,128)(2,1)S(1)}, bf16[216,128]{1,0:T(8,128)(2,1)}, u32[]{:S(2)}) copy-start(bf16[216,128]{1,0:T(8,128)(2,1)} %param.7) | copy-start | bytes 165892
  3.1 23.2 %collective-permute-start.5 = (bf16[352,343]{0,1:T(8,128)(2,1)S(1)}, bf16[352,343]{0,1:T(8,128)(2,1)S(1)}, u32[]{:S(2)}, u32[]{:S(2)}) collective-permute-start(bf16[352,343]{0,1:T(8,128)(2,1)S(1)} %pad.16), channel_id=1, source_target_pairs={{0,3},{1,2},{2,1},{3,0},{4,7},{5,6},{6,5},{7,4},{8,11},{9,10},{10,... | collective-permute-start | bytes 724424 | tf_op jit(solution)/shard_map/ppermute | solution.py:59
  5.8 7.1 %collective-permute-start = (bf16[108,128]{1,0:T(8,128)(2,1)S(1)}, bf16[108,128]{1,0:T(8,128)(2,1)S(1)}, u32[]{:S(2)}, u32[]{:S(2)}) collective-permute-start(bf16[108,128]{1,0:T(8,128)(2,1)S(1)} %pad_maximum_fusion.23), channel_id=1, source_target_pairs={{0,3},{1,2},{2,1},{3,0},{4,7},{5,6},{6,5},{7,4},{8,11},{9,10},{10,... | collective-permute-start | bytes 82952 | tf_op jit(solution)/shard_map/ppermute | solution.py:59
  6.1 47.4 %copy-start.7 = (pred[128]{0:T(512)(128)(4,1)}, pred[128]{0:T(512)(128)(4,1)S(1)}, u32[]{:S(2)}) copy-start(pred[128]{0:T(512)(128)(4,1)S(1)} %get-tuple-element.143) | copy-start | bytes 388
  6.1 47.1 %copy-start.9 = (pred[128]{0:T(512)(128)(4,1)}, pred[128]{0:T(512)(128)(4,1)S(1)}, u32[]{:S(2)}) copy-start(pred[128]{0:T(512)(128)(4,1)S(1)} %get-tuple-element.145) | copy-start | bytes 388
  6.1 47.7 %copy-start.5 = (pred[128]{0:T(512)(128)(4,1)}, pred[128]{0:T(512)(128)(4,1)S(1)}, u32[]{:S(2)}) copy-start(pred[128]{0:T(512)(128)(4,1)S(1)} %get-tuple-element.146) | copy-start | bytes 388
  13.2 1.3 %collective-permute-start.1 = (bf16[108,128]{1,0:T(8,128)(2,1)S(1)}, bf16[108,128]{1,0:T(8,128)(2,1)S(1)}, u32[]{:S(2)}, u32[]{:S(2)}) collective-permute-start(bf16[108,128]{1,0:T(8,128)(2,1)S(1)} %pad_maximum_fusion.24), channel_id=1, source_target_pairs={{0,1},{1,0},{2,3},{3,2},{4,5},{5,4},{6,7},{7,6},{8,9},{9,8},{10,11... | collective-permute-start | bytes 82952 | tf_op jit(solution)/shard_map/ppermute | solution.py:59
  15.1 4.7 %collective-permute-start.3 = (bf16[7,1,7,128]{3,0,2,1:T(8,128)(2,1)S(1)}, bf16[7,1,7,128]{3,0,2,1:T(8,128)(2,1)S(1)}, u32[]{:S(2)}, u32[]{:S(2)}) collective-permute-start(bf16[7,1,7,128]{3,0,2,1:T(8,128)(2,1)S(1)} %slice.516), channel_id=1, source_target_pairs={{0,13},{1,12},{2,15},{3,14},{4,9},{5,8},{6,11},{7,10},{8,5},{9,4},... | collective-permute-start | bytes 37640 | tf_op jit(solution)/shard_map/ppermute | solution.py:41
  18.4 3.1 %collective-permute-start.2 = (bf16[7,1,7,128]{3,0,2,1:T(8,128)(2,1)S(1)}, bf16[7,1,7,128]{3,0,2,1:T(8,128)(2,1)S(1)}, u32[]{:S(2)}, u32[]{:S(2)}) collective-permute-start(bf16[7,1,7,128]{3,0,2,1:T(8,128)(2,1)S(1)} %slice.516), channel_id=1, source_target_pairs={{0,5},{1,4},{2,7},{3,6},{4,1},{5,0},{6,3},{7,2},{8,13},{9,12},{10,... | collective-permute-start | bytes 37640 | tf_op jit(solution)/shard_map/ppermute | solution.py:41
  21.6 4.7 %collective-permute-start.4 = (bf16[1,7,7,128]{3,0,2,1:T(2,128)(2,1)S(1)}, bf16[1,7,7,128]{3,0,2,1:T(2,128)(2,1)S(1)}, u32[]{:S(2)}, u32[]{:S(2)}) collective-permute-start(bf16[1,7,7,128]{3,0,2,1:T(2,128)(2,1)S(1)} %pad_maximum_fusion.25), channel_id=1, source_target_pairs={{0,17},{1,16},{2,19},{3,18},{4,21},{5,20},{6,23},{7,22},{8,25},{9,... | collective-permute-start | bytes 37640 | tf_op jit(solution)/shard_map/ppermute | solution.py:41
  26.5 2.0 %collective-permute-start.6 = (bf16[704,343]{0,1:T(8,128)(2,1)S(1)}, bf16[704,343]{0,1:T(8,128)(2,1)S(1)}, u32[]{:S(2)}, u32[]{:S(2)}) collective-permute-start(bf16[704,343]{0,1:T(8,128)(2,1)S(1)} %pad_maximum_fusion.1), channel_id=1, source_target_pairs={{0,1},{1,0},{2,3},{3,2},{4,5},{5,4},{6,7},{7,6},{8,9},{9,8},{10,11... | collective-permute-start | bytes 1448840 | tf_op jit(solution)/shard_map/ppermute | solution.py:59
  29.6 7.3 %copy-start.3 = (bf16[216,704]{1,0:T(8,128)(2,1)S(1)}, bf16[216,704]{1,0:T(8,128)(2,1)}, u32[]{:S(2)}) copy-start(bf16[216,704]{1,0:T(8,128)(2,1)} %param.11) | copy-start | bytes 912388
  29.6 4.1 %collective-permute-start.8 = (bf16[7,1,7,128]{3,0,2,1:T(8,128)(2,1)S(1)}, bf16[7,1,7,128]{3,0,2,1:T(8,128)(2,1)S(1)}, u32[]{:S(2)}, u32[]{:S(2)}) collective-permute-start(bf16[7,1,7,128]{3,0,2,1:T(8,128)(2,1)S(1)} %broadcast_select_fusion.43), channel_id=1, source_target_pairs={{0,13},{1,12},{2,15},{3,14},{4,9},{5,8},{6,11},{7,10},{8,5},{9,4},... | collective-permute-start | bytes 37640 | tf_op jit(solution)/shard_map/ppermute | solution.py:41
  30.2 3.5 %collective-permute-start.7 = (bf16[7,1,7,128]{3,0,2,1:T(8,128)(2,1)S(1)}, bf16[7,1,7,128]{3,0,2,1:T(8,128)(2,1)S(1)}, u32[]{:S(2)}, u32[]{:S(2)}) collective-permute-start(bf16[7,1,7,128]{3,0,2,1:T(8,128)(2,1)S(1)} %get-tuple-element.50), channel_id=1, source_target_pairs={{0,5},{1,4},{2,7},{3,6},{4,1},{5,0},{6,3},{7,2},{8,13},{9,12},{10,... | collective-permute-start | bytes 37640 | tf_op jit(solution)/shard_map/ppermute | solution.py:41
  33.9 4.2 %collective-permute-start.10 = (bf16[1,7,7,128]{3,0,2,1:T(2,128)(2,1)S(1)}, bf16[1,7,7,128]{3,0,2,1:T(2,128)(2,1)S(1)}, u32[]{:S(2)}, u32[]{:S(2)}) collective-permute-start(bf16[1,7,7,128]{3,0,2,1:T(2,128)(2,1)S(1)} %broadcast_select_fusion.40), channel_id=1, source_target_pairs={{0,17},{1,16},{2,19},{3,18},{4,21},{5,20},{6,23},{7,22},{8,25},{9,... | collective-permute-start | bytes 37640 | tf_op jit(solution)/shard_map/ppermute | solution.py:41
  37.1 6.5 %collective-permute-start.9 = (bf16[36,704]{1,0:T(8,128)(2,1)S(1)}, bf16[36,704]{1,0:T(8,128)(2,1)S(1)}, u32[]{:S(2)}, u32[]{:S(2)}) collective-permute-start(bf16[36,704]{1,0:T(8,128)(2,1)S(1)} %slice.432), channel_id=1, source_target_pairs={{0,16},{1,17},{2,18},{3,19},{4,20},{5,21},{6,22},{7,23},{8,24},{9,... | collective-permute-start | bytes 152072 | tf_op jit(solution)/shard_map/ppermute | solution.py:41
  43.9 4.1 %collective-permute-start.13 = (bf16[7,1,7,128]{3,0,2,1:T(8,128)(2,1)S(1)}, bf16[7,1,7,128]{3,0,2,1:T(8,128)(2,1)S(1)}, u32[]{:S(2)}, u32[]{:S(2)}) collective-permute-start(bf16[7,1,7,128]{3,0,2,1:T(8,128)(2,1)S(1)} %get-tuple-element.130), channel_id=1, source_target_pairs={{0,13},{1,12},{2,15},{3,14},{4,9},{5,8},{6,11},{7,10},{8,5},{9,4},... | collective-permute-start | bytes 37640 | tf_op jit(solution)/shard_map/ppermute | solution.py:41
  44.0 4.0 %collective-permute-start.12 = (bf16[7,1,7,128]{3,0,2,1:T(8,128)(2,1)S(1)}, bf16[7,1,7,128]{3,0,2,1:T(8,128)(2,1)S(1)}, u32[]{:S(2)}, u32[]{:S(2)}) collective-permute-start(bf16[7,1,7,128]{3,0,2,1:T(8,128)(2,1)S(1)} %get-tuple-element.129), channel_id=1, source_target_pairs={{0,5},{1,4},{2,7},{3,6},{4,1},{5,0},{6,3},{7,2},{8,13},{9,12},{10,... | collective-permute-start | bytes 37640 | tf_op jit(solution)/shard_map/ppermute | solution.py:41
  48.1 4.6 %collective-permute-start.14 = (bf16[1,7,7,128]{3,0,2,1:T(2,128)(2,1)S(1)}, bf16[1,7,7,128]{3,0,2,1:T(2,128)(2,1)S(1)}, u32[]{:S(2)}, u32[]{:S(2)}) collective-permute-start(bf16[1,7,7,128]{3,0,2,1:T(2,128)(2,1)S(1)} %broadcast_select_fusion.37), channel_id=1, source_target_pairs={{0,17},{1,16},{2,19},{3,18},{4,21},{5,20},{6,23},{7,22},{8,25},{9,... | collective-permute-start | bytes 37640 | tf_op jit(solution)/shard_map/ppermute | solution.py:41
  51.1 10.4 %collective-permute-start.11 = (bf16[252,704]{0,1:T(8,128)(2,1)S(1)}, bf16[252,704]{0,1:T(8,128)(2,1)S(1)}, u32[]{:S(2)}, u32[]{:S(2)}) collective-permute-start(bf16[252,704]{0,1:T(8,128)(2,1)S(1)} %pad_maximum_fusion.2), channel_id=1, source_target_pairs={{0,3},{1,2},{2,1},{3,0},{4,7},{5,6},{6,5},{7,4},{8,11},{9,10},{10,... | collective-permute-start | bytes 1064456 | tf_op jit(solution)/shard_map/ppermute | solution.py:59
  61.5 4.0 %collective-permute-start.16 = (bf16[7,1,7,128]{3,0,2,1:T(8,128)(2,1)S(1)}, bf16[7,1,7,128]{3,0,2,1:T(8,128)(2,1)S(1)}, u32[]{:S(2)}, u32[]{:S(2)}) collective-permute-start(bf16[7,1,7,128]{3,0,2,1:T(8,128)(2,1)S(1)} %slice.698), channel_id=1, source_target_pairs={{0,13},{1,12},{2,15},{3,14},{4,9},{5,8},{6,11},{7,10},{8,5},{9,4},... | collective-permute-start | bytes 37640 | tf_op jit(solution)/shard_map/ppermute | solution.py:41
  62.2 3.3 %collective-permute-start.15 = (bf16[7,1,7,128]{3,0,2,1:T(8,128)(2,1)S(1)}, bf16[7,1,7,128]{3,0,2,1:T(8,128)(2,1)S(1)}, u32[]{:S(2)}, u32[]{:S(2)}) collective-permute-start(bf16[7,1,7,128]{3,0,2,1:T(8,128)(2,1)S(1)} %slice.698), channel_id=1, source_target_pairs={{0,5},{1,4},{2,7},{3,6},{4,1},{5,0},{6,3},{7,2},{8,13},{9,12},{10,... | collective-permute-start | bytes 37640 | tf_op jit(solution)/shard_map/ppermute | solution.py:41
  62.4 4.3 %collective-permute-start.17 = (bf16[2,252,704]{1,2,0:T(8,128)(2,1)S(1)}, bf16[2,252,704]{1,2,0:T(8,128)(2,1)S(1)}, u32[]{:S(2)}, u32[]{:S(2)}) collective-permute-start(bf16[2,252,704]{1,2,0:T(8,128)(2,1)S(1)} %pad_maximum_fusion), channel_id=1, source_target_pairs={{0,1},{1,0},{2,3},{3,2},{4,5},{5,4},{6,7},{7,6},{8,9},{9,8},{10,11... | collective-permute-start | bytes 2128904 | tf_op jit(solution)/shard_map/ppermute | solution.py:59
  68.0 6.2 %collective-permute-start.18 = (bf16[212,128]{1,0:T(8,128)(2,1)S(1)}, bf16[212,128]{1,0:T(8,128)(2,1)S(1)}, u32[]{:S(2)}, u32[]{:S(2)}) collective-permute-start(bf16[212,128]{1,0:T(8,128)(2,1)S(1)} %pad_maximum_fusion.14), channel_id=1, source_target_pairs={{0,17},{1,16},{2,19},{3,18},{4,21},{5,20},{6,23},{7,22},{8,25},{9,... | collective-permute-start | bytes 162824 | tf_op jit(solution)/shard_map/ppermute | solution.py:59
  74.5 3.7 %collective-permute-start.19 = (bf16[176,128]{1,0:T(8,128)(2,1)S(1)}, bf16[176,128]{1,0:T(8,128)(2,1)S(1)}, u32[]{:S(2)}, u32[]{:S(2)}) collective-permute-start(bf16[176,128]{1,0:T(8,128)(2,1)S(1)} %add_convert_fusion.2), channel_id=1, source_target_pairs={{0,5},{1,4},{2,7},{3,6},{4,1},{5,0},{6,3},{7,2},{8,13},{9,12},{10,... | collective-permute-start | bytes 135176 | tf_op jit(solution)/shard_map/ppermute | solution.py:41
  78.3 4.6 %collective-permute-start.20 = (bf16[176,128]{1,0:T(8,128)(2,1)S(1)}, bf16[176,128]{1,0:T(8,128)(2,1)S(1)}, u32[]{:S(2)}, u32[]{:S(2)}) collective-permute-start(bf16[176,128]{1,0:T(8,128)(2,1)S(1)} %add_convert_fusion.1), channel_id=1, source_target_pairs={{0,13},{1,12},{2,15},{3,14},{4,9},{5,8},{6,11},{7,10},{8,5},{9,4},... | collective-permute-start | bytes 135176 | tf_op jit(solution)/shard_map/ppermute | solution.py:41
  82.9 6.1 %copy-start.11 = (s32[512]{0:T(512)S(1)}, s32[512]{0:T(512)}, u32[]{:S(2)}) copy-start(s32[512]{0:T(512)} %get-tuple-element.149) | copy-start | bytes 6148
  82.9 6.1 %copy-start.12 = (s32[512]{0:T(512)S(1)}, s32[512]{0:T(512)}, u32[]{:S(2)}) copy-start(s32[512]{0:T(512)} %get-tuple-element.150) | copy-start | bytes 6148
  82.9 6.1 %copy-start.13 = (s32[512]{0:T(512)S(1)}, s32[512]{0:T(512)}, u32[]{:S(2)}) copy-start(s32[512]{0:T(512)} %get-tuple-element.151) | copy-start | bytes 6148
  82.9 6.1 %copy-start.14 = (s32[512]{0:T(512)S(1)}, s32[512]{0:T(512)}, u32[]{:S(2)}) copy-start(s32[512]{0:T(512)} %get-tuple-element.152) | copy-start | bytes 6148
  83.1 4.3 %collective-permute-start.21 = (bf16[284,128]{1,0:T(8,128)(2,1)S(1)}, bf16[284,128]{1,0:T(8,128)(2,1)S(1)}, u32[]{:S(2)}, u32[]{:S(2)}) collective-permute-start(bf16[284,128]{1,0:T(8,128)(2,1)S(1)} %maximum_maximum_fusion.1), channel_id=1, source_target_pairs={{0,3},{1,2},{2,1},{3,0},{4,7},{5,6},{6,5},{7,4},{8,11},{9,10},{10,... | collective-permute-start | bytes 218120 | tf_op jit(solution)/shard_map/ppermute | solution.py:59
  87.6 1.4 %collective-permute-start.22 = (bf16[460,128]{1,0:T(8,128)(2,1)S(1)}, bf16[460,128]{1,0:T(8,128)(2,1)S(1)}, u32[]{:S(2)}, u32[]{:S(2)}) collective-permute-start(bf16[460,128]{1,0:T(8,128)(2,1)S(1)} %maximum_maximum_fusion), channel_id=1, source_target_pairs={{0,1},{1,0},{2,3},{3,2},{4,5},{5,4},{6,7},{7,6},{8,9},{9,8},{10,11... | collective-permute-start | bytes 353288 | tf_op jit(solution)/shard_map/ppermute | solution.py:59
  (6 other events, 9.7 us)

commit v8 on v7

--- a/solution.py
+++ b/solution.py
@@ -89,7 +89,7 @@
     return [value[:, i * width : (i + 1) * width] for i in range(parts)]
 
 
-def to_shares(grid, block):
+def to_shares(grid, block, other):
     shares = split(block, GRID_Z)
     width = shares[0].shape[1]
     high = grid.has(2)
@@ -99,9 +99,11 @@
     low = grid.share_low
     own = [jnp.where(low, kept[1], kept[0]), jnp.where(low, came[1], came[0])]
     away = [jnp.where(low, kept[0], kept[1]), jnp.where(low, came[0], came[1])]
-    came = unpacked(grid.partner(packed(away), SECOND), width)
+    away, other = lax.optimization_barrier((packed(away), other))
+    came = unpacked(grid.partner(away, SECOND), width)
+    other = by_rows(grid.partner(other, SECOND))
     near = [own[0], came[0], came[1], own[1]]
-    return jnp.concatenate(placed(near, high, grid.has(1)), axis=1)
+    return jnp.concatenate(placed(near, high, grid.has(1)), axis=1), other
 
 
 def by_rows(value):
@@ -188,26 +190,32 @@
     grid = Grid()
     shape = (SIDE, SIDE, SIDE, columns)
 
-    matrix = slots_matrix(cell_matrix, connectivity, potential)
-    padded = jnp.pad(matrix, ((0, -slot_count % 16), (0, 0)))
-    other = grid.partner(padded, FIRST)
-    both = grid.partner(jnp.concatenate([padded, other], axis=0), SECOND)
-    above = padded.shape[0]
-    matrices = [padded, both[:above], both[above:], other]
-    matrices = [m[:slot_count] for m in matrices]
+    field = block.reshape(edge, edge, edge, columns)
+    high = plane(field, 1, edge - 1)
+    cell_matrix, high = lax.optimization_barrier((cell_matrix, high))
+    matrix = by_rows(slots_matrix(cell_matrix, connectivity, potential))
+    other = by_rows(grid.partner(matrix, FIRST))
+    field = jnp.concatenate([grid.exchanged(high, high, 1, cross=0)[0], field], axis=1)
+    high = plane(field, 0, edge - 1)
+
+    locked, high = lax.optimization_barrier((locked, high))
+    top = by_rows(locked[-edge * edge :])
+    bottom = by_rows(grid.exchanged(top, top, 0, cross=0)[0])
+    locked = jnp.concatenate([bottom, locked], axis=0)
+    other_locked = grid.partner(locked, FIRST)
+
+    field = jnp.concatenate([grid.exchanged(high, high, 0, cross=0)[0], field], axis=0)
+    rows = field.reshape(SIDE * SIDE * edge, columns)
+    second = by_rows(grid.partner(matrix, SECOND))
+    mine, both = to_shares(grid, jnp.pad(rows, ((0, -rows.shape[0] % 16), (0, 0))), other)
+    mine, both = lax.optimization_barrier((mine, both))
+    matrices = [matrix, second, both, other]
+    field = mine[: rows.shape[0]].reshape(SIDE, SIDE, edge, columns)
+    low = to_next_partition(plane(field, 2, edge - 1), width)
+    field = jnp.concatenate([low, field], axis=2)
+
     lane_owner = lax.broadcasted_iota(jnp.int32, (1, columns), 1) // width
     owner_near = lane_owner ^ grid.coords[2]
-
-    mine = to_shares(grid, block)
-    field = (
-        jnp.zeros(shape, jnp.bfloat16)
-        .at[1:, 1:, 1:]
-        .set(mine.reshape(edge, edge, edge, columns))
-    )
-    field = with_ends(field, 2, to_next_partition(plane(field, 2, SIDE - 1), width), None)
-    for dim in (1, 0):
-        high = plane(field, dim, SIDE - 1)
-        field = with_ends(field, dim, grid.exchanged(high, high, dim)[0], None)
 
     inside = jnp.ones(shape, jnp.bool_)
     first = (grid.coords[0] == 0, grid.coords[1] == 0, lane_owner.reshape(1, 1, 1, columns) == 0)
@@ -239,14 +247,8 @@
         for dim in (1, 0):
             low, high = plane(partial, dim, 0), plane(partial, dim, SIDE - 1)
             low16, high16 = low.astype(jnp.bfloat16), high.astype(jnp.bfloat16)
-            if (step, dim) == (0, 0):
-                locked, low16, high16 = lax.optimization_barrier((locked, low16, high16))
-                top = by_rows(locked[-edge * edge :])
-                bottom = by_rows(grid.exchanged(top, top, 0, cross=0)[0])
-                locked = jnp.concatenate([bottom, locked], axis=0)
             if (step, dim) == (1, 1):
-                locked, low16, high16 = lax.optimization_barrier((locked, low16, high16))
-                other_locked = grid.partner(locked, FIRST)
+                low16, other_locked = lax.optimization_barrier((low16, other_locked))
             to_low, to_high = grid.exchanged(low16, high16, dim)
             partial = with_ends(
                 partial,
@@ -260,11 +262,12 @@
         following = rounded(jnp.where(inside, following, 0.0))
         older = current
         current = following
+        if step == 1:
+            both_locked = grid.partner(jnp.stack([locked, other_locked]), SECOND)
+            current, both_locked = lax.optimization_barrier((current, both_locked))
+            all_locked = [locked, both_locked[0], both_locked[1], other_locked]
 
     low = plane(partial, 1, 0).astype(jnp.bfloat16)
-    locked, other_locked, low = lax.optimization_barrier((locked, other_locked, low))
-    both_locked = grid.partner(jnp.stack([locked, other_locked]), SECOND)
-    all_locked = [locked, both_locked[0], both_locked[1], other_locked]
     to_high = grid.exchanged(low, low, 1)[1].astype(jnp.float32)
     partial = with_ends(partial, 1, None, plane(partial, 1, SIDE - 1) + to_high)
     partial = coeffs[0] * partial[:, 1:, 1:].reshape(SIDE, edge * edge, columns)

time: 91.9 us -> 85.7 us (0.933)
  waiting for transfers between devices: 49.1 us -> 45.2 us
  other arithmetic: 8.27 us -> 5.52 us
  local copies, waits for them, and re-layouts: 3.29 us -> 5.1 us
  matrix products: 7.26 us -> 5.52 us
    ppermute x9 -> x10, waiting for transfers between devices: 24.1 us -> 19.5 us  [partner(): lax.ppermute(value, AXIS, [(i, i ^ bits) for i in range(self.devices)])]
    ppermute x14, starting transfers between devices: 14.4 us -> 18.1 us  [swapped(): arrived = lax.ppermute(jnp.where(lower, high, low), AXIS, pairs)]
    ppermute x9 -> x10, starting transfers between devices: 7.73 us -> 4.5 us  [partner(): lax.ppermute(value, AXIS, [(i, i ^ bits) for i in range(self.devices)])]
    unnamed x39 -> x12, local copies, waits for them, and re-layouts: 0.96 us -> 2.23 us
    dot_general x12, matrix products: 3.93 us -> 2.94 us  [per_device(): jnp.dot(matrices[r], own, preferred_element_type=jnp.float32)]
    reshape x0 -> x3, local copies, waits for them, and re-layouts: none -> 0.94 us  [the longest x1 0.88 us: per_device(): field = block.reshape(edge, edge, edge, columns)]
  transfers between devices with their start and end apart: 23 -> 24, of which waited for: 18 -> 17; matrix products, arithmetic and copies ran while one was open for 10% -> 7% of each run, Pallas kernels for 0% -> 0%
where the time goes in v8:
time: 85.7 us; the launch traced here: 85.5 us
  waiting for transfers between devices  45.2 us (53%)
  starting transfers between devices  22.6 us (26%)
  other arithmetic  5.52 us (6%)
  matrix products  5.52 us (6%)
  local copies, waits for them, and re-layouts  5.1 us (6%)
  between operations  1.5 us (2%)
    ppermute x14, waiting for transfers between devices, swapped(): arrived = lax.ppermute(jnp.where(lower, high, low), AXIS, pairs)  25.7 us
    ppermute x10, waiting for transfers between devices, partner(): lax.ppermute(value, AXIS, [(i, i ^ bits) for i in range(self.devices)])  19.5 us
    ppermute x14, starting transfers between devices, swapped(): arrived = lax.ppermute(jnp.where(lower, high, low), AXIS, pairs)  18.1 us
    ppermute x10, starting transfers between devices, partner(): lax.ppermute(value, AXIS, [(i, i ^ bits) for i in range(self.devices)])  4.5 us
    dot_general x12, matrix products, per_device(): jnp.dot(matrices[r], own, preferred_element_type=jnp.float32)  2.94 us
    unnamed x12, local copies, waits for them, and re-layouts  2.23 us
  transfers between devices with their start and end apart: 24, of which 17 were waited for; matrix products, arithmetic and copies ran while one was open for 7% of the time, Pallas kernels for 0%

profile of v8, /device:TPU:0, one launch (start us, length us, event | category | flops | bytes accessed | tf_op | source)
XLA Modules:
  0.0 85.5 jit_solution(6056592652388395231)
XLA Ops:
  0.6 0.9 %reshape.193 = bf16[6,6,6,128]{3,2,1,0:T(8,128)(2,1)S(1)} reshape(bf16[216,128]{1,0:T(8,128)(2,1)} %param.5) | data formatting | bytes 110592 | tf_op jit(solution)/shard_map/reshape | solution.py:193
  1.6 4.0 %collective-permute-start.1 = (bf16[6,1,6,128]{3,2,1,0:T(8,128)(2,1)S(1)}, bf16[6,1,6,128]{3,2,1,0:T(8,128)(2,1)S(1)}, u32[]{:S(2)}, u32[]{:S(2)}) collective-permute-start(bf16[6,1,6,128]{3,2,1,0:T(8,128)(2,1)S(1)} %slice.439), channel_id=1, source_target_pairs={{0,12},{1,13},{2,14},{3,15},{4,8},{5,9},{6,10},{7,11},{8,4},{9,5},... | collective-permute-start | bytes 27656 | tf_op jit(solution)/shard_map/ppermute | solution.py:41
  6.2 0.7 fusion
  7.3 1.2 %collective-permute-start.8 = (bf16[343,343]{1,0:T(8,128)(2,1)S(1)}, bf16[343,343]{1,0:T(8,128)(2,1)S(1)}, u32[]{:S(2)}, u32[]{:S(2)}) collective-permute-start(bf16[343,343]{1,0:T(8,128)(2,1)S(1)} %fusion), channel_id=1, source_target_pairs={{0,1},{1,0},{2,3},{3,2},{4,5},{5,4},{6,7},{7,6},{8,9},{9,8},{10,11... | collective-permute-start | bytes 705902 | tf_op jit(solution)/shard_map/ppermute | solution.py:59
  9.3 2.7 %collective-permute-start.3 = (bf16[1,7,6,128]{3,2,1,0:T(8,128)(2,1)S(1)}, bf16[1,7,6,128]{3,2,1,0:T(8,128)(2,1)S(1)}, u32[]{:S(2)}, u32[]{:S(2)}) collective-permute-start(bf16[1,7,6,128]{3,2,1,0:T(8,128)(2,1)S(1)} %pad_maximum_fusion.23), channel_id=1, source_target_pairs={{0,16},{1,17},{2,18},{3,19},{4,20},{5,21},{6,22},{7,23},{8,24},{9,... | collective-permute-start | bytes 32264 | tf_op jit(solution)/shard_map/ppermute | solution.py:41
  12.0 2.1 %collective-permute-done.3 = bf16[1,7,6,128]{3,2,1,0:T(8,128)(2,1)S(1)} collective-permute-done((bf16[1,7,6,128]{3,2,1,0:T(8,128)(2,1)S(1)}, bf16[1,7,6,128]{3,2,1,0:T(8,128)(2,1)S(1)}, u32[]{:S(2)}, u32[]{:S(2)}) %collective-permute-start.3) | collective-permute-done | bytes 10784 | tf_op jit(solution)/shard_map/ppermute | solution.py:41
  15.5 2.6 %collective-permute-start.2 = (bf16[36,704]{1,0:T(8,128)(2,1)S(1)}, bf16[36,704]{1,0:T(8,128)(2,1)S(1)}, u32[]{:S(2)}, u32[]{:S(2)}) collective-permute-start(bf16[36,704]{1,0:T(8,128)(2,1)S(1)} %slice.337), channel_id=1, source_target_pairs={{0,16},{1,17},{2,18},{3,19},{4,20},{5,21},{6,22},{7,23},{8,24},{9,... | collective-permute-start | bytes 152072 | tf_op jit(solution)/shard_map/ppermute | solution.py:41
  18.6 0.7 collective-permute-start.6
  19.3 3.2 %collective-permute-done.2 = bf16[36,704]{1,0:T(8,128)(2,1)S(1)} collective-permute-done((bf16[36,704]{1,0:T(8,128)(2,1)S(1)}, bf16[36,704]{1,0:T(8,128)(2,1)S(1)}, u32[]{:S(2)}, u32[]{:S(2)}) %collective-permute-start.2) | collective-permute-done | bytes 50720 | tf_op jit(solution)/shard_map/ppermute | solution.py:41
  23.3 1.0 %collective-permute-done.7 = bf16[343,343]{1,0:T(8,128)(2,1)S(1)} collective-permute-done((bf16[343,343]{1,0:T(8,128)(2,1)S(1)}, bf16[343,343]{1,0:T(8,128)(2,1)S(1)}, u32[]{:S(2)}, u32[]{:S(2)}) %collective-permute-start.7) | collective-permute-done | bytes 235330 | tf_op jit(solution)/shard_map/ppermute | solution.py:59
  26.1 0.6 collective-permute-start.9
  26.9 3.1 %collective-permute-done.10 = bf16[7,1,7,128]{3,2,1,0:T(8,128)(2,1)S(1)} collective-permute-done((bf16[7,1,7,128]{3,2,1,0:T(8,128)(2,1)S(1)}, bf16[7,1,7,128]{3,2,1,0:T(8,128)(2,1)S(1)}, u32[]{:S(2)}, u32[]{:S(2)}) %collective-permute-start.10) | collective-permute-done | bytes 12576 | tf_op jit(solution)/shard_map/ppermute | solution.py:41
  30.1 2.6 %collective-permute-start.11 = (bf16[1,7,7,128]{3,2,1,0:T(8,128)(2,1)S(1)}, bf16[1,7,7,128]{3,2,1,0:T(8,128)(2,1)S(1)}, u32[]{:S(2)}, u32[]{:S(2)}) collective-permute-start(bf16[1,7,7,128]{3,2,1,0:T(8,128)(2,1)S(1)} %fusion.117), channel_id=1, source_target_pairs={{0,17},{1,16},{2,19},{3,18},{4,21},{5,20},{6,23},{7,22},{8,25},{9,... | collective-permute-start | bytes 37640 | tf_op jit(solution)/shard_map/ppermute | solution.py:41
  33.5 0.7 collective-permute-done.11
  35.8 7.7 %collective-permute-done.12 = bf16[252,704]{0,1:T(8,128)(2,1)S(1)} collective-permute-done((bf16[252,704]{0,1:T(8,128)(2,1)S(1)}, bf16[252,704]{0,1:T(8,128)(2,1)S(1)}, u32[]{:S(2)}, u32[]{:S(2)}) %collective-permute-start.12) | collective-permute-done | bytes 354848 | tf_op jit(solution)/shard_map/ppermute | solution.py:59
  43.5 0.7 collective-permute-start.14
  45.2 2.4 %collective-permute-done.14 = bf16[7,1,7,128]{3,2,1,0:T(8,128)(2,1)S(1)} collective-permute-done((bf16[7,1,7,128]{3,2,1,0:T(8,128)(2,1)S(1)}, bf16[7,1,7,128]{3,2,1,0:T(8,128)(2,1)S(1)}, u32[]{:S(2)}, u32[]{:S(2)}) %collective-permute-start.14) | collective-permute-done | bytes 12576 | tf_op jit(solution)/shard_map/ppermute | solution.py:41
  47.7 0.9 %collective-permute-start.15 = (bf16[1,7,7,128]{3,2,1,0:T(8,128)(2,1)S(1)}, bf16[1,7,7,128]{3,2,1,0:T(8,128)(2,1)S(1)}, u32[]{:S(2)}, u32[]{:S(2)}) collective-permute-start(bf16[1,7,7,128]{3,2,1,0:T(8,128)(2,1)S(1)} %fusion.118), channel_id=1, source_target_pairs={{0,17},{1,16},{2,19},{3,18},{4,21},{5,20},{6,23},{7,22},{8,25},{9,... | collective-permute-start | bytes 37640 | tf_op jit(solution)/shard_map/ppermute | solution.py:41
  48.6 3.2 %collective-permute-done.15 = bf16[1,7,7,128]{3,2,1,0:T(8,128)(2,1)S(1)} collective-permute-done((bf16[1,7,7,128]{3,2,1,0:T(8,128)(2,1)S(1)}, bf16[1,7,7,128]{3,2,1,0:T(8,128)(2,1)S(1)}, u32[]{:S(2)}, u32[]{:S(2)}) %collective-permute-start.15) | collective-permute-done | bytes 12576 | tf_op jit(solution)/shard_map/ppermute | solution.py:41
  52.1 0.9 %copy-done.1 = bf16[2,252,704]{1,2,0:T(8,128)(2,1)} copy-done((bf16[2,252,704]{1,2,0:T(8,128)(2,1)}, bf16[2,252,704]{1,2,0:T(8,128)(2,1)S(1)}, u32[]{:S(2)}) %copy-start.1) | copy-done | bytes 709656
  54.4 1.8 %collective-permute-start.18 = (bf16[7,1,7,128]{3,2,1,0:T(8,128)(2,1)S(1)}, bf16[7,1,7,128]{3,2,1,0:T(8,128)(2,1)S(1)}, u32[]{:S(2)}, u32[]{:S(2)}) collective-permute-start(bf16[7,1,7,128]{3,2,1,0:T(8,128)(2,1)S(1)} %slice.605), channel_id=1, source_target_pairs={{0,13},{1,12},{2,15},{3,14},{4,9},{5,8},{6,11},{7,10},{8,5},{9,4},... | collective-permute-start | bytes 37640 | tf_op jit(solution)/shard_map/ppermute | solution.py:41
  56.7 1.8 %collective-permute-done.18 = bf16[7,1,7,128]{3,2,1,0:T(8,128)(2,1)S(1)} collective-permute-done((bf16[7,1,7,128]{3,2,1,0:T(8,128)(2,1)S(1)}, bf16[7,1,7,128]{3,2,1,0:T(8,128)(2,1)S(1)}, u32[]{:S(2)}, u32[]{:S(2)}) %collective-permute-start.18) | collective-permute-done | bytes 12576 | tf_op jit(solution)/shard_map/ppermute | solution.py:41
  58.5 0.9 %collective-permute-done.17 = bf16[7,1,7,128]{3,2,1,0:T(8,128)(2,1)S(1)} collective-permute-done((bf16[7,1,7,128]{3,2,1,0:T(8,128)(2,1)S(1)}, bf16[7,1,7,128]{3,2,1,0:T(8,128)(2,1)S(1)}, u32[]{:S(2)}, u32[]{:S(2)}) %collective-permute-start.17) | collective-permute-done | bytes 12576 | tf_op jit(solution)/shard_map/ppermute | solution.py:41
  59.7 0.9 %copy-done.2 = bf16[2,252,704]{1,2,0:T(8,128)(2,1)S(1)} copy-done((bf16[2,252,704]{1,2,0:T(8,128)(2,1)S(1)}, bf16[2,252,704]{1,2,0:T(8,128)(2,1)}, u32[]{:S(2)}) %copy-start.2) | copy-done | bytes 709656
  62.3 5.8 %collective-permute-done.19 = bf16[212,128]{1,0:T(8,128)(2,1)S(1)} collective-permute-done((bf16[212,128]{1,0:T(8,128)(2,1)S(1)}, bf16[212,128]{1,0:T(8,128)(2,1)S(1)}, u32[]{:S(2)}, u32[]{:S(2)}) %collective-permute-start.19) | collective-permute-done | bytes 54304 | tf_op jit(solution)/shard_map/ppermute | solution.py:59
  68.8 3.3 %collective-permute-done.20 = bf16[176,128]{1,0:T(8,128)(2,1)S(1)} collective-permute-done((bf16[176,128]{1,0:T(8,128)(2,1)S(1)}, bf16[176,128]{1,0:T(8,128)(2,1)S(1)}, u32[]{:S(2)}, u32[]{:S(2)}) %collective-permute-start.20) | collective-permute-done | bytes 45088 | tf_op jit(solution)/shard_map/ppermute | solution.py:41
  72.2 4.5 %collective-permute-done.21 = bf16[176,128]{1,0:T(8,128)(2,1)S(1)} collective-permute-done((bf16[176,128]{1,0:T(8,128)(2,1)S(1)}, bf16[176,128]{1,0:T(8,128)(2,1)S(1)}, u32[]{:S(2)}, u32[]{:S(2)}) %collective-permute-start.21) | collective-permute-done | bytes 45088 | tf_op jit(solution)/shard_map/ppermute | solution.py:41
  77.5 3.7 %collective-permute-done.22 = bf16[284,128]{1,0:T(8,128)(2,1)S(1)} collective-permute-done((bf16[284,128]{1,0:T(8,128)(2,1)S(1)}, bf16[284,128]{1,0:T(8,128)(2,1)S(1)}, u32[]{:S(2)}, u32[]{:S(2)}) %collective-permute-start.22) | collective-permute-done | bytes 72736 | tf_op jit(solution)/shard_map/ppermute | solution.py:59
  81.6 1.2 %collective-permute-done.23 = bf16[460,128]{1,0:T(8,128)(2,1)S(1)} collective-permute-done((bf16[460,128]{1,0:T(8,128)(2,1)S(1)}, bf16[460,128]{1,0:T(8,128)(2,1)S(1)}, u32[]{:S(2)}, u32[]{:S(2)}) %collective-permute-start.23) | collective-permute-done | bytes 117792 | tf_op jit(solution)/shard_map/ppermute | solution.py:59
  82.8 0.9 %fusion.9 = f32[176,512]{1,0:T(8,128)S(1)} fusion(s32[512]{0:T(512)S(1)} %get-tuple-element.127, s32[512]{0:T(512)S(1)} %get-tuple-element.129, s32[]{:T(128)S(6)} %add.288, s32[512]{0:T(512)S(1)} %get-tuple-element.128, s32[512]{0:T(512)S(1)} %get-tuple-element.132, s32[512]{0:T(512)S(1)} %get-tuple-element.126, s32[512]{0:T(512)S(1)} %get-tuple-element.133, ...), kind=kOutput, calls=%fused_computation.25 | convolution fusion | flops 98238464 | bytes 554500 | tf_op jit(solution)/shard_map/dot_general | solution.py:332
  84.0 0.7 pad_maximum_fusion.16
  84.7 0.8 pad_maximum_fusion.2
  (169 shorter events, 15.9 us)
Async XLA Ops:
  0.6 5.5 %copy-start = (bf16[1,343,343]{2,1,0:T(8,128)(2,1)S(1)}, bf16[1,343,343]{2,1,0:T(8,128)(2,1)}, u32[]{:S(2)}) copy-start(bf16[1,343,343]{2,1,0:T(8,128)(2,1)} %param.6) | copy-start | bytes 705898
  1.5 4.6 %copy-start.4 = (s32[1,343]{1,0:T(1,128)S(1)}, s32[1,343]{1,0:T(1,128)}, u32[]{:S(2)}) copy-start(s32[1,343]{1,0:T(1,128)} %param.7) | copy-start | bytes 4120
  1.5 4.6 %copy-start.5 = (f32[343]{0:T(512)S(1)}, f32[343]{0:T(512)}, u32[]{:S(2)}) copy-start(f32[343]{0:T(512)} %param.8) | copy-start | bytes 4120
  1.6 7.2 %collective-permute-start.1 = (bf16[6,1,6,128]{3,2,1,0:T(8,128)(2,1)S(1)}, bf16[6,1,6,128]{3,2,1,0:T(8,128)(2,1)S(1)}, u32[]{:S(2)}, u32[]{:S(2)}) collective-permute-start(bf16[6,1,6,128]{3,2,1,0:T(8,128)(2,1)S(1)} %slice.439), channel_id=1, source_target_pairs={{0,12},{1,13},{2,14},{3,15},{4,8},{5,9},{6,10},{7,11},{8,4},{9,5},... | collective-permute-start | bytes 27656 | tf_op jit(solution)/shard_map/ppermute | solution.py:41
  5.6 3.7 %collective-permute-start = (bf16[6,1,6,128]{3,2,1,0:T(8,128)(2,1)S(1)}, bf16[6,1,6,128]{3,2,1,0:T(8,128)(2,1)S(1)}, u32[]{:S(2)}, u32[]{:S(2)}) collective-permute-start(bf16[6,1,6,128]{3,2,1,0:T(8,128)(2,1)S(1)} %slice.439), channel_id=1, source_target_pairs={{0,4},{1,5},{2,6},{3,7},{4,0},{5,1},{6,2},{7,3},{8,12},{9,13},{10,... | collective-permute-start | bytes 27656 | tf_op jit(solution)/shard_map/ppermute | solution.py:41
  6.9 11.7 %collective-permute-start.5 = (bf16[343,343]{1,0:T(8,128)(2,1)S(1)}, bf16[343,343]{1,0:T(8,128)(2,1)S(1)}, u32[]{:S(2)}, u32[]{:S(2)}) collective-permute-start(bf16[343,343]{1,0:T(8,128)(2,1)S(1)} %fusion), channel_id=1, source_target_pairs={{0,3},{1,2},{2,1},{3,0},{4,7},{5,6},{6,5},{7,4},{8,11},{9,10},{10,... | collective-permute-start | bytes 705902 | tf_op jit(solution)/shard_map/ppermute | solution.py:59
  7.3 17.7 %collective-permute-start.8 = (bf16[343,343]{1,0:T(8,128)(2,1)S(1)}, bf16[343,343]{1,0:T(8,128)(2,1)S(1)}, u32[]{:S(2)}, u32[]{:S(2)}) collective-permute-start(bf16[343,343]{1,0:T(8,128)(2,1)S(1)} %fusion), channel_id=1, source_target_pairs={{0,1},{1,0},{2,3},{3,2},{4,5},{5,4},{6,7},{7,6},{8,9},{9,8},{10,11... | collective-permute-start | bytes 705902 | tf_op jit(solution)/shard_map/ppermute | solution.py:59
  9.3 4.7 %collective-permute-start.3 = (bf16[1,7,6,128]{3,2,1,0:T(8,128)(2,1)S(1)}, bf16[1,7,6,128]{3,2,1,0:T(8,128)(2,1)S(1)}, u32[]{:S(2)}, u32[]{:S(2)}) collective-permute-start(bf16[1,7,6,128]{3,2,1,0:T(8,128)(2,1)S(1)} %pad_maximum_fusion.23), channel_id=1, source_target_pairs={{0,16},{1,17},{2,18},{3,19},{4,20},{5,21},{6,22},{7,23},{8,24},{9,... | collective-permute-start | bytes 32264 | tf_op jit(solution)/shard_map/ppermute | solution.py:41
  14.3 1.0 %copy-start.3 = (bf16[216,704]{1,0:T(8,128)(2,1)S(1)}, bf16[216,704]{1,0:T(8,128)(2,1)}, u32[]{:S(2)}) copy-start(bf16[216,704]{1,0:T(8,128)(2,1)} %param.9) | copy-start | bytes 912388
  14.5 3.8 %collective-permute-start.4 = (bf16[152,128]{1,0:T(8,128)(2,1)S(1)}, bf16[152,128]{1,0:T(8,128)(2,1)S(1)}, u32[]{:S(2)}, u32[]{:S(2)}) collective-permute-start(bf16[152,128]{1,0:T(8,128)(2,1)S(1)} %pad_maximum_fusion.17), channel_id=1, source_target_pairs={{0,3},{1,2},{2,1},{3,0},{4,7},{5,6},{6,5},{7,4},{8,11},{9,10},{10,... | collective-permute-start | bytes 116744 | tf_op jit(solution)/shard_map/ppermute | solution.py:59
  15.5 7.0 %collective-permute-start.2 = (bf16[36,704]{1,0:T(8,128)(2,1)S(1)}, bf16[36,704]{1,0:T(8,128)(2,1)S(1)}, u32[]{:S(2)}, u32[]{:S(2)}) collective-permute-start(bf16[36,704]{1,0:T(8,128)(2,1)S(1)} %slice.337), channel_id=1, source_target_pairs={{0,16},{1,17},{2,18},{3,19},{4,20},{5,21},{6,22},{7,23},{8,24},{9,... | collective-permute-start | bytes 152072 | tf_op jit(solution)/shard_map/ppermute | solution.py:41
  18.6 4.2 %collective-permute-start.6 = (bf16[152,128]{1,0:T(8,128)(2,1)S(1)}, bf16[152,128]{1,0:T(8,128)(2,1)S(1)}, u32[]{:S(2)}, u32[]{:S(2)}) collective-permute-start(bf16[152,128]{1,0:T(8,128)(2,1)S(1)} %pad_maximum_fusion.18), channel_id=1, source_target_pairs={{0,1},{1,0},{2,3},{3,2},{4,5},{5,4},{6,7},{7,6},{8,9},{9,8},{10,11... | collective-permute-start | bytes 116744 | tf_op jit(solution)/shard_map/ppermute | solution.py:59
  22.7 1.6 %collective-permute-start.7 = (bf16[343,343]{1,0:T(8,128)(2,1)S(1)}, bf16[343,343]{1,0:T(8,128)(2,1)S(1)}, u32[]{:S(2)}, u32[]{:S(2)}) collective-permute-start(bf16[343,343]{1,0:T(8,128)(2,1)S(1)} %collective-permute-done.5), channel_id=1, source_target_pairs={{0,1},{1,0},{2,3},{3,2},{4,5},{5,4},{6,7},{7,6},{8,9},{9,8},{10,11... | collective-permute-start | bytes 705902 | tf_op jit(solution)/shard_map/ppermute | solution.py:59
  25.9 4.1 %collective-permute-start.10 = (bf16[7,1,7,128]{3,2,1,0:T(8,128)(2,1)S(1)}, bf16[7,1,7,128]{3,2,1,0:T(8,128)(2,1)S(1)}, u32[]{:S(2)}, u32[]{:S(2)}) collective-permute-start(bf16[7,1,7,128]{3,2,1,0:T(8,128)(2,1)S(1)} %broadcast_select_fusion.36), channel_id=1, source_target_pairs={{0,13},{1,12},{2,15},{3,14},{4,9},{5,8},{6,11},{7,10},{8,5},{9,4},... | collective-permute-start | bytes 37640 | tf_op jit(solution)/shard_map/ppermute | solution.py:41
  26.1 3.9 %collective-permute-start.9 = (bf16[7,1,7,128]{3,2,1,0:T(8,128)(2,1)S(1)}, bf16[7,1,7,128]{3,2,1,0:T(8,128)(2,1)S(1)}, u32[]{:S(2)}, u32[]{:S(2)}) collective-permute-start(bf16[7,1,7,128]{3,2,1,0:T(8,128)(2,1)S(1)} %get-tuple-element.41), channel_id=1, source_target_pairs={{0,5},{1,4},{2,7},{3,6},{4,1},{5,0},{6,3},{7,2},{8,13},{9,12},{10,... | collective-permute-start | bytes 37640 | tf_op jit(solution)/shard_map/ppermute | solution.py:41
  30.1 4.1 %collective-permute-start.11 = (bf16[1,7,7,128]{3,2,1,0:T(8,128)(2,1)S(1)}, bf16[1,7,7,128]{3,2,1,0:T(8,128)(2,1)S(1)}, u32[]{:S(2)}, u32[]{:S(2)}) collective-permute-start(bf16[1,7,7,128]{3,2,1,0:T(8,128)(2,1)S(1)} %fusion.117), channel_id=1, source_target_pairs={{0,17},{1,16},{2,19},{3,18},{4,21},{5,20},{6,23},{7,22},{8,25},{9,... | collective-permute-start | bytes 37640 | tf_op jit(solution)/shard_map/ppermute | solution.py:41
  32.9 10.5 %collective-permute-start.12 = (bf16[252,704]{0,1:T(8,128)(2,1)S(1)}, bf16[252,704]{0,1:T(8,128)(2,1)S(1)}, u32[]{:S(2)}, u32[]{:S(2)}) collective-permute-start(bf16[252,704]{0,1:T(8,128)(2,1)S(1)} %pad_maximum_fusion.1), channel_id=1, source_target_pairs={{0,3},{1,2},{2,1},{3,0},{4,7},{5,6},{6,5},{7,4},{8,11},{9,10},{10,... | collective-permute-start | bytes 1064456 | tf_op jit(solution)/shard_map/ppermute | solution.py:59
  43.5 4.1 %collective-permute-start.14 = (bf16[7,1,7,128]{3,2,1,0:T(8,128)(2,1)S(1)}, bf16[7,1,7,128]{3,2,1,0:T(8,128)(2,1)S(1)}, u32[]{:S(2)}, u32[]{:S(2)}) collective-permute-start(bf16[7,1,7,128]{3,2,1,0:T(8,128)(2,1)S(1)} %broadcast_select_fusion.35), channel_id=1, source_target_pairs={{0,13},{1,12},{2,15},{3,14},{4,9},{5,8},{6,11},{7,10},{8,5},{9,4},... | collective-permute-start | bytes 37640 | tf_op jit(solution)/shard_map/ppermute | solution.py:41
  44.2 3.4 %collective-permute-start.13 = (bf16[7,1,7,128]{3,2,1,0:T(8,128)(2,1)S(1)}, bf16[7,1,7,128]{3,2,1,0:T(8,128)(2,1)S(1)}, u32[]{:S(2)}, u32[]{:S(2)}) collective-permute-start(bf16[7,1,7,128]{3,2,1,0:T(8,128)(2,1)S(1)} %get-tuple-element.37), channel_id=1, source_target_pairs={{0,5},{1,4},{2,7},{3,6},{4,1},{5,0},{6,3},{7,2},{8,13},{9,12},{10,... | collective-permute-start | bytes 37640 | tf_op jit(solution)/shard_map/ppermute | solution.py:41
  44.8 7.2 %collective-permute-start.16 = (bf16[2,252,704]{1,2,0:T(8,128)(2,1)S(1)}, bf16[2,252,704]{1,2,0:T(8,128)(2,1)S(1)}, u32[]{:S(2)}, u32[]{:S(2)}) collective-permute-start(bf16[2,252,704]{1,2,0:T(8,128)(2,1)S(1)} %pad_maximum_fusion), channel_id=1, source_target_pairs={{0,1},{1,0},{2,3},{3,2},{4,5},{5,4},{6,7},{7,6},{8,9},{9,8},{10,11... | collective-permute-start | bytes 2128904 | tf_op jit(solution)/shard_map/ppermute | solution.py:59
  47.7 4.1 %collective-permute-start.15 = (bf16[1,7,7,128]{3,2,1,0:T(8,128)(2,1)S(1)}, bf16[1,7,7,128]{3,2,1,0:T(8,128)(2,1)S(1)}, u32[]{:S(2)}, u32[]{:S(2)}) collective-permute-start(bf16[1,7,7,128]{3,2,1,0:T(8,128)(2,1)S(1)} %fusion.118), channel_id=1, source_target_pairs={{0,17},{1,16},{2,19},{3,18},{4,21},{5,20},{6,23},{7,22},{8,25},{9,... | collective-permute-start | bytes 37640 | tf_op jit(solution)/shard_map/ppermute | solution.py:41
  52.1 0.9 %copy-start.1 = (bf16[2,252,704]{1,2,0:T(8,128)(2,1)}, bf16[2,252,704]{1,2,0:T(8,128)(2,1)S(1)}, u32[]{:S(2)}) copy-start(bf16[2,252,704]{1,2,0:T(8,128)(2,1)S(1)} %collective-permute-done.16) | copy-start | bytes 2128900
  54.4 4.1 %collective-permute-start.18 = (bf16[7,1,7,128]{3,2,1,0:T(8,128)(2,1)S(1)}, bf16[7,1,7,128]{3,2,1,0:T(8,128)(2,1)S(1)}, u32[]{:S(2)}, u32[]{:S(2)}) collective-permute-start(bf16[7,1,7,128]{3,2,1,0:T(8,128)(2,1)S(1)} %slice.605), channel_id=1, source_target_pairs={{0,13},{1,12},{2,15},{3,14},{4,9},{5,8},{6,11},{7,10},{8,5},{9,4},... | collective-permute-start | bytes 37640 | tf_op jit(solution)/shard_map/ppermute | solution.py:41
  56.3 3.1 %collective-permute-start.17 = (bf16[7,1,7,128]{3,2,1,0:T(8,128)(2,1)S(1)}, bf16[7,1,7,128]{3,2,1,0:T(8,128)(2,1)S(1)}, u32[]{:S(2)}, u32[]{:S(2)}) collective-permute-start(bf16[7,1,7,128]{3,2,1,0:T(8,128)(2,1)S(1)} %slice.605), channel_id=1, source_target_pairs={{0,5},{1,4},{2,7},{3,6},{4,1},{5,0},{6,3},{7,2},{8,13},{9,12},{10,... | collective-permute-start | bytes 37640 | tf_op jit(solution)/shard_map/ppermute | solution.py:41
  59.5 1.1 %copy-start.2 = (bf16[2,252,704]{1,2,0:T(8,128)(2,1)S(1)}, bf16[2,252,704]{1,2,0:T(8,128)(2,1)}, u32[]{:S(2)}) copy-start(bf16[2,252,704]{1,2,0:T(8,128)(2,1)} %copy-done.1) | copy-start | bytes 2128900
  62.1 6.0 %collective-permute-start.19 = (bf16[212,128]{1,0:T(8,128)(2,1)S(1)}, bf16[212,128]{1,0:T(8,128)(2,1)S(1)}, u32[]{:S(2)}, u32[]{:S(2)}) collective-permute-start(bf16[212,128]{1,0:T(8,128)(2,1)S(1)} %pad_maximum_fusion.12), channel_id=1, source_target_pairs={{0,17},{1,16},{2,19},{3,18},{4,21},{5,20},{6,23},{7,22},{8,25},{9,... | collective-permute-start | bytes 162824 | tf_op jit(solution)/shard_map/ppermute | solution.py:59
  68.4 3.7 %collective-permute-start.20 = (bf16[176,128]{1,0:T(8,128)(2,1)S(1)}, bf16[176,128]{1,0:T(8,128)(2,1)S(1)}, u32[]{:S(2)}, u32[]{:S(2)}) collective-permute-start(bf16[176,128]{1,0:T(8,128)(2,1)S(1)} %add_convert_fusion.2), channel_id=1, source_target_pairs={{0,5},{1,4},{2,7},{3,6},{4,1},{5,0},{6,3},{7,2},{8,13},{9,12},{10,... | collective-permute-start | bytes 135176 | tf_op jit(solution)/shard_map/ppermute | solution.py:41
  72.1 4.6 %collective-permute-start.21 = (bf16[176,128]{1,0:T(8,128)(2,1)S(1)}, bf16[176,128]{1,0:T(8,128)(2,1)S(1)}, u32[]{:S(2)}, u32[]{:S(2)}) collective-permute-start(bf16[176,128]{1,0:T(8,128)(2,1)S(1)} %add_convert_fusion.1), channel_id=1, source_target_pairs={{0,13},{1,12},{2,15},{3,14},{4,9},{5,8},{6,11},{7,10},{8,5},{9,4},... | collective-permute-start | bytes 135176 | tf_op jit(solution)/shard_map/ppermute | solution.py:41
  76.8 4.3 %collective-permute-start.22 = (bf16[284,128]{1,0:T(8,128)(2,1)S(1)}, bf16[284,128]{1,0:T(8,128)(2,1)S(1)}, u32[]{:S(2)}, u32[]{:S(2)}) collective-permute-start(bf16[284,128]{1,0:T(8,128)(2,1)S(1)} %maximum_maximum_fusion.2), channel_id=1, source_target_pairs={{0,3},{1,2},{2,1},{3,0},{4,7},{5,6},{6,5},{7,4},{8,11},{9,10},{10,... | collective-permute-start | bytes 218120 | tf_op jit(solution)/shard_map/ppermute | solution.py:59
  81.4 1.4 %collective-permute-start.23 = (bf16[460,128]{1,0:T(8,128)(2,1)S(1)}, bf16[460,128]{1,0:T(8,128)(2,1)S(1)}, u32[]{:S(2)}, u32[]{:S(2)}) collective-permute-start(bf16[460,128]{1,0:T(8,128)(2,1)S(1)} %maximum_maximum_fusion), channel_id=1, source_target_pairs={{0,1},{1,0},{2,3},{3,2},{4,5},{5,4},{6,7},{7,6},{8,9},{9,8},{10,11... | collective-permute-start | bytes 353288 | tf_op jit(solution)/shard_map/ppermute | solution.py:59

commit v9 on v8

--- a/solution.py
+++ b/solution.py
@@ -247,8 +247,6 @@
         for dim in (1, 0):
             low, high = plane(partial, dim, 0), plane(partial, dim, SIDE - 1)
             low16, high16 = low.astype(jnp.bfloat16), high.astype(jnp.bfloat16)
-            if (step, dim) == (1, 1):
-                low16, other_locked = lax.optimization_barrier((low16, other_locked))
             to_low, to_high = grid.exchanged(low16, high16, dim)
             partial = with_ends(
                 partial,

time: 85.7 us -> 82 us (0.957)
  waiting for transfers between devices: 45.2 us -> 39.1 us
  starting transfers between devices: 22.6 us -> 25.1 us
    ppermute x14, waiting for transfers between devices: 25.7 us -> 22.4 us  [swapped(): arrived = lax.ppermute(jnp.where(lower, high, low), AXIS, pairs)]
    ppermute x10, waiting for transfers between devices: 19.5 us -> 16.7 us  [partner(): lax.ppermute(value, AXIS, [(i, i ^ bits) for i in range(self.devices)])]
    ppermute x14, starting transfers between devices: 18.1 us -> 20.5 us  [swapped(): arrived = lax.ppermute(jnp.where(lower, high, low), AXIS, pairs)]
  transfers between devices with their start and end apart: 24 -> 24, of which waited for: 17 -> 16; matrix products, arithmetic and copies ran while one was open for 7% -> 7% of each run, Pallas kernels for 0% -> 0%
where the time goes in v9:
time: 82 us; the launch traced here: 81.8 us
  waiting for transfers between devices  39.1 us (48%)
  starting transfers between devices  25.1 us (31%)
  other arithmetic  5.52 us (7%)
  matrix products  5.52 us (7%)
  local copies, waits for them, and re-layouts  5.1 us (6%)
  between operations  1.51 us (2%)
    ppermute x14, waiting for transfers between devices, swapped(): arrived = lax.ppermute(jnp.where(lower, high, low), AXIS, pairs)  22.4 us
    ppermute x14, starting transfers between devices, swapped(): arrived = lax.ppermute(jnp.where(lower, high, low), AXIS, pairs)  20.5 us
    ppermute x10, waiting for transfers between devices, partner(): lax.ppermute(value, AXIS, [(i, i ^ bits) for i in range(self.devices)])  16.7 us
    ppermute x10, starting transfers between devices, partner(): lax.ppermute(value, AXIS, [(i, i ^ bits) for i in range(self.devices)])  4.6 us
    dot_general x12, matrix products, per_device(): jnp.dot(matrices[r], own, preferred_element_type=jnp.float32)  2.93 us
    unnamed x12, local copies, waits for them, and re-layouts  2.22 us
  transfers between devices with their start and end apart: 24, of which 16 were waited for; matrix products, arithmetic and copies ran while one was open for 7% of the time, Pallas kernels for 0%

profile of v9, /device:TPU:0, one launch (start us, length us, event | category | flops | bytes accessed | tf_op | source)
XLA Modules:
  0.0 81.8 jit_solution(7048068989023851949)
XLA Ops:
  0.6 0.9 %reshape.193 = bf16[6,6,6,128]{3,2,1,0:T(8,128)(2,1)S(1)} reshape(bf16[216,128]{1,0:T(8,128)(2,1)} %param.5) | data formatting | bytes 110592 | tf_op jit(solution)/shard_map/reshape | solution.py:193
  1.6 3.0 %collective-permute-start = (bf16[6,1,6,128]{3,2,1,0:T(8,128)(2,1)S(1)}, bf16[6,1,6,128]{3,2,1,0:T(8,128)(2,1)S(1)}, u32[]{:S(2)}, u32[]{:S(2)}) collective-permute-start(bf16[6,1,6,128]{3,2,1,0:T(8,128)(2,1)S(1)} %slice.439), channel_id=1, source_target_pairs={{0,4},{1,5},{2,6},{3,7},{4,0},{5,1},{6,2},{7,3},{8,12},{9,13},{10,... | collective-permute-start | bytes 27656 | tf_op jit(solution)/shard_map/ppermute | solution.py:41
  4.6 1.5 %collective-permute-start.1 = (bf16[6,1,6,128]{3,2,1,0:T(8,128)(2,1)S(1)}, bf16[6,1,6,128]{3,2,1,0:T(8,128)(2,1)S(1)}, u32[]{:S(2)}, u32[]{:S(2)}) collective-permute-start(bf16[6,1,6,128]{3,2,1,0:T(8,128)(2,1)S(1)} %slice.439), channel_id=1, source_target_pairs={{0,12},{1,13},{2,14},{3,15},{4,8},{5,9},{6,10},{7,11},{8,4},{9,5},... | collective-permute-start | bytes 27656 | tf_op jit(solution)/shard_map/ppermute | solution.py:41
  6.2 0.7 fusion
  7.3 1.2 %collective-permute-start.8 = (bf16[343,343]{1,0:T(8,128)(2,1)S(1)}, bf16[343,343]{1,0:T(8,128)(2,1)S(1)}, u32[]{:S(2)}, u32[]{:S(2)}) collective-permute-start(bf16[343,343]{1,0:T(8,128)(2,1)S(1)} %fusion), channel_id=1, source_target_pairs={{0,1},{1,0},{2,3},{3,2},{4,5},{5,4},{6,7},{7,6},{8,9},{9,8},{10,11... | collective-permute-start | bytes 705902 | tf_op jit(solution)/shard_map/ppermute | solution.py:59
  9.2 2.7 %collective-permute-start.3 = (bf16[1,7,6,128]{3,2,1,0:T(8,128)(2,1)S(1)}, bf16[1,7,6,128]{3,2,1,0:T(8,128)(2,1)S(1)}, u32[]{:S(2)}, u32[]{:S(2)}) collective-permute-start(bf16[1,7,6,128]{3,2,1,0:T(8,128)(2,1)S(1)} %pad_maximum_fusion.23), channel_id=1, source_target_pairs={{0,16},{1,17},{2,18},{3,19},{4,20},{5,21},{6,22},{7,23},{8,24},{9,... | collective-permute-start | bytes 32264 | tf_op jit(solution)/shard_map/ppermute | solution.py:41
  11.9 2.0 %collective-permute-done.3 = bf16[1,7,6,128]{3,2,1,0:T(8,128)(2,1)S(1)} collective-permute-done((bf16[1,7,6,128]{3,2,1,0:T(8,128)(2,1)S(1)}, bf16[1,7,6,128]{3,2,1,0:T(8,128)(2,1)S(1)}, u32[]{:S(2)}, u32[]{:S(2)}) %collective-permute-start.3) | collective-permute-done | bytes 10784 | tf_op jit(solution)/shard_map/ppermute | solution.py:41
  15.3 2.7 %collective-permute-start.2 = (bf16[36,704]{1,0:T(8,128)(2,1)S(1)}, bf16[36,704]{1,0:T(8,128)(2,1)S(1)}, u32[]{:S(2)}, u32[]{:S(2)}) collective-permute-start(bf16[36,704]{1,0:T(8,128)(2,1)S(1)} %slice.337), channel_id=1, source_target_pairs={{0,16},{1,17},{2,18},{3,19},{4,20},{5,21},{6,22},{7,23},{8,24},{9,... | collective-permute-start | bytes 152072 | tf_op jit(solution)/shard_map/ppermute | solution.py:41
  18.4 0.8 collective-permute-start.6
  19.2 3.1 %collective-permute-done.2 = bf16[36,704]{1,0:T(8,128)(2,1)S(1)} collective-permute-done((bf16[36,704]{1,0:T(8,128)(2,1)S(1)}, bf16[36,704]{1,0:T(8,128)(2,1)S(1)}, u32[]{:S(2)}, u32[]{:S(2)}) %collective-permute-start.2) | collective-permute-done | bytes 50720 | tf_op jit(solution)/shard_map/ppermute | solution.py:41
  23.1 1.0 %collective-permute-done.7 = bf16[343,343]{1,0:T(8,128)(2,1)S(1)} collective-permute-done((bf16[343,343]{1,0:T(8,128)(2,1)S(1)}, bf16[343,343]{1,0:T(8,128)(2,1)S(1)}, u32[]{:S(2)}, u32[]{:S(2)}) %collective-permute-start.7) | collective-permute-done | bytes 235330 | tf_op jit(solution)/shard_map/ppermute | solution.py:59
  26.4 1.4 %collective-permute-start.9 = (bf16[7,1,7,128]{3,2,1,0:T(8,128)(2,1)S(1)}, bf16[7,1,7,128]{3,2,1,0:T(8,128)(2,1)S(1)}, u32[]{:S(2)}, u32[]{:S(2)}) collective-permute-start(bf16[7,1,7,128]{3,2,1,0:T(8,128)(2,1)S(1)} %get-tuple-element.36), channel_id=1, source_target_pairs={{0,5},{1,4},{2,7},{3,6},{4,1},{5,0},{6,3},{7,2},{8,13},{9,12},{10,... | collective-permute-start | bytes 37640 | tf_op jit(solution)/shard_map/ppermute | solution.py:41
  28.0 1.8 %collective-permute-done.10 = bf16[7,1,7,128]{3,2,1,0:T(8,128)(2,1)S(1)} collective-permute-done((bf16[7,1,7,128]{3,2,1,0:T(8,128)(2,1)S(1)}, bf16[7,1,7,128]{3,2,1,0:T(8,128)(2,1)S(1)}, u32[]{:S(2)}, u32[]{:S(2)}) %collective-permute-start.10) | collective-permute-done | bytes 12576 | tf_op jit(solution)/shard_map/ppermute | solution.py:41
  29.9 3.0 %collective-permute-start.11 = (bf16[1,7,7,128]{3,2,1,0:T(8,128)(2,1)S(1)}, bf16[1,7,7,128]{3,2,1,0:T(8,128)(2,1)S(1)}, u32[]{:S(2)}, u32[]{:S(2)}) collective-permute-start(bf16[1,7,7,128]{3,2,1,0:T(8,128)(2,1)S(1)} %fusion.117), channel_id=1, source_target_pairs={{0,17},{1,16},{2,19},{3,18},{4,21},{5,20},{6,23},{7,22},{8,25},{9,... | collective-permute-start | bytes 37640 | tf_op jit(solution)/shard_map/ppermute | solution.py:41
  35.9 1.5 %collective-permute-start.13 = (bf16[7,1,7,128]{3,2,1,0:T(8,128)(2,1)S(1)}, bf16[7,1,7,128]{3,2,1,0:T(8,128)(2,1)S(1)}, u32[]{:S(2)}, u32[]{:S(2)}) collective-permute-start(bf16[7,1,7,128]{3,2,1,0:T(8,128)(2,1)S(1)} %broadcast_select_fusion.35), channel_id=1, source_target_pairs={{0,13},{1,12},{2,15},{3,14},{4,9},{5,8},{6,11},{7,10},{8,5},{9,4},... | collective-permute-start | bytes 37640 | tf_op jit(solution)/shard_map/ppermute | solution.py:41
  37.4 0.8 collective-permute-start.12
  38.2 5.3 %collective-permute-done.15 = bf16[252,704]{0,1:T(8,128)(2,1)S(1)} collective-permute-done((bf16[252,704]{0,1:T(8,128)(2,1)S(1)}, bf16[252,704]{0,1:T(8,128)(2,1)S(1)}, u32[]{:S(2)}, u32[]{:S(2)}) %collective-permute-start.15) | collective-permute-done | bytes 354848 | tf_op jit(solution)/shard_map/ppermute | solution.py:59
  44.1 4.0 %collective-permute-done.14 = bf16[1,7,7,128]{3,2,1,0:T(8,128)(2,1)S(1)} collective-permute-done((bf16[1,7,7,128]{3,2,1,0:T(8,128)(2,1)S(1)}, bf16[1,7,7,128]{3,2,1,0:T(8,128)(2,1)S(1)}, u32[]{:S(2)}, u32[]{:S(2)}) %collective-permute-start.14) | collective-permute-done | bytes 12576 | tf_op jit(solution)/shard_map/ppermute | solution.py:41
  48.4 0.9 %copy-done.1 = bf16[2,252,704]{1,2,0:T(8,128)(2,1)} copy-done((bf16[2,252,704]{1,2,0:T(8,128)(2,1)}, bf16[2,252,704]{1,2,0:T(8,128)(2,1)S(1)}, u32[]{:S(2)}) %copy-start.1) | copy-done | bytes 709656
  50.7 1.6 %collective-permute-start.17 = (bf16[7,1,7,128]{3,2,1,0:T(8,128)(2,1)S(1)}, bf16[7,1,7,128]{3,2,1,0:T(8,128)(2,1)S(1)}, u32[]{:S(2)}, u32[]{:S(2)}) collective-permute-start(bf16[7,1,7,128]{3,2,1,0:T(8,128)(2,1)S(1)} %slice.605), channel_id=1, source_target_pairs={{0,5},{1,4},{2,7},{3,6},{4,1},{5,0},{6,3},{7,2},{8,13},{9,12},{10,... | collective-permute-start | bytes 37640 | tf_op jit(solution)/shard_map/ppermute | solution.py:41
  53.1 0.9 %collective-permute-done.17 = bf16[7,1,7,128]{3,2,1,0:T(8,128)(2,1)S(1)} collective-permute-done((bf16[7,1,7,128]{3,2,1,0:T(8,128)(2,1)S(1)}, bf16[7,1,7,128]{3,2,1,0:T(8,128)(2,1)S(1)}, u32[]{:S(2)}, u32[]{:S(2)}) %collective-permute-start.17) | collective-permute-done | bytes 12576 | tf_op jit(solution)/shard_map/ppermute | solution.py:41
  54.0 2.4 %collective-permute-done.18 = bf16[7,1,7,128]{3,2,1,0:T(8,128)(2,1)S(1)} collective-permute-done((bf16[7,1,7,128]{3,2,1,0:T(8,128)(2,1)S(1)}, bf16[7,1,7,128]{3,2,1,0:T(8,128)(2,1)S(1)}, u32[]{:S(2)}, u32[]{:S(2)}) %collective-permute-start.18) | collective-permute-done | bytes 12576 | tf_op jit(solution)/shard_map/ppermute | solution.py:41
  56.7 0.9 %copy-done.2 = bf16[2,252,704]{1,2,0:T(8,128)(2,1)S(1)} copy-done((bf16[2,252,704]{1,2,0:T(8,128)(2,1)S(1)}, bf16[2,252,704]{1,2,0:T(8,128)(2,1)}, u32[]{:S(2)}) %copy-start.2) | copy-done | bytes 709656
  59.2 5.4 %collective-permute-done.19 = bf16[212,128]{1,0:T(8,128)(2,1)S(1)} collective-permute-done((bf16[212,128]{1,0:T(8,128)(2,1)S(1)}, bf16[212,128]{1,0:T(8,128)(2,1)S(1)}, u32[]{:S(2)}, u32[]{:S(2)}) %collective-permute-start.19) | collective-permute-done | bytes 54304 | tf_op jit(solution)/shard_map/ppermute | solution.py:59
  64.7 0.9 %collective-permute-start.20 = (bf16[176,128]{1,0:T(8,128)(2,1)S(1)}, bf16[176,128]{1,0:T(8,128)(2,1)S(1)}, u32[]{:S(2)}, u32[]{:S(2)}) collective-permute-start(bf16[176,128]{1,0:T(8,128)(2,1)S(1)} %add_convert_fusion.2), channel_id=1, source_target_pairs={{0,5},{1,4},{2,7},{3,6},{4,1},{5,0},{6,3},{7,2},{8,13},{9,12},{10,... | collective-permute-start | bytes 135176 | tf_op jit(solution)/shard_map/ppermute | solution.py:41
  65.8 2.7 %collective-permute-done.20 = bf16[176,128]{1,0:T(8,128)(2,1)S(1)} collective-permute-done((bf16[176,128]{1,0:T(8,128)(2,1)S(1)}, bf16[176,128]{1,0:T(8,128)(2,1)S(1)}, u32[]{:S(2)}, u32[]{:S(2)}) %collective-permute-start.20) | collective-permute-done | bytes 45088 | tf_op jit(solution)/shard_map/ppermute | solution.py:41
  68.5 4.5 %collective-permute-done.21 = bf16[176,128]{1,0:T(8,128)(2,1)S(1)} collective-permute-done((bf16[176,128]{1,0:T(8,128)(2,1)S(1)}, bf16[176,128]{1,0:T(8,128)(2,1)S(1)}, u32[]{:S(2)}, u32[]{:S(2)}) %collective-permute-start.21) | collective-permute-done | bytes 45088 | tf_op jit(solution)/shard_map/ppermute | solution.py:41
  73.9 3.6 %collective-permute-done.22 = bf16[284,128]{1,0:T(8,128)(2,1)S(1)} collective-permute-done((bf16[284,128]{1,0:T(8,128)(2,1)S(1)}, bf16[284,128]{1,0:T(8,128)(2,1)S(1)}, u32[]{:S(2)}, u32[]{:S(2)}) %collective-permute-start.22) | collective-permute-done | bytes 72736 | tf_op jit(solution)/shard_map/ppermute | solution.py:59
  77.9 1.2 %collective-permute-done.23 = bf16[460,128]{1,0:T(8,128)(2,1)S(1)} collective-permute-done((bf16[460,128]{1,0:T(8,128)(2,1)S(1)}, bf16[460,128]{1,0:T(8,128)(2,1)S(1)}, u32[]{:S(2)}, u32[]{:S(2)}) %collective-permute-start.23) | collective-permute-done | bytes 117792 | tf_op jit(solution)/shard_map/ppermute | solution.py:59
  79.2 0.9 %fusion.9 = f32[176,512]{1,0:T(8,128)S(1)} fusion(s32[512]{0:T(512)S(1)} %get-tuple-element.120, s32[512]{0:T(512)S(1)} %get-tuple-element.122, s32[]{:T(128)S(6)} %add.288, s32[512]{0:T(512)S(1)} %get-tuple-element.121, s32[512]{0:T(512)S(1)} %get-tuple-element.125, s32[512]{0:T(512)S(1)} %get-tuple-element.119, s32[512]{0:T(512)S(1)} %get-tuple-element.126, ...), kind=kOutput, calls=%fused_computation.25 | convolution fusion | flops 98238464 | bytes 554500 | tf_op jit(solution)/shard_map/dot_general | solution.py:330
  80.3 0.8 pad_maximum_fusion.2
  81.1 0.7 pad_maximum_fusion.16
  (169 shorter events, 15.7 us)
Async XLA Ops:
  0.6 5.5 %copy-start = (bf16[1,343,343]{2,1,0:T(8,128)(2,1)S(1)}, bf16[1,343,343]{2,1,0:T(8,128)(2,1)}, u32[]{:S(2)}) copy-start(bf16[1,343,343]{2,1,0:T(8,128)(2,1)} %param.6) | copy-start | bytes 705898
  1.5 4.6 %copy-start.4 = (s32[1,343]{1,0:T(1,128)S(1)}, s32[1,343]{1,0:T(1,128)}, u32[]{:S(2)}) copy-start(s32[1,343]{1,0:T(1,128)} %param.7) | copy-start | bytes 4120
  1.5 4.6 %copy-start.5 = (f32[343]{0:T(512)S(1)}, f32[343]{0:T(512)}, u32[]{:S(2)}) copy-start(f32[343]{0:T(512)} %param.8) | copy-start | bytes 4120
  1.6 7.2 %collective-permute-start = (bf16[6,1,6,128]{3,2,1,0:T(8,128)(2,1)S(1)}, bf16[6,1,6,128]{3,2,1,0:T(8,128)(2,1)S(1)}, u32[]{:S(2)}, u32[]{:S(2)}) collective-permute-start(bf16[6,1,6,128]{3,2,1,0:T(8,128)(2,1)S(1)} %slice.439), channel_id=1, source_target_pairs={{0,4},{1,5},{2,6},{3,7},{4,0},{5,1},{6,2},{7,3},{8,12},{9,13},{10,... | collective-permute-start | bytes 27656 | tf_op jit(solution)/shard_map/ppermute | solution.py:41
  4.6 4.6 %collective-permute-start.1 = (bf16[6,1,6,128]{3,2,1,0:T(8,128)(2,1)S(1)}, bf16[6,1,6,128]{3,2,1,0:T(8,128)(2,1)S(1)}, u32[]{:S(2)}, u32[]{:S(2)}) collective-permute-start(bf16[6,1,6,128]{3,2,1,0:T(8,128)(2,1)S(1)} %slice.439), channel_id=1, source_target_pairs={{0,12},{1,13},{2,14},{3,15},{4,8},{5,9},{6,10},{7,11},{8,4},{9,5},... | collective-permute-start | bytes 27656 | tf_op jit(solution)/shard_map/ppermute | solution.py:41
  6.9 11.6 %collective-permute-start.5 = (bf16[343,343]{1,0:T(8,128)(2,1)S(1)}, bf16[343,343]{1,0:T(8,128)(2,1)S(1)}, u32[]{:S(2)}, u32[]{:S(2)}) collective-permute-start(bf16[343,343]{1,0:T(8,128)(2,1)S(1)} %fusion), channel_id=1, source_target_pairs={{0,3},{1,2},{2,1},{3,0},{4,7},{5,6},{6,5},{7,4},{8,11},{9,10},{10,... | collective-permute-start | bytes 705902 | tf_op jit(solution)/shard_map/ppermute | solution.py:59
  7.3 17.5 %collective-permute-start.8 = (bf16[343,343]{1,0:T(8,128)(2,1)S(1)}, bf16[343,343]{1,0:T(8,128)(2,1)S(1)}, u32[]{:S(2)}, u32[]{:S(2)}) collective-permute-start(bf16[343,343]{1,0:T(8,128)(2,1)S(1)} %fusion), channel_id=1, source_target_pairs={{0,1},{1,0},{2,3},{3,2},{4,5},{5,4},{6,7},{7,6},{8,9},{9,8},{10,11... | collective-permute-start | bytes 705902 | tf_op jit(solution)/shard_map/ppermute | solution.py:59
  9.2 4.7 %collective-permute-start.3 = (bf16[1,7,6,128]{3,2,1,0:T(8,128)(2,1)S(1)}, bf16[1,7,6,128]{3,2,1,0:T(8,128)(2,1)S(1)}, u32[]{:S(2)}, u32[]{:S(2)}) collective-permute-start(bf16[1,7,6,128]{3,2,1,0:T(8,128)(2,1)S(1)} %pad_maximum_fusion.23), channel_id=1, source_target_pairs={{0,16},{1,17},{2,18},{3,19},{4,20},{5,21},{6,22},{7,23},{8,24},{9,... | collective-permute-start | bytes 32264 | tf_op jit(solution)/shard_map/ppermute | solution.py:41
  14.2 1.0 %copy-start.3 = (bf16[216,704]{1,0:T(8,128)(2,1)S(1)}, bf16[216,704]{1,0:T(8,128)(2,1)}, u32[]{:S(2)}) copy-start(bf16[216,704]{1,0:T(8,128)(2,1)} %param.9) | copy-start | bytes 912388
  14.3 3.8 %collective-permute-start.4 = (bf16[152,128]{1,0:T(8,128)(2,1)S(1)}, bf16[152,128]{1,0:T(8,128)(2,1)S(1)}, u32[]{:S(2)}, u32[]{:S(2)}) collective-permute-start(bf16[152,128]{1,0:T(8,128)(2,1)S(1)} %pad_maximum_fusion.17), channel_id=1, source_target_pairs={{0,3},{1,2},{2,1},{3,0},{4,7},{5,6},{6,5},{7,4},{8,11},{9,10},{10,... | collective-permute-start | bytes 116744 | tf_op jit(solution)/shard_map/ppermute | solution.py:59
  15.3 7.0 %collective-permute-start.2 = (bf16[36,704]{1,0:T(8,128)(2,1)S(1)}, bf16[36,704]{1,0:T(8,128)(2,1)S(1)}, u32[]{:S(2)}, u32[]{:S(2)}) collective-permute-start(bf16[36,704]{1,0:T(8,128)(2,1)S(1)} %slice.337), channel_id=1, source_target_pairs={{0,16},{1,17},{2,18},{3,19},{4,20},{5,21},{6,22},{7,23},{8,24},{9,... | collective-permute-start | bytes 152072 | tf_op jit(solution)/shard_map/ppermute | solution.py:41
  18.4 4.2 %collective-permute-start.6 = (bf16[152,128]{1,0:T(8,128)(2,1)S(1)}, bf16[152,128]{1,0:T(8,128)(2,1)S(1)}, u32[]{:S(2)}, u32[]{:S(2)}) collective-permute-start(bf16[152,128]{1,0:T(8,128)(2,1)S(1)} %pad_maximum_fusion.18), channel_id=1, source_target_pairs={{0,1},{1,0},{2,3},{3,2},{4,5},{5,4},{6,7},{7,6},{8,9},{9,8},{10,11... | collective-permute-start | bytes 116744 | tf_op jit(solution)/shard_map/ppermute | solution.py:59
  22.5 1.6 %collective-permute-start.7 = (bf16[343,343]{1,0:T(8,128)(2,1)S(1)}, bf16[343,343]{1,0:T(8,128)(2,1)S(1)}, u32[]{:S(2)}, u32[]{:S(2)}) collective-permute-start(bf16[343,343]{1,0:T(8,128)(2,1)S(1)} %collective-permute-done.5), channel_id=1, source_target_pairs={{0,1},{1,0},{2,3},{3,2},{4,5},{5,4},{6,7},{7,6},{8,9},{9,8},{10,11... | collective-permute-start | bytes 705902 | tf_op jit(solution)/shard_map/ppermute | solution.py:59
  25.7 4.1 %collective-permute-start.10 = (bf16[7,1,7,128]{3,2,1,0:T(8,128)(2,1)S(1)}, bf16[7,1,7,128]{3,2,1,0:T(8,128)(2,1)S(1)}, u32[]{:S(2)}, u32[]{:S(2)}) collective-permute-start(bf16[7,1,7,128]{3,2,1,0:T(8,128)(2,1)S(1)} %broadcast_select_fusion.36), channel_id=1, source_target_pairs={{0,13},{1,12},{2,15},{3,14},{4,9},{5,8},{6,11},{7,10},{8,5},{9,4},... | collective-permute-start | bytes 37640 | tf_op jit(solution)/shard_map/ppermute | solution.py:41
  26.4 3.4 %collective-permute-start.9 = (bf16[7,1,7,128]{3,2,1,0:T(8,128)(2,1)S(1)}, bf16[7,1,7,128]{3,2,1,0:T(8,128)(2,1)S(1)}, u32[]{:S(2)}, u32[]{:S(2)}) collective-permute-start(bf16[7,1,7,128]{3,2,1,0:T(8,128)(2,1)S(1)} %get-tuple-element.36), channel_id=1, source_target_pairs={{0,5},{1,4},{2,7},{3,6},{4,1},{5,0},{6,3},{7,2},{8,13},{9,12},{10,... | collective-permute-start | bytes 37640 | tf_op jit(solution)/shard_map/ppermute | solution.py:41
  29.9 4.4 %collective-permute-start.11 = (bf16[1,7,7,128]{3,2,1,0:T(8,128)(2,1)S(1)}, bf16[1,7,7,128]{3,2,1,0:T(8,128)(2,1)S(1)}, u32[]{:S(2)}, u32[]{:S(2)}) collective-permute-start(bf16[1,7,7,128]{3,2,1,0:T(8,128)(2,1)S(1)} %fusion.117), channel_id=1, source_target_pairs={{0,17},{1,16},{2,19},{3,18},{4,21},{5,20},{6,23},{7,22},{8,25},{9,... | collective-permute-start | bytes 37640 | tf_op jit(solution)/shard_map/ppermute | solution.py:41
  33.1 10.4 %collective-permute-start.15 = (bf16[252,704]{0,1:T(8,128)(2,1)S(1)}, bf16[252,704]{0,1:T(8,128)(2,1)S(1)}, u32[]{:S(2)}, u32[]{:S(2)}) collective-permute-start(bf16[252,704]{0,1:T(8,128)(2,1)S(1)} %pad_maximum_fusion.1), channel_id=1, source_target_pairs={{0,3},{1,2},{2,1},{3,0},{4,7},{5,6},{6,5},{7,4},{8,11},{9,10},{10,... | collective-permute-start | bytes 1064456 | tf_op jit(solution)/shard_map/ppermute | solution.py:59
  35.9 8.0 %collective-permute-start.13 = (bf16[7,1,7,128]{3,2,1,0:T(8,128)(2,1)S(1)}, bf16[7,1,7,128]{3,2,1,0:T(8,128)(2,1)S(1)}, u32[]{:S(2)}, u32[]{:S(2)}) collective-permute-start(bf16[7,1,7,128]{3,2,1,0:T(8,128)(2,1)S(1)} %broadcast_select_fusion.35), channel_id=1, source_target_pairs={{0,13},{1,12},{2,15},{3,14},{4,9},{5,8},{6,11},{7,10},{8,5},{9,4},... | collective-permute-start | bytes 37640 | tf_op jit(solution)/shard_map/ppermute | solution.py:41
  37.4 6.5 %collective-permute-start.12 = (bf16[7,1,7,128]{3,2,1,0:T(8,128)(2,1)S(1)}, bf16[7,1,7,128]{3,2,1,0:T(8,128)(2,1)S(1)}, u32[]{:S(2)}, u32[]{:S(2)}) collective-permute-start(bf16[7,1,7,128]{3,2,1,0:T(8,128)(2,1)S(1)} %get-tuple-element.33), channel_id=1, source_target_pairs={{0,5},{1,4},{2,7},{3,6},{4,1},{5,0},{6,3},{7,2},{8,13},{9,12},{10,... | collective-permute-start | bytes 37640 | tf_op jit(solution)/shard_map/ppermute | solution.py:41
  43.7 4.7 %collective-permute-start.16 = (bf16[2,252,704]{1,2,0:T(8,128)(2,1)S(1)}, bf16[2,252,704]{1,2,0:T(8,128)(2,1)S(1)}, u32[]{:S(2)}, u32[]{:S(2)}) collective-permute-start(bf16[2,252,704]{1,2,0:T(8,128)(2,1)S(1)} %pad_maximum_fusion), channel_id=1, source_target_pairs={{0,1},{1,0},{2,3},{3,2},{4,5},{5,4},{6,7},{7,6},{8,9},{9,8},{10,11... | collective-permute-start | bytes 2128904 | tf_op jit(solution)/shard_map/ppermute | solution.py:59
  44.0 4.1 %collective-permute-start.14 = (bf16[1,7,7,128]{3,2,1,0:T(8,128)(2,1)S(1)}, bf16[1,7,7,128]{3,2,1,0:T(8,128)(2,1)S(1)}, u32[]{:S(2)}, u32[]{:S(2)}) collective-permute-start(bf16[1,7,7,128]{3,2,1,0:T(8,128)(2,1)S(1)} %fusion.118), channel_id=1, source_target_pairs={{0,17},{1,16},{2,19},{3,18},{4,21},{5,20},{6,23},{7,22},{8,25},{9,... | collective-permute-start | bytes 37640 | tf_op jit(solution)/shard_map/ppermute | solution.py:41
  48.4 0.9 %copy-start.1 = (bf16[2,252,704]{1,2,0:T(8,128)(2,1)}, bf16[2,252,704]{1,2,0:T(8,128)(2,1)S(1)}, u32[]{:S(2)}) copy-start(bf16[2,252,704]{1,2,0:T(8,128)(2,1)S(1)} %collective-permute-done.16) | copy-start | bytes 2128900
  50.7 3.2 %collective-permute-start.17 = (bf16[7,1,7,128]{3,2,1,0:T(8,128)(2,1)S(1)}, bf16[7,1,7,128]{3,2,1,0:T(8,128)(2,1)S(1)}, u32[]{:S(2)}, u32[]{:S(2)}) collective-permute-start(bf16[7,1,7,128]{3,2,1,0:T(8,128)(2,1)S(1)} %slice.605), channel_id=1, source_target_pairs={{0,5},{1,4},{2,7},{3,6},{4,1},{5,0},{6,3},{7,2},{8,13},{9,12},{10,... | collective-permute-start | bytes 37640 | tf_op jit(solution)/shard_map/ppermute | solution.py:41
  52.3 4.0 %collective-permute-start.18 = (bf16[7,1,7,128]{3,2,1,0:T(8,128)(2,1)S(1)}, bf16[7,1,7,128]{3,2,1,0:T(8,128)(2,1)S(1)}, u32[]{:S(2)}, u32[]{:S(2)}) collective-permute-start(bf16[7,1,7,128]{3,2,1,0:T(8,128)(2,1)S(1)} %slice.605), channel_id=1, source_target_pairs={{0,13},{1,12},{2,15},{3,14},{4,9},{5,8},{6,11},{7,10},{8,5},{9,4},... | collective-permute-start | bytes 37640 | tf_op jit(solution)/shard_map/ppermute | solution.py:41
  56.4 1.1 %copy-start.2 = (bf16[2,252,704]{1,2,0:T(8,128)(2,1)S(1)}, bf16[2,252,704]{1,2,0:T(8,128)(2,1)}, u32[]{:S(2)}) copy-start(bf16[2,252,704]{1,2,0:T(8,128)(2,1)} %copy-done.1) | copy-start | bytes 2128900
  59.1 5.5 %collective-permute-start.19 = (bf16[212,128]{1,0:T(8,128)(2,1)S(1)}, bf16[212,128]{1,0:T(8,128)(2,1)S(1)}, u32[]{:S(2)}, u32[]{:S(2)}) collective-permute-start(bf16[212,128]{1,0:T(8,128)(2,1)S(1)} %pad_maximum_fusion.12), channel_id=1, source_target_pairs={{0,17},{1,16},{2,19},{3,18},{4,21},{5,20},{6,23},{7,22},{8,25},{9,... | collective-permute-start | bytes 162824 | tf_op jit(solution)/shard_map/ppermute | solution.py:59
  64.7 3.7 %collective-permute-start.20 = (bf16[176,128]{1,0:T(8,128)(2,1)S(1)}, bf16[176,128]{1,0:T(8,128)(2,1)S(1)}, u32[]{:S(2)}, u32[]{:S(2)}) collective-permute-start(bf16[176,128]{1,0:T(8,128)(2,1)S(1)} %add_convert_fusion.2), channel_id=1, source_target_pairs={{0,5},{1,4},{2,7},{3,6},{4,1},{5,0},{6,3},{7,2},{8,13},{9,12},{10,... | collective-permute-start | bytes 135176 | tf_op jit(solution)/shard_map/ppermute | solution.py:41
  68.4 4.6 %collective-permute-start.21 = (bf16[176,128]{1,0:T(8,128)(2,1)S(1)}, bf16[176,128]{1,0:T(8,128)(2,1)S(1)}, u32[]{:S(2)}, u32[]{:S(2)}) collective-permute-start(bf16[176,128]{1,0:T(8,128)(2,1)S(1)} %add_convert_fusion.1), channel_id=1, source_target_pairs={{0,13},{1,12},{2,15},{3,14},{4,9},{5,8},{6,11},{7,10},{8,5},{9,4},... | collective-permute-start | bytes 135176 | tf_op jit(solution)/shard_map/ppermute | solution.py:41
  73.2 4.3 %collective-permute-start.22 = (bf16[284,128]{1,0:T(8,128)(2,1)S(1)}, bf16[284,128]{1,0:T(8,128)(2,1)S(1)}, u32[]{:S(2)}, u32[]{:S(2)}) collective-permute-start(bf16[284,128]{1,0:T(8,128)(2,1)S(1)} %maximum_maximum_fusion.2), channel_id=1, source_target_pairs={{0,3},{1,2},{2,1},{3,0},{4,7},{5,6},{6,5},{7,4},{8,11},{9,10},{10,... | collective-permute-start | bytes 218120 | tf_op jit(solution)/shard_map/ppermute | solution.py:59
  77.7 1.4 %collective-permute-start.23 = (bf16[460,128]{1,0:T(8,128)(2,1)S(1)}, bf16[460,128]{1,0:T(8,128)(2,1)S(1)}, u32[]{:S(2)}, u32[]{:S(2)}) collective-permute-start(bf16[460,128]{1,0:T(8,128)(2,1)S(1)} %maximum_maximum_fusion), channel_id=1, source_target_pairs={{0,1},{1,0},{2,3},{3,2},{4,5},{5,4},{6,7},{7,6},{8,9},{9,8},{10,11... | collective-permute-start | bytes 353288 | tf_op jit(solution)/shard_map/ppermute | solution.py:59

commit v10 on v9

--- a/solution.py
+++ b/solution.py
@@ -196,20 +196,29 @@
     matrix = by_rows(slots_matrix(cell_matrix, connectivity, potential))
     other = by_rows(grid.partner(matrix, FIRST))
     field = jnp.concatenate([grid.exchanged(high, high, 1, cross=0)[0], field], axis=1)
-    high = plane(field, 0, edge - 1)
-
-    locked, high = lax.optimization_barrier((locked, high))
-    top = by_rows(locked[-edge * edge :])
-    bottom = by_rows(grid.exchanged(top, top, 0, cross=0)[0])
+
+    high = field[edge - 1].reshape(SIDE * edge, columns)
+    tiles = -(-locked.shape[1] // columns)
+    top = jnp.pad(locked[-edge * edge :], ((0, 0), (0, -locked.shape[1] % columns)))
+    top = jnp.concatenate(split(top, tiles), axis=0)
+    sent = jnp.concatenate([top, high], axis=0)
+    arrived = grid.exchanged(sent, sent, 0, cross=0)[0]
+    bottom = jnp.split(arrived[: top.shape[0]], tiles, axis=0)
+    bottom = jnp.concatenate(bottom, axis=1)[:, : locked.shape[1]]
     locked = jnp.concatenate([bottom, locked], axis=0)
-    other_locked = grid.partner(locked, FIRST)
-
-    field = jnp.concatenate([grid.exchanged(high, high, 0, cross=0)[0], field], axis=0)
+    field = jnp.concatenate(
+        [arrived[top.shape[0] :].reshape(1, SIDE, edge, columns), field], axis=0
+    )
+
     rows = field.reshape(SIDE * SIDE * edge, columns)
     second = by_rows(grid.partner(matrix, SECOND))
     mine, both = to_shares(grid, jnp.pad(rows, ((0, -rows.shape[0] % 16), (0, 0))), other)
     mine, both = lax.optimization_barrier((mine, both))
     matrices = [matrix, second, both, other]
+
+    locked, mine = lax.optimization_barrier((locked, mine))
+    parts = [locked[:128], locked[128:]]
+    other_parts = [grid.partner(part, FIRST) for part in parts]
     field = mine[: rows.shape[0]].reshape(SIDE, SIDE, edge, columns)
     low = to_next_partition(plane(field, 2, edge - 1), width)
     field = jnp.concatenate([low, field], axis=2)
@@ -247,6 +256,10 @@
         for dim in (1, 0):
             low, high = plane(partial, dim, 0), plane(partial, dim, SIDE - 1)
             low16, high16 = low.astype(jnp.bfloat16), high.astype(jnp.bfloat16)
+            if step == 1:
+                low16, other_parts[1 - dim] = lax.optimization_barrier(
+                    (low16, other_parts[1 - dim])
+                )
             to_low, to_high = grid.exchanged(low16, high16, dim)
             partial = with_ends(
                 partial,
@@ -260,12 +273,11 @@
         following = rounded(jnp.where(inside, following, 0.0))
         older = current
         current = following
-        if step == 1:
-            both_locked = grid.partner(jnp.stack([locked, other_locked]), SECOND)
-            current, both_locked = lax.optimization_barrier((current, both_locked))
-            all_locked = [locked, both_locked[0], both_locked[1], other_locked]
-
+    other_locked = jnp.concatenate(other_parts, axis=0)
+    both_locked = grid.partner(jnp.stack([locked, other_locked]), SECOND)
     low = plane(partial, 1, 0).astype(jnp.bfloat16)
+    low, both_locked = lax.optimization_barrier((low, both_locked))
+    all_locked = [locked, both_locked[0], both_locked[1], other_locked]
     to_high = grid.exchanged(low, low, 1)[1].astype(jnp.float32)
     partial = with_ends(partial, 1, None, plane(partial, 1, SIDE - 1) + to_high)
     partial = coeffs[0] * partial[:, 1:, 1:].reshape(SIDE, edge * edge, columns)

time: 82 us -> 84.8 us (1.034)
  other arithmetic: 5.52 us -> 8.71 us
  waiting for transfers between devices: 39.1 us -> 37 us
  matrix products: 5.52 us -> 7.49 us
    ppermute x14 -> x13, starting transfers between devices: 20.5 us -> 18.2 us  [swapped(): arrived = lax.ppermute(jnp.where(lower, high, low), AXIS, pairs)]
    dot_general x4, matrix products: 1 us -> 2.98 us  [per_device(): lax.dot_general(all_locked[r], jnp.where(owner_near == r, weights, jnp.ze...]
    ppermute x14 -> x13, waiting for transfers between devices: 22.4 us -> 20.4 us  [swapped(): arrived = lax.ppermute(jnp.where(lower, high, low), AXIS, pairs)]
    ppermute x10 -> x11, starting transfers between devices: 4.6 us -> 6.15 us  [partner(): lax.ppermute(value, AXIS, [(i, i ^ bits) for i in range(self.devices)])]
    unnamed x12 -> x27, local copies, waits for them, and re-layouts: 2.22 us -> 1.85 us
    ppermute x10 -> x11, waiting for transfers between devices: 16.7 us -> 16.6 us  [partner(): lax.ppermute(value, AXIS, [(i, i ^ bits) for i in range(self.devices)])]
  transfers between devices with their start and end apart: 24 -> 24, of which waited for: 16 -> 16; matrix products, arithmetic and copies ran while one was open for 7% -> 13% of each run, Pallas kernels for 0% -> 0%
where the time goes in v10:
time: 84.8 us; the launch traced here: 84.5 us
  waiting for transfers between devices  37 us (44%)
  starting transfers between devices  24.4 us (29%)
  other arithmetic  8.71 us (10%)
  matrix products  7.49 us (9%)
  local copies, waits for them, and re-layouts  5.11 us (6%)
  between operations  1.8 us (2%)
    ppermute x13, waiting for transfers between devices, swapped(): arrived = lax.ppermute(jnp.where(lower, high, low), AXIS, pairs)  20.4 us
    ppermute x13, starting transfers between devices, swapped(): arrived = lax.ppermute(jnp.where(lower, high, low), AXIS, pairs)  18.2 us
    ppermute x11, waiting for transfers between devices, partner(): lax.ppermute(value, AXIS, [(i, i ^ bits) for i in range(self.devices)])  16.6 us
    ppermute x11, starting transfers between devices, partner(): lax.ppermute(value, AXIS, [(i, i ^ bits) for i in range(self.devices)])  6.15 us
    dot_general x4, matrix products, per_device(): lax.dot_general(all_locked[r], jnp.where(owner_near == r, weights, jnp.ze...  2.98 us
    dot_general x12, matrix products, per_device(): jnp.dot(matrices[r], own, preferred_element_type=jnp.float32)  2.93 us
    unnamed x27, local copies, waits for them, and re-layouts  1.85 us
  transfers between devices with their start and end apart: 24, of which 16 were waited for; matrix products, arithmetic and copies ran while one was open for 13% of the time, Pallas kernels for 0%

profile of v10, /device:TPU:0, one launch (start us, length us, event | category | flops | bytes accessed | tf_op | source)
XLA Modules:
  0.0 84.5 jit_solution(6760933499712656079)
XLA Ops:
  0.6 0.9 %reshape.200 = bf16[6,6,6,128]{3,2,1,0:T(8,128)(2,1)S(1)} reshape(bf16[216,128]{1,0:T(8,128)(2,1)} %param.5) | data formatting | bytes 110592 | tf_op jit(solution)/shard_map/reshape | solution.py:193
  1.6 4.0 %collective-permute-start.1 = (bf16[6,1,6,128]{3,2,1,0:T(8,128)(2,1)S(1)}, bf16[6,1,6,128]{3,2,1,0:T(8,128)(2,1)S(1)}, u32[]{:S(2)}, u32[]{:S(2)}) collective-permute-start(bf16[6,1,6,128]{3,2,1,0:T(8,128)(2,1)S(1)} %slice.496), channel_id=1, source_target_pairs={{0,12},{1,13},{2,14},{3,15},{4,8},{5,9},{6,10},{7,11},{8,4},{9,5},... | collective-permute-start | bytes 27656 | tf_op jit(solution)/shard_map/ppermute | solution.py:41
  7.3 1.2 %collective-permute-start.7 = (bf16[343,343]{1,0:T(8,128)(2,1)S(1)}, bf16[343,343]{1,0:T(8,128)(2,1)S(1)}, u32[]{:S(2)}, u32[]{:S(2)}) collective-permute-start(bf16[343,343]{1,0:T(8,128)(2,1)S(1)} %fusion), channel_id=1, source_target_pairs={{0,1},{1,0},{2,3},{3,2},{4,5},{5,4},{6,7},{7,6},{8,9},{9,8},{10,11... | collective-permute-start | bytes 705902 | tf_op jit(solution)/shard_map/ppermute | solution.py:59
  10.3 2.7 %collective-permute-start.2 = (bf16[258,128]{1,0:T(8,128)(2,1)S(1)}, bf16[258,128]{1,0:T(8,128)(2,1)S(1)}, u32[]{:S(2)}, u32[]{:S(2)}) collective-permute-start(bf16[258,128]{1,0:T(8,128)(2,1)S(1)} %concatenate.135), channel_id=1, source_target_pairs={{0,16},{1,17},{2,18},{3,19},{4,20},{5,21},{6,22},{7,23},{8,24},{9,... | collective-permute-start | bytes 198152 | tf_op jit(solution)/shard_map/ppermute | solution.py:41
  13.0 3.7 %collective-permute-done.2 = bf16[258,128]{1,0:T(8,128)(2,1)S(1)} collective-permute-done((bf16[258,128]{1,0:T(8,128)(2,1)S(1)}, bf16[258,128]{1,0:T(8,128)(2,1)S(1)}, u32[]{:S(2)}, u32[]{:S(2)}) %collective-permute-start.2) | collective-permute-done | bytes 66080 | tf_op jit(solution)/shard_map/ppermute | solution.py:41
  17.5 3.6 %collective-permute-done.3 = bf16[152,128]{1,0:T(8,128)(2,1)S(1)} collective-permute-done((bf16[152,128]{1,0:T(8,128)(2,1)S(1)}, bf16[152,128]{1,0:T(8,128)(2,1)S(1)}, u32[]{:S(2)}, u32[]{:S(2)}) %collective-permute-start.3) | collective-permute-done | bytes 38944 | tf_op jit(solution)/shard_map/ppermute | solution.py:59
  23.4 0.8 fusion.146
  26.3 1.0 %collective-permute-start.8 = (bf16[7,1,7,128]{3,2,1,0:T(8,128)(2,1)S(1)}, bf16[7,1,7,128]{3,2,1,0:T(8,128)(2,1)S(1)}, u32[]{:S(2)}, u32[]{:S(2)}) collective-permute-start(bf16[7,1,7,128]{3,2,1,0:T(8,128)(2,1)S(1)} %get-tuple-element.47), channel_id=1, source_target_pairs={{0,5},{1,4},{2,7},{3,6},{4,1},{5,0},{6,3},{7,2},{8,13},{9,12},{10,... | collective-permute-start | bytes 37640 | tf_op jit(solution)/shard_map/ppermute | solution.py:41
  27.3 2.4 %collective-permute-done.9 = bf16[7,1,7,128]{3,2,1,0:T(8,128)(2,1)S(1)} collective-permute-done((bf16[7,1,7,128]{3,2,1,0:T(8,128)(2,1)S(1)}, bf16[7,1,7,128]{3,2,1,0:T(8,128)(2,1)S(1)}, u32[]{:S(2)}, u32[]{:S(2)}) %collective-permute-start.9) | collective-permute-done | bytes 12576 | tf_op jit(solution)/shard_map/ppermute | solution.py:41
  29.8 2.9 %collective-permute-start.10 = (bf16[1,7,7,128]{3,2,1,0:T(8,128)(2,1)S(1)}, bf16[1,7,7,128]{3,2,1,0:T(8,128)(2,1)S(1)}, u32[]{:S(2)}, u32[]{:S(2)}) collective-permute-start(bf16[1,7,7,128]{3,2,1,0:T(8,128)(2,1)S(1)} %fusion.115), channel_id=1, source_target_pairs={{0,17},{1,16},{2,19},{3,18},{4,21},{5,20},{6,23},{7,22},{8,25},{9,... | collective-permute-start | bytes 37640 | tf_op jit(solution)/shard_map/ppermute | solution.py:41
  33.6 0.9 %collective-permute-start.11 = (bf16[128,704]{0,1:T(8,128)(2,1)S(1)}, bf16[128,704]{0,1:T(8,128)(2,1)S(1)}, u32[]{:S(2)}, u32[]{:S(2)}) collective-permute-start(bf16[128,704]{0,1:T(8,128)(2,1)S(1)} %slice.433), channel_id=1, source_target_pairs={{0,3},{1,2},{2,1},{3,0},{4,7},{5,6},{6,5},{7,4},{8,11},{9,10},{10,... | collective-permute-start | bytes 540680 | tf_op jit(solution)/shard_map/ppermute | solution.py:59
  34.5 0.9 %collective-permute-start.14 = (bf16[124,704]{0,1:T(8,128)(2,1)S(1)}, bf16[124,704]{0,1:T(8,128)(2,1)S(1)}, u32[]{:S(2)}, u32[]{:S(2)}) collective-permute-start(bf16[124,704]{0,1:T(8,128)(2,1)S(1)} %slice.437), channel_id=1, source_target_pairs={{0,3},{1,2},{2,1},{3,0},{4,7},{5,6},{6,5},{7,4},{8,11},{9,10},{10,... | collective-permute-start | bytes 523784 | tf_op jit(solution)/shard_map/ppermute | solution.py:59
  35.5 0.8 convert_multiply_fusion.3
  37.8 2.3 %collective-permute-done.11 = bf16[128,704]{0,1:T(8,128)(2,1)S(1)} collective-permute-done((bf16[128,704]{0,1:T(8,128)(2,1)S(1)}, bf16[128,704]{0,1:T(8,128)(2,1)S(1)}, u32[]{:S(2)}, u32[]{:S(2)}) %collective-permute-start.11) | collective-permute-done | bytes 180256 | tf_op jit(solution)/shard_map/ppermute | solution.py:59
  40.1 1.7 %collective-permute-start.13 = (bf16[7,1,7,128]{3,2,1,0:T(8,128)(2,1)S(1)}, bf16[7,1,7,128]{3,2,1,0:T(8,128)(2,1)S(1)}, u32[]{:S(2)}, u32[]{:S(2)}) collective-permute-start(bf16[7,1,7,128]{3,2,1,0:T(8,128)(2,1)S(1)} %broadcast_select_fusion.35), channel_id=1, source_target_pairs={{0,13},{1,12},{2,15},{3,14},{4,9},{5,8},{6,11},{7,10},{8,5},{9,4},... | collective-permute-start | bytes 37640 | tf_op jit(solution)/shard_map/ppermute | solution.py:41
  41.9 2.4 %collective-permute-done.13 = bf16[7,1,7,128]{3,2,1,0:T(8,128)(2,1)S(1)} collective-permute-done((bf16[7,1,7,128]{3,2,1,0:T(8,128)(2,1)S(1)}, bf16[7,1,7,128]{3,2,1,0:T(8,128)(2,1)S(1)}, u32[]{:S(2)}, u32[]{:S(2)}) %collective-permute-start.13) | collective-permute-done | bytes 12576 | tf_op jit(solution)/shard_map/ppermute | solution.py:41
  44.2 0.8 collective-permute-done.12
  46.5 2.8 %collective-permute-done.15 = bf16[1,7,7,128]{3,2,1,0:T(8,128)(2,1)S(1)} collective-permute-done((bf16[1,7,7,128]{3,2,1,0:T(8,128)(2,1)S(1)}, bf16[1,7,7,128]{3,2,1,0:T(8,128)(2,1)S(1)}, u32[]{:S(2)}, u32[]{:S(2)}) %collective-permute-start.15) | collective-permute-done | bytes 12576 | tf_op jit(solution)/shard_map/ppermute | solution.py:41
  51.5 1.1 %collective-permute-start.18 = (bf16[7,1,7,128]{3,2,1,0:T(8,128)(2,1)S(1)}, bf16[7,1,7,128]{3,2,1,0:T(8,128)(2,1)S(1)}, u32[]{:S(2)}, u32[]{:S(2)}) collective-permute-start(bf16[7,1,7,128]{3,2,1,0:T(8,128)(2,1)S(1)} %slice.690), channel_id=1, source_target_pairs={{0,13},{1,12},{2,15},{3,14},{4,9},{5,8},{6,11},{7,10},{8,5},{9,4},... | collective-permute-start | bytes 37640 | tf_op jit(solution)/shard_map/ppermute | solution.py:41
  52.6 1.3 %collective-permute-start.17 = (bf16[7,1,7,128]{3,2,1,0:T(8,128)(2,1)S(1)}, bf16[7,1,7,128]{3,2,1,0:T(8,128)(2,1)S(1)}, u32[]{:S(2)}, u32[]{:S(2)}) collective-permute-start(bf16[7,1,7,128]{3,2,1,0:T(8,128)(2,1)S(1)} %slice.690), channel_id=1, source_target_pairs={{0,5},{1,4},{2,7},{3,6},{4,1},{5,0},{6,3},{7,2},{8,13},{9,12},{10,... | collective-permute-start | bytes 37640 | tf_op jit(solution)/shard_map/ppermute | solution.py:41
  53.9 1.8 %collective-permute-done.18 = bf16[7,1,7,128]{3,2,1,0:T(8,128)(2,1)S(1)} collective-permute-done((bf16[7,1,7,128]{3,2,1,0:T(8,128)(2,1)S(1)}, bf16[7,1,7,128]{3,2,1,0:T(8,128)(2,1)S(1)}, u32[]{:S(2)}, u32[]{:S(2)}) %collective-permute-start.18) | collective-permute-done | bytes 12576 | tf_op jit(solution)/shard_map/ppermute | solution.py:41
  55.9 0.8 copy-done.1
  57.3 1.2 %convolution_add_fusion.3 = f32[704,128]{1,0:T(8,128)S(1)} fusion(f32[704,128]{1,0:T(8,128)S(1)} %fusion.97, bf16[252,128]{1,0:T(8,128)(2,1)S(1)} %select_n.600, bf16[2,252,704]{1,2,0:T(8,128)(2,1)} %collective-permute-done.16), kind=kOutput, calls=%fused_computation.10 | convolution fusion | flops 45506560 | bytes 1145856 | tf_op jit(solution)/shard_map/dot_general | solution.py:293
  58.6 1.2 %convolution_add_fusion.2 = f32[704,128]{1,0:T(8,128)S(1)} fusion(f32[704,128]{1,0:T(8,128)S(1)} %convolution_add_fusion.3, bf16[252,128]{1,0:T(8,128)(2,1)S(1)} %select_n.602, bf16[2,252,704]{1,2,0:T(8,128)(2,1)} %collective-permute-done.16), kind=kOutput, calls=%fused_computation.9 | convolution fusion | flops 45506560 | bytes 1145856 | tf_op jit(solution)/shard_map/dot_general | solution.py:293
  60.6 0.8 collective-permute-start.19
  61.4 5.0 %collective-permute-done.19 = bf16[212,128]{1,0:T(8,128)(2,1)S(1)} collective-permute-done((bf16[212,128]{1,0:T(8,128)(2,1)S(1)}, bf16[212,128]{1,0:T(8,128)(2,1)S(1)}, u32[]{:S(2)}, u32[]{:S(2)}) %collective-permute-start.19) | collective-permute-done | bytes 54304 | tf_op jit(solution)/shard_map/ppermute | solution.py:59
  66.8 1.1 %collective-permute-start.20 = (bf16[176,128]{1,0:T(8,128)(2,1)S(1)}, bf16[176,128]{1,0:T(8,128)(2,1)S(1)}, u32[]{:S(2)}, u32[]{:S(2)}) collective-permute-start(bf16[176,128]{1,0:T(8,128)(2,1)S(1)} %add_convert_fusion.2), channel_id=1, source_target_pairs={{0,5},{1,4},{2,7},{3,6},{4,1},{5,0},{6,3},{7,2},{8,13},{9,12},{10,... | collective-permute-start | bytes 135176 | tf_op jit(solution)/shard_map/ppermute | solution.py:41
  67.9 2.5 %collective-permute-done.20 = bf16[176,128]{1,0:T(8,128)(2,1)S(1)} collective-permute-done((bf16[176,128]{1,0:T(8,128)(2,1)S(1)}, bf16[176,128]{1,0:T(8,128)(2,1)S(1)}, u32[]{:S(2)}, u32[]{:S(2)}) %collective-permute-start.20) | collective-permute-done | bytes 45088 | tf_op jit(solution)/shard_map/ppermute | solution.py:41
  71.2 3.9 %collective-permute-done.21 = bf16[176,128]{1,0:T(8,128)(2,1)S(1)} collective-permute-done((bf16[176,128]{1,0:T(8,128)(2,1)S(1)}, bf16[176,128]{1,0:T(8,128)(2,1)S(1)}, u32[]{:S(2)}, u32[]{:S(2)}) %collective-permute-start.21) | collective-permute-done | bytes 45088 | tf_op jit(solution)/shard_map/ppermute | solution.py:41
  75.7 3.8 %collective-permute-done.22 = bf16[284,128]{1,0:T(8,128)(2,1)S(1)} collective-permute-done((bf16[284,128]{1,0:T(8,128)(2,1)S(1)}, bf16[284,128]{1,0:T(8,128)(2,1)S(1)}, u32[]{:S(2)}, u32[]{:S(2)}) %collective-permute-start.22) | collective-permute-done | bytes 72736 | tf_op jit(solution)/shard_map/ppermute | solution.py:59
  80.0 1.2 %collective-permute-done.23 = bf16[460,128]{1,0:T(8,128)(2,1)S(1)} collective-permute-done((bf16[460,128]{1,0:T(8,128)(2,1)S(1)}, bf16[460,128]{1,0:T(8,128)(2,1)S(1)}, u32[]{:S(2)}, u32[]{:S(2)}) %collective-permute-start.23) | collective-permute-done | bytes 117792 | tf_op jit(solution)/shard_map/ppermute | solution.py:59
  81.9 0.9 %fusion.9 = f32[176,512]{1,0:T(8,128)S(1)} fusion(s32[512]{0:T(512)S(1)} %copy-done.7, s32[512]{0:T(512)S(1)} %get-tuple-element.141, s32[]{:T(128)S(6)} %add.289, s32[512]{0:T(512)S(1)} %get-tuple-element.140, s32[512]{0:T(512)S(1)} %get-tuple-element.144, s32[512]{0:T(512)S(1)} %copy-done.6, s32[512]{0:T(512)S(1)} %get-tuple-element.145, ...), kind=kOutput, calls=%fused_computation.25 | convolution fusion | flops 98238464 | bytes 554500 | tf_op jit(solution)/shard_map/dot_general | solution.py:342
  (194 shorter events, 20.5 us)
Async XLA Ops:
  0.6 5.5 %copy-start = (bf16[1,343,343]{2,1,0:T(8,128)(2,1)S(1)}, bf16[1,343,343]{2,1,0:T(8,128)(2,1)}, u32[]{:S(2)}) copy-start(bf16[1,343,343]{2,1,0:T(8,128)(2,1)} %param.6) | copy-start | bytes 705898
  1.5 4.6 %copy-start.8 = (s32[1,343]{1,0:T(1,128)S(1)}, s32[1,343]{1,0:T(1,128)}, u32[]{:S(2)}) copy-start(s32[1,343]{1,0:T(1,128)} %param.7) | copy-start | bytes 4120
  1.5 4.6 %copy-start.9 = (f32[343]{0:T(512)S(1)}, f32[343]{0:T(512)}, u32[]{:S(2)}) copy-start(f32[343]{0:T(512)} %param.8) | copy-start | bytes 4120
  1.6 8.2 %collective-permute-start.1 = (bf16[6,1,6,128]{3,2,1,0:T(8,128)(2,1)S(1)}, bf16[6,1,6,128]{3,2,1,0:T(8,128)(2,1)S(1)}, u32[]{:S(2)}, u32[]{:S(2)}) collective-permute-start(bf16[6,1,6,128]{3,2,1,0:T(8,128)(2,1)S(1)} %slice.496), channel_id=1, source_target_pairs={{0,12},{1,13},{2,14},{3,15},{4,8},{5,9},{6,10},{7,11},{8,4},{9,5},... | collective-permute-start | bytes 27656 | tf_op jit(solution)/shard_map/ppermute | solution.py:41
  5.6 4.2 %collective-permute-start = (bf16[6,1,6,128]{3,2,1,0:T(8,128)(2,1)S(1)}, bf16[6,1,6,128]{3,2,1,0:T(8,128)(2,1)S(1)}, u32[]{:S(2)}, u32[]{:S(2)}) collective-permute-start(bf16[6,1,6,128]{3,2,1,0:T(8,128)(2,1)S(1)} %slice.496), channel_id=1, source_target_pairs={{0,4},{1,5},{2,6},{3,7},{4,0},{5,1},{6,2},{7,3},{8,12},{9,13},{10,... | collective-permute-start | bytes 27656 | tf_op jit(solution)/shard_map/ppermute | solution.py:41
  6.2 2.4 %copy-start.2 = (bf16[216,704]{1,0:T(8,128)(2,1)S(1)}, bf16[216,704]{1,0:T(8,128)(2,1)}, u32[]{:S(2)}) copy-start(bf16[216,704]{1,0:T(8,128)(2,1)} %param.9) | copy-start | bytes 912388
  6.9 14.4 %collective-permute-start.4 = (bf16[343,343]{1,0:T(8,128)(2,1)S(1)}, bf16[343,343]{1,0:T(8,128)(2,1)S(1)}, u32[]{:S(2)}, u32[]{:S(2)}) collective-permute-start(bf16[343,343]{1,0:T(8,128)(2,1)S(1)} %fusion), channel_id=1, source_target_pairs={{0,3},{1,2},{2,1},{3,0},{4,7},{5,6},{6,5},{7,4},{8,11},{9,10},{10,... | collective-permute-start | bytes 705902 | tf_op jit(solution)/shard_map/ppermute | solution.py:59
  7.3 17.4 %collective-permute-start.7 = (bf16[343,343]{1,0:T(8,128)(2,1)S(1)}, bf16[343,343]{1,0:T(8,128)(2,1)S(1)}, u32[]{:S(2)}, u32[]{:S(2)}) collective-permute-start(bf16[343,343]{1,0:T(8,128)(2,1)S(1)} %fusion), channel_id=1, source_target_pairs={{0,1},{1,0},{2,3},{3,2},{4,5},{5,4},{6,7},{7,6},{8,9},{9,8},{10,11... | collective-permute-start | bytes 705902 | tf_op jit(solution)/shard_map/ppermute | solution.py:59
  10.3 6.3 %collective-permute-start.2 = (bf16[258,128]{1,0:T(8,128)(2,1)S(1)}, bf16[258,128]{1,0:T(8,128)(2,1)S(1)}, u32[]{:S(2)}, u32[]{:S(2)}) collective-permute-start(bf16[258,128]{1,0:T(8,128)(2,1)S(1)} %concatenate.135), channel_id=1, source_target_pairs={{0,16},{1,17},{2,18},{3,19},{4,20},{5,21},{6,22},{7,23},{8,24},{9,... | collective-permute-start | bytes 198152 | tf_op jit(solution)/shard_map/ppermute | solution.py:41
  17.2 3.8 %collective-permute-start.3 = (bf16[152,128]{1,0:T(8,128)(2,1)S(1)}, bf16[152,128]{1,0:T(8,128)(2,1)S(1)}, u32[]{:S(2)}, u32[]{:S(2)}) collective-permute-start(bf16[152,128]{1,0:T(8,128)(2,1)S(1)} %pad_maximum_fusion.18), channel_id=1, source_target_pairs={{0,3},{1,2},{2,1},{3,0},{4,7},{5,6},{6,5},{7,4},{8,11},{9,10},{10,... | collective-permute-start | bytes 116744 | tf_op jit(solution)/shard_map/ppermute | solution.py:59
  21.3 1.3 %collective-permute-start.5 = (bf16[152,128]{1,0:T(8,128)(2,1)S(1)}, bf16[152,128]{1,0:T(8,128)(2,1)S(1)}, u32[]{:S(2)}, u32[]{:S(2)}) collective-permute-start(bf16[152,128]{1,0:T(8,128)(2,1)S(1)} %pad_maximum_fusion.19), channel_id=1, source_target_pairs={{0,1},{1,0},{2,3},{3,2},{4,5},{5,4},{6,7},{7,6},{8,9},{9,8},{10,11... | collective-permute-start | bytes 116744 | tf_op jit(solution)/shard_map/ppermute | solution.py:59
  21.7 1.6 %collective-permute-start.6 = (bf16[343,343]{1,0:T(8,128)(2,1)S(1)}, bf16[343,343]{1,0:T(8,128)(2,1)S(1)}, u32[]{:S(2)}, u32[]{:S(2)}) collective-permute-start(bf16[343,343]{1,0:T(8,128)(2,1)S(1)} %collective-permute-done.4), channel_id=1, source_target_pairs={{0,1},{1,0},{2,3},{3,2},{4,5},{5,4},{6,7},{7,6},{8,9},{9,8},{10,11... | collective-permute-start | bytes 705902 | tf_op jit(solution)/shard_map/ppermute | solution.py:59
  25.6 4.1 %collective-permute-start.9 = (bf16[7,1,7,128]{3,2,1,0:T(8,128)(2,1)S(1)}, bf16[7,1,7,128]{3,2,1,0:T(8,128)(2,1)S(1)}, u32[]{:S(2)}, u32[]{:S(2)}) collective-permute-start(bf16[7,1,7,128]{3,2,1,0:T(8,128)(2,1)S(1)} %broadcast_select_fusion.36), channel_id=1, source_target_pairs={{0,13},{1,12},{2,15},{3,14},{4,9},{5,8},{6,11},{7,10},{8,5},{9,4},... | collective-permute-start | bytes 37640 | tf_op jit(solution)/shard_map/ppermute | solution.py:41
  26.3 3.5 %collective-permute-start.8 = (bf16[7,1,7,128]{3,2,1,0:T(8,128)(2,1)S(1)}, bf16[7,1,7,128]{3,2,1,0:T(8,128)(2,1)S(1)}, u32[]{:S(2)}, u32[]{:S(2)}) collective-permute-start(bf16[7,1,7,128]{3,2,1,0:T(8,128)(2,1)S(1)} %get-tuple-element.47), channel_id=1, source_target_pairs={{0,5},{1,4},{2,7},{3,6},{4,1},{5,0},{6,3},{7,2},{8,13},{9,12},{10,... | collective-permute-start | bytes 37640 | tf_op jit(solution)/shard_map/ppermute | solution.py:41
  29.8 5.6 %collective-permute-start.10 = (bf16[1,7,7,128]{3,2,1,0:T(8,128)(2,1)S(1)}, bf16[1,7,7,128]{3,2,1,0:T(8,128)(2,1)S(1)}, u32[]{:S(2)}, u32[]{:S(2)}) collective-permute-start(bf16[1,7,7,128]{3,2,1,0:T(8,128)(2,1)S(1)} %fusion.115), channel_id=1, source_target_pairs={{0,17},{1,16},{2,19},{3,18},{4,21},{5,20},{6,23},{7,22},{8,25},{9,... | collective-permute-start | bytes 37640 | tf_op jit(solution)/shard_map/ppermute | solution.py:41
  33.6 2.7 %copy-start.5 = (pred[343]{0:T(512)(128)(4,1)}, pred[343]{0:T(512)(128)(4,1)S(1)}, u32[]{:S(2)}) copy-start(pred[343]{0:T(512)(128)(4,1)S(1)} %iota.91) | copy-start | bytes 1033
  33.6 6.5 %collective-permute-start.11 = (bf16[128,704]{0,1:T(8,128)(2,1)S(1)}, bf16[128,704]{0,1:T(8,128)(2,1)S(1)}, u32[]{:S(2)}, u32[]{:S(2)}) collective-permute-start(bf16[128,704]{0,1:T(8,128)(2,1)S(1)} %slice.433), channel_id=1, source_target_pairs={{0,3},{1,2},{2,1},{3,0},{4,7},{5,6},{6,5},{7,4},{8,11},{9,10},{10,... | collective-permute-start | bytes 540680 | tf_op jit(solution)/shard_map/ppermute | solution.py:59
  34.5 10.6 %collective-permute-start.14 = (bf16[124,704]{0,1:T(8,128)(2,1)S(1)}, bf16[124,704]{0,1:T(8,128)(2,1)S(1)}, u32[]{:S(2)}, u32[]{:S(2)}) collective-permute-start(bf16[124,704]{0,1:T(8,128)(2,1)S(1)} %slice.437), channel_id=1, source_target_pairs={{0,3},{1,2},{2,1},{3,0},{4,7},{5,6},{6,5},{7,4},{8,11},{9,10},{10,... | collective-permute-start | bytes 523784 | tf_op jit(solution)/shard_map/ppermute | solution.py:59
  40.1 4.1 %collective-permute-start.13 = (bf16[7,1,7,128]{3,2,1,0:T(8,128)(2,1)S(1)}, bf16[7,1,7,128]{3,2,1,0:T(8,128)(2,1)S(1)}, u32[]{:S(2)}, u32[]{:S(2)}) collective-permute-start(bf16[7,1,7,128]{3,2,1,0:T(8,128)(2,1)S(1)} %broadcast_select_fusion.35), channel_id=1, source_target_pairs={{0,13},{1,12},{2,15},{3,14},{4,9},{5,8},{6,11},{7,10},{8,5},{9,4},... | collective-permute-start | bytes 37640 | tf_op jit(solution)/shard_map/ppermute | solution.py:41
  41.8 3.2 %collective-permute-start.12 = (bf16[7,1,7,128]{3,2,1,0:T(8,128)(2,1)S(1)}, bf16[7,1,7,128]{3,2,1,0:T(8,128)(2,1)S(1)}, u32[]{:S(2)}, u32[]{:S(2)}) collective-permute-start(bf16[7,1,7,128]{3,2,1,0:T(8,128)(2,1)S(1)} %get-tuple-element.43), channel_id=1, source_target_pairs={{0,5},{1,4},{2,7},{3,6},{4,1},{5,0},{6,3},{7,2},{8,13},{9,12},{10,... | collective-permute-start | bytes 37640 | tf_op jit(solution)/shard_map/ppermute | solution.py:41
  45.1 4.1 %collective-permute-start.15 = (bf16[1,7,7,128]{3,2,1,0:T(8,128)(2,1)S(1)}, bf16[1,7,7,128]{3,2,1,0:T(8,128)(2,1)S(1)}, u32[]{:S(2)}, u32[]{:S(2)}) collective-permute-start(bf16[1,7,7,128]{3,2,1,0:T(8,128)(2,1)S(1)} %fusion.116), channel_id=1, source_target_pairs={{0,17},{1,16},{2,19},{3,18},{4,21},{5,20},{6,23},{7,22},{8,25},{9,... | collective-permute-start | bytes 37640 | tf_op jit(solution)/shard_map/ppermute | solution.py:41
  46.0 5.5 %collective-permute-start.16 = (bf16[2,252,704]{1,2,0:T(8,128)(2,1)S(1)}, bf16[2,252,704]{1,2,0:T(8,128)(2,1)}, u32[]{:S(2)}, u32[]{:S(2)}) collective-permute-start(bf16[2,252,704]{1,2,0:T(8,128)(2,1)S(1)} %pad_maximum_fusion), channel_id=1, source_target_pairs={{0,1},{1,0},{2,3},{3,2},{4,5},{5,4},{6,7},{7,6},{8,9},{9,8},{10,11... | collective-permute-start | bytes 2128904 | tf_op jit(solution)/shard_map/ppermute | solution.py:59
  51.5 4.1 %collective-permute-start.18 = (bf16[7,1,7,128]{3,2,1,0:T(8,128)(2,1)S(1)}, bf16[7,1,7,128]{3,2,1,0:T(8,128)(2,1)S(1)}, u32[]{:S(2)}, u32[]{:S(2)}) collective-permute-start(bf16[7,1,7,128]{3,2,1,0:T(8,128)(2,1)S(1)} %slice.690), channel_id=1, source_target_pairs={{0,13},{1,12},{2,15},{3,14},{4,9},{5,8},{6,11},{7,10},{8,5},{9,4},... | collective-permute-start | bytes 37640 | tf_op jit(solution)/shard_map/ppermute | solution.py:41
  52.6 3.2 %collective-permute-start.17 = (bf16[7,1,7,128]{3,2,1,0:T(8,128)(2,1)S(1)}, bf16[7,1,7,128]{3,2,1,0:T(8,128)(2,1)S(1)}, u32[]{:S(2)}, u32[]{:S(2)}) collective-permute-start(bf16[7,1,7,128]{3,2,1,0:T(8,128)(2,1)S(1)} %slice.690), channel_id=1, source_target_pairs={{0,5},{1,4},{2,7},{3,6},{4,1},{5,0},{6,3},{7,2},{8,13},{9,12},{10,... | collective-permute-start | bytes 37640 | tf_op jit(solution)/shard_map/ppermute | solution.py:41
  55.8 1.0 %copy-start.3 = (bf16[7,7,7,128]{3,2,1,0:T(8,128)(2,1)S(1)}, bf16[7,7,7,128]{3,2,1,0:T(8,128)(2,1)}, u32[]{:S(2)}) copy-start(bf16[7,7,7,128]{3,2,1,0:T(8,128)(2,1)} %get-tuple-element.40) | copy-start | bytes 263428
  55.9 0.9 %copy-start.4 = (pred[7,7,7,128]{3,2,1,0:T(8,128)(4,1)S(1)}, pred[7,7,7,128]{3,2,1,0:T(8,128)(4,1)}, u32[]{:S(2)}) copy-start(pred[7,7,7,128]{3,2,1,0:T(8,128)(4,1)} %not_and_fusion) | copy-start | bytes 131716
  60.6 5.9 %collective-permute-start.19 = (bf16[212,128]{1,0:T(8,128)(2,1)S(1)}, bf16[212,128]{1,0:T(8,128)(2,1)S(1)}, u32[]{:S(2)}, u32[]{:S(2)}) collective-permute-start(bf16[212,128]{1,0:T(8,128)(2,1)S(1)} %pad_maximum_fusion.13), channel_id=1, source_target_pairs={{0,17},{1,16},{2,19},{3,18},{4,21},{5,20},{6,23},{7,22},{8,25},{9,... | collective-permute-start | bytes 162824 | tf_op jit(solution)/shard_map/ppermute | solution.py:59
  66.8 3.7 %collective-permute-start.20 = (bf16[176,128]{1,0:T(8,128)(2,1)S(1)}, bf16[176,128]{1,0:T(8,128)(2,1)S(1)}, u32[]{:S(2)}, u32[]{:S(2)}) collective-permute-start(bf16[176,128]{1,0:T(8,128)(2,1)S(1)} %add_convert_fusion.2), channel_id=1, source_target_pairs={{0,5},{1,4},{2,7},{3,6},{4,1},{5,0},{6,3},{7,2},{8,13},{9,12},{10,... | collective-permute-start | bytes 135176 | tf_op jit(solution)/shard_map/ppermute | solution.py:41
  70.4 4.6 %collective-permute-start.21 = (bf16[176,128]{1,0:T(8,128)(2,1)S(1)}, bf16[176,128]{1,0:T(8,128)(2,1)S(1)}, u32[]{:S(2)}, u32[]{:S(2)}) collective-permute-start(bf16[176,128]{1,0:T(8,128)(2,1)S(1)} %add_convert_fusion.1), channel_id=1, source_target_pairs={{0,13},{1,12},{2,15},{3,14},{4,9},{5,8},{6,11},{7,10},{8,5},{9,4},... | collective-permute-start | bytes 135176 | tf_op jit(solution)/shard_map/ppermute | solution.py:41
  75.2 4.3 %collective-permute-start.22 = (bf16[284,128]{1,0:T(8,128)(2,1)S(1)}, bf16[284,128]{1,0:T(8,128)(2,1)S(1)}, u32[]{:S(2)}, u32[]{:S(2)}) collective-permute-start(bf16[284,128]{1,0:T(8,128)(2,1)S(1)} %maximum_maximum_fusion.2), channel_id=1, source_target_pairs={{0,3},{1,2},{2,1},{3,0},{4,7},{5,6},{6,5},{7,4},{8,11},{9,10},{10,... | collective-permute-start | bytes 218120 | tf_op jit(solution)/shard_map/ppermute | solution.py:59
  79.7 1.5 %copy-start.7 = (s32[512]{0:T(512)S(1)}, s32[512]{0:T(512)}, u32[]{:S(2)}) copy-start(s32[512]{0:T(512)} %get-tuple-element.139) | copy-start | bytes 6148
  79.8 1.4 %collective-permute-start.23 = (bf16[460,128]{1,0:T(8,128)(2,1)S(1)}, bf16[460,128]{1,0:T(8,128)(2,1)S(1)}, u32[]{:S(2)}, u32[]{:S(2)}) collective-permute-start(bf16[460,128]{1,0:T(8,128)(2,1)S(1)} %maximum_maximum_fusion), channel_id=1, source_target_pairs={{0,1},{1,0},{2,3},{3,2},{4,5},{5,4},{6,7},{7,6},{8,9},{9,8},{10,11... | collective-permute-start | bytes 353288 | tf_op jit(solution)/shard_map/ppermute | solution.py:59
  (2 other events, 1.6 us)

commit v11 on v10

--- a/solution.py
+++ b/solution.py
@@ -226,12 +226,6 @@
     lane_owner = lax.broadcasted_iota(jnp.int32, (1, columns), 1) // width
     owner_near = lane_owner ^ grid.coords[2]
 
-    inside = jnp.ones(shape, jnp.bool_)
-    first = (grid.coords[0] == 0, grid.coords[1] == 0, lane_owner.reshape(1, 1, 1, columns) == 0)
-    for dim in range(3):
-        at = lax.broadcasted_iota(jnp.int32, shape, dim)
-        inside = inside & ~((at == 0) & first[dim])
-
     older = field
     current = field
     steps = len(chebyshev_coeffs)
@@ -248,7 +242,7 @@
         partial = with_ends(
             partial,
             2,
-            low + to_next_partition(high, width),
+            jnp.where(lane_owner > 0, low + to_next_partition(high, width), 0.0),
             high + to_previous_partition(low, width),
         )
         if step == steps - 1:
@@ -264,13 +258,13 @@
             partial = with_ends(
                 partial,
                 dim,
-                low + to_low.astype(jnp.float32),
+                jnp.where(grid.coords[dim] > 0, low + to_low.astype(jnp.float32), 0.0),
                 high + to_high.astype(jnp.float32),
             )
         following = coeffs[0] * (partial - centre * current.astype(jnp.float32)) - coeffs[
             1
         ] * older.astype(jnp.float32)
-        following = rounded(jnp.where(inside, following, 0.0))
+        following = rounded(following)
         older = current
         current = following
     other_locked = jnp.concatenate(other_parts, axis=0)
@@ -332,15 +326,14 @@
     others = arrived[: 2 * deep].reshape(held.shape)
     came = unpacked(arrived[2 * deep :], width)
     filtered = jnp.concatenate(placed([own[0], came[0], own[1], came[1]], high, low), axis=1)
-    held = jnp.concatenate([held[0], others[0], held[1], others[1]], axis=1)
-    size = (GRID_Z * columns, GRID_Z * columns)
-    to, at = lax.broadcasted_iota(jnp.int32, size, 1), lax.broadcasted_iota(jnp.int32, size, 0)
-    base = jnp.where(high, 2, 0) + jnp.where(low, 1, 0)
-    goal = (
-        (at // width % GRID_Z) * columns + ((at // columns) ^ base) * width + at % width
-    )
-    spread = jnp.dot(held, (goal == to).astype(jnp.bfloat16), preferred_element_type=jnp.float32)
-    intersection = jnp.concatenate(split(spread, GRID_Z), axis=0)
+    held = placed([held[0], others[0], held[1], others[1]], high, low)
+    intersection = jnp.concatenate(
+        [
+            jnp.concatenate([h[:, q * width : (q + 1) * width] for h in held], axis=1)
+            for q in range(GRID_Z)
+        ],
+        axis=0,
+    ).astype(jnp.float32)
     return filtered, intersection
 
 

time: 84.8 us -> 80.8 us (0.953)
  other arithmetic: 8.71 us -> 6.61 us
  waiting for transfers between devices: 37 us -> 35.4 us
  starting transfers between devices: 24.4 us -> 25.8 us
  matrix products: 7.49 us -> 6.61 us
    ppermute x11, waiting for transfers between devices: 16.6 us -> 15.6 us  [partner(): lax.ppermute(value, AXIS, [(i, i ^ bits) for i in range(self.devices)])]
    convert_element_type x0 -> x1, other arithmetic: none -> 0.98 us  [per_device(): intersection = jnp.concatenate([jnp.concatenate([h[:, q * width:(q + 1) *...]
    dot_general x1 -> x0, matrix products: 0.86 us -> none  [per_device(): jnp.dot(held, (goal == to).astype(jnp.bfloat16), preferred_element_type=j...]
    unnamed x27 -> x19, local copies, waits for them, and re-layouts: 1.85 us -> 1.19 us
  transfers between devices with their start and end apart: 24 -> 24, of which waited for: 16 -> 17; matrix products, arithmetic and copies ran while one was open for 13% -> 10% of each run, Pallas kernels for 0% -> 0%
where the time goes in v11:
time: 80.8 us; the launch traced here: 80.6 us
  waiting for transfers between devices  35.4 us (44%)
  starting transfers between devices  25.8 us (32%)
  other arithmetic  6.61 us (8%)
  matrix products  6.61 us (8%)
  local copies, waits for them, and re-layouts  4.56 us (6%)
  between operations  1.69 us (2%)
    ppermute x13, waiting for transfers between devices, swapped(): arrived = lax.ppermute(jnp.where(lower, high, low), AXIS, pairs)  19.8 us
    ppermute x13, starting transfers between devices, swapped(): arrived = lax.ppermute(jnp.where(lower, high, low), AXIS, pairs)  18.8 us
    ppermute x11, waiting for transfers between devices, partner(): lax.ppermute(value, AXIS, [(i, i ^ bits) for i in range(self.devices)])  15.6 us
    ppermute x11, starting transfers between devices, partner(): lax.ppermute(value, AXIS, [(i, i ^ bits) for i in range(self.devices)])  6.97 us
    dot_general x4, matrix products, per_device(): lax.dot_general(all_locked[r], jnp.where(owner_near == r, weights, jnp.ze...  2.96 us
    dot_general x12, matrix products, per_device(): jnp.dot(matrices[r], own, preferred_element_type=jnp.float32)  2.93 us
  transfers between devices with their start and end apart: 24, of which 17 were waited for; matrix products, arithmetic and copies ran while one was open for 10% of the time, Pallas kernels for 0%

profile of v11, /device:TPU:0, one launch (start us, length us, event | category | flops | bytes accessed | tf_op | source)
XLA Modules:
  0.0 80.6 jit_solution(12536483132067398816)
XLA Ops:
  0.6 0.9 %reshape.172 = bf16[6,6,6,128]{3,2,1,0:T(8,128)(2,1)S(1)} reshape(bf16[216,128]{1,0:T(8,128)(2,1)} %param.5) | data formatting | bytes 110592 | tf_op jit(solution)/shard_map/reshape | solution.py:193
  1.6 4.0 %collective-permute-start.1 = (bf16[6,1,6,128]{3,2,1,0:T(8,128)(2,1)S(1)}, bf16[6,1,6,128]{3,2,1,0:T(8,128)(2,1)S(1)}, u32[]{:S(2)}, u32[]{:S(2)}) collective-permute-start(bf16[6,1,6,128]{3,2,1,0:T(8,128)(2,1)S(1)} %slice.544), channel_id=1, source_target_pairs={{0,12},{1,13},{2,14},{3,15},{4,8},{5,9},{6,10},{7,11},{8,4},{9,5},... | collective-permute-start | bytes 27656 | tf_op jit(solution)/shard_map/ppermute | solution.py:41
  7.3 1.2 %collective-permute-start.7 = (bf16[343,343]{1,0:T(8,128)(2,1)S(1)}, bf16[343,343]{1,0:T(8,128)(2,1)S(1)}, u32[]{:S(2)}, u32[]{:S(2)}) collective-permute-start(bf16[343,343]{1,0:T(8,128)(2,1)S(1)} %fusion), channel_id=1, source_target_pairs={{0,1},{1,0},{2,3},{3,2},{4,5},{5,4},{6,7},{7,6},{8,9},{9,8},{10,11... | collective-permute-start | bytes 705902 | tf_op jit(solution)/shard_map/ppermute | solution.py:59
  9.8 2.7 %collective-permute-start.2 = (bf16[258,128]{1,0:T(8,128)(2,1)S(1)}, bf16[258,128]{1,0:T(8,128)(2,1)S(1)}, u32[]{:S(2)}, u32[]{:S(2)}) collective-permute-start(bf16[258,128]{1,0:T(8,128)(2,1)S(1)} %concatenate.144), channel_id=1, source_target_pairs={{0,16},{1,17},{2,18},{3,19},{4,20},{5,21},{6,22},{7,23},{8,24},{9,... | collective-permute-start | bytes 198152 | tf_op jit(solution)/shard_map/ppermute | solution.py:41
  12.4 3.4 %collective-permute-done.2 = bf16[258,128]{1,0:T(8,128)(2,1)S(1)} collective-permute-done((bf16[258,128]{1,0:T(8,128)(2,1)S(1)}, bf16[258,128]{1,0:T(8,128)(2,1)S(1)}, u32[]{:S(2)}, u32[]{:S(2)}) %collective-permute-start.2) | collective-permute-done | bytes 66080 | tf_op jit(solution)/shard_map/ppermute | solution.py:41
  16.7 3.4 %collective-permute-done.3 = bf16[152,128]{1,0:T(8,128)(2,1)S(1)} collective-permute-done((bf16[152,128]{1,0:T(8,128)(2,1)S(1)}, bf16[152,128]{1,0:T(8,128)(2,1)S(1)}, u32[]{:S(2)}, u32[]{:S(2)}) %collective-permute-start.3) | collective-permute-done | bytes 38944 | tf_op jit(solution)/shard_map/ppermute | solution.py:59
  22.5 0.8 fusion.101
  24.7 0.8 %collective-permute-start.9 = (bf16[7,1,7,128]{3,2,1,0:T(8,128)(2,1)S(1)}, bf16[7,1,7,128]{3,2,1,0:T(8,128)(2,1)S(1)}, u32[]{:S(2)}, u32[]{:S(2)}) collective-permute-start(bf16[7,1,7,128]{3,2,1,0:T(8,128)(2,1)S(1)} %broadcast_select_fusion.47), channel_id=1, source_target_pairs={{0,13},{1,12},{2,15},{3,14},{4,9},{5,8},{6,11},{7,10},{8,5},{9,4},... | collective-permute-start | bytes 37640 | tf_op jit(solution)/shard_map/ppermute | solution.py:41
  25.5 1.0 %collective-permute-start.8 = (bf16[7,1,7,128]{3,2,1,0:T(8,128)(2,1)S(1)}, bf16[7,1,7,128]{3,2,1,0:T(8,128)(2,1)S(1)}, u32[]{:S(2)}, u32[]{:S(2)}) collective-permute-start(bf16[7,1,7,128]{3,2,1,0:T(8,128)(2,1)S(1)} %get-tuple-element.47), channel_id=1, source_target_pairs={{0,5},{1,4},{2,7},{3,6},{4,1},{5,0},{6,3},{7,2},{8,13},{9,12},{10,... | collective-permute-start | bytes 37640 | tf_op jit(solution)/shard_map/ppermute | solution.py:41
  26.5 2.4 %collective-permute-done.9 = bf16[7,1,7,128]{3,2,1,0:T(8,128)(2,1)S(1)} collective-permute-done((bf16[7,1,7,128]{3,2,1,0:T(8,128)(2,1)S(1)}, bf16[7,1,7,128]{3,2,1,0:T(8,128)(2,1)S(1)}, u32[]{:S(2)}, u32[]{:S(2)}) %collective-permute-start.9) | collective-permute-done | bytes 12576 | tf_op jit(solution)/shard_map/ppermute | solution.py:41
  28.9 3.0 %collective-permute-start.10 = (bf16[1,7,7,128]{3,2,1,0:T(8,128)(2,1)S(1)}, bf16[1,7,7,128]{3,2,1,0:T(8,128)(2,1)S(1)}, u32[]{:S(2)}, u32[]{:S(2)}) collective-permute-start(bf16[1,7,7,128]{3,2,1,0:T(8,128)(2,1)S(1)} %fusion.83), channel_id=1, source_target_pairs={{0,17},{1,16},{2,19},{3,18},{4,21},{5,20},{6,23},{7,22},{8,25},{9,... | collective-permute-start | bytes 37640 | tf_op jit(solution)/shard_map/ppermute | solution.py:41
  31.9 1.0 %collective-permute-start.11 = (bf16[128,704]{0,1:T(8,128)(2,1)S(1)}, bf16[128,704]{0,1:T(8,128)(2,1)S(1)}, u32[]{:S(2)}, u32[]{:S(2)}) collective-permute-start(bf16[128,704]{0,1:T(8,128)(2,1)S(1)} %slice.469), channel_id=1, source_target_pairs={{0,3},{1,2},{2,1},{3,0},{4,7},{5,6},{6,5},{7,4},{8,11},{9,10},{10,... | collective-permute-start | bytes 540680 | tf_op jit(solution)/shard_map/ppermute | solution.py:59
  35.9 2.5 %collective-permute-done.11 = bf16[128,704]{0,1:T(8,128)(2,1)S(1)} collective-permute-done((bf16[128,704]{0,1:T(8,128)(2,1)S(1)}, bf16[128,704]{0,1:T(8,128)(2,1)S(1)}, u32[]{:S(2)}, u32[]{:S(2)}) %collective-permute-start.11) | collective-permute-done | bytes 180256 | tf_op jit(solution)/shard_map/ppermute | solution.py:59
  38.4 1.7 %collective-permute-start.13 = (bf16[7,1,7,128]{3,2,1,0:T(8,128)(2,1)S(1)}, bf16[7,1,7,128]{3,2,1,0:T(8,128)(2,1)S(1)}, u32[]{:S(2)}, u32[]{:S(2)}) collective-permute-start(bf16[7,1,7,128]{3,2,1,0:T(8,128)(2,1)S(1)} %broadcast_select_fusion.46), channel_id=1, source_target_pairs={{0,13},{1,12},{2,15},{3,14},{4,9},{5,8},{6,11},{7,10},{8,5},{9,4},... | collective-permute-start | bytes 37640 | tf_op jit(solution)/shard_map/ppermute | solution.py:41
  40.2 2.3 %collective-permute-done.13 = bf16[7,1,7,128]{3,2,1,0:T(8,128)(2,1)S(1)} collective-permute-done((bf16[7,1,7,128]{3,2,1,0:T(8,128)(2,1)S(1)}, bf16[7,1,7,128]{3,2,1,0:T(8,128)(2,1)S(1)}, u32[]{:S(2)}, u32[]{:S(2)}) %collective-permute-start.13) | collective-permute-done | bytes 12576 | tf_op jit(solution)/shard_map/ppermute | solution.py:41
  42.5 0.8 %collective-permute-done.12 = bf16[7,1,7,128]{3,2,1,0:T(8,128)(2,1)S(1)} collective-permute-done((bf16[7,1,7,128]{3,2,1,0:T(8,128)(2,1)S(1)}, bf16[7,1,7,128]{3,2,1,0:T(8,128)(2,1)S(1)}, u32[]{:S(2)}, u32[]{:S(2)}) %collective-permute-start.12) | collective-permute-done | bytes 12576 | tf_op jit(solution)/shard_map/ppermute | solution.py:41
  44.6 3.0 %collective-permute-done.15 = bf16[1,7,7,128]{3,2,1,0:T(8,128)(2,1)S(1)} collective-permute-done((bf16[1,7,7,128]{3,2,1,0:T(8,128)(2,1)S(1)}, bf16[1,7,7,128]{3,2,1,0:T(8,128)(2,1)S(1)}, u32[]{:S(2)}, u32[]{:S(2)}) %collective-permute-start.15) | collective-permute-done | bytes 12576 | tf_op jit(solution)/shard_map/ppermute | solution.py:41
  49.1 1.1 %collective-permute-start.18 = (bf16[7,1,7,128]{3,2,1,0:T(8,128)(2,1)S(1)}, bf16[7,1,7,128]{3,2,1,0:T(8,128)(2,1)S(1)}, u32[]{:S(2)}, u32[]{:S(2)}) collective-permute-start(bf16[7,1,7,128]{3,2,1,0:T(8,128)(2,1)S(1)} %slice.782), channel_id=1, source_target_pairs={{0,13},{1,12},{2,15},{3,14},{4,9},{5,8},{6,11},{7,10},{8,5},{9,4},... | collective-permute-start | bytes 37640 | tf_op jit(solution)/shard_map/ppermute | solution.py:41
  50.2 1.3 %collective-permute-start.17 = (bf16[7,1,7,128]{3,2,1,0:T(8,128)(2,1)S(1)}, bf16[7,1,7,128]{3,2,1,0:T(8,128)(2,1)S(1)}, u32[]{:S(2)}, u32[]{:S(2)}) collective-permute-start(bf16[7,1,7,128]{3,2,1,0:T(8,128)(2,1)S(1)} %slice.782), channel_id=1, source_target_pairs={{0,5},{1,4},{2,7},{3,6},{4,1},{5,0},{6,3},{7,2},{8,13},{9,12},{10,... | collective-permute-start | bytes 37640 | tf_op jit(solution)/shard_map/ppermute | solution.py:41
  51.5 1.7 %collective-permute-done.18 = bf16[7,1,7,128]{3,2,1,0:T(8,128)(2,1)S(1)} collective-permute-done((bf16[7,1,7,128]{3,2,1,0:T(8,128)(2,1)S(1)}, bf16[7,1,7,128]{3,2,1,0:T(8,128)(2,1)S(1)}, u32[]{:S(2)}, u32[]{:S(2)}) %collective-permute-start.18) | collective-permute-done | bytes 12576 | tf_op jit(solution)/shard_map/ppermute | solution.py:41
  53.5 0.8 %copy-done.1 = f32[7,7,7,128]{3,2,1,0:T(8,128)S(1)} copy-done((f32[7,7,7,128]{3,2,1,0:T(8,128)S(1)}, f32[7,7,7,128]{3,2,1,0:T(8,128)}, u32[]{:S(2)}) %copy-start.1) | copy-done | bytes 175640
  54.9 1.2 %convolution_add_fusion.3 = f32[704,128]{1,0:T(8,128)S(1)} fusion(f32[704,128]{1,0:T(8,128)S(1)} %fusion.65, bf16[252,128]{1,0:T(8,128)(2,1)S(1)} %select_n.631, bf16[2,252,704]{1,2,0:T(8,128)(2,1)} %collective-permute-done.16), kind=kOutput, calls=%fused_computation.5 | convolution fusion | flops 45506560 | bytes 1145856 | tf_op jit(solution)/shard_map/dot_general | solution.py:287
  56.2 1.2 %convolution_add_fusion.2 = f32[704,128]{1,0:T(8,128)S(1)} fusion(f32[704,128]{1,0:T(8,128)S(1)} %convolution_add_fusion.3, bf16[252,128]{1,0:T(8,128)(2,1)S(1)} %select_n.633, bf16[2,252,704]{1,2,0:T(8,128)(2,1)} %collective-permute-done.16), kind=kOutput, calls=%fused_computation.4 | convolution fusion | flops 45506560 | bytes 1145856 | tf_op jit(solution)/shard_map/dot_general | solution.py:287
  59.0 4.9 %collective-permute-done.19 = bf16[212,128]{1,0:T(8,128)(2,1)S(1)} collective-permute-done((bf16[212,128]{1,0:T(8,128)(2,1)S(1)}, bf16[212,128]{1,0:T(8,128)(2,1)S(1)}, u32[]{:S(2)}, u32[]{:S(2)}) %collective-permute-start.19) | collective-permute-done | bytes 54304 | tf_op jit(solution)/shard_map/ppermute | solution.py:59
  64.2 1.3 %collective-permute-start.20 = (bf16[176,128]{1,0:T(8,128)(2,1)S(1)}, bf16[176,128]{1,0:T(8,128)(2,1)S(1)}, u32[]{:S(2)}, u32[]{:S(2)}) collective-permute-start(bf16[176,128]{1,0:T(8,128)(2,1)S(1)} %add_convert_fusion.2), channel_id=1, source_target_pairs={{0,5},{1,4},{2,7},{3,6},{4,1},{5,0},{6,3},{7,2},{8,13},{9,12},{10,... | collective-permute-start | bytes 135176 | tf_op jit(solution)/shard_map/ppermute | solution.py:41
  65.5 2.2 %collective-permute-done.20 = bf16[176,128]{1,0:T(8,128)(2,1)S(1)} collective-permute-done((bf16[176,128]{1,0:T(8,128)(2,1)S(1)}, bf16[176,128]{1,0:T(8,128)(2,1)S(1)}, u32[]{:S(2)}, u32[]{:S(2)}) %collective-permute-start.20) | collective-permute-done | bytes 45088 | tf_op jit(solution)/shard_map/ppermute | solution.py:41
  67.8 1.0 %collective-permute-start.21 = (bf16[176,128]{1,0:T(8,128)(2,1)S(1)}, bf16[176,128]{1,0:T(8,128)(2,1)S(1)}, u32[]{:S(2)}, u32[]{:S(2)}) collective-permute-start(bf16[176,128]{1,0:T(8,128)(2,1)S(1)} %add_convert_fusion.1), channel_id=1, source_target_pairs={{0,13},{1,12},{2,15},{3,14},{4,9},{5,8},{6,11},{7,10},{8,5},{9,4},... | collective-permute-start | bytes 135176 | tf_op jit(solution)/shard_map/ppermute | solution.py:41
  68.8 3.5 %collective-permute-done.21 = bf16[176,128]{1,0:T(8,128)(2,1)S(1)} collective-permute-done((bf16[176,128]{1,0:T(8,128)(2,1)S(1)}, bf16[176,128]{1,0:T(8,128)(2,1)S(1)}, u32[]{:S(2)}, u32[]{:S(2)}) %collective-permute-start.21) | collective-permute-done | bytes 45088 | tf_op jit(solution)/shard_map/ppermute | solution.py:41
  72.4 1.2 %collective-permute-start.22 = (bf16[284,128]{1,0:T(8,128)(2,1)S(1)}, bf16[284,128]{1,0:T(8,128)(2,1)S(1)}, u32[]{:S(2)}, u32[]{:S(2)}) collective-permute-start(bf16[284,128]{1,0:T(8,128)(2,1)S(1)} %maximum_maximum_fusion.2), channel_id=1, source_target_pairs={{0,3},{1,2},{2,1},{3,0},{4,7},{5,6},{6,5},{7,4},{8,11},{9,10},{10,... | collective-permute-start | bytes 218120 | tf_op jit(solution)/shard_map/ppermute | solution.py:59
  73.5 3.0 %collective-permute-done.22 = bf16[284,128]{1,0:T(8,128)(2,1)S(1)} collective-permute-done((bf16[284,128]{1,0:T(8,128)(2,1)S(1)}, bf16[284,128]{1,0:T(8,128)(2,1)S(1)}, u32[]{:S(2)}, u32[]{:S(2)}) %collective-permute-start.22) | collective-permute-done | bytes 72736 | tf_op jit(solution)/shard_map/ppermute | solution.py:59
  77.1 1.0 %collective-permute-done.23 = bf16[460,128]{1,0:T(8,128)(2,1)S(1)} collective-permute-done((bf16[460,128]{1,0:T(8,128)(2,1)S(1)}, bf16[460,128]{1,0:T(8,128)(2,1)S(1)}, u32[]{:S(2)}, u32[]{:S(2)}) %collective-permute-start.23) | collective-permute-done | bytes 117792 | tf_op jit(solution)/shard_map/ppermute | solution.py:59
  79.6 1.0 %maximum_convert_fusion = f32[704,128]{1,0:T(8,128)} fusion(bf16[176,32]{1,0:T(8,128)(2,1)S(1)} %get-tuple-element.131, bf16[176,32]{1,0:T(8,128)(2,1)S(1)} %get-tuple-element.127, bf16[176,32]{1,0:T(8,128)(2,1)S(1)} %get-tuple-element.123, bf16[176,32]{1,0:T(8,128)(2,1)S(1)} %get-tuple-element.119, bf16[176,32]{1,0:T(8,128)(2,1)S(1)} %get-tuple-element.132, ...), kind=kLoop, calls=%fused_computation.49 | loop fusion | flops 2883584 | bytes 540672 | tf_op jit(solution)/shard_map/convert_element_type | solution.py:336
  (175 shorter events, 17.5 us)
Async XLA Ops:
  0.6 5.5 %copy-start = (bf16[1,343,343]{2,1,0:T(8,128)(2,1)S(1)}, bf16[1,343,343]{2,1,0:T(8,128)(2,1)}, u32[]{:S(2)}) copy-start(bf16[1,343,343]{2,1,0:T(8,128)(2,1)} %param.6) | copy-start | bytes 705898
  1.5 4.6 %copy-start.4 = (s32[1,343]{1,0:T(1,128)S(1)}, s32[1,343]{1,0:T(1,128)}, u32[]{:S(2)}) copy-start(s32[1,343]{1,0:T(1,128)} %param.7) | copy-start | bytes 4120
  1.5 4.6 %copy-start.5 = (f32[343]{0:T(512)S(1)}, f32[343]{0:T(512)}, u32[]{:S(2)}) copy-start(f32[343]{0:T(512)} %param.8) | copy-start | bytes 4120
  1.6 7.4 %collective-permute-start.1 = (bf16[6,1,6,128]{3,2,1,0:T(8,128)(2,1)S(1)}, bf16[6,1,6,128]{3,2,1,0:T(8,128)(2,1)S(1)}, u32[]{:S(2)}, u32[]{:S(2)}) collective-permute-start(bf16[6,1,6,128]{3,2,1,0:T(8,128)(2,1)S(1)} %slice.544), channel_id=1, source_target_pairs={{0,12},{1,13},{2,14},{3,15},{4,8},{5,9},{6,10},{7,11},{8,4},{9,5},... | collective-permute-start | bytes 27656 | tf_op jit(solution)/shard_map/ppermute | solution.py:41
  5.6 3.7 %collective-permute-start = (bf16[6,1,6,128]{3,2,1,0:T(8,128)(2,1)S(1)}, bf16[6,1,6,128]{3,2,1,0:T(8,128)(2,1)S(1)}, u32[]{:S(2)}, u32[]{:S(2)}) collective-permute-start(bf16[6,1,6,128]{3,2,1,0:T(8,128)(2,1)S(1)} %slice.544), channel_id=1, source_target_pairs={{0,4},{1,5},{2,6},{3,7},{4,0},{5,1},{6,2},{7,3},{8,12},{9,13},{10,... | collective-permute-start | bytes 27656 | tf_op jit(solution)/shard_map/ppermute | solution.py:41
  6.2 2.4 %copy-start.2 = (bf16[216,704]{1,0:T(8,128)(2,1)S(1)}, bf16[216,704]{1,0:T(8,128)(2,1)}, u32[]{:S(2)}) copy-start(bf16[216,704]{1,0:T(8,128)(2,1)} %param.9) | copy-start | bytes 912388
  6.9 13.5 %collective-permute-start.4 = (bf16[343,343]{1,0:T(8,128)(2,1)S(1)}, bf16[343,343]{1,0:T(8,128)(2,1)S(1)}, u32[]{:S(2)}, u32[]{:S(2)}) collective-permute-start(bf16[343,343]{1,0:T(8,128)(2,1)S(1)} %fusion), channel_id=1, source_target_pairs={{0,3},{1,2},{2,1},{3,0},{4,7},{5,6},{6,5},{7,4},{8,11},{9,10},{10,... | collective-permute-start | bytes 705902 | tf_op jit(solution)/shard_map/ppermute | solution.py:59
  7.3 16.5 %collective-permute-start.7 = (bf16[343,343]{1,0:T(8,128)(2,1)S(1)}, bf16[343,343]{1,0:T(8,128)(2,1)S(1)}, u32[]{:S(2)}, u32[]{:S(2)}) collective-permute-start(bf16[343,343]{1,0:T(8,128)(2,1)S(1)} %fusion), channel_id=1, source_target_pairs={{0,1},{1,0},{2,3},{3,2},{4,5},{5,4},{6,7},{7,6},{8,9},{9,8},{10,11... | collective-permute-start | bytes 705902 | tf_op jit(solution)/shard_map/ppermute | solution.py:59
  9.8 6.1 %collective-permute-start.2 = (bf16[258,128]{1,0:T(8,128)(2,1)S(1)}, bf16[258,128]{1,0:T(8,128)(2,1)S(1)}, u32[]{:S(2)}, u32[]{:S(2)}) collective-permute-start(bf16[258,128]{1,0:T(8,128)(2,1)S(1)} %concatenate.144), channel_id=1, source_target_pairs={{0,16},{1,17},{2,18},{3,19},{4,20},{5,21},{6,22},{7,23},{8,24},{9,... | collective-permute-start | bytes 198152 | tf_op jit(solution)/shard_map/ppermute | solution.py:41
  16.4 3.7 %collective-permute-start.3 = (bf16[152,128]{1,0:T(8,128)(2,1)S(1)}, bf16[152,128]{1,0:T(8,128)(2,1)S(1)}, u32[]{:S(2)}, u32[]{:S(2)}) collective-permute-start(bf16[152,128]{1,0:T(8,128)(2,1)S(1)} %pad_maximum_fusion.17), channel_id=1, source_target_pairs={{0,3},{1,2},{2,1},{3,0},{4,7},{5,6},{6,5},{7,4},{8,11},{9,10},{10,... | collective-permute-start | bytes 116744 | tf_op jit(solution)/shard_map/ppermute | solution.py:59
  20.4 1.3 %collective-permute-start.5 = (bf16[152,128]{1,0:T(8,128)(2,1)S(1)}, bf16[152,128]{1,0:T(8,128)(2,1)S(1)}, u32[]{:S(2)}, u32[]{:S(2)}) collective-permute-start(bf16[152,128]{1,0:T(8,128)(2,1)S(1)} %pad_maximum_fusion.18), channel_id=1, source_target_pairs={{0,1},{1,0},{2,3},{3,2},{4,5},{5,4},{6,7},{7,6},{8,9},{9,8},{10,11... | collective-permute-start | bytes 116744 | tf_op jit(solution)/shard_map/ppermute | solution.py:59
  20.7 1.7 %collective-permute-start.6 = (bf16[343,343]{1,0:T(8,128)(2,1)S(1)}, bf16[343,343]{1,0:T(8,128)(2,1)S(1)}, u32[]{:S(2)}, u32[]{:S(2)}) collective-permute-start(bf16[343,343]{1,0:T(8,128)(2,1)S(1)} %collective-permute-done.4), channel_id=1, source_target_pairs={{0,1},{1,0},{2,3},{3,2},{4,5},{5,4},{6,7},{7,6},{8,9},{9,8},{10,11... | collective-permute-start | bytes 705902 | tf_op jit(solution)/shard_map/ppermute | solution.py:59
  24.7 4.1 %collective-permute-start.9 = (bf16[7,1,7,128]{3,2,1,0:T(8,128)(2,1)S(1)}, bf16[7,1,7,128]{3,2,1,0:T(8,128)(2,1)S(1)}, u32[]{:S(2)}, u32[]{:S(2)}) collective-permute-start(bf16[7,1,7,128]{3,2,1,0:T(8,128)(2,1)S(1)} %broadcast_select_fusion.47), channel_id=1, source_target_pairs={{0,13},{1,12},{2,15},{3,14},{4,9},{5,8},{6,11},{7,10},{8,5},{9,4},... | collective-permute-start | bytes 37640 | tf_op jit(solution)/shard_map/ppermute | solution.py:41
  25.5 3.3 %collective-permute-start.8 = (bf16[7,1,7,128]{3,2,1,0:T(8,128)(2,1)S(1)}, bf16[7,1,7,128]{3,2,1,0:T(8,128)(2,1)S(1)}, u32[]{:S(2)}, u32[]{:S(2)}) collective-permute-start(bf16[7,1,7,128]{3,2,1,0:T(8,128)(2,1)S(1)} %get-tuple-element.47), channel_id=1, source_target_pairs={{0,5},{1,4},{2,7},{3,6},{4,1},{5,0},{6,3},{7,2},{8,13},{9,12},{10,... | collective-permute-start | bytes 37640 | tf_op jit(solution)/shard_map/ppermute | solution.py:41
  28.9 4.9 %collective-permute-start.10 = (bf16[1,7,7,128]{3,2,1,0:T(8,128)(2,1)S(1)}, bf16[1,7,7,128]{3,2,1,0:T(8,128)(2,1)S(1)}, u32[]{:S(2)}, u32[]{:S(2)}) collective-permute-start(bf16[1,7,7,128]{3,2,1,0:T(8,128)(2,1)S(1)} %fusion.83), channel_id=1, source_target_pairs={{0,17},{1,16},{2,19},{3,18},{4,21},{5,20},{6,23},{7,22},{8,25},{9,... | collective-permute-start | bytes 37640 | tf_op jit(solution)/shard_map/ppermute | solution.py:41
  31.9 6.4 %collective-permute-start.11 = (bf16[128,704]{0,1:T(8,128)(2,1)S(1)}, bf16[128,704]{0,1:T(8,128)(2,1)S(1)}, u32[]{:S(2)}, u32[]{:S(2)}) collective-permute-start(bf16[128,704]{0,1:T(8,128)(2,1)S(1)} %slice.469), channel_id=1, source_target_pairs={{0,3},{1,2},{2,1},{3,0},{4,7},{5,6},{6,5},{7,4},{8,11},{9,10},{10,... | collective-permute-start | bytes 540680 | tf_op jit(solution)/shard_map/ppermute | solution.py:59
  33.0 10.5 %collective-permute-start.14 = (bf16[124,704]{0,1:T(8,128)(2,1)S(1)}, bf16[124,704]{0,1:T(8,128)(2,1)S(1)}, u32[]{:S(2)}, u32[]{:S(2)}) collective-permute-start(bf16[124,704]{0,1:T(8,128)(2,1)S(1)} %slice.473), channel_id=1, source_target_pairs={{0,3},{1,2},{2,1},{3,0},{4,7},{5,6},{6,5},{7,4},{8,11},{9,10},{10,... | collective-permute-start | bytes 523784 | tf_op jit(solution)/shard_map/ppermute | solution.py:59
  38.4 4.1 %collective-permute-start.13 = (bf16[7,1,7,128]{3,2,1,0:T(8,128)(2,1)S(1)}, bf16[7,1,7,128]{3,2,1,0:T(8,128)(2,1)S(1)}, u32[]{:S(2)}, u32[]{:S(2)}) collective-permute-start(bf16[7,1,7,128]{3,2,1,0:T(8,128)(2,1)S(1)} %broadcast_select_fusion.46), channel_id=1, source_target_pairs={{0,13},{1,12},{2,15},{3,14},{4,9},{5,8},{6,11},{7,10},{8,5},{9,4},... | collective-permute-start | bytes 37640 | tf_op jit(solution)/shard_map/ppermute | solution.py:41
  40.2 3.2 %collective-permute-start.12 = (bf16[7,1,7,128]{3,2,1,0:T(8,128)(2,1)S(1)}, bf16[7,1,7,128]{3,2,1,0:T(8,128)(2,1)S(1)}, u32[]{:S(2)}, u32[]{:S(2)}) collective-permute-start(bf16[7,1,7,128]{3,2,1,0:T(8,128)(2,1)S(1)} %get-tuple-element.43), channel_id=1, source_target_pairs={{0,5},{1,4},{2,7},{3,6},{4,1},{5,0},{6,3},{7,2},{8,13},{9,12},{10,... | collective-permute-start | bytes 37640 | tf_op jit(solution)/shard_map/ppermute | solution.py:41
  43.5 4.1 %collective-permute-start.15 = (bf16[1,7,7,128]{3,2,1,0:T(8,128)(2,1)S(1)}, bf16[1,7,7,128]{3,2,1,0:T(8,128)(2,1)S(1)}, u32[]{:S(2)}, u32[]{:S(2)}) collective-permute-start(bf16[1,7,7,128]{3,2,1,0:T(8,128)(2,1)S(1)} %fusion.84), channel_id=1, source_target_pairs={{0,17},{1,16},{2,19},{3,18},{4,21},{5,20},{6,23},{7,22},{8,25},{9,... | collective-permute-start | bytes 37640 | tf_op jit(solution)/shard_map/ppermute | solution.py:41
  44.2 5.0 %collective-permute-start.16 = (bf16[2,252,704]{1,2,0:T(8,128)(2,1)S(1)}, bf16[2,252,704]{1,2,0:T(8,128)(2,1)}, u32[]{:S(2)}, u32[]{:S(2)}) collective-permute-start(bf16[2,252,704]{1,2,0:T(8,128)(2,1)S(1)} %pad_maximum_fusion), channel_id=1, source_target_pairs={{0,1},{1,0},{2,3},{3,2},{4,5},{5,4},{6,7},{7,6},{8,9},{9,8},{10,11... | collective-permute-start | bytes 2128904 | tf_op jit(solution)/shard_map/ppermute | solution.py:59
  49.1 4.1 %collective-permute-start.18 = (bf16[7,1,7,128]{3,2,1,0:T(8,128)(2,1)S(1)}, bf16[7,1,7,128]{3,2,1,0:T(8,128)(2,1)S(1)}, u32[]{:S(2)}, u32[]{:S(2)}) collective-permute-start(bf16[7,1,7,128]{3,2,1,0:T(8,128)(2,1)S(1)} %slice.782), channel_id=1, source_target_pairs={{0,13},{1,12},{2,15},{3,14},{4,9},{5,8},{6,11},{7,10},{8,5},{9,4},... | collective-permute-start | bytes 37640 | tf_op jit(solution)/shard_map/ppermute | solution.py:41
  50.2 3.2 %collective-permute-start.17 = (bf16[7,1,7,128]{3,2,1,0:T(8,128)(2,1)S(1)}, bf16[7,1,7,128]{3,2,1,0:T(8,128)(2,1)S(1)}, u32[]{:S(2)}, u32[]{:S(2)}) collective-permute-start(bf16[7,1,7,128]{3,2,1,0:T(8,128)(2,1)S(1)} %slice.782), channel_id=1, source_target_pairs={{0,5},{1,4},{2,7},{3,6},{4,1},{5,0},{6,3},{7,2},{8,13},{9,12},{10,... | collective-permute-start | bytes 37640 | tf_op jit(solution)/shard_map/ppermute | solution.py:41
  53.4 0.9 %copy-start.1 = (f32[7,7,7,128]{3,2,1,0:T(8,128)S(1)}, f32[7,7,7,128]{3,2,1,0:T(8,128)}, u32[]{:S(2)}) copy-start(f32[7,7,7,128]{3,2,1,0:T(8,128)} %get-tuple-element.41) | copy-start | bytes 526852
  53.4 1.0 %copy-start.3 = (bf16[7,7,7,128]{3,2,1,0:T(8,128)(2,1)S(1)}, bf16[7,7,7,128]{3,2,1,0:T(8,128)(2,1)}, u32[]{:S(2)}) copy-start(bf16[7,7,7,128]{3,2,1,0:T(8,128)(2,1)} %get-tuple-element.40) | copy-start | bytes 263428
  58.2 5.8 %collective-permute-start.19 = (bf16[212,128]{1,0:T(8,128)(2,1)S(1)}, bf16[212,128]{1,0:T(8,128)(2,1)S(1)}, u32[]{:S(2)}, u32[]{:S(2)}) collective-permute-start(bf16[212,128]{1,0:T(8,128)(2,1)S(1)} %pad_maximum_fusion.12), channel_id=1, source_target_pairs={{0,17},{1,16},{2,19},{3,18},{4,21},{5,20},{6,23},{7,22},{8,25},{9,... | collective-permute-start | bytes 162824 | tf_op jit(solution)/shard_map/ppermute | solution.py:59
  64.2 3.6 %collective-permute-start.20 = (bf16[176,128]{1,0:T(8,128)(2,1)S(1)}, bf16[176,128]{1,0:T(8,128)(2,1)S(1)}, u32[]{:S(2)}, u32[]{:S(2)}) collective-permute-start(bf16[176,128]{1,0:T(8,128)(2,1)S(1)} %add_convert_fusion.2), channel_id=1, source_target_pairs={{0,5},{1,4},{2,7},{3,6},{4,1},{5,0},{6,3},{7,2},{8,13},{9,12},{10,... | collective-permute-start | bytes 135176 | tf_op jit(solution)/shard_map/ppermute | solution.py:41
  67.8 4.4 %collective-permute-start.21 = (bf16[176,128]{1,0:T(8,128)(2,1)S(1)}, bf16[176,128]{1,0:T(8,128)(2,1)S(1)}, u32[]{:S(2)}, u32[]{:S(2)}) collective-permute-start(bf16[176,128]{1,0:T(8,128)(2,1)S(1)} %add_convert_fusion.1), channel_id=1, source_target_pairs={{0,13},{1,12},{2,15},{3,14},{4,9},{5,8},{6,11},{7,10},{8,5},{9,4},... | collective-permute-start | bytes 135176 | tf_op jit(solution)/shard_map/ppermute | solution.py:41
  72.4 4.2 %collective-permute-start.22 = (bf16[284,128]{1,0:T(8,128)(2,1)S(1)}, bf16[284,128]{1,0:T(8,128)(2,1)S(1)}, u32[]{:S(2)}, u32[]{:S(2)}) collective-permute-start(bf16[284,128]{1,0:T(8,128)(2,1)S(1)} %maximum_maximum_fusion.2), channel_id=1, source_target_pairs={{0,3},{1,2},{2,1},{3,0},{4,7},{5,6},{6,5},{7,4},{8,11},{9,10},{10,... | collective-permute-start | bytes 218120 | tf_op jit(solution)/shard_map/ppermute | solution.py:59
  76.7 1.4 %collective-permute-start.23 = (bf16[460,128]{1,0:T(8,128)(2,1)S(1)}, bf16[460,128]{1,0:T(8,128)(2,1)S(1)}, u32[]{:S(2)}, u32[]{:S(2)}) collective-permute-start(bf16[460,128]{1,0:T(8,128)(2,1)S(1)} %maximum_maximum_fusion), channel_id=1, source_target_pairs={{0,1},{1,0},{2,3},{3,2},{4,5},{5,4},{6,7},{7,6},{8,9},{9,8},{10,11... | collective-permute-start | bytes 353288 | tf_op jit(solution)/shard_map/ppermute | solution.py:59

commit v12 on v11

--- a/solution.py
+++ b/solution.py
@@ -226,8 +226,8 @@
     lane_owner = lax.broadcasted_iota(jnp.int32, (1, columns), 1) // width
     owner_near = lane_owner ^ grid.coords[2]
 
-    older = field
     current = field
+    older = lax.optimization_barrier(field)
     steps = len(chebyshev_coeffs)
     for step, coeffs in enumerate(chebyshev_coeffs):
         rows = current.reshape(slot_count, columns)
@@ -265,12 +265,11 @@
             1
         ] * older.astype(jnp.float32)
         following = rounded(following)
-        older = current
+        older = lax.optimization_barrier(current)
         current = following
     other_locked = jnp.concatenate(other_parts, axis=0)
     both_locked = grid.partner(jnp.stack([locked, other_locked]), SECOND)
     low = plane(partial, 1, 0).astype(jnp.bfloat16)
-    low, both_locked = lax.optimization_barrier((low, both_locked))
     all_locked = [locked, both_locked[0], both_locked[1], other_locked]
     to_high = grid.exchanged(low, low, 1)[1].astype(jnp.float32)
     partial = with_ends(partial, 1, None, plane(partial, 1, SIDE - 1) + to_high)

time: 80.8 us -> 79.2 us (0.980)
  other arithmetic: 6.61 us -> 5.25 us
  waiting for transfers between devices: 35.4 us -> 36.3 us
  local copies, waits for them, and re-layouts: 4.56 us -> 3.69 us
    convert_element_type x2 -> x0, other arithmetic: 1.49 us -> none  [per_device(): current.astype(jnp.float32)]
    unnamed x19 -> x15, local copies, waits for them, and re-layouts: 1.19 us -> 0.28 us
  transfers between devices with their start and end apart: 24 -> 24, of which waited for: 17 -> 17; matrix products, arithmetic and copies ran while one was open for 10% -> 8% of each run, Pallas kernels for 0% -> 0%
where the time goes in v12:
time: 79.2 us; the launch traced here: 79 us
  waiting for transfers between devices  36.3 us (46%)
  starting transfers between devices  25.4 us (32%)
  matrix products  6.62 us (8%)
  other arithmetic  5.25 us (7%)
  local copies, waits for them, and re-layouts  3.69 us (5%)
  between operations  1.68 us (2%)
    ppermute x13, waiting for transfers between devices, swapped(): arrived = lax.ppermute(jnp.where(lower, high, low), AXIS, pairs)  20.1 us
    ppermute x13, starting transfers between devices, swapped(): arrived = lax.ppermute(jnp.where(lower, high, low), AXIS, pairs)  18.8 us
    ppermute x11, waiting for transfers between devices, partner(): lax.ppermute(value, AXIS, [(i, i ^ bits) for i in range(self.devices)])  16.2 us
    ppermute x11, starting transfers between devices, partner(): lax.ppermute(value, AXIS, [(i, i ^ bits) for i in range(self.devices)])  6.66 us
    dot_general x4, matrix products, per_device(): lax.dot_general(all_locked[r], jnp.where(owner_near == r, weights, jnp.ze...  2.96 us
    dot_general x12, matrix products, per_device(): jnp.dot(matrices[r], own, preferred_element_type=jnp.float32)  2.93 us
  transfers between devices with their start and end apart: 24, of which 17 were waited for; matrix products, arithmetic and copies ran while one was open for 8% of the time, Pallas kernels for 0%

profile of v12, /device:TPU:0, one launch (start us, length us, event | category | flops | bytes accessed | tf_op | source)
XLA Modules:
  0.0 79.0 jit_solution(18074937000354064603)
XLA Ops:
  0.6 0.9 %reshape.171 = bf16[6,6,6,128]{3,2,1,0:T(8,128)(2,1)S(1)} reshape(bf16[216,128]{1,0:T(8,128)(2,1)} %param.5) | data formatting | bytes 110592 | tf_op jit(solution)/shard_map/reshape | solution.py:193
  1.6 4.0 %collective-permute-start.1 = (bf16[6,1,6,128]{3,2,1,0:T(8,128)(2,1)S(1)}, bf16[6,1,6,128]{3,2,1,0:T(8,128)(2,1)S(1)}, u32[]{:S(2)}, u32[]{:S(2)}) collective-permute-start(bf16[6,1,6,128]{3,2,1,0:T(8,128)(2,1)S(1)} %slice.544), channel_id=1, source_target_pairs={{0,12},{1,13},{2,14},{3,15},{4,8},{5,9},{6,10},{7,11},{8,4},{9,5},... | collective-permute-start | bytes 27656 | tf_op jit(solution)/shard_map/ppermute | solution.py:41
  7.3 1.2 %collective-permute-start.7 = (bf16[343,343]{1,0:T(8,128)(2,1)S(1)}, bf16[343,343]{1,0:T(8,128)(2,1)S(1)}, u32[]{:S(2)}, u32[]{:S(2)}) collective-permute-start(bf16[343,343]{1,0:T(8,128)(2,1)S(1)} %fusion), channel_id=1, source_target_pairs={{0,1},{1,0},{2,3},{3,2},{4,5},{5,4},{6,7},{7,6},{8,9},{9,8},{10,11... | collective-permute-start | bytes 705902 | tf_op jit(solution)/shard_map/ppermute | solution.py:59
  9.8 2.7 %collective-permute-start.2 = (bf16[258,128]{1,0:T(8,128)(2,1)S(1)}, bf16[258,128]{1,0:T(8,128)(2,1)S(1)}, u32[]{:S(2)}, u32[]{:S(2)}) collective-permute-start(bf16[258,128]{1,0:T(8,128)(2,1)S(1)} %concatenate.140), channel_id=1, source_target_pairs={{0,16},{1,17},{2,18},{3,19},{4,20},{5,21},{6,22},{7,23},{8,24},{9,... | collective-permute-start | bytes 198152 | tf_op jit(solution)/shard_map/ppermute | solution.py:41
  12.4 3.4 %collective-permute-done.2 = bf16[258,128]{1,0:T(8,128)(2,1)S(1)} collective-permute-done((bf16[258,128]{1,0:T(8,128)(2,1)S(1)}, bf16[258,128]{1,0:T(8,128)(2,1)S(1)}, u32[]{:S(2)}, u32[]{:S(2)}) %collective-permute-start.2) | collective-permute-done | bytes 66080 | tf_op jit(solution)/shard_map/ppermute | solution.py:41
  16.7 3.4 %collective-permute-done.3 = bf16[152,128]{1,0:T(8,128)(2,1)S(1)} collective-permute-done((bf16[152,128]{1,0:T(8,128)(2,1)S(1)}, bf16[152,128]{1,0:T(8,128)(2,1)S(1)}, u32[]{:S(2)}, u32[]{:S(2)}) %collective-permute-start.3) | collective-permute-done | bytes 38944 | tf_op jit(solution)/shard_map/ppermute | solution.py:59
  24.0 0.8 %collective-permute-start.9 = (bf16[7,1,7,128]{3,2,1,0:T(8,128)(2,1)S(1)}, bf16[7,1,7,128]{3,2,1,0:T(8,128)(2,1)S(1)}, u32[]{:S(2)}, u32[]{:S(2)}) collective-permute-start(bf16[7,1,7,128]{3,2,1,0:T(8,128)(2,1)S(1)} %broadcast_select_fusion.47), channel_id=1, source_target_pairs={{0,13},{1,12},{2,15},{3,14},{4,9},{5,8},{6,11},{7,10},{8,5},{9,4},... | collective-permute-start | bytes 37640 | tf_op jit(solution)/shard_map/ppermute | solution.py:41
  24.8 1.0 %collective-permute-start.8 = (bf16[7,1,7,128]{3,2,1,0:T(8,128)(2,1)S(1)}, bf16[7,1,7,128]{3,2,1,0:T(8,128)(2,1)S(1)}, u32[]{:S(2)}, u32[]{:S(2)}) collective-permute-start(bf16[7,1,7,128]{3,2,1,0:T(8,128)(2,1)S(1)} %get-tuple-element.39), channel_id=1, source_target_pairs={{0,5},{1,4},{2,7},{3,6},{4,1},{5,0},{6,3},{7,2},{8,13},{9,12},{10,... | collective-permute-start | bytes 37640 | tf_op jit(solution)/shard_map/ppermute | solution.py:41
  25.8 2.4 %collective-permute-done.9 = bf16[7,1,7,128]{3,2,1,0:T(8,128)(2,1)S(1)} collective-permute-done((bf16[7,1,7,128]{3,2,1,0:T(8,128)(2,1)S(1)}, bf16[7,1,7,128]{3,2,1,0:T(8,128)(2,1)S(1)}, u32[]{:S(2)}, u32[]{:S(2)}) %collective-permute-start.9) | collective-permute-done | bytes 12576 | tf_op jit(solution)/shard_map/ppermute | solution.py:41
  28.2 3.0 %collective-permute-start.10 = (bf16[1,7,7,128]{3,2,1,0:T(8,128)(2,1)S(1)}, bf16[1,7,7,128]{3,2,1,0:T(8,128)(2,1)S(1)}, u32[]{:S(2)}, u32[]{:S(2)}) collective-permute-start(bf16[1,7,7,128]{3,2,1,0:T(8,128)(2,1)S(1)} %fusion.77), channel_id=1, source_target_pairs={{0,17},{1,16},{2,19},{3,18},{4,21},{5,20},{6,23},{7,22},{8,25},{9,... | collective-permute-start | bytes 37640 | tf_op jit(solution)/shard_map/ppermute | solution.py:41
  31.3 1.0 %collective-permute-start.11 = (bf16[128,704]{0,1:T(8,128)(2,1)S(1)}, bf16[128,704]{0,1:T(8,128)(2,1)S(1)}, u32[]{:S(2)}, u32[]{:S(2)}) collective-permute-start(bf16[128,704]{0,1:T(8,128)(2,1)S(1)} %slice.469), channel_id=1, source_target_pairs={{0,3},{1,2},{2,1},{3,0},{4,7},{5,6},{6,5},{7,4},{8,11},{9,10},{10,... | collective-permute-start | bytes 540680 | tf_op jit(solution)/shard_map/ppermute | solution.py:59
  32.3 0.8 collective-permute-start.14
  34.6 3.1 %collective-permute-done.11 = bf16[128,704]{0,1:T(8,128)(2,1)S(1)} collective-permute-done((bf16[128,704]{0,1:T(8,128)(2,1)S(1)}, bf16[128,704]{0,1:T(8,128)(2,1)S(1)}, u32[]{:S(2)}, u32[]{:S(2)}) %collective-permute-start.11) | collective-permute-done | bytes 180256 | tf_op jit(solution)/shard_map/ppermute | solution.py:59
  37.7 1.7 %collective-permute-start.13 = (bf16[7,1,7,128]{3,2,1,0:T(8,128)(2,1)S(1)}, bf16[7,1,7,128]{3,2,1,0:T(8,128)(2,1)S(1)}, u32[]{:S(2)}, u32[]{:S(2)}) collective-permute-start(bf16[7,1,7,128]{3,2,1,0:T(8,128)(2,1)S(1)} %broadcast_select_fusion.46), channel_id=1, source_target_pairs={{0,13},{1,12},{2,15},{3,14},{4,9},{5,8},{6,11},{7,10},{8,5},{9,4},... | collective-permute-start | bytes 37640 | tf_op jit(solution)/shard_map/ppermute | solution.py:41
  39.5 2.3 %collective-permute-done.13 = bf16[7,1,7,128]{3,2,1,0:T(8,128)(2,1)S(1)} collective-permute-done((bf16[7,1,7,128]{3,2,1,0:T(8,128)(2,1)S(1)}, bf16[7,1,7,128]{3,2,1,0:T(8,128)(2,1)S(1)}, u32[]{:S(2)}, u32[]{:S(2)}) %collective-permute-start.13) | collective-permute-done | bytes 12576 | tf_op jit(solution)/shard_map/ppermute | solution.py:41
  41.8 0.8 %collective-permute-done.12 = bf16[7,1,7,128]{3,2,1,0:T(8,128)(2,1)S(1)} collective-permute-done((bf16[7,1,7,128]{3,2,1,0:T(8,128)(2,1)S(1)}, bf16[7,1,7,128]{3,2,1,0:T(8,128)(2,1)S(1)}, u32[]{:S(2)}, u32[]{:S(2)}) %collective-permute-start.12) | collective-permute-done | bytes 12576 | tf_op jit(solution)/shard_map/ppermute | solution.py:41
  43.3 3.6 %collective-permute-done.15 = bf16[1,7,7,128]{3,2,1,0:T(8,128)(2,1)S(1)} collective-permute-done((bf16[1,7,7,128]{3,2,1,0:T(8,128)(2,1)S(1)}, bf16[1,7,7,128]{3,2,1,0:T(8,128)(2,1)S(1)}, u32[]{:S(2)}, u32[]{:S(2)}) %collective-permute-start.15) | collective-permute-done | bytes 12576 | tf_op jit(solution)/shard_map/ppermute | solution.py:41
  48.4 1.1 %collective-permute-start.17 = (bf16[7,1,7,128]{3,2,1,0:T(8,128)(2,1)S(1)}, bf16[7,1,7,128]{3,2,1,0:T(8,128)(2,1)S(1)}, u32[]{:S(2)}, u32[]{:S(2)}) collective-permute-start(bf16[7,1,7,128]{3,2,1,0:T(8,128)(2,1)S(1)} %slice.758), channel_id=1, source_target_pairs={{0,13},{1,12},{2,15},{3,14},{4,9},{5,8},{6,11},{7,10},{8,5},{9,4},... | collective-permute-start | bytes 37640 | tf_op jit(solution)/shard_map/ppermute | solution.py:41
  49.5 1.3 %collective-permute-start.16 = (bf16[7,1,7,128]{3,2,1,0:T(8,128)(2,1)S(1)}, bf16[7,1,7,128]{3,2,1,0:T(8,128)(2,1)S(1)}, u32[]{:S(2)}, u32[]{:S(2)}) collective-permute-start(bf16[7,1,7,128]{3,2,1,0:T(8,128)(2,1)S(1)} %slice.758), channel_id=1, source_target_pairs={{0,5},{1,4},{2,7},{3,6},{4,1},{5,0},{6,3},{7,2},{8,13},{9,12},{10,... | collective-permute-start | bytes 37640 | tf_op jit(solution)/shard_map/ppermute | solution.py:41
  51.1 1.5 %collective-permute-done.17 = bf16[7,1,7,128]{3,2,1,0:T(8,128)(2,1)S(1)} collective-permute-done((bf16[7,1,7,128]{3,2,1,0:T(8,128)(2,1)S(1)}, bf16[7,1,7,128]{3,2,1,0:T(8,128)(2,1)S(1)}, u32[]{:S(2)}, u32[]{:S(2)}) %collective-permute-start.17) | collective-permute-done | bytes 12576 | tf_op jit(solution)/shard_map/ppermute | solution.py:41
  53.5 1.2 %convolution_add_fusion.2 = f32[704,128]{1,0:T(8,128)S(1)} fusion(f32[704,128]{1,0:T(8,128)S(1)} %fusion.59, bf16[252,128]{1,0:T(8,128)(2,1)S(1)} %select_n.631, bf16[2,252,704]{1,2,0:T(8,128)(2,1)} %collective-permute-done.18), kind=kOutput, calls=%fused_computation.5 | convolution fusion | flops 45506560 | bytes 1145856 | tf_op jit(solution)/shard_map/dot_general | solution.py:286
  54.8 1.2 %fusion.1 = f32[704,128]{1,0:T(8,128)S(1)} fusion(f32[704,128]{1,0:T(8,128)S(1)} %fusion.57, f32[704,128]{1,0:T(8,128)S(1)} %convolution_add_fusion.2, bf16[252,128]{1,0:T(8,128)(2,1)S(1)} %select_n.633, bf16[2,252,704]{1,2,0:T(8,128)(2,1)} %collective-permute-done.18), kind=kOutput, calls=%fused_computation.4 | convolution fusion | flops 45596672 | bytes 1506304 | tf_op jit(solution)/shard_map/dot_general | solution.py:286
  56.5 0.8 %collective-permute-start.19 = (bf16[212,128]{1,0:T(8,128)(2,1)S(1)}, bf16[212,128]{1,0:T(8,128)(2,1)S(1)}, u32[]{:S(2)}, u32[]{:S(2)}) collective-permute-start(bf16[212,128]{1,0:T(8,128)(2,1)S(1)} %pad_maximum_fusion.10), channel_id=1, source_target_pairs={{0,17},{1,16},{2,19},{3,18},{4,21},{5,20},{6,23},{7,22},{8,25},{9,... | collective-permute-start | bytes 162824 | tf_op jit(solution)/shard_map/ppermute | solution.py:59
  57.3 5.0 %collective-permute-done.19 = bf16[212,128]{1,0:T(8,128)(2,1)S(1)} collective-permute-done((bf16[212,128]{1,0:T(8,128)(2,1)S(1)}, bf16[212,128]{1,0:T(8,128)(2,1)S(1)}, u32[]{:S(2)}, u32[]{:S(2)}) %collective-permute-start.19) | collective-permute-done | bytes 54304 | tf_op jit(solution)/shard_map/ppermute | solution.py:59
  62.6 1.3 %collective-permute-start.20 = (bf16[176,128]{1,0:T(8,128)(2,1)S(1)}, bf16[176,128]{1,0:T(8,128)(2,1)S(1)}, u32[]{:S(2)}, u32[]{:S(2)}) collective-permute-start(bf16[176,128]{1,0:T(8,128)(2,1)S(1)} %add_convert_fusion.2), channel_id=1, source_target_pairs={{0,5},{1,4},{2,7},{3,6},{4,1},{5,0},{6,3},{7,2},{8,13},{9,12},{10,... | collective-permute-start | bytes 135176 | tf_op jit(solution)/shard_map/ppermute | solution.py:41
  63.9 2.2 %collective-permute-done.20 = bf16[176,128]{1,0:T(8,128)(2,1)S(1)} collective-permute-done((bf16[176,128]{1,0:T(8,128)(2,1)S(1)}, bf16[176,128]{1,0:T(8,128)(2,1)S(1)}, u32[]{:S(2)}, u32[]{:S(2)}) %collective-permute-start.20) | collective-permute-done | bytes 45088 | tf_op jit(solution)/shard_map/ppermute | solution.py:41
  66.1 1.0 %collective-permute-start.21 = (bf16[176,128]{1,0:T(8,128)(2,1)S(1)}, bf16[176,128]{1,0:T(8,128)(2,1)S(1)}, u32[]{:S(2)}, u32[]{:S(2)}) collective-permute-start(bf16[176,128]{1,0:T(8,128)(2,1)S(1)} %add_convert_fusion.1), channel_id=1, source_target_pairs={{0,13},{1,12},{2,15},{3,14},{4,9},{5,8},{6,11},{7,10},{8,5},{9,4},... | collective-permute-start | bytes 135176 | tf_op jit(solution)/shard_map/ppermute | solution.py:41
  67.1 3.4 %collective-permute-done.21 = bf16[176,128]{1,0:T(8,128)(2,1)S(1)} collective-permute-done((bf16[176,128]{1,0:T(8,128)(2,1)S(1)}, bf16[176,128]{1,0:T(8,128)(2,1)S(1)}, u32[]{:S(2)}, u32[]{:S(2)}) %collective-permute-start.21) | collective-permute-done | bytes 45088 | tf_op jit(solution)/shard_map/ppermute | solution.py:41
  70.7 1.2 %collective-permute-start.22 = (bf16[284,128]{1,0:T(8,128)(2,1)S(1)}, bf16[284,128]{1,0:T(8,128)(2,1)S(1)}, u32[]{:S(2)}, u32[]{:S(2)}) collective-permute-start(bf16[284,128]{1,0:T(8,128)(2,1)S(1)} %maximum_maximum_fusion.2), channel_id=1, source_target_pairs={{0,3},{1,2},{2,1},{3,0},{4,7},{5,6},{6,5},{7,4},{8,11},{9,10},{10,... | collective-permute-start | bytes 218120 | tf_op jit(solution)/shard_map/ppermute | solution.py:59
  71.9 2.9 %collective-permute-done.22 = bf16[284,128]{1,0:T(8,128)(2,1)S(1)} collective-permute-done((bf16[284,128]{1,0:T(8,128)(2,1)S(1)}, bf16[284,128]{1,0:T(8,128)(2,1)S(1)}, u32[]{:S(2)}, u32[]{:S(2)}) %collective-permute-start.22) | collective-permute-done | bytes 72736 | tf_op jit(solution)/shard_map/ppermute | solution.py:59
  75.4 1.1 %collective-permute-done.23 = bf16[460,128]{1,0:T(8,128)(2,1)S(1)} collective-permute-done((bf16[460,128]{1,0:T(8,128)(2,1)S(1)}, bf16[460,128]{1,0:T(8,128)(2,1)S(1)}, u32[]{:S(2)}, u32[]{:S(2)}) %collective-permute-start.23) | collective-permute-done | bytes 117792 | tf_op jit(solution)/shard_map/ppermute | solution.py:59
  78.0 1.0 %maximum_convert_fusion = f32[704,128]{1,0:T(8,128)} fusion(bf16[176,32]{1,0:T(8,128)(2,1)S(1)} %get-tuple-element.122, bf16[176,32]{1,0:T(8,128)(2,1)S(1)} %get-tuple-element.118, bf16[176,32]{1,0:T(8,128)(2,1)S(1)} %get-tuple-element.114, bf16[176,32]{1,0:T(8,128)(2,1)S(1)} %get-tuple-element.110, bf16[176,32]{1,0:T(8,128)(2,1)S(1)} %get-tuple-element.123, ...), kind=kLoop, calls=%fused_computation.53 | loop fusion | flops 2883584 | bytes 540672 | tf_op jit(solution)/shard_map/convert_element_type | solution.py:335
  (169 shorter events, 15.0 us)
Async XLA Ops:
  0.6 5.5 %copy-start = (bf16[1,343,343]{2,1,0:T(8,128)(2,1)S(1)}, bf16[1,343,343]{2,1,0:T(8,128)(2,1)}, u32[]{:S(2)}) copy-start(bf16[1,343,343]{2,1,0:T(8,128)(2,1)} %param.6) | copy-start | bytes 705898
  1.5 4.6 %copy-start.2 = (s32[1,343]{1,0:T(1,128)S(1)}, s32[1,343]{1,0:T(1,128)}, u32[]{:S(2)}) copy-start(s32[1,343]{1,0:T(1,128)} %param.7) | copy-start | bytes 4120
  1.5 4.6 %copy-start.3 = (f32[343]{0:T(512)S(1)}, f32[343]{0:T(512)}, u32[]{:S(2)}) copy-start(f32[343]{0:T(512)} %param.8) | copy-start | bytes 4120
  1.6 7.4 %collective-permute-start.1 = (bf16[6,1,6,128]{3,2,1,0:T(8,128)(2,1)S(1)}, bf16[6,1,6,128]{3,2,1,0:T(8,128)(2,1)S(1)}, u32[]{:S(2)}, u32[]{:S(2)}) collective-permute-start(bf16[6,1,6,128]{3,2,1,0:T(8,128)(2,1)S(1)} %slice.544), channel_id=1, source_target_pairs={{0,12},{1,13},{2,14},{3,15},{4,8},{5,9},{6,10},{7,11},{8,4},{9,5},... | collective-permute-start | bytes 27656 | tf_op jit(solution)/shard_map/ppermute | solution.py:41
  5.6 3.7 %collective-permute-start = (bf16[6,1,6,128]{3,2,1,0:T(8,128)(2,1)S(1)}, bf16[6,1,6,128]{3,2,1,0:T(8,128)(2,1)S(1)}, u32[]{:S(2)}, u32[]{:S(2)}) collective-permute-start(bf16[6,1,6,128]{3,2,1,0:T(8,128)(2,1)S(1)} %slice.544), channel_id=1, source_target_pairs={{0,4},{1,5},{2,6},{3,7},{4,0},{5,1},{6,2},{7,3},{8,12},{9,13},{10,... | collective-permute-start | bytes 27656 | tf_op jit(solution)/shard_map/ppermute | solution.py:41
  6.2 2.4 %copy-start.1 = (bf16[216,704]{1,0:T(8,128)(2,1)S(1)}, bf16[216,704]{1,0:T(8,128)(2,1)}, u32[]{:S(2)}) copy-start(bf16[216,704]{1,0:T(8,128)(2,1)} %param.9) | copy-start | bytes 912388
  6.9 13.5 %collective-permute-start.4 = (bf16[343,343]{1,0:T(8,128)(2,1)S(1)}, bf16[343,343]{1,0:T(8,128)(2,1)S(1)}, u32[]{:S(2)}, u32[]{:S(2)}) collective-permute-start(bf16[343,343]{1,0:T(8,128)(2,1)S(1)} %fusion), channel_id=1, source_target_pairs={{0,3},{1,2},{2,1},{3,0},{4,7},{5,6},{6,5},{7,4},{8,11},{9,10},{10,... | collective-permute-start | bytes 705902 | tf_op jit(solution)/shard_map/ppermute | solution.py:59
  7.3 15.8 %collective-permute-start.7 = (bf16[343,343]{1,0:T(8,128)(2,1)S(1)}, bf16[343,343]{1,0:T(8,128)(2,1)S(1)}, u32[]{:S(2)}, u32[]{:S(2)}) collective-permute-start(bf16[343,343]{1,0:T(8,128)(2,1)S(1)} %fusion), channel_id=1, source_target_pairs={{0,1},{1,0},{2,3},{3,2},{4,5},{5,4},{6,7},{7,6},{8,9},{9,8},{10,11... | collective-permute-start | bytes 705902 | tf_op jit(solution)/shard_map/ppermute | solution.py:59
  9.8 6.1 %collective-permute-start.2 = (bf16[258,128]{1,0:T(8,128)(2,1)S(1)}, bf16[258,128]{1,0:T(8,128)(2,1)S(1)}, u32[]{:S(2)}, u32[]{:S(2)}) collective-permute-start(bf16[258,128]{1,0:T(8,128)(2,1)S(1)} %concatenate.140), channel_id=1, source_target_pairs={{0,16},{1,17},{2,18},{3,19},{4,20},{5,21},{6,22},{7,23},{8,24},{9,... | collective-permute-start | bytes 198152 | tf_op jit(solution)/shard_map/ppermute | solution.py:41
  16.4 3.7 %collective-permute-start.3 = (bf16[152,128]{1,0:T(8,128)(2,1)S(1)}, bf16[152,128]{1,0:T(8,128)(2,1)S(1)}, u32[]{:S(2)}, u32[]{:S(2)}) collective-permute-start(bf16[152,128]{1,0:T(8,128)(2,1)S(1)} %pad_maximum_fusion.15), channel_id=1, source_target_pairs={{0,3},{1,2},{2,1},{3,0},{4,7},{5,6},{6,5},{7,4},{8,11},{9,10},{10,... | collective-permute-start | bytes 116744 | tf_op jit(solution)/shard_map/ppermute | solution.py:59
  20.4 1.3 %collective-permute-start.5 = (bf16[152,128]{1,0:T(8,128)(2,1)S(1)}, bf16[152,128]{1,0:T(8,128)(2,1)S(1)}, u32[]{:S(2)}, u32[]{:S(2)}) collective-permute-start(bf16[152,128]{1,0:T(8,128)(2,1)S(1)} %pad_maximum_fusion.16), channel_id=1, source_target_pairs={{0,1},{1,0},{2,3},{3,2},{4,5},{5,4},{6,7},{7,6},{8,9},{9,8},{10,11... | collective-permute-start | bytes 116744 | tf_op jit(solution)/shard_map/ppermute | solution.py:59
  20.7 1.7 %collective-permute-start.6 = (bf16[343,343]{1,0:T(8,128)(2,1)S(1)}, bf16[343,343]{1,0:T(8,128)(2,1)S(1)}, u32[]{:S(2)}, u32[]{:S(2)}) collective-permute-start(bf16[343,343]{1,0:T(8,128)(2,1)S(1)} %collective-permute-done.4), channel_id=1, source_target_pairs={{0,1},{1,0},{2,3},{3,2},{4,5},{5,4},{6,7},{7,6},{8,9},{9,8},{10,11... | collective-permute-start | bytes 705902 | tf_op jit(solution)/shard_map/ppermute | solution.py:59
  24.0 4.1 %collective-permute-start.9 = (bf16[7,1,7,128]{3,2,1,0:T(8,128)(2,1)S(1)}, bf16[7,1,7,128]{3,2,1,0:T(8,128)(2,1)S(1)}, u32[]{:S(2)}, u32[]{:S(2)}) collective-permute-start(bf16[7,1,7,128]{3,2,1,0:T(8,128)(2,1)S(1)} %broadcast_select_fusion.47), channel_id=1, source_target_pairs={{0,13},{1,12},{2,15},{3,14},{4,9},{5,8},{6,11},{7,10},{8,5},{9,4},... | collective-permute-start | bytes 37640 | tf_op jit(solution)/shard_map/ppermute | solution.py:41
  24.8 3.3 %collective-permute-start.8 = (bf16[7,1,7,128]{3,2,1,0:T(8,128)(2,1)S(1)}, bf16[7,1,7,128]{3,2,1,0:T(8,128)(2,1)S(1)}, u32[]{:S(2)}, u32[]{:S(2)}) collective-permute-start(bf16[7,1,7,128]{3,2,1,0:T(8,128)(2,1)S(1)} %get-tuple-element.39), channel_id=1, source_target_pairs={{0,5},{1,4},{2,7},{3,6},{4,1},{5,0},{6,3},{7,2},{8,13},{9,12},{10,... | collective-permute-start | bytes 37640 | tf_op jit(solution)/shard_map/ppermute | solution.py:41
  28.2 4.9 %collective-permute-start.10 = (bf16[1,7,7,128]{3,2,1,0:T(8,128)(2,1)S(1)}, bf16[1,7,7,128]{3,2,1,0:T(8,128)(2,1)S(1)}, u32[]{:S(2)}, u32[]{:S(2)}) collective-permute-start(bf16[1,7,7,128]{3,2,1,0:T(8,128)(2,1)S(1)} %fusion.77), channel_id=1, source_target_pairs={{0,17},{1,16},{2,19},{3,18},{4,21},{5,20},{6,23},{7,22},{8,25},{9,... | collective-permute-start | bytes 37640 | tf_op jit(solution)/shard_map/ppermute | solution.py:41
  31.3 6.4 %collective-permute-start.11 = (bf16[128,704]{0,1:T(8,128)(2,1)S(1)}, bf16[128,704]{0,1:T(8,128)(2,1)S(1)}, u32[]{:S(2)}, u32[]{:S(2)}) collective-permute-start(bf16[128,704]{0,1:T(8,128)(2,1)S(1)} %slice.469), channel_id=1, source_target_pairs={{0,3},{1,2},{2,1},{3,0},{4,7},{5,6},{6,5},{7,4},{8,11},{9,10},{10,... | collective-permute-start | bytes 540680 | tf_op jit(solution)/shard_map/ppermute | solution.py:59
  32.3 10.5 %collective-permute-start.14 = (bf16[124,704]{0,1:T(8,128)(2,1)S(1)}, bf16[124,704]{0,1:T(8,128)(2,1)S(1)}, u32[]{:S(2)}, u32[]{:S(2)}) collective-permute-start(bf16[124,704]{0,1:T(8,128)(2,1)S(1)} %slice.473), channel_id=1, source_target_pairs={{0,3},{1,2},{2,1},{3,0},{4,7},{5,6},{6,5},{7,4},{8,11},{9,10},{10,... | collective-permute-start | bytes 523784 | tf_op jit(solution)/shard_map/ppermute | solution.py:59
  37.7 4.1 %collective-permute-start.13 = (bf16[7,1,7,128]{3,2,1,0:T(8,128)(2,1)S(1)}, bf16[7,1,7,128]{3,2,1,0:T(8,128)(2,1)S(1)}, u32[]{:S(2)}, u32[]{:S(2)}) collective-permute-start(bf16[7,1,7,128]{3,2,1,0:T(8,128)(2,1)S(1)} %broadcast_select_fusion.46), channel_id=1, source_target_pairs={{0,13},{1,12},{2,15},{3,14},{4,9},{5,8},{6,11},{7,10},{8,5},{9,4},... | collective-permute-start | bytes 37640 | tf_op jit(solution)/shard_map/ppermute | solution.py:41
  39.5 3.2 %collective-permute-start.12 = (bf16[7,1,7,128]{3,2,1,0:T(8,128)(2,1)S(1)}, bf16[7,1,7,128]{3,2,1,0:T(8,128)(2,1)S(1)}, u32[]{:S(2)}, u32[]{:S(2)}) collective-permute-start(bf16[7,1,7,128]{3,2,1,0:T(8,128)(2,1)S(1)} %get-tuple-element.35), channel_id=1, source_target_pairs={{0,5},{1,4},{2,7},{3,6},{4,1},{5,0},{6,3},{7,2},{8,13},{9,12},{10,... | collective-permute-start | bytes 37640 | tf_op jit(solution)/shard_map/ppermute | solution.py:41
  42.8 4.1 %collective-permute-start.15 = (bf16[1,7,7,128]{3,2,1,0:T(8,128)(2,1)S(1)}, bf16[1,7,7,128]{3,2,1,0:T(8,128)(2,1)S(1)}, u32[]{:S(2)}, u32[]{:S(2)}) collective-permute-start(bf16[1,7,7,128]{3,2,1,0:T(8,128)(2,1)S(1)} %fusion.78), channel_id=1, source_target_pairs={{0,17},{1,16},{2,19},{3,18},{4,21},{5,20},{6,23},{7,22},{8,25},{9,... | collective-permute-start | bytes 37640 | tf_op jit(solution)/shard_map/ppermute | solution.py:41
  48.4 4.1 %collective-permute-start.17 = (bf16[7,1,7,128]{3,2,1,0:T(8,128)(2,1)S(1)}, bf16[7,1,7,128]{3,2,1,0:T(8,128)(2,1)S(1)}, u32[]{:S(2)}, u32[]{:S(2)}) collective-permute-start(bf16[7,1,7,128]{3,2,1,0:T(8,128)(2,1)S(1)} %slice.758), channel_id=1, source_target_pairs={{0,13},{1,12},{2,15},{3,14},{4,9},{5,8},{6,11},{7,10},{8,5},{9,4},... | collective-permute-start | bytes 37640 | tf_op jit(solution)/shard_map/ppermute | solution.py:41
  49.5 3.2 %collective-permute-start.16 = (bf16[7,1,7,128]{3,2,1,0:T(8,128)(2,1)S(1)}, bf16[7,1,7,128]{3,2,1,0:T(8,128)(2,1)S(1)}, u32[]{:S(2)}, u32[]{:S(2)}) collective-permute-start(bf16[7,1,7,128]{3,2,1,0:T(8,128)(2,1)S(1)} %slice.758), channel_id=1, source_target_pairs={{0,5},{1,4},{2,7},{3,6},{4,1},{5,0},{6,3},{7,2},{8,13},{9,12},{10,... | collective-permute-start | bytes 37640 | tf_op jit(solution)/shard_map/ppermute | solution.py:41
  51.0 2.6 %collective-permute-start.18 = (bf16[2,252,704]{1,2,0:T(8,128)(2,1)S(1)}, bf16[2,252,704]{1,2,0:T(8,128)(2,1)}, u32[]{:S(2)}, u32[]{:S(2)}) collective-permute-start(bf16[2,252,704]{1,2,0:T(8,128)(2,1)S(1)} %pad_maximum_fusion), channel_id=1, source_target_pairs={{0,1},{1,0},{2,3},{3,2},{4,5},{5,4},{6,7},{7,6},{8,9},{9,8},{10,11... | collective-permute-start | bytes 2128904 | tf_op jit(solution)/shard_map/ppermute | solution.py:59
  56.5 5.8 %collective-permute-start.19 = (bf16[212,128]{1,0:T(8,128)(2,1)S(1)}, bf16[212,128]{1,0:T(8,128)(2,1)S(1)}, u32[]{:S(2)}, u32[]{:S(2)}) collective-permute-start(bf16[212,128]{1,0:T(8,128)(2,1)S(1)} %pad_maximum_fusion.10), channel_id=1, source_target_pairs={{0,17},{1,16},{2,19},{3,18},{4,21},{5,20},{6,23},{7,22},{8,25},{9,... | collective-permute-start | bytes 162824 | tf_op jit(solution)/shard_map/ppermute | solution.py:59
  62.6 3.5 %collective-permute-start.20 = (bf16[176,128]{1,0:T(8,128)(2,1)S(1)}, bf16[176,128]{1,0:T(8,128)(2,1)S(1)}, u32[]{:S(2)}, u32[]{:S(2)}) collective-permute-start(bf16[176,128]{1,0:T(8,128)(2,1)S(1)} %add_convert_fusion.2), channel_id=1, source_target_pairs={{0,5},{1,4},{2,7},{3,6},{4,1},{5,0},{6,3},{7,2},{8,13},{9,12},{10,... | collective-permute-start | bytes 135176 | tf_op jit(solution)/shard_map/ppermute | solution.py:41
  66.1 4.4 %collective-permute-start.21 = (bf16[176,128]{1,0:T(8,128)(2,1)S(1)}, bf16[176,128]{1,0:T(8,128)(2,1)S(1)}, u32[]{:S(2)}, u32[]{:S(2)}) collective-permute-start(bf16[176,128]{1,0:T(8,128)(2,1)S(1)} %add_convert_fusion.1), channel_id=1, source_target_pairs={{0,13},{1,12},{2,15},{3,14},{4,9},{5,8},{6,11},{7,10},{8,5},{9,4},... | collective-permute-start | bytes 135176 | tf_op jit(solution)/shard_map/ppermute | solution.py:41
  70.7 4.2 %collective-permute-start.22 = (bf16[284,128]{1,0:T(8,128)(2,1)S(1)}, bf16[284,128]{1,0:T(8,128)(2,1)S(1)}, u32[]{:S(2)}, u32[]{:S(2)}) collective-permute-start(bf16[284,128]{1,0:T(8,128)(2,1)S(1)} %maximum_maximum_fusion.2), channel_id=1, source_target_pairs={{0,3},{1,2},{2,1},{3,0},{4,7},{5,6},{6,5},{7,4},{8,11},{9,10},{10,... | collective-permute-start | bytes 218120 | tf_op jit(solution)/shard_map/ppermute | solution.py:59
  75.1 1.4 %collective-permute-start.23 = (bf16[460,128]{1,0:T(8,128)(2,1)S(1)}, bf16[460,128]{1,0:T(8,128)(2,1)S(1)}, u32[]{:S(2)}, u32[]{:S(2)}) collective-permute-start(bf16[460,128]{1,0:T(8,128)(2,1)S(1)} %maximum_maximum_fusion), channel_id=1, source_target_pairs={{0,1},{1,0},{2,3},{3,2},{4,5},{5,4},{6,7},{7,6},{8,9},{9,8},{10,11... | collective-permute-start | bytes 353288 | tf_op jit(solution)/shard_map/ppermute | solution.py:59

commit v13 on v12

--- a/solution.py
+++ b/solution.py
@@ -202,6 +202,7 @@
     top = jnp.pad(locked[-edge * edge :], ((0, 0), (0, -locked.shape[1] % columns)))
     top = jnp.concatenate(split(top, tiles), axis=0)
     sent = jnp.concatenate([top, high], axis=0)
+    sent, matrix = lax.optimization_barrier((sent, matrix))
     arrived = grid.exchanged(sent, sent, 0, cross=0)[0]
     bottom = jnp.split(arrived[: top.shape[0]], tiles, axis=0)
     bottom = jnp.concatenate(bottom, axis=1)[:, : locked.shape[1]]
@@ -268,7 +269,7 @@
         older = lax.optimization_barrier(current)
         current = following
     other_locked = jnp.concatenate(other_parts, axis=0)
-    both_locked = grid.partner(jnp.stack([locked, other_locked]), SECOND)
+    both_locked = [grid.partner(l, SECOND) for l in (locked, other_locked)]
     low = plane(partial, 1, 0).astype(jnp.bfloat16)
     all_locked = [locked, both_locked[0], both_locked[1], other_locked]
     to_high = grid.exchanged(low, low, 1)[1].astype(jnp.float32)

time: 79.2 us -> 81.8 us (1.033)
  waiting for transfers between devices: 36.3 us -> 40 us
  matrix products: 6.62 us -> 4.88 us
  starting transfers between devices: 25.4 us -> 26.9 us
    ppermute x11 -> x12, waiting for transfers between devices: 16.2 us -> 22.2 us  [partner(): lax.ppermute(value, AXIS, [(i, i ^ bits) for i in range(self.devices)])]
    ppermute x13, starting transfers between devices: 18.8 us -> 21.8 us  [swapped(): arrived = lax.ppermute(jnp.where(lower, high, low), AXIS, pairs)]
    ppermute x13, waiting for transfers between devices: 20.1 us -> 17.8 us  [swapped(): arrived = lax.ppermute(jnp.where(lower, high, low), AXIS, pairs)]
    dot_general x4, matrix products: 2.96 us -> 1.22 us  [per_device(): lax.dot_general(all_locked[r], jnp.where(owner_near == r, weights, jnp.ze...]
    ppermute x11 -> x12, starting transfers between devices: 6.66 us -> 5.14 us  [partner(): lax.ppermute(value, AXIS, [(i, i ^ bits) for i in range(self.devices)])]
  transfers between devices with their start and end apart: 24 -> 25, of which waited for: 17 -> 20; matrix products, arithmetic and copies ran while one was open for 8% -> 9% of each run, Pallas kernels for 0% -> 0%
where the time goes in v13:
time: 81.8 us; the launch traced here: 81.6 us
  waiting for transfers between devices  40 us (49%)
  starting transfers between devices  26.9 us (33%)
  other arithmetic  4.99 us (6%)
  matrix products  4.88 us (6%)
  local copies, waits for them, and re-layouts  3.29 us (4%)
  between operations  1.61 us (2%)
    ppermute x12, waiting for transfers between devices, partner(): lax.ppermute(value, AXIS, [(i, i ^ bits) for i in range(self.devices)])  22.2 us
    ppermute x13, starting transfers between devices, swapped(): arrived = lax.ppermute(jnp.where(lower, high, low), AXIS, pairs)  21.8 us
    ppermute x13, waiting for transfers between devices, swapped(): arrived = lax.ppermute(jnp.where(lower, high, low), AXIS, pairs)  17.8 us
    ppermute x12, starting transfers between devices, partner(): lax.ppermute(value, AXIS, [(i, i ^ bits) for i in range(self.devices)])  5.14 us
    dot_general x12, matrix products, per_device(): jnp.dot(matrices[r], own, preferred_element_type=jnp.float32)  2.93 us
  transfers between devices with their start and end apart: 25, of which 20 were waited for; matrix products, arithmetic and copies ran while one was open for 9% of the time, Pallas kernels for 0%

profile of v13, /device:TPU:0, one launch (start us, length us, event | category | flops | bytes accessed | tf_op | source)
XLA Modules:
  0.0 81.6 jit_solution(13236721076889597650)
XLA Ops:
  0.6 0.9 %reshape.124 = bf16[6,6,6,128]{3,2,1,0:T(8,128)(2,1)S(1)} reshape(bf16[216,128]{1,0:T(8,128)(2,1)} %param.5) | data formatting | bytes 110592 | tf_op jit(solution)/shard_map/reshape | solution.py:193
  1.6 3.0 %collective-permute-start = (bf16[6,1,6,128]{3,2,1,0:T(8,128)(2,1)S(1)}, bf16[6,1,6,128]{3,2,1,0:T(8,128)(2,1)S(1)}, u32[]{:S(2)}, u32[]{:S(2)}) collective-permute-start(bf16[6,1,6,128]{3,2,1,0:T(8,128)(2,1)S(1)} %slice.535), channel_id=1, source_target_pairs={{0,4},{1,5},{2,6},{3,7},{4,0},{5,1},{6,2},{7,3},{8,12},{9,13},{10,... | collective-permute-start | bytes 27656 | tf_op jit(solution)/shard_map/ppermute | solution.py:41
  4.6 1.5 %collective-permute-start.1 = (bf16[6,1,6,128]{3,2,1,0:T(8,128)(2,1)S(1)}, bf16[6,1,6,128]{3,2,1,0:T(8,128)(2,1)S(1)}, u32[]{:S(2)}, u32[]{:S(2)}) collective-permute-start(bf16[6,1,6,128]{3,2,1,0:T(8,128)(2,1)S(1)} %slice.535), channel_id=1, source_target_pairs={{0,12},{1,13},{2,14},{3,15},{4,8},{5,9},{6,10},{7,11},{8,4},{9,5},... | collective-permute-start | bytes 27656 | tf_op jit(solution)/shard_map/ppermute | solution.py:41
  6.2 0.7 fusion
  7.6 1.6 %collective-permute-done.1 = bf16[6,1,6,128]{3,2,1,0:T(8,128)(2,1)S(1)} collective-permute-done((bf16[6,1,6,128]{3,2,1,0:T(8,128)(2,1)S(1)}, bf16[6,1,6,128]{3,2,1,0:T(8,128)(2,1)S(1)}, u32[]{:S(2)}, u32[]{:S(2)}) %collective-permute-start.1) | collective-permute-done | bytes 9248 | tf_op jit(solution)/shard_map/ppermute | solution.py:41
  9.7 2.7 %collective-permute-start.2 = (bf16[258,128]{1,0:T(8,128)(2,1)S(1)}, bf16[258,128]{1,0:T(8,128)(2,1)S(1)}, u32[]{:S(2)}, u32[]{:S(2)}) collective-permute-start(bf16[258,128]{1,0:T(8,128)(2,1)S(1)} %concatenate.141), channel_id=1, source_target_pairs={{0,16},{1,17},{2,18},{3,19},{4,20},{5,21},{6,22},{7,23},{8,24},{9,... | collective-permute-start | bytes 198152 | tf_op jit(solution)/shard_map/ppermute | solution.py:41
  12.3 2.6 %collective-permute-done.2 = bf16[258,128]{1,0:T(8,128)(2,1)S(1)} collective-permute-done((bf16[258,128]{1,0:T(8,128)(2,1)S(1)}, bf16[258,128]{1,0:T(8,128)(2,1)S(1)}, u32[]{:S(2)}, u32[]{:S(2)}) %collective-permute-start.2) | collective-permute-done | bytes 66080 | tf_op jit(solution)/shard_map/ppermute | solution.py:41
  15.6 3.7 %collective-permute-done.3 = bf16[152,128]{1,0:T(8,128)(2,1)S(1)} collective-permute-done((bf16[152,128]{1,0:T(8,128)(2,1)S(1)}, bf16[152,128]{1,0:T(8,128)(2,1)S(1)}, u32[]{:S(2)}, u32[]{:S(2)}) %collective-permute-start.3) | collective-permute-done | bytes 38944 | tf_op jit(solution)/shard_map/ppermute | solution.py:59
  23.1 1.6 %collective-permute-start.9 = (bf16[7,1,7,128]{3,2,1,0:T(8,128)(2,1)S(1)}, bf16[7,1,7,128]{3,2,1,0:T(8,128)(2,1)S(1)}, u32[]{:S(2)}, u32[]{:S(2)}) collective-permute-start(bf16[7,1,7,128]{3,2,1,0:T(8,128)(2,1)S(1)} %broadcast_select_fusion.45), channel_id=1, source_target_pairs={{0,13},{1,12},{2,15},{3,14},{4,9},{5,8},{6,11},{7,10},{8,5},{9,4},... | collective-permute-start | bytes 37640 | tf_op jit(solution)/shard_map/ppermute | solution.py:41
  24.7 1.2 %collective-permute-start.8 = (bf16[7,1,7,128]{3,2,1,0:T(8,128)(2,1)S(1)}, bf16[7,1,7,128]{3,2,1,0:T(8,128)(2,1)S(1)}, u32[]{:S(2)}, u32[]{:S(2)}) collective-permute-start(bf16[7,1,7,128]{3,2,1,0:T(8,128)(2,1)S(1)} %get-tuple-element.43), channel_id=1, source_target_pairs={{0,5},{1,4},{2,7},{3,6},{4,1},{5,0},{6,3},{7,2},{8,13},{9,12},{10,... | collective-permute-start | bytes 37640 | tf_op jit(solution)/shard_map/ppermute | solution.py:41
  25.9 1.3 %collective-permute-done.9 = bf16[7,1,7,128]{3,2,1,0:T(8,128)(2,1)S(1)} collective-permute-done((bf16[7,1,7,128]{3,2,1,0:T(8,128)(2,1)S(1)}, bf16[7,1,7,128]{3,2,1,0:T(8,128)(2,1)S(1)}, u32[]{:S(2)}, u32[]{:S(2)}) %collective-permute-start.9) | collective-permute-done | bytes 12576 | tf_op jit(solution)/shard_map/ppermute | solution.py:41
  27.2 0.7 collective-permute-done.8
  28.0 2.9 %collective-permute-start.10 = (bf16[1,7,7,128]{3,2,1,0:T(8,128)(2,1)S(1)}, bf16[1,7,7,128]{3,2,1,0:T(8,128)(2,1)S(1)}, u32[]{:S(2)}, u32[]{:S(2)}) collective-permute-start(bf16[1,7,7,128]{3,2,1,0:T(8,128)(2,1)S(1)} %fusion.83), channel_id=1, source_target_pairs={{0,17},{1,16},{2,19},{3,18},{4,21},{5,20},{6,23},{7,22},{8,25},{9,... | collective-permute-start | bytes 37640 | tf_op jit(solution)/shard_map/ppermute | solution.py:41
  31.0 1.1 %collective-permute-start.11 = (bf16[128,704]{1,0:T(8,128)(2,1)S(1)}, bf16[128,704]{1,0:T(8,128)(2,1)S(1)}, u32[]{:S(2)}, u32[]{:S(2)}) collective-permute-start(bf16[128,704]{1,0:T(8,128)(2,1)S(1)} %slice.463), channel_id=1, source_target_pairs={{0,3},{1,2},{2,1},{3,0},{4,7},{5,6},{6,5},{7,4},{8,11},{9,10},{10,... | collective-permute-start | bytes 540680 | tf_op jit(solution)/shard_map/ppermute | solution.py:59
  33.9 3.9 %collective-permute-done.11 = bf16[128,704]{1,0:T(8,128)(2,1)S(1)} collective-permute-done((bf16[128,704]{1,0:T(8,128)(2,1)S(1)}, bf16[128,704]{1,0:T(8,128)(2,1)S(1)}, u32[]{:S(2)}, u32[]{:S(2)}) %collective-permute-start.11) | collective-permute-done | bytes 180256 | tf_op jit(solution)/shard_map/ppermute | solution.py:59
  37.8 1.1 %collective-permute-start.13 = (bf16[7,1,7,128]{3,2,1,0:T(8,128)(2,1)S(1)}, bf16[7,1,7,128]{3,2,1,0:T(8,128)(2,1)S(1)}, u32[]{:S(2)}, u32[]{:S(2)}) collective-permute-start(bf16[7,1,7,128]{3,2,1,0:T(8,128)(2,1)S(1)} %broadcast_select_fusion.44), channel_id=1, source_target_pairs={{0,13},{1,12},{2,15},{3,14},{4,9},{5,8},{6,11},{7,10},{8,5},{9,4},... | collective-permute-start | bytes 37640 | tf_op jit(solution)/shard_map/ppermute | solution.py:41
  38.9 1.4 %collective-permute-start.12 = (bf16[7,1,7,128]{3,2,1,0:T(8,128)(2,1)S(1)}, bf16[7,1,7,128]{3,2,1,0:T(8,128)(2,1)S(1)}, u32[]{:S(2)}, u32[]{:S(2)}) collective-permute-start(bf16[7,1,7,128]{3,2,1,0:T(8,128)(2,1)S(1)} %get-tuple-element.39), channel_id=1, source_target_pairs={{0,5},{1,4},{2,7},{3,6},{4,1},{5,0},{6,3},{7,2},{8,13},{9,12},{10,... | collective-permute-start | bytes 37640 | tf_op jit(solution)/shard_map/ppermute | solution.py:41
  40.5 1.1 %collective-permute-start.14 = (bf16[124,704]{1,0:T(8,128)(2,1)S(1)}, bf16[124,704]{1,0:T(8,128)(2,1)S(1)}, u32[]{:S(2)}, u32[]{:S(2)}) collective-permute-start(bf16[124,704]{1,0:T(8,128)(2,1)S(1)} %slice.467), channel_id=1, source_target_pairs={{0,3},{1,2},{2,1},{3,0},{4,7},{5,6},{6,5},{7,4},{8,11},{9,10},{10,... | collective-permute-start | bytes 523784 | tf_op jit(solution)/shard_map/ppermute | solution.py:59
  42.2 5.1 %collective-permute-done.14 = bf16[124,704]{1,0:T(8,128)(2,1)S(1)} collective-permute-done((bf16[124,704]{1,0:T(8,128)(2,1)S(1)}, bf16[124,704]{1,0:T(8,128)(2,1)S(1)}, u32[]{:S(2)}, u32[]{:S(2)}) %collective-permute-start.14) | collective-permute-done | bytes 174624 | tf_op jit(solution)/shard_map/ppermute | solution.py:59
  47.8 3.6 %collective-permute-done.15 = bf16[1,7,7,128]{3,2,1,0:T(8,128)(2,1)S(1)} collective-permute-done((bf16[1,7,7,128]{3,2,1,0:T(8,128)(2,1)S(1)}, bf16[1,7,7,128]{3,2,1,0:T(8,128)(2,1)S(1)}, u32[]{:S(2)}, u32[]{:S(2)}) %collective-permute-start.15) | collective-permute-done | bytes 12576 | tf_op jit(solution)/shard_map/ppermute | solution.py:41
  53.5 1.9 %collective-permute-start.17 = (bf16[7,1,7,128]{3,2,1,0:T(8,128)(2,1)S(1)}, bf16[7,1,7,128]{3,2,1,0:T(8,128)(2,1)S(1)}, u32[]{:S(2)}, u32[]{:S(2)}) collective-permute-start(bf16[7,1,7,128]{3,2,1,0:T(8,128)(2,1)S(1)} %slice.744), channel_id=1, source_target_pairs={{0,13},{1,12},{2,15},{3,14},{4,9},{5,8},{6,11},{7,10},{8,5},{9,4},... | collective-permute-start | bytes 37640 | tf_op jit(solution)/shard_map/ppermute | solution.py:41
  56.1 1.4 %collective-permute-done.17 = bf16[7,1,7,128]{3,2,1,0:T(8,128)(2,1)S(1)} collective-permute-done((bf16[7,1,7,128]{3,2,1,0:T(8,128)(2,1)S(1)}, bf16[7,1,7,128]{3,2,1,0:T(8,128)(2,1)S(1)}, u32[]{:S(2)}, u32[]{:S(2)}) %collective-permute-start.17) | collective-permute-done | bytes 12576 | tf_op jit(solution)/shard_map/ppermute | solution.py:41
  59.7 4.7 %collective-permute-done.20 = bf16[212,128]{1,0:T(8,128)(2,1)S(1)} collective-permute-done((bf16[212,128]{1,0:T(8,128)(2,1)S(1)}, bf16[212,128]{1,0:T(8,128)(2,1)S(1)}, u32[]{:S(2)}, u32[]{:S(2)}) %collective-permute-start.20) | collective-permute-done | bytes 54304 | tf_op jit(solution)/shard_map/ppermute | solution.py:59
  64.4 2.6 %collective-permute-start.21 = (bf16[176,128]{1,0:T(8,128)(2,1)S(1)}, bf16[176,128]{1,0:T(8,128)(2,1)S(1)}, u32[]{:S(2)}, u32[]{:S(2)}) collective-permute-start(bf16[176,128]{1,0:T(8,128)(2,1)S(1)} %add_convert_fusion.2), channel_id=1, source_target_pairs={{0,5},{1,4},{2,7},{3,6},{4,1},{5,0},{6,3},{7,2},{8,13},{9,12},{10,... | collective-permute-start | bytes 135176 | tf_op jit(solution)/shard_map/ppermute | solution.py:41
  67.2 1.6 %collective-permute-done.21 = bf16[176,128]{1,0:T(8,128)(2,1)S(1)} collective-permute-done((bf16[176,128]{1,0:T(8,128)(2,1)S(1)}, bf16[176,128]{1,0:T(8,128)(2,1)S(1)}, u32[]{:S(2)}, u32[]{:S(2)}) %collective-permute-start.21) | collective-permute-done | bytes 45088 | tf_op jit(solution)/shard_map/ppermute | solution.py:41
  68.8 0.9 %collective-permute-start.22 = (bf16[176,128]{1,0:T(8,128)(2,1)S(1)}, bf16[176,128]{1,0:T(8,128)(2,1)S(1)}, u32[]{:S(2)}, u32[]{:S(2)}) collective-permute-start(bf16[176,128]{1,0:T(8,128)(2,1)S(1)} %add_convert_fusion.1), channel_id=1, source_target_pairs={{0,13},{1,12},{2,15},{3,14},{4,9},{5,8},{6,11},{7,10},{8,5},{9,4},... | collective-permute-start | bytes 135176 | tf_op jit(solution)/shard_map/ppermute | solution.py:41
  69.8 3.5 %collective-permute-done.22 = bf16[176,128]{1,0:T(8,128)(2,1)S(1)} collective-permute-done((bf16[176,128]{1,0:T(8,128)(2,1)S(1)}, bf16[176,128]{1,0:T(8,128)(2,1)S(1)}, u32[]{:S(2)}, u32[]{:S(2)}) %collective-permute-start.22) | collective-permute-done | bytes 45088 | tf_op jit(solution)/shard_map/ppermute | solution.py:41
  73.4 1.1 %collective-permute-start.23 = (bf16[284,128]{1,0:T(8,128)(2,1)S(1)}, bf16[284,128]{1,0:T(8,128)(2,1)S(1)}, u32[]{:S(2)}, u32[]{:S(2)}) collective-permute-start(bf16[284,128]{1,0:T(8,128)(2,1)S(1)} %maximum_maximum_fusion.2), channel_id=1, source_target_pairs={{0,3},{1,2},{2,1},{3,0},{4,7},{5,6},{6,5},{7,4},{8,11},{9,10},{10,... | collective-permute-start | bytes 218120 | tf_op jit(solution)/shard_map/ppermute | solution.py:59
  74.5 3.1 %collective-permute-done.23 = bf16[284,128]{1,0:T(8,128)(2,1)S(1)} collective-permute-done((bf16[284,128]{1,0:T(8,128)(2,1)S(1)}, bf16[284,128]{1,0:T(8,128)(2,1)S(1)}, u32[]{:S(2)}, u32[]{:S(2)}) %collective-permute-start.23) | collective-permute-done | bytes 72736 | tf_op jit(solution)/shard_map/ppermute | solution.py:59
  78.1 1.1 %collective-permute-done.24 = bf16[460,128]{1,0:T(8,128)(2,1)S(1)} collective-permute-done((bf16[460,128]{1,0:T(8,128)(2,1)S(1)}, bf16[460,128]{1,0:T(8,128)(2,1)S(1)}, u32[]{:S(2)}, u32[]{:S(2)}) %collective-permute-start.24) | collective-permute-done | bytes 117792 | tf_op jit(solution)/shard_map/ppermute | solution.py:59
  79.9 0.7 pad_maximum_fusion.14
  80.7 1.0 %maximum_convert_fusion = f32[704,128]{1,0:T(8,128)} fusion(bf16[176,32]{1,0:T(8,128)(2,1)S(1)} %get-tuple-element.126, bf16[176,32]{1,0:T(8,128)(2,1)S(1)} %get-tuple-element.122, bf16[176,32]{1,0:T(8,128)(2,1)S(1)} %get-tuple-element.118, bf16[176,32]{1,0:T(8,128)(2,1)S(1)} %get-tuple-element.114, bf16[176,32]{1,0:T(8,128)(2,1)S(1)} %get-tuple-element.127, ...), kind=kLoop, calls=%fused_computation.50 | loop fusion | flops 2883584 | bytes 540672 | tf_op jit(solution)/shard_map/convert_element_type | solution.py:336
  (166 shorter events, 15.0 us)
Async XLA Ops:
  0.6 5.5 %copy-start = (bf16[1,343,343]{2,1,0:T(8,128)(2,1)S(1)}, bf16[1,343,343]{2,1,0:T(8,128)(2,1)}, u32[]{:S(2)}) copy-start(bf16[1,343,343]{2,1,0:T(8,128)(2,1)} %param.6) | copy-start | bytes 705898
  1.5 4.6 %copy-start.2 = (s32[1,343]{1,0:T(1,128)S(1)}, s32[1,343]{1,0:T(1,128)}, u32[]{:S(2)}) copy-start(s32[1,343]{1,0:T(1,128)} %param.7) | copy-start | bytes 4120
  1.5 4.6 %copy-start.3 = (f32[343]{0:T(512)S(1)}, f32[343]{0:T(512)}, u32[]{:S(2)}) copy-start(f32[343]{0:T(512)} %param.8) | copy-start | bytes 4120
  1.6 6.0 %collective-permute-start = (bf16[6,1,6,128]{3,2,1,0:T(8,128)(2,1)S(1)}, bf16[6,1,6,128]{3,2,1,0:T(8,128)(2,1)S(1)}, u32[]{:S(2)}, u32[]{:S(2)}) collective-permute-start(bf16[6,1,6,128]{3,2,1,0:T(8,128)(2,1)S(1)} %slice.535), channel_id=1, source_target_pairs={{0,4},{1,5},{2,6},{3,7},{4,0},{5,1},{6,2},{7,3},{8,12},{9,13},{10,... | collective-permute-start | bytes 27656 | tf_op jit(solution)/shard_map/ppermute | solution.py:41
  4.6 4.6 %collective-permute-start.1 = (bf16[6,1,6,128]{3,2,1,0:T(8,128)(2,1)S(1)}, bf16[6,1,6,128]{3,2,1,0:T(8,128)(2,1)S(1)}, u32[]{:S(2)}, u32[]{:S(2)}) collective-permute-start(bf16[6,1,6,128]{3,2,1,0:T(8,128)(2,1)S(1)} %slice.535), channel_id=1, source_target_pairs={{0,12},{1,13},{2,14},{3,15},{4,8},{5,9},{6,10},{7,11},{8,4},{9,5},... | collective-permute-start | bytes 27656 | tf_op jit(solution)/shard_map/ppermute | solution.py:41
  6.2 1.2 %copy-start.1 = (bf16[216,704]{1,0:T(8,128)(2,1)S(1)}, bf16[216,704]{1,0:T(8,128)(2,1)}, u32[]{:S(2)}) copy-start(bf16[216,704]{1,0:T(8,128)(2,1)} %param.9) | copy-start | bytes 912388
  6.9 12.7 %collective-permute-start.4 = (bf16[343,343]{1,0:T(8,128)(2,1)S(1)}, bf16[343,343]{1,0:T(8,128)(2,1)S(1)}, u32[]{:S(2)}, u32[]{:S(2)}) collective-permute-start(bf16[343,343]{1,0:T(8,128)(2,1)S(1)} %fusion), channel_id=1, source_target_pairs={{0,3},{1,2},{2,1},{3,0},{4,7},{5,6},{6,5},{7,4},{8,11},{9,10},{10,... | collective-permute-start | bytes 705902 | tf_op jit(solution)/shard_map/ppermute | solution.py:59
  9.7 5.3 %collective-permute-start.2 = (bf16[258,128]{1,0:T(8,128)(2,1)S(1)}, bf16[258,128]{1,0:T(8,128)(2,1)S(1)}, u32[]{:S(2)}, u32[]{:S(2)}) collective-permute-start(bf16[258,128]{1,0:T(8,128)(2,1)S(1)} %concatenate.141), channel_id=1, source_target_pairs={{0,16},{1,17},{2,18},{3,19},{4,20},{5,21},{6,22},{7,23},{8,24},{9,... | collective-permute-start | bytes 198152 | tf_op jit(solution)/shard_map/ppermute | solution.py:41
  12.3 9.9 %collective-permute-start.7 = (bf16[343,343]{1,0:T(8,128)(2,1)S(1)}, bf16[343,343]{1,0:T(8,128)(2,1)S(1)}, u32[]{:S(2)}, u32[]{:S(2)}) collective-permute-start(bf16[343,343]{1,0:T(8,128)(2,1)S(1)} %fusion), channel_id=1, source_target_pairs={{0,1},{1,0},{2,3},{3,2},{4,5},{5,4},{6,7},{7,6},{8,9},{9,8},{10,11... | collective-permute-start | bytes 705902 | tf_op jit(solution)/shard_map/ppermute | solution.py:59
  15.4 3.9 %collective-permute-start.3 = (bf16[152,128]{1,0:T(8,128)(2,1)S(1)}, bf16[152,128]{1,0:T(8,128)(2,1)S(1)}, u32[]{:S(2)}, u32[]{:S(2)}) collective-permute-start(bf16[152,128]{1,0:T(8,128)(2,1)S(1)} %pad_maximum_fusion.15), channel_id=1, source_target_pairs={{0,3},{1,2},{2,1},{3,0},{4,7},{5,6},{6,5},{7,4},{8,11},{9,10},{10,... | collective-permute-start | bytes 116744 | tf_op jit(solution)/shard_map/ppermute | solution.py:59
  19.6 1.3 %collective-permute-start.5 = (bf16[152,128]{1,0:T(8,128)(2,1)S(1)}, bf16[152,128]{1,0:T(8,128)(2,1)S(1)}, u32[]{:S(2)}, u32[]{:S(2)}) collective-permute-start(bf16[152,128]{1,0:T(8,128)(2,1)S(1)} %pad_maximum_fusion.16), channel_id=1, source_target_pairs={{0,1},{1,0},{2,3},{3,2},{4,5},{5,4},{6,7},{7,6},{8,9},{9,8},{10,11... | collective-permute-start | bytes 116744 | tf_op jit(solution)/shard_map/ppermute | solution.py:59
  19.9 1.6 %collective-permute-start.6 = (bf16[343,343]{1,0:T(8,128)(2,1)S(1)}, bf16[343,343]{1,0:T(8,128)(2,1)S(1)}, u32[]{:S(2)}, u32[]{:S(2)}) collective-permute-start(bf16[343,343]{1,0:T(8,128)(2,1)S(1)} %collective-permute-done.4), channel_id=1, source_target_pairs={{0,1},{1,0},{2,3},{3,2},{4,5},{5,4},{6,7},{7,6},{8,9},{9,8},{10,11... | collective-permute-start | bytes 705902 | tf_op jit(solution)/shard_map/ppermute | solution.py:59
  23.1 4.1 %collective-permute-start.9 = (bf16[7,1,7,128]{3,2,1,0:T(8,128)(2,1)S(1)}, bf16[7,1,7,128]{3,2,1,0:T(8,128)(2,1)S(1)}, u32[]{:S(2)}, u32[]{:S(2)}) collective-permute-start(bf16[7,1,7,128]{3,2,1,0:T(8,128)(2,1)S(1)} %broadcast_select_fusion.45), channel_id=1, source_target_pairs={{0,13},{1,12},{2,15},{3,14},{4,9},{5,8},{6,11},{7,10},{8,5},{9,4},... | collective-permute-start | bytes 37640 | tf_op jit(solution)/shard_map/ppermute | solution.py:41
  24.7 3.2 %collective-permute-start.8 = (bf16[7,1,7,128]{3,2,1,0:T(8,128)(2,1)S(1)}, bf16[7,1,7,128]{3,2,1,0:T(8,128)(2,1)S(1)}, u32[]{:S(2)}, u32[]{:S(2)}) collective-permute-start(bf16[7,1,7,128]{3,2,1,0:T(8,128)(2,1)S(1)} %get-tuple-element.43), channel_id=1, source_target_pairs={{0,5},{1,4},{2,7},{3,6},{4,1},{5,0},{6,3},{7,2},{8,13},{9,12},{10,... | collective-permute-start | bytes 37640 | tf_op jit(solution)/shard_map/ppermute | solution.py:41
  28.0 4.4 %collective-permute-start.10 = (bf16[1,7,7,128]{3,2,1,0:T(8,128)(2,1)S(1)}, bf16[1,7,7,128]{3,2,1,0:T(8,128)(2,1)S(1)}, u32[]{:S(2)}, u32[]{:S(2)}) collective-permute-start(bf16[1,7,7,128]{3,2,1,0:T(8,128)(2,1)S(1)} %fusion.83), channel_id=1, source_target_pairs={{0,17},{1,16},{2,19},{3,18},{4,21},{5,20},{6,23},{7,22},{8,25},{9,... | collective-permute-start | bytes 37640 | tf_op jit(solution)/shard_map/ppermute | solution.py:41
  31.0 6.8 %collective-permute-start.11 = (bf16[128,704]{1,0:T(8,128)(2,1)S(1)}, bf16[128,704]{1,0:T(8,128)(2,1)S(1)}, u32[]{:S(2)}, u32[]{:S(2)}) collective-permute-start(bf16[128,704]{1,0:T(8,128)(2,1)S(1)} %slice.463), channel_id=1, source_target_pairs={{0,3},{1,2},{2,1},{3,0},{4,7},{5,6},{6,5},{7,4},{8,11},{9,10},{10,... | collective-permute-start | bytes 540680 | tf_op jit(solution)/shard_map/ppermute | solution.py:59
  37.8 4.1 %collective-permute-start.13 = (bf16[7,1,7,128]{3,2,1,0:T(8,128)(2,1)S(1)}, bf16[7,1,7,128]{3,2,1,0:T(8,128)(2,1)S(1)}, u32[]{:S(2)}, u32[]{:S(2)}) collective-permute-start(bf16[7,1,7,128]{3,2,1,0:T(8,128)(2,1)S(1)} %broadcast_select_fusion.44), channel_id=1, source_target_pairs={{0,13},{1,12},{2,15},{3,14},{4,9},{5,8},{6,11},{7,10},{8,5},{9,4},... | collective-permute-start | bytes 37640 | tf_op jit(solution)/shard_map/ppermute | solution.py:41
  38.9 3.2 %collective-permute-start.12 = (bf16[7,1,7,128]{3,2,1,0:T(8,128)(2,1)S(1)}, bf16[7,1,7,128]{3,2,1,0:T(8,128)(2,1)S(1)}, u32[]{:S(2)}, u32[]{:S(2)}) collective-permute-start(bf16[7,1,7,128]{3,2,1,0:T(8,128)(2,1)S(1)} %get-tuple-element.39), channel_id=1, source_target_pairs={{0,5},{1,4},{2,7},{3,6},{4,1},{5,0},{6,3},{7,2},{8,13},{9,12},{10,... | collective-permute-start | bytes 37640 | tf_op jit(solution)/shard_map/ppermute | solution.py:41
  40.3 18.1 %collective-permute-start.18 = (bf16[252,704]{1,0:T(8,128)(2,1)S(1)}, bf16[252,704]{1,0:T(8,128)(2,1)S(1)}, u32[]{:S(2)}, u32[]{:S(2)}) collective-permute-start(bf16[252,704]{1,0:T(8,128)(2,1)S(1)} %pad_maximum_fusion), channel_id=1, source_target_pairs={{0,1},{1,0},{2,3},{3,2},{4,5},{5,4},{6,7},{7,6},{8,9},{9,8},{10,11... | collective-permute-start | bytes 1064456 | tf_op jit(solution)/shard_map/ppermute | solution.py:59
  40.5 6.7 %collective-permute-start.14 = (bf16[124,704]{1,0:T(8,128)(2,1)S(1)}, bf16[124,704]{1,0:T(8,128)(2,1)S(1)}, u32[]{:S(2)}, u32[]{:S(2)}) collective-permute-start(bf16[124,704]{1,0:T(8,128)(2,1)S(1)} %slice.467), channel_id=1, source_target_pairs={{0,3},{1,2},{2,1},{3,0},{4,7},{5,6},{6,5},{7,4},{8,11},{9,10},{10,... | collective-permute-start | bytes 523784 | tf_op jit(solution)/shard_map/ppermute | solution.py:59
  47.3 4.1 %collective-permute-start.15 = (bf16[1,7,7,128]{3,2,1,0:T(8,128)(2,1)S(1)}, bf16[1,7,7,128]{3,2,1,0:T(8,128)(2,1)S(1)}, u32[]{:S(2)}, u32[]{:S(2)}) collective-permute-start(bf16[1,7,7,128]{3,2,1,0:T(8,128)(2,1)S(1)} %fusion.84), channel_id=1, source_target_pairs={{0,17},{1,16},{2,19},{3,18},{4,21},{5,20},{6,23},{7,22},{8,25},{9,... | collective-permute-start | bytes 37640 | tf_op jit(solution)/shard_map/ppermute | solution.py:41
  52.9 3.2 %collective-permute-start.16 = (bf16[7,1,7,128]{3,2,1,0:T(8,128)(2,1)S(1)}, bf16[7,1,7,128]{3,2,1,0:T(8,128)(2,1)S(1)}, u32[]{:S(2)}, u32[]{:S(2)}) collective-permute-start(bf16[7,1,7,128]{3,2,1,0:T(8,128)(2,1)S(1)} %slice.744), channel_id=1, source_target_pairs={{0,5},{1,4},{2,7},{3,6},{4,1},{5,0},{6,3},{7,2},{8,13},{9,12},{10,... | collective-permute-start | bytes 37640 | tf_op jit(solution)/shard_map/ppermute | solution.py:41
  53.5 4.0 %collective-permute-start.17 = (bf16[7,1,7,128]{3,2,1,0:T(8,128)(2,1)S(1)}, bf16[7,1,7,128]{3,2,1,0:T(8,128)(2,1)S(1)}, u32[]{:S(2)}, u32[]{:S(2)}) collective-permute-start(bf16[7,1,7,128]{3,2,1,0:T(8,128)(2,1)S(1)} %slice.744), channel_id=1, source_target_pairs={{0,13},{1,12},{2,15},{3,14},{4,9},{5,8},{6,11},{7,10},{8,5},{9,4},... | collective-permute-start | bytes 37640 | tf_op jit(solution)/shard_map/ppermute | solution.py:41
  55.3 3.4 %collective-permute-start.19 = (bf16[252,704]{1,0:T(8,128)(2,1)S(1)}, bf16[252,704]{1,0:T(8,128)(2,1)S(1)}, u32[]{:S(2)}, u32[]{:S(2)}) collective-permute-start(bf16[252,704]{1,0:T(8,128)(2,1)S(1)} %constant_dynamic-update-slice_fusion.6), channel_id=1, source_target_pairs={{0,1},{1,0},{2,3},{3,2},{4,5},{5,4},{6,7},{7,6},{8,9},{9,8},{10,11... | collective-permute-start | bytes 1064456 | tf_op jit(solution)/shard_map/ppermute | solution.py:59
  59.5 4.8 %collective-permute-start.20 = (bf16[212,128]{1,0:T(8,128)(2,1)S(1)}, bf16[212,128]{1,0:T(8,128)(2,1)S(1)}, u32[]{:S(2)}, u32[]{:S(2)}) collective-permute-start(bf16[212,128]{1,0:T(8,128)(2,1)S(1)} %pad_maximum_fusion.10), channel_id=1, source_target_pairs={{0,17},{1,16},{2,19},{3,18},{4,21},{5,20},{6,23},{7,22},{8,25},{9,... | collective-permute-start | bytes 162824 | tf_op jit(solution)/shard_map/ppermute | solution.py:59
  64.4 4.3 %collective-permute-start.21 = (bf16[176,128]{1,0:T(8,128)(2,1)S(1)}, bf16[176,128]{1,0:T(8,128)(2,1)S(1)}, u32[]{:S(2)}, u32[]{:S(2)}) collective-permute-start(bf16[176,128]{1,0:T(8,128)(2,1)S(1)} %add_convert_fusion.2), channel_id=1, source_target_pairs={{0,5},{1,4},{2,7},{3,6},{4,1},{5,0},{6,3},{7,2},{8,13},{9,12},{10,... | collective-permute-start | bytes 135176 | tf_op jit(solution)/shard_map/ppermute | solution.py:41
  68.8 4.5 %collective-permute-start.22 = (bf16[176,128]{1,0:T(8,128)(2,1)S(1)}, bf16[176,128]{1,0:T(8,128)(2,1)S(1)}, u32[]{:S(2)}, u32[]{:S(2)}) collective-permute-start(bf16[176,128]{1,0:T(8,128)(2,1)S(1)} %add_convert_fusion.1), channel_id=1, source_target_pairs={{0,13},{1,12},{2,15},{3,14},{4,9},{5,8},{6,11},{7,10},{8,5},{9,4},... | collective-permute-start | bytes 135176 | tf_op jit(solution)/shard_map/ppermute | solution.py:41
  73.4 4.2 %collective-permute-start.23 = (bf16[284,128]{1,0:T(8,128)(2,1)S(1)}, bf16[284,128]{1,0:T(8,128)(2,1)S(1)}, u32[]{:S(2)}, u32[]{:S(2)}) collective-permute-start(bf16[284,128]{1,0:T(8,128)(2,1)S(1)} %maximum_maximum_fusion.2), channel_id=1, source_target_pairs={{0,3},{1,2},{2,1},{3,0},{4,7},{5,6},{6,5},{7,4},{8,11},{9,10},{10,... | collective-permute-start | bytes 218120 | tf_op jit(solution)/shard_map/ppermute | solution.py:59
  77.8 1.4 %collective-permute-start.24 = (bf16[460,128]{1,0:T(8,128)(2,1)S(1)}, bf16[460,128]{1,0:T(8,128)(2,1)S(1)}, u32[]{:S(2)}, u32[]{:S(2)}) collective-permute-start(bf16[460,128]{1,0:T(8,128)(2,1)S(1)} %maximum_maximum_fusion), channel_id=1, source_target_pairs={{0,1},{1,0},{2,3},{3,2},{4,5},{5,4},{6,7},{7,6},{8,9},{9,8},{10,11... | collective-permute-start | bytes 353288 | tf_op jit(solution)/shard_map/ppermute | solution.py:59

commit v14 on v13

--- a/solution.py
+++ b/solution.py
@@ -206,7 +206,8 @@
     arrived = grid.exchanged(sent, sent, 0, cross=0)[0]
     bottom = jnp.split(arrived[: top.shape[0]], tiles, axis=0)
     bottom = jnp.concatenate(bottom, axis=1)[:, : locked.shape[1]]
-    locked = jnp.concatenate([bottom, locked], axis=0)
+    other_locked = grid.partner(locked, FIRST)
+    other_bottom = grid.partner(bottom, FIRST)
     field = jnp.concatenate(
         [arrived[top.shape[0] :].reshape(1, SIDE, edge, columns), field], axis=0
     )
@@ -214,12 +215,8 @@
     rows = field.reshape(SIDE * SIDE * edge, columns)
     second = by_rows(grid.partner(matrix, SECOND))
     mine, both = to_shares(grid, jnp.pad(rows, ((0, -rows.shape[0] % 16), (0, 0))), other)
-    mine, both = lax.optimization_barrier((mine, both))
+    mine, both, other_locked = lax.optimization_barrier((mine, both, other_locked))
     matrices = [matrix, second, both, other]
-
-    locked, mine = lax.optimization_barrier((locked, mine))
-    parts = [locked[:128], locked[128:]]
-    other_parts = [grid.partner(part, FIRST) for part in parts]
     field = mine[: rows.shape[0]].reshape(SIDE, SIDE, edge, columns)
     low = to_next_partition(plane(field, 2, edge - 1), width)
     field = jnp.concatenate([low, field], axis=2)
@@ -251,10 +248,8 @@
         for dim in (1, 0):
             low, high = plane(partial, dim, 0), plane(partial, dim, SIDE - 1)
             low16, high16 = low.astype(jnp.bfloat16), high.astype(jnp.bfloat16)
-            if step == 1:
-                low16, other_parts[1 - dim] = lax.optimization_barrier(
-                    (low16, other_parts[1 - dim])
-                )
+            if (step, dim) == (1, 1):
+                low16, other_bottom = lax.optimization_barrier((low16, other_bottom))
             to_low, to_high = grid.exchanged(low16, high16, dim)
             partial = with_ends(
                 partial,
@@ -268,7 +263,8 @@
         following = rounded(following)
         older = lax.optimization_barrier(current)
         current = following
-    other_locked = jnp.concatenate(other_parts, axis=0)
+    locked = jnp.concatenate([bottom, locked], axis=0)
+    other_locked = jnp.concatenate([other_bottom, other_locked], axis=0)
     both_locked = [grid.partner(l, SECOND) for l in (locked, other_locked)]
     low = plane(partial, 1, 0).astype(jnp.bfloat16)
     all_locked = [locked, both_locked[0], both_locked[1], other_locked]

time: 81.8 us -> 80.5 us (0.984)
  starting transfers between devices: 26.9 us -> 25.4 us
  local copies, waits for them, and re-layouts: 3.29 us -> 4.35 us
  waiting for transfers between devices: 40 us -> 39 us
    ppermute x12, waiting for transfers between devices: 22.2 us -> 18.3 us  [partner(): lax.ppermute(value, AXIS, [(i, i ^ bits) for i in range(self.devices)])]
    ppermute x13, starting transfers between devices: 21.8 us -> 18.4 us  [swapped(): arrived = lax.ppermute(jnp.where(lower, high, low), AXIS, pairs)]
    ppermute x13, waiting for transfers between devices: 17.8 us -> 20.7 us  [swapped(): arrived = lax.ppermute(jnp.where(lower, high, low), AXIS, pairs)]
    ppermute x12, starting transfers between devices: 5.14 us -> 6.97 us  [partner(): lax.ppermute(value, AXIS, [(i, i ^ bits) for i in range(self.devices)])]
    unnamed x14 -> x19, local copies, waits for them, and re-layouts: 0.09 us -> 1.2 us
  transfers between devices with their start and end apart: 25 -> 25, of which waited for: 20 -> 19; matrix products, arithmetic and copies ran while one was open for 9% -> 9% of each run, Pallas kernels for 0% -> 0%
where the time goes in v14:
time: 80.5 us; the launch traced here: 80.4 us
  waiting for transfers between devices  39 us (48%)
  starting transfers between devices  25.4 us (32%)
  other arithmetic  5.08 us (6%)
  matrix products  4.88 us (6%)
  local copies, waits for them, and re-layouts  4.35 us (5%)
  between operations  1.62 us (2%)
    ppermute x13, waiting for transfers between devices, swapped(): arrived = lax.ppermute(jnp.where(lower, high, low), AXIS, pairs)  20.7 us
    ppermute x13, starting transfers between devices, swapped(): arrived = lax.ppermute(jnp.where(lower, high, low), AXIS, pairs)  18.4 us
    ppermute x12, waiting for transfers between devices, partner(): lax.ppermute(value, AXIS, [(i, i ^ bits) for i in range(self.devices)])  18.3 us
    ppermute x12, starting transfers between devices, partner(): lax.ppermute(value, AXIS, [(i, i ^ bits) for i in range(self.devices)])  6.97 us
    dot_general x12, matrix products, per_device(): jnp.dot(matrices[r], own, preferred_element_type=jnp.float32)  2.93 us
  transfers between devices with their start and end apart: 25, of which 19 were waited for; matrix products, arithmetic and copies ran while one was open for 9% of the time, Pallas kernels for 0%

profile of v14, /device:TPU:0, one launch (start us, length us, event | category | flops | bytes accessed | tf_op | source)
XLA Modules:
  0.0 80.4 jit_solution(2909371251673224323)
XLA Ops:
  0.6 0.9 %reshape.124 = bf16[6,6,6,128]{3,2,1,0:T(8,128)(2,1)S(1)} reshape(bf16[216,128]{1,0:T(8,128)(2,1)} %param.5) | data formatting | bytes 110592 | tf_op jit(solution)/shard_map/reshape | solution.py:193
  1.6 3.0 %collective-permute-start = (bf16[6,1,6,128]{3,2,1,0:T(8,128)(2,1)S(1)}, bf16[6,1,6,128]{3,2,1,0:T(8,128)(2,1)S(1)}, u32[]{:S(2)}, u32[]{:S(2)}) collective-permute-start(bf16[6,1,6,128]{3,2,1,0:T(8,128)(2,1)S(1)} %slice.527), channel_id=1, source_target_pairs={{0,4},{1,5},{2,6},{3,7},{4,0},{5,1},{6,2},{7,3},{8,12},{9,13},{10,... | collective-permute-start | bytes 27656 | tf_op jit(solution)/shard_map/ppermute | solution.py:41
  4.6 1.5 %collective-permute-start.1 = (bf16[6,1,6,128]{3,2,1,0:T(8,128)(2,1)S(1)}, bf16[6,1,6,128]{3,2,1,0:T(8,128)(2,1)S(1)}, u32[]{:S(2)}, u32[]{:S(2)}) collective-permute-start(bf16[6,1,6,128]{3,2,1,0:T(8,128)(2,1)S(1)} %slice.527), channel_id=1, source_target_pairs={{0,12},{1,13},{2,14},{3,15},{4,8},{5,9},{6,10},{7,11},{8,4},{9,5},... | collective-permute-start | bytes 27656 | tf_op jit(solution)/shard_map/ppermute | solution.py:41
  6.2 0.7 fusion
  7.3 1.4 %collective-permute-start.7 = (bf16[216,704]{1,0:T(8,128)(2,1)S(1)}, bf16[216,704]{1,0:T(8,128)(2,1)S(1)}, u32[]{:S(2)}, u32[]{:S(2)}) collective-permute-start(bf16[216,704]{1,0:T(8,128)(2,1)S(1)} %copy-done.1), channel_id=1, source_target_pairs={{0,3},{1,2},{2,1},{3,0},{4,7},{5,6},{6,5},{7,4},{8,11},{9,10},{10,... | collective-permute-start | bytes 912392 | tf_op jit(solution)/shard_map/ppermute | solution.py:59
  9.7 2.7 %collective-permute-start.2 = (bf16[258,128]{1,0:T(8,128)(2,1)S(1)}, bf16[258,128]{1,0:T(8,128)(2,1)S(1)}, u32[]{:S(2)}, u32[]{:S(2)}) collective-permute-start(bf16[258,128]{1,0:T(8,128)(2,1)S(1)} %concatenate.141), channel_id=1, source_target_pairs={{0,16},{1,17},{2,18},{3,19},{4,20},{5,21},{6,22},{7,23},{8,24},{9,... | collective-permute-start | bytes 198152 | tf_op jit(solution)/shard_map/ppermute | solution.py:41
  12.3 2.8 %collective-permute-done.2 = bf16[258,128]{1,0:T(8,128)(2,1)S(1)} collective-permute-done((bf16[258,128]{1,0:T(8,128)(2,1)S(1)}, bf16[258,128]{1,0:T(8,128)(2,1)S(1)}, u32[]{:S(2)}, u32[]{:S(2)}) %collective-permute-start.2) | collective-permute-done | bytes 66080 | tf_op jit(solution)/shard_map/ppermute | solution.py:41
  15.7 7.8 %collective-permute-done.3 = bf16[152,128]{1,0:T(8,128)(2,1)S(1)} collective-permute-done((bf16[152,128]{1,0:T(8,128)(2,1)S(1)}, bf16[152,128]{1,0:T(8,128)(2,1)S(1)}, u32[]{:S(2)}, u32[]{:S(2)}) %collective-permute-start.3) | collective-permute-done | bytes 38944 | tf_op jit(solution)/shard_map/ppermute | solution.py:59
  24.4 0.6 collective-permute-done.5
  27.2 1.4 %collective-permute-start.10 = (bf16[7,1,7,128]{3,2,1,0:T(8,128)(2,1)S(1)}, bf16[7,1,7,128]{3,2,1,0:T(8,128)(2,1)S(1)}, u32[]{:S(2)}, u32[]{:S(2)}) collective-permute-start(bf16[7,1,7,128]{3,2,1,0:T(8,128)(2,1)S(1)} %broadcast_select_fusion.45), channel_id=1, source_target_pairs={{0,13},{1,12},{2,15},{3,14},{4,9},{5,8},{6,11},{7,10},{8,5},{9,4},... | collective-permute-start | bytes 37640 | tf_op jit(solution)/shard_map/ppermute | solution.py:41
  28.9 2.5 %collective-permute-done.10 = bf16[7,1,7,128]{3,2,1,0:T(8,128)(2,1)S(1)} collective-permute-done((bf16[7,1,7,128]{3,2,1,0:T(8,128)(2,1)S(1)}, bf16[7,1,7,128]{3,2,1,0:T(8,128)(2,1)S(1)}, u32[]{:S(2)}, u32[]{:S(2)}) %collective-permute-start.10) | collective-permute-done | bytes 12576 | tf_op jit(solution)/shard_map/ppermute | solution.py:41
  31.9 2.4 %collective-permute-start.11 = (bf16[1,7,7,128]{3,2,1,0:T(8,128)(2,1)S(1)}, bf16[1,7,7,128]{3,2,1,0:T(8,128)(2,1)S(1)}, u32[]{:S(2)}, u32[]{:S(2)}) collective-permute-start(bf16[1,7,7,128]{3,2,1,0:T(8,128)(2,1)S(1)} %fusion.83), channel_id=1, source_target_pairs={{0,17},{1,16},{2,19},{3,18},{4,21},{5,20},{6,23},{7,22},{8,25},{9,... | collective-permute-start | bytes 37640 | tf_op jit(solution)/shard_map/ppermute | solution.py:41
  34.3 1.0 %collective-permute-start.12 = (bf16[36,704]{1,0:T(8,128)(2,1)S(1)}, bf16[36,704]{1,0:T(8,128)(2,1)S(1)}, u32[]{:S(2)}, u32[]{:S(2)}) collective-permute-start(bf16[36,704]{1,0:T(8,128)(2,1)S(1)} %bitcast.30), channel_id=1, source_target_pairs={{0,3},{1,2},{2,1},{3,0},{4,7},{5,6},{6,5},{7,4},{8,11},{9,10},{10,... | collective-permute-start | bytes 152072 | tf_op jit(solution)/shard_map/ppermute | solution.py:59
  35.4 0.6 collective-permute-done.11
  37.6 0.7 collective-permute-done.12
  38.9 1.5 %collective-permute-start.14 = (bf16[7,1,7,128]{3,2,1,0:T(8,128)(2,1)S(1)}, bf16[7,1,7,128]{3,2,1,0:T(8,128)(2,1)S(1)}, u32[]{:S(2)}, u32[]{:S(2)}) collective-permute-start(bf16[7,1,7,128]{3,2,1,0:T(8,128)(2,1)S(1)} %broadcast_select_fusion.44), channel_id=1, source_target_pairs={{0,13},{1,12},{2,15},{3,14},{4,9},{5,8},{6,11},{7,10},{8,5},{9,4},... | collective-permute-start | bytes 37640 | tf_op jit(solution)/shard_map/ppermute | solution.py:41
  40.4 1.3 %collective-permute-start.13 = (bf16[7,1,7,128]{3,2,1,0:T(8,128)(2,1)S(1)}, bf16[7,1,7,128]{3,2,1,0:T(8,128)(2,1)S(1)}, u32[]{:S(2)}, u32[]{:S(2)}) collective-permute-start(bf16[7,1,7,128]{3,2,1,0:T(8,128)(2,1)S(1)} %get-tuple-element.33), channel_id=1, source_target_pairs={{0,5},{1,4},{2,7},{3,6},{4,1},{5,0},{6,3},{7,2},{8,13},{9,12},{10,... | collective-permute-start | bytes 37640 | tf_op jit(solution)/shard_map/ppermute | solution.py:41
  41.7 1.3 %collective-permute-done.14 = bf16[7,1,7,128]{3,2,1,0:T(8,128)(2,1)S(1)} collective-permute-done((bf16[7,1,7,128]{3,2,1,0:T(8,128)(2,1)S(1)}, bf16[7,1,7,128]{3,2,1,0:T(8,128)(2,1)S(1)}, u32[]{:S(2)}, u32[]{:S(2)}) %collective-permute-start.14) | collective-permute-done | bytes 12576 | tf_op jit(solution)/shard_map/ppermute | solution.py:41
  43.7 1.8 %collective-permute-start.15 = (bf16[1,7,7,128]{3,2,1,0:T(8,128)(2,1)S(1)}, bf16[1,7,7,128]{3,2,1,0:T(8,128)(2,1)S(1)}, u32[]{:S(2)}, u32[]{:S(2)}) collective-permute-start(bf16[1,7,7,128]{3,2,1,0:T(8,128)(2,1)S(1)} %fusion.84), channel_id=1, source_target_pairs={{0,17},{1,16},{2,19},{3,18},{4,21},{5,20},{6,23},{7,22},{8,25},{9,... | collective-permute-start | bytes 37640 | tf_op jit(solution)/shard_map/ppermute | solution.py:41
  45.9 1.9 %collective-permute-done.15 = bf16[1,7,7,128]{3,2,1,0:T(8,128)(2,1)S(1)} collective-permute-done((bf16[1,7,7,128]{3,2,1,0:T(8,128)(2,1)S(1)}, bf16[1,7,7,128]{3,2,1,0:T(8,128)(2,1)S(1)}, u32[]{:S(2)}, u32[]{:S(2)}) %collective-permute-start.15) | collective-permute-done | bytes 12576 | tf_op jit(solution)/shard_map/ppermute | solution.py:41
  49.3 1.3 %collective-permute-start.16 = (bf16[7,1,7,128]{3,2,1,0:T(8,128)(2,1)S(1)}, bf16[7,1,7,128]{3,2,1,0:T(8,128)(2,1)S(1)}, u32[]{:S(2)}, u32[]{:S(2)}) collective-permute-start(bf16[7,1,7,128]{3,2,1,0:T(8,128)(2,1)S(1)} %slice.738), channel_id=1, source_target_pairs={{0,5},{1,4},{2,7},{3,6},{4,1},{5,0},{6,3},{7,2},{8,13},{9,12},{10,... | collective-permute-start | bytes 37640 | tf_op jit(solution)/shard_map/ppermute | solution.py:41
  50.7 1.0 %collective-permute-start.17 = (bf16[7,1,7,128]{3,2,1,0:T(8,128)(2,1)S(1)}, bf16[7,1,7,128]{3,2,1,0:T(8,128)(2,1)S(1)}, u32[]{:S(2)}, u32[]{:S(2)}) collective-permute-start(bf16[7,1,7,128]{3,2,1,0:T(8,128)(2,1)S(1)} %slice.738), channel_id=1, source_target_pairs={{0,13},{1,12},{2,15},{3,14},{4,9},{5,8},{6,11},{7,10},{8,5},{9,4},... | collective-permute-start | bytes 37640 | tf_op jit(solution)/shard_map/ppermute | solution.py:41
  52.5 2.2 %collective-permute-done.17 = bf16[7,1,7,128]{3,2,1,0:T(8,128)(2,1)S(1)} collective-permute-done((bf16[7,1,7,128]{3,2,1,0:T(8,128)(2,1)S(1)}, bf16[7,1,7,128]{3,2,1,0:T(8,128)(2,1)S(1)}, u32[]{:S(2)}, u32[]{:S(2)}) %collective-permute-start.17) | collective-permute-done | bytes 12576 | tf_op jit(solution)/shard_map/ppermute | solution.py:41
  57.2 1.7 %collective-permute-start.20 = (bf16[212,128]{1,0:T(8,128)(2,1)S(1)}, bf16[212,128]{1,0:T(8,128)(2,1)S(1)}, u32[]{:S(2)}, u32[]{:S(2)}) collective-permute-start(bf16[212,128]{1,0:T(8,128)(2,1)S(1)} %pad_maximum_fusion.11), channel_id=1, source_target_pairs={{0,17},{1,16},{2,19},{3,18},{4,21},{5,20},{6,23},{7,22},{8,25},{9,... | collective-permute-start | bytes 162824 | tf_op jit(solution)/shard_map/ppermute | solution.py:59
  59.0 4.3 %collective-permute-done.20 = bf16[212,128]{1,0:T(8,128)(2,1)S(1)} collective-permute-done((bf16[212,128]{1,0:T(8,128)(2,1)S(1)}, bf16[212,128]{1,0:T(8,128)(2,1)S(1)}, u32[]{:S(2)}, u32[]{:S(2)}) %collective-permute-start.20) | collective-permute-done | bytes 54304 | tf_op jit(solution)/shard_map/ppermute | solution.py:59
  63.9 3.3 %collective-permute-done.21 = bf16[176,128]{1,0:T(8,128)(2,1)S(1)} collective-permute-done((bf16[176,128]{1,0:T(8,128)(2,1)S(1)}, bf16[176,128]{1,0:T(8,128)(2,1)S(1)}, u32[]{:S(2)}, u32[]{:S(2)}) %collective-permute-start.21) | collective-permute-done | bytes 45088 | tf_op jit(solution)/shard_map/ppermute | solution.py:41
  67.3 4.5 %collective-permute-done.22 = bf16[176,128]{1,0:T(8,128)(2,1)S(1)} collective-permute-done((bf16[176,128]{1,0:T(8,128)(2,1)S(1)}, bf16[176,128]{1,0:T(8,128)(2,1)S(1)}, u32[]{:S(2)}, u32[]{:S(2)}) %collective-permute-start.22) | collective-permute-done | bytes 45088 | tf_op jit(solution)/shard_map/ppermute | solution.py:41
  72.0 0.8 collective-permute-start.23
  72.7 3.5 %collective-permute-done.23 = bf16[284,128]{1,0:T(8,128)(2,1)S(1)} collective-permute-done((bf16[284,128]{1,0:T(8,128)(2,1)S(1)}, bf16[284,128]{1,0:T(8,128)(2,1)S(1)}, u32[]{:S(2)}, u32[]{:S(2)}) %collective-permute-start.23) | collective-permute-done | bytes 72736 | tf_op jit(solution)/shard_map/ppermute | solution.py:59
  76.7 1.2 %collective-permute-done.24 = bf16[460,128]{1,0:T(8,128)(2,1)S(1)} collective-permute-done((bf16[460,128]{1,0:T(8,128)(2,1)S(1)}, bf16[460,128]{1,0:T(8,128)(2,1)S(1)}, u32[]{:S(2)}, u32[]{:S(2)}) %collective-permute-start.24) | collective-permute-done | bytes 117792 | tf_op jit(solution)/shard_map/ppermute | solution.py:59
  78.6 0.7 pad_maximum_fusion.15
  79.4 1.0 %maximum_convert_fusion = f32[704,128]{1,0:T(8,128)} fusion(bf16[176,32]{1,0:T(8,128)(2,1)S(1)} %get-tuple-element.120, bf16[176,32]{1,0:T(8,128)(2,1)S(1)} %get-tuple-element.116, bf16[176,32]{1,0:T(8,128)(2,1)S(1)} %get-tuple-element.112, bf16[176,32]{1,0:T(8,128)(2,1)S(1)} %get-tuple-element.108, bf16[176,32]{1,0:T(8,128)(2,1)S(1)} %get-tuple-element.121, ...), kind=kLoop, calls=%fused_computation.51 | loop fusion | flops 2883584 | bytes 540672 | tf_op jit(solution)/shard_map/convert_element_type | solution.py:332
  (168 shorter events, 15.2 us)
Async XLA Ops:
  0.6 5.5 %copy-start = (bf16[1,343,343]{2,1,0:T(8,128)(2,1)S(1)}, bf16[1,343,343]{2,1,0:T(8,128)(2,1)}, u32[]{:S(2)}) copy-start(bf16[1,343,343]{2,1,0:T(8,128)(2,1)} %param.6) | copy-start | bytes 705898
  1.5 4.6 %copy-start.5 = (s32[1,343]{1,0:T(1,128)S(1)}, s32[1,343]{1,0:T(1,128)}, u32[]{:S(2)}) copy-start(s32[1,343]{1,0:T(1,128)} %param.7) | copy-start | bytes 4120
  1.5 4.6 %copy-start.6 = (f32[343]{0:T(512)S(1)}, f32[343]{0:T(512)}, u32[]{:S(2)}) copy-start(f32[343]{0:T(512)} %param.8) | copy-start | bytes 4120
  1.6 7.4 %collective-permute-start = (bf16[6,1,6,128]{3,2,1,0:T(8,128)(2,1)S(1)}, bf16[6,1,6,128]{3,2,1,0:T(8,128)(2,1)S(1)}, u32[]{:S(2)}, u32[]{:S(2)}) collective-permute-start(bf16[6,1,6,128]{3,2,1,0:T(8,128)(2,1)S(1)} %slice.527), channel_id=1, source_target_pairs={{0,4},{1,5},{2,6},{3,7},{4,0},{5,1},{6,2},{7,3},{8,12},{9,13},{10,... | collective-permute-start | bytes 27656 | tf_op jit(solution)/shard_map/ppermute | solution.py:41
  4.6 4.6 %collective-permute-start.1 = (bf16[6,1,6,128]{3,2,1,0:T(8,128)(2,1)S(1)}, bf16[6,1,6,128]{3,2,1,0:T(8,128)(2,1)S(1)}, u32[]{:S(2)}, u32[]{:S(2)}) collective-permute-start(bf16[6,1,6,128]{3,2,1,0:T(8,128)(2,1)S(1)} %slice.527), channel_id=1, source_target_pairs={{0,12},{1,13},{2,14},{3,15},{4,8},{5,9},{6,10},{7,11},{8,4},{9,5},... | collective-permute-start | bytes 27656 | tf_op jit(solution)/shard_map/ppermute | solution.py:41
  6.2 1.2 %copy-start.1 = (bf16[216,704]{1,0:T(8,128)(2,1)S(1)}, bf16[216,704]{1,0:T(8,128)(2,1)}, u32[]{:S(2)}) copy-start(bf16[216,704]{1,0:T(8,128)(2,1)} %param.9) | copy-start | bytes 912388
  6.9 16.9 %collective-permute-start.4 = (bf16[343,343]{1,0:T(8,128)(2,1)S(1)}, bf16[343,343]{1,0:T(8,128)(2,1)S(1)}, u32[]{:S(2)}, u32[]{:S(2)}) collective-permute-start(bf16[343,343]{1,0:T(8,128)(2,1)S(1)} %fusion), channel_id=1, source_target_pairs={{0,3},{1,2},{2,1},{3,0},{4,7},{5,6},{6,5},{7,4},{8,11},{9,10},{10,... | collective-permute-start | bytes 705902 | tf_op jit(solution)/shard_map/ppermute | solution.py:59
  7.3 18.2 %collective-permute-start.7 = (bf16[216,704]{1,0:T(8,128)(2,1)S(1)}, bf16[216,704]{1,0:T(8,128)(2,1)S(1)}, u32[]{:S(2)}, u32[]{:S(2)}) collective-permute-start(bf16[216,704]{1,0:T(8,128)(2,1)S(1)} %copy-done.1), channel_id=1, source_target_pairs={{0,3},{1,2},{2,1},{3,0},{4,7},{5,6},{6,5},{7,4},{8,11},{9,10},{10,... | collective-permute-start | bytes 912392 | tf_op jit(solution)/shard_map/ppermute | solution.py:59
  9.7 5.5 %collective-permute-start.2 = (bf16[258,128]{1,0:T(8,128)(2,1)S(1)}, bf16[258,128]{1,0:T(8,128)(2,1)S(1)}, u32[]{:S(2)}, u32[]{:S(2)}) collective-permute-start(bf16[258,128]{1,0:T(8,128)(2,1)S(1)} %concatenate.141), channel_id=1, source_target_pairs={{0,16},{1,17},{2,18},{3,19},{4,20},{5,21},{6,22},{7,23},{8,24},{9,... | collective-permute-start | bytes 198152 | tf_op jit(solution)/shard_map/ppermute | solution.py:41
  12.3 14.0 %collective-permute-start.8 = (bf16[343,343]{1,0:T(8,128)(2,1)S(1)}, bf16[343,343]{1,0:T(8,128)(2,1)S(1)}, u32[]{:S(2)}, u32[]{:S(2)}) collective-permute-start(bf16[343,343]{1,0:T(8,128)(2,1)S(1)} %fusion), channel_id=1, source_target_pairs={{0,1},{1,0},{2,3},{3,2},{4,5},{5,4},{6,7},{7,6},{8,9},{9,8},{10,11... | collective-permute-start | bytes 705902 | tf_op jit(solution)/shard_map/ppermute | solution.py:59
  15.6 7.9 %collective-permute-start.3 = (bf16[152,128]{1,0:T(8,128)(2,1)S(1)}, bf16[152,128]{1,0:T(8,128)(2,1)S(1)}, u32[]{:S(2)}, u32[]{:S(2)}) collective-permute-start(bf16[152,128]{1,0:T(8,128)(2,1)S(1)} %pad_maximum_fusion.16), channel_id=1, source_target_pairs={{0,3},{1,2},{2,1},{3,0},{4,7},{5,6},{6,5},{7,4},{8,11},{9,10},{10,... | collective-permute-start | bytes 116744 | tf_op jit(solution)/shard_map/ppermute | solution.py:59
  23.8 1.3 %collective-permute-start.5 = (bf16[152,128]{1,0:T(8,128)(2,1)S(1)}, bf16[152,128]{1,0:T(8,128)(2,1)S(1)}, u32[]{:S(2)}, u32[]{:S(2)}) collective-permute-start(bf16[152,128]{1,0:T(8,128)(2,1)S(1)} %pad_maximum_fusion.17), channel_id=1, source_target_pairs={{0,1},{1,0},{2,3},{3,2},{4,5},{5,4},{6,7},{7,6},{8,9},{9,8},{10,11... | collective-permute-start | bytes 116744 | tf_op jit(solution)/shard_map/ppermute | solution.py:59
  24.0 1.6 %collective-permute-start.6 = (bf16[343,343]{1,0:T(8,128)(2,1)S(1)}, bf16[343,343]{1,0:T(8,128)(2,1)S(1)}, u32[]{:S(2)}, u32[]{:S(2)}) collective-permute-start(bf16[343,343]{1,0:T(8,128)(2,1)S(1)} %collective-permute-done.4), channel_id=1, source_target_pairs={{0,1},{1,0},{2,3},{3,2},{4,5},{5,4},{6,7},{7,6},{8,9},{9,8},{10,11... | collective-permute-start | bytes 705902 | tf_op jit(solution)/shard_map/ppermute | solution.py:59
  27.2 4.1 %collective-permute-start.10 = (bf16[7,1,7,128]{3,2,1,0:T(8,128)(2,1)S(1)}, bf16[7,1,7,128]{3,2,1,0:T(8,128)(2,1)S(1)}, u32[]{:S(2)}, u32[]{:S(2)}) collective-permute-start(bf16[7,1,7,128]{3,2,1,0:T(8,128)(2,1)S(1)} %broadcast_select_fusion.45), channel_id=1, source_target_pairs={{0,13},{1,12},{2,15},{3,14},{4,9},{5,8},{6,11},{7,10},{8,5},{9,4},... | collective-permute-start | bytes 37640 | tf_op jit(solution)/shard_map/ppermute | solution.py:41
  28.7 3.2 %collective-permute-start.9 = (bf16[7,1,7,128]{3,2,1,0:T(8,128)(2,1)S(1)}, bf16[7,1,7,128]{3,2,1,0:T(8,128)(2,1)S(1)}, u32[]{:S(2)}, u32[]{:S(2)}) collective-permute-start(bf16[7,1,7,128]{3,2,1,0:T(8,128)(2,1)S(1)} %get-tuple-element.37), channel_id=1, source_target_pairs={{0,5},{1,4},{2,7},{3,6},{4,1},{5,0},{6,3},{7,2},{8,13},{9,12},{10,... | collective-permute-start | bytes 37640 | tf_op jit(solution)/shard_map/ppermute | solution.py:41
  31.9 4.1 %collective-permute-start.11 = (bf16[1,7,7,128]{3,2,1,0:T(8,128)(2,1)S(1)}, bf16[1,7,7,128]{3,2,1,0:T(8,128)(2,1)S(1)}, u32[]{:S(2)}, u32[]{:S(2)}) collective-permute-start(bf16[1,7,7,128]{3,2,1,0:T(8,128)(2,1)S(1)} %fusion.83), channel_id=1, source_target_pairs={{0,17},{1,16},{2,19},{3,18},{4,21},{5,20},{6,23},{7,22},{8,25},{9,... | collective-permute-start | bytes 37640 | tf_op jit(solution)/shard_map/ppermute | solution.py:41
  34.3 3.9 %collective-permute-start.12 = (bf16[36,704]{1,0:T(8,128)(2,1)S(1)}, bf16[36,704]{1,0:T(8,128)(2,1)S(1)}, u32[]{:S(2)}, u32[]{:S(2)}) collective-permute-start(bf16[36,704]{1,0:T(8,128)(2,1)S(1)} %bitcast.30), channel_id=1, source_target_pairs={{0,3},{1,2},{2,1},{3,0},{4,7},{5,6},{6,5},{7,4},{8,11},{9,10},{10,... | collective-permute-start | bytes 152072 | tf_op jit(solution)/shard_map/ppermute | solution.py:59
  38.3 0.6 copy-start.2
  38.9 4.0 %collective-permute-start.14 = (bf16[7,1,7,128]{3,2,1,0:T(8,128)(2,1)S(1)}, bf16[7,1,7,128]{3,2,1,0:T(8,128)(2,1)S(1)}, u32[]{:S(2)}, u32[]{:S(2)}) collective-permute-start(bf16[7,1,7,128]{3,2,1,0:T(8,128)(2,1)S(1)} %broadcast_select_fusion.44), channel_id=1, source_target_pairs={{0,13},{1,12},{2,15},{3,14},{4,9},{5,8},{6,11},{7,10},{8,5},{9,4},... | collective-permute-start | bytes 37640 | tf_op jit(solution)/shard_map/ppermute | solution.py:41
  40.4 3.2 %collective-permute-start.13 = (bf16[7,1,7,128]{3,2,1,0:T(8,128)(2,1)S(1)}, bf16[7,1,7,128]{3,2,1,0:T(8,128)(2,1)S(1)}, u32[]{:S(2)}, u32[]{:S(2)}) collective-permute-start(bf16[7,1,7,128]{3,2,1,0:T(8,128)(2,1)S(1)} %get-tuple-element.33), channel_id=1, source_target_pairs={{0,5},{1,4},{2,7},{3,6},{4,1},{5,0},{6,3},{7,2},{8,13},{9,12},{10,... | collective-permute-start | bytes 37640 | tf_op jit(solution)/shard_map/ppermute | solution.py:41
  43.7 4.1 %collective-permute-start.15 = (bf16[1,7,7,128]{3,2,1,0:T(8,128)(2,1)S(1)}, bf16[1,7,7,128]{3,2,1,0:T(8,128)(2,1)S(1)}, u32[]{:S(2)}, u32[]{:S(2)}) collective-permute-start(bf16[1,7,7,128]{3,2,1,0:T(8,128)(2,1)S(1)} %fusion.84), channel_id=1, source_target_pairs={{0,17},{1,16},{2,19},{3,18},{4,21},{5,20},{6,23},{7,22},{8,25},{9,... | collective-permute-start | bytes 37640 | tf_op jit(solution)/shard_map/ppermute | solution.py:41
  45.6 10.5 %collective-permute-start.18 = (bf16[252,704]{1,0:T(8,128)(2,1)S(1)}, bf16[252,704]{1,0:T(8,128)(2,1)S(1)}, u32[]{:S(2)}, u32[]{:S(2)}) collective-permute-start(bf16[252,704]{1,0:T(8,128)(2,1)S(1)} %pad_maximum_fusion), channel_id=1, source_target_pairs={{0,1},{1,0},{2,3},{3,2},{4,5},{5,4},{6,7},{7,6},{8,9},{9,8},{10,11... | collective-permute-start | bytes 1064456 | tf_op jit(solution)/shard_map/ppermute | solution.py:59
  49.2 2.5 %copy-start.3 = (bf16[36,704]{1,0:T(8,128)(2,1)S(1)}, bf16[36,704]{1,0:T(8,128)(2,1)}, u32[]{:S(2)}) copy-start(bf16[36,704]{1,0:T(8,128)(2,1)} %copy-done.2) | copy-start | bytes 152068
  49.3 3.2 %collective-permute-start.16 = (bf16[7,1,7,128]{3,2,1,0:T(8,128)(2,1)S(1)}, bf16[7,1,7,128]{3,2,1,0:T(8,128)(2,1)S(1)}, u32[]{:S(2)}, u32[]{:S(2)}) collective-permute-start(bf16[7,1,7,128]{3,2,1,0:T(8,128)(2,1)S(1)} %slice.738), channel_id=1, source_target_pairs={{0,5},{1,4},{2,7},{3,6},{4,1},{5,0},{6,3},{7,2},{8,13},{9,12},{10,... | collective-permute-start | bytes 37640 | tf_op jit(solution)/shard_map/ppermute | solution.py:41
  50.7 4.0 %collective-permute-start.17 = (bf16[7,1,7,128]{3,2,1,0:T(8,128)(2,1)S(1)}, bf16[7,1,7,128]{3,2,1,0:T(8,128)(2,1)S(1)}, u32[]{:S(2)}, u32[]{:S(2)}) collective-permute-start(bf16[7,1,7,128]{3,2,1,0:T(8,128)(2,1)S(1)} %slice.738), channel_id=1, source_target_pairs={{0,13},{1,12},{2,15},{3,14},{4,9},{5,8},{6,11},{7,10},{8,5},{9,4},... | collective-permute-start | bytes 37640 | tf_op jit(solution)/shard_map/ppermute | solution.py:41
  51.8 4.6 %collective-permute-start.19 = (bf16[252,704]{1,0:T(8,128)(2,1)S(1)}, bf16[252,704]{1,0:T(8,128)(2,1)S(1)}, u32[]{:S(2)}, u32[]{:S(2)}) collective-permute-start(bf16[252,704]{1,0:T(8,128)(2,1)S(1)} %pad_maximum_fusion.1), channel_id=1, source_target_pairs={{0,1},{1,0},{2,3},{3,2},{4,5},{5,4},{6,7},{7,6},{8,9},{9,8},{10,11... | collective-permute-start | bytes 1064456 | tf_op jit(solution)/shard_map/ppermute | solution.py:59
  54.9 0.8 %copy-start.4 = (bf16[36,704]{1,0:T(8,128)(2,1)S(1)}, bf16[36,704]{1,0:T(8,128)(2,1)}, u32[]{:S(2)}) copy-start(bf16[36,704]{1,0:T(8,128)(2,1)} %copy-done.2) | copy-start | bytes 152068
  57.2 6.1 %collective-permute-start.20 = (bf16[212,128]{1,0:T(8,128)(2,1)S(1)}, bf16[212,128]{1,0:T(8,128)(2,1)S(1)}, u32[]{:S(2)}, u32[]{:S(2)}) collective-permute-start(bf16[212,128]{1,0:T(8,128)(2,1)S(1)} %pad_maximum_fusion.11), channel_id=1, source_target_pairs={{0,17},{1,16},{2,19},{3,18},{4,21},{5,20},{6,23},{7,22},{8,25},{9,... | collective-permute-start | bytes 162824 | tf_op jit(solution)/shard_map/ppermute | solution.py:59
  63.5 3.7 %collective-permute-start.21 = (bf16[176,128]{1,0:T(8,128)(2,1)S(1)}, bf16[176,128]{1,0:T(8,128)(2,1)S(1)}, u32[]{:S(2)}, u32[]{:S(2)}) collective-permute-start(bf16[176,128]{1,0:T(8,128)(2,1)S(1)} %add_convert_fusion.2), channel_id=1, source_target_pairs={{0,5},{1,4},{2,7},{3,6},{4,1},{5,0},{6,3},{7,2},{8,13},{9,12},{10,... | collective-permute-start | bytes 135176 | tf_op jit(solution)/shard_map/ppermute | solution.py:41
  67.2 4.6 %collective-permute-start.22 = (bf16[176,128]{1,0:T(8,128)(2,1)S(1)}, bf16[176,128]{1,0:T(8,128)(2,1)S(1)}, u32[]{:S(2)}, u32[]{:S(2)}) collective-permute-start(bf16[176,128]{1,0:T(8,128)(2,1)S(1)} %add_convert_fusion.1), channel_id=1, source_target_pairs={{0,13},{1,12},{2,15},{3,14},{4,9},{5,8},{6,11},{7,10},{8,5},{9,4},... | collective-permute-start | bytes 135176 | tf_op jit(solution)/shard_map/ppermute | solution.py:41
  72.0 4.3 %collective-permute-start.23 = (bf16[284,128]{1,0:T(8,128)(2,1)S(1)}, bf16[284,128]{1,0:T(8,128)(2,1)S(1)}, u32[]{:S(2)}, u32[]{:S(2)}) collective-permute-start(bf16[284,128]{1,0:T(8,128)(2,1)S(1)} %maximum_maximum_fusion.2), channel_id=1, source_target_pairs={{0,3},{1,2},{2,1},{3,0},{4,7},{5,6},{6,5},{7,4},{8,11},{9,10},{10,... | collective-permute-start | bytes 218120 | tf_op jit(solution)/shard_map/ppermute | solution.py:59
  76.5 1.4 %collective-permute-start.24 = (bf16[460,128]{1,0:T(8,128)(2,1)S(1)}, bf16[460,128]{1,0:T(8,128)(2,1)S(1)}, u32[]{:S(2)}, u32[]{:S(2)}) collective-permute-start(bf16[460,128]{1,0:T(8,128)(2,1)S(1)} %maximum_maximum_fusion), channel_id=1, source_target_pairs={{0,1},{1,0},{2,3},{3,2},{4,5},{5,4},{6,7},{7,6},{8,9},{9,8},{10,11... | collective-permute-start | bytes 353288 | tf_op jit(solution)/shard_map/ppermute | solution.py:59

commit v15 on v14

--- a/solution.py
+++ b/solution.py
@@ -206,8 +206,9 @@
     arrived = grid.exchanged(sent, sent, 0, cross=0)[0]
     bottom = jnp.split(arrived[: top.shape[0]], tiles, axis=0)
     bottom = jnp.concatenate(bottom, axis=1)[:, : locked.shape[1]]
-    other_locked = grid.partner(locked, FIRST)
-    other_bottom = grid.partner(bottom, FIRST)
+    cut = max(0, 128 - bottom.shape[0])
+    other_late = grid.partner(jnp.concatenate([bottom, locked[:cut]], axis=0), FIRST)
+    other_early = grid.partner(locked[cut:], FIRST)
     field = jnp.concatenate(
         [arrived[top.shape[0] :].reshape(1, SIDE, edge, columns), field], axis=0
     )
@@ -215,7 +216,7 @@
     rows = field.reshape(SIDE * SIDE * edge, columns)
     second = by_rows(grid.partner(matrix, SECOND))
     mine, both = to_shares(grid, jnp.pad(rows, ((0, -rows.shape[0] % 16), (0, 0))), other)
-    mine, both, other_locked = lax.optimization_barrier((mine, both, other_locked))
+    mine, both, other_early = lax.optimization_barrier((mine, both, other_early))
     matrices = [matrix, second, both, other]
     field = mine[: rows.shape[0]].reshape(SIDE, SIDE, edge, columns)
     low = to_next_partition(plane(field, 2, edge - 1), width)
@@ -248,8 +249,6 @@
         for dim in (1, 0):
             low, high = plane(partial, dim, 0), plane(partial, dim, SIDE - 1)
             low16, high16 = low.astype(jnp.bfloat16), high.astype(jnp.bfloat16)
-            if (step, dim) == (1, 1):
-                low16, other_bottom = lax.optimization_barrier((low16, other_bottom))
             to_low, to_high = grid.exchanged(low16, high16, dim)
             partial = with_ends(
                 partial,
@@ -264,7 +263,7 @@
         older = lax.optimization_barrier(current)
         current = following
     locked = jnp.concatenate([bottom, locked], axis=0)
-    other_locked = jnp.concatenate([other_bottom, other_locked], axis=0)
+    other_locked = jnp.concatenate([other_late, other_early], axis=0)
     both_locked = [grid.partner(l, SECOND) for l in (locked, other_locked)]
     low = plane(partial, 1, 0).astype(jnp.bfloat16)
     all_locked = [locked, both_locked[0], both_locked[1], other_locked]

time: 80.5 us -> 76.6 us (0.952)
  waiting for transfers between devices: 39 us -> 33.7 us
  starting transfers between devices: 25.4 us -> 27.3 us
    ppermute x13, waiting for transfers between devices: 20.7 us -> 17.5 us  [swapped(): arrived = lax.ppermute(jnp.where(lower, high, low), AXIS, pairs)]
    ppermute x12, waiting for transfers between devices: 18.3 us -> 16.2 us  [partner(): lax.ppermute(value, AXIS, [(i, i ^ bits) for i in range(self.devices)])]
    ppermute x13, starting transfers between devices: 18.4 us -> 19.7 us  [swapped(): arrived = lax.ppermute(jnp.where(lower, high, low), AXIS, pairs)]
  transfers between devices with their start and end apart: 25 -> 25, of which waited for: 19 -> 17; matrix products, arithmetic and copies ran while one was open for 9% -> 10% of each run, Pallas kernels for 0% -> 0%
where the time goes in v15:
time: 76.6 us; the launch traced here: 76.5 us
  waiting for transfers between devices  33.7 us (44%)
  starting transfers between devices  27.3 us (36%)
  other arithmetic  5.04 us (7%)
  matrix products  4.87 us (6%)
  local copies, waits for them, and re-layouts  3.97 us (5%)
  between operations  1.66 us (2%)
    ppermute x13, starting transfers between devices, swapped(): arrived = lax.ppermute(jnp.where(lower, high, low), AXIS, pairs)  19.7 us
    ppermute x13, waiting for transfers between devices, swapped(): arrived = lax.ppermute(jnp.where(lower, high, low), AXIS, pairs)  17.5 us
    ppermute x12, waiting for transfers between devices, partner(): lax.ppermute(value, AXIS, [(i, i ^ bits) for i in range(self.devices)])  16.2 us
    ppermute x12, starting transfers between devices, partner(): lax.ppermute(value, AXIS, [(i, i ^ bits) for i in range(self.devices)])  7.54 us
    dot_general x12, matrix products, per_device(): jnp.dot(matrices[r], own, preferred_element_type=jnp.float32)  2.94 us
  transfers between devices with their start and end apart: 25, of which 17 were waited for; matrix products, arithmetic and copies ran while one was open for 10% of the time, Pallas kernels for 0%

profile of v15, /device:TPU:0, one launch (start us, length us, event | category | flops | bytes accessed | tf_op | source)
XLA Modules:
  0.0 76.5 jit_solution(14032767566721077947)
XLA Ops:
  0.6 0.9 %reshape.124 = bf16[6,6,6,128]{3,2,1,0:T(8,128)(2,1)S(1)} reshape(bf16[216,128]{1,0:T(8,128)(2,1)} %param.5) | data formatting | bytes 110592 | tf_op jit(solution)/shard_map/reshape | solution.py:193
  1.6 3.0 %collective-permute-start = (bf16[6,1,6,128]{3,2,1,0:T(8,128)(2,1)S(1)}, bf16[6,1,6,128]{3,2,1,0:T(8,128)(2,1)S(1)}, u32[]{:S(2)}, u32[]{:S(2)}) collective-permute-start(bf16[6,1,6,128]{3,2,1,0:T(8,128)(2,1)S(1)} %slice.535), channel_id=1, source_target_pairs={{0,4},{1,5},{2,6},{3,7},{4,0},{5,1},{6,2},{7,3},{8,12},{9,13},{10,... | collective-permute-start | bytes 27656 | tf_op jit(solution)/shard_map/ppermute | solution.py:41
  4.6 1.5 %collective-permute-start.1 = (bf16[6,1,6,128]{3,2,1,0:T(8,128)(2,1)S(1)}, bf16[6,1,6,128]{3,2,1,0:T(8,128)(2,1)S(1)}, u32[]{:S(2)}, u32[]{:S(2)}) collective-permute-start(bf16[6,1,6,128]{3,2,1,0:T(8,128)(2,1)S(1)} %slice.535), channel_id=1, source_target_pairs={{0,12},{1,13},{2,14},{3,15},{4,8},{5,9},{6,10},{7,11},{8,4},{9,5},... | collective-permute-start | bytes 27656 | tf_op jit(solution)/shard_map/ppermute | solution.py:41
  6.2 0.7 fusion
  7.4 1.4 %collective-permute-start.7 = (bf16[124,704]{1,0:T(8,128)(2,1)S(1)}, bf16[124,704]{1,0:T(8,128)(2,1)S(1)}, u32[]{:S(2)}, u32[]{:S(2)}) collective-permute-start(bf16[124,704]{1,0:T(8,128)(2,1)S(1)} %slice.443), channel_id=1, source_target_pairs={{0,3},{1,2},{2,1},{3,0},{4,7},{5,6},{6,5},{7,4},{8,11},{9,10},{10,... | collective-permute-start | bytes 523784 | tf_op jit(solution)/shard_map/ppermute | solution.py:59
  9.7 2.7 %collective-permute-start.2 = (bf16[258,128]{1,0:T(8,128)(2,1)S(1)}, bf16[258,128]{1,0:T(8,128)(2,1)S(1)}, u32[]{:S(2)}, u32[]{:S(2)}) collective-permute-start(bf16[258,128]{1,0:T(8,128)(2,1)S(1)} %concatenate.144), channel_id=1, source_target_pairs={{0,16},{1,17},{2,18},{3,19},{4,20},{5,21},{6,22},{7,23},{8,24},{9,... | collective-permute-start | bytes 198152 | tf_op jit(solution)/shard_map/ppermute | solution.py:41
  12.3 2.9 %collective-permute-done.2 = bf16[258,128]{1,0:T(8,128)(2,1)S(1)} collective-permute-done((bf16[258,128]{1,0:T(8,128)(2,1)S(1)}, bf16[258,128]{1,0:T(8,128)(2,1)S(1)}, u32[]{:S(2)}, u32[]{:S(2)}) %collective-permute-start.2) | collective-permute-done | bytes 66080 | tf_op jit(solution)/shard_map/ppermute | solution.py:41
  15.9 4.8 %collective-permute-done.3 = bf16[152,128]{1,0:T(8,128)(2,1)S(1)} collective-permute-done((bf16[152,128]{1,0:T(8,128)(2,1)S(1)}, bf16[152,128]{1,0:T(8,128)(2,1)S(1)}, u32[]{:S(2)}, u32[]{:S(2)}) %collective-permute-start.3) | collective-permute-done | bytes 38944 | tf_op jit(solution)/shard_map/ppermute | solution.py:59
  21.5 0.7 collective-permute-done.5
  24.3 1.4 %collective-permute-start.10 = (bf16[7,1,7,128]{3,2,1,0:T(8,128)(2,1)S(1)}, bf16[7,1,7,128]{3,2,1,0:T(8,128)(2,1)S(1)}, u32[]{:S(2)}, u32[]{:S(2)}) collective-permute-start(bf16[7,1,7,128]{3,2,1,0:T(8,128)(2,1)S(1)} %broadcast_select_fusion.45), channel_id=1, source_target_pairs={{0,13},{1,12},{2,15},{3,14},{4,9},{5,8},{6,11},{7,10},{8,5},{9,4},... | collective-permute-start | bytes 37640 | tf_op jit(solution)/shard_map/ppermute | solution.py:41
  25.9 2.5 %collective-permute-done.10 = bf16[7,1,7,128]{3,2,1,0:T(8,128)(2,1)S(1)} collective-permute-done((bf16[7,1,7,128]{3,2,1,0:T(8,128)(2,1)S(1)}, bf16[7,1,7,128]{3,2,1,0:T(8,128)(2,1)S(1)}, u32[]{:S(2)}, u32[]{:S(2)}) %collective-permute-start.10) | collective-permute-done | bytes 12576 | tf_op jit(solution)/shard_map/ppermute | solution.py:41
  29.0 2.6 %collective-permute-start.11 = (bf16[1,7,7,128]{3,2,1,0:T(8,128)(2,1)S(1)}, bf16[1,7,7,128]{3,2,1,0:T(8,128)(2,1)S(1)}, u32[]{:S(2)}, u32[]{:S(2)}) collective-permute-start(bf16[1,7,7,128]{3,2,1,0:T(8,128)(2,1)S(1)} %fusion.83), channel_id=1, source_target_pairs={{0,17},{1,16},{2,19},{3,18},{4,21},{5,20},{6,23},{7,22},{8,25},{9,... | collective-permute-start | bytes 37640 | tf_op jit(solution)/shard_map/ppermute | solution.py:41
  32.1 1.0 %collective-permute-done.11 = bf16[1,7,7,128]{3,2,1,0:T(8,128)(2,1)S(1)} collective-permute-done((bf16[1,7,7,128]{3,2,1,0:T(8,128)(2,1)S(1)}, bf16[1,7,7,128]{3,2,1,0:T(8,128)(2,1)S(1)}, u32[]{:S(2)}, u32[]{:S(2)}) %collective-permute-start.11) | collective-permute-done | bytes 12576 | tf_op jit(solution)/shard_map/ppermute | solution.py:41
  34.7 1.4 %collective-permute-start.13 = (bf16[7,1,7,128]{3,2,1,0:T(8,128)(2,1)S(1)}, bf16[7,1,7,128]{3,2,1,0:T(8,128)(2,1)S(1)}, u32[]{:S(2)}, u32[]{:S(2)}) collective-permute-start(bf16[7,1,7,128]{3,2,1,0:T(8,128)(2,1)S(1)} %broadcast_select_fusion.44), channel_id=1, source_target_pairs={{0,13},{1,12},{2,15},{3,14},{4,9},{5,8},{6,11},{7,10},{8,5},{9,4},... | collective-permute-start | bytes 37640 | tf_op jit(solution)/shard_map/ppermute | solution.py:41
  36.1 1.4 %collective-permute-start.12 = (bf16[7,1,7,128]{3,2,1,0:T(8,128)(2,1)S(1)}, bf16[7,1,7,128]{3,2,1,0:T(8,128)(2,1)S(1)}, u32[]{:S(2)}, u32[]{:S(2)}) collective-permute-start(bf16[7,1,7,128]{3,2,1,0:T(8,128)(2,1)S(1)} %get-tuple-element.29), channel_id=1, source_target_pairs={{0,5},{1,4},{2,7},{3,6},{4,1},{5,0},{6,3},{7,2},{8,13},{9,12},{10,... | collective-permute-start | bytes 37640 | tf_op jit(solution)/shard_map/ppermute | solution.py:41
  37.5 0.8 %collective-permute-start.18 = (bf16[128,704]{1,0:T(8,128)(2,1)S(1)}, bf16[128,704]{1,0:T(8,128)(2,1)S(1)}, u32[]{:S(2)}, u32[]{:S(2)}) collective-permute-start(bf16[128,704]{1,0:T(8,128)(2,1)S(1)} %pad_maximum_fusion.2), channel_id=1, source_target_pairs={{0,3},{1,2},{2,1},{3,0},{4,7},{5,6},{6,5},{7,4},{8,11},{9,10},{10,... | collective-permute-start | bytes 540680 | tf_op jit(solution)/shard_map/ppermute | solution.py:59
  39.4 2.5 %collective-permute-start.14 = (bf16[1,7,7,128]{3,2,1,0:T(8,128)(2,1)S(1)}, bf16[1,7,7,128]{3,2,1,0:T(8,128)(2,1)S(1)}, u32[]{:S(2)}, u32[]{:S(2)}) collective-permute-start(bf16[1,7,7,128]{3,2,1,0:T(8,128)(2,1)S(1)} %fusion.84), channel_id=1, source_target_pairs={{0,17},{1,16},{2,19},{3,18},{4,21},{5,20},{6,23},{7,22},{8,25},{9,... | collective-permute-start | bytes 37640 | tf_op jit(solution)/shard_map/ppermute | solution.py:41
  42.0 2.4 %collective-permute-done.18 = bf16[128,704]{1,0:T(8,128)(2,1)S(1)} collective-permute-done((bf16[128,704]{1,0:T(8,128)(2,1)S(1)}, bf16[128,704]{1,0:T(8,128)(2,1)S(1)}, u32[]{:S(2)}, u32[]{:S(2)}) %collective-permute-start.18) | collective-permute-done | bytes 180256 | tf_op jit(solution)/shard_map/ppermute | solution.py:59
  46.7 1.0 %collective-permute-start.16 = (bf16[7,1,7,128]{3,2,1,0:T(8,128)(2,1)S(1)}, bf16[7,1,7,128]{3,2,1,0:T(8,128)(2,1)S(1)}, u32[]{:S(2)}, u32[]{:S(2)}) collective-permute-start(bf16[7,1,7,128]{3,2,1,0:T(8,128)(2,1)S(1)} %slice.746), channel_id=1, source_target_pairs={{0,13},{1,12},{2,15},{3,14},{4,9},{5,8},{6,11},{7,10},{8,5},{9,4},... | collective-permute-start | bytes 37640 | tf_op jit(solution)/shard_map/ppermute | solution.py:41
  48.0 1.2 %collective-permute-done.15 = bf16[7,1,7,128]{3,2,1,0:T(8,128)(2,1)S(1)} collective-permute-done((bf16[7,1,7,128]{3,2,1,0:T(8,128)(2,1)S(1)}, bf16[7,1,7,128]{3,2,1,0:T(8,128)(2,1)S(1)}, u32[]{:S(2)}, u32[]{:S(2)}) %collective-permute-start.15) | collective-permute-done | bytes 12576 | tf_op jit(solution)/shard_map/ppermute | solution.py:41
  49.2 1.5 %collective-permute-done.16 = bf16[7,1,7,128]{3,2,1,0:T(8,128)(2,1)S(1)} collective-permute-done((bf16[7,1,7,128]{3,2,1,0:T(8,128)(2,1)S(1)}, bf16[7,1,7,128]{3,2,1,0:T(8,128)(2,1)S(1)}, u32[]{:S(2)}, u32[]{:S(2)}) %collective-permute-start.16) | collective-permute-done | bytes 12576 | tf_op jit(solution)/shard_map/ppermute | solution.py:41
  51.3 0.7 copy-done.2
  53.4 2.4 %collective-permute-start.20 = (bf16[212,128]{1,0:T(8,128)(2,1)S(1)}, bf16[212,128]{1,0:T(8,128)(2,1)S(1)}, u32[]{:S(2)}, u32[]{:S(2)}) collective-permute-start(bf16[212,128]{1,0:T(8,128)(2,1)S(1)} %pad_maximum_fusion.11), channel_id=1, source_target_pairs={{0,17},{1,16},{2,19},{3,18},{4,21},{5,20},{6,23},{7,22},{8,25},{9,... | collective-permute-start | bytes 162824 | tf_op jit(solution)/shard_map/ppermute | solution.py:59
  55.9 3.6 %collective-permute-done.20 = bf16[212,128]{1,0:T(8,128)(2,1)S(1)} collective-permute-done((bf16[212,128]{1,0:T(8,128)(2,1)S(1)}, bf16[212,128]{1,0:T(8,128)(2,1)S(1)}, u32[]{:S(2)}, u32[]{:S(2)}) %collective-permute-start.20) | collective-permute-done | bytes 54304 | tf_op jit(solution)/shard_map/ppermute | solution.py:59
  59.6 0.9 %collective-permute-start.21 = (bf16[176,128]{1,0:T(8,128)(2,1)S(1)}, bf16[176,128]{1,0:T(8,128)(2,1)S(1)}, u32[]{:S(2)}, u32[]{:S(2)}) collective-permute-start(bf16[176,128]{1,0:T(8,128)(2,1)S(1)} %add_convert_fusion.2), channel_id=1, source_target_pairs={{0,5},{1,4},{2,7},{3,6},{4,1},{5,0},{6,3},{7,2},{8,13},{9,12},{10,... | collective-permute-start | bytes 135176 | tf_op jit(solution)/shard_map/ppermute | solution.py:41
  60.7 2.6 %collective-permute-done.21 = bf16[176,128]{1,0:T(8,128)(2,1)S(1)} collective-permute-done((bf16[176,128]{1,0:T(8,128)(2,1)S(1)}, bf16[176,128]{1,0:T(8,128)(2,1)S(1)}, u32[]{:S(2)}, u32[]{:S(2)}) %collective-permute-start.21) | collective-permute-done | bytes 45088 | tf_op jit(solution)/shard_map/ppermute | solution.py:41
  63.7 4.2 %collective-permute-done.22 = bf16[176,128]{1,0:T(8,128)(2,1)S(1)} collective-permute-done((bf16[176,128]{1,0:T(8,128)(2,1)S(1)}, bf16[176,128]{1,0:T(8,128)(2,1)S(1)}, u32[]{:S(2)}, u32[]{:S(2)}) %collective-permute-start.22) | collective-permute-done | bytes 45088 | tf_op jit(solution)/shard_map/ppermute | solution.py:41
  68.1 0.9 %collective-permute-start.23 = (bf16[284,128]{1,0:T(8,128)(2,1)S(1)}, bf16[284,128]{1,0:T(8,128)(2,1)S(1)}, u32[]{:S(2)}, u32[]{:S(2)}) collective-permute-start(bf16[284,128]{1,0:T(8,128)(2,1)S(1)} %maximum_maximum_fusion.2), channel_id=1, source_target_pairs={{0,3},{1,2},{2,1},{3,0},{4,7},{5,6},{6,5},{7,4},{8,11},{9,10},{10,... | collective-permute-start | bytes 218120 | tf_op jit(solution)/shard_map/ppermute | solution.py:59
  69.0 3.4 %collective-permute-done.23 = bf16[284,128]{1,0:T(8,128)(2,1)S(1)} collective-permute-done((bf16[284,128]{1,0:T(8,128)(2,1)S(1)}, bf16[284,128]{1,0:T(8,128)(2,1)S(1)}, u32[]{:S(2)}, u32[]{:S(2)}) %collective-permute-start.23) | collective-permute-done | bytes 72736 | tf_op jit(solution)/shard_map/ppermute | solution.py:59
  72.8 1.2 %collective-permute-done.24 = bf16[460,128]{1,0:T(8,128)(2,1)S(1)} collective-permute-done((bf16[460,128]{1,0:T(8,128)(2,1)S(1)}, bf16[460,128]{1,0:T(8,128)(2,1)S(1)}, u32[]{:S(2)}, u32[]{:S(2)}) %collective-permute-start.24) | collective-permute-done | bytes 117792 | tf_op jit(solution)/shard_map/ppermute | solution.py:59
  74.8 0.7 pad_maximum_fusion.15
  75.5 1.0 %maximum_convert_fusion = f32[704,128]{1,0:T(8,128)} fusion(bf16[176,32]{1,0:T(8,128)(2,1)S(1)} %get-tuple-element.115, bf16[176,32]{1,0:T(8,128)(2,1)S(1)} %get-tuple-element.111, bf16[176,32]{1,0:T(8,128)(2,1)S(1)} %get-tuple-element.107, bf16[176,32]{1,0:T(8,128)(2,1)S(1)} %get-tuple-element.103, bf16[176,32]{1,0:T(8,128)(2,1)S(1)} %get-tuple-element.116, ...), kind=kLoop, calls=%fused_computation.51 | loop fusion | flops 2883584 | bytes 540672 | tf_op jit(solution)/shard_map/convert_element_type | solution.py:331
  (168 shorter events, 14.7 us)
Async XLA Ops:
  0.6 5.5 %copy-start = (bf16[1,343,343]{2,1,0:T(8,128)(2,1)S(1)}, bf16[1,343,343]{2,1,0:T(8,128)(2,1)}, u32[]{:S(2)}) copy-start(bf16[1,343,343]{2,1,0:T(8,128)(2,1)} %param.6) | copy-start | bytes 705898
  1.5 4.6 %copy-start.3 = (s32[1,343]{1,0:T(1,128)S(1)}, s32[1,343]{1,0:T(1,128)}, u32[]{:S(2)}) copy-start(s32[1,343]{1,0:T(1,128)} %param.7) | copy-start | bytes 4120
  1.5 4.6 %copy-start.4 = (f32[343]{0:T(512)S(1)}, f32[343]{0:T(512)}, u32[]{:S(2)}) copy-start(f32[343]{0:T(512)} %param.8) | copy-start | bytes 4120
  1.6 7.5 %collective-permute-start = (bf16[6,1,6,128]{3,2,1,0:T(8,128)(2,1)S(1)}, bf16[6,1,6,128]{3,2,1,0:T(8,128)(2,1)S(1)}, u32[]{:S(2)}, u32[]{:S(2)}) collective-permute-start(bf16[6,1,6,128]{3,2,1,0:T(8,128)(2,1)S(1)} %slice.535), channel_id=1, source_target_pairs={{0,4},{1,5},{2,6},{3,7},{4,0},{5,1},{6,2},{7,3},{8,12},{9,13},{10,... | collective-permute-start | bytes 27656 | tf_op jit(solution)/shard_map/ppermute | solution.py:41
  4.6 4.6 %collective-permute-start.1 = (bf16[6,1,6,128]{3,2,1,0:T(8,128)(2,1)S(1)}, bf16[6,1,6,128]{3,2,1,0:T(8,128)(2,1)S(1)}, u32[]{:S(2)}, u32[]{:S(2)}) collective-permute-start(bf16[6,1,6,128]{3,2,1,0:T(8,128)(2,1)S(1)} %slice.535), channel_id=1, source_target_pairs={{0,12},{1,13},{2,14},{3,15},{4,8},{5,9},{6,10},{7,11},{8,4},{9,5},... | collective-permute-start | bytes 27656 | tf_op jit(solution)/shard_map/ppermute | solution.py:41
  6.2 1.2 %copy-start.1 = (bf16[216,704]{1,0:T(8,128)(2,1)S(1)}, bf16[216,704]{1,0:T(8,128)(2,1)}, u32[]{:S(2)}) copy-start(bf16[216,704]{1,0:T(8,128)(2,1)} %param.9) | copy-start | bytes 912388
  6.9 14.0 %collective-permute-start.4 = (bf16[343,343]{1,0:T(8,128)(2,1)S(1)}, bf16[343,343]{1,0:T(8,128)(2,1)S(1)}, u32[]{:S(2)}, u32[]{:S(2)}) collective-permute-start(bf16[343,343]{1,0:T(8,128)(2,1)S(1)} %fusion), channel_id=1, source_target_pairs={{0,3},{1,2},{2,1},{3,0},{4,7},{5,6},{6,5},{7,4},{8,11},{9,10},{10,... | collective-permute-start | bytes 705902 | tf_op jit(solution)/shard_map/ppermute | solution.py:59
  7.4 15.2 %collective-permute-start.7 = (bf16[124,704]{1,0:T(8,128)(2,1)S(1)}, bf16[124,704]{1,0:T(8,128)(2,1)S(1)}, u32[]{:S(2)}, u32[]{:S(2)}) collective-permute-start(bf16[124,704]{1,0:T(8,128)(2,1)S(1)} %slice.443), channel_id=1, source_target_pairs={{0,3},{1,2},{2,1},{3,0},{4,7},{5,6},{6,5},{7,4},{8,11},{9,10},{10,... | collective-permute-start | bytes 523784 | tf_op jit(solution)/shard_map/ppermute | solution.py:59
  9.7 5.6 %collective-permute-start.2 = (bf16[258,128]{1,0:T(8,128)(2,1)S(1)}, bf16[258,128]{1,0:T(8,128)(2,1)S(1)}, u32[]{:S(2)}, u32[]{:S(2)}) collective-permute-start(bf16[258,128]{1,0:T(8,128)(2,1)S(1)} %concatenate.144), channel_id=1, source_target_pairs={{0,16},{1,17},{2,18},{3,19},{4,20},{5,21},{6,22},{7,23},{8,24},{9,... | collective-permute-start | bytes 198152 | tf_op jit(solution)/shard_map/ppermute | solution.py:41
  12.3 11.1 %collective-permute-start.8 = (bf16[343,343]{1,0:T(8,128)(2,1)S(1)}, bf16[343,343]{1,0:T(8,128)(2,1)S(1)}, u32[]{:S(2)}, u32[]{:S(2)}) collective-permute-start(bf16[343,343]{1,0:T(8,128)(2,1)S(1)} %fusion), channel_id=1, source_target_pairs={{0,1},{1,0},{2,3},{3,2},{4,5},{5,4},{6,7},{7,6},{8,9},{9,8},{10,11... | collective-permute-start | bytes 705902 | tf_op jit(solution)/shard_map/ppermute | solution.py:59
  15.7 4.9 %collective-permute-start.3 = (bf16[152,128]{1,0:T(8,128)(2,1)S(1)}, bf16[152,128]{1,0:T(8,128)(2,1)S(1)}, u32[]{:S(2)}, u32[]{:S(2)}) collective-permute-start(bf16[152,128]{1,0:T(8,128)(2,1)S(1)} %pad_maximum_fusion.16), channel_id=1, source_target_pairs={{0,3},{1,2},{2,1},{3,0},{4,7},{5,6},{6,5},{7,4},{8,11},{9,10},{10,... | collective-permute-start | bytes 116744 | tf_op jit(solution)/shard_map/ppermute | solution.py:59
  20.9 1.3 %collective-permute-start.5 = (bf16[152,128]{1,0:T(8,128)(2,1)S(1)}, bf16[152,128]{1,0:T(8,128)(2,1)S(1)}, u32[]{:S(2)}, u32[]{:S(2)}) collective-permute-start(bf16[152,128]{1,0:T(8,128)(2,1)S(1)} %pad_maximum_fusion.17), channel_id=1, source_target_pairs={{0,1},{1,0},{2,3},{3,2},{4,5},{5,4},{6,7},{7,6},{8,9},{9,8},{10,11... | collective-permute-start | bytes 116744 | tf_op jit(solution)/shard_map/ppermute | solution.py:59
  21.1 1.6 %collective-permute-start.6 = (bf16[343,343]{1,0:T(8,128)(2,1)S(1)}, bf16[343,343]{1,0:T(8,128)(2,1)S(1)}, u32[]{:S(2)}, u32[]{:S(2)}) collective-permute-start(bf16[343,343]{1,0:T(8,128)(2,1)S(1)} %collective-permute-done.4), channel_id=1, source_target_pairs={{0,1},{1,0},{2,3},{3,2},{4,5},{5,4},{6,7},{7,6},{8,9},{9,8},{10,11... | collective-permute-start | bytes 705902 | tf_op jit(solution)/shard_map/ppermute | solution.py:59
  24.3 4.1 %collective-permute-start.10 = (bf16[7,1,7,128]{3,2,1,0:T(8,128)(2,1)S(1)}, bf16[7,1,7,128]{3,2,1,0:T(8,128)(2,1)S(1)}, u32[]{:S(2)}, u32[]{:S(2)}) collective-permute-start(bf16[7,1,7,128]{3,2,1,0:T(8,128)(2,1)S(1)} %broadcast_select_fusion.45), channel_id=1, source_target_pairs={{0,13},{1,12},{2,15},{3,14},{4,9},{5,8},{6,11},{7,10},{8,5},{9,4},... | collective-permute-start | bytes 37640 | tf_op jit(solution)/shard_map/ppermute | solution.py:41
  25.7 3.2 %collective-permute-start.9 = (bf16[7,1,7,128]{3,2,1,0:T(8,128)(2,1)S(1)}, bf16[7,1,7,128]{3,2,1,0:T(8,128)(2,1)S(1)}, u32[]{:S(2)}, u32[]{:S(2)}) collective-permute-start(bf16[7,1,7,128]{3,2,1,0:T(8,128)(2,1)S(1)} %get-tuple-element.32), channel_id=1, source_target_pairs={{0,5},{1,4},{2,7},{3,6},{4,1},{5,0},{6,3},{7,2},{8,13},{9,12},{10,... | collective-permute-start | bytes 37640 | tf_op jit(solution)/shard_map/ppermute | solution.py:41
  29.0 4.1 %collective-permute-start.11 = (bf16[1,7,7,128]{3,2,1,0:T(8,128)(2,1)S(1)}, bf16[1,7,7,128]{3,2,1,0:T(8,128)(2,1)S(1)}, u32[]{:S(2)}, u32[]{:S(2)}) collective-permute-start(bf16[1,7,7,128]{3,2,1,0:T(8,128)(2,1)S(1)} %fusion.83), channel_id=1, source_target_pairs={{0,17},{1,16},{2,19},{3,18},{4,21},{5,20},{6,23},{7,22},{8,25},{9,... | collective-permute-start | bytes 37640 | tf_op jit(solution)/shard_map/ppermute | solution.py:41
  31.6 20.6 %collective-permute-start.17 = (bf16[252,704]{1,0:T(8,128)(2,1)S(1)}, bf16[252,704]{1,0:T(8,128)(2,1)S(1)}, u32[]{:S(2)}, u32[]{:S(2)}) collective-permute-start(bf16[252,704]{1,0:T(8,128)(2,1)S(1)} %pad_maximum_fusion), channel_id=1, source_target_pairs={{0,1},{1,0},{2,3},{3,2},{4,5},{5,4},{6,7},{7,6},{8,9},{9,8},{10,11... | collective-permute-start | bytes 1064456 | tf_op jit(solution)/shard_map/ppermute | solution.py:59
  34.6 2.9 %slice-start = ((bf16[216,704]{1,0:T(8,128)(2,1)}), bf16[92,704]{1,0:T(8,128)(2,1)S(1)}, s32[]{:S(2)}) async-start(bf16[216,704]{1,0:T(8,128)(2,1)} %param.9), calls=%async_computation | async-start | bytes 294912 | tf_op jit(solution)/shard_map/slice | solution.py:210
  34.7 4.1 %collective-permute-start.13 = (bf16[7,1,7,128]{3,2,1,0:T(8,128)(2,1)S(1)}, bf16[7,1,7,128]{3,2,1,0:T(8,128)(2,1)S(1)}, u32[]{:S(2)}, u32[]{:S(2)}) collective-permute-start(bf16[7,1,7,128]{3,2,1,0:T(8,128)(2,1)S(1)} %broadcast_select_fusion.44), channel_id=1, source_target_pairs={{0,13},{1,12},{2,15},{3,14},{4,9},{5,8},{6,11},{7,10},{8,5},{9,4},... | collective-permute-start | bytes 37640 | tf_op jit(solution)/shard_map/ppermute | solution.py:41
  36.1 3.3 %collective-permute-start.12 = (bf16[7,1,7,128]{3,2,1,0:T(8,128)(2,1)S(1)}, bf16[7,1,7,128]{3,2,1,0:T(8,128)(2,1)S(1)}, u32[]{:S(2)}, u32[]{:S(2)}) collective-permute-start(bf16[7,1,7,128]{3,2,1,0:T(8,128)(2,1)S(1)} %get-tuple-element.29), channel_id=1, source_target_pairs={{0,5},{1,4},{2,7},{3,6},{4,1},{5,0},{6,3},{7,2},{8,13},{9,12},{10,... | collective-permute-start | bytes 37640 | tf_op jit(solution)/shard_map/ppermute | solution.py:41
  37.5 6.9 %collective-permute-start.18 = (bf16[128,704]{1,0:T(8,128)(2,1)S(1)}, bf16[128,704]{1,0:T(8,128)(2,1)S(1)}, u32[]{:S(2)}, u32[]{:S(2)}) collective-permute-start(bf16[128,704]{1,0:T(8,128)(2,1)S(1)} %pad_maximum_fusion.2), channel_id=1, source_target_pairs={{0,3},{1,2},{2,1},{3,0},{4,7},{5,6},{6,5},{7,4},{8,11},{9,10},{10,... | collective-permute-start | bytes 540680 | tf_op jit(solution)/shard_map/ppermute | solution.py:59
  39.4 5.0 %collective-permute-start.14 = (bf16[1,7,7,128]{3,2,1,0:T(8,128)(2,1)S(1)}, bf16[1,7,7,128]{3,2,1,0:T(8,128)(2,1)S(1)}, u32[]{:S(2)}, u32[]{:S(2)}) collective-permute-start(bf16[1,7,7,128]{3,2,1,0:T(8,128)(2,1)S(1)} %fusion.84), channel_id=1, source_target_pairs={{0,17},{1,16},{2,19},{3,18},{4,21},{5,20},{6,23},{7,22},{8,25},{9,... | collective-permute-start | bytes 37640 | tf_op jit(solution)/shard_map/ppermute | solution.py:41
  46.0 3.2 %collective-permute-start.15 = (bf16[7,1,7,128]{3,2,1,0:T(8,128)(2,1)S(1)}, bf16[7,1,7,128]{3,2,1,0:T(8,128)(2,1)S(1)}, u32[]{:S(2)}, u32[]{:S(2)}) collective-permute-start(bf16[7,1,7,128]{3,2,1,0:T(8,128)(2,1)S(1)} %slice.746), channel_id=1, source_target_pairs={{0,5},{1,4},{2,7},{3,6},{4,1},{5,0},{6,3},{7,2},{8,13},{9,12},{10,... | collective-permute-start | bytes 37640 | tf_op jit(solution)/shard_map/ppermute | solution.py:41
  46.7 4.0 %collective-permute-start.16 = (bf16[7,1,7,128]{3,2,1,0:T(8,128)(2,1)S(1)}, bf16[7,1,7,128]{3,2,1,0:T(8,128)(2,1)S(1)}, u32[]{:S(2)}, u32[]{:S(2)}) collective-permute-start(bf16[7,1,7,128]{3,2,1,0:T(8,128)(2,1)S(1)} %slice.746), channel_id=1, source_target_pairs={{0,13},{1,12},{2,15},{3,14},{4,9},{5,8},{6,11},{7,10},{8,5},{9,4},... | collective-permute-start | bytes 37640 | tf_op jit(solution)/shard_map/ppermute | solution.py:41
  47.7 4.8 %collective-permute-start.19 = (bf16[252,704]{1,0:T(8,128)(2,1)S(1)}, bf16[252,704]{1,0:T(8,128)(2,1)S(1)}, u32[]{:S(2)}, u32[]{:S(2)}) collective-permute-start(bf16[252,704]{1,0:T(8,128)(2,1)S(1)} %constant_dynamic-update-slice_fusion.6), channel_id=1, source_target_pairs={{0,1},{1,0},{2,3},{3,2},{4,5},{5,4},{6,7},{7,6},{8,9},{9,8},{10,11... | collective-permute-start | bytes 1064456 | tf_op jit(solution)/shard_map/ppermute | solution.py:59
  51.0 1.0 %copy-start.2 = (bf16[216,704]{1,0:T(8,128)(2,1)S(1)}, bf16[216,704]{1,0:T(8,128)(2,1)}, u32[]{:S(2)}) copy-start(bf16[216,704]{1,0:T(8,128)(2,1)} %param.9) | copy-start | bytes 912388
  53.4 6.1 %collective-permute-start.20 = (bf16[212,128]{1,0:T(8,128)(2,1)S(1)}, bf16[212,128]{1,0:T(8,128)(2,1)S(1)}, u32[]{:S(2)}, u32[]{:S(2)}) collective-permute-start(bf16[212,128]{1,0:T(8,128)(2,1)S(1)} %pad_maximum_fusion.11), channel_id=1, source_target_pairs={{0,17},{1,16},{2,19},{3,18},{4,21},{5,20},{6,23},{7,22},{8,25},{9,... | collective-permute-start | bytes 162824 | tf_op jit(solution)/shard_map/ppermute | solution.py:59
  59.6 3.7 %collective-permute-start.21 = (bf16[176,128]{1,0:T(8,128)(2,1)S(1)}, bf16[176,128]{1,0:T(8,128)(2,1)S(1)}, u32[]{:S(2)}, u32[]{:S(2)}) collective-permute-start(bf16[176,128]{1,0:T(8,128)(2,1)S(1)} %add_convert_fusion.2), channel_id=1, source_target_pairs={{0,5},{1,4},{2,7},{3,6},{4,1},{5,0},{6,3},{7,2},{8,13},{9,12},{10,... | collective-permute-start | bytes 135176 | tf_op jit(solution)/shard_map/ppermute | solution.py:41
  63.3 4.6 %collective-permute-start.22 = (bf16[176,128]{1,0:T(8,128)(2,1)S(1)}, bf16[176,128]{1,0:T(8,128)(2,1)S(1)}, u32[]{:S(2)}, u32[]{:S(2)}) collective-permute-start(bf16[176,128]{1,0:T(8,128)(2,1)S(1)} %add_convert_fusion.1), channel_id=1, source_target_pairs={{0,13},{1,12},{2,15},{3,14},{4,9},{5,8},{6,11},{7,10},{8,5},{9,4},... | collective-permute-start | bytes 135176 | tf_op jit(solution)/shard_map/ppermute | solution.py:41
  68.1 4.3 %collective-permute-start.23 = (bf16[284,128]{1,0:T(8,128)(2,1)S(1)}, bf16[284,128]{1,0:T(8,128)(2,1)S(1)}, u32[]{:S(2)}, u32[]{:S(2)}) collective-permute-start(bf16[284,128]{1,0:T(8,128)(2,1)S(1)} %maximum_maximum_fusion.2), channel_id=1, source_target_pairs={{0,3},{1,2},{2,1},{3,0},{4,7},{5,6},{6,5},{7,4},{8,11},{9,10},{10,... | collective-permute-start | bytes 218120 | tf_op jit(solution)/shard_map/ppermute | solution.py:59
  72.6 1.4 %collective-permute-start.24 = (bf16[460,128]{1,0:T(8,128)(2,1)S(1)}, bf16[460,128]{1,0:T(8,128)(2,1)S(1)}, u32[]{:S(2)}, u32[]{:S(2)}) collective-permute-start(bf16[460,128]{1,0:T(8,128)(2,1)S(1)} %maximum_maximum_fusion), channel_id=1, source_target_pairs={{0,1},{1,0},{2,3},{3,2},{4,5},{5,4},{6,7},{7,6},{8,9},{9,8},{10,11... | collective-permute-start | bytes 353288 | tf_op jit(solution)/shard_map/ppermute | solution.py:59

commit v16 on v15

--- a/solution.py
+++ b/solution.py
@@ -197,21 +197,15 @@
     other = by_rows(grid.partner(matrix, FIRST))
     field = jnp.concatenate([grid.exchanged(high, high, 1, cross=0)[0], field], axis=1)
 
-    high = field[edge - 1].reshape(SIDE * edge, columns)
-    tiles = -(-locked.shape[1] // columns)
-    top = jnp.pad(locked[-edge * edge :], ((0, 0), (0, -locked.shape[1] % columns)))
-    top = jnp.concatenate(split(top, tiles), axis=0)
-    sent = jnp.concatenate([top, high], axis=0)
-    sent, matrix = lax.optimization_barrier((sent, matrix))
-    arrived = grid.exchanged(sent, sent, 0, cross=0)[0]
-    bottom = jnp.split(arrived[: top.shape[0]], tiles, axis=0)
-    bottom = jnp.concatenate(bottom, axis=1)[:, : locked.shape[1]]
+    high = plane(field, 0, edge - 1)
+    high, matrix = lax.optimization_barrier((high, matrix))
+    field = jnp.concatenate([grid.exchanged(high, high, 0, cross=0)[0], field], axis=0)
+    top = by_rows(locked[-edge * edge :])
+    bottom = by_rows(grid.exchanged(top, top, 0, cross=0)[0])
+
     cut = max(0, 128 - bottom.shape[0])
     other_late = grid.partner(jnp.concatenate([bottom, locked[:cut]], axis=0), FIRST)
     other_early = grid.partner(locked[cut:], FIRST)
-    field = jnp.concatenate(
-        [arrived[top.shape[0] :].reshape(1, SIDE, edge, columns), field], axis=0
-    )
 
     rows = field.reshape(SIDE * SIDE * edge, columns)
     second = by_rows(grid.partner(matrix, SECOND))
@@ -262,7 +256,7 @@
         following = rounded(following)
         older = lax.optimization_barrier(current)
         current = following
-    locked = jnp.concatenate([bottom, locked], axis=0)
+    locked = lax.optimization_barrier(jnp.concatenate([bottom, locked], axis=0))
     other_locked = jnp.concatenate([other_late, other_early], axis=0)
     both_locked = [grid.partner(l, SECOND) for l in (locked, other_locked)]
     low = plane(partial, 1, 0).astype(jnp.bfloat16)

time: 76.6 us -> 76.3 us (level)
  local copies, waits for them, and re-layouts: 3.97 us -> 2.76 us
  waiting for transfers between devices: 33.7 us -> 34.6 us
    ppermute x13 -> x14, waiting for transfers between devices: 17.5 us -> 19.2 us  [swapped(): arrived = lax.ppermute(jnp.where(lower, high, low), AXIS, pairs)]
    ppermute x13 -> x14, starting transfers between devices: 19.7 us -> 19.6 us  [swapped(): arrived = lax.ppermute(jnp.where(lower, high, low), AXIS, pairs)]
  transfers between devices with their start and end apart: 25 -> 26, of which waited for: 17 -> 17; matrix products, arithmetic and copies ran while one was open for 10% -> 11% of each run, Pallas kernels for 0% -> 0%
where the time goes in v16:
time: 76.3 us; the launch traced here: 76.2 us
  waiting for transfers between devices  34.6 us (45%)
  starting transfers between devices  27.4 us (36%)
  other arithmetic  5.03 us (7%)
  matrix products  4.87 us (6%)
  local copies, waits for them, and re-layouts  2.76 us (4%)
  between operations  1.5 us (2%)
    ppermute x14, starting transfers between devices, swapped(): arrived = lax.ppermute(jnp.where(lower, high, low), AXIS, pairs)  19.6 us
    ppermute x14, waiting for transfers between devices, swapped(): arrived = lax.ppermute(jnp.where(lower, high, low), AXIS, pairs)  19.2 us
    ppermute x12, waiting for transfers between devices, partner(): lax.ppermute(value, AXIS, [(i, i ^ bits) for i in range(self.devices)])  15.4 us
    ppermute x12, starting transfers between devices, partner(): lax.ppermute(value, AXIS, [(i, i ^ bits) for i in range(self.devices)])  7.8 us
    dot_general x12, matrix products, per_device(): jnp.dot(matrices[r], own, preferred_element_type=jnp.float32)  2.93 us
  transfers between devices with their start and end apart: 26, of which 17 were waited for; matrix products, arithmetic and copies ran while one was open for 11% of the time, Pallas kernels for 0%

profile of v16, /device:TPU:0, one launch (start us, length us, event | category | flops | bytes accessed | tf_op | source)
XLA Modules:
  0.0 76.2 jit_solution(6800437385302423522)
XLA Ops:
  0.6 0.9 %reshape.121 = bf16[6,6,6,128]{3,2,1,0:T(8,128)(2,1)S(1)} reshape(bf16[216,128]{1,0:T(8,128)(2,1)} %param.5) | data formatting | bytes 110592 | tf_op jit(solution)/shard_map/reshape | solution.py:193
  1.6 3.0 %collective-permute-start.1 = (bf16[6,1,6,128]{3,2,1,0:T(8,128)(2,1)S(1)}, bf16[6,1,6,128]{3,2,1,0:T(8,128)(2,1)S(1)}, u32[]{:S(2)}, u32[]{:S(2)}) collective-permute-start(bf16[6,1,6,128]{3,2,1,0:T(8,128)(2,1)S(1)} %slice.486), channel_id=1, source_target_pairs={{0,4},{1,5},{2,6},{3,7},{4,0},{5,1},{6,2},{7,3},{8,12},{9,13},{10,... | collective-permute-start | bytes 27656 | tf_op jit(solution)/shard_map/ppermute | solution.py:41
  4.6 1.5 %collective-permute-start.2 = (bf16[6,1,6,128]{3,2,1,0:T(8,128)(2,1)S(1)}, bf16[6,1,6,128]{3,2,1,0:T(8,128)(2,1)S(1)}, u32[]{:S(2)}, u32[]{:S(2)}) collective-permute-start(bf16[6,1,6,128]{3,2,1,0:T(8,128)(2,1)S(1)} %slice.486), channel_id=1, source_target_pairs={{0,12},{1,13},{2,14},{3,15},{4,8},{5,9},{6,10},{7,11},{8,4},{9,5},... | collective-permute-start | bytes 27656 | tf_op jit(solution)/shard_map/ppermute | solution.py:41
  6.2 0.7 fusion
  7.4 1.4 %collective-permute-start.8 = (bf16[124,704]{1,0:T(8,128)(2,1)S(1)}, bf16[124,704]{1,0:T(8,128)(2,1)S(1)}, u32[]{:S(2)}, u32[]{:S(2)}) collective-permute-start(bf16[124,704]{1,0:T(8,128)(2,1)S(1)} %slice.394), channel_id=1, source_target_pairs={{0,3},{1,2},{2,1},{3,0},{4,7},{5,6},{6,5},{7,4},{8,11},{9,10},{10,... | collective-permute-start | bytes 523784 | tf_op jit(solution)/shard_map/ppermute | solution.py:59
  8.8 2.7 %collective-permute-start = (bf16[36,704]{1,0:T(8,128)(2,1)S(1)}, bf16[36,704]{1,0:T(8,128)(2,1)S(1)}, u32[]{:S(2)}, u32[]{:S(2)}) collective-permute-start(bf16[36,704]{1,0:T(8,128)(2,1)S(1)} %slice.371), channel_id=1, source_target_pairs={{0,16},{1,17},{2,18},{3,19},{4,20},{5,21},{6,22},{7,23},{8,24},{9,... | collective-permute-start | bytes 152072 | tf_op jit(solution)/shard_map/ppermute | solution.py:41
  12.0 4.3 %collective-permute-done.3 = bf16[1,7,6,128]{3,2,1,0:T(8,128)(2,1)S(1)} collective-permute-done((bf16[1,7,6,128]{3,2,1,0:T(8,128)(2,1)S(1)}, bf16[1,7,6,128]{3,2,1,0:T(8,128)(2,1)S(1)}, u32[]{:S(2)}, u32[]{:S(2)}) %collective-permute-start.3) | collective-permute-done | bytes 10784 | tf_op jit(solution)/shard_map/ppermute | solution.py:41
  16.9 3.8 %collective-permute-done.4 = bf16[152,128]{1,0:T(8,128)(2,1)S(1)} collective-permute-done((bf16[152,128]{1,0:T(8,128)(2,1)S(1)}, bf16[152,128]{1,0:T(8,128)(2,1)S(1)}, u32[]{:S(2)}, u32[]{:S(2)}) %collective-permute-start.4) | collective-permute-done | bytes 38944 | tf_op jit(solution)/shard_map/ppermute | solution.py:59
  24.6 1.5 %collective-permute-start.11 = (bf16[7,1,7,128]{3,2,1,0:T(8,128)(2,1)S(1)}, bf16[7,1,7,128]{3,2,1,0:T(8,128)(2,1)S(1)}, u32[]{:S(2)}, u32[]{:S(2)}) collective-permute-start(bf16[7,1,7,128]{3,2,1,0:T(8,128)(2,1)S(1)} %broadcast_select_fusion.45), channel_id=1, source_target_pairs={{0,13},{1,12},{2,15},{3,14},{4,9},{5,8},{6,11},{7,10},{8,5},{9,4},... | collective-permute-start | bytes 37640 | tf_op jit(solution)/shard_map/ppermute | solution.py:41
  26.3 2.4 %collective-permute-done.11 = bf16[7,1,7,128]{3,2,1,0:T(8,128)(2,1)S(1)} collective-permute-done((bf16[7,1,7,128]{3,2,1,0:T(8,128)(2,1)S(1)}, bf16[7,1,7,128]{3,2,1,0:T(8,128)(2,1)S(1)}, u32[]{:S(2)}, u32[]{:S(2)}) %collective-permute-start.11) | collective-permute-done | bytes 12576 | tf_op jit(solution)/shard_map/ppermute | solution.py:41
  28.8 0.7 collective-permute-done.10
  29.5 2.2 %collective-permute-start.12 = (bf16[1,7,7,128]{3,2,1,0:T(8,128)(2,1)S(1)}, bf16[1,7,7,128]{3,2,1,0:T(8,128)(2,1)S(1)}, u32[]{:S(2)}, u32[]{:S(2)}) collective-permute-start(bf16[1,7,7,128]{3,2,1,0:T(8,128)(2,1)S(1)} %fusion.83), channel_id=1, source_target_pairs={{0,17},{1,16},{2,19},{3,18},{4,21},{5,20},{6,23},{7,22},{8,25},{9,... | collective-permute-start | bytes 37640 | tf_op jit(solution)/shard_map/ppermute | solution.py:41
  32.3 1.3 %collective-permute-done.12 = bf16[1,7,7,128]{3,2,1,0:T(8,128)(2,1)S(1)} collective-permute-done((bf16[1,7,7,128]{3,2,1,0:T(8,128)(2,1)S(1)}, bf16[1,7,7,128]{3,2,1,0:T(8,128)(2,1)S(1)}, u32[]{:S(2)}, u32[]{:S(2)}) %collective-permute-start.12) | collective-permute-done | bytes 12576 | tf_op jit(solution)/shard_map/ppermute | solution.py:41
  35.2 1.3 %collective-permute-start.14 = (bf16[7,1,7,128]{3,2,1,0:T(8,128)(2,1)S(1)}, bf16[7,1,7,128]{3,2,1,0:T(8,128)(2,1)S(1)}, u32[]{:S(2)}, u32[]{:S(2)}) collective-permute-start(bf16[7,1,7,128]{3,2,1,0:T(8,128)(2,1)S(1)} %broadcast_select_fusion.44), channel_id=1, source_target_pairs={{0,13},{1,12},{2,15},{3,14},{4,9},{5,8},{6,11},{7,10},{8,5},{9,4},... | collective-permute-start | bytes 37640 | tf_op jit(solution)/shard_map/ppermute | solution.py:41
  36.5 1.4 %collective-permute-start.13 = (bf16[7,1,7,128]{3,2,1,0:T(8,128)(2,1)S(1)}, bf16[7,1,7,128]{3,2,1,0:T(8,128)(2,1)S(1)}, u32[]{:S(2)}, u32[]{:S(2)}) collective-permute-start(bf16[7,1,7,128]{3,2,1,0:T(8,128)(2,1)S(1)} %get-tuple-element.29), channel_id=1, source_target_pairs={{0,5},{1,4},{2,7},{3,6},{4,1},{5,0},{6,3},{7,2},{8,13},{9,12},{10,... | collective-permute-start | bytes 37640 | tf_op jit(solution)/shard_map/ppermute | solution.py:41
  37.9 0.9 %collective-permute-start.19 = (bf16[128,704]{1,0:T(8,128)(2,1)S(1)}, bf16[128,704]{1,0:T(8,128)(2,1)S(1)}, u32[]{:S(2)}, u32[]{:S(2)}) collective-permute-start(bf16[128,704]{1,0:T(8,128)(2,1)S(1)} %pad_maximum_fusion.2), channel_id=1, source_target_pairs={{0,3},{1,2},{2,1},{3,0},{4,7},{5,6},{6,5},{7,4},{8,11},{9,10},{10,... | collective-permute-start | bytes 540680 | tf_op jit(solution)/shard_map/ppermute | solution.py:59
  39.9 2.5 %collective-permute-start.15 = (bf16[1,7,7,128]{3,2,1,0:T(8,128)(2,1)S(1)}, bf16[1,7,7,128]{3,2,1,0:T(8,128)(2,1)S(1)}, u32[]{:S(2)}, u32[]{:S(2)}) collective-permute-start(bf16[1,7,7,128]{3,2,1,0:T(8,128)(2,1)S(1)} %fusion.84), channel_id=1, source_target_pairs={{0,17},{1,16},{2,19},{3,18},{4,21},{5,20},{6,23},{7,22},{8,25},{9,... | collective-permute-start | bytes 37640 | tf_op jit(solution)/shard_map/ppermute | solution.py:41
  42.3 2.5 %collective-permute-done.19 = bf16[128,704]{1,0:T(8,128)(2,1)S(1)} collective-permute-done((bf16[128,704]{1,0:T(8,128)(2,1)S(1)}, bf16[128,704]{1,0:T(8,128)(2,1)S(1)}, u32[]{:S(2)}, u32[]{:S(2)}) %collective-permute-start.19) | collective-permute-done | bytes 180256 | tf_op jit(solution)/shard_map/ppermute | solution.py:59
  46.4 0.6 collective-permute-start.16
  47.1 1.3 %collective-permute-start.17 = (bf16[7,1,7,128]{3,2,1,0:T(8,128)(2,1)S(1)}, bf16[7,1,7,128]{3,2,1,0:T(8,128)(2,1)S(1)}, u32[]{:S(2)}, u32[]{:S(2)}) collective-permute-start(bf16[7,1,7,128]{3,2,1,0:T(8,128)(2,1)S(1)} %slice.694), channel_id=1, source_target_pairs={{0,13},{1,12},{2,15},{3,14},{4,9},{5,8},{6,11},{7,10},{8,5},{9,4},... | collective-permute-start | bytes 37640 | tf_op jit(solution)/shard_map/ppermute | solution.py:41
  48.6 1.1 %collective-permute-done.16 = bf16[7,1,7,128]{3,2,1,0:T(8,128)(2,1)S(1)} collective-permute-done((bf16[7,1,7,128]{3,2,1,0:T(8,128)(2,1)S(1)}, bf16[7,1,7,128]{3,2,1,0:T(8,128)(2,1)S(1)}, u32[]{:S(2)}, u32[]{:S(2)}) %collective-permute-start.16) | collective-permute-done | bytes 12576 | tf_op jit(solution)/shard_map/ppermute | solution.py:41
  49.6 1.5 %collective-permute-done.17 = bf16[7,1,7,128]{3,2,1,0:T(8,128)(2,1)S(1)} collective-permute-done((bf16[7,1,7,128]{3,2,1,0:T(8,128)(2,1)S(1)}, bf16[7,1,7,128]{3,2,1,0:T(8,128)(2,1)S(1)}, u32[]{:S(2)}, u32[]{:S(2)}) %collective-permute-start.17) | collective-permute-done | bytes 12576 | tf_op jit(solution)/shard_map/ppermute | solution.py:41
  53.1 2.5 %collective-permute-start.21 = (bf16[212,128]{1,0:T(8,128)(2,1)S(1)}, bf16[212,128]{1,0:T(8,128)(2,1)S(1)}, u32[]{:S(2)}, u32[]{:S(2)}) collective-permute-start(bf16[212,128]{1,0:T(8,128)(2,1)S(1)} %pad_maximum_fusion.11), channel_id=1, source_target_pairs={{0,17},{1,16},{2,19},{3,18},{4,21},{5,20},{6,23},{7,22},{8,25},{9,... | collective-permute-start | bytes 162824 | tf_op jit(solution)/shard_map/ppermute | solution.py:59
  55.6 3.6 %collective-permute-done.21 = bf16[212,128]{1,0:T(8,128)(2,1)S(1)} collective-permute-done((bf16[212,128]{1,0:T(8,128)(2,1)S(1)}, bf16[212,128]{1,0:T(8,128)(2,1)S(1)}, u32[]{:S(2)}, u32[]{:S(2)}) %collective-permute-start.21) | collective-permute-done | bytes 54304 | tf_op jit(solution)/shard_map/ppermute | solution.py:59
  59.3 1.1 %collective-permute-start.22 = (bf16[176,128]{1,0:T(8,128)(2,1)S(1)}, bf16[176,128]{1,0:T(8,128)(2,1)S(1)}, u32[]{:S(2)}, u32[]{:S(2)}) collective-permute-start(bf16[176,128]{1,0:T(8,128)(2,1)S(1)} %add_convert_fusion.2), channel_id=1, source_target_pairs={{0,5},{1,4},{2,7},{3,6},{4,1},{5,0},{6,3},{7,2},{8,13},{9,12},{10,... | collective-permute-start | bytes 135176 | tf_op jit(solution)/shard_map/ppermute | solution.py:41
  60.5 2.5 %collective-permute-done.22 = bf16[176,128]{1,0:T(8,128)(2,1)S(1)} collective-permute-done((bf16[176,128]{1,0:T(8,128)(2,1)S(1)}, bf16[176,128]{1,0:T(8,128)(2,1)S(1)}, u32[]{:S(2)}, u32[]{:S(2)}) %collective-permute-start.22) | collective-permute-done | bytes 45088 | tf_op jit(solution)/shard_map/ppermute | solution.py:41
  63.1 4.5 %collective-permute-done.23 = bf16[176,128]{1,0:T(8,128)(2,1)S(1)} collective-permute-done((bf16[176,128]{1,0:T(8,128)(2,1)S(1)}, bf16[176,128]{1,0:T(8,128)(2,1)S(1)}, u32[]{:S(2)}, u32[]{:S(2)}) %collective-permute-start.23) | collective-permute-done | bytes 45088 | tf_op jit(solution)/shard_map/ppermute | solution.py:41
  67.8 0.9 %collective-permute-start.24 = (bf16[284,128]{1,0:T(8,128)(2,1)S(1)}, bf16[284,128]{1,0:T(8,128)(2,1)S(1)}, u32[]{:S(2)}, u32[]{:S(2)}) collective-permute-start(bf16[284,128]{1,0:T(8,128)(2,1)S(1)} %maximum_maximum_fusion.2), channel_id=1, source_target_pairs={{0,3},{1,2},{2,1},{3,0},{4,7},{5,6},{6,5},{7,4},{8,11},{9,10},{10,... | collective-permute-start | bytes 218120 | tf_op jit(solution)/shard_map/ppermute | solution.py:59
  68.7 3.4 %collective-permute-done.24 = bf16[284,128]{1,0:T(8,128)(2,1)S(1)} collective-permute-done((bf16[284,128]{1,0:T(8,128)(2,1)S(1)}, bf16[284,128]{1,0:T(8,128)(2,1)S(1)}, u32[]{:S(2)}, u32[]{:S(2)}) %collective-permute-start.24) | collective-permute-done | bytes 72736 | tf_op jit(solution)/shard_map/ppermute | solution.py:59
  72.5 1.2 %collective-permute-done.25 = bf16[460,128]{1,0:T(8,128)(2,1)S(1)} collective-permute-done((bf16[460,128]{1,0:T(8,128)(2,1)S(1)}, bf16[460,128]{1,0:T(8,128)(2,1)S(1)}, u32[]{:S(2)}, u32[]{:S(2)}) %collective-permute-start.25) | collective-permute-done | bytes 117792 | tf_op jit(solution)/shard_map/ppermute | solution.py:59
  74.4 0.7 pad_maximum_fusion.15
  75.2 1.0 %maximum_convert_fusion = f32[704,128]{1,0:T(8,128)} fusion(bf16[176,32]{1,0:T(8,128)(2,1)S(1)} %get-tuple-element.110, bf16[176,32]{1,0:T(8,128)(2,1)S(1)} %get-tuple-element.106, bf16[176,32]{1,0:T(8,128)(2,1)S(1)} %get-tuple-element.102, bf16[176,32]{1,0:T(8,128)(2,1)S(1)} %get-tuple-element.98, bf16[176,32]{1,0:T(8,128)(2,1)S(1)} %get-tuple-element.111, ...), kind=kLoop, calls=%fused_computation.51 | loop fusion | flops 2883584 | bytes 540672 | tf_op jit(solution)/shard_map/convert_element_type | solution.py:325
  (158 shorter events, 13.9 us)
Async XLA Ops:
  0.6 5.5 %copy-start = (bf16[1,343,343]{2,1,0:T(8,128)(2,1)S(1)}, bf16[1,343,343]{2,1,0:T(8,128)(2,1)}, u32[]{:S(2)}) copy-start(bf16[1,343,343]{2,1,0:T(8,128)(2,1)} %param.6) | copy-start | bytes 705898
  1.5 4.6 %copy-start.2 = (s32[1,343]{1,0:T(1,128)S(1)}, s32[1,343]{1,0:T(1,128)}, u32[]{:S(2)}) copy-start(s32[1,343]{1,0:T(1,128)} %param.7) | copy-start | bytes 4120
  1.5 4.6 %copy-start.3 = (f32[343]{0:T(512)S(1)}, f32[343]{0:T(512)}, u32[]{:S(2)}) copy-start(f32[343]{0:T(512)} %param.8) | copy-start | bytes 4120
  1.6 10.0 %collective-permute-start.1 = (bf16[6,1,6,128]{3,2,1,0:T(8,128)(2,1)S(1)}, bf16[6,1,6,128]{3,2,1,0:T(8,128)(2,1)S(1)}, u32[]{:S(2)}, u32[]{:S(2)}) collective-permute-start(bf16[6,1,6,128]{3,2,1,0:T(8,128)(2,1)S(1)} %slice.486), channel_id=1, source_target_pairs={{0,4},{1,5},{2,6},{3,7},{4,0},{5,1},{6,2},{7,3},{8,12},{9,13},{10,... | collective-permute-start | bytes 27656 | tf_op jit(solution)/shard_map/ppermute | solution.py:41
  4.6 7.0 %collective-permute-start.2 = (bf16[6,1,6,128]{3,2,1,0:T(8,128)(2,1)S(1)}, bf16[6,1,6,128]{3,2,1,0:T(8,128)(2,1)S(1)}, u32[]{:S(2)}, u32[]{:S(2)}) collective-permute-start(bf16[6,1,6,128]{3,2,1,0:T(8,128)(2,1)S(1)} %slice.486), channel_id=1, source_target_pairs={{0,12},{1,13},{2,14},{3,15},{4,8},{5,9},{6,10},{7,11},{8,4},{9,5},... | collective-permute-start | bytes 27656 | tf_op jit(solution)/shard_map/ppermute | solution.py:41
  6.2 1.2 %copy-start.1 = (bf16[216,704]{1,0:T(8,128)(2,1)S(1)}, bf16[216,704]{1,0:T(8,128)(2,1)}, u32[]{:S(2)}) copy-start(bf16[216,704]{1,0:T(8,128)(2,1)} %param.9) | copy-start | bytes 912388
  6.9 14.0 %collective-permute-start.5 = (bf16[343,343]{1,0:T(8,128)(2,1)S(1)}, bf16[343,343]{1,0:T(8,128)(2,1)S(1)}, u32[]{:S(2)}, u32[]{:S(2)}) collective-permute-start(bf16[343,343]{1,0:T(8,128)(2,1)S(1)} %fusion), channel_id=1, source_target_pairs={{0,3},{1,2},{2,1},{3,0},{4,7},{5,6},{6,5},{7,4},{8,11},{9,10},{10,... | collective-permute-start | bytes 705902 | tf_op jit(solution)/shard_map/ppermute | solution.py:59
  7.4 15.3 %collective-permute-start.8 = (bf16[124,704]{1,0:T(8,128)(2,1)S(1)}, bf16[124,704]{1,0:T(8,128)(2,1)S(1)}, u32[]{:S(2)}, u32[]{:S(2)}) collective-permute-start(bf16[124,704]{1,0:T(8,128)(2,1)S(1)} %slice.394), channel_id=1, source_target_pairs={{0,3},{1,2},{2,1},{3,0},{4,7},{5,6},{6,5},{7,4},{8,11},{9,10},{10,... | collective-permute-start | bytes 523784 | tf_op jit(solution)/shard_map/ppermute | solution.py:59
  8.8 17.5 %collective-permute-start = (bf16[36,704]{1,0:T(8,128)(2,1)S(1)}, bf16[36,704]{1,0:T(8,128)(2,1)S(1)}, u32[]{:S(2)}, u32[]{:S(2)}) collective-permute-start(bf16[36,704]{1,0:T(8,128)(2,1)S(1)} %slice.371), channel_id=1, source_target_pairs={{0,16},{1,17},{2,18},{3,19},{4,20},{5,21},{6,22},{7,23},{8,24},{9,... | collective-permute-start | bytes 152072 | tf_op jit(solution)/shard_map/ppermute | solution.py:41
  11.6 4.7 %collective-permute-start.3 = (bf16[1,7,6,128]{3,2,1,0:T(8,128)(2,1)S(1)}, bf16[1,7,6,128]{3,2,1,0:T(8,128)(2,1)S(1)}, u32[]{:S(2)}, u32[]{:S(2)}) collective-permute-start(bf16[1,7,6,128]{3,2,1,0:T(8,128)(2,1)S(1)} %pad_maximum_fusion.22), channel_id=1, source_target_pairs={{0,16},{1,17},{2,18},{3,19},{4,20},{5,21},{6,22},{7,23},{8,24},{9,... | collective-permute-start | bytes 32264 | tf_op jit(solution)/shard_map/ppermute | solution.py:41
  16.8 3.8 %collective-permute-start.4 = (bf16[152,128]{1,0:T(8,128)(2,1)S(1)}, bf16[152,128]{1,0:T(8,128)(2,1)S(1)}, u32[]{:S(2)}, u32[]{:S(2)}) collective-permute-start(bf16[152,128]{1,0:T(8,128)(2,1)S(1)} %pad_maximum_fusion.16), channel_id=1, source_target_pairs={{0,3},{1,2},{2,1},{3,0},{4,7},{5,6},{6,5},{7,4},{8,11},{9,10},{10,... | collective-permute-start | bytes 116744 | tf_op jit(solution)/shard_map/ppermute | solution.py:59
  20.9 1.3 %collective-permute-start.6 = (bf16[152,128]{1,0:T(8,128)(2,1)S(1)}, bf16[152,128]{1,0:T(8,128)(2,1)S(1)}, u32[]{:S(2)}, u32[]{:S(2)}) collective-permute-start(bf16[152,128]{1,0:T(8,128)(2,1)S(1)} %pad_maximum_fusion.17), channel_id=1, source_target_pairs={{0,1},{1,0},{2,3},{3,2},{4,5},{5,4},{6,7},{7,6},{8,9},{9,8},{10,11... | collective-permute-start | bytes 116744 | tf_op jit(solution)/shard_map/ppermute | solution.py:59
  21.1 2.7 %collective-permute-start.9 = (bf16[343,343]{1,0:T(8,128)(2,1)S(1)}, bf16[343,343]{1,0:T(8,128)(2,1)S(1)}, u32[]{:S(2)}, u32[]{:S(2)}) collective-permute-start(bf16[343,343]{1,0:T(8,128)(2,1)S(1)} %fusion), channel_id=1, source_target_pairs={{0,1},{1,0},{2,3},{3,2},{4,5},{5,4},{6,7},{7,6},{8,9},{9,8},{10,11... | collective-permute-start | bytes 705902 | tf_op jit(solution)/shard_map/ppermute | solution.py:59
  21.5 1.5 %collective-permute-start.7 = (bf16[343,343]{1,0:T(8,128)(2,1)S(1)}, bf16[343,343]{1,0:T(8,128)(2,1)S(1)}, u32[]{:S(2)}, u32[]{:S(2)}) collective-permute-start(bf16[343,343]{1,0:T(8,128)(2,1)S(1)} %collective-permute-done.5), channel_id=1, source_target_pairs={{0,1},{1,0},{2,3},{3,2},{4,5},{5,4},{6,7},{7,6},{8,9},{9,8},{10,11... | collective-permute-start | bytes 705902 | tf_op jit(solution)/shard_map/ppermute | solution.py:59
  24.6 4.1 %collective-permute-start.11 = (bf16[7,1,7,128]{3,2,1,0:T(8,128)(2,1)S(1)}, bf16[7,1,7,128]{3,2,1,0:T(8,128)(2,1)S(1)}, u32[]{:S(2)}, u32[]{:S(2)}) collective-permute-start(bf16[7,1,7,128]{3,2,1,0:T(8,128)(2,1)S(1)} %broadcast_select_fusion.45), channel_id=1, source_target_pairs={{0,13},{1,12},{2,15},{3,14},{4,9},{5,8},{6,11},{7,10},{8,5},{9,4},... | collective-permute-start | bytes 37640 | tf_op jit(solution)/shard_map/ppermute | solution.py:41
  26.1 3.3 %collective-permute-start.10 = (bf16[7,1,7,128]{3,2,1,0:T(8,128)(2,1)S(1)}, bf16[7,1,7,128]{3,2,1,0:T(8,128)(2,1)S(1)}, u32[]{:S(2)}, u32[]{:S(2)}) collective-permute-start(bf16[7,1,7,128]{3,2,1,0:T(8,128)(2,1)S(1)} %get-tuple-element.32), channel_id=1, source_target_pairs={{0,5},{1,4},{2,7},{3,6},{4,1},{5,0},{6,3},{7,2},{8,13},{9,12},{10,... | collective-permute-start | bytes 37640 | tf_op jit(solution)/shard_map/ppermute | solution.py:41
  29.5 4.1 %collective-permute-start.12 = (bf16[1,7,7,128]{3,2,1,0:T(8,128)(2,1)S(1)}, bf16[1,7,7,128]{3,2,1,0:T(8,128)(2,1)S(1)}, u32[]{:S(2)}, u32[]{:S(2)}) collective-permute-start(bf16[1,7,7,128]{3,2,1,0:T(8,128)(2,1)S(1)} %fusion.83), channel_id=1, source_target_pairs={{0,17},{1,16},{2,19},{3,18},{4,21},{5,20},{6,23},{7,22},{8,25},{9,... | collective-permute-start | bytes 37640 | tf_op jit(solution)/shard_map/ppermute | solution.py:41
  31.8 19.8 %collective-permute-start.18 = (bf16[252,704]{1,0:T(8,128)(2,1)S(1)}, bf16[252,704]{1,0:T(8,128)(2,1)S(1)}, u32[]{:S(2)}, u32[]{:S(2)}) collective-permute-start(bf16[252,704]{1,0:T(8,128)(2,1)S(1)} %pad_maximum_fusion), channel_id=1, source_target_pairs={{0,1},{1,0},{2,3},{3,2},{4,5},{5,4},{6,7},{7,6},{8,9},{9,8},{10,11... | collective-permute-start | bytes 1064456 | tf_op jit(solution)/shard_map/ppermute | solution.py:59
  35.1 2.7 %slice-start = ((bf16[216,704]{1,0:T(8,128)(2,1)}), bf16[92,704]{1,0:T(8,128)(2,1)S(1)}, s32[]{:S(2)}) async-start(bf16[216,704]{1,0:T(8,128)(2,1)} %param.9), calls=%async_computation | async-start | bytes 294912 | tf_op jit(solution)/shard_map/slice | solution.py:207
  35.2 4.1 %collective-permute-start.14 = (bf16[7,1,7,128]{3,2,1,0:T(8,128)(2,1)S(1)}, bf16[7,1,7,128]{3,2,1,0:T(8,128)(2,1)S(1)}, u32[]{:S(2)}, u32[]{:S(2)}) collective-permute-start(bf16[7,1,7,128]{3,2,1,0:T(8,128)(2,1)S(1)} %broadcast_select_fusion.44), channel_id=1, source_target_pairs={{0,13},{1,12},{2,15},{3,14},{4,9},{5,8},{6,11},{7,10},{8,5},{9,4},... | collective-permute-start | bytes 37640 | tf_op jit(solution)/shard_map/ppermute | solution.py:41
  36.5 3.3 %collective-permute-start.13 = (bf16[7,1,7,128]{3,2,1,0:T(8,128)(2,1)S(1)}, bf16[7,1,7,128]{3,2,1,0:T(8,128)(2,1)S(1)}, u32[]{:S(2)}, u32[]{:S(2)}) collective-permute-start(bf16[7,1,7,128]{3,2,1,0:T(8,128)(2,1)S(1)} %get-tuple-element.29), channel_id=1, source_target_pairs={{0,5},{1,4},{2,7},{3,6},{4,1},{5,0},{6,3},{7,2},{8,13},{9,12},{10,... | collective-permute-start | bytes 37640 | tf_op jit(solution)/shard_map/ppermute | solution.py:41
  37.9 6.9 %collective-permute-start.19 = (bf16[128,704]{1,0:T(8,128)(2,1)S(1)}, bf16[128,704]{1,0:T(8,128)(2,1)S(1)}, u32[]{:S(2)}, u32[]{:S(2)}) collective-permute-start(bf16[128,704]{1,0:T(8,128)(2,1)S(1)} %pad_maximum_fusion.2), channel_id=1, source_target_pairs={{0,3},{1,2},{2,1},{3,0},{4,7},{5,6},{6,5},{7,4},{8,11},{9,10},{10,... | collective-permute-start | bytes 540680 | tf_op jit(solution)/shard_map/ppermute | solution.py:59
  39.9 5.0 %collective-permute-start.15 = (bf16[1,7,7,128]{3,2,1,0:T(8,128)(2,1)S(1)}, bf16[1,7,7,128]{3,2,1,0:T(8,128)(2,1)S(1)}, u32[]{:S(2)}, u32[]{:S(2)}) collective-permute-start(bf16[1,7,7,128]{3,2,1,0:T(8,128)(2,1)S(1)} %fusion.84), channel_id=1, source_target_pairs={{0,17},{1,16},{2,19},{3,18},{4,21},{5,20},{6,23},{7,22},{8,25},{9,... | collective-permute-start | bytes 37640 | tf_op jit(solution)/shard_map/ppermute | solution.py:41
  46.4 3.2 %collective-permute-start.16 = (bf16[7,1,7,128]{3,2,1,0:T(8,128)(2,1)S(1)}, bf16[7,1,7,128]{3,2,1,0:T(8,128)(2,1)S(1)}, u32[]{:S(2)}, u32[]{:S(2)}) collective-permute-start(bf16[7,1,7,128]{3,2,1,0:T(8,128)(2,1)S(1)} %slice.694), channel_id=1, source_target_pairs={{0,5},{1,4},{2,7},{3,6},{4,1},{5,0},{6,3},{7,2},{8,13},{9,12},{10,... | collective-permute-start | bytes 37640 | tf_op jit(solution)/shard_map/ppermute | solution.py:41
  47.1 4.0 %collective-permute-start.17 = (bf16[7,1,7,128]{3,2,1,0:T(8,128)(2,1)S(1)}, bf16[7,1,7,128]{3,2,1,0:T(8,128)(2,1)S(1)}, u32[]{:S(2)}, u32[]{:S(2)}) collective-permute-start(bf16[7,1,7,128]{3,2,1,0:T(8,128)(2,1)S(1)} %slice.694), channel_id=1, source_target_pairs={{0,13},{1,12},{2,15},{3,14},{4,9},{5,8},{6,11},{7,10},{8,5},{9,4},... | collective-permute-start | bytes 37640 | tf_op jit(solution)/shard_map/ppermute | solution.py:41
  48.3 3.9 %collective-permute-start.20 = (bf16[252,704]{1,0:T(8,128)(2,1)S(1)}, bf16[252,704]{1,0:T(8,128)(2,1)S(1)}, u32[]{:S(2)}, u32[]{:S(2)}) collective-permute-start(bf16[252,704]{1,0:T(8,128)(2,1)S(1)} %constant_dynamic-update-slice_fusion), channel_id=1, source_target_pairs={{0,1},{1,0},{2,3},{3,2},{4,5},{5,4},{6,7},{7,6},{8,9},{9,8},{10,11... | collective-permute-start | bytes 1064456 | tf_op jit(solution)/shard_map/ppermute | solution.py:59
  53.1 6.1 %collective-permute-start.21 = (bf16[212,128]{1,0:T(8,128)(2,1)S(1)}, bf16[212,128]{1,0:T(8,128)(2,1)S(1)}, u32[]{:S(2)}, u32[]{:S(2)}) collective-permute-start(bf16[212,128]{1,0:T(8,128)(2,1)S(1)} %pad_maximum_fusion.11), channel_id=1, source_target_pairs={{0,17},{1,16},{2,19},{3,18},{4,21},{5,20},{6,23},{7,22},{8,25},{9,... | collective-permute-start | bytes 162824 | tf_op jit(solution)/shard_map/ppermute | solution.py:59
  59.3 3.7 %collective-permute-start.22 = (bf16[176,128]{1,0:T(8,128)(2,1)S(1)}, bf16[176,128]{1,0:T(8,128)(2,1)S(1)}, u32[]{:S(2)}, u32[]{:S(2)}) collective-permute-start(bf16[176,128]{1,0:T(8,128)(2,1)S(1)} %add_convert_fusion.2), channel_id=1, source_target_pairs={{0,5},{1,4},{2,7},{3,6},{4,1},{5,0},{6,3},{7,2},{8,13},{9,12},{10,... | collective-permute-start | bytes 135176 | tf_op jit(solution)/shard_map/ppermute | solution.py:41
  63.0 4.6 %collective-permute-start.23 = (bf16[176,128]{1,0:T(8,128)(2,1)S(1)}, bf16[176,128]{1,0:T(8,128)(2,1)S(1)}, u32[]{:S(2)}, u32[]{:S(2)}) collective-permute-start(bf16[176,128]{1,0:T(8,128)(2,1)S(1)} %add_convert_fusion.1), channel_id=1, source_target_pairs={{0,13},{1,12},{2,15},{3,14},{4,9},{5,8},{6,11},{7,10},{8,5},{9,4},... | collective-permute-start | bytes 135176 | tf_op jit(solution)/shard_map/ppermute | solution.py:41
  67.8 4.3 %collective-permute-start.24 = (bf16[284,128]{1,0:T(8,128)(2,1)S(1)}, bf16[284,128]{1,0:T(8,128)(2,1)S(1)}, u32[]{:S(2)}, u32[]{:S(2)}) collective-permute-start(bf16[284,128]{1,0:T(8,128)(2,1)S(1)} %maximum_maximum_fusion.2), channel_id=1, source_target_pairs={{0,3},{1,2},{2,1},{3,0},{4,7},{5,6},{6,5},{7,4},{8,11},{9,10},{10,... | collective-permute-start | bytes 218120 | tf_op jit(solution)/shard_map/ppermute | solution.py:59
  72.3 1.4 %collective-permute-start.25 = (bf16[460,128]{1,0:T(8,128)(2,1)S(1)}, bf16[460,128]{1,0:T(8,128)(2,1)S(1)}, u32[]{:S(2)}, u32[]{:S(2)}) collective-permute-start(bf16[460,128]{1,0:T(8,128)(2,1)S(1)} %maximum_maximum_fusion), channel_id=1, source_target_pairs={{0,1},{1,0},{2,3},{3,2},{4,5},{5,4},{6,7},{7,6},{8,9},{9,8},{10,11... | collective-permute-start | bytes 353288 | tf_op jit(solution)/shard_map/ppermute | solution.py:59

commit v17 on v15

--- a/solution.py
+++ b/solution.py
@@ -192,8 +192,8 @@
 
     field = block.reshape(edge, edge, edge, columns)
     high = plane(field, 1, edge - 1)
-    cell_matrix, high = lax.optimization_barrier((cell_matrix, high))
     matrix = by_rows(slots_matrix(cell_matrix, connectivity, potential))
+    matrix, high = lax.optimization_barrier((matrix, high))
     other = by_rows(grid.partner(matrix, FIRST))
     field = jnp.concatenate([grid.exchanged(high, high, 1, cross=0)[0], field], axis=1)
 
@@ -262,7 +262,7 @@
         following = rounded(following)
         older = lax.optimization_barrier(current)
         current = following
-    locked = jnp.concatenate([bottom, locked], axis=0)
+    locked = lax.optimization_barrier(jnp.concatenate([bottom, locked], axis=0))
     other_locked = jnp.concatenate([other_late, other_early], axis=0)
     both_locked = [grid.partner(l, SECOND) for l in (locked, other_locked)]
     low = plane(partial, 1, 0).astype(jnp.bfloat16)

time: 76.6 us -> 76.1 us (level)
  waiting for transfers between devices: 33.7 us -> 27.6 us
  starting transfers between devices: 27.3 us -> 32.2 us
    ppermute x13, starting transfers between devices: 19.7 us -> 23.3 us  [swapped(): arrived = lax.ppermute(jnp.where(lower, high, low), AXIS, pairs)]
    ppermute x12, waiting for transfers between devices: 16.2 us -> 13.1 us  [partner(): lax.ppermute(value, AXIS, [(i, i ^ bits) for i in range(self.devices)])]
    ppermute x13, waiting for transfers between devices: 17.5 us -> 14.5 us  [swapped(): arrived = lax.ppermute(jnp.where(lower, high, low), AXIS, pairs)]
    ppermute x12, starting transfers between devices: 7.54 us -> 8.89 us  [partner(): lax.ppermute(value, AXIS, [(i, i ^ bits) for i in range(self.devices)])]
  transfers between devices with their start and end apart: 25 -> 25, of which waited for: 17 -> 17; matrix products, arithmetic and copies ran while one was open for 10% -> 9% of each run, Pallas kernels for 0% -> 0%
where the time goes in v17:
time: 76.1 us; the launch traced here: 75.9 us
  starting transfers between devices  32.2 us (42%)
  waiting for transfers between devices  27.6 us (36%)
  other arithmetic  5.03 us (7%)
  matrix products  4.87 us (6%)
  local copies, waits for them, and re-layouts  4.61 us (6%)
  between operations  1.63 us (2%)
    ppermute x13, starting transfers between devices, swapped(): arrived = lax.ppermute(jnp.where(lower, high, low), AXIS, pairs)  23.3 us
    ppermute x13, waiting for transfers between devices, swapped(): arrived = lax.ppermute(jnp.where(lower, high, low), AXIS, pairs)  14.5 us
    ppermute x12, waiting for transfers between devices, partner(): lax.ppermute(value, AXIS, [(i, i ^ bits) for i in range(self.devices)])  13.1 us
    ppermute x12, starting transfers between devices, partner(): lax.ppermute(value, AXIS, [(i, i ^ bits) for i in range(self.devices)])  8.89 us
    dot_general x12, matrix products, per_device(): jnp.dot(matrices[r], own, preferred_element_type=jnp.float32)  2.93 us
  transfers between devices with their start and end apart: 25, of which 17 were waited for; matrix products, arithmetic and copies ran while one was open for 9% of the time, Pallas kernels for 0%

profile of v17, /device:TPU:0, one launch (start us, length us, event | category | flops | bytes accessed | tf_op | source)
XLA Modules:
  0.0 75.9 jit_solution(2921498962214770709)
XLA Ops:
  0.6 0.9 %reshape.124 = bf16[6,6,6,128]{3,2,1,0:T(8,128)(2,1)S(1)} reshape(bf16[216,128]{1,0:T(8,128)(2,1)} %param.5) | data formatting | bytes 110592 | tf_op jit(solution)/shard_map/reshape | solution.py:193
  3.6 3.0 %collective-permute-start = (bf16[6,1,6,128]{3,2,1,0:T(8,128)(2,1)S(1)}, bf16[6,1,6,128]{3,2,1,0:T(8,128)(2,1)S(1)}, u32[]{:S(2)}, u32[]{:S(2)}) collective-permute-start(bf16[6,1,6,128]{3,2,1,0:T(8,128)(2,1)S(1)} %slice.535), channel_id=1, source_target_pairs={{0,4},{1,5},{2,6},{3,7},{4,0},{5,1},{6,2},{7,3},{8,12},{9,13},{10,... | collective-permute-start | bytes 27656 | tf_op jit(solution)/shard_map/ppermute | solution.py:41
  6.7 1.5 %collective-permute-start.1 = (bf16[6,1,6,128]{3,2,1,0:T(8,128)(2,1)S(1)}, bf16[6,1,6,128]{3,2,1,0:T(8,128)(2,1)S(1)}, u32[]{:S(2)}, u32[]{:S(2)}) collective-permute-start(bf16[6,1,6,128]{3,2,1,0:T(8,128)(2,1)S(1)} %slice.535), channel_id=1, source_target_pairs={{0,12},{1,13},{2,14},{3,15},{4,8},{5,9},{6,10},{7,11},{8,4},{9,5},... | collective-permute-start | bytes 27656 | tf_op jit(solution)/shard_map/ppermute | solution.py:41
  8.6 1.4 %collective-permute-start.7 = (bf16[124,704]{1,0:T(8,128)(2,1)S(1)}, bf16[124,704]{1,0:T(8,128)(2,1)S(1)}, u32[]{:S(2)}, u32[]{:S(2)}) collective-permute-start(bf16[124,704]{1,0:T(8,128)(2,1)S(1)} %slice.443), channel_id=1, source_target_pairs={{0,3},{1,2},{2,1},{3,0},{4,7},{5,6},{6,5},{7,4},{8,11},{9,10},{10,... | collective-permute-start | bytes 523784 | tf_op jit(solution)/shard_map/ppermute | solution.py:59
  10.3 0.9 %collective-permute-done.1 = bf16[6,1,6,128]{3,2,1,0:T(8,128)(2,1)S(1)} collective-permute-done((bf16[6,1,6,128]{3,2,1,0:T(8,128)(2,1)S(1)}, bf16[6,1,6,128]{3,2,1,0:T(8,128)(2,1)S(1)}, u32[]{:S(2)}, u32[]{:S(2)}) %collective-permute-start.1) | collective-permute-done | bytes 9248 | tf_op jit(solution)/shard_map/ppermute | solution.py:41
  11.7 2.7 %collective-permute-start.2 = (bf16[258,128]{1,0:T(8,128)(2,1)S(1)}, bf16[258,128]{1,0:T(8,128)(2,1)S(1)}, u32[]{:S(2)}, u32[]{:S(2)}) collective-permute-start(bf16[258,128]{1,0:T(8,128)(2,1)S(1)} %concatenate.144), channel_id=1, source_target_pairs={{0,16},{1,17},{2,18},{3,19},{4,20},{5,21},{6,22},{7,23},{8,24},{9,... | collective-permute-start | bytes 198152 | tf_op jit(solution)/shard_map/ppermute | solution.py:41
  14.4 2.6 %collective-permute-done.2 = bf16[258,128]{1,0:T(8,128)(2,1)S(1)} collective-permute-done((bf16[258,128]{1,0:T(8,128)(2,1)S(1)}, bf16[258,128]{1,0:T(8,128)(2,1)S(1)}, u32[]{:S(2)}, u32[]{:S(2)}) %collective-permute-start.2) | collective-permute-done | bytes 66080 | tf_op jit(solution)/shard_map/ppermute | solution.py:41
  17.6 4.2 %collective-permute-done.3 = bf16[152,128]{1,0:T(8,128)(2,1)S(1)} collective-permute-done((bf16[152,128]{1,0:T(8,128)(2,1)S(1)}, bf16[152,128]{1,0:T(8,128)(2,1)S(1)}, u32[]{:S(2)}, u32[]{:S(2)}) %collective-permute-start.3) | collective-permute-done | bytes 38944 | tf_op jit(solution)/shard_map/ppermute | solution.py:59
  25.5 1.4 %collective-permute-start.10 = (bf16[7,1,7,128]{3,2,1,0:T(8,128)(2,1)S(1)}, bf16[7,1,7,128]{3,2,1,0:T(8,128)(2,1)S(1)}, u32[]{:S(2)}, u32[]{:S(2)}) collective-permute-start(bf16[7,1,7,128]{3,2,1,0:T(8,128)(2,1)S(1)} %broadcast_select_fusion.45), channel_id=1, source_target_pairs={{0,13},{1,12},{2,15},{3,14},{4,9},{5,8},{6,11},{7,10},{8,5},{9,4},... | collective-permute-start | bytes 37640 | tf_op jit(solution)/shard_map/ppermute | solution.py:41
  26.9 0.9 %collective-permute-start.9 = (bf16[7,1,7,128]{3,2,1,0:T(8,128)(2,1)S(1)}, bf16[7,1,7,128]{3,2,1,0:T(8,128)(2,1)S(1)}, u32[]{:S(2)}, u32[]{:S(2)}) collective-permute-start(bf16[7,1,7,128]{3,2,1,0:T(8,128)(2,1)S(1)} %get-tuple-element.32), channel_id=1, source_target_pairs={{0,5},{1,4},{2,7},{3,6},{4,1},{5,0},{6,3},{7,2},{8,13},{9,12},{10,... | collective-permute-start | bytes 37640 | tf_op jit(solution)/shard_map/ppermute | solution.py:41
  27.8 1.8 %collective-permute-done.10 = bf16[7,1,7,128]{3,2,1,0:T(8,128)(2,1)S(1)} collective-permute-done((bf16[7,1,7,128]{3,2,1,0:T(8,128)(2,1)S(1)}, bf16[7,1,7,128]{3,2,1,0:T(8,128)(2,1)S(1)}, u32[]{:S(2)}, u32[]{:S(2)}) %collective-permute-start.10) | collective-permute-done | bytes 12576 | tf_op jit(solution)/shard_map/ppermute | solution.py:41
  30.2 2.7 %collective-permute-start.11 = (bf16[1,7,7,128]{3,2,1,0:T(8,128)(2,1)S(1)}, bf16[1,7,7,128]{3,2,1,0:T(8,128)(2,1)S(1)}, u32[]{:S(2)}, u32[]{:S(2)}) collective-permute-start(bf16[1,7,7,128]{3,2,1,0:T(8,128)(2,1)S(1)} %fusion.83), channel_id=1, source_target_pairs={{0,17},{1,16},{2,19},{3,18},{4,21},{5,20},{6,23},{7,22},{8,25},{9,... | collective-permute-start | bytes 37640 | tf_op jit(solution)/shard_map/ppermute | solution.py:41
  33.4 0.9 %collective-permute-done.11 = bf16[1,7,7,128]{3,2,1,0:T(8,128)(2,1)S(1)} collective-permute-done((bf16[1,7,7,128]{3,2,1,0:T(8,128)(2,1)S(1)}, bf16[1,7,7,128]{3,2,1,0:T(8,128)(2,1)S(1)}, u32[]{:S(2)}, u32[]{:S(2)}) %collective-permute-start.11) | collective-permute-done | bytes 12576 | tf_op jit(solution)/shard_map/ppermute | solution.py:41
  35.9 1.4 %collective-permute-start.13 = (bf16[7,1,7,128]{3,2,1,0:T(8,128)(2,1)S(1)}, bf16[7,1,7,128]{3,2,1,0:T(8,128)(2,1)S(1)}, u32[]{:S(2)}, u32[]{:S(2)}) collective-permute-start(bf16[7,1,7,128]{3,2,1,0:T(8,128)(2,1)S(1)} %broadcast_select_fusion.44), channel_id=1, source_target_pairs={{0,13},{1,12},{2,15},{3,14},{4,9},{5,8},{6,11},{7,10},{8,5},{9,4},... | collective-permute-start | bytes 37640 | tf_op jit(solution)/shard_map/ppermute | solution.py:41
  37.3 1.4 %collective-permute-start.12 = (bf16[7,1,7,128]{3,2,1,0:T(8,128)(2,1)S(1)}, bf16[7,1,7,128]{3,2,1,0:T(8,128)(2,1)S(1)}, u32[]{:S(2)}, u32[]{:S(2)}) collective-permute-start(bf16[7,1,7,128]{3,2,1,0:T(8,128)(2,1)S(1)} %get-tuple-element.29), channel_id=1, source_target_pairs={{0,5},{1,4},{2,7},{3,6},{4,1},{5,0},{6,3},{7,2},{8,13},{9,12},{10,... | collective-permute-start | bytes 37640 | tf_op jit(solution)/shard_map/ppermute | solution.py:41
  38.7 0.8 %collective-permute-start.18 = (bf16[128,704]{1,0:T(8,128)(2,1)S(1)}, bf16[128,704]{1,0:T(8,128)(2,1)S(1)}, u32[]{:S(2)}, u32[]{:S(2)}) collective-permute-start(bf16[128,704]{1,0:T(8,128)(2,1)S(1)} %pad_maximum_fusion.2), channel_id=1, source_target_pairs={{0,3},{1,2},{2,1},{3,0},{4,7},{5,6},{6,5},{7,4},{8,11},{9,10},{10,... | collective-permute-start | bytes 540680 | tf_op jit(solution)/shard_map/ppermute | solution.py:59
  40.7 2.4 %collective-permute-start.14 = (bf16[1,7,7,128]{3,2,1,0:T(8,128)(2,1)S(1)}, bf16[1,7,7,128]{3,2,1,0:T(8,128)(2,1)S(1)}, u32[]{:S(2)}, u32[]{:S(2)}) collective-permute-start(bf16[1,7,7,128]{3,2,1,0:T(8,128)(2,1)S(1)} %fusion.84), channel_id=1, source_target_pairs={{0,17},{1,16},{2,19},{3,18},{4,21},{5,20},{6,23},{7,22},{8,25},{9,... | collective-permute-start | bytes 37640 | tf_op jit(solution)/shard_map/ppermute | solution.py:41
  43.1 2.6 %collective-permute-done.18 = bf16[128,704]{1,0:T(8,128)(2,1)S(1)} collective-permute-done((bf16[128,704]{1,0:T(8,128)(2,1)S(1)}, bf16[128,704]{1,0:T(8,128)(2,1)S(1)}, u32[]{:S(2)}, u32[]{:S(2)}) %collective-permute-start.18) | collective-permute-done | bytes 180256 | tf_op jit(solution)/shard_map/ppermute | solution.py:59
  47.9 1.3 %collective-permute-start.16 = (bf16[7,1,7,128]{3,2,1,0:T(8,128)(2,1)S(1)}, bf16[7,1,7,128]{3,2,1,0:T(8,128)(2,1)S(1)}, u32[]{:S(2)}, u32[]{:S(2)}) collective-permute-start(bf16[7,1,7,128]{3,2,1,0:T(8,128)(2,1)S(1)} %slice.746), channel_id=1, source_target_pairs={{0,13},{1,12},{2,15},{3,14},{4,9},{5,8},{6,11},{7,10},{8,5},{9,4},... | collective-permute-start | bytes 37640 | tf_op jit(solution)/shard_map/ppermute | solution.py:41
  49.5 0.9 %collective-permute-done.15 = bf16[7,1,7,128]{3,2,1,0:T(8,128)(2,1)S(1)} collective-permute-done((bf16[7,1,7,128]{3,2,1,0:T(8,128)(2,1)S(1)}, bf16[7,1,7,128]{3,2,1,0:T(8,128)(2,1)S(1)}, u32[]{:S(2)}, u32[]{:S(2)}) %collective-permute-start.15) | collective-permute-done | bytes 12576 | tf_op jit(solution)/shard_map/ppermute | solution.py:41
  50.5 1.5 %collective-permute-done.16 = bf16[7,1,7,128]{3,2,1,0:T(8,128)(2,1)S(1)} collective-permute-done((bf16[7,1,7,128]{3,2,1,0:T(8,128)(2,1)S(1)}, bf16[7,1,7,128]{3,2,1,0:T(8,128)(2,1)S(1)}, u32[]{:S(2)}, u32[]{:S(2)}) %collective-permute-start.16) | collective-permute-done | bytes 12576 | tf_op jit(solution)/shard_map/ppermute | solution.py:41
  54.0 2.4 %collective-permute-start.20 = (bf16[212,128]{1,0:T(8,128)(2,1)S(1)}, bf16[212,128]{1,0:T(8,128)(2,1)S(1)}, u32[]{:S(2)}, u32[]{:S(2)}) collective-permute-start(bf16[212,128]{1,0:T(8,128)(2,1)S(1)} %pad_maximum_fusion.11), channel_id=1, source_target_pairs={{0,17},{1,16},{2,19},{3,18},{4,21},{5,20},{6,23},{7,22},{8,25},{9,... | collective-permute-start | bytes 162824 | tf_op jit(solution)/shard_map/ppermute | solution.py:59
  56.4 2.3 %collective-permute-done.20 = bf16[212,128]{1,0:T(8,128)(2,1)S(1)} collective-permute-done((bf16[212,128]{1,0:T(8,128)(2,1)S(1)}, bf16[212,128]{1,0:T(8,128)(2,1)S(1)}, u32[]{:S(2)}, u32[]{:S(2)}) %collective-permute-start.20) | collective-permute-done | bytes 54304 | tf_op jit(solution)/shard_map/ppermute | solution.py:59
  58.8 2.3 %collective-permute-start.21 = (bf16[176,128]{1,0:T(8,128)(2,1)S(1)}, bf16[176,128]{1,0:T(8,128)(2,1)S(1)}, u32[]{:S(2)}, u32[]{:S(2)}) collective-permute-start(bf16[176,128]{1,0:T(8,128)(2,1)S(1)} %add_convert_fusion.2), channel_id=1, source_target_pairs={{0,5},{1,4},{2,7},{3,6},{4,1},{5,0},{6,3},{7,2},{8,13},{9,12},{10,... | collective-permute-start | bytes 135176 | tf_op jit(solution)/shard_map/ppermute | solution.py:41
  61.3 1.6 %collective-permute-done.21 = bf16[176,128]{1,0:T(8,128)(2,1)S(1)} collective-permute-done((bf16[176,128]{1,0:T(8,128)(2,1)S(1)}, bf16[176,128]{1,0:T(8,128)(2,1)S(1)}, u32[]{:S(2)}, u32[]{:S(2)}) %collective-permute-start.21) | collective-permute-done | bytes 45088 | tf_op jit(solution)/shard_map/ppermute | solution.py:41
  62.8 1.7 %collective-permute-start.22 = (bf16[176,128]{1,0:T(8,128)(2,1)S(1)}, bf16[176,128]{1,0:T(8,128)(2,1)S(1)}, u32[]{:S(2)}, u32[]{:S(2)}) collective-permute-start(bf16[176,128]{1,0:T(8,128)(2,1)S(1)} %add_convert_fusion.1), channel_id=1, source_target_pairs={{0,13},{1,12},{2,15},{3,14},{4,9},{5,8},{6,11},{7,10},{8,5},{9,4},... | collective-permute-start | bytes 135176 | tf_op jit(solution)/shard_map/ppermute | solution.py:41
  64.6 2.7 %collective-permute-done.22 = bf16[176,128]{1,0:T(8,128)(2,1)S(1)} collective-permute-done((bf16[176,128]{1,0:T(8,128)(2,1)S(1)}, bf16[176,128]{1,0:T(8,128)(2,1)S(1)}, u32[]{:S(2)}, u32[]{:S(2)}) %collective-permute-start.22) | collective-permute-done | bytes 45088 | tf_op jit(solution)/shard_map/ppermute | solution.py:41
  67.4 1.6 %collective-permute-start.23 = (bf16[284,128]{1,0:T(8,128)(2,1)S(1)}, bf16[284,128]{1,0:T(8,128)(2,1)S(1)}, u32[]{:S(2)}, u32[]{:S(2)}) collective-permute-start(bf16[284,128]{1,0:T(8,128)(2,1)S(1)} %maximum_maximum_fusion.2), channel_id=1, source_target_pairs={{0,3},{1,2},{2,1},{3,0},{4,7},{5,6},{6,5},{7,4},{8,11},{9,10},{10,... | collective-permute-start | bytes 218120 | tf_op jit(solution)/shard_map/ppermute | solution.py:59
  69.0 2.3 %collective-permute-done.23 = bf16[284,128]{1,0:T(8,128)(2,1)S(1)} collective-permute-done((bf16[284,128]{1,0:T(8,128)(2,1)S(1)}, bf16[284,128]{1,0:T(8,128)(2,1)S(1)}, u32[]{:S(2)}, u32[]{:S(2)}) %collective-permute-start.23) | collective-permute-done | bytes 72736 | tf_op jit(solution)/shard_map/ppermute | solution.py:59
  71.5 1.0 %collective-permute-start.24 = (bf16[460,128]{1,0:T(8,128)(2,1)S(1)}, bf16[460,128]{1,0:T(8,128)(2,1)S(1)}, u32[]{:S(2)}, u32[]{:S(2)}) collective-permute-start(bf16[460,128]{1,0:T(8,128)(2,1)S(1)} %maximum_maximum_fusion), channel_id=1, source_target_pairs={{0,1},{1,0},{2,3},{3,2},{4,5},{5,4},{6,7},{7,6},{8,9},{9,8},{10,11... | collective-permute-start | bytes 353288 | tf_op jit(solution)/shard_map/ppermute | solution.py:59
  72.5 1.0 %collective-permute-done.24 = bf16[460,128]{1,0:T(8,128)(2,1)S(1)} collective-permute-done((bf16[460,128]{1,0:T(8,128)(2,1)S(1)}, bf16[460,128]{1,0:T(8,128)(2,1)S(1)}, u32[]{:S(2)}, u32[]{:S(2)}) %collective-permute-start.24) | collective-permute-done | bytes 117792 | tf_op jit(solution)/shard_map/ppermute | solution.py:59
  74.9 1.0 %maximum_convert_fusion = f32[704,128]{1,0:T(8,128)} fusion(bf16[176,32]{1,0:T(8,128)(2,1)S(1)} %get-tuple-element.115, bf16[176,32]{1,0:T(8,128)(2,1)S(1)} %get-tuple-element.111, bf16[176,32]{1,0:T(8,128)(2,1)S(1)} %get-tuple-element.107, bf16[176,32]{1,0:T(8,128)(2,1)S(1)} %get-tuple-element.103, bf16[176,32]{1,0:T(8,128)(2,1)S(1)} %get-tuple-element.116, ...), kind=kLoop, calls=%fused_computation.51 | loop fusion | flops 2883584 | bytes 540672 | tf_op jit(solution)/shard_map/convert_element_type | solution.py:331
  (166 shorter events, 17.2 us)
Async XLA Ops:
  0.6 1.6 %copy-start = (bf16[1,343,343]{2,1,0:T(8,128)(2,1)S(1)}, bf16[1,343,343]{2,1,0:T(8,128)(2,1)}, u32[]{:S(2)}) copy-start(bf16[1,343,343]{2,1,0:T(8,128)(2,1)} %param.6) | copy-start | bytes 705898
  1.5 0.7 copy-start.2
  2.2 0.7 copy-start.3
  2.9 5.7 %copy-start.1 = (bf16[216,704]{1,0:T(8,128)(2,1)S(1)}, bf16[216,704]{1,0:T(8,128)(2,1)}, u32[]{:S(2)}) copy-start(bf16[216,704]{1,0:T(8,128)(2,1)} %param.9) | copy-start | bytes 912388
  3.6 6.7 %collective-permute-start = (bf16[6,1,6,128]{3,2,1,0:T(8,128)(2,1)S(1)}, bf16[6,1,6,128]{3,2,1,0:T(8,128)(2,1)S(1)}, u32[]{:S(2)}, u32[]{:S(2)}) collective-permute-start(bf16[6,1,6,128]{3,2,1,0:T(8,128)(2,1)S(1)} %slice.535), channel_id=1, source_target_pairs={{0,4},{1,5},{2,6},{3,7},{4,0},{5,1},{6,2},{7,3},{8,12},{9,13},{10,... | collective-permute-start | bytes 27656 | tf_op jit(solution)/shard_map/ppermute | solution.py:41
  6.7 4.6 %collective-permute-start.1 = (bf16[6,1,6,128]{3,2,1,0:T(8,128)(2,1)S(1)}, bf16[6,1,6,128]{3,2,1,0:T(8,128)(2,1)S(1)}, u32[]{:S(2)}, u32[]{:S(2)}) collective-permute-start(bf16[6,1,6,128]{3,2,1,0:T(8,128)(2,1)S(1)} %slice.535), channel_id=1, source_target_pairs={{0,12},{1,13},{2,14},{3,15},{4,8},{5,9},{6,10},{7,11},{8,4},{9,5},... | collective-permute-start | bytes 27656 | tf_op jit(solution)/shard_map/ppermute | solution.py:41
  8.2 13.9 %collective-permute-start.4 = (bf16[343,343]{1,0:T(8,128)(2,1)S(1)}, bf16[343,343]{1,0:T(8,128)(2,1)S(1)}, u32[]{:S(2)}, u32[]{:S(2)}) collective-permute-start(bf16[343,343]{1,0:T(8,128)(2,1)S(1)} %fusion), channel_id=1, source_target_pairs={{0,3},{1,2},{2,1},{3,0},{4,7},{5,6},{6,5},{7,4},{8,11},{9,10},{10,... | collective-permute-start | bytes 705902 | tf_op jit(solution)/shard_map/ppermute | solution.py:59
  8.6 15.3 %collective-permute-start.7 = (bf16[124,704]{1,0:T(8,128)(2,1)S(1)}, bf16[124,704]{1,0:T(8,128)(2,1)S(1)}, u32[]{:S(2)}, u32[]{:S(2)}) collective-permute-start(bf16[124,704]{1,0:T(8,128)(2,1)S(1)} %slice.443), channel_id=1, source_target_pairs={{0,3},{1,2},{2,1},{3,0},{4,7},{5,6},{6,5},{7,4},{8,11},{9,10},{10,... | collective-permute-start | bytes 523784 | tf_op jit(solution)/shard_map/ppermute | solution.py:59
  11.7 5.3 %collective-permute-start.2 = (bf16[258,128]{1,0:T(8,128)(2,1)S(1)}, bf16[258,128]{1,0:T(8,128)(2,1)S(1)}, u32[]{:S(2)}, u32[]{:S(2)}) collective-permute-start(bf16[258,128]{1,0:T(8,128)(2,1)S(1)} %concatenate.144), channel_id=1, source_target_pairs={{0,16},{1,17},{2,18},{3,19},{4,20},{5,21},{6,22},{7,23},{8,24},{9,... | collective-permute-start | bytes 198152 | tf_op jit(solution)/shard_map/ppermute | solution.py:41
  14.4 10.2 %collective-permute-start.8 = (bf16[343,343]{1,0:T(8,128)(2,1)S(1)}, bf16[343,343]{1,0:T(8,128)(2,1)S(1)}, u32[]{:S(2)}, u32[]{:S(2)}) collective-permute-start(bf16[343,343]{1,0:T(8,128)(2,1)S(1)} %fusion), channel_id=1, source_target_pairs={{0,1},{1,0},{2,3},{3,2},{4,5},{5,4},{6,7},{7,6},{8,9},{9,8},{10,11... | collective-permute-start | bytes 705902 | tf_op jit(solution)/shard_map/ppermute | solution.py:59
  17.5 4.4 %collective-permute-start.3 = (bf16[152,128]{1,0:T(8,128)(2,1)S(1)}, bf16[152,128]{1,0:T(8,128)(2,1)S(1)}, u32[]{:S(2)}, u32[]{:S(2)}) collective-permute-start(bf16[152,128]{1,0:T(8,128)(2,1)S(1)} %pad_maximum_fusion.16), channel_id=1, source_target_pairs={{0,3},{1,2},{2,1},{3,0},{4,7},{5,6},{6,5},{7,4},{8,11},{9,10},{10,... | collective-permute-start | bytes 116744 | tf_op jit(solution)/shard_map/ppermute | solution.py:59
  22.1 1.3 %collective-permute-start.5 = (bf16[152,128]{1,0:T(8,128)(2,1)S(1)}, bf16[152,128]{1,0:T(8,128)(2,1)S(1)}, u32[]{:S(2)}, u32[]{:S(2)}) collective-permute-start(bf16[152,128]{1,0:T(8,128)(2,1)S(1)} %pad_maximum_fusion.17), channel_id=1, source_target_pairs={{0,1},{1,0},{2,3},{3,2},{4,5},{5,4},{6,7},{7,6},{8,9},{9,8},{10,11... | collective-permute-start | bytes 116744 | tf_op jit(solution)/shard_map/ppermute | solution.py:59
  22.3 1.6 %collective-permute-start.6 = (bf16[343,343]{1,0:T(8,128)(2,1)S(1)}, bf16[343,343]{1,0:T(8,128)(2,1)S(1)}, u32[]{:S(2)}, u32[]{:S(2)}) collective-permute-start(bf16[343,343]{1,0:T(8,128)(2,1)S(1)} %collective-permute-done.4), channel_id=1, source_target_pairs={{0,1},{1,0},{2,3},{3,2},{4,5},{5,4},{6,7},{7,6},{8,9},{9,8},{10,11... | collective-permute-start | bytes 705902 | tf_op jit(solution)/shard_map/ppermute | solution.py:59
  25.5 4.1 %collective-permute-start.10 = (bf16[7,1,7,128]{3,2,1,0:T(8,128)(2,1)S(1)}, bf16[7,1,7,128]{3,2,1,0:T(8,128)(2,1)S(1)}, u32[]{:S(2)}, u32[]{:S(2)}) collective-permute-start(bf16[7,1,7,128]{3,2,1,0:T(8,128)(2,1)S(1)} %broadcast_select_fusion.45), channel_id=1, source_target_pairs={{0,13},{1,12},{2,15},{3,14},{4,9},{5,8},{6,11},{7,10},{8,5},{9,4},... | collective-permute-start | bytes 37640 | tf_op jit(solution)/shard_map/ppermute | solution.py:41
  26.9 3.2 %collective-permute-start.9 = (bf16[7,1,7,128]{3,2,1,0:T(8,128)(2,1)S(1)}, bf16[7,1,7,128]{3,2,1,0:T(8,128)(2,1)S(1)}, u32[]{:S(2)}, u32[]{:S(2)}) collective-permute-start(bf16[7,1,7,128]{3,2,1,0:T(8,128)(2,1)S(1)} %get-tuple-element.32), channel_id=1, source_target_pairs={{0,5},{1,4},{2,7},{3,6},{4,1},{5,0},{6,3},{7,2},{8,13},{9,12},{10,... | collective-permute-start | bytes 37640 | tf_op jit(solution)/shard_map/ppermute | solution.py:41
  30.2 4.1 %collective-permute-start.11 = (bf16[1,7,7,128]{3,2,1,0:T(8,128)(2,1)S(1)}, bf16[1,7,7,128]{3,2,1,0:T(8,128)(2,1)S(1)}, u32[]{:S(2)}, u32[]{:S(2)}) collective-permute-start(bf16[1,7,7,128]{3,2,1,0:T(8,128)(2,1)S(1)} %fusion.83), channel_id=1, source_target_pairs={{0,17},{1,16},{2,19},{3,18},{4,21},{5,20},{6,23},{7,22},{8,25},{9,... | collective-permute-start | bytes 37640 | tf_op jit(solution)/shard_map/ppermute | solution.py:41
  33.0 19.9 %collective-permute-start.17 = (bf16[252,704]{1,0:T(8,128)(2,1)S(1)}, bf16[252,704]{1,0:T(8,128)(2,1)S(1)}, u32[]{:S(2)}, u32[]{:S(2)}) collective-permute-start(bf16[252,704]{1,0:T(8,128)(2,1)S(1)} %pad_maximum_fusion), channel_id=1, source_target_pairs={{0,1},{1,0},{2,3},{3,2},{4,5},{5,4},{6,7},{7,6},{8,9},{9,8},{10,11... | collective-permute-start | bytes 1064456 | tf_op jit(solution)/shard_map/ppermute | solution.py:59
  35.8 2.9 %slice-start = ((bf16[216,704]{1,0:T(8,128)(2,1)}), bf16[92,704]{1,0:T(8,128)(2,1)S(1)}, s32[]{:S(2)}) async-start(bf16[216,704]{1,0:T(8,128)(2,1)} %param.9), calls=%async_computation | async-start | bytes 294912 | tf_op jit(solution)/shard_map/slice | solution.py:210
  35.9 4.1 %collective-permute-start.13 = (bf16[7,1,7,128]{3,2,1,0:T(8,128)(2,1)S(1)}, bf16[7,1,7,128]{3,2,1,0:T(8,128)(2,1)S(1)}, u32[]{:S(2)}, u32[]{:S(2)}) collective-permute-start(bf16[7,1,7,128]{3,2,1,0:T(8,128)(2,1)S(1)} %broadcast_select_fusion.44), channel_id=1, source_target_pairs={{0,13},{1,12},{2,15},{3,14},{4,9},{5,8},{6,11},{7,10},{8,5},{9,4},... | collective-permute-start | bytes 37640 | tf_op jit(solution)/shard_map/ppermute | solution.py:41
  37.3 3.3 %collective-permute-start.12 = (bf16[7,1,7,128]{3,2,1,0:T(8,128)(2,1)S(1)}, bf16[7,1,7,128]{3,2,1,0:T(8,128)(2,1)S(1)}, u32[]{:S(2)}, u32[]{:S(2)}) collective-permute-start(bf16[7,1,7,128]{3,2,1,0:T(8,128)(2,1)S(1)} %get-tuple-element.29), channel_id=1, source_target_pairs={{0,5},{1,4},{2,7},{3,6},{4,1},{5,0},{6,3},{7,2},{8,13},{9,12},{10,... | collective-permute-start | bytes 37640 | tf_op jit(solution)/shard_map/ppermute | solution.py:41
  38.7 6.9 %collective-permute-start.18 = (bf16[128,704]{1,0:T(8,128)(2,1)S(1)}, bf16[128,704]{1,0:T(8,128)(2,1)S(1)}, u32[]{:S(2)}, u32[]{:S(2)}) collective-permute-start(bf16[128,704]{1,0:T(8,128)(2,1)S(1)} %pad_maximum_fusion.2), channel_id=1, source_target_pairs={{0,3},{1,2},{2,1},{3,0},{4,7},{5,6},{6,5},{7,4},{8,11},{9,10},{10,... | collective-permute-start | bytes 540680 | tf_op jit(solution)/shard_map/ppermute | solution.py:59
  40.7 5.0 %collective-permute-start.14 = (bf16[1,7,7,128]{3,2,1,0:T(8,128)(2,1)S(1)}, bf16[1,7,7,128]{3,2,1,0:T(8,128)(2,1)S(1)}, u32[]{:S(2)}, u32[]{:S(2)}) collective-permute-start(bf16[1,7,7,128]{3,2,1,0:T(8,128)(2,1)S(1)} %fusion.84), channel_id=1, source_target_pairs={{0,17},{1,16},{2,19},{3,18},{4,21},{5,20},{6,23},{7,22},{8,25},{9,... | collective-permute-start | bytes 37640 | tf_op jit(solution)/shard_map/ppermute | solution.py:41
  47.2 3.2 %collective-permute-start.15 = (bf16[7,1,7,128]{3,2,1,0:T(8,128)(2,1)S(1)}, bf16[7,1,7,128]{3,2,1,0:T(8,128)(2,1)S(1)}, u32[]{:S(2)}, u32[]{:S(2)}) collective-permute-start(bf16[7,1,7,128]{3,2,1,0:T(8,128)(2,1)S(1)} %slice.746), channel_id=1, source_target_pairs={{0,5},{1,4},{2,7},{3,6},{4,1},{5,0},{6,3},{7,2},{8,13},{9,12},{10,... | collective-permute-start | bytes 37640 | tf_op jit(solution)/shard_map/ppermute | solution.py:41
  47.9 4.0 %collective-permute-start.16 = (bf16[7,1,7,128]{3,2,1,0:T(8,128)(2,1)S(1)}, bf16[7,1,7,128]{3,2,1,0:T(8,128)(2,1)S(1)}, u32[]{:S(2)}, u32[]{:S(2)}) collective-permute-start(bf16[7,1,7,128]{3,2,1,0:T(8,128)(2,1)S(1)} %slice.746), channel_id=1, source_target_pairs={{0,13},{1,12},{2,15},{3,14},{4,9},{5,8},{6,11},{7,10},{8,5},{9,4},... | collective-permute-start | bytes 37640 | tf_op jit(solution)/shard_map/ppermute | solution.py:41
  49.3 3.9 %collective-permute-start.19 = (bf16[252,704]{1,0:T(8,128)(2,1)S(1)}, bf16[252,704]{1,0:T(8,128)(2,1)S(1)}, u32[]{:S(2)}, u32[]{:S(2)}) collective-permute-start(bf16[252,704]{1,0:T(8,128)(2,1)S(1)} %constant_dynamic-update-slice_fusion.6), channel_id=1, source_target_pairs={{0,1},{1,0},{2,3},{3,2},{4,5},{5,4},{6,7},{7,6},{8,9},{9,8},{10,11... | collective-permute-start | bytes 1064456 | tf_op jit(solution)/shard_map/ppermute | solution.py:59
  54.0 4.7 %collective-permute-start.20 = (bf16[212,128]{1,0:T(8,128)(2,1)S(1)}, bf16[212,128]{1,0:T(8,128)(2,1)S(1)}, u32[]{:S(2)}, u32[]{:S(2)}) collective-permute-start(bf16[212,128]{1,0:T(8,128)(2,1)S(1)} %pad_maximum_fusion.11), channel_id=1, source_target_pairs={{0,17},{1,16},{2,19},{3,18},{4,21},{5,20},{6,23},{7,22},{8,25},{9,... | collective-permute-start | bytes 162824 | tf_op jit(solution)/shard_map/ppermute | solution.py:59
  58.8 4.0 %collective-permute-start.21 = (bf16[176,128]{1,0:T(8,128)(2,1)S(1)}, bf16[176,128]{1,0:T(8,128)(2,1)S(1)}, u32[]{:S(2)}, u32[]{:S(2)}) collective-permute-start(bf16[176,128]{1,0:T(8,128)(2,1)S(1)} %add_convert_fusion.2), channel_id=1, source_target_pairs={{0,5},{1,4},{2,7},{3,6},{4,1},{5,0},{6,3},{7,2},{8,13},{9,12},{10,... | collective-permute-start | bytes 135176 | tf_op jit(solution)/shard_map/ppermute | solution.py:41
  62.8 4.4 %collective-permute-start.22 = (bf16[176,128]{1,0:T(8,128)(2,1)S(1)}, bf16[176,128]{1,0:T(8,128)(2,1)S(1)}, u32[]{:S(2)}, u32[]{:S(2)}) collective-permute-start(bf16[176,128]{1,0:T(8,128)(2,1)S(1)} %add_convert_fusion.1), channel_id=1, source_target_pairs={{0,13},{1,12},{2,15},{3,14},{4,9},{5,8},{6,11},{7,10},{8,5},{9,4},... | collective-permute-start | bytes 135176 | tf_op jit(solution)/shard_map/ppermute | solution.py:41
  67.4 3.8 %collective-permute-start.23 = (bf16[284,128]{1,0:T(8,128)(2,1)S(1)}, bf16[284,128]{1,0:T(8,128)(2,1)S(1)}, u32[]{:S(2)}, u32[]{:S(2)}) collective-permute-start(bf16[284,128]{1,0:T(8,128)(2,1)S(1)} %maximum_maximum_fusion.2), channel_id=1, source_target_pairs={{0,3},{1,2},{2,1},{3,0},{4,7},{5,6},{6,5},{7,4},{8,11},{9,10},{10,... | collective-permute-start | bytes 218120 | tf_op jit(solution)/shard_map/ppermute | solution.py:59
  71.5 2.0 %collective-permute-start.24 = (bf16[460,128]{1,0:T(8,128)(2,1)S(1)}, bf16[460,128]{1,0:T(8,128)(2,1)S(1)}, u32[]{:S(2)}, u32[]{:S(2)}) collective-permute-start(bf16[460,128]{1,0:T(8,128)(2,1)S(1)} %maximum_maximum_fusion), channel_id=1, source_target_pairs={{0,1},{1,0},{2,3},{3,2},{4,5},{5,4},{6,7},{7,6},{8,9},{9,8},{10,11... | collective-permute-start | bytes 353288 | tf_op jit(solution)/shard_map/ppermute | solution.py:59

commit v18 on v17

--- a/solution.py
+++ b/solution.py
@@ -192,15 +192,15 @@
 
     field = block.reshape(edge, edge, edge, columns)
     high = plane(field, 1, edge - 1)
+    cell_matrix, high = lax.optimization_barrier((cell_matrix, high))
     matrix = by_rows(slots_matrix(cell_matrix, connectivity, potential))
-    matrix, high = lax.optimization_barrier((matrix, high))
     other = by_rows(grid.partner(matrix, FIRST))
     field = jnp.concatenate([grid.exchanged(high, high, 1, cross=0)[0], field], axis=1)
 
     high = field[edge - 1].reshape(SIDE * edge, columns)
     tiles = -(-locked.shape[1] // columns)
     top = jnp.pad(locked[-edge * edge :], ((0, 0), (0, -locked.shape[1] % columns)))
-    top = jnp.concatenate(split(top, tiles), axis=0)
+    top = lax.optimization_barrier(jnp.concatenate(split(top, tiles), axis=0))
     sent = jnp.concatenate([top, high], axis=0)
     sent, matrix = lax.optimization_barrier((sent, matrix))
     arrived = grid.exchanged(sent, sent, 0, cross=0)[0]

time: 76.1 us -> 75.9 us (level)
  waiting for transfers between devices: 27.6 us -> 33.2 us
  starting transfers between devices: 32.2 us -> 27.6 us
  local copies, waits for them, and re-layouts: 4.61 us -> 3.34 us
    ppermute x13, waiting for transfers between devices: 14.5 us -> 18 us  [swapped(): arrived = lax.ppermute(jnp.where(lower, high, low), AXIS, pairs)]
    ppermute x13, starting transfers between devices: 23.3 us -> 19.9 us  [swapped(): arrived = lax.ppermute(jnp.where(lower, high, low), AXIS, pairs)]
    ppermute x12, waiting for transfers between devices: 13.1 us -> 15.2 us  [partner(): lax.ppermute(value, AXIS, [(i, i ^ bits) for i in range(self.devices)])]
    unnamed x14, local copies, waits for them, and re-layouts: 1.4 us -> 0.09 us
    ppermute x12, starting transfers between devices: 8.89 us -> 7.68 us  [partner(): lax.ppermute(value, AXIS, [(i, i ^ bits) for i in range(self.devices)])]
  transfers between devices with their start and end apart: 25 -> 25, of which waited for: 17 -> 16; matrix products, arithmetic and copies ran while one was open for 9% -> 10% of each run, Pallas kernels for 0% -> 0%
where the time goes in v18:
time: 75.9 us; the launch traced here: 75.7 us
  waiting for transfers between devices  33.2 us (44%)
  starting transfers between devices  27.6 us (36%)
  other arithmetic  5.04 us (7%)
  matrix products  4.87 us (6%)
  local copies, waits for them, and re-layouts  3.34 us (4%)
  between operations  1.72 us (2%)
    ppermute x13, starting transfers between devices, swapped(): arrived = lax.ppermute(jnp.where(lower, high, low), AXIS, pairs)  19.9 us
    ppermute x13, waiting for transfers between devices, swapped(): arrived = lax.ppermute(jnp.where(lower, high, low), AXIS, pairs)  18 us
    ppermute x12, waiting for transfers between devices, partner(): lax.ppermute(value, AXIS, [(i, i ^ bits) for i in range(self.devices)])  15.2 us
    ppermute x12, starting transfers between devices, partner(): lax.ppermute(value, AXIS, [(i, i ^ bits) for i in range(self.devices)])  7.68 us
    dot_general x12, matrix products, per_device(): jnp.dot(matrices[r], own, preferred_element_type=jnp.float32)  2.93 us
  transfers between devices with their start and end apart: 25, of which 16 were waited for; matrix products, arithmetic and copies ran while one was open for 10% of the time, Pallas kernels for 0%

profile of v18, /device:TPU:0, one launch (start us, length us, event | category | flops | bytes accessed | tf_op | source)
XLA Modules:
  0.0 75.7 jit_solution(17425052994567417221)
XLA Ops:
  0.6 0.9 %reshape.124 = bf16[6,6,6,128]{3,2,1,0:T(8,128)(2,1)S(1)} reshape(bf16[216,128]{1,0:T(8,128)(2,1)} %param.5) | data formatting | bytes 110592 | tf_op jit(solution)/shard_map/reshape | solution.py:193
  1.6 3.0 %collective-permute-start = (bf16[6,1,6,128]{3,2,1,0:T(8,128)(2,1)S(1)}, bf16[6,1,6,128]{3,2,1,0:T(8,128)(2,1)S(1)}, u32[]{:S(2)}, u32[]{:S(2)}) collective-permute-start(bf16[6,1,6,128]{3,2,1,0:T(8,128)(2,1)S(1)} %slice.535), channel_id=1, source_target_pairs={{0,4},{1,5},{2,6},{3,7},{4,0},{5,1},{6,2},{7,3},{8,12},{9,13},{10,... | collective-permute-start | bytes 27656 | tf_op jit(solution)/shard_map/ppermute | solution.py:41
  4.6 1.5 %collective-permute-start.1 = (bf16[6,1,6,128]{3,2,1,0:T(8,128)(2,1)S(1)}, bf16[6,1,6,128]{3,2,1,0:T(8,128)(2,1)S(1)}, u32[]{:S(2)}, u32[]{:S(2)}) collective-permute-start(bf16[6,1,6,128]{3,2,1,0:T(8,128)(2,1)S(1)} %slice.535), channel_id=1, source_target_pairs={{0,12},{1,13},{2,14},{3,15},{4,8},{5,9},{6,10},{7,11},{8,4},{9,5},... | collective-permute-start | bytes 27656 | tf_op jit(solution)/shard_map/ppermute | solution.py:41
  6.2 0.7 fusion
  7.4 1.4 %collective-permute-start.7 = (bf16[124,704]{1,0:T(8,128)(2,1)S(1)}, bf16[124,704]{1,0:T(8,128)(2,1)S(1)}, u32[]{:S(2)}, u32[]{:S(2)}) collective-permute-start(bf16[124,704]{1,0:T(8,128)(2,1)S(1)} %slice.443), channel_id=1, source_target_pairs={{0,3},{1,2},{2,1},{3,0},{4,7},{5,6},{6,5},{7,4},{8,11},{9,10},{10,... | collective-permute-start | bytes 523784 | tf_op jit(solution)/shard_map/ppermute | solution.py:59
  9.7 2.7 %collective-permute-start.2 = (bf16[258,128]{1,0:T(8,128)(2,1)S(1)}, bf16[258,128]{1,0:T(8,128)(2,1)S(1)}, u32[]{:S(2)}, u32[]{:S(2)}) collective-permute-start(bf16[258,128]{1,0:T(8,128)(2,1)S(1)} %pad_maximum_fusion.11), channel_id=1, source_target_pairs={{0,16},{1,17},{2,18},{3,19},{4,20},{5,21},{6,22},{7,23},{8,24},{9,... | collective-permute-start | bytes 198152 | tf_op jit(solution)/shard_map/ppermute | solution.py:41
  12.3 3.7 %collective-permute-done.2 = bf16[258,128]{1,0:T(8,128)(2,1)S(1)} collective-permute-done((bf16[258,128]{1,0:T(8,128)(2,1)S(1)}, bf16[258,128]{1,0:T(8,128)(2,1)S(1)}, u32[]{:S(2)}, u32[]{:S(2)}) %collective-permute-start.2) | collective-permute-done | bytes 66080 | tf_op jit(solution)/shard_map/ppermute | solution.py:41
  16.6 4.0 %collective-permute-done.3 = bf16[152,128]{1,0:T(8,128)(2,1)S(1)} collective-permute-done((bf16[152,128]{1,0:T(8,128)(2,1)S(1)}, bf16[152,128]{1,0:T(8,128)(2,1)S(1)}, u32[]{:S(2)}, u32[]{:S(2)}) %collective-permute-start.3) | collective-permute-done | bytes 38944 | tf_op jit(solution)/shard_map/ppermute | solution.py:59
  21.5 0.7 collective-permute-done.5
  24.3 1.4 %collective-permute-start.10 = (bf16[7,1,7,128]{3,2,1,0:T(8,128)(2,1)S(1)}, bf16[7,1,7,128]{3,2,1,0:T(8,128)(2,1)S(1)}, u32[]{:S(2)}, u32[]{:S(2)}) collective-permute-start(bf16[7,1,7,128]{3,2,1,0:T(8,128)(2,1)S(1)} %broadcast_select_fusion.45), channel_id=1, source_target_pairs={{0,13},{1,12},{2,15},{3,14},{4,9},{5,8},{6,11},{7,10},{8,5},{9,4},... | collective-permute-start | bytes 37640 | tf_op jit(solution)/shard_map/ppermute | solution.py:41
  25.9 2.5 %collective-permute-done.10 = bf16[7,1,7,128]{3,2,1,0:T(8,128)(2,1)S(1)} collective-permute-done((bf16[7,1,7,128]{3,2,1,0:T(8,128)(2,1)S(1)}, bf16[7,1,7,128]{3,2,1,0:T(8,128)(2,1)S(1)}, u32[]{:S(2)}, u32[]{:S(2)}) %collective-permute-start.10) | collective-permute-done | bytes 12576 | tf_op jit(solution)/shard_map/ppermute | solution.py:41
  29.0 2.6 %collective-permute-start.11 = (bf16[1,7,7,128]{3,2,1,0:T(8,128)(2,1)S(1)}, bf16[1,7,7,128]{3,2,1,0:T(8,128)(2,1)S(1)}, u32[]{:S(2)}, u32[]{:S(2)}) collective-permute-start(bf16[1,7,7,128]{3,2,1,0:T(8,128)(2,1)S(1)} %fusion.83), channel_id=1, source_target_pairs={{0,17},{1,16},{2,19},{3,18},{4,21},{5,20},{6,23},{7,22},{8,25},{9,... | collective-permute-start | bytes 37640 | tf_op jit(solution)/shard_map/ppermute | solution.py:41
  32.1 1.0 %collective-permute-done.11 = bf16[1,7,7,128]{3,2,1,0:T(8,128)(2,1)S(1)} collective-permute-done((bf16[1,7,7,128]{3,2,1,0:T(8,128)(2,1)S(1)}, bf16[1,7,7,128]{3,2,1,0:T(8,128)(2,1)S(1)}, u32[]{:S(2)}, u32[]{:S(2)}) %collective-permute-start.11) | collective-permute-done | bytes 12576 | tf_op jit(solution)/shard_map/ppermute | solution.py:41
  34.6 1.4 %collective-permute-start.13 = (bf16[7,1,7,128]{3,2,1,0:T(8,128)(2,1)S(1)}, bf16[7,1,7,128]{3,2,1,0:T(8,128)(2,1)S(1)}, u32[]{:S(2)}, u32[]{:S(2)}) collective-permute-start(bf16[7,1,7,128]{3,2,1,0:T(8,128)(2,1)S(1)} %broadcast_select_fusion.44), channel_id=1, source_target_pairs={{0,13},{1,12},{2,15},{3,14},{4,9},{5,8},{6,11},{7,10},{8,5},{9,4},... | collective-permute-start | bytes 37640 | tf_op jit(solution)/shard_map/ppermute | solution.py:41
  36.1 1.4 %collective-permute-start.12 = (bf16[7,1,7,128]{3,2,1,0:T(8,128)(2,1)S(1)}, bf16[7,1,7,128]{3,2,1,0:T(8,128)(2,1)S(1)}, u32[]{:S(2)}, u32[]{:S(2)}) collective-permute-start(bf16[7,1,7,128]{3,2,1,0:T(8,128)(2,1)S(1)} %get-tuple-element.29), channel_id=1, source_target_pairs={{0,5},{1,4},{2,7},{3,6},{4,1},{5,0},{6,3},{7,2},{8,13},{9,12},{10,... | collective-permute-start | bytes 37640 | tf_op jit(solution)/shard_map/ppermute | solution.py:41
  37.5 0.8 %collective-permute-start.18 = (bf16[128,704]{1,0:T(8,128)(2,1)S(1)}, bf16[128,704]{1,0:T(8,128)(2,1)S(1)}, u32[]{:S(2)}, u32[]{:S(2)}) collective-permute-start(bf16[128,704]{1,0:T(8,128)(2,1)S(1)} %pad_maximum_fusion.2), channel_id=1, source_target_pairs={{0,3},{1,2},{2,1},{3,0},{4,7},{5,6},{6,5},{7,4},{8,11},{9,10},{10,... | collective-permute-start | bytes 540680 | tf_op jit(solution)/shard_map/ppermute | solution.py:59
  39.4 2.5 %collective-permute-start.14 = (bf16[1,7,7,128]{3,2,1,0:T(8,128)(2,1)S(1)}, bf16[1,7,7,128]{3,2,1,0:T(8,128)(2,1)S(1)}, u32[]{:S(2)}, u32[]{:S(2)}) collective-permute-start(bf16[1,7,7,128]{3,2,1,0:T(8,128)(2,1)S(1)} %fusion.84), channel_id=1, source_target_pairs={{0,17},{1,16},{2,19},{3,18},{4,21},{5,20},{6,23},{7,22},{8,25},{9,... | collective-permute-start | bytes 37640 | tf_op jit(solution)/shard_map/ppermute | solution.py:41
  42.0 2.4 %collective-permute-done.18 = bf16[128,704]{1,0:T(8,128)(2,1)S(1)} collective-permute-done((bf16[128,704]{1,0:T(8,128)(2,1)S(1)}, bf16[128,704]{1,0:T(8,128)(2,1)S(1)}, u32[]{:S(2)}, u32[]{:S(2)}) %collective-permute-start.18) | collective-permute-done | bytes 180256 | tf_op jit(solution)/shard_map/ppermute | solution.py:59
  46.0 0.6 collective-permute-start.15
  46.7 1.0 %collective-permute-start.16 = (bf16[7,1,7,128]{3,2,1,0:T(8,128)(2,1)S(1)}, bf16[7,1,7,128]{3,2,1,0:T(8,128)(2,1)S(1)}, u32[]{:S(2)}, u32[]{:S(2)}) collective-permute-start(bf16[7,1,7,128]{3,2,1,0:T(8,128)(2,1)S(1)} %slice.746), channel_id=1, source_target_pairs={{0,13},{1,12},{2,15},{3,14},{4,9},{5,8},{6,11},{7,10},{8,5},{9,4},... | collective-permute-start | bytes 37640 | tf_op jit(solution)/shard_map/ppermute | solution.py:41
  48.0 1.2 %collective-permute-done.15 = bf16[7,1,7,128]{3,2,1,0:T(8,128)(2,1)S(1)} collective-permute-done((bf16[7,1,7,128]{3,2,1,0:T(8,128)(2,1)S(1)}, bf16[7,1,7,128]{3,2,1,0:T(8,128)(2,1)S(1)}, u32[]{:S(2)}, u32[]{:S(2)}) %collective-permute-start.15) | collective-permute-done | bytes 12576 | tf_op jit(solution)/shard_map/ppermute | solution.py:41
  49.2 1.5 %collective-permute-done.16 = bf16[7,1,7,128]{3,2,1,0:T(8,128)(2,1)S(1)} collective-permute-done((bf16[7,1,7,128]{3,2,1,0:T(8,128)(2,1)S(1)}, bf16[7,1,7,128]{3,2,1,0:T(8,128)(2,1)S(1)}, u32[]{:S(2)}, u32[]{:S(2)}) %collective-permute-start.16) | collective-permute-done | bytes 12576 | tf_op jit(solution)/shard_map/ppermute | solution.py:41
  52.7 2.5 %collective-permute-start.20 = (bf16[212,128]{1,0:T(8,128)(2,1)S(1)}, bf16[212,128]{1,0:T(8,128)(2,1)S(1)}, u32[]{:S(2)}, u32[]{:S(2)}) collective-permute-start(bf16[212,128]{1,0:T(8,128)(2,1)S(1)} %pad_maximum_fusion.12), channel_id=1, source_target_pairs={{0,17},{1,16},{2,19},{3,18},{4,21},{5,20},{6,23},{7,22},{8,25},{9,... | collective-permute-start | bytes 162824 | tf_op jit(solution)/shard_map/ppermute | solution.py:59
  55.2 3.5 %collective-permute-done.20 = bf16[212,128]{1,0:T(8,128)(2,1)S(1)} collective-permute-done((bf16[212,128]{1,0:T(8,128)(2,1)S(1)}, bf16[212,128]{1,0:T(8,128)(2,1)S(1)}, u32[]{:S(2)}, u32[]{:S(2)}) %collective-permute-start.20) | collective-permute-done | bytes 54304 | tf_op jit(solution)/shard_map/ppermute | solution.py:59
  58.9 1.0 %collective-permute-start.21 = (bf16[176,128]{1,0:T(8,128)(2,1)S(1)}, bf16[176,128]{1,0:T(8,128)(2,1)S(1)}, u32[]{:S(2)}, u32[]{:S(2)}) collective-permute-start(bf16[176,128]{1,0:T(8,128)(2,1)S(1)} %add_convert_fusion.2), channel_id=1, source_target_pairs={{0,5},{1,4},{2,7},{3,6},{4,1},{5,0},{6,3},{7,2},{8,13},{9,12},{10,... | collective-permute-start | bytes 135176 | tf_op jit(solution)/shard_map/ppermute | solution.py:41
  60.1 2.5 %collective-permute-done.21 = bf16[176,128]{1,0:T(8,128)(2,1)S(1)} collective-permute-done((bf16[176,128]{1,0:T(8,128)(2,1)S(1)}, bf16[176,128]{1,0:T(8,128)(2,1)S(1)}, u32[]{:S(2)}, u32[]{:S(2)}) %collective-permute-start.21) | collective-permute-done | bytes 45088 | tf_op jit(solution)/shard_map/ppermute | solution.py:41
  63.0 4.2 %collective-permute-done.22 = bf16[176,128]{1,0:T(8,128)(2,1)S(1)} collective-permute-done((bf16[176,128]{1,0:T(8,128)(2,1)S(1)}, bf16[176,128]{1,0:T(8,128)(2,1)S(1)}, u32[]{:S(2)}, u32[]{:S(2)}) %collective-permute-start.22) | collective-permute-done | bytes 45088 | tf_op jit(solution)/shard_map/ppermute | solution.py:41
  67.3 1.0 %collective-permute-start.23 = (bf16[284,128]{1,0:T(8,128)(2,1)S(1)}, bf16[284,128]{1,0:T(8,128)(2,1)S(1)}, u32[]{:S(2)}, u32[]{:S(2)}) collective-permute-start(bf16[284,128]{1,0:T(8,128)(2,1)S(1)} %maximum_maximum_fusion.2), channel_id=1, source_target_pairs={{0,3},{1,2},{2,1},{3,0},{4,7},{5,6},{6,5},{7,4},{8,11},{9,10},{10,... | collective-permute-start | bytes 218120 | tf_op jit(solution)/shard_map/ppermute | solution.py:59
  68.3 3.3 %collective-permute-done.23 = bf16[284,128]{1,0:T(8,128)(2,1)S(1)} collective-permute-done((bf16[284,128]{1,0:T(8,128)(2,1)S(1)}, bf16[284,128]{1,0:T(8,128)(2,1)S(1)}, u32[]{:S(2)}, u32[]{:S(2)}) %collective-permute-start.23) | collective-permute-done | bytes 72736 | tf_op jit(solution)/shard_map/ppermute | solution.py:59
  72.1 1.2 %collective-permute-done.24 = bf16[460,128]{1,0:T(8,128)(2,1)S(1)} collective-permute-done((bf16[460,128]{1,0:T(8,128)(2,1)S(1)}, bf16[460,128]{1,0:T(8,128)(2,1)S(1)}, u32[]{:S(2)}, u32[]{:S(2)}) %collective-permute-start.24) | collective-permute-done | bytes 117792 | tf_op jit(solution)/shard_map/ppermute | solution.py:59
  74.0 0.7 pad_maximum_fusion.16
  74.7 1.0 %maximum_convert_fusion = f32[704,128]{1,0:T(8,128)} fusion(bf16[176,32]{1,0:T(8,128)(2,1)S(1)} %get-tuple-element.115, bf16[176,32]{1,0:T(8,128)(2,1)S(1)} %get-tuple-element.111, bf16[176,32]{1,0:T(8,128)(2,1)S(1)} %get-tuple-element.107, bf16[176,32]{1,0:T(8,128)(2,1)S(1)} %get-tuple-element.103, bf16[176,32]{1,0:T(8,128)(2,1)S(1)} %get-tuple-element.116, ...), kind=kLoop, calls=%fused_computation.51 | loop fusion | flops 2883584 | bytes 540672 | tf_op jit(solution)/shard_map/convert_element_type | solution.py:331
  (167 shorter events, 14.0 us)
Async XLA Ops:
  0.6 5.5 %copy-start = (bf16[1,343,343]{2,1,0:T(8,128)(2,1)S(1)}, bf16[1,343,343]{2,1,0:T(8,128)(2,1)}, u32[]{:S(2)}) copy-start(bf16[1,343,343]{2,1,0:T(8,128)(2,1)} %param.6) | copy-start | bytes 705898
  1.5 4.6 %copy-start.2 = (s32[1,343]{1,0:T(1,128)S(1)}, s32[1,343]{1,0:T(1,128)}, u32[]{:S(2)}) copy-start(s32[1,343]{1,0:T(1,128)} %param.7) | copy-start | bytes 4120
  1.5 4.6 %copy-start.3 = (f32[343]{0:T(512)S(1)}, f32[343]{0:T(512)}, u32[]{:S(2)}) copy-start(f32[343]{0:T(512)} %param.8) | copy-start | bytes 4120
  1.6 8.0 %collective-permute-start = (bf16[6,1,6,128]{3,2,1,0:T(8,128)(2,1)S(1)}, bf16[6,1,6,128]{3,2,1,0:T(8,128)(2,1)S(1)}, u32[]{:S(2)}, u32[]{:S(2)}) collective-permute-start(bf16[6,1,6,128]{3,2,1,0:T(8,128)(2,1)S(1)} %slice.535), channel_id=1, source_target_pairs={{0,4},{1,5},{2,6},{3,7},{4,0},{5,1},{6,2},{7,3},{8,12},{9,13},{10,... | collective-permute-start | bytes 27656 | tf_op jit(solution)/shard_map/ppermute | solution.py:41
  4.6 5.0 %collective-permute-start.1 = (bf16[6,1,6,128]{3,2,1,0:T(8,128)(2,1)S(1)}, bf16[6,1,6,128]{3,2,1,0:T(8,128)(2,1)S(1)}, u32[]{:S(2)}, u32[]{:S(2)}) collective-permute-start(bf16[6,1,6,128]{3,2,1,0:T(8,128)(2,1)S(1)} %slice.535), channel_id=1, source_target_pairs={{0,12},{1,13},{2,14},{3,15},{4,8},{5,9},{6,10},{7,11},{8,4},{9,5},... | collective-permute-start | bytes 27656 | tf_op jit(solution)/shard_map/ppermute | solution.py:41
  6.2 1.2 %copy-start.1 = (bf16[216,704]{1,0:T(8,128)(2,1)S(1)}, bf16[216,704]{1,0:T(8,128)(2,1)}, u32[]{:S(2)}) copy-start(bf16[216,704]{1,0:T(8,128)(2,1)} %param.9) | copy-start | bytes 912388
  6.9 14.0 %collective-permute-start.4 = (bf16[343,343]{1,0:T(8,128)(2,1)S(1)}, bf16[343,343]{1,0:T(8,128)(2,1)S(1)}, u32[]{:S(2)}, u32[]{:S(2)}) collective-permute-start(bf16[343,343]{1,0:T(8,128)(2,1)S(1)} %fusion), channel_id=1, source_target_pairs={{0,3},{1,2},{2,1},{3,0},{4,7},{5,6},{6,5},{7,4},{8,11},{9,10},{10,... | collective-permute-start | bytes 705902 | tf_op jit(solution)/shard_map/ppermute | solution.py:59
  7.4 15.2 %collective-permute-start.7 = (bf16[124,704]{1,0:T(8,128)(2,1)S(1)}, bf16[124,704]{1,0:T(8,128)(2,1)S(1)}, u32[]{:S(2)}, u32[]{:S(2)}) collective-permute-start(bf16[124,704]{1,0:T(8,128)(2,1)S(1)} %slice.443), channel_id=1, source_target_pairs={{0,3},{1,2},{2,1},{3,0},{4,7},{5,6},{6,5},{7,4},{8,11},{9,10},{10,... | collective-permute-start | bytes 523784 | tf_op jit(solution)/shard_map/ppermute | solution.py:59
  9.7 6.4 %collective-permute-start.2 = (bf16[258,128]{1,0:T(8,128)(2,1)S(1)}, bf16[258,128]{1,0:T(8,128)(2,1)S(1)}, u32[]{:S(2)}, u32[]{:S(2)}) collective-permute-start(bf16[258,128]{1,0:T(8,128)(2,1)S(1)} %pad_maximum_fusion.11), channel_id=1, source_target_pairs={{0,16},{1,17},{2,18},{3,19},{4,20},{5,21},{6,22},{7,23},{8,24},{9,... | collective-permute-start | bytes 198152 | tf_op jit(solution)/shard_map/ppermute | solution.py:41
  12.3 11.1 %collective-permute-start.8 = (bf16[343,343]{1,0:T(8,128)(2,1)S(1)}, bf16[343,343]{1,0:T(8,128)(2,1)S(1)}, u32[]{:S(2)}, u32[]{:S(2)}) collective-permute-start(bf16[343,343]{1,0:T(8,128)(2,1)S(1)} %fusion), channel_id=1, source_target_pairs={{0,1},{1,0},{2,3},{3,2},{4,5},{5,4},{6,7},{7,6},{8,9},{9,8},{10,11... | collective-permute-start | bytes 705902 | tf_op jit(solution)/shard_map/ppermute | solution.py:59
  16.5 4.1 %collective-permute-start.3 = (bf16[152,128]{1,0:T(8,128)(2,1)S(1)}, bf16[152,128]{1,0:T(8,128)(2,1)S(1)}, u32[]{:S(2)}, u32[]{:S(2)}) collective-permute-start(bf16[152,128]{1,0:T(8,128)(2,1)S(1)} %pad_maximum_fusion.17), channel_id=1, source_target_pairs={{0,3},{1,2},{2,1},{3,0},{4,7},{5,6},{6,5},{7,4},{8,11},{9,10},{10,... | collective-permute-start | bytes 116744 | tf_op jit(solution)/shard_map/ppermute | solution.py:59
  20.9 1.3 %collective-permute-start.5 = (bf16[152,128]{1,0:T(8,128)(2,1)S(1)}, bf16[152,128]{1,0:T(8,128)(2,1)S(1)}, u32[]{:S(2)}, u32[]{:S(2)}) collective-permute-start(bf16[152,128]{1,0:T(8,128)(2,1)S(1)} %pad_maximum_fusion.18), channel_id=1, source_target_pairs={{0,1},{1,0},{2,3},{3,2},{4,5},{5,4},{6,7},{7,6},{8,9},{9,8},{10,11... | collective-permute-start | bytes 116744 | tf_op jit(solution)/shard_map/ppermute | solution.py:59
  21.1 1.6 %collective-permute-start.6 = (bf16[343,343]{1,0:T(8,128)(2,1)S(1)}, bf16[343,343]{1,0:T(8,128)(2,1)S(1)}, u32[]{:S(2)}, u32[]{:S(2)}) collective-permute-start(bf16[343,343]{1,0:T(8,128)(2,1)S(1)} %collective-permute-done.4), channel_id=1, source_target_pairs={{0,1},{1,0},{2,3},{3,2},{4,5},{5,4},{6,7},{7,6},{8,9},{9,8},{10,11... | collective-permute-start | bytes 705902 | tf_op jit(solution)/shard_map/ppermute | solution.py:59
  24.3 4.1 %collective-permute-start.10 = (bf16[7,1,7,128]{3,2,1,0:T(8,128)(2,1)S(1)}, bf16[7,1,7,128]{3,2,1,0:T(8,128)(2,1)S(1)}, u32[]{:S(2)}, u32[]{:S(2)}) collective-permute-start(bf16[7,1,7,128]{3,2,1,0:T(8,128)(2,1)S(1)} %broadcast_select_fusion.45), channel_id=1, source_target_pairs={{0,13},{1,12},{2,15},{3,14},{4,9},{5,8},{6,11},{7,10},{8,5},{9,4},... | collective-permute-start | bytes 37640 | tf_op jit(solution)/shard_map/ppermute | solution.py:41
  25.7 3.2 %collective-permute-start.9 = (bf16[7,1,7,128]{3,2,1,0:T(8,128)(2,1)S(1)}, bf16[7,1,7,128]{3,2,1,0:T(8,128)(2,1)S(1)}, u32[]{:S(2)}, u32[]{:S(2)}) collective-permute-start(bf16[7,1,7,128]{3,2,1,0:T(8,128)(2,1)S(1)} %get-tuple-element.32), channel_id=1, source_target_pairs={{0,5},{1,4},{2,7},{3,6},{4,1},{5,0},{6,3},{7,2},{8,13},{9,12},{10,... | collective-permute-start | bytes 37640 | tf_op jit(solution)/shard_map/ppermute | solution.py:41
  29.0 4.1 %collective-permute-start.11 = (bf16[1,7,7,128]{3,2,1,0:T(8,128)(2,1)S(1)}, bf16[1,7,7,128]{3,2,1,0:T(8,128)(2,1)S(1)}, u32[]{:S(2)}, u32[]{:S(2)}) collective-permute-start(bf16[1,7,7,128]{3,2,1,0:T(8,128)(2,1)S(1)} %fusion.83), channel_id=1, source_target_pairs={{0,17},{1,16},{2,19},{3,18},{4,21},{5,20},{6,23},{7,22},{8,25},{9,... | collective-permute-start | bytes 37640 | tf_op jit(solution)/shard_map/ppermute | solution.py:41
  31.6 20.0 %collective-permute-start.17 = (bf16[252,704]{1,0:T(8,128)(2,1)S(1)}, bf16[252,704]{1,0:T(8,128)(2,1)S(1)}, u32[]{:S(2)}, u32[]{:S(2)}) collective-permute-start(bf16[252,704]{1,0:T(8,128)(2,1)S(1)} %pad_maximum_fusion), channel_id=1, source_target_pairs={{0,1},{1,0},{2,3},{3,2},{4,5},{5,4},{6,7},{7,6},{8,9},{9,8},{10,11... | collective-permute-start | bytes 1064456 | tf_op jit(solution)/shard_map/ppermute | solution.py:59
  34.6 2.9 %slice-start = ((bf16[216,704]{1,0:T(8,128)(2,1)}), bf16[92,704]{1,0:T(8,128)(2,1)S(1)}, s32[]{:S(2)}) async-start(bf16[216,704]{1,0:T(8,128)(2,1)} %param.9), calls=%async_computation | async-start | bytes 294912 | tf_op jit(solution)/shard_map/slice | solution.py:210
  34.6 4.1 %collective-permute-start.13 = (bf16[7,1,7,128]{3,2,1,0:T(8,128)(2,1)S(1)}, bf16[7,1,7,128]{3,2,1,0:T(8,128)(2,1)S(1)}, u32[]{:S(2)}, u32[]{:S(2)}) collective-permute-start(bf16[7,1,7,128]{3,2,1,0:T(8,128)(2,1)S(1)} %broadcast_select_fusion.44), channel_id=1, source_target_pairs={{0,13},{1,12},{2,15},{3,14},{4,9},{5,8},{6,11},{7,10},{8,5},{9,4},... | collective-permute-start | bytes 37640 | tf_op jit(solution)/shard_map/ppermute | solution.py:41
  36.1 3.3 %collective-permute-start.12 = (bf16[7,1,7,128]{3,2,1,0:T(8,128)(2,1)S(1)}, bf16[7,1,7,128]{3,2,1,0:T(8,128)(2,1)S(1)}, u32[]{:S(2)}, u32[]{:S(2)}) collective-permute-start(bf16[7,1,7,128]{3,2,1,0:T(8,128)(2,1)S(1)} %get-tuple-element.29), channel_id=1, source_target_pairs={{0,5},{1,4},{2,7},{3,6},{4,1},{5,0},{6,3},{7,2},{8,13},{9,12},{10,... | collective-permute-start | bytes 37640 | tf_op jit(solution)/shard_map/ppermute | solution.py:41
  37.5 6.9 %collective-permute-start.18 = (bf16[128,704]{1,0:T(8,128)(2,1)S(1)}, bf16[128,704]{1,0:T(8,128)(2,1)S(1)}, u32[]{:S(2)}, u32[]{:S(2)}) collective-permute-start(bf16[128,704]{1,0:T(8,128)(2,1)S(1)} %pad_maximum_fusion.2), channel_id=1, source_target_pairs={{0,3},{1,2},{2,1},{3,0},{4,7},{5,6},{6,5},{7,4},{8,11},{9,10},{10,... | collective-permute-start | bytes 540680 | tf_op jit(solution)/shard_map/ppermute | solution.py:59
  39.4 5.0 %collective-permute-start.14 = (bf16[1,7,7,128]{3,2,1,0:T(8,128)(2,1)S(1)}, bf16[1,7,7,128]{3,2,1,0:T(8,128)(2,1)S(1)}, u32[]{:S(2)}, u32[]{:S(2)}) collective-permute-start(bf16[1,7,7,128]{3,2,1,0:T(8,128)(2,1)S(1)} %fusion.84), channel_id=1, source_target_pairs={{0,17},{1,16},{2,19},{3,18},{4,21},{5,20},{6,23},{7,22},{8,25},{9,... | collective-permute-start | bytes 37640 | tf_op jit(solution)/shard_map/ppermute | solution.py:41
  46.0 3.2 %collective-permute-start.15 = (bf16[7,1,7,128]{3,2,1,0:T(8,128)(2,1)S(1)}, bf16[7,1,7,128]{3,2,1,0:T(8,128)(2,1)S(1)}, u32[]{:S(2)}, u32[]{:S(2)}) collective-permute-start(bf16[7,1,7,128]{3,2,1,0:T(8,128)(2,1)S(1)} %slice.746), channel_id=1, source_target_pairs={{0,5},{1,4},{2,7},{3,6},{4,1},{5,0},{6,3},{7,2},{8,13},{9,12},{10,... | collective-permute-start | bytes 37640 | tf_op jit(solution)/shard_map/ppermute | solution.py:41
  46.7 4.0 %collective-permute-start.16 = (bf16[7,1,7,128]{3,2,1,0:T(8,128)(2,1)S(1)}, bf16[7,1,7,128]{3,2,1,0:T(8,128)(2,1)S(1)}, u32[]{:S(2)}, u32[]{:S(2)}) collective-permute-start(bf16[7,1,7,128]{3,2,1,0:T(8,128)(2,1)S(1)} %slice.746), channel_id=1, source_target_pairs={{0,13},{1,12},{2,15},{3,14},{4,9},{5,8},{6,11},{7,10},{8,5},{9,4},... | collective-permute-start | bytes 37640 | tf_op jit(solution)/shard_map/ppermute | solution.py:41
  47.7 4.2 %collective-permute-start.19 = (bf16[252,704]{1,0:T(8,128)(2,1)S(1)}, bf16[252,704]{1,0:T(8,128)(2,1)S(1)}, u32[]{:S(2)}, u32[]{:S(2)}) collective-permute-start(bf16[252,704]{1,0:T(8,128)(2,1)S(1)} %constant_dynamic-update-slice_fusion.6), channel_id=1, source_target_pairs={{0,1},{1,0},{2,3},{3,2},{4,5},{5,4},{6,7},{7,6},{8,9},{9,8},{10,11... | collective-permute-start | bytes 1064456 | tf_op jit(solution)/shard_map/ppermute | solution.py:59
  52.7 6.0 %collective-permute-start.20 = (bf16[212,128]{1,0:T(8,128)(2,1)S(1)}, bf16[212,128]{1,0:T(8,128)(2,1)S(1)}, u32[]{:S(2)}, u32[]{:S(2)}) collective-permute-start(bf16[212,128]{1,0:T(8,128)(2,1)S(1)} %pad_maximum_fusion.12), channel_id=1, source_target_pairs={{0,17},{1,16},{2,19},{3,18},{4,21},{5,20},{6,23},{7,22},{8,25},{9,... | collective-permute-start | bytes 162824 | tf_op jit(solution)/shard_map/ppermute | solution.py:59
  58.9 3.7 %collective-permute-start.21 = (bf16[176,128]{1,0:T(8,128)(2,1)S(1)}, bf16[176,128]{1,0:T(8,128)(2,1)S(1)}, u32[]{:S(2)}, u32[]{:S(2)}) collective-permute-start(bf16[176,128]{1,0:T(8,128)(2,1)S(1)} %add_convert_fusion.2), channel_id=1, source_target_pairs={{0,5},{1,4},{2,7},{3,6},{4,1},{5,0},{6,3},{7,2},{8,13},{9,12},{10,... | collective-permute-start | bytes 135176 | tf_op jit(solution)/shard_map/ppermute | solution.py:41
  62.6 4.6 %collective-permute-start.22 = (bf16[176,128]{1,0:T(8,128)(2,1)S(1)}, bf16[176,128]{1,0:T(8,128)(2,1)S(1)}, u32[]{:S(2)}, u32[]{:S(2)}) collective-permute-start(bf16[176,128]{1,0:T(8,128)(2,1)S(1)} %add_convert_fusion.1), channel_id=1, source_target_pairs={{0,13},{1,12},{2,15},{3,14},{4,9},{5,8},{6,11},{7,10},{8,5},{9,4},... | collective-permute-start | bytes 135176 | tf_op jit(solution)/shard_map/ppermute | solution.py:41
  67.3 4.3 %collective-permute-start.23 = (bf16[284,128]{1,0:T(8,128)(2,1)S(1)}, bf16[284,128]{1,0:T(8,128)(2,1)S(1)}, u32[]{:S(2)}, u32[]{:S(2)}) collective-permute-start(bf16[284,128]{1,0:T(8,128)(2,1)S(1)} %maximum_maximum_fusion.2), channel_id=1, source_target_pairs={{0,3},{1,2},{2,1},{3,0},{4,7},{5,6},{6,5},{7,4},{8,11},{9,10},{10,... | collective-permute-start | bytes 218120 | tf_op jit(solution)/shard_map/ppermute | solution.py:59
  71.9 1.4 %collective-permute-start.24 = (bf16[460,128]{1,0:T(8,128)(2,1)S(1)}, bf16[460,128]{1,0:T(8,128)(2,1)S(1)}, u32[]{:S(2)}, u32[]{:S(2)}) collective-permute-start(bf16[460,128]{1,0:T(8,128)(2,1)S(1)} %maximum_maximum_fusion), channel_id=1, source_target_pairs={{0,1},{1,0},{2,3},{3,2},{4,5},{5,4},{6,7},{7,6},{8,9},{9,8},{10,11... | collective-permute-start | bytes 353288 | tf_op jit(solution)/shard_map/ppermute | solution.py:59

commit v19 on v18

--- a/solution.py
+++ b/solution.py
@@ -312,14 +312,12 @@
     near = placed(split(filtered, GRID_Z), high, grid.has(1))
     sent = jnp.concatenate([share, packed([near[3], near[2]])], axis=0)
     arrived = grid.partner(sent, FIRST)
-    held = jnp.stack([share, arrived[:deep]])
+    held = [share, arrived[:deep]]
     came = unpacked(arrived[deep:], width)
     own = [near[0], came[0]]
     away = [near[1], came[1]]
-    sent = jnp.concatenate([held.reshape(-1, columns), packed(away)], axis=0)
-    arrived = grid.partner(sent, SECOND)
-    others = arrived[: 2 * deep].reshape(held.shape)
-    came = unpacked(arrived[2 * deep :], width)
+    came = unpacked(grid.partner(packed(away), SECOND), width)
+    others = [grid.partner(h, SECOND) for h in held]
     filtered = jnp.concatenate(placed([own[0], came[0], own[1], came[1]], high, low), axis=1)
     held = placed([held[0], others[0], held[1], others[1]], high, low)
     intersection = jnp.concatenate(

time: 75.9 us -> 75.7 us (level)
    ppermute x12 -> x14, waiting for transfers between devices: 15.2 us -> 14.5 us  [partner(): lax.ppermute(value, AXIS, [(i, i ^ bits) for i in range(self.devices)])]
    ppermute x12 -> x14, starting transfers between devices: 7.68 us -> 8.19 us  [partner(): lax.ppermute(value, AXIS, [(i, i ^ bits) for i in range(self.devices)])]
  transfers between devices with their start and end apart: 25 -> 27, of which waited for: 16 -> 16; matrix products, arithmetic and copies ran while one was open for 10% -> 12% of each run, Pallas kernels for 0% -> 0%
where the time goes in v19:
time: 75.7 us; the launch traced here: 75.6 us
  waiting for transfers between devices  32.5 us (43%)
  starting transfers between devices  28.1 us (37%)
  other arithmetic  5.03 us (7%)
  matrix products  4.87 us (6%)
  local copies, waits for them, and re-layouts  3.34 us (4%)
  between operations  1.72 us (2%)
    ppermute x13, starting transfers between devices, swapped(): arrived = lax.ppermute(jnp.where(lower, high, low), AXIS, pairs)  19.9 us
    ppermute x13, waiting for transfers between devices, swapped(): arrived = lax.ppermute(jnp.where(lower, high, low), AXIS, pairs)  18 us
    ppermute x14, waiting for transfers between devices, partner(): lax.ppermute(value, AXIS, [(i, i ^ bits) for i in range(self.devices)])  14.5 us
    ppermute x14, starting transfers between devices, partner(): lax.ppermute(value, AXIS, [(i, i ^ bits) for i in range(self.devices)])  8.19 us
    dot_general x12, matrix products, per_device(): jnp.dot(matrices[r], own, preferred_element_type=jnp.float32)  2.93 us
  transfers between devices with their start and end apart: 27, of which 16 were waited for; matrix products, arithmetic and copies ran while one was open for 12% of the time, Pallas kernels for 0%

profile of v19, /device:TPU:0, one launch (start us, length us, event | category | flops | bytes accessed | tf_op | source)
XLA Modules:
  0.0 75.6 jit_solution(12232709657447887171)
XLA Ops:
  0.6 0.9 %reshape.116 = bf16[6,6,6,128]{3,2,1,0:T(8,128)(2,1)S(1)} reshape(bf16[216,128]{1,0:T(8,128)(2,1)} %param.5) | data formatting | bytes 110592 | tf_op jit(solution)/shard_map/reshape | solution.py:193
  1.6 3.0 %collective-permute-start = (bf16[6,1,6,128]{3,2,1,0:T(8,128)(2,1)S(1)}, bf16[6,1,6,128]{3,2,1,0:T(8,128)(2,1)S(1)}, u32[]{:S(2)}, u32[]{:S(2)}) collective-permute-start(bf16[6,1,6,128]{3,2,1,0:T(8,128)(2,1)S(1)} %slice.517), channel_id=1, source_target_pairs={{0,4},{1,5},{2,6},{3,7},{4,0},{5,1},{6,2},{7,3},{8,12},{9,13},{10,... | collective-permute-start | bytes 27656 | tf_op jit(solution)/shard_map/ppermute | solution.py:41
  4.6 1.5 %collective-permute-start.1 = (bf16[6,1,6,128]{3,2,1,0:T(8,128)(2,1)S(1)}, bf16[6,1,6,128]{3,2,1,0:T(8,128)(2,1)S(1)}, u32[]{:S(2)}, u32[]{:S(2)}) collective-permute-start(bf16[6,1,6,128]{3,2,1,0:T(8,128)(2,1)S(1)} %slice.517), channel_id=1, source_target_pairs={{0,12},{1,13},{2,14},{3,15},{4,8},{5,9},{6,10},{7,11},{8,4},{9,5},... | collective-permute-start | bytes 27656 | tf_op jit(solution)/shard_map/ppermute | solution.py:41
  6.2 0.7 fusion
  7.4 1.4 %collective-permute-start.7 = (bf16[124,704]{1,0:T(8,128)(2,1)S(1)}, bf16[124,704]{1,0:T(8,128)(2,1)S(1)}, u32[]{:S(2)}, u32[]{:S(2)}) collective-permute-start(bf16[124,704]{1,0:T(8,128)(2,1)S(1)} %slice.426), channel_id=1, source_target_pairs={{0,3},{1,2},{2,1},{3,0},{4,7},{5,6},{6,5},{7,4},{8,11},{9,10},{10,... | collective-permute-start | bytes 523784 | tf_op jit(solution)/shard_map/ppermute | solution.py:59
  9.7 2.7 %collective-permute-start.2 = (bf16[258,128]{1,0:T(8,128)(2,1)S(1)}, bf16[258,128]{1,0:T(8,128)(2,1)S(1)}, u32[]{:S(2)}, u32[]{:S(2)}) collective-permute-start(bf16[258,128]{1,0:T(8,128)(2,1)S(1)} %pad_maximum_fusion.10), channel_id=1, source_target_pairs={{0,16},{1,17},{2,18},{3,19},{4,20},{5,21},{6,22},{7,23},{8,24},{9,... | collective-permute-start | bytes 198152 | tf_op jit(solution)/shard_map/ppermute | solution.py:41
  12.3 3.7 %collective-permute-done.2 = bf16[258,128]{1,0:T(8,128)(2,1)S(1)} collective-permute-done((bf16[258,128]{1,0:T(8,128)(2,1)S(1)}, bf16[258,128]{1,0:T(8,128)(2,1)S(1)}, u32[]{:S(2)}, u32[]{:S(2)}) %collective-permute-start.2) | collective-permute-done | bytes 66080 | tf_op jit(solution)/shard_map/ppermute | solution.py:41
  16.6 4.0 %collective-permute-done.3 = bf16[152,128]{1,0:T(8,128)(2,1)S(1)} collective-permute-done((bf16[152,128]{1,0:T(8,128)(2,1)S(1)}, bf16[152,128]{1,0:T(8,128)(2,1)S(1)}, u32[]{:S(2)}, u32[]{:S(2)}) %collective-permute-start.3) | collective-permute-done | bytes 38944 | tf_op jit(solution)/shard_map/ppermute | solution.py:59
  21.5 0.7 collective-permute-done.5
  24.3 1.4 %collective-permute-start.10 = (bf16[7,1,7,128]{3,2,1,0:T(8,128)(2,1)S(1)}, bf16[7,1,7,128]{3,2,1,0:T(8,128)(2,1)S(1)}, u32[]{:S(2)}, u32[]{:S(2)}) collective-permute-start(bf16[7,1,7,128]{3,2,1,0:T(8,128)(2,1)S(1)} %broadcast_select_fusion.45), channel_id=1, source_target_pairs={{0,13},{1,12},{2,15},{3,14},{4,9},{5,8},{6,11},{7,10},{8,5},{9,4},... | collective-permute-start | bytes 37640 | tf_op jit(solution)/shard_map/ppermute | solution.py:41
  25.9 2.5 %collective-permute-done.10 = bf16[7,1,7,128]{3,2,1,0:T(8,128)(2,1)S(1)} collective-permute-done((bf16[7,1,7,128]{3,2,1,0:T(8,128)(2,1)S(1)}, bf16[7,1,7,128]{3,2,1,0:T(8,128)(2,1)S(1)}, u32[]{:S(2)}, u32[]{:S(2)}) %collective-permute-start.10) | collective-permute-done | bytes 12576 | tf_op jit(solution)/shard_map/ppermute | solution.py:41
  29.0 2.6 %collective-permute-start.11 = (bf16[1,7,7,128]{3,2,1,0:T(8,128)(2,1)S(1)}, bf16[1,7,7,128]{3,2,1,0:T(8,128)(2,1)S(1)}, u32[]{:S(2)}, u32[]{:S(2)}) collective-permute-start(bf16[1,7,7,128]{3,2,1,0:T(8,128)(2,1)S(1)} %fusion.83), channel_id=1, source_target_pairs={{0,17},{1,16},{2,19},{3,18},{4,21},{5,20},{6,23},{7,22},{8,25},{9,... | collective-permute-start | bytes 37640 | tf_op jit(solution)/shard_map/ppermute | solution.py:41
  32.1 1.0 %collective-permute-done.11 = bf16[1,7,7,128]{3,2,1,0:T(8,128)(2,1)S(1)} collective-permute-done((bf16[1,7,7,128]{3,2,1,0:T(8,128)(2,1)S(1)}, bf16[1,7,7,128]{3,2,1,0:T(8,128)(2,1)S(1)}, u32[]{:S(2)}, u32[]{:S(2)}) %collective-permute-start.11) | collective-permute-done | bytes 12576 | tf_op jit(solution)/shard_map/ppermute | solution.py:41
  34.6 1.4 %collective-permute-start.13 = (bf16[7,1,7,128]{3,2,1,0:T(8,128)(2,1)S(1)}, bf16[7,1,7,128]{3,2,1,0:T(8,128)(2,1)S(1)}, u32[]{:S(2)}, u32[]{:S(2)}) collective-permute-start(bf16[7,1,7,128]{3,2,1,0:T(8,128)(2,1)S(1)} %broadcast_select_fusion.44), channel_id=1, source_target_pairs={{0,13},{1,12},{2,15},{3,14},{4,9},{5,8},{6,11},{7,10},{8,5},{9,4},... | collective-permute-start | bytes 37640 | tf_op jit(solution)/shard_map/ppermute | solution.py:41
  36.1 1.4 %collective-permute-start.12 = (bf16[7,1,7,128]{3,2,1,0:T(8,128)(2,1)S(1)}, bf16[7,1,7,128]{3,2,1,0:T(8,128)(2,1)S(1)}, u32[]{:S(2)}, u32[]{:S(2)}) collective-permute-start(bf16[7,1,7,128]{3,2,1,0:T(8,128)(2,1)S(1)} %get-tuple-element.29), channel_id=1, source_target_pairs={{0,5},{1,4},{2,7},{3,6},{4,1},{5,0},{6,3},{7,2},{8,13},{9,12},{10,... | collective-permute-start | bytes 37640 | tf_op jit(solution)/shard_map/ppermute | solution.py:41
  37.5 0.8 %collective-permute-start.18 = (bf16[128,704]{1,0:T(8,128)(2,1)S(1)}, bf16[128,704]{1,0:T(8,128)(2,1)S(1)}, u32[]{:S(2)}, u32[]{:S(2)}) collective-permute-start(bf16[128,704]{1,0:T(8,128)(2,1)S(1)} %pad_maximum_fusion.2), channel_id=1, source_target_pairs={{0,3},{1,2},{2,1},{3,0},{4,7},{5,6},{6,5},{7,4},{8,11},{9,10},{10,... | collective-permute-start | bytes 540680 | tf_op jit(solution)/shard_map/ppermute | solution.py:59
  38.8 0.6 collective-permute-done.12
  39.4 2.5 %collective-permute-start.14 = (bf16[1,7,7,128]{3,2,1,0:T(8,128)(2,1)S(1)}, bf16[1,7,7,128]{3,2,1,0:T(8,128)(2,1)S(1)}, u32[]{:S(2)}, u32[]{:S(2)}) collective-permute-start(bf16[1,7,7,128]{3,2,1,0:T(8,128)(2,1)S(1)} %fusion.84), channel_id=1, source_target_pairs={{0,17},{1,16},{2,19},{3,18},{4,21},{5,20},{6,23},{7,22},{8,25},{9,... | collective-permute-start | bytes 37640 | tf_op jit(solution)/shard_map/ppermute | solution.py:41
  42.0 2.4 %collective-permute-done.18 = bf16[128,704]{1,0:T(8,128)(2,1)S(1)} collective-permute-done((bf16[128,704]{1,0:T(8,128)(2,1)S(1)}, bf16[128,704]{1,0:T(8,128)(2,1)S(1)}, u32[]{:S(2)}, u32[]{:S(2)}) %collective-permute-start.18) | collective-permute-done | bytes 180256 | tf_op jit(solution)/shard_map/ppermute | solution.py:59
  46.0 0.6 collective-permute-start.15
  46.7 1.0 %collective-permute-start.16 = (bf16[7,1,7,128]{3,2,1,0:T(8,128)(2,1)S(1)}, bf16[7,1,7,128]{3,2,1,0:T(8,128)(2,1)S(1)}, u32[]{:S(2)}, u32[]{:S(2)}) collective-permute-start(bf16[7,1,7,128]{3,2,1,0:T(8,128)(2,1)S(1)} %slice.699), channel_id=1, source_target_pairs={{0,13},{1,12},{2,15},{3,14},{4,9},{5,8},{6,11},{7,10},{8,5},{9,4},... | collective-permute-start | bytes 37640 | tf_op jit(solution)/shard_map/ppermute | solution.py:41
  48.0 1.2 %collective-permute-done.15 = bf16[7,1,7,128]{3,2,1,0:T(8,128)(2,1)S(1)} collective-permute-done((bf16[7,1,7,128]{3,2,1,0:T(8,128)(2,1)S(1)}, bf16[7,1,7,128]{3,2,1,0:T(8,128)(2,1)S(1)}, u32[]{:S(2)}, u32[]{:S(2)}) %collective-permute-start.15) | collective-permute-done | bytes 12576 | tf_op jit(solution)/shard_map/ppermute | solution.py:41
  49.2 1.5 %collective-permute-done.16 = bf16[7,1,7,128]{3,2,1,0:T(8,128)(2,1)S(1)} collective-permute-done((bf16[7,1,7,128]{3,2,1,0:T(8,128)(2,1)S(1)}, bf16[7,1,7,128]{3,2,1,0:T(8,128)(2,1)S(1)}, u32[]{:S(2)}, u32[]{:S(2)}) %collective-permute-start.16) | collective-permute-done | bytes 12576 | tf_op jit(solution)/shard_map/ppermute | solution.py:41
  52.7 2.5 %collective-permute-start.20 = (bf16[212,128]{1,0:T(8,128)(2,1)S(1)}, bf16[212,128]{1,0:T(8,128)(2,1)S(1)}, u32[]{:S(2)}, u32[]{:S(2)}) collective-permute-start(bf16[212,128]{1,0:T(8,128)(2,1)S(1)} %pad_maximum_fusion.11), channel_id=1, source_target_pairs={{0,17},{1,16},{2,19},{3,18},{4,21},{5,20},{6,23},{7,22},{8,25},{9,... | collective-permute-start | bytes 162824 | tf_op jit(solution)/shard_map/ppermute | solution.py:59
  55.2 3.5 %collective-permute-done.20 = bf16[212,128]{1,0:T(8,128)(2,1)S(1)} collective-permute-done((bf16[212,128]{1,0:T(8,128)(2,1)S(1)}, bf16[212,128]{1,0:T(8,128)(2,1)S(1)}, u32[]{:S(2)}, u32[]{:S(2)}) %collective-permute-start.20) | collective-permute-done | bytes 54304 | tf_op jit(solution)/shard_map/ppermute | solution.py:59
  58.9 1.0 %collective-permute-start.21 = (bf16[176,128]{1,0:T(8,128)(2,1)S(1)}, bf16[176,128]{1,0:T(8,128)(2,1)S(1)}, u32[]{:S(2)}, u32[]{:S(2)}) collective-permute-start(bf16[176,128]{1,0:T(8,128)(2,1)S(1)} %add_convert_fusion.2), channel_id=1, source_target_pairs={{0,5},{1,4},{2,7},{3,6},{4,1},{5,0},{6,3},{7,2},{8,13},{9,12},{10,... | collective-permute-start | bytes 135176 | tf_op jit(solution)/shard_map/ppermute | solution.py:41
  60.1 2.5 %collective-permute-done.21 = bf16[176,128]{1,0:T(8,128)(2,1)S(1)} collective-permute-done((bf16[176,128]{1,0:T(8,128)(2,1)S(1)}, bf16[176,128]{1,0:T(8,128)(2,1)S(1)}, u32[]{:S(2)}, u32[]{:S(2)}) %collective-permute-start.21) | collective-permute-done | bytes 45088 | tf_op jit(solution)/shard_map/ppermute | solution.py:41
  63.0 4.2 %collective-permute-done.22 = bf16[176,128]{1,0:T(8,128)(2,1)S(1)} collective-permute-done((bf16[176,128]{1,0:T(8,128)(2,1)S(1)}, bf16[176,128]{1,0:T(8,128)(2,1)S(1)}, u32[]{:S(2)}, u32[]{:S(2)}) %collective-permute-start.22) | collective-permute-done | bytes 45088 | tf_op jit(solution)/shard_map/ppermute | solution.py:41
  67.3 1.0 %collective-permute-start.23 = (bf16[284,128]{1,0:T(8,128)(2,1)S(1)}, bf16[284,128]{1,0:T(8,128)(2,1)S(1)}, u32[]{:S(2)}, u32[]{:S(2)}) collective-permute-start(bf16[284,128]{1,0:T(8,128)(2,1)S(1)} %maximum_maximum_fusion.1), channel_id=1, source_target_pairs={{0,3},{1,2},{2,1},{3,0},{4,7},{5,6},{6,5},{7,4},{8,11},{9,10},{10,... | collective-permute-start | bytes 218120 | tf_op jit(solution)/shard_map/ppermute | solution.py:59
  68.3 3.3 %collective-permute-done.23 = bf16[284,128]{1,0:T(8,128)(2,1)S(1)} collective-permute-done((bf16[284,128]{1,0:T(8,128)(2,1)S(1)}, bf16[284,128]{1,0:T(8,128)(2,1)S(1)}, u32[]{:S(2)}, u32[]{:S(2)}) %collective-permute-start.23) | collective-permute-done | bytes 72736 | tf_op jit(solution)/shard_map/ppermute | solution.py:59
  73.4 0.7 pad_maximum_fusion.15
  74.6 1.0 %maximum_convert_fusion = f32[704,128]{1,0:T(8,128)} fusion(bf16[176,32]{1,0:T(8,128)(2,1)S(1)} %get-tuple-element.114, bf16[176,32]{1,0:T(8,128)(2,1)S(1)} %get-tuple-element.110, bf16[176,32]{1,0:T(8,128)(2,1)S(1)} %get-tuple-element.106, bf16[176,32]{1,0:T(8,128)(2,1)S(1)} %get-tuple-element.102, bf16[176,32]{1,0:T(8,128)(2,1)S(1)} %get-tuple-element.115, ...), kind=kLoop, calls=%fused_computation.51 | loop fusion | flops 2883584 | bytes 540672 | tf_op jit(solution)/shard_map/convert_element_type | solution.py:329
  (170 shorter events, 14.5 us)
Async XLA Ops:
  0.6 5.5 %copy-start = (bf16[1,343,343]{2,1,0:T(8,128)(2,1)S(1)}, bf16[1,343,343]{2,1,0:T(8,128)(2,1)}, u32[]{:S(2)}) copy-start(bf16[1,343,343]{2,1,0:T(8,128)(2,1)} %param.6) | copy-start | bytes 705898
  1.5 4.6 %copy-start.2 = (s32[1,343]{1,0:T(1,128)S(1)}, s32[1,343]{1,0:T(1,128)}, u32[]{:S(2)}) copy-start(s32[1,343]{1,0:T(1,128)} %param.7) | copy-start | bytes 4120
  1.5 4.6 %copy-start.3 = (f32[343]{0:T(512)S(1)}, f32[343]{0:T(512)}, u32[]{:S(2)}) copy-start(f32[343]{0:T(512)} %param.8) | copy-start | bytes 4120
  1.6 8.0 %collective-permute-start = (bf16[6,1,6,128]{3,2,1,0:T(8,128)(2,1)S(1)}, bf16[6,1,6,128]{3,2,1,0:T(8,128)(2,1)S(1)}, u32[]{:S(2)}, u32[]{:S(2)}) collective-permute-start(bf16[6,1,6,128]{3,2,1,0:T(8,128)(2,1)S(1)} %slice.517), channel_id=1, source_target_pairs={{0,4},{1,5},{2,6},{3,7},{4,0},{5,1},{6,2},{7,3},{8,12},{9,13},{10,... | collective-permute-start | bytes 27656 | tf_op jit(solution)/shard_map/ppermute | solution.py:41
  4.6 5.0 %collective-permute-start.1 = (bf16[6,1,6,128]{3,2,1,0:T(8,128)(2,1)S(1)}, bf16[6,1,6,128]{3,2,1,0:T(8,128)(2,1)S(1)}, u32[]{:S(2)}, u32[]{:S(2)}) collective-permute-start(bf16[6,1,6,128]{3,2,1,0:T(8,128)(2,1)S(1)} %slice.517), channel_id=1, source_target_pairs={{0,12},{1,13},{2,14},{3,15},{4,8},{5,9},{6,10},{7,11},{8,4},{9,5},... | collective-permute-start | bytes 27656 | tf_op jit(solution)/shard_map/ppermute | solution.py:41
  6.2 1.2 %copy-start.1 = (bf16[216,704]{1,0:T(8,128)(2,1)S(1)}, bf16[216,704]{1,0:T(8,128)(2,1)}, u32[]{:S(2)}) copy-start(bf16[216,704]{1,0:T(8,128)(2,1)} %param.9) | copy-start | bytes 912388
  6.9 14.0 %collective-permute-start.4 = (bf16[343,343]{1,0:T(8,128)(2,1)S(1)}, bf16[343,343]{1,0:T(8,128)(2,1)S(1)}, u32[]{:S(2)}, u32[]{:S(2)}) collective-permute-start(bf16[343,343]{1,0:T(8,128)(2,1)S(1)} %fusion), channel_id=1, source_target_pairs={{0,3},{1,2},{2,1},{3,0},{4,7},{5,6},{6,5},{7,4},{8,11},{9,10},{10,... | collective-permute-start | bytes 705902 | tf_op jit(solution)/shard_map/ppermute | solution.py:59
  7.4 15.2 %collective-permute-start.7 = (bf16[124,704]{1,0:T(8,128)(2,1)S(1)}, bf16[124,704]{1,0:T(8,128)(2,1)S(1)}, u32[]{:S(2)}, u32[]{:S(2)}) collective-permute-start(bf16[124,704]{1,0:T(8,128)(2,1)S(1)} %slice.426), channel_id=1, source_target_pairs={{0,3},{1,2},{2,1},{3,0},{4,7},{5,6},{6,5},{7,4},{8,11},{9,10},{10,... | collective-permute-start | bytes 523784 | tf_op jit(solution)/shard_map/ppermute | solution.py:59
  9.7 6.4 %collective-permute-start.2 = (bf16[258,128]{1,0:T(8,128)(2,1)S(1)}, bf16[258,128]{1,0:T(8,128)(2,1)S(1)}, u32[]{:S(2)}, u32[]{:S(2)}) collective-permute-start(bf16[258,128]{1,0:T(8,128)(2,1)S(1)} %pad_maximum_fusion.10), channel_id=1, source_target_pairs={{0,16},{1,17},{2,18},{3,19},{4,20},{5,21},{6,22},{7,23},{8,24},{9,... | collective-permute-start | bytes 198152 | tf_op jit(solution)/shard_map/ppermute | solution.py:41
  12.3 11.1 %collective-permute-start.8 = (bf16[343,343]{1,0:T(8,128)(2,1)S(1)}, bf16[343,343]{1,0:T(8,128)(2,1)S(1)}, u32[]{:S(2)}, u32[]{:S(2)}) collective-permute-start(bf16[343,343]{1,0:T(8,128)(2,1)S(1)} %fusion), channel_id=1, source_target_pairs={{0,1},{1,0},{2,3},{3,2},{4,5},{5,4},{6,7},{7,6},{8,9},{9,8},{10,11... | collective-permute-start | bytes 705902 | tf_op jit(solution)/shard_map/ppermute | solution.py:59
  16.5 4.1 %collective-permute-start.3 = (bf16[152,128]{1,0:T(8,128)(2,1)S(1)}, bf16[152,128]{1,0:T(8,128)(2,1)S(1)}, u32[]{:S(2)}, u32[]{:S(2)}) collective-permute-start(bf16[152,128]{1,0:T(8,128)(2,1)S(1)} %pad_maximum_fusion.16), channel_id=1, source_target_pairs={{0,3},{1,2},{2,1},{3,0},{4,7},{5,6},{6,5},{7,4},{8,11},{9,10},{10,... | collective-permute-start | bytes 116744 | tf_op jit(solution)/shard_map/ppermute | solution.py:59
  20.9 1.3 %collective-permute-start.5 = (bf16[152,128]{1,0:T(8,128)(2,1)S(1)}, bf16[152,128]{1,0:T(8,128)(2,1)S(1)}, u32[]{:S(2)}, u32[]{:S(2)}) collective-permute-start(bf16[152,128]{1,0:T(8,128)(2,1)S(1)} %pad_maximum_fusion.17), channel_id=1, source_target_pairs={{0,1},{1,0},{2,3},{3,2},{4,5},{5,4},{6,7},{7,6},{8,9},{9,8},{10,11... | collective-permute-start | bytes 116744 | tf_op jit(solution)/shard_map/ppermute | solution.py:59
  21.1 1.6 %collective-permute-start.6 = (bf16[343,343]{1,0:T(8,128)(2,1)S(1)}, bf16[343,343]{1,0:T(8,128)(2,1)S(1)}, u32[]{:S(2)}, u32[]{:S(2)}) collective-permute-start(bf16[343,343]{1,0:T(8,128)(2,1)S(1)} %collective-permute-done.4), channel_id=1, source_target_pairs={{0,1},{1,0},{2,3},{3,2},{4,5},{5,4},{6,7},{7,6},{8,9},{9,8},{10,11... | collective-permute-start | bytes 705902 | tf_op jit(solution)/shard_map/ppermute | solution.py:59
  24.3 4.1 %collective-permute-start.10 = (bf16[7,1,7,128]{3,2,1,0:T(8,128)(2,1)S(1)}, bf16[7,1,7,128]{3,2,1,0:T(8,128)(2,1)S(1)}, u32[]{:S(2)}, u32[]{:S(2)}) collective-permute-start(bf16[7,1,7,128]{3,2,1,0:T(8,128)(2,1)S(1)} %broadcast_select_fusion.45), channel_id=1, source_target_pairs={{0,13},{1,12},{2,15},{3,14},{4,9},{5,8},{6,11},{7,10},{8,5},{9,4},... | collective-permute-start | bytes 37640 | tf_op jit(solution)/shard_map/ppermute | solution.py:41
  25.7 3.2 %collective-permute-start.9 = (bf16[7,1,7,128]{3,2,1,0:T(8,128)(2,1)S(1)}, bf16[7,1,7,128]{3,2,1,0:T(8,128)(2,1)S(1)}, u32[]{:S(2)}, u32[]{:S(2)}) collective-permute-start(bf16[7,1,7,128]{3,2,1,0:T(8,128)(2,1)S(1)} %get-tuple-element.32), channel_id=1, source_target_pairs={{0,5},{1,4},{2,7},{3,6},{4,1},{5,0},{6,3},{7,2},{8,13},{9,12},{10,... | collective-permute-start | bytes 37640 | tf_op jit(solution)/shard_map/ppermute | solution.py:41
  29.0 4.1 %collective-permute-start.11 = (bf16[1,7,7,128]{3,2,1,0:T(8,128)(2,1)S(1)}, bf16[1,7,7,128]{3,2,1,0:T(8,128)(2,1)S(1)}, u32[]{:S(2)}, u32[]{:S(2)}) collective-permute-start(bf16[1,7,7,128]{3,2,1,0:T(8,128)(2,1)S(1)} %fusion.83), channel_id=1, source_target_pairs={{0,17},{1,16},{2,19},{3,18},{4,21},{5,20},{6,23},{7,22},{8,25},{9,... | collective-permute-start | bytes 37640 | tf_op jit(solution)/shard_map/ppermute | solution.py:41
  31.6 20.0 %collective-permute-start.17 = (bf16[252,704]{1,0:T(8,128)(2,1)S(1)}, bf16[252,704]{1,0:T(8,128)(2,1)S(1)}, u32[]{:S(2)}, u32[]{:S(2)}) collective-permute-start(bf16[252,704]{1,0:T(8,128)(2,1)S(1)} %pad_maximum_fusion), channel_id=1, source_target_pairs={{0,1},{1,0},{2,3},{3,2},{4,5},{5,4},{6,7},{7,6},{8,9},{9,8},{10,11... | collective-permute-start | bytes 1064456 | tf_op jit(solution)/shard_map/ppermute | solution.py:59
  34.6 2.9 %slice-start = ((bf16[216,704]{1,0:T(8,128)(2,1)}), bf16[92,704]{1,0:T(8,128)(2,1)S(1)}, s32[]{:S(2)}) async-start(bf16[216,704]{1,0:T(8,128)(2,1)} %param.9), calls=%async_computation | async-start | bytes 294912 | tf_op jit(solution)/shard_map/slice | solution.py:210
  34.6 4.1 %collective-permute-start.13 = (bf16[7,1,7,128]{3,2,1,0:T(8,128)(2,1)S(1)}, bf16[7,1,7,128]{3,2,1,0:T(8,128)(2,1)S(1)}, u32[]{:S(2)}, u32[]{:S(2)}) collective-permute-start(bf16[7,1,7,128]{3,2,1,0:T(8,128)(2,1)S(1)} %broadcast_select_fusion.44), channel_id=1, source_target_pairs={{0,13},{1,12},{2,15},{3,14},{4,9},{5,8},{6,11},{7,10},{8,5},{9,4},... | collective-permute-start | bytes 37640 | tf_op jit(solution)/shard_map/ppermute | solution.py:41
  36.1 3.3 %collective-permute-start.12 = (bf16[7,1,7,128]{3,2,1,0:T(8,128)(2,1)S(1)}, bf16[7,1,7,128]{3,2,1,0:T(8,128)(2,1)S(1)}, u32[]{:S(2)}, u32[]{:S(2)}) collective-permute-start(bf16[7,1,7,128]{3,2,1,0:T(8,128)(2,1)S(1)} %get-tuple-element.29), channel_id=1, source_target_pairs={{0,5},{1,4},{2,7},{3,6},{4,1},{5,0},{6,3},{7,2},{8,13},{9,12},{10,... | collective-permute-start | bytes 37640 | tf_op jit(solution)/shard_map/ppermute | solution.py:41
  37.5 6.9 %collective-permute-start.18 = (bf16[128,704]{1,0:T(8,128)(2,1)S(1)}, bf16[128,704]{1,0:T(8,128)(2,1)S(1)}, u32[]{:S(2)}, u32[]{:S(2)}) collective-permute-start(bf16[128,704]{1,0:T(8,128)(2,1)S(1)} %pad_maximum_fusion.2), channel_id=1, source_target_pairs={{0,3},{1,2},{2,1},{3,0},{4,7},{5,6},{6,5},{7,4},{8,11},{9,10},{10,... | collective-permute-start | bytes 540680 | tf_op jit(solution)/shard_map/ppermute | solution.py:59
  39.4 5.0 %collective-permute-start.14 = (bf16[1,7,7,128]{3,2,1,0:T(8,128)(2,1)S(1)}, bf16[1,7,7,128]{3,2,1,0:T(8,128)(2,1)S(1)}, u32[]{:S(2)}, u32[]{:S(2)}) collective-permute-start(bf16[1,7,7,128]{3,2,1,0:T(8,128)(2,1)S(1)} %fusion.84), channel_id=1, source_target_pairs={{0,17},{1,16},{2,19},{3,18},{4,21},{5,20},{6,23},{7,22},{8,25},{9,... | collective-permute-start | bytes 37640 | tf_op jit(solution)/shard_map/ppermute | solution.py:41
  46.0 3.2 %collective-permute-start.15 = (bf16[7,1,7,128]{3,2,1,0:T(8,128)(2,1)S(1)}, bf16[7,1,7,128]{3,2,1,0:T(8,128)(2,1)S(1)}, u32[]{:S(2)}, u32[]{:S(2)}) collective-permute-start(bf16[7,1,7,128]{3,2,1,0:T(8,128)(2,1)S(1)} %slice.699), channel_id=1, source_target_pairs={{0,5},{1,4},{2,7},{3,6},{4,1},{5,0},{6,3},{7,2},{8,13},{9,12},{10,... | collective-permute-start | bytes 37640 | tf_op jit(solution)/shard_map/ppermute | solution.py:41
  46.7 4.0 %collective-permute-start.16 = (bf16[7,1,7,128]{3,2,1,0:T(8,128)(2,1)S(1)}, bf16[7,1,7,128]{3,2,1,0:T(8,128)(2,1)S(1)}, u32[]{:S(2)}, u32[]{:S(2)}) collective-permute-start(bf16[7,1,7,128]{3,2,1,0:T(8,128)(2,1)S(1)} %slice.699), channel_id=1, source_target_pairs={{0,13},{1,12},{2,15},{3,14},{4,9},{5,8},{6,11},{7,10},{8,5},{9,4},... | collective-permute-start | bytes 37640 | tf_op jit(solution)/shard_map/ppermute | solution.py:41
  47.7 4.2 %collective-permute-start.19 = (bf16[252,704]{1,0:T(8,128)(2,1)S(1)}, bf16[252,704]{1,0:T(8,128)(2,1)S(1)}, u32[]{:S(2)}, u32[]{:S(2)}) collective-permute-start(bf16[252,704]{1,0:T(8,128)(2,1)S(1)} %constant_dynamic-update-slice_fusion.6), channel_id=1, source_target_pairs={{0,1},{1,0},{2,3},{3,2},{4,5},{5,4},{6,7},{7,6},{8,9},{9,8},{10,11... | collective-permute-start | bytes 1064456 | tf_op jit(solution)/shard_map/ppermute | solution.py:59
  52.7 6.0 %collective-permute-start.20 = (bf16[212,128]{1,0:T(8,128)(2,1)S(1)}, bf16[212,128]{1,0:T(8,128)(2,1)S(1)}, u32[]{:S(2)}, u32[]{:S(2)}) collective-permute-start(bf16[212,128]{1,0:T(8,128)(2,1)S(1)} %pad_maximum_fusion.11), channel_id=1, source_target_pairs={{0,17},{1,16},{2,19},{3,18},{4,21},{5,20},{6,23},{7,22},{8,25},{9,... | collective-permute-start | bytes 162824 | tf_op jit(solution)/shard_map/ppermute | solution.py:59
  58.9 3.7 %collective-permute-start.21 = (bf16[176,128]{1,0:T(8,128)(2,1)S(1)}, bf16[176,128]{1,0:T(8,128)(2,1)S(1)}, u32[]{:S(2)}, u32[]{:S(2)}) collective-permute-start(bf16[176,128]{1,0:T(8,128)(2,1)S(1)} %add_convert_fusion.2), channel_id=1, source_target_pairs={{0,5},{1,4},{2,7},{3,6},{4,1},{5,0},{6,3},{7,2},{8,13},{9,12},{10,... | collective-permute-start | bytes 135176 | tf_op jit(solution)/shard_map/ppermute | solution.py:41
  62.6 4.6 %collective-permute-start.22 = (bf16[176,128]{1,0:T(8,128)(2,1)S(1)}, bf16[176,128]{1,0:T(8,128)(2,1)S(1)}, u32[]{:S(2)}, u32[]{:S(2)}) collective-permute-start(bf16[176,128]{1,0:T(8,128)(2,1)S(1)} %add_convert_fusion.1), channel_id=1, source_target_pairs={{0,13},{1,12},{2,15},{3,14},{4,9},{5,8},{6,11},{7,10},{8,5},{9,4},... | collective-permute-start | bytes 135176 | tf_op jit(solution)/shard_map/ppermute | solution.py:41
  67.3 4.3 %collective-permute-start.23 = (bf16[284,128]{1,0:T(8,128)(2,1)S(1)}, bf16[284,128]{1,0:T(8,128)(2,1)S(1)}, u32[]{:S(2)}, u32[]{:S(2)}) collective-permute-start(bf16[284,128]{1,0:T(8,128)(2,1)S(1)} %maximum_maximum_fusion.1), channel_id=1, source_target_pairs={{0,3},{1,2},{2,1},{3,0},{4,7},{5,6},{6,5},{7,4},{8,11},{9,10},{10,... | collective-permute-start | bytes 218120 | tf_op jit(solution)/shard_map/ppermute | solution.py:59
  71.8 1.3 %collective-permute-start.24 = (bf16[108,128]{1,0:T(8,128)(2,1)S(1)}, bf16[108,128]{1,0:T(8,128)(2,1)S(1)}, u32[]{:S(2)}, u32[]{:S(2)}) collective-permute-start(bf16[108,128]{1,0:T(8,128)(2,1)S(1)} %pad_maximum_fusion.22), channel_id=1, source_target_pairs={{0,1},{1,0},{2,3},{3,2},{4,5},{5,4},{6,7},{7,6},{8,9},{9,8},{10,11... | collective-permute-start | bytes 82952 | tf_op jit(solution)/shard_map/ppermute | solution.py:59
  72.0 2.1 %collective-permute-start.26 = (bf16[176,128]{1,0:T(8,128)(2,1)S(1)}, bf16[176,128]{1,0:T(8,128)(2,1)S(1)}, u32[]{:S(2)}, u32[]{:S(2)}) collective-permute-start(bf16[176,128]{1,0:T(8,128)(2,1)S(1)} %add_convert_fusion), channel_id=1, source_target_pairs={{0,1},{1,0},{2,3},{3,2},{4,5},{5,4},{6,7},{7,6},{8,9},{9,8},{10,11... | collective-permute-start | bytes 135176 | tf_op jit(solution)/shard_map/ppermute | solution.py:59
  72.4 1.7 %collective-permute-start.25 = (bf16[176,128]{1,0:T(8,128)(2,1)S(1)}, bf16[176,128]{1,0:T(8,128)(2,1)S(1)}, u32[]{:S(2)}, u32[]{:S(2)}) collective-permute-start(bf16[176,128]{1,0:T(8,128)(2,1)S(1)} %slice.595), channel_id=1, source_target_pairs={{0,1},{1,0},{2,3},{3,2},{4,5},{5,4},{6,7},{7,6},{8,9},{9,8},{10,11... | collective-permute-start | bytes 135176 | tf_op jit(solution)/shard_map/ppermute | solution.py:59

commit v20 on v19

--- a/solution.py
+++ b/solution.py
@@ -202,13 +202,13 @@
     top = jnp.pad(locked[-edge * edge :], ((0, 0), (0, -locked.shape[1] % columns)))
     top = lax.optimization_barrier(jnp.concatenate(split(top, tiles), axis=0))
     sent = jnp.concatenate([top, high], axis=0)
-    sent, matrix = lax.optimization_barrier((sent, matrix))
+    cut = max(0, 128 - edge * edge)
+    sent, matrix, early = lax.optimization_barrier((sent, matrix, locked[cut:]))
     arrived = grid.exchanged(sent, sent, 0, cross=0)[0]
     bottom = jnp.split(arrived[: top.shape[0]], tiles, axis=0)
     bottom = jnp.concatenate(bottom, axis=1)[:, : locked.shape[1]]
-    cut = max(0, 128 - bottom.shape[0])
     other_late = grid.partner(jnp.concatenate([bottom, locked[:cut]], axis=0), FIRST)
-    other_early = grid.partner(locked[cut:], FIRST)
+    other_early = grid.partner(early, FIRST)
     field = jnp.concatenate(
         [arrived[top.shape[0] :].reshape(1, SIDE, edge, columns), field], axis=0
     )

time: 75.7 us -> 75.9 us (level)
  transfers between devices with their start and end apart: 27 -> 27, of which waited for: 16 -> 17; matrix products, arithmetic and copies ran while one was open for 12% -> 12% of each run, Pallas kernels for 0% -> 0%
where the time goes in v20:
time: 75.9 us; the launch traced here: 75.8 us
  waiting for transfers between devices  32.8 us (43%)
  starting transfers between devices  28 us (37%)
  other arithmetic  5.03 us (7%)
  matrix products  4.87 us (6%)
  local copies, waits for them, and re-layouts  3.34 us (4%)
  between operations  1.71 us (2%)
    ppermute x13, starting transfers between devices, swapped(): arrived = lax.ppermute(jnp.where(lower, high, low), AXIS, pairs)  19.9 us
    ppermute x13, waiting for transfers between devices, swapped(): arrived = lax.ppermute(jnp.where(lower, high, low), AXIS, pairs)  17.6 us
    ppermute x14, waiting for transfers between devices, partner(): lax.ppermute(value, AXIS, [(i, i ^ bits) for i in range(self.devices)])  15.1 us
    ppermute x14, starting transfers between devices, partner(): lax.ppermute(value, AXIS, [(i, i ^ bits) for i in range(self.devices)])  8.09 us
    dot_general x12, matrix products, per_device(): jnp.dot(matrices[r], own, preferred_element_type=jnp.float32)  2.93 us
  transfers between devices with their start and end apart: 27, of which 17 were waited for; matrix products, arithmetic and copies ran while one was open for 12% of the time, Pallas kernels for 0%

profile of v20, /device:TPU:0, one launch (start us, length us, event | category | flops | bytes accessed | tf_op | source)
XLA Modules:
  0.0 75.8 jit_solution(14665081083656006890)
XLA Ops:
  0.6 0.9 %reshape.116 = bf16[6,6,6,128]{3,2,1,0:T(8,128)(2,1)S(1)} reshape(bf16[216,128]{1,0:T(8,128)(2,1)} %param.5) | data formatting | bytes 110592 | tf_op jit(solution)/shard_map/reshape | solution.py:193
  1.6 3.0 %collective-permute-start = (bf16[6,1,6,128]{3,2,1,0:T(8,128)(2,1)S(1)}, bf16[6,1,6,128]{3,2,1,0:T(8,128)(2,1)S(1)}, u32[]{:S(2)}, u32[]{:S(2)}) collective-permute-start(bf16[6,1,6,128]{3,2,1,0:T(8,128)(2,1)S(1)} %slice.517), channel_id=1, source_target_pairs={{0,4},{1,5},{2,6},{3,7},{4,0},{5,1},{6,2},{7,3},{8,12},{9,13},{10,... | collective-permute-start | bytes 27656 | tf_op jit(solution)/shard_map/ppermute | solution.py:41
  4.6 1.5 %collective-permute-start.1 = (bf16[6,1,6,128]{3,2,1,0:T(8,128)(2,1)S(1)}, bf16[6,1,6,128]{3,2,1,0:T(8,128)(2,1)S(1)}, u32[]{:S(2)}, u32[]{:S(2)}) collective-permute-start(bf16[6,1,6,128]{3,2,1,0:T(8,128)(2,1)S(1)} %slice.517), channel_id=1, source_target_pairs={{0,12},{1,13},{2,14},{3,15},{4,8},{5,9},{6,10},{7,11},{8,4},{9,5},... | collective-permute-start | bytes 27656 | tf_op jit(solution)/shard_map/ppermute | solution.py:41
  6.2 0.7 fusion
  8.1 1.0 %collective-permute-done.1 = bf16[6,1,6,128]{3,2,1,0:T(8,128)(2,1)S(1)} collective-permute-done((bf16[6,1,6,128]{3,2,1,0:T(8,128)(2,1)S(1)}, bf16[6,1,6,128]{3,2,1,0:T(8,128)(2,1)S(1)}, u32[]{:S(2)}, u32[]{:S(2)}) %collective-permute-start.1) | collective-permute-done | bytes 9248 | tf_op jit(solution)/shard_map/ppermute | solution.py:41
  9.2 2.7 %collective-permute-start.2 = (bf16[258,128]{1,0:T(8,128)(2,1)S(1)}, bf16[258,128]{1,0:T(8,128)(2,1)S(1)}, u32[]{:S(2)}, u32[]{:S(2)}) collective-permute-start(bf16[258,128]{1,0:T(8,128)(2,1)S(1)} %pad_maximum_fusion.10), channel_id=1, source_target_pairs={{0,16},{1,17},{2,18},{3,19},{4,20},{5,21},{6,22},{7,23},{8,24},{9,... | collective-permute-start | bytes 198152 | tf_op jit(solution)/shard_map/ppermute | solution.py:41
  12.0 1.5 %collective-permute-start.8 = (bf16[343,343]{1,0:T(8,128)(2,1)S(1)}, bf16[343,343]{1,0:T(8,128)(2,1)S(1)}, u32[]{:S(2)}, u32[]{:S(2)}) collective-permute-start(bf16[343,343]{1,0:T(8,128)(2,1)S(1)} %fusion), channel_id=1, source_target_pairs={{0,1},{1,0},{2,3},{3,2},{4,5},{5,4},{6,7},{7,6},{8,9},{9,8},{10,11... | collective-permute-start | bytes 705902 | tf_op jit(solution)/shard_map/ppermute | solution.py:59
  13.5 2.3 %collective-permute-done.2 = bf16[258,128]{1,0:T(8,128)(2,1)S(1)} collective-permute-done((bf16[258,128]{1,0:T(8,128)(2,1)S(1)}, bf16[258,128]{1,0:T(8,128)(2,1)S(1)}, u32[]{:S(2)}, u32[]{:S(2)}) %collective-permute-start.2) | collective-permute-done | bytes 66080 | tf_op jit(solution)/shard_map/ppermute | solution.py:41
  16.4 4.2 %collective-permute-done.3 = bf16[152,128]{1,0:T(8,128)(2,1)S(1)} collective-permute-done((bf16[152,128]{1,0:T(8,128)(2,1)S(1)}, bf16[152,128]{1,0:T(8,128)(2,1)S(1)}, u32[]{:S(2)}, u32[]{:S(2)}) %collective-permute-start.3) | collective-permute-done | bytes 38944 | tf_op jit(solution)/shard_map/ppermute | solution.py:59
  21.5 0.7 collective-permute-done.5
  24.3 1.4 %collective-permute-start.10 = (bf16[7,1,7,128]{3,2,1,0:T(8,128)(2,1)S(1)}, bf16[7,1,7,128]{3,2,1,0:T(8,128)(2,1)S(1)}, u32[]{:S(2)}, u32[]{:S(2)}) collective-permute-start(bf16[7,1,7,128]{3,2,1,0:T(8,128)(2,1)S(1)} %broadcast_select_fusion.45), channel_id=1, source_target_pairs={{0,13},{1,12},{2,15},{3,14},{4,9},{5,8},{6,11},{7,10},{8,5},{9,4},... | collective-permute-start | bytes 37640 | tf_op jit(solution)/shard_map/ppermute | solution.py:41
  25.7 0.7 collective-permute-start.9
  26.4 2.0 %collective-permute-done.10 = bf16[7,1,7,128]{3,2,1,0:T(8,128)(2,1)S(1)} collective-permute-done((bf16[7,1,7,128]{3,2,1,0:T(8,128)(2,1)S(1)}, bf16[7,1,7,128]{3,2,1,0:T(8,128)(2,1)S(1)}, u32[]{:S(2)}, u32[]{:S(2)}) %collective-permute-start.10) | collective-permute-done | bytes 12576 | tf_op jit(solution)/shard_map/ppermute | solution.py:41
  29.0 2.4 %collective-permute-start.11 = (bf16[1,7,7,128]{3,2,1,0:T(8,128)(2,1)S(1)}, bf16[1,7,7,128]{3,2,1,0:T(8,128)(2,1)S(1)}, u32[]{:S(2)}, u32[]{:S(2)}) collective-permute-start(bf16[1,7,7,128]{3,2,1,0:T(8,128)(2,1)S(1)} %fusion.83), channel_id=1, source_target_pairs={{0,17},{1,16},{2,19},{3,18},{4,21},{5,20},{6,23},{7,22},{8,25},{9,... | collective-permute-start | bytes 37640 | tf_op jit(solution)/shard_map/ppermute | solution.py:41
  31.9 1.2 %collective-permute-done.11 = bf16[1,7,7,128]{3,2,1,0:T(8,128)(2,1)S(1)} collective-permute-done((bf16[1,7,7,128]{3,2,1,0:T(8,128)(2,1)S(1)}, bf16[1,7,7,128]{3,2,1,0:T(8,128)(2,1)S(1)}, u32[]{:S(2)}, u32[]{:S(2)}) %collective-permute-start.11) | collective-permute-done | bytes 12576 | tf_op jit(solution)/shard_map/ppermute | solution.py:41
  34.6 1.4 %collective-permute-start.13 = (bf16[7,1,7,128]{3,2,1,0:T(8,128)(2,1)S(1)}, bf16[7,1,7,128]{3,2,1,0:T(8,128)(2,1)S(1)}, u32[]{:S(2)}, u32[]{:S(2)}) collective-permute-start(bf16[7,1,7,128]{3,2,1,0:T(8,128)(2,1)S(1)} %broadcast_select_fusion.44), channel_id=1, source_target_pairs={{0,13},{1,12},{2,15},{3,14},{4,9},{5,8},{6,11},{7,10},{8,5},{9,4},... | collective-permute-start | bytes 37640 | tf_op jit(solution)/shard_map/ppermute | solution.py:41
  36.1 1.4 %collective-permute-start.12 = (bf16[7,1,7,128]{3,2,1,0:T(8,128)(2,1)S(1)}, bf16[7,1,7,128]{3,2,1,0:T(8,128)(2,1)S(1)}, u32[]{:S(2)}, u32[]{:S(2)}) collective-permute-start(bf16[7,1,7,128]{3,2,1,0:T(8,128)(2,1)S(1)} %get-tuple-element.31), channel_id=1, source_target_pairs={{0,5},{1,4},{2,7},{3,6},{4,1},{5,0},{6,3},{7,2},{8,13},{9,12},{10,... | collective-permute-start | bytes 37640 | tf_op jit(solution)/shard_map/ppermute | solution.py:41
  37.5 0.8 %collective-permute-start.18 = (bf16[128,704]{1,0:T(8,128)(2,1)S(1)}, bf16[128,704]{1,0:T(8,128)(2,1)S(1)}, u32[]{:S(2)}, u32[]{:S(2)}) collective-permute-start(bf16[128,704]{1,0:T(8,128)(2,1)S(1)} %pad_maximum_fusion.2), channel_id=1, source_target_pairs={{0,3},{1,2},{2,1},{3,0},{4,7},{5,6},{6,5},{7,4},{8,11},{9,10},{10,... | collective-permute-start | bytes 540680 | tf_op jit(solution)/shard_map/ppermute | solution.py:59
  39.3 2.6 %collective-permute-start.14 = (bf16[1,7,7,128]{3,2,1,0:T(8,128)(2,1)S(1)}, bf16[1,7,7,128]{3,2,1,0:T(8,128)(2,1)S(1)}, u32[]{:S(2)}, u32[]{:S(2)}) collective-permute-start(bf16[1,7,7,128]{3,2,1,0:T(8,128)(2,1)S(1)} %fusion.84), channel_id=1, source_target_pairs={{0,17},{1,16},{2,19},{3,18},{4,21},{5,20},{6,23},{7,22},{8,25},{9,... | collective-permute-start | bytes 37640 | tf_op jit(solution)/shard_map/ppermute | solution.py:41
  41.9 2.5 %collective-permute-done.18 = bf16[128,704]{1,0:T(8,128)(2,1)S(1)} collective-permute-done((bf16[128,704]{1,0:T(8,128)(2,1)S(1)}, bf16[128,704]{1,0:T(8,128)(2,1)S(1)}, u32[]{:S(2)}, u32[]{:S(2)}) %collective-permute-start.18) | collective-permute-done | bytes 180256 | tf_op jit(solution)/shard_map/ppermute | solution.py:59
  46.7 1.1 %collective-permute-start.16 = (bf16[7,1,7,128]{3,2,1,0:T(8,128)(2,1)S(1)}, bf16[7,1,7,128]{3,2,1,0:T(8,128)(2,1)S(1)}, u32[]{:S(2)}, u32[]{:S(2)}) collective-permute-start(bf16[7,1,7,128]{3,2,1,0:T(8,128)(2,1)S(1)} %slice.699), channel_id=1, source_target_pairs={{0,13},{1,12},{2,15},{3,14},{4,9},{5,8},{6,11},{7,10},{8,5},{9,4},... | collective-permute-start | bytes 37640 | tf_op jit(solution)/shard_map/ppermute | solution.py:41
  48.0 1.2 %collective-permute-done.15 = bf16[7,1,7,128]{3,2,1,0:T(8,128)(2,1)S(1)} collective-permute-done((bf16[7,1,7,128]{3,2,1,0:T(8,128)(2,1)S(1)}, bf16[7,1,7,128]{3,2,1,0:T(8,128)(2,1)S(1)}, u32[]{:S(2)}, u32[]{:S(2)}) %collective-permute-start.15) | collective-permute-done | bytes 12576 | tf_op jit(solution)/shard_map/ppermute | solution.py:41
  49.2 1.5 %collective-permute-done.16 = bf16[7,1,7,128]{3,2,1,0:T(8,128)(2,1)S(1)} collective-permute-done((bf16[7,1,7,128]{3,2,1,0:T(8,128)(2,1)S(1)}, bf16[7,1,7,128]{3,2,1,0:T(8,128)(2,1)S(1)}, u32[]{:S(2)}, u32[]{:S(2)}) %collective-permute-start.16) | collective-permute-done | bytes 12576 | tf_op jit(solution)/shard_map/ppermute | solution.py:41
  52.8 2.4 %collective-permute-start.20 = (bf16[212,128]{1,0:T(8,128)(2,1)S(1)}, bf16[212,128]{1,0:T(8,128)(2,1)S(1)}, u32[]{:S(2)}, u32[]{:S(2)}) collective-permute-start(bf16[212,128]{1,0:T(8,128)(2,1)S(1)} %pad_maximum_fusion.11), channel_id=1, source_target_pairs={{0,17},{1,16},{2,19},{3,18},{4,21},{5,20},{6,23},{7,22},{8,25},{9,... | collective-permute-start | bytes 162824 | tf_op jit(solution)/shard_map/ppermute | solution.py:59
  55.2 3.7 %collective-permute-done.20 = bf16[212,128]{1,0:T(8,128)(2,1)S(1)} collective-permute-done((bf16[212,128]{1,0:T(8,128)(2,1)S(1)}, bf16[212,128]{1,0:T(8,128)(2,1)S(1)}, u32[]{:S(2)}, u32[]{:S(2)}) %collective-permute-start.20) | collective-permute-done | bytes 54304 | tf_op jit(solution)/shard_map/ppermute | solution.py:59
  59.0 1.0 %collective-permute-start.21 = (bf16[176,128]{1,0:T(8,128)(2,1)S(1)}, bf16[176,128]{1,0:T(8,128)(2,1)S(1)}, u32[]{:S(2)}, u32[]{:S(2)}) collective-permute-start(bf16[176,128]{1,0:T(8,128)(2,1)S(1)} %add_convert_fusion.2), channel_id=1, source_target_pairs={{0,5},{1,4},{2,7},{3,6},{4,1},{5,0},{6,3},{7,2},{8,13},{9,12},{10,... | collective-permute-start | bytes 135176 | tf_op jit(solution)/shard_map/ppermute | solution.py:41
  60.2 2.5 %collective-permute-done.21 = bf16[176,128]{1,0:T(8,128)(2,1)S(1)} collective-permute-done((bf16[176,128]{1,0:T(8,128)(2,1)S(1)}, bf16[176,128]{1,0:T(8,128)(2,1)S(1)}, u32[]{:S(2)}, u32[]{:S(2)}) %collective-permute-start.21) | collective-permute-done | bytes 45088 | tf_op jit(solution)/shard_map/ppermute | solution.py:41
  62.8 4.5 %collective-permute-done.22 = bf16[176,128]{1,0:T(8,128)(2,1)S(1)} collective-permute-done((bf16[176,128]{1,0:T(8,128)(2,1)S(1)}, bf16[176,128]{1,0:T(8,128)(2,1)S(1)}, u32[]{:S(2)}, u32[]{:S(2)}) %collective-permute-start.22) | collective-permute-done | bytes 45088 | tf_op jit(solution)/shard_map/ppermute | solution.py:41
  67.5 0.8 %collective-permute-start.23 = (bf16[284,128]{1,0:T(8,128)(2,1)S(1)}, bf16[284,128]{1,0:T(8,128)(2,1)S(1)}, u32[]{:S(2)}, u32[]{:S(2)}) collective-permute-start(bf16[284,128]{1,0:T(8,128)(2,1)S(1)} %maximum_maximum_fusion.1), channel_id=1, source_target_pairs={{0,3},{1,2},{2,1},{3,0},{4,7},{5,6},{6,5},{7,4},{8,11},{9,10},{10,... | collective-permute-start | bytes 218120 | tf_op jit(solution)/shard_map/ppermute | solution.py:59
  68.3 3.5 %collective-permute-done.23 = bf16[284,128]{1,0:T(8,128)(2,1)S(1)} collective-permute-done((bf16[284,128]{1,0:T(8,128)(2,1)S(1)}, bf16[284,128]{1,0:T(8,128)(2,1)S(1)}, u32[]{:S(2)}, u32[]{:S(2)}) %collective-permute-start.23) | collective-permute-done | bytes 72736 | tf_op jit(solution)/shard_map/ppermute | solution.py:59
  73.6 0.7 pad_maximum_fusion.15
  74.8 1.0 %maximum_convert_fusion = f32[704,128]{1,0:T(8,128)} fusion(bf16[176,32]{1,0:T(8,128)(2,1)S(1)} %get-tuple-element.116, bf16[176,32]{1,0:T(8,128)(2,1)S(1)} %get-tuple-element.112, bf16[176,32]{1,0:T(8,128)(2,1)S(1)} %get-tuple-element.108, bf16[176,32]{1,0:T(8,128)(2,1)S(1)} %get-tuple-element.104, bf16[176,32]{1,0:T(8,128)(2,1)S(1)} %get-tuple-element.117, ...), kind=kLoop, calls=%fused_computation.51 | loop fusion | flops 2883584 | bytes 540672 | tf_op jit(solution)/shard_map/convert_element_type | solution.py:329
  (170 shorter events, 15.1 us)
Async XLA Ops:
  0.6 5.5 %copy-start = (bf16[1,343,343]{2,1,0:T(8,128)(2,1)S(1)}, bf16[1,343,343]{2,1,0:T(8,128)(2,1)}, u32[]{:S(2)}) copy-start(bf16[1,343,343]{2,1,0:T(8,128)(2,1)} %param.6) | copy-start | bytes 705898
  1.5 4.6 %copy-start.2 = (s32[1,343]{1,0:T(1,128)S(1)}, s32[1,343]{1,0:T(1,128)}, u32[]{:S(2)}) copy-start(s32[1,343]{1,0:T(1,128)} %param.7) | copy-start | bytes 4120
  1.5 4.6 %copy-start.3 = (f32[343]{0:T(512)S(1)}, f32[343]{0:T(512)}, u32[]{:S(2)}) copy-start(f32[343]{0:T(512)} %param.8) | copy-start | bytes 4120
  1.6 6.6 %collective-permute-start = (bf16[6,1,6,128]{3,2,1,0:T(8,128)(2,1)S(1)}, bf16[6,1,6,128]{3,2,1,0:T(8,128)(2,1)S(1)}, u32[]{:S(2)}, u32[]{:S(2)}) collective-permute-start(bf16[6,1,6,128]{3,2,1,0:T(8,128)(2,1)S(1)} %slice.517), channel_id=1, source_target_pairs={{0,4},{1,5},{2,6},{3,7},{4,0},{5,1},{6,2},{7,3},{8,12},{9,13},{10,... | collective-permute-start | bytes 27656 | tf_op jit(solution)/shard_map/ppermute | solution.py:41
  4.6 4.6 %collective-permute-start.1 = (bf16[6,1,6,128]{3,2,1,0:T(8,128)(2,1)S(1)}, bf16[6,1,6,128]{3,2,1,0:T(8,128)(2,1)S(1)}, u32[]{:S(2)}, u32[]{:S(2)}) collective-permute-start(bf16[6,1,6,128]{3,2,1,0:T(8,128)(2,1)S(1)} %slice.517), channel_id=1, source_target_pairs={{0,12},{1,13},{2,14},{3,15},{4,8},{5,9},{6,10},{7,11},{8,4},{9,5},... | collective-permute-start | bytes 27656 | tf_op jit(solution)/shard_map/ppermute | solution.py:41
  6.2 1.2 %copy-start.1 = (bf16[216,704]{1,0:T(8,128)(2,1)S(1)}, bf16[216,704]{1,0:T(8,128)(2,1)}, u32[]{:S(2)}) copy-start(bf16[216,704]{1,0:T(8,128)(2,1)} %param.9) | copy-start | bytes 912388
  6.9 14.0 %collective-permute-start.4 = (bf16[343,343]{1,0:T(8,128)(2,1)S(1)}, bf16[343,343]{1,0:T(8,128)(2,1)S(1)}, u32[]{:S(2)}, u32[]{:S(2)}) collective-permute-start(bf16[343,343]{1,0:T(8,128)(2,1)S(1)} %fusion), channel_id=1, source_target_pairs={{0,3},{1,2},{2,1},{3,0},{4,7},{5,6},{6,5},{7,4},{8,11},{9,10},{10,... | collective-permute-start | bytes 705902 | tf_op jit(solution)/shard_map/ppermute | solution.py:59
  9.2 6.6 %collective-permute-start.2 = (bf16[258,128]{1,0:T(8,128)(2,1)S(1)}, bf16[258,128]{1,0:T(8,128)(2,1)S(1)}, u32[]{:S(2)}, u32[]{:S(2)}) collective-permute-start(bf16[258,128]{1,0:T(8,128)(2,1)S(1)} %pad_maximum_fusion.10), channel_id=1, source_target_pairs={{0,16},{1,17},{2,18},{3,19},{4,20},{5,21},{6,22},{7,23},{8,24},{9,... | collective-permute-start | bytes 198152 | tf_op jit(solution)/shard_map/ppermute | solution.py:41
  11.9 10.7 %collective-permute-start.7 = (bf16[124,704]{1,0:T(8,128)(2,1)S(1)}, bf16[124,704]{1,0:T(8,128)(2,1)S(1)}, u32[]{:S(2)}, u32[]{:S(2)}) collective-permute-start(bf16[124,704]{1,0:T(8,128)(2,1)S(1)} %slice.405), channel_id=1, source_target_pairs={{0,3},{1,2},{2,1},{3,0},{4,7},{5,6},{6,5},{7,4},{8,11},{9,10},{10,... | collective-permute-start | bytes 523784 | tf_op jit(solution)/shard_map/ppermute | solution.py:59
  12.0 11.4 %collective-permute-start.8 = (bf16[343,343]{1,0:T(8,128)(2,1)S(1)}, bf16[343,343]{1,0:T(8,128)(2,1)S(1)}, u32[]{:S(2)}, u32[]{:S(2)}) collective-permute-start(bf16[343,343]{1,0:T(8,128)(2,1)S(1)} %fusion), channel_id=1, source_target_pairs={{0,1},{1,0},{2,3},{3,2},{4,5},{5,4},{6,7},{7,6},{8,9},{9,8},{10,11... | collective-permute-start | bytes 705902 | tf_op jit(solution)/shard_map/ppermute | solution.py:59
  16.3 4.3 %collective-permute-start.3 = (bf16[152,128]{1,0:T(8,128)(2,1)S(1)}, bf16[152,128]{1,0:T(8,128)(2,1)S(1)}, u32[]{:S(2)}, u32[]{:S(2)}) collective-permute-start(bf16[152,128]{1,0:T(8,128)(2,1)S(1)} %pad_maximum_fusion.16), channel_id=1, source_target_pairs={{0,3},{1,2},{2,1},{3,0},{4,7},{5,6},{6,5},{7,4},{8,11},{9,10},{10,... | collective-permute-start | bytes 116744 | tf_op jit(solution)/shard_map/ppermute | solution.py:59
  20.9 1.3 %collective-permute-start.5 = (bf16[152,128]{1,0:T(8,128)(2,1)S(1)}, bf16[152,128]{1,0:T(8,128)(2,1)S(1)}, u32[]{:S(2)}, u32[]{:S(2)}) collective-permute-start(bf16[152,128]{1,0:T(8,128)(2,1)S(1)} %pad_maximum_fusion.17), channel_id=1, source_target_pairs={{0,1},{1,0},{2,3},{3,2},{4,5},{5,4},{6,7},{7,6},{8,9},{9,8},{10,11... | collective-permute-start | bytes 116744 | tf_op jit(solution)/shard_map/ppermute | solution.py:59
  21.1 1.6 %collective-permute-start.6 = (bf16[343,343]{1,0:T(8,128)(2,1)S(1)}, bf16[343,343]{1,0:T(8,128)(2,1)S(1)}, u32[]{:S(2)}, u32[]{:S(2)}) collective-permute-start(bf16[343,343]{1,0:T(8,128)(2,1)S(1)} %collective-permute-done.4), channel_id=1, source_target_pairs={{0,1},{1,0},{2,3},{3,2},{4,5},{5,4},{6,7},{7,6},{8,9},{9,8},{10,11... | collective-permute-start | bytes 705902 | tf_op jit(solution)/shard_map/ppermute | solution.py:59
  24.3 4.1 %collective-permute-start.10 = (bf16[7,1,7,128]{3,2,1,0:T(8,128)(2,1)S(1)}, bf16[7,1,7,128]{3,2,1,0:T(8,128)(2,1)S(1)}, u32[]{:S(2)}, u32[]{:S(2)}) collective-permute-start(bf16[7,1,7,128]{3,2,1,0:T(8,128)(2,1)S(1)} %broadcast_select_fusion.45), channel_id=1, source_target_pairs={{0,13},{1,12},{2,15},{3,14},{4,9},{5,8},{6,11},{7,10},{8,5},{9,4},... | collective-permute-start | bytes 37640 | tf_op jit(solution)/shard_map/ppermute | solution.py:41
  25.7 3.2 %collective-permute-start.9 = (bf16[7,1,7,128]{3,2,1,0:T(8,128)(2,1)S(1)}, bf16[7,1,7,128]{3,2,1,0:T(8,128)(2,1)S(1)}, u32[]{:S(2)}, u32[]{:S(2)}) collective-permute-start(bf16[7,1,7,128]{3,2,1,0:T(8,128)(2,1)S(1)} %get-tuple-element.34), channel_id=1, source_target_pairs={{0,5},{1,4},{2,7},{3,6},{4,1},{5,0},{6,3},{7,2},{8,13},{9,12},{10,... | collective-permute-start | bytes 37640 | tf_op jit(solution)/shard_map/ppermute | solution.py:41
  29.0 4.1 %collective-permute-start.11 = (bf16[1,7,7,128]{3,2,1,0:T(8,128)(2,1)S(1)}, bf16[1,7,7,128]{3,2,1,0:T(8,128)(2,1)S(1)}, u32[]{:S(2)}, u32[]{:S(2)}) collective-permute-start(bf16[1,7,7,128]{3,2,1,0:T(8,128)(2,1)S(1)} %fusion.83), channel_id=1, source_target_pairs={{0,17},{1,16},{2,19},{3,18},{4,21},{5,20},{6,23},{7,22},{8,25},{9,... | collective-permute-start | bytes 37640 | tf_op jit(solution)/shard_map/ppermute | solution.py:41
  31.5 20.2 %collective-permute-start.17 = (bf16[252,704]{1,0:T(8,128)(2,1)S(1)}, bf16[252,704]{1,0:T(8,128)(2,1)S(1)}, u32[]{:S(2)}, u32[]{:S(2)}) collective-permute-start(bf16[252,704]{1,0:T(8,128)(2,1)S(1)} %pad_maximum_fusion), channel_id=1, source_target_pairs={{0,1},{1,0},{2,3},{3,2},{4,5},{5,4},{6,7},{7,6},{8,9},{9,8},{10,11... | collective-permute-start | bytes 1064456 | tf_op jit(solution)/shard_map/ppermute | solution.py:59
  34.6 2.9 %slice-start = ((bf16[216,704]{1,0:T(8,128)(2,1)}), bf16[92,704]{1,0:T(8,128)(2,1)S(1)}, s32[]{:S(2)}) async-start(bf16[216,704]{1,0:T(8,128)(2,1)} %param.9), calls=%async_computation | async-start | bytes 294912 | tf_op jit(solution)/shard_map/slice | solution.py:210
  34.6 4.1 %collective-permute-start.13 = (bf16[7,1,7,128]{3,2,1,0:T(8,128)(2,1)S(1)}, bf16[7,1,7,128]{3,2,1,0:T(8,128)(2,1)S(1)}, u32[]{:S(2)}, u32[]{:S(2)}) collective-permute-start(bf16[7,1,7,128]{3,2,1,0:T(8,128)(2,1)S(1)} %broadcast_select_fusion.44), channel_id=1, source_target_pairs={{0,13},{1,12},{2,15},{3,14},{4,9},{5,8},{6,11},{7,10},{8,5},{9,4},... | collective-permute-start | bytes 37640 | tf_op jit(solution)/shard_map/ppermute | solution.py:41
  36.1 3.2 %collective-permute-start.12 = (bf16[7,1,7,128]{3,2,1,0:T(8,128)(2,1)S(1)}, bf16[7,1,7,128]{3,2,1,0:T(8,128)(2,1)S(1)}, u32[]{:S(2)}, u32[]{:S(2)}) collective-permute-start(bf16[7,1,7,128]{3,2,1,0:T(8,128)(2,1)S(1)} %get-tuple-element.31), channel_id=1, source_target_pairs={{0,5},{1,4},{2,7},{3,6},{4,1},{5,0},{6,3},{7,2},{8,13},{9,12},{10,... | collective-permute-start | bytes 37640 | tf_op jit(solution)/shard_map/ppermute | solution.py:41
  37.5 6.9 %collective-permute-start.18 = (bf16[128,704]{1,0:T(8,128)(2,1)S(1)}, bf16[128,704]{1,0:T(8,128)(2,1)S(1)}, u32[]{:S(2)}, u32[]{:S(2)}) collective-permute-start(bf16[128,704]{1,0:T(8,128)(2,1)S(1)} %pad_maximum_fusion.2), channel_id=1, source_target_pairs={{0,3},{1,2},{2,1},{3,0},{4,7},{5,6},{6,5},{7,4},{8,11},{9,10},{10,... | collective-permute-start | bytes 540680 | tf_op jit(solution)/shard_map/ppermute | solution.py:59
  39.3 5.1 %collective-permute-start.14 = (bf16[1,7,7,128]{3,2,1,0:T(8,128)(2,1)S(1)}, bf16[1,7,7,128]{3,2,1,0:T(8,128)(2,1)S(1)}, u32[]{:S(2)}, u32[]{:S(2)}) collective-permute-start(bf16[1,7,7,128]{3,2,1,0:T(8,128)(2,1)S(1)} %fusion.84), channel_id=1, source_target_pairs={{0,17},{1,16},{2,19},{3,18},{4,21},{5,20},{6,23},{7,22},{8,25},{9,... | collective-permute-start | bytes 37640 | tf_op jit(solution)/shard_map/ppermute | solution.py:41
  46.0 3.2 %collective-permute-start.15 = (bf16[7,1,7,128]{3,2,1,0:T(8,128)(2,1)S(1)}, bf16[7,1,7,128]{3,2,1,0:T(8,128)(2,1)S(1)}, u32[]{:S(2)}, u32[]{:S(2)}) collective-permute-start(bf16[7,1,7,128]{3,2,1,0:T(8,128)(2,1)S(1)} %slice.699), channel_id=1, source_target_pairs={{0,5},{1,4},{2,7},{3,6},{4,1},{5,0},{6,3},{7,2},{8,13},{9,12},{10,... | collective-permute-start | bytes 37640 | tf_op jit(solution)/shard_map/ppermute | solution.py:41
  46.7 4.1 %collective-permute-start.16 = (bf16[7,1,7,128]{3,2,1,0:T(8,128)(2,1)S(1)}, bf16[7,1,7,128]{3,2,1,0:T(8,128)(2,1)S(1)}, u32[]{:S(2)}, u32[]{:S(2)}) collective-permute-start(bf16[7,1,7,128]{3,2,1,0:T(8,128)(2,1)S(1)} %slice.699), channel_id=1, source_target_pairs={{0,13},{1,12},{2,15},{3,14},{4,9},{5,8},{6,11},{7,10},{8,5},{9,4},... | collective-permute-start | bytes 37640 | tf_op jit(solution)/shard_map/ppermute | solution.py:41
  47.8 4.2 %collective-permute-start.19 = (bf16[252,704]{1,0:T(8,128)(2,1)S(1)}, bf16[252,704]{1,0:T(8,128)(2,1)S(1)}, u32[]{:S(2)}, u32[]{:S(2)}) collective-permute-start(bf16[252,704]{1,0:T(8,128)(2,1)S(1)} %constant_dynamic-update-slice_fusion.6), channel_id=1, source_target_pairs={{0,1},{1,0},{2,3},{3,2},{4,5},{5,4},{6,7},{7,6},{8,9},{9,8},{10,11... | collective-permute-start | bytes 1064456 | tf_op jit(solution)/shard_map/ppermute | solution.py:59
  52.8 6.1 %collective-permute-start.20 = (bf16[212,128]{1,0:T(8,128)(2,1)S(1)}, bf16[212,128]{1,0:T(8,128)(2,1)S(1)}, u32[]{:S(2)}, u32[]{:S(2)}) collective-permute-start(bf16[212,128]{1,0:T(8,128)(2,1)S(1)} %pad_maximum_fusion.11), channel_id=1, source_target_pairs={{0,17},{1,16},{2,19},{3,18},{4,21},{5,20},{6,23},{7,22},{8,25},{9,... | collective-permute-start | bytes 162824 | tf_op jit(solution)/shard_map/ppermute | solution.py:59
  59.0 3.7 %collective-permute-start.21 = (bf16[176,128]{1,0:T(8,128)(2,1)S(1)}, bf16[176,128]{1,0:T(8,128)(2,1)S(1)}, u32[]{:S(2)}, u32[]{:S(2)}) collective-permute-start(bf16[176,128]{1,0:T(8,128)(2,1)S(1)} %add_convert_fusion.2), channel_id=1, source_target_pairs={{0,5},{1,4},{2,7},{3,6},{4,1},{5,0},{6,3},{7,2},{8,13},{9,12},{10,... | collective-permute-start | bytes 135176 | tf_op jit(solution)/shard_map/ppermute | solution.py:41
  62.7 4.6 %collective-permute-start.22 = (bf16[176,128]{1,0:T(8,128)(2,1)S(1)}, bf16[176,128]{1,0:T(8,128)(2,1)S(1)}, u32[]{:S(2)}, u32[]{:S(2)}) collective-permute-start(bf16[176,128]{1,0:T(8,128)(2,1)S(1)} %add_convert_fusion.1), channel_id=1, source_target_pairs={{0,13},{1,12},{2,15},{3,14},{4,9},{5,8},{6,11},{7,10},{8,5},{9,4},... | collective-permute-start | bytes 135176 | tf_op jit(solution)/shard_map/ppermute | solution.py:41
  67.5 4.3 %collective-permute-start.23 = (bf16[284,128]{1,0:T(8,128)(2,1)S(1)}, bf16[284,128]{1,0:T(8,128)(2,1)S(1)}, u32[]{:S(2)}, u32[]{:S(2)}) collective-permute-start(bf16[284,128]{1,0:T(8,128)(2,1)S(1)} %maximum_maximum_fusion.1), channel_id=1, source_target_pairs={{0,3},{1,2},{2,1},{3,0},{4,7},{5,6},{6,5},{7,4},{8,11},{9,10},{10,... | collective-permute-start | bytes 218120 | tf_op jit(solution)/shard_map/ppermute | solution.py:59
  72.0 1.3 %collective-permute-start.24 = (bf16[108,128]{1,0:T(8,128)(2,1)S(1)}, bf16[108,128]{1,0:T(8,128)(2,1)S(1)}, u32[]{:S(2)}, u32[]{:S(2)}) collective-permute-start(bf16[108,128]{1,0:T(8,128)(2,1)S(1)} %pad_maximum_fusion.22), channel_id=1, source_target_pairs={{0,1},{1,0},{2,3},{3,2},{4,5},{5,4},{6,7},{7,6},{8,9},{9,8},{10,11... | collective-permute-start | bytes 82952 | tf_op jit(solution)/shard_map/ppermute | solution.py:59
  72.2 2.1 %collective-permute-start.26 = (bf16[176,128]{1,0:T(8,128)(2,1)S(1)}, bf16[176,128]{1,0:T(8,128)(2,1)S(1)}, u32[]{:S(2)}, u32[]{:S(2)}) collective-permute-start(bf16[176,128]{1,0:T(8,128)(2,1)S(1)} %add_convert_fusion), channel_id=1, source_target_pairs={{0,1},{1,0},{2,3},{3,2},{4,5},{5,4},{6,7},{7,6},{8,9},{9,8},{10,11... | collective-permute-start | bytes 135176 | tf_op jit(solution)/shard_map/ppermute | solution.py:59
  72.6 1.7 %collective-permute-start.25 = (bf16[176,128]{1,0:T(8,128)(2,1)S(1)}, bf16[176,128]{1,0:T(8,128)(2,1)S(1)}, u32[]{:S(2)}, u32[]{:S(2)}) collective-permute-start(bf16[176,128]{1,0:T(8,128)(2,1)S(1)} %slice.595), channel_id=1, source_target_pairs={{0,1},{1,0},{2,3},{3,2},{4,5},{5,4},{6,7},{7,6},{8,9},{9,8},{10,11... | collective-permute-start | bytes 135176 | tf_op jit(solution)/shard_map/ppermute | solution.py:59

commit v21 on v19

--- a/solution.py
+++ b/solution.py
@@ -316,8 +316,10 @@
     came = unpacked(arrived[deep:], width)
     own = [near[0], came[0]]
     away = [near[1], came[1]]
-    came = unpacked(grid.partner(packed(away), SECOND), width)
-    others = [grid.partner(h, SECOND) for h in held]
+    first = grid.partner(share, SECOND)
+    away, first = lax.optimization_barrier((packed(away), first))
+    came = unpacked(grid.partner(away, SECOND), width)
+    others = [first, grid.partner(held[1], SECOND)]
     filtered = jnp.concatenate(placed([own[0], came[0], own[1], came[1]], high, low), axis=1)
     held = placed([held[0], others[0], held[1], others[1]], high, low)
     intersection = jnp.concatenate(

time: 75.7 us -> 75.7 us (level)
  no operation moved by 1% of the time
where the time goes in v21:
time: 75.7 us; the launch traced here: 75.6 us
  waiting for transfers between devices  32.2 us (43%)
  starting transfers between devices  28.4 us (38%)
  other arithmetic  5.03 us (7%)
  matrix products  4.87 us (6%)
  local copies, waits for them, and re-layouts  3.34 us (4%)
  between operations  1.73 us (2%)
    ppermute x13, starting transfers between devices, swapped(): arrived = lax.ppermute(jnp.where(lower, high, low), AXIS, pairs)  19.9 us
    ppermute x13, waiting for transfers between devices, swapped(): arrived = lax.ppermute(jnp.where(lower, high, low), AXIS, pairs)  18 us
    ppermute x14, waiting for transfers between devices, partner(): lax.ppermute(value, AXIS, [(i, i ^ bits) for i in range(self.devices)])  14.2 us
    ppermute x14, starting transfers between devices, partner(): lax.ppermute(value, AXIS, [(i, i ^ bits) for i in range(self.devices)])  8.51 us
    dot_general x12, matrix products, per_device(): jnp.dot(matrices[r], own, preferred_element_type=jnp.float32)  2.93 us
  transfers between devices with their start and end apart: 27, of which 16 were waited for; matrix products, arithmetic and copies ran while one was open for 12% of the time, Pallas kernels for 0%

profile of v21, /device:TPU:0, one launch (start us, length us, event | category | flops | bytes accessed | tf_op | source)
XLA Modules:
  0.0 75.6 jit_solution(12552314460799683718)
XLA Ops:
  0.6 0.9 %reshape.116 = bf16[6,6,6,128]{3,2,1,0:T(8,128)(2,1)S(1)} reshape(bf16[216,128]{1,0:T(8,128)(2,1)} %param.5) | data formatting | bytes 110592 | tf_op jit(solution)/shard_map/reshape | solution.py:193
  1.6 3.0 %collective-permute-start = (bf16[6,1,6,128]{3,2,1,0:T(8,128)(2,1)S(1)}, bf16[6,1,6,128]{3,2,1,0:T(8,128)(2,1)S(1)}, u32[]{:S(2)}, u32[]{:S(2)}) collective-permute-start(bf16[6,1,6,128]{3,2,1,0:T(8,128)(2,1)S(1)} %slice.517), channel_id=1, source_target_pairs={{0,4},{1,5},{2,6},{3,7},{4,0},{5,1},{6,2},{7,3},{8,12},{9,13},{10,... | collective-permute-start | bytes 27656 | tf_op jit(solution)/shard_map/ppermute | solution.py:41
  4.6 1.5 %collective-permute-start.1 = (bf16[6,1,6,128]{3,2,1,0:T(8,128)(2,1)S(1)}, bf16[6,1,6,128]{3,2,1,0:T(8,128)(2,1)S(1)}, u32[]{:S(2)}, u32[]{:S(2)}) collective-permute-start(bf16[6,1,6,128]{3,2,1,0:T(8,128)(2,1)S(1)} %slice.517), channel_id=1, source_target_pairs={{0,12},{1,13},{2,14},{3,15},{4,8},{5,9},{6,10},{7,11},{8,4},{9,5},... | collective-permute-start | bytes 27656 | tf_op jit(solution)/shard_map/ppermute | solution.py:41
  6.2 0.7 fusion
  7.4 1.4 %collective-permute-start.7 = (bf16[124,704]{1,0:T(8,128)(2,1)S(1)}, bf16[124,704]{1,0:T(8,128)(2,1)S(1)}, u32[]{:S(2)}, u32[]{:S(2)}) collective-permute-start(bf16[124,704]{1,0:T(8,128)(2,1)S(1)} %slice.426), channel_id=1, source_target_pairs={{0,3},{1,2},{2,1},{3,0},{4,7},{5,6},{6,5},{7,4},{8,11},{9,10},{10,... | collective-permute-start | bytes 523784 | tf_op jit(solution)/shard_map/ppermute | solution.py:59
  9.7 2.7 %collective-permute-start.2 = (bf16[258,128]{1,0:T(8,128)(2,1)S(1)}, bf16[258,128]{1,0:T(8,128)(2,1)S(1)}, u32[]{:S(2)}, u32[]{:S(2)}) collective-permute-start(bf16[258,128]{1,0:T(8,128)(2,1)S(1)} %pad_maximum_fusion.10), channel_id=1, source_target_pairs={{0,16},{1,17},{2,18},{3,19},{4,20},{5,21},{6,22},{7,23},{8,24},{9,... | collective-permute-start | bytes 198152 | tf_op jit(solution)/shard_map/ppermute | solution.py:41
  12.3 3.7 %collective-permute-done.2 = bf16[258,128]{1,0:T(8,128)(2,1)S(1)} collective-permute-done((bf16[258,128]{1,0:T(8,128)(2,1)S(1)}, bf16[258,128]{1,0:T(8,128)(2,1)S(1)}, u32[]{:S(2)}, u32[]{:S(2)}) %collective-permute-start.2) | collective-permute-done | bytes 66080 | tf_op jit(solution)/shard_map/ppermute | solution.py:41
  16.6 4.0 %collective-permute-done.3 = bf16[152,128]{1,0:T(8,128)(2,1)S(1)} collective-permute-done((bf16[152,128]{1,0:T(8,128)(2,1)S(1)}, bf16[152,128]{1,0:T(8,128)(2,1)S(1)}, u32[]{:S(2)}, u32[]{:S(2)}) %collective-permute-start.3) | collective-permute-done | bytes 38944 | tf_op jit(solution)/shard_map/ppermute | solution.py:59
  21.5 0.7 collective-permute-done.5
  24.3 1.4 %collective-permute-start.10 = (bf16[7,1,7,128]{3,2,1,0:T(8,128)(2,1)S(1)}, bf16[7,1,7,128]{3,2,1,0:T(8,128)(2,1)S(1)}, u32[]{:S(2)}, u32[]{:S(2)}) collective-permute-start(bf16[7,1,7,128]{3,2,1,0:T(8,128)(2,1)S(1)} %broadcast_select_fusion.45), channel_id=1, source_target_pairs={{0,13},{1,12},{2,15},{3,14},{4,9},{5,8},{6,11},{7,10},{8,5},{9,4},... | collective-permute-start | bytes 37640 | tf_op jit(solution)/shard_map/ppermute | solution.py:41
  25.9 2.5 %collective-permute-done.10 = bf16[7,1,7,128]{3,2,1,0:T(8,128)(2,1)S(1)} collective-permute-done((bf16[7,1,7,128]{3,2,1,0:T(8,128)(2,1)S(1)}, bf16[7,1,7,128]{3,2,1,0:T(8,128)(2,1)S(1)}, u32[]{:S(2)}, u32[]{:S(2)}) %collective-permute-start.10) | collective-permute-done | bytes 12576 | tf_op jit(solution)/shard_map/ppermute | solution.py:41
  29.0 2.6 %collective-permute-start.11 = (bf16[1,7,7,128]{3,2,1,0:T(8,128)(2,1)S(1)}, bf16[1,7,7,128]{3,2,1,0:T(8,128)(2,1)S(1)}, u32[]{:S(2)}, u32[]{:S(2)}) collective-permute-start(bf16[1,7,7,128]{3,2,1,0:T(8,128)(2,1)S(1)} %fusion.83), channel_id=1, source_target_pairs={{0,17},{1,16},{2,19},{3,18},{4,21},{5,20},{6,23},{7,22},{8,25},{9,... | collective-permute-start | bytes 37640 | tf_op jit(solution)/shard_map/ppermute | solution.py:41
  32.1 1.0 %collective-permute-done.11 = bf16[1,7,7,128]{3,2,1,0:T(8,128)(2,1)S(1)} collective-permute-done((bf16[1,7,7,128]{3,2,1,0:T(8,128)(2,1)S(1)}, bf16[1,7,7,128]{3,2,1,0:T(8,128)(2,1)S(1)}, u32[]{:S(2)}, u32[]{:S(2)}) %collective-permute-start.11) | collective-permute-done | bytes 12576 | tf_op jit(solution)/shard_map/ppermute | solution.py:41
  34.6 1.4 %collective-permute-start.13 = (bf16[7,1,7,128]{3,2,1,0:T(8,128)(2,1)S(1)}, bf16[7,1,7,128]{3,2,1,0:T(8,128)(2,1)S(1)}, u32[]{:S(2)}, u32[]{:S(2)}) collective-permute-start(bf16[7,1,7,128]{3,2,1,0:T(8,128)(2,1)S(1)} %broadcast_select_fusion.44), channel_id=1, source_target_pairs={{0,13},{1,12},{2,15},{3,14},{4,9},{5,8},{6,11},{7,10},{8,5},{9,4},... | collective-permute-start | bytes 37640 | tf_op jit(solution)/shard_map/ppermute | solution.py:41
  36.1 1.4 %collective-permute-start.12 = (bf16[7,1,7,128]{3,2,1,0:T(8,128)(2,1)S(1)}, bf16[7,1,7,128]{3,2,1,0:T(8,128)(2,1)S(1)}, u32[]{:S(2)}, u32[]{:S(2)}) collective-permute-start(bf16[7,1,7,128]{3,2,1,0:T(8,128)(2,1)S(1)} %get-tuple-element.33), channel_id=1, source_target_pairs={{0,5},{1,4},{2,7},{3,6},{4,1},{5,0},{6,3},{7,2},{8,13},{9,12},{10,... | collective-permute-start | bytes 37640 | tf_op jit(solution)/shard_map/ppermute | solution.py:41
  37.5 0.8 %collective-permute-start.18 = (bf16[128,704]{1,0:T(8,128)(2,1)S(1)}, bf16[128,704]{1,0:T(8,128)(2,1)S(1)}, u32[]{:S(2)}, u32[]{:S(2)}) collective-permute-start(bf16[128,704]{1,0:T(8,128)(2,1)S(1)} %pad_maximum_fusion.2), channel_id=1, source_target_pairs={{0,3},{1,2},{2,1},{3,0},{4,7},{5,6},{6,5},{7,4},{8,11},{9,10},{10,... | collective-permute-start | bytes 540680 | tf_op jit(solution)/shard_map/ppermute | solution.py:59
  39.4 2.5 %collective-permute-start.14 = (bf16[1,7,7,128]{3,2,1,0:T(8,128)(2,1)S(1)}, bf16[1,7,7,128]{3,2,1,0:T(8,128)(2,1)S(1)}, u32[]{:S(2)}, u32[]{:S(2)}) collective-permute-start(bf16[1,7,7,128]{3,2,1,0:T(8,128)(2,1)S(1)} %fusion.84), channel_id=1, source_target_pairs={{0,17},{1,16},{2,19},{3,18},{4,21},{5,20},{6,23},{7,22},{8,25},{9,... | collective-permute-start | bytes 37640 | tf_op jit(solution)/shard_map/ppermute | solution.py:41
  42.0 2.4 %collective-permute-done.18 = bf16[128,704]{1,0:T(8,128)(2,1)S(1)} collective-permute-done((bf16[128,704]{1,0:T(8,128)(2,1)S(1)}, bf16[128,704]{1,0:T(8,128)(2,1)S(1)}, u32[]{:S(2)}, u32[]{:S(2)}) %collective-permute-start.18) | collective-permute-done | bytes 180256 | tf_op jit(solution)/shard_map/ppermute | solution.py:59
  46.0 0.6 collective-permute-start.15
  46.7 1.0 %collective-permute-start.16 = (bf16[7,1,7,128]{3,2,1,0:T(8,128)(2,1)S(1)}, bf16[7,1,7,128]{3,2,1,0:T(8,128)(2,1)S(1)}, u32[]{:S(2)}, u32[]{:S(2)}) collective-permute-start(bf16[7,1,7,128]{3,2,1,0:T(8,128)(2,1)S(1)} %slice.699), channel_id=1, source_target_pairs={{0,13},{1,12},{2,15},{3,14},{4,9},{5,8},{6,11},{7,10},{8,5},{9,4},... | collective-permute-start | bytes 37640 | tf_op jit(solution)/shard_map/ppermute | solution.py:41
  48.0 1.2 %collective-permute-done.15 = bf16[7,1,7,128]{3,2,1,0:T(8,128)(2,1)S(1)} collective-permute-done((bf16[7,1,7,128]{3,2,1,0:T(8,128)(2,1)S(1)}, bf16[7,1,7,128]{3,2,1,0:T(8,128)(2,1)S(1)}, u32[]{:S(2)}, u32[]{:S(2)}) %collective-permute-start.15) | collective-permute-done | bytes 12576 | tf_op jit(solution)/shard_map/ppermute | solution.py:41
  49.2 1.5 %collective-permute-done.16 = bf16[7,1,7,128]{3,2,1,0:T(8,128)(2,1)S(1)} collective-permute-done((bf16[7,1,7,128]{3,2,1,0:T(8,128)(2,1)S(1)}, bf16[7,1,7,128]{3,2,1,0:T(8,128)(2,1)S(1)}, u32[]{:S(2)}, u32[]{:S(2)}) %collective-permute-start.16) | collective-permute-done | bytes 12576 | tf_op jit(solution)/shard_map/ppermute | solution.py:41
  52.7 2.5 %collective-permute-start.20 = (bf16[212,128]{1,0:T(8,128)(2,1)S(1)}, bf16[212,128]{1,0:T(8,128)(2,1)S(1)}, u32[]{:S(2)}, u32[]{:S(2)}) collective-permute-start(bf16[212,128]{1,0:T(8,128)(2,1)S(1)} %pad_maximum_fusion.11), channel_id=1, source_target_pairs={{0,17},{1,16},{2,19},{3,18},{4,21},{5,20},{6,23},{7,22},{8,25},{9,... | collective-permute-start | bytes 162824 | tf_op jit(solution)/shard_map/ppermute | solution.py:59
  55.2 3.5 %collective-permute-done.20 = bf16[212,128]{1,0:T(8,128)(2,1)S(1)} collective-permute-done((bf16[212,128]{1,0:T(8,128)(2,1)S(1)}, bf16[212,128]{1,0:T(8,128)(2,1)S(1)}, u32[]{:S(2)}, u32[]{:S(2)}) %collective-permute-start.20) | collective-permute-done | bytes 54304 | tf_op jit(solution)/shard_map/ppermute | solution.py:59
  58.9 1.0 %collective-permute-start.21 = (bf16[176,128]{1,0:T(8,128)(2,1)S(1)}, bf16[176,128]{1,0:T(8,128)(2,1)S(1)}, u32[]{:S(2)}, u32[]{:S(2)}) collective-permute-start(bf16[176,128]{1,0:T(8,128)(2,1)S(1)} %add_convert_fusion.2), channel_id=1, source_target_pairs={{0,5},{1,4},{2,7},{3,6},{4,1},{5,0},{6,3},{7,2},{8,13},{9,12},{10,... | collective-permute-start | bytes 135176 | tf_op jit(solution)/shard_map/ppermute | solution.py:41
  60.1 2.5 %collective-permute-done.21 = bf16[176,128]{1,0:T(8,128)(2,1)S(1)} collective-permute-done((bf16[176,128]{1,0:T(8,128)(2,1)S(1)}, bf16[176,128]{1,0:T(8,128)(2,1)S(1)}, u32[]{:S(2)}, u32[]{:S(2)}) %collective-permute-start.21) | collective-permute-done | bytes 45088 | tf_op jit(solution)/shard_map/ppermute | solution.py:41
  63.0 4.2 %collective-permute-done.22 = bf16[176,128]{1,0:T(8,128)(2,1)S(1)} collective-permute-done((bf16[176,128]{1,0:T(8,128)(2,1)S(1)}, bf16[176,128]{1,0:T(8,128)(2,1)S(1)}, u32[]{:S(2)}, u32[]{:S(2)}) %collective-permute-start.22) | collective-permute-done | bytes 45088 | tf_op jit(solution)/shard_map/ppermute | solution.py:41
  67.3 1.0 %collective-permute-start.23 = (bf16[284,128]{1,0:T(8,128)(2,1)S(1)}, bf16[284,128]{1,0:T(8,128)(2,1)S(1)}, u32[]{:S(2)}, u32[]{:S(2)}) collective-permute-start(bf16[284,128]{1,0:T(8,128)(2,1)S(1)} %maximum_maximum_fusion.1), channel_id=1, source_target_pairs={{0,3},{1,2},{2,1},{3,0},{4,7},{5,6},{6,5},{7,4},{8,11},{9,10},{10,... | collective-permute-start | bytes 218120 | tf_op jit(solution)/shard_map/ppermute | solution.py:59
  68.7 2.9 %collective-permute-done.23 = bf16[284,128]{1,0:T(8,128)(2,1)S(1)} collective-permute-done((bf16[284,128]{1,0:T(8,128)(2,1)S(1)}, bf16[284,128]{1,0:T(8,128)(2,1)S(1)}, u32[]{:S(2)}, u32[]{:S(2)}) %collective-permute-start.23) | collective-permute-done | bytes 72736 | tf_op jit(solution)/shard_map/ppermute | solution.py:59
  72.4 0.7 collective-permute-done.25
  73.4 0.7 pad_maximum_fusion.15
  74.6 1.0 %maximum_convert_fusion = f32[704,128]{1,0:T(8,128)} fusion(bf16[176,32]{1,0:T(8,128)(2,1)S(1)} %get-tuple-element.118, bf16[176,32]{1,0:T(8,128)(2,1)S(1)} %get-tuple-element.114, bf16[176,32]{1,0:T(8,128)(2,1)S(1)} %get-tuple-element.110, bf16[176,32]{1,0:T(8,128)(2,1)S(1)} %get-tuple-element.106, bf16[176,32]{1,0:T(8,128)(2,1)S(1)} %get-tuple-element.119, ...), kind=kLoop, calls=%fused_computation.51 | loop fusion | flops 2883584 | bytes 540672 | tf_op jit(solution)/shard_map/convert_element_type | solution.py:331
  (170 shorter events, 14.9 us)
Async XLA Ops:
  0.6 5.5 %copy-start = (bf16[1,343,343]{2,1,0:T(8,128)(2,1)S(1)}, bf16[1,343,343]{2,1,0:T(8,128)(2,1)}, u32[]{:S(2)}) copy-start(bf16[1,343,343]{2,1,0:T(8,128)(2,1)} %param.6) | copy-start | bytes 705898
  1.5 4.6 %copy-start.2 = (s32[1,343]{1,0:T(1,128)S(1)}, s32[1,343]{1,0:T(1,128)}, u32[]{:S(2)}) copy-start(s32[1,343]{1,0:T(1,128)} %param.7) | copy-start | bytes 4120
  1.5 4.6 %copy-start.3 = (f32[343]{0:T(512)S(1)}, f32[343]{0:T(512)}, u32[]{:S(2)}) copy-start(f32[343]{0:T(512)} %param.8) | copy-start | bytes 4120
  1.6 8.0 %collective-permute-start = (bf16[6,1,6,128]{3,2,1,0:T(8,128)(2,1)S(1)}, bf16[6,1,6,128]{3,2,1,0:T(8,128)(2,1)S(1)}, u32[]{:S(2)}, u32[]{:S(2)}) collective-permute-start(bf16[6,1,6,128]{3,2,1,0:T(8,128)(2,1)S(1)} %slice.517), channel_id=1, source_target_pairs={{0,4},{1,5},{2,6},{3,7},{4,0},{5,1},{6,2},{7,3},{8,12},{9,13},{10,... | collective-permute-start | bytes 27656 | tf_op jit(solution)/shard_map/ppermute | solution.py:41
  4.6 5.0 %collective-permute-start.1 = (bf16[6,1,6,128]{3,2,1,0:T(8,128)(2,1)S(1)}, bf16[6,1,6,128]{3,2,1,0:T(8,128)(2,1)S(1)}, u32[]{:S(2)}, u32[]{:S(2)}) collective-permute-start(bf16[6,1,6,128]{3,2,1,0:T(8,128)(2,1)S(1)} %slice.517), channel_id=1, source_target_pairs={{0,12},{1,13},{2,14},{3,15},{4,8},{5,9},{6,10},{7,11},{8,4},{9,5},... | collective-permute-start | bytes 27656 | tf_op jit(solution)/shard_map/ppermute | solution.py:41
  6.2 1.2 %copy-start.1 = (bf16[216,704]{1,0:T(8,128)(2,1)S(1)}, bf16[216,704]{1,0:T(8,128)(2,1)}, u32[]{:S(2)}) copy-start(bf16[216,704]{1,0:T(8,128)(2,1)} %param.9) | copy-start | bytes 912388
  6.9 14.0 %collective-permute-start.4 = (bf16[343,343]{1,0:T(8,128)(2,1)S(1)}, bf16[343,343]{1,0:T(8,128)(2,1)S(1)}, u32[]{:S(2)}, u32[]{:S(2)}) collective-permute-start(bf16[343,343]{1,0:T(8,128)(2,1)S(1)} %fusion), channel_id=1, source_target_pairs={{0,3},{1,2},{2,1},{3,0},{4,7},{5,6},{6,5},{7,4},{8,11},{9,10},{10,... | collective-permute-start | bytes 705902 | tf_op jit(solution)/shard_map/ppermute | solution.py:59
  7.4 15.2 %collective-permute-start.7 = (bf16[124,704]{1,0:T(8,128)(2,1)S(1)}, bf16[124,704]{1,0:T(8,128)(2,1)S(1)}, u32[]{:S(2)}, u32[]{:S(2)}) collective-permute-start(bf16[124,704]{1,0:T(8,128)(2,1)S(1)} %slice.426), channel_id=1, source_target_pairs={{0,3},{1,2},{2,1},{3,0},{4,7},{5,6},{6,5},{7,4},{8,11},{9,10},{10,... | collective-permute-start | bytes 523784 | tf_op jit(solution)/shard_map/ppermute | solution.py:59
  9.7 6.4 %collective-permute-start.2 = (bf16[258,128]{1,0:T(8,128)(2,1)S(1)}, bf16[258,128]{1,0:T(8,128)(2,1)S(1)}, u32[]{:S(2)}, u32[]{:S(2)}) collective-permute-start(bf16[258,128]{1,0:T(8,128)(2,1)S(1)} %pad_maximum_fusion.10), channel_id=1, source_target_pairs={{0,16},{1,17},{2,18},{3,19},{4,20},{5,21},{6,22},{7,23},{8,24},{9,... | collective-permute-start | bytes 198152 | tf_op jit(solution)/shard_map/ppermute | solution.py:41
  12.3 11.1 %collective-permute-start.8 = (bf16[343,343]{1,0:T(8,128)(2,1)S(1)}, bf16[343,343]{1,0:T(8,128)(2,1)S(1)}, u32[]{:S(2)}, u32[]{:S(2)}) collective-permute-start(bf16[343,343]{1,0:T(8,128)(2,1)S(1)} %fusion), channel_id=1, source_target_pairs={{0,1},{1,0},{2,3},{3,2},{4,5},{5,4},{6,7},{7,6},{8,9},{9,8},{10,11... | collective-permute-start | bytes 705902 | tf_op jit(solution)/shard_map/ppermute | solution.py:59
  16.5 4.1 %collective-permute-start.3 = (bf16[152,128]{1,0:T(8,128)(2,1)S(1)}, bf16[152,128]{1,0:T(8,128)(2,1)S(1)}, u32[]{:S(2)}, u32[]{:S(2)}) collective-permute-start(bf16[152,128]{1,0:T(8,128)(2,1)S(1)} %pad_maximum_fusion.16), channel_id=1, source_target_pairs={{0,3},{1,2},{2,1},{3,0},{4,7},{5,6},{6,5},{7,4},{8,11},{9,10},{10,... | collective-permute-start | bytes 116744 | tf_op jit(solution)/shard_map/ppermute | solution.py:59
  20.9 1.3 %collective-permute-start.5 = (bf16[152,128]{1,0:T(8,128)(2,1)S(1)}, bf16[152,128]{1,0:T(8,128)(2,1)S(1)}, u32[]{:S(2)}, u32[]{:S(2)}) collective-permute-start(bf16[152,128]{1,0:T(8,128)(2,1)S(1)} %pad_maximum_fusion.17), channel_id=1, source_target_pairs={{0,1},{1,0},{2,3},{3,2},{4,5},{5,4},{6,7},{7,6},{8,9},{9,8},{10,11... | collective-permute-start | bytes 116744 | tf_op jit(solution)/shard_map/ppermute | solution.py:59
  21.1 1.6 %collective-permute-start.6 = (bf16[343,343]{1,0:T(8,128)(2,1)S(1)}, bf16[343,343]{1,0:T(8,128)(2,1)S(1)}, u32[]{:S(2)}, u32[]{:S(2)}) collective-permute-start(bf16[343,343]{1,0:T(8,128)(2,1)S(1)} %collective-permute-done.4), channel_id=1, source_target_pairs={{0,1},{1,0},{2,3},{3,2},{4,5},{5,4},{6,7},{7,6},{8,9},{9,8},{10,11... | collective-permute-start | bytes 705902 | tf_op jit(solution)/shard_map/ppermute | solution.py:59
  24.3 4.1 %collective-permute-start.10 = (bf16[7,1,7,128]{3,2,1,0:T(8,128)(2,1)S(1)}, bf16[7,1,7,128]{3,2,1,0:T(8,128)(2,1)S(1)}, u32[]{:S(2)}, u32[]{:S(2)}) collective-permute-start(bf16[7,1,7,128]{3,2,1,0:T(8,128)(2,1)S(1)} %broadcast_select_fusion.45), channel_id=1, source_target_pairs={{0,13},{1,12},{2,15},{3,14},{4,9},{5,8},{6,11},{7,10},{8,5},{9,4},... | collective-permute-start | bytes 37640 | tf_op jit(solution)/shard_map/ppermute | solution.py:41
  25.7 3.2 %collective-permute-start.9 = (bf16[7,1,7,128]{3,2,1,0:T(8,128)(2,1)S(1)}, bf16[7,1,7,128]{3,2,1,0:T(8,128)(2,1)S(1)}, u32[]{:S(2)}, u32[]{:S(2)}) collective-permute-start(bf16[7,1,7,128]{3,2,1,0:T(8,128)(2,1)S(1)} %get-tuple-element.36), channel_id=1, source_target_pairs={{0,5},{1,4},{2,7},{3,6},{4,1},{5,0},{6,3},{7,2},{8,13},{9,12},{10,... | collective-permute-start | bytes 37640 | tf_op jit(solution)/shard_map/ppermute | solution.py:41
  29.0 4.1 %collective-permute-start.11 = (bf16[1,7,7,128]{3,2,1,0:T(8,128)(2,1)S(1)}, bf16[1,7,7,128]{3,2,1,0:T(8,128)(2,1)S(1)}, u32[]{:S(2)}, u32[]{:S(2)}) collective-permute-start(bf16[1,7,7,128]{3,2,1,0:T(8,128)(2,1)S(1)} %fusion.83), channel_id=1, source_target_pairs={{0,17},{1,16},{2,19},{3,18},{4,21},{5,20},{6,23},{7,22},{8,25},{9,... | collective-permute-start | bytes 37640 | tf_op jit(solution)/shard_map/ppermute | solution.py:41
  31.6 20.0 %collective-permute-start.17 = (bf16[252,704]{1,0:T(8,128)(2,1)S(1)}, bf16[252,704]{1,0:T(8,128)(2,1)S(1)}, u32[]{:S(2)}, u32[]{:S(2)}) collective-permute-start(bf16[252,704]{1,0:T(8,128)(2,1)S(1)} %pad_maximum_fusion), channel_id=1, source_target_pairs={{0,1},{1,0},{2,3},{3,2},{4,5},{5,4},{6,7},{7,6},{8,9},{9,8},{10,11... | collective-permute-start | bytes 1064456 | tf_op jit(solution)/shard_map/ppermute | solution.py:59
  34.6 2.9 %slice-start = ((bf16[216,704]{1,0:T(8,128)(2,1)}), bf16[92,704]{1,0:T(8,128)(2,1)S(1)}, s32[]{:S(2)}) async-start(bf16[216,704]{1,0:T(8,128)(2,1)} %param.9), calls=%async_computation | async-start | bytes 294912 | tf_op jit(solution)/shard_map/slice | solution.py:210
  34.6 4.1 %collective-permute-start.13 = (bf16[7,1,7,128]{3,2,1,0:T(8,128)(2,1)S(1)}, bf16[7,1,7,128]{3,2,1,0:T(8,128)(2,1)S(1)}, u32[]{:S(2)}, u32[]{:S(2)}) collective-permute-start(bf16[7,1,7,128]{3,2,1,0:T(8,128)(2,1)S(1)} %broadcast_select_fusion.44), channel_id=1, source_target_pairs={{0,13},{1,12},{2,15},{3,14},{4,9},{5,8},{6,11},{7,10},{8,5},{9,4},... | collective-permute-start | bytes 37640 | tf_op jit(solution)/shard_map/ppermute | solution.py:41
  36.1 3.3 %collective-permute-start.12 = (bf16[7,1,7,128]{3,2,1,0:T(8,128)(2,1)S(1)}, bf16[7,1,7,128]{3,2,1,0:T(8,128)(2,1)S(1)}, u32[]{:S(2)}, u32[]{:S(2)}) collective-permute-start(bf16[7,1,7,128]{3,2,1,0:T(8,128)(2,1)S(1)} %get-tuple-element.33), channel_id=1, source_target_pairs={{0,5},{1,4},{2,7},{3,6},{4,1},{5,0},{6,3},{7,2},{8,13},{9,12},{10,... | collective-permute-start | bytes 37640 | tf_op jit(solution)/shard_map/ppermute | solution.py:41
  37.5 6.9 %collective-permute-start.18 = (bf16[128,704]{1,0:T(8,128)(2,1)S(1)}, bf16[128,704]{1,0:T(8,128)(2,1)S(1)}, u32[]{:S(2)}, u32[]{:S(2)}) collective-permute-start(bf16[128,704]{1,0:T(8,128)(2,1)S(1)} %pad_maximum_fusion.2), channel_id=1, source_target_pairs={{0,3},{1,2},{2,1},{3,0},{4,7},{5,6},{6,5},{7,4},{8,11},{9,10},{10,... | collective-permute-start | bytes 540680 | tf_op jit(solution)/shard_map/ppermute | solution.py:59
  39.4 5.0 %collective-permute-start.14 = (bf16[1,7,7,128]{3,2,1,0:T(8,128)(2,1)S(1)}, bf16[1,7,7,128]{3,2,1,0:T(8,128)(2,1)S(1)}, u32[]{:S(2)}, u32[]{:S(2)}) collective-permute-start(bf16[1,7,7,128]{3,2,1,0:T(8,128)(2,1)S(1)} %fusion.84), channel_id=1, source_target_pairs={{0,17},{1,16},{2,19},{3,18},{4,21},{5,20},{6,23},{7,22},{8,25},{9,... | collective-permute-start | bytes 37640 | tf_op jit(solution)/shard_map/ppermute | solution.py:41
  46.0 3.2 %collective-permute-start.15 = (bf16[7,1,7,128]{3,2,1,0:T(8,128)(2,1)S(1)}, bf16[7,1,7,128]{3,2,1,0:T(8,128)(2,1)S(1)}, u32[]{:S(2)}, u32[]{:S(2)}) collective-permute-start(bf16[7,1,7,128]{3,2,1,0:T(8,128)(2,1)S(1)} %slice.699), channel_id=1, source_target_pairs={{0,5},{1,4},{2,7},{3,6},{4,1},{5,0},{6,3},{7,2},{8,13},{9,12},{10,... | collective-permute-start | bytes 37640 | tf_op jit(solution)/shard_map/ppermute | solution.py:41
  46.7 4.0 %collective-permute-start.16 = (bf16[7,1,7,128]{3,2,1,0:T(8,128)(2,1)S(1)}, bf16[7,1,7,128]{3,2,1,0:T(8,128)(2,1)S(1)}, u32[]{:S(2)}, u32[]{:S(2)}) collective-permute-start(bf16[7,1,7,128]{3,2,1,0:T(8,128)(2,1)S(1)} %slice.699), channel_id=1, source_target_pairs={{0,13},{1,12},{2,15},{3,14},{4,9},{5,8},{6,11},{7,10},{8,5},{9,4},... | collective-permute-start | bytes 37640 | tf_op jit(solution)/shard_map/ppermute | solution.py:41
  47.7 4.2 %collective-permute-start.19 = (bf16[252,704]{1,0:T(8,128)(2,1)S(1)}, bf16[252,704]{1,0:T(8,128)(2,1)S(1)}, u32[]{:S(2)}, u32[]{:S(2)}) collective-permute-start(bf16[252,704]{1,0:T(8,128)(2,1)S(1)} %constant_dynamic-update-slice_fusion.6), channel_id=1, source_target_pairs={{0,1},{1,0},{2,3},{3,2},{4,5},{5,4},{6,7},{7,6},{8,9},{9,8},{10,11... | collective-permute-start | bytes 1064456 | tf_op jit(solution)/shard_map/ppermute | solution.py:59
  52.7 6.0 %collective-permute-start.20 = (bf16[212,128]{1,0:T(8,128)(2,1)S(1)}, bf16[212,128]{1,0:T(8,128)(2,1)S(1)}, u32[]{:S(2)}, u32[]{:S(2)}) collective-permute-start(bf16[212,128]{1,0:T(8,128)(2,1)S(1)} %pad_maximum_fusion.11), channel_id=1, source_target_pairs={{0,17},{1,16},{2,19},{3,18},{4,21},{5,20},{6,23},{7,22},{8,25},{9,... | collective-permute-start | bytes 162824 | tf_op jit(solution)/shard_map/ppermute | solution.py:59
  58.9 3.7 %collective-permute-start.21 = (bf16[176,128]{1,0:T(8,128)(2,1)S(1)}, bf16[176,128]{1,0:T(8,128)(2,1)S(1)}, u32[]{:S(2)}, u32[]{:S(2)}) collective-permute-start(bf16[176,128]{1,0:T(8,128)(2,1)S(1)} %add_convert_fusion.2), channel_id=1, source_target_pairs={{0,5},{1,4},{2,7},{3,6},{4,1},{5,0},{6,3},{7,2},{8,13},{9,12},{10,... | collective-permute-start | bytes 135176 | tf_op jit(solution)/shard_map/ppermute | solution.py:41
  62.6 4.6 %collective-permute-start.22 = (bf16[176,128]{1,0:T(8,128)(2,1)S(1)}, bf16[176,128]{1,0:T(8,128)(2,1)S(1)}, u32[]{:S(2)}, u32[]{:S(2)}) collective-permute-start(bf16[176,128]{1,0:T(8,128)(2,1)S(1)} %add_convert_fusion.1), channel_id=1, source_target_pairs={{0,13},{1,12},{2,15},{3,14},{4,9},{5,8},{6,11},{7,10},{8,5},{9,4},... | collective-permute-start | bytes 135176 | tf_op jit(solution)/shard_map/ppermute | solution.py:41
  67.3 4.3 %collective-permute-start.23 = (bf16[284,128]{1,0:T(8,128)(2,1)S(1)}, bf16[284,128]{1,0:T(8,128)(2,1)S(1)}, u32[]{:S(2)}, u32[]{:S(2)}) collective-permute-start(bf16[284,128]{1,0:T(8,128)(2,1)S(1)} %maximum_maximum_fusion.1), channel_id=1, source_target_pairs={{0,3},{1,2},{2,1},{3,0},{4,7},{5,6},{6,5},{7,4},{8,11},{9,10},{10,... | collective-permute-start | bytes 218120 | tf_op jit(solution)/shard_map/ppermute | solution.py:59
  68.3 3.5 %collective-permute-start.24 = (bf16[176,128]{1,0:T(8,128)(2,1)S(1)}, bf16[176,128]{1,0:T(8,128)(2,1)S(1)}, u32[]{:S(2)}, u32[]{:S(2)}) collective-permute-start(bf16[176,128]{1,0:T(8,128)(2,1)S(1)} %add_convert_fusion), channel_id=1, source_target_pairs={{0,1},{1,0},{2,3},{3,2},{4,5},{5,4},{6,7},{7,6},{8,9},{9,8},{10,11... | collective-permute-start | bytes 135176 | tf_op jit(solution)/shard_map/ppermute | solution.py:59
  71.8 1.3 %collective-permute-start.25 = (bf16[108,128]{1,0:T(8,128)(2,1)S(1)}, bf16[108,128]{1,0:T(8,128)(2,1)S(1)}, u32[]{:S(2)}, u32[]{:S(2)}) collective-permute-start(bf16[108,128]{1,0:T(8,128)(2,1)S(1)} %pad_maximum_fusion.22), channel_id=1, source_target_pairs={{0,1},{1,0},{2,3},{3,2},{4,5},{5,4},{6,7},{7,6},{8,9},{9,8},{10,11... | collective-permute-start | bytes 82952 | tf_op jit(solution)/shard_map/ppermute | solution.py:59
  72.0 2.1 %collective-permute-start.26 = (bf16[176,128]{1,0:T(8,128)(2,1)S(1)}, bf16[176,128]{1,0:T(8,128)(2,1)S(1)}, u32[]{:S(2)}, u32[]{:S(2)}) collective-permute-start(bf16[176,128]{1,0:T(8,128)(2,1)S(1)} %slice.595), channel_id=1, source_target_pairs={{0,1},{1,0},{2,3},{3,2},{4,5},{5,4},{6,7},{7,6},{8,9},{9,8},{10,11... | collective-permute-start | bytes 135176 | tf_op jit(solution)/shard_map/ppermute | solution.py:59
